TPU v7x, 32 devices: a whole 2x2x4 slice. The times are simulated.
32 devices in a mesh: groups: 2 (over x), seq: 8 (over z, y), dp: 2 (over core).
Axes of the slice: x: 2, y: 2, z: 4, core: 2. Of those that a mesh axis runs over, the one named last changes fastest.
Arguments:
- tower_input: bfloat16 [4, 2048, 384], P(('groups', 'dp'), 'seq'), parts along dimension 0, may hold values from -8 to 8
- conv_weight: bfloat16 [5, 384, 768], replicated, may hold values from -0.125 to 0.125
- norm_gain: float32 [768], replicated, may hold values from 0.25 to 1.75
- query_weight: bfloat16 [768, 1024], replicated, may hold values from -0.25 to 0.25
- key_weight: bfloat16 [768, 128], replicated, may hold values from -8 to 8
- value_weight: bfloat16 [768, 192], replicated, may hold values from -0.21875 to 0.21875
- cotangent: bfloat16 [4, 1024, 1536], P(('groups', 'dp'), 'seq'), parts along dimension 0, may hold values from -6 to 6
Outputs:
- attended: bfloat16 [4, 1024, 1536], P(('groups', 'dp'), 'seq'), parts along dimension 0
- input_grad: bfloat16 [4, 2048, 384], P(('groups', 'dp'), 'seq'), parts along dimension 0
- conv_grad: float32 [3840, 768], P(('groups', 'seq', 'dp')), parts along dimension 0
- query_grad: float32 [1536, 1024], P(('groups', 'seq', 'dp')), parts along dimension 0
- key_grad: float32 [1536, 128], P(('groups', 'seq', 'dp')), parts along dimension 0
- value_grad: float32 [1536, 192], P(('groups', 'seq', 'dp')), parts along dimension 0
- gain_grad: float32 [1536], P(('groups', 'seq', 'dp')), parts along dimension 0
There are 2 independent parts, one for each index of `groups`. A program takes and returns all parts, laid end to end along the dimension named above; an argument that names none is the same for every part. Nothing has to cross between parts.
All inputs are finite; a program needn't handle non-finite values.
Results may differ from a plain program's by a relative error of at most 0.038.
The roundings to bfloat16 on the way count: a program that leaves them out, or rounds other values in their place, can miss the bound.
Values may be sent and summed in bfloat16 or wider, within the bound.
No kernel may reach another device: no remote copies, remote signals or barrier semaphores. Data moves between devices by JAX's collectives and lax.ppermute only.
A program may use at most 128 MiB of HBM per device.

v0:
```python
import math

import jax
import jax.numpy as jnp
from jax import lax
from jax.sharding import PartitionSpec as P


def padded_2(value, sides, width):
    for axis, dim in sides:
        devices, length = (lax.axis_size(axis), value.shape[dim])
        up = [(i, (i + 1) % devices) for i in range(devices - 1)]
        down = [(j, i) for i, j in up]
        last = lax.slice_in_dim(value, length - width, length, axis=dim)
        initial = lax.slice_in_dim(value, 0, width, axis=dim)
        before = lax.ppermute(last, axis, up)
        after = lax.ppermute(initial, axis, down)
        value = jnp.concatenate([before, value, after], axis=dim)
    return value


def gelu_slope(values_in):
    root_ratio = math.sqrt(2.0 / math.pi)
    inner = root_ratio * (values_in + 0.044715 * values_in * values_in * values_in)
    tangent = jnp.tanh(inner)
    return 0.5 * (1.0 + tangent) + 0.5 * values_in * (1.0 - tangent * tangent) * root_ratio * (
        1.0 + 3.0 * 0.044715 * values_in * values_in
    )


def on_device(
    tower_input, conv_weight, norm_gain, query_weight, key_weight, value_weight, cotangent
):
    seq_count, position_count, channels_in = tower_input.shape
    token_count = position_count // 2
    tap_count = conv_weight.shape[0]
    model_width = conv_weight.shape[2]
    key_size = key_weight.shape[1]
    value_size = value_weight.shape[1]
    head_count = cotangent.shape[2] // value_size
    input_wide = tower_input.astype(jnp.float32)
    activated = jax.nn.gelu(input_wide, approximate=True).astype(jnp.bfloat16)
    padded = padded_2(activated, (("seq", 1),), 2)
    conv_out = jnp.zeros((seq_count, position_count, model_width), jnp.float32)
    for offset in range(tap_count):
        conv_out = conv_out + jnp.einsum(
            "spc,cd->spd",
            padded[:, offset : offset + position_count],
            conv_weight[offset],
            preferred_element_type=jnp.float32,
        )
    paired = conv_out.reshape(seq_count, token_count, 2, model_width)
    pooled = 0.5 * (paired[:, :, 0] + paired[:, :, 1])
    inv_rms = lax.rsqrt(jnp.mean(pooled * pooled, axis=-1, keepdims=True) + 1e-06)
    normed = (pooled * inv_rms * norm_gain).astype(jnp.bfloat16)
    queries = (
        jnp.einsum("std,de->ste", normed, query_weight, preferred_element_type=jnp.float32)
        * key_size ** (-0.5)
    ).astype(jnp.bfloat16)
    keys = jnp.einsum("std,de->ste", normed, key_weight, preferred_element_type=jnp.float32).astype(
        jnp.bfloat16
    )
    values = jnp.einsum(
        "std,de->ste", normed, value_weight, preferred_element_type=jnp.float32
    ).astype(jnp.bfloat16)
    keys_all, values_all = (
        lax.all_gather(keys, "seq", axis=1, tiled=True),
        lax.all_gather(values, "seq", axis=1, tiled=True),
    )
    length_all = keys_all.shape[1]
    row_count = token_count * head_count
    query_rows = queries.reshape(seq_count, row_count, key_size)
    cot_rows = cotangent.reshape(seq_count, row_count, value_size)
    block_len = math.gcd(length_all, 512)
    block_count = length_all // block_len

    def block_scores(index, key_source):
        key_piece = lax.dynamic_slice_in_dim(key_source, index * block_len, block_len, 1)
        return (
            key_piece,
            jnp.einsum("srd,skd->srk", query_rows, key_piece, preferred_element_type=jnp.float32),
        )

    def total_step(index, state_now):
        row_max, exp_total = state_now
        key_piece, scores = block_scores(index, keys_all)
        new_max = jnp.maximum(row_max, jnp.max(scores, axis=-1))
        exp_total = exp_total * jnp.exp(row_max - new_max) + jnp.sum(
            jnp.exp(scores - new_max[..., None]), axis=-1
        )
        return (new_max, exp_total)

    start_max = jnp.full((seq_count, row_count), -jnp.inf, jnp.float32)
    start_total = jnp.zeros((seq_count, row_count), jnp.float32)
    row_max, exp_total = lax.fori_loop(0, block_count, total_step, (start_max, start_total))
    log_total = row_max + jnp.log(exp_total)

    def output_step(index, accumulated):
        key_piece, scores = block_scores(index, keys_all)
        value_piece = lax.dynamic_slice_in_dim(values_all, index * block_len, block_len, 1)
        weights = jnp.exp(scores - log_total[..., None]).astype(jnp.bfloat16)
        return accumulated + jnp.einsum(
            "srk,skc->src", weights, value_piece, preferred_element_type=jnp.float32
        )

    output = lax.fori_loop(
        0, block_count, output_step, jnp.zeros((seq_count, row_count, value_size), jnp.float32)
    )
    attended_rows = output.astype(jnp.bfloat16)
    attended = attended_rows.reshape(seq_count, token_count, head_count * value_size)
    keys_back, values_back = (keys_all, values_all)
    row_delta = jnp.sum(cot_rows.astype(jnp.float32) * attended_rows.astype(jnp.float32), axis=-1)

    def backward_step(index, state_now):
        query_acc, key_buffer, value_buffer = state_now
        key_piece, scores = block_scores(index, keys_back)
        value_piece = lax.dynamic_slice_in_dim(values_back, index * block_len, block_len, 1)
        probabilities = jnp.exp(scores - log_total[..., None])
        weights = probabilities.astype(jnp.bfloat16)
        prob_cot = jnp.einsum(
            "src,skc->srk", cot_rows, value_piece, preferred_element_type=jnp.float32
        )
        score_cot = (probabilities * (prob_cot - row_delta[..., None])).astype(jnp.bfloat16)
        query_acc = query_acc + jnp.einsum(
            "srk,skd->srd", score_cot, key_piece, preferred_element_type=jnp.float32
        )
        key_piece_cot = jnp.einsum(
            "srk,srd->skd", score_cot, query_rows, preferred_element_type=jnp.float32
        )
        value_piece_cot = jnp.einsum(
            "srk,src->skc", weights, cot_rows, preferred_element_type=jnp.float32
        )
        key_buffer = lax.dynamic_update_slice_in_dim(
            key_buffer, key_piece_cot, index * block_len, 1
        )
        value_buffer = lax.dynamic_update_slice_in_dim(
            value_buffer, value_piece_cot, index * block_len, 1
        )
        return (query_acc, key_buffer, value_buffer)

    start_back = (
        jnp.zeros((seq_count, row_count, key_size), jnp.float32),
        jnp.zeros((seq_count, length_all, key_size), jnp.float32),
        jnp.zeros((seq_count, length_all, value_size), jnp.float32),
    )
    query_acc, key_buffer, value_buffer = lax.fori_loop(0, block_count, backward_step, start_back)
    key_total, value_total = (
        lax.psum_scatter(key_buffer, "seq", scatter_dimension=1, tiled=True),
        lax.psum_scatter(value_buffer, "seq", scatter_dimension=1, tiled=True),
    )
    key_cot = key_total.astype(jnp.bfloat16)
    value_cot = value_total.astype(jnp.bfloat16)
    query_cot = (
        (query_acc * key_size ** (-0.5))
        .astype(jnp.bfloat16)
        .reshape(seq_count, token_count, head_count * key_size)
    )
    query_term = jnp.einsum("std,ste->de", normed, query_cot, preferred_element_type=jnp.float32)
    key_term = jnp.einsum("std,ste->de", normed, key_cot, preferred_element_type=jnp.float32)
    value_term = jnp.einsum("std,ste->de", normed, value_cot, preferred_element_type=jnp.float32)
    normed_cot = jnp.einsum(
        "ste,de->std", query_cot, query_weight, preferred_element_type=jnp.float32
    )
    normed_cot = normed_cot + jnp.einsum(
        "ste,de->std", key_cot, key_weight, preferred_element_type=jnp.float32
    )
    normed_cot = normed_cot + jnp.einsum(
        "ste,de->std", value_cot, value_weight, preferred_element_type=jnp.float32
    )
    gain_term = jnp.sum(normed_cot * pooled * inv_rms, axis=(0, 1))
    gained = norm_gain * normed_cot
    pooled_cot = (
        inv_rms * gained
        - pooled
        * inv_rms
        * inv_rms
        * inv_rms
        * jnp.sum(gained * pooled, axis=-1, keepdims=True)
        / model_width
    )
    half_cot = 0.5 * pooled_cot
    conv_cot = (
        jnp.broadcast_to(half_cot[:, :, None, :], (seq_count, token_count, 2, model_width))
        .reshape(seq_count, position_count, model_width)
        .astype(jnp.bfloat16)
    )
    conv_term = jnp.concatenate(
        [
            jnp.einsum(
                "spc,spd->cd",
                padded[:, offset : offset + position_count],
                conv_cot,
                preferred_element_type=jnp.float32,
            )
            for offset in range(tap_count)
        ],
        axis=0,
    )
    padded_cot = padded_2(conv_cot, (("seq", 1),), 2)
    active_cot = jnp.zeros((seq_count, position_count, channels_in), jnp.float32)
    for offset in range(tap_count):
        active_cot = active_cot + jnp.einsum(
            "spd,cd->spc",
            padded_cot[:, 4 - offset : 4 - offset + position_count],
            conv_weight[offset],
            preferred_element_type=jnp.float32,
        )
    input_grad = (active_cot * gelu_slope(input_wide)).astype(jnp.bfloat16)
    conv_grad, query_grad, key_grad, value_grad, gain_grad = (
        lax.psum_scatter(conv_term, ("seq", "dp"), scatter_dimension=0, tiled=True),
        lax.psum_scatter(query_term, ("seq", "dp"), scatter_dimension=0, tiled=True),
        lax.psum_scatter(key_term, ("seq", "dp"), scatter_dimension=0, tiled=True),
        lax.psum_scatter(value_term, ("seq", "dp"), scatter_dimension=0, tiled=True),
        lax.psum_scatter(gain_term, ("seq", "dp"), scatter_dimension=0, tiled=True),
    )
    return (attended, input_grad, conv_grad, query_grad, key_grad, value_grad, gain_grad)


def solution(mesh):
    placed = (
        P(("groups", "dp"), "seq", None),
        P(),
        P(),
        P(),
        P(),
        P(),
        P(("groups", "dp"), "seq", None),
    )
    return jax.shard_map(
        on_device,
        mesh=mesh,
        in_specs=placed,
        out_specs=(
            P(("groups", "dp"), "seq", None),
            P(("groups", "dp"), "seq", None),
            P(("groups", "seq", "dp"), None),
            P(("groups", "seq", "dp"), None),
            P(("groups", "seq", "dp"), None),
            P(("groups", "seq", "dp"), None),
            P(("groups", "seq", "dp")),
        ),
        check_vma=False,
    )
```

profile of v0, /device:TPU:0, one launch (start us, length us, event | category | flops | bytes accessed | tf_op | source)
XLA Modules:
  0.0 522.1 jit_solution(10240440311484805771)
XLA Ops:
  8.5 4.9 collective-permute-start
  14.7 1.4 reshape.462
  16.2 1.6 fusion.56
  17.8 1.4 convolution_add_fusion.3
  21.3 2.5 reshape.459
  23.8 2.1 fusion.125
  30.6 33.3 %all-gather = bf16[1024,128]{1,0:T(8,128)(2,1)S(1)} all-gather(bf16[128,128]{1,0:T(8,128)(2,1)} %convolution_convert_fusion.1), channel_id=2, replica_groups=mesh['groups'=2,'seq'=8,'dp'=2] {'seq'}, dimensions={0}, use_global_device_ids=true | all-gather | bytes 294912 | tf_op jit(solution)/shard_map/all_gather | solution.py:67
  64.0 1.7 while.48
  65.7 28.3 %all-gather.1 = bf16[1024,192]{0,1:T(8,128)(2,1)} all-gather(bf16[128,192]{0,1:T(8,128)(2,1)} %convolution_convert_fusion), channel_id=3, replica_groups=mesh['groups'=2,'seq'=8,'dp'=2] {'seq'}, dimensions={0}, use_global_device_ids=true | all-gather | bytes 442368 | tf_op jit(solution)/shard_map/all_gather | solution.py:68
  94.0 2.0 copy.26
  96.0 5.3 %while.49 = (s32[]{:T(128)}, f32[1,1024,192]{1,2,0:T(8,128)}, bf16[1,1024,128]{2,1,0:T(8,128)(2,1)S(1)}, bf16[1,1024,128]{2,1,0:T(8,128)(2,1)S(1)}, f32[1,1024]{...) while((s32[]{:T(128)}, f32[1,1024,192]{1,2,0:T(8,128)}, ...), condition=%wide.region_6.0_spmd.clone, body=%wide.region_5.0_spmd.clone.sunk | while | flops 336986112 | bytes 2234020 | solution.py:106
  96.1 2.5 fusion.179
  98.6 2.8 fusion.179
  101.4 2.1 copy.27
  106.6 8.5 %while.50 = (s32[]{:T(128)}, f32[1,1024,128]{2,1,0:T(8,128)S(1)}, f32[1,1024,128]{2,1,0:T(8,128)}, f32[1,1024,192]{1,2,0:T(8,128)}, bf16[1,1024,128]{2,1,0:T(8,1...) while((s32[]{:T(128)}, f32[1,1024,128]{2,1,0:T(8,128)S(1)}, ...), condition=%wide.region_9.0_spmd.clone, body=%wide.region_8.0_spmd.clone.sunk | while | flops 808714240 | bytes 18886956 | solution.py:146
  117.0 58.2 %reduce-scatter.7.cloned.1.call-done = f32[1,128,128]{2,1,0:T(8,128)} async-done(((f32[1,1024,128]{2,1,0:T(8,128)}), f32[1,128,128]{2,1,0:T(8,128)}) %reduce-scatter.7.cloned.1.call-update) | async-done | bytes 65552 | tf_op jit(solution)/shard_map/reduce_scatter | solution.py:148
  175.2 1.8 fusion.105
  177.1 64.0 %reduce-scatter.9.cloned.1.call-done = f32[1,128,192]{1,2,0:T(8,128)} async-done(((f32[1,1024,192]{1,2,0:T(8,128)}), f32[1,128,192]{1,2,0:T(8,128)}) %reduce-scatter.9.cloned.1.call-update) | async-done | bytes 98320 | tf_op jit(solution)/shard_map/reduce_scatter | solution.py:149
  241.1 2.0 fusion.102
  243.4 2.3 fusion.129
  248.8 1.4 convolution_dynamic-update-slice_fusion.4
  251.6 1.5 convolution_dynamic-update-slice_fusion.2
  260.4 1.4 fusion.51
  261.9 4.6 collective-permute-start.3
  266.5 29.5 %all-reduce = f32[768]{0:T(1024)S(1)} all-reduce(f32[768]{0:T(1024)S(1)} %get-tuple-element.508), channel_id=10, replica_groups=mesh['groups'=2,'seq'=8,'dp'=2] {'seq','dp'}, use_global_device_ids=true, to_apply=%region_18.0.clone | all-reduce | flops 768 | bytes 6144
  296.6 1.4 fusion.54
  298.1 1.5 fusion.45
  299.6 1.5 convolution_add_fusion.7
  301.0 2.3 fusion.46
  303.3 56.4 %reduce-scatter.17.cloned.1.call-done = f32[48,192]{1,0:T(8,128)} async-done(((f32[768,192]{1,0:T(8,128)}), f32[48,192]{1,0:T(8,128)}) %reduce-scatter.17.cloned.1.call-update) | async-done | bytes 36880 | tf_op jit(solution)/shard_map/reduce_scatter | solution.py:213
  359.7 69.4 %reduce-scatter.13.cloned.1.call-done = f32[48,1024]{1,0:T(8,128)} async-done(((f32[768,1024]{1,0:T(8,128)}), f32[48,1024]{1,0:T(8,128)}) %reduce-scatter.13.cloned.1.call-update) | async-done | bytes 196624 | tf_op jit(solution)/shard_map/reduce_scatter | solution.py:211
  429.2 86.1 %reduce-scatter.11.cloned.1.call-done = f32[120,768]{1,0:T(8,128)} async-done(((f32[1920,768]{1,0:T(8,128)}), f32[120,768]{1,0:T(8,128)}) %reduce-scatter.11.cloned.1.call-update) | async-done | bytes 368656 | tf_op jit(solution)/shard_map/reduce_scatter | solution.py:210
  (128 shorter events, 36.4 us)
Async XLA Ops:
  7.2 21.3 %copy-start = (bf16[768,1024]{1,0:T(8,128)(2,1)S(1)}, bf16[768,1024]{1,0:T(8,128)(2,1)}, u32[]{:S(2)}) copy-start(bf16[768,1024]{1,0:T(8,128)(2,1)} %param.16) | copy-start | bytes 4718596
  7.2 12.0 %copy-start.9 = (bf16[1,256,384]{2,1,0:T(8,128)(2,1)S(1)}, bf16[1,256,384]{2,1,0:T(8,128)(2,1)}, u32[]{:S(2)}) copy-start(bf16[1,256,384]{2,1,0:T(8,128)(2,1)} %param.13) | copy-start | bytes 589828
  7.2 168.0 %reduce-scatter.7.cloned.1.call-start = ((), (), s32[]{:S(2)}) async-start(), calls=%async_computation.6 | async-start | bytes 589824 | tf_op jit(solution)/shard_map/reduce_scatter | solution.py:148
  8.5 7.7 %collective-permute-start = (bf16[1,2,384]{2,1,0:T(2,128)(2,1)S(1)}, bf16[1,2,384]{2,1,0:T(2,128)(2,1)S(1)}, u32[]{:S(2)}, u32[]{:S(2)}) collective-permute-start(bf16[1,2,384]{2,1,0:T(2,128)(2,1)S(1)} %get-tuple-element.561), channel_id=1, source_target_pairs={{0,2},{2,4},{4,6},{6,8},{8,10},{10,12},{12,14},{1,3},{3,5},{5,7},{... | collective-permute-start | bytes 4616 | tf_op jit(solution)/shard_map/ppermute | solution.py:16
  13.4 6.3 %collective-permute-start.1 = (bf16[1,2,384]{2,1,0:T(2,128)(2,1)S(1)}, bf16[1,2,384]{2,1,0:T(2,128)(2,1)S(1)}, u32[]{:S(2)}, u32[]{:S(2)}) collective-permute-start(bf16[1,2,384]{2,1,0:T(2,128)(2,1)S(1)} %get-tuple-element.560), channel_id=1, source_target_pairs={{2,0},{4,2},{6,4},{8,6},{10,8},{12,10},{14,12},{3,1},{5,3},{7,5},{... | collective-permute-start | bytes 4616 | tf_op jit(solution)/shard_map/ppermute | solution.py:17
  16.1 3.1 copy-start.4
  16.2 3.5 copy-start.16
  19.7 4.2 copy-start.14
  20.0 6.6 %copy-start.13 = (f32[768]{0:T(1024)S(1)}, f32[768]{0:T(1024)}, u32[]{:S(2)}) copy-start(f32[768]{0:T(1024)} %param.15) | copy-start | bytes 9220
  23.8 2.9 copy-start.10
  23.8 3.8 copy-start.8
  26.1 2.4 copy-start.1
  26.7 37.3 %copy-start.18 = (f32[128]{0:T(128)}, f32[128]{0:T(128)S(1)}, u32[]{:S(2)}) copy-start(f32[128]{0:T(128)S(1)} %get-tuple-element.563) | copy-start | bytes 1540
  106.6 9.3 %copy-start.19 = (f32[128]{0:T(128)S(1)}, f32[128]{0:T(128)}, u32[]{:S(2)}) copy-start(f32[128]{0:T(128)} %copy-done.18) | copy-start | bytes 1540
  106.6 1.7 copy-start.3
  108.3 1.2 copy-start.6
  110.8 1.8 copy-start.3
  112.6 1.2 copy-start.6
  115.1 126.0 %reduce-scatter.9.cloned.1.call-start = ((), (), s32[]{:S(2)}) async-start(), calls=%async_computation.7 | async-start | bytes 884736 | tf_op jit(solution)/shard_map/reduce_scatter | solution.py:149
  115.9 187.4 %reduce-scatter.15.cloned.1.call-start = ((), (), s32[]{:S(2)}) async-start(), calls=%async_computation.10 | async-start | bytes 417792 | tf_op jit(solution)/shard_map/reduce_scatter | solution.py:212
  177.1 182.7 %reduce-scatter.17.cloned.1.call-start = ((), (), s32[]{:S(2)}) async-start(), calls=%async_computation.11 | async-start | bytes 835584 | tf_op jit(solution)/shard_map/reduce_scatter | solution.py:213
  243.2 186.0 %reduce-scatter.13.cloned.1.call-start = ((), (), s32[]{:S(2)}) async-start(), calls=%async_computation.9 | async-start | bytes 3342336 | tf_op jit(solution)/shard_map/reduce_scatter | solution.py:211
  245.7 0.9 copy-start.11
  245.7 0.9 copy-start.12
  245.7 1.2 copy-start.2
  245.7 269.6 %reduce-scatter.11.cloned.1.call-start = ((), (), s32[]{:S(2)}) async-start(), calls=%async_computation.8 | async-start | bytes 6266880 | tf_op jit(solution)/shard_map/reduce_scatter | solution.py:210
  245.9 2.3 copy-start.20
  246.6 2.2 copy-start.17
  248.7 4.4 copy-start.15
  255.9 1.9 copy-start.5
  259.1 37.5 %collective-permute-start.2 = (bf16[1,2,768]{2,1,0:T(2,128)(2,1)S(1)}, bf16[1,2,768]{2,1,0:T(2,128)(2,1)S(1)}, u32[]{:S(2)}, u32[]{:S(2)}) collective-permute-start(bf16[1,2,768]{2,1,0:T(2,128)(2,1)S(1)} %get-tuple-element.559), channel_id=1, source_target_pairs={{2,0},{4,2},{6,4},{8,6},{10,8},{12,10},{14,12},{3,1},{5,3},{7,5},{... | collective-permute-start | bytes 9224 | tf_op jit(solution)/shard_map/ppermute | solution.py:17
  261.9 37.6 %collective-permute-start.3 = (bf16[1,2,768]{2,1,0:T(2,128)(2,1)S(1)}, bf16[1,2,768]{2,1,0:T(2,128)(2,1)S(1)}, u32[]{:S(2)}, u32[]{:S(2)}) collective-permute-start(bf16[1,2,768]{2,1,0:T(2,128)(2,1)S(1)} %get-tuple-element.558), channel_id=1, source_target_pairs={{0,2},{2,4},{4,6},{6,8},{8,10},{10,12},{12,14},{1,3},{3,5},{5,7},{... | collective-permute-start | bytes 9224 | tf_op jit(solution)/shard_map/ppermute | solution.py:16
  (3 other events, 2.3 us)
Sparse Core Ops, SparseCore 0:
  115.2 59.9 reduce-scatter.6
  178.9 62.1 reduce-scatter.8
  245.2 54.5 reduce-scatter.14
  304.1 55.5 reduce-scatter.16
  364.0 65.1 reduce-scatter.12
  433.5 81.7 reduce-scatter.10
where the time goes:
time: 523 us; the launch traced here: 522 us
  waiting for transfers between devices  335 us (64%)
  blocking collectives  91.2 us (17%)
  matrix products  44.4 us (8%)
  local copies, waits for them, and re-layouts  18.4 us (4%)
  between operations  15.2 us (3%)
  starting transfers between devices  12.4 us (2%)
  other arithmetic  5.4 us (1%)
    reduce_scatter x1, waiting for transfers between devices, on_device(): lax.psum_scatter(conv_term, ('seq', 'dp'), scatter_dimension=0, tiled=True)  86.1 us
    reduce_scatter x1, waiting for transfers between devices, on_device(): lax.psum_scatter(query_term, ('seq', 'dp'), scatter_dimension=0, tiled=True)  69.4 us
    reduce_scatter x1, waiting for transfers between devices, on_device(): lax.psum_scatter(value_buffer, 'seq', scatter_dimension=1, tiled=True)  64 us
    reduce_scatter x1, waiting for transfers between devices, on_device(): lax.psum_scatter(key_buffer, 'seq', scatter_dimension=1, tiled=True)  58.2 us
    reduce_scatter x1, waiting for transfers between devices, on_device(): lax.psum_scatter(value_term, ('seq', 'dp'), scatter_dimension=0, tiled=True)  56.4 us
    all_gather x1, blocking collectives, on_device(): lax.all_gather(keys, 'seq', axis=1, tiled=True)  33.3 us
    unnamed x1, blocking collectives  29.5 us
    all_gather x1, blocking collectives, on_device(): lax.all_gather(values, 'seq', axis=1, tiled=True)  28.3 us
  transfers between devices with their start and end apart: 10, of which 5 were waited for; matrix products, arithmetic and copies ran while one was open for 6% of the time, Pallas kernels for 0%

commit v1 on v0

v1 whole, which is shorter than its diff:
```python
import math

import jax
import jax.numpy as jnp
from jax import lax
from jax.experimental import pallas as pl
from jax.experimental.pallas import tpu as pltpu
from jax.sharding import PartitionSpec as P

BF = jnp.bfloat16
F32 = jnp.float32
ROOT = math.sqrt(2.0 / math.pi)
EPS = 1e-06
LANES = 128
VMEM_BYTES = 40 * 2**20


def dot(a, b):
    return lax.dot_general(a, b, (((1,), (0,)), ((), ())), preferred_element_type=F32)


def dot_t(a, b):
    return lax.dot_general(a, b, (((1,), (1,)), ((), ())), preferred_element_type=F32)


def run(body, outs, args, scratch=(), flops=0, name=None):
    size = sum(math.prod(a.shape) * a.dtype.itemsize for a in args)
    size += sum(math.prod(s) * jnp.dtype(t).itemsize for s, t in outs)
    vmem = pl.BlockSpec(memory_space=pltpu.VMEM)
    return pl.pallas_call(
        body,
        out_shape=[jax.ShapeDtypeStruct(s, t) for s, t in outs],
        in_specs=[vmem] * len(args),
        out_specs=[vmem] * len(outs),
        scratch_shapes=list(scratch),
        compiler_params=pltpu.CompilerParams(vmem_limit_bytes=VMEM_BYTES),
        cost_estimate=pl.CostEstimate(flops=flops, bytes_accessed=size, transcendentals=0),
        name=name,
    )(*args)


def gelu(v):
    return v * (0.5 * (1.0 + jnp.tanh(ROOT * (v + 0.044715 * (v * v * v)))))


def gelu_slope(v):
    tangent = jnp.tanh(ROOT * (v + 0.044715 * v * v * v))
    return 0.5 * (1.0 + tangent) + 0.5 * v * (1.0 - tangent * tangent) * ROOT * (
        1.0 + 3.0 * 0.044715 * v * v
    )


def round_up(value, step):
    return -(-value // step) * step


def pack_kv(keys, values):
    tokens, size = keys.shape
    rest = values[:, size:]
    half = tokens // 2
    tail = jnp.concatenate([rest[:half], rest[half:]], axis=1)
    return jnp.concatenate([keys, values[:, :size], tail], axis=0)


def unpack_values(packed, tokens, size):
    tail = packed[2 * tokens :]
    width = tail.shape[1] // 2
    rest = jnp.concatenate([tail[:, :width], tail[:, width:]], axis=0)
    return jnp.concatenate([packed[tokens : 2 * tokens], rest], axis=1)


def put(ref, start, rows):
    for c in range(ref.shape[0]):
        ref[c, start : start + rows.shape[0]] = rows[:, c * LANES : (c + 1) * LANES]


def every_second(ref, start, count):
    parts = [ref[c, pl.ds(start, count, stride=2)] for c in range(ref.shape[0])]
    return jnp.concatenate(parts, axis=1)


def front_kernel(x, before, after, weight, gain, wk, wv, kv_out, early, pooled_out, pad):
    positions, channels = x.shape
    tokens = positions // 2
    ext = early.shape[0] // 2 - tokens
    put(pad, 6, gelu(before[...].astype(F32)).astype(BF).astype(F32))
    put(pad, 8, gelu(x[...].astype(F32)).astype(BF).astype(F32))
    put(pad, 8 + positions, jnp.zeros((pad.shape[1] - 8 - positions, channels), F32))
    put(pad, 8 + positions, gelu(after[...].astype(F32)).astype(BF).astype(F32))
    pieces = [every_second(pad, 6 + u, tokens).astype(BF) for u in range(6)]
    total = None
    for tap in range(5):
        rows = jnp.concatenate([pieces[tap], pieces[tap + 1]], axis=0)
        term = dot(rows, weight[tap])
        total = term if total is None else total + term
    pooled = 0.5 * (total[:tokens] + total[tokens:])
    inv = lax.rsqrt(jnp.mean(pooled * pooled, axis=-1, keepdims=True) + EPS)
    normed = (pooled * inv * gain[...]).astype(BF)
    pooled_out[...] = pooled
    kv_out[...] = pack_kv(dot(normed, wk[...]), dot(normed, wv[...])).astype(BF)
    early[0:ext] = every_second(pad, 6, ext).astype(BF)
    early[ext : 2 * ext] = every_second(pad, 7, ext).astype(BF)
    early[2 * ext : 2 * ext + tokens] = normed[:, :channels]
    early[2 * ext + tokens :] = normed[:, channels:]


def query_kernel(early, wq, out, *, ext, scale):
    tokens = out.shape[0]
    normed = jnp.concatenate(
        [early[2 * ext : 2 * ext + tokens], early[2 * ext + tokens :]], axis=1
    )
    out[...] = (dot(normed, wq[...]) * scale).astype(BF)


def attend_kernel(*refs, blocks, heads, key_size, value_size, scale):
    q, cot = refs[:2]
    parts = refs[2 : 2 + blocks]
    att, dq, near, far, ks, vs, kt, vt, dk, dv = refs[2 + blocks :]
    tokens = q.shape[0]
    half = tokens // 2
    wide = value_size - key_size
    for i, part in enumerate(parts):
        at = i * tokens
        ks[at : at + tokens] = part[:tokens]
        vs[at : at + tokens, :key_size] = part[tokens : 2 * tokens]
        vs[at : at + half, key_size:] = part[2 * tokens :, :wide]
        vs[at + half : at + tokens, key_size:] = part[2 * tokens :, wide:]
        kt[:, at : at + tokens] = ks[at : at + tokens].astype(F32).T.astype(BF)
        vt[:, at : at + tokens] = vs[at : at + tokens].astype(F32).T.astype(BF)
    for pair in range(heads // 2):
        ql, cl, al = 2 * pair * key_size, 2 * pair * value_size, 2 * pair * value_size
        qs = jnp.concatenate(
            [q[:, ql : ql + key_size], q[:, ql + key_size : ql + 2 * key_size]], axis=0
        )
        both = cot[:, cl : cl + 2 * value_size]
        cs = jnp.concatenate([both[:, :value_size], both[:, value_size:]], axis=0)
        scores = dot_t(ks[...], qs)
        raised = jnp.exp(scores - jnp.max(scores, axis=0, keepdims=True))
        probs = raised * (1.0 / jnp.sum(raised, axis=0, keepdims=True))
        weights = probs.astype(BF)
        out_t = dot(vt[...], weights).astype(BF).astype(F32)
        delta = jnp.sum(cs.astype(F32).T * out_t, axis=0, keepdims=True)
        prob_cot = dot_t(vs[...], cs)
        score_cot = (probs * (prob_cot - delta)).astype(BF)
        dq_t = dot(kt[...], score_cot) * scale
        dk_term = dot(score_cot, qs)
        dv_term = dot(weights, cs)
        if pair == 0:
            dk[...] = dk_term
            dv[...] = dv_term
        else:
            dk[...] += dk_term
            dv[...] += dv_term
        out_rows = jnp.concatenate([out_t[:, :tokens].T, out_t[:, tokens:].T], axis=1)
        att[:, al : al + 2 * value_size] = out_rows.astype(BF)
        dq_rows = jnp.concatenate([dq_t[:, :tokens].T, dq_t[:, tokens:].T], axis=1)
        dq[:, ql : ql + 2 * key_size] = dq_rows.astype(BF)
    count = blocks // 2
    for i in range(blocks):
        at = slice(i * tokens, (i + 1) * tokens)
        packed = pack_kv(dk[at], dv[at])
        if i < count:
            near[i] = packed
        else:
            far[i - count] = packed.astype(BF)


def add_kernel(near, far, own, *others):
    own[...] = near[0] + far[0].astype(F32)
    for k, other in enumerate(others):
        other[...] = (near[k + 1] + far[k + 1].astype(F32)).astype(BF)


def query_cot_kernel(dq, wq, out):
    out[...] = dot_t(dq[...], wq[...])


def make_middle(count):
    def middle(*refs):
        own, others = refs[0], refs[1:count]
        part, pooled_in, gain_in, wk, wv, message, edge = refs[count:]
        size = own.shape[1]
        tokens, width = pooled_in.shape
        total = own[...]
        for other in others:
            total = total + other[...].astype(F32)
        total = total.astype(BF).astype(F32)
        key_cot = total[:tokens]
        value_cot = unpack_values(total, tokens, size)
        normed_cot = part[...] + dot_t(key_cot.astype(BF), wk[...])
        normed_cot = normed_cot + dot_t(value_cot.astype(BF), wv[...])
        pooled, gain = pooled_in[...], gain_in[...]
        inv = lax.rsqrt(jnp.mean(pooled * pooled, axis=-1, keepdims=True) + EPS)
        gain_term = jnp.sum(normed_cot * pooled * inv, axis=0, keepdims=True)
        gained = gain * normed_cot
        pooled_cot = inv * gained - pooled * (inv * inv * inv) * (
            jnp.sum(gained * pooled, axis=-1, keepdims=True) / width
        )
        conv_cot = 0.5 * pooled_cot
        high = gain_term.astype(BF).astype(F32)
        low = gain_term - high
        row = lax.broadcasted_iota(jnp.int32, (16, width), 0)
        gains = jnp.where(row == 0, high, jnp.where(row == 1, low, 0.0))
        both = jnp.concatenate([key_cot, value_cot], axis=1)
        fill = width // 2 - both.shape[1]
        both = jnp.concatenate([both, jnp.zeros((tokens, fill), F32)], axis=1)
        side = jnp.concatenate([both[: tokens // 2], both[tokens // 2 :]], axis=1)
        message[:tokens] = conv_cot.astype(BF)
        message[tokens : tokens + 16] = gains.astype(BF)
        message[tokens + 16 :] = side.astype(BF)
        ends = jnp.where(row == 0, conv_cot[:1], jnp.where(row == 1, conv_cot[tokens - 1 :], 0.0))
        edge[...] = ends.astype(BF)

    return middle


def place():
    seq, dp = lax.axis_index("seq"), lax.axis_index("dp")
    high, low = seq // 2, seq % 2
    return lambda k: ((high ^ k) * 2 + low) * 2 + dp


def chosen(rows, padded, columns, block):
    row = lax.broadcasted_iota(jnp.int32, (padded, columns), 0)
    column = lax.broadcasted_iota(jnp.int32, (padded, columns), 1)
    hit = (column == row + block * rows) & (row < rows)
    return jnp.where(hit, 1.0, 0.0).astype(BF)


def select_kernel(*refs, groups, conv_rows, conv_pad, norm_rows, norm_pad):
    blocks = refs[:4]
    conv_out, norm_out, even, odd = refs[4:]
    ext, channels = even.shape
    tokens = (blocks[0].shape[0] - 2 * ext) // 2
    block_of = place()
    conv_pick = jnp.concatenate(
        [chosen(conv_rows, conv_pad, 5 * channels, block_of(k)) for k in range(groups)], axis=0
    )
    norm_pick = jnp.concatenate(
        [chosen(norm_rows, norm_pad, 2 * channels, block_of(k)) for k in range(groups)], axis=0
    )
    for i, block in enumerate(blocks):
        even[...] = block[:ext].astype(F32)
        odd[...] = block[ext : 2 * ext].astype(F32)
        pieces = []
        for shift in range(3):
            pieces += [even[shift : shift + tokens].astype(BF), odd[shift : shift + tokens].astype(BF)]
        rows = jnp.concatenate(
            [jnp.concatenate(pieces[:5], axis=1), jnp.concatenate(pieces[1:], axis=1)], axis=0
        )
        conv_out[:, 2 * i * tokens : 2 * (i + 1) * tokens] = dot_t(conv_pick, rows).astype(BF)
        normed = jnp.concatenate(
            [block[2 * ext : 2 * ext + tokens], block[2 * ext + tokens :]], axis=1
        )
        norm_out[:, i * tokens : (i + 1) * tokens] = dot_t(norm_pick, normed).astype(BF)


def query_grad_kernel(*refs, pad):
    pick, blocks = refs[0], refs[1:5]
    outs, right = refs[5:-1], refs[-1]
    tokens = blocks[0].shape[0]
    for i, block in enumerate(blocks):
        right[i * tokens : (i + 1) * tokens] = block[...]
    for k, out in enumerate(outs):
        out[...] = dot(pick[k * pad : (k + 1) * pad], right[...]).astype(out.dtype)


def query_sum_kernel(*refs):
    parts, out = refs[:-1], refs[-1]
    total = parts[0][...]
    for part in parts[1:]:
        total = total + part[...].astype(F32)
    out[...] = total[: out.shape[0]]


def conv_grad_kernel(*refs, conv_rows, conv_pad, norm_pad):
    pick, norm_pick, blocks = refs[0], refs[1], refs[2:6]
    outs, right, side = refs[6:-2], refs[-2], refs[-1]
    width = right.shape[1]
    tokens = side.shape[0] // 4
    half = tokens // 2
    gain = None
    for i, block in enumerate(blocks):
        piece = block[:tokens]
        right[2 * i * tokens : (2 * i + 1) * tokens] = piece
        right[(2 * i + 1) * tokens : (2 * i + 2) * tokens] = piece
        side[i * tokens : i * tokens + half] = block[tokens + 16 :, : width // 2]
        side[i * tokens + half : (i + 1) * tokens] = block[tokens + 16 :, width // 2 :]
        two = block[tokens : tokens + 16].astype(F32)
        term = two[0:1] + two[1:2]
        gain = term if gain is None else gain + term
    high = gain.astype(BF).astype(F32)
    low = gain - high
    row = lax.broadcasted_iota(jnp.int32, (conv_pad, width), 0)
    split = norm_pad // 2
    for k, out in enumerate(outs):
        conv = dot(pick[k * conv_pad : (k + 1) * conv_pad], right[...])
        conv = jnp.where(row == conv_rows, high, jnp.where(row == conv_rows + 1, low, conv))
        both = dot(norm_pick[k * norm_pad : (k + 1) * norm_pad], side[...])
        out[:conv_pad] = conv.astype(out.dtype)
        packed = jnp.concatenate([both[:split], both[split:]], axis=1)
        fill = out.shape[0] - conv_pad - split
        if fill:
            packed = jnp.concatenate([packed, jnp.zeros((fill, width), F32)], axis=0)
        out[conv_pad:] = packed.astype(out.dtype)


def final_kernel(*refs, conv_pad, norm_pad):
    parts = refs[:-4]
    conv, key, value, gain = refs[-4:]
    total = parts[0][...]
    for part in parts[1:]:
        total = total + part[...].astype(F32)
    rows, width = conv.shape
    count = key.shape[0]
    split = norm_pad // 2
    conv[...] = total[:rows]
    packed = total[conv_pad : conv_pad + split]
    both = jnp.concatenate([packed[:, : width // 2], packed[:, width // 2 :]], axis=0)
    size = key.shape[1]
    key[...] = both[:count, :size]
    value[...] = both[:count, size : size + value.shape[1]]
    line = jnp.broadcast_to(total[rows : rows + 1] + total[rows + 1 : rows + 2], (8, width))
    start = place()(0) * count
    gain[...] = pltpu.roll(line, lax.rem(width - start, width), 1)[:1, :count]


def input_kernel(x, cc, pair_cc, edge, weight, out, ext, mixed):
    tokens = x.shape[0] // 2
    low = lax.axis_index("seq") % 2
    ext[8 : 8 + tokens] = cc[:tokens].astype(F32)
    pair_first = pair_cc[0:16].astype(F32)[0:1]
    pair_last = pair_cc[tokens - 16 : tokens].astype(F32)[15:16]
    ends = edge[...].astype(F32)
    ext[7:8] = jnp.where(low == 0, ends[1:2], pair_last)
    ext[8 + tokens : 9 + tokens] = jnp.where(low == 0, pair_first, ends[0:1])
    back = ext[7 : 7 + tokens].astype(BF)
    here = ext[8 : 8 + tokens].astype(BF)
    ahead = ext[9 : 9 + tokens].astype(BF)
    evens = (ahead, here, here, back, back)
    odds = (ahead, ahead, here, here, back)
    total = None
    for tap in range(5):
        term = dot_t(jnp.concatenate([evens[tap], odds[tap]], axis=0), weight[tap])
        total = term if total is None else total + term
    for c in range(mixed.shape[0]):
        lanes = slice(c * LANES, (c + 1) * LANES)
        mixed[c, pl.ds(0, tokens, stride=2)] = total[:tokens, lanes]
        mixed[c, pl.ds(1, tokens, stride=2)] = total[tokens:, lanes]
        out[:, lanes] = (mixed[c] * gelu_slope(x[:, lanes].astype(F32))).astype(BF)


def on_device(x, conv_weight, norm_gain, wq, wk, wv, cotangent):
    devices = lax.axis_size("seq")
    both_axes = ("seq", "dp")
    x, cotangent = x[0], cotangent[0]
    positions, channels = x.shape
    tokens = positions // 2
    taps, _, width = conv_weight.shape
    key_size, value_size = wk.shape[1], wv.shape[1]
    heads = cotangent.shape[1] // value_size
    scale = key_size ** (-0.5)
    groups = devices // 2
    owners = devices * 2
    conv_rows, norm_rows = taps * channels // owners, width // owners
    conv_pad, norm_pad = round_up(conv_rows + 2, 16), round_up(norm_rows, 16)
    ext = tokens + 16
    gain = norm_gain.reshape(1, width)

    def swap(value, seq_bits, dp_bit=0):
        mask = 2 * seq_bits + dp_bit
        return lax.ppermute(value, both_axes, [(i, i ^ mask) for i in range(owners)])

    def quad(value):
        core = swap(value, 0, 1)
        near = swap(value, 1)
        return [value, core, near, swap(near, 0, 1)]

    up = [(i, i + 1) for i in range(devices - 1)]
    down = [(j, i) for i, j in up]
    before = lax.ppermute(x[positions - 2 :], "seq", up)
    after = lax.ppermute(x[:2], "seq", down)
    kv, early, pooled = run(
        front_kernel,
        [
            ((5 * tokens // 2, key_size), BF),
            ((2 * ext + 2 * tokens, channels), BF),
            ((tokens, width), F32),
        ],
        [x, before, after, conv_weight, gain, wk, wv],
        [pltpu.VMEM((channels // LANES, 8 + 2 * ext + 8, LANES), F32)],
        flops=2 * positions * taps * channels * width,
        name="front",
    )
    near_kv = [kv] + [swap(kv, 2 * k) for k in range(1, groups)]
    far_kv = [swap(block, 1) for block in near_kv]
    (queries,) = run(
        lambda e, w, o: query_kernel(e, w, o, ext=ext, scale=scale),
        [((tokens, heads * key_size), BF)],
        [early, wq],
        flops=2 * tokens * width * heads * key_size,
        name="queries",
    )
    length = devices * tokens
    attended, query_cot, near_cot, far_cot = run(
        lambda *refs: attend_kernel(
            *refs,
            blocks=devices,
            heads=heads,
            key_size=key_size,
            value_size=value_size,
            scale=scale,
        ),
        [
            ((tokens, heads * value_size), BF),
            ((tokens, heads * key_size), BF),
            ((groups, 5 * tokens // 2, key_size), F32),
            ((groups, 5 * tokens // 2, key_size), BF),
        ],
        [queries, cotangent] + near_kv + far_kv,
        [
            pltpu.VMEM((length, key_size), BF),
            pltpu.VMEM((length, value_size), BF),
            pltpu.VMEM((key_size, length), BF),
            pltpu.VMEM((value_size, length), BF),
            pltpu.VMEM((length, key_size), F32),
            pltpu.VMEM((length, value_size), F32),
        ],
        flops=6 * tokens * heads * length * (key_size + value_size),
        name="attend",
    )
    early_blocks = quad(early)
    conv_pick, norm_pick = run(
        lambda *refs: select_kernel(
            *refs,
            groups=groups,
            conv_rows=conv_rows,
            conv_pad=conv_pad,
            norm_rows=norm_rows,
            norm_pad=norm_pad,
        ),
        [((groups * conv_pad, 8 * tokens), BF), ((groups * norm_pad, 4 * tokens), BF)],
        early_blocks,
        [pltpu.VMEM((ext, channels), F32), pltpu.VMEM((ext, channels), F32)],
        flops=2 * groups * conv_pad * taps * channels * 8 * tokens,
        name="select",
    )
    far_sum = swap(far_cot, 1)
    block_shape = (5 * tokens // 2, key_size)
    own, *others = run(
        add_kernel,
        [(block_shape, F32)] + [(block_shape, BF)] * (groups - 1),
        [near_cot, far_sum],
        name="kv_cot_sum",
    )
    arrived = [swap(other, 2 * (k + 1)) for k, other in enumerate(others)]
    (normed_cot,) = run(
        query_cot_kernel,
        [((tokens, width), F32)],
        [query_cot, wq],
        flops=2 * tokens * width * heads * key_size,
        name="query_part",
    )
    query_blocks = quad(query_cot)
    query_parts = run(
        lambda *refs: query_grad_kernel(*refs, pad=norm_pad),
        [((norm_pad, heads * key_size), F32 if k == 0 else BF) for k in range(groups)],
        [norm_pick] + query_blocks,
        [pltpu.VMEM((4 * tokens, heads * key_size), BF)],
        flops=2 * groups * norm_pad * 4 * tokens * heads * key_size,
        name="query_grad",
    )
    message, edge = run(
        make_middle(groups),
        [((tokens + 16 + tokens // 2, width), BF), ((16, width), BF)],
        [own] + arrived + [normed_cot, pooled, gain, wk, wv],
        flops=2 * tokens * width * (key_size + value_size),
        name="conv_cot",
    )
    blocks = quad(message)
    crossing = [(i, i + 1) for i in range(1, devices - 1, 2)]
    crossing = crossing + [(j, i) for i, j in crossing]
    edge_in = lax.ppermute(edge, "seq", crossing)
    chunk_rows = round_up(conv_pad + norm_pad // 2, 16)
    conv_parts = run(
        lambda *refs: conv_grad_kernel(
            *refs, conv_rows=conv_rows, conv_pad=conv_pad, norm_pad=norm_pad
        ),
        [((chunk_rows, width), F32 if k == 0 else BF) for k in range(groups)],
        [conv_pick, norm_pick] + blocks,
        [pltpu.VMEM((8 * tokens, width), BF), pltpu.VMEM((4 * tokens, width // 2), BF)],
        flops=2 * groups * conv_pad * 8 * tokens * width,
        name="conv_grad",
    )
    conv_in = [swap(part, 2 * (k + 1)) for k, part in enumerate(conv_parts[1:])]
    query_in = [swap(part, 2 * (k + 1)) for k, part in enumerate(query_parts[1:])]
    (input_grad,) = run(
        input_kernel,
        [((positions, channels), BF)],
        [x, message, blocks[2], edge_in, conv_weight],
        [pltpu.VMEM((tokens + 16, width), F32), pltpu.VMEM((channels // LANES, positions, LANES), F32)],
        flops=2 * positions * taps * channels * width,
        name="input_grad",
    )
    (query_grad,) = run(
        query_sum_kernel,
        [((norm_rows, heads * key_size), F32)],
        [query_parts[0]] + query_in,
        name="query_sum",
    )
    conv_grad, key_grad, value_grad, gain_grad = run(
        lambda *refs: final_kernel(*refs, conv_pad=conv_pad, norm_pad=norm_pad),
        [
            ((conv_rows, width), F32),
            ((norm_rows, key_size), F32),
            ((norm_rows, value_size), F32),
            ((1, norm_rows), F32),
        ],
        [conv_parts[0]] + conv_in,
        name="conv_sum",
    )
    return (
        attended[None],
        input_grad[None],
        conv_grad,
        query_grad,
        key_grad,
        value_grad,
        gain_grad.reshape(norm_rows),
    )


def solution(mesh):
    placed = (
        P(("groups", "dp"), "seq", None),
        P(),
        P(),
        P(),
        P(),
        P(),
        P(("groups", "dp"), "seq", None),
    )
    return jax.shard_map(
        on_device,
        mesh=mesh,
        in_specs=placed,
        out_specs=(
            P(("groups", "dp"), "seq", None),
            P(("groups", "dp"), "seq", None),
            P(("groups", "seq", "dp"), None),
            P(("groups", "seq", "dp"), None),
            P(("groups", "seq", "dp"), None),
            P(("groups", "seq", "dp"), None),
            P(("groups", "seq", "dp")),
        ),
        check_vma=False,
    )
```

time: 523 us -> 116 us (0.22)
  waiting for transfers between devices: 335 us -> 34.3 us
  blocking collectives: 91.2 us -> 0 us
  matrix products: 44.4 us -> 0 us
  starting transfers between devices: 12.4 us -> 55.1 us
  Pallas kernels: 0 us -> 19.1 us
  between operations: 15.2 us -> 0.84 us
  local copies, waits for them, and re-layouts: 18.4 us -> 6.24 us
  other arithmetic: 5.4 us -> 0 us
    reduce_scatter x6 -> x0, waiting for transfers between devices: 334 us -> none  [the longest x1 86.1 us: on_device(): lax.psum_scatter(conv_term, ('seq', 'dp'), scatter_dimension=0, tiled=True)]
    all_gather x2 -> x0, blocking collectives: 61.7 us -> none  [the longest x1 33.3 us: on_device(): lax.all_gather(keys, 'seq', axis=1, tiled=True)]
    dot_general x38 -> x0, matrix products: 44.4 us -> none  [the longest x5 8.08 us: on_device(): jnp.einsum('spd,cd->spc', padded_cot[:, 4 - offset:4 - offset + position_...]
    ppermute x4 -> x29, starting transfers between devices: 12 us -> 55.1 us  [the longest x26 48.2 us: swap(): lax.ppermute(value, both_axes, [(i, i ^ mask) for i in range(owners)])]
    ppermute x4 -> x29, waiting for transfers between devices: 0.01 us -> 34.3 us  [the longest x26 32 us: swap(): lax.ppermute(value, both_axes, [(i, i ^ mask) for i in range(owners)])]
    unnamed x1 -> x0, blocking collectives: 29.5 us -> none
    pallas_call x0 -> x12, Pallas kernels: none -> 19.1 us  [run(): pl.pallas_call(body, out_shape=[jax.ShapeDtypeStruct(s, t) for s, t in ou...]
    reshape x4 -> x1, local copies, waits for them, and re-layouts: 6.14 us -> 0.69 us  [on_device(): gain = norm_gain.reshape(1, width)]
  transfers between devices with their start and end apart: 10 -> 29, of which waited for: 5 -> 11; matrix products, arithmetic and copies ran while one was open for 6% -> 2% of each run, Pallas kernels for 0% -> 8%
where the time goes in v1:
time: 116 us; the launch traced here: 115 us
  starting transfers between devices  55.1 us (48%)
  waiting for transfers between devices  34.3 us (30%)
  Pallas kernels  19.1 us (16%)
  local copies, waits for them, and re-layouts  6.24 us (5%)
    ppermute x26, starting transfers between devices, swap(): lax.ppermute(value, both_axes, [(i, i ^ mask) for i in range(owners)])  48.2 us
    ppermute x26, waiting for transfers between devices, swap(): lax.ppermute(value, both_axes, [(i, i ^ mask) for i in range(owners)])  32 us
    pallas_call x12, Pallas kernels, run(): pl.pallas_call(body, out_shape=[jax.ShapeDtypeStruct(s, t) for s, t in ou...  19.1 us
    ppermute x1, starting transfers between devices, on_device(): before = lax.ppermute(x[positions - 2:], 'seq', up)  4.86 us
    unnamed x15, local copies, waits for them, and re-layouts  4.83 us
    ppermute x1, waiting for transfers between devices, on_device(): after = lax.ppermute(x[:2], 'seq', down)  2.34 us
  transfers between devices with their start and end apart: 29, of which 11 were waited for; matrix products, arithmetic and copies ran while one was open for 2% of the time, Pallas kernels for 8%

profile of v1, /device:TPU:0, one launch (start us, length us, event | category | flops | bytes accessed | tf_op | source)
XLA Modules:
  0.0 115.5 jit_solution(13833557045171781729)
XLA Ops:
  1.3 4.9 %collective-permute-start = (bf16[2,384]{1,0:T(2,128)(2,1)S(1)}, bf16[2,384]{1,0:T(2,128)(2,1)S(1)}, u32[]{:S(2)}, u32[]{:S(2)}) collective-permute-start(bf16[2,384]{1,0:T(2,128)(2,1)S(1)} %get-tuple-element.62), channel_id=1, source_target_pairs={{0,2},{2,4},{4,6},{6,8},{8,10},{10,12},{12,14},{1,3},{3,5},{5,7},{... | collective-permute-start | bytes 4616 | tf_op jit(solution)/shard_map/ppermute | solution.py:381
  6.2 1.3 %collective-permute-start.1 = (bf16[2,384]{1,0:T(2,128)(2,1)S(1)}, bf16[2,384]{1,0:T(2,128)(2,1)S(1)}, u32[]{:S(2)}, u32[]{:S(2)}) collective-permute-start(bf16[2,384]{1,0:T(2,128)(2,1)S(1)} %get-tuple-element.61), channel_id=1, source_target_pairs={{2,0},{4,2},{6,4},{8,6},{10,8},{12,10},{14,12},{3,1},{5,3},{7,5},{... | collective-permute-start | bytes 4616 | tf_op jit(solution)/shard_map/ppermute | solution.py:382
  8.2 1.1 copy.14.wv.refs_8_
  9.4 2.3 %collective-permute-done.1.after = bf16[2,384]{1,0:T(2,128)(2,1)S(1)} collective-permute-done((bf16[2,384]{1,0:T(2,128)(2,1)S(1)}, bf16[2,384]{1,0:T(2,128)(2,1)S(1)}, u32[]{:S(2)}, u32[]{:S(2)}) %collective-permute-start.1) | collective-permute-done | bytes 1568 | tf_op jit(solution)/shard_map/ppermute | solution.py:382
  11.7 1.8 %copy-done = bf16[5,384,768]{2,1,0:T(8,128)(2,1)S(1)} copy-done((bf16[5,384,768]{2,1,0:T(8,128)(2,1)S(1)}, bf16[5,384,768]{2,1,0:T(8,128)(2,1)}, u32[]{:S(2)}) %copy-start) | copy-done | bytes 2949144
  13.5 0.9 copy-done.3
  14.5 0.9 copy-done.5
  15.4 1.9 %front.1 = (bf16[320,128]{1,0:T(8,128)(2,1)S(1)}, bf16[544,384]{1,0:T(8,128)(2,1)S(1)}, f32[128,768]{1,0:T(8,128)S(1)}) custom-call(bf16[256,384]{1,0:T(8,128)(2,1)S(1)} %bitcast.9, bf16[2,384]{1,0:T(2,128)(2,1)S(1)} %collective-permute-done.before, bf16[2,384]{1,0:T(2,128)(2,1)S(1)} %collective-permute-done.1.after, bf16[5,384,768]{2,1,0:T(8,128)(2,1)S(1)} %copy-done, ...), custom_call_target="tpu_custom_call" | custom-call | flops 754974720 | bytes 4536320 | tf_op jit(solution)/shard_map/front/pallas_call | solution.py:30
  17.2 1.6 %collective-permute-start.2 = (bf16[320,128]{1,0:T(8,128)(2,1)S(1)}, bf16[320,128]{1,0:T(8,128)(2,1)S(1)}, u32[]{:S(2)}, u32[]{:S(2)}) collective-permute-start(bf16[320,128]{1,0:T(8,128)(2,1)S(1)} %get-tuple-element.35.refs_2_), channel_id=1, source_target_pairs={{0,4},{1,5},{2,6},{3,7},{4,0},{5,1},{6,2},{7,3},{8,12},{9,13},{10,... | collective-permute-start | bytes 245768 | tf_op jit(solution)/shard_map/ppermute | solution.py:372
  18.9 2.6 %collective-permute-start.3 = (bf16[320,128]{1,0:T(8,128)(2,1)S(1)}, bf16[320,128]{1,0:T(8,128)(2,1)S(1)}, u32[]{:S(2)}, u32[]{:S(2)}) collective-permute-start(bf16[320,128]{1,0:T(8,128)(2,1)S(1)} %get-tuple-element.35.refs_2_), channel_id=1, source_target_pairs={{0,8},{1,9},{2,10},{3,11},{4,12},{5,13},{6,14},{7,15},{8,0},{9,1},... | collective-permute-start | bytes 245768 | tf_op jit(solution)/shard_map/ppermute | solution.py:372
  21.7 2.4 %collective-permute-start.5 = (bf16[320,128]{1,0:T(8,128)(2,1)S(1)}, bf16[320,128]{1,0:T(8,128)(2,1)S(1)}, u32[]{:S(2)}, u32[]{:S(2)}) collective-permute-start(bf16[320,128]{1,0:T(8,128)(2,1)S(1)} %get-tuple-element.35.refs_2_), channel_id=1, source_target_pairs={{0,2},{1,3},{2,0},{3,1},{4,6},{5,7},{6,4},{7,5},{8,10},{9,11},{10,... | collective-permute-start | bytes 245768 | tf_op jit(solution)/shard_map/ppermute | solution.py:372
  24.6 1.7 %collective-permute-done.3.refs_4_ = bf16[320,128]{1,0:T(8,128)(2,1)S(1)} collective-permute-done((bf16[320,128]{1,0:T(8,128)(2,1)S(1)}, bf16[320,128]{1,0:T(8,128)(2,1)S(1)}, u32[]{:S(2)}, u32[]{:S(2)}) %collective-permute-start.3) | collective-permute-done | bytes 81952 | tf_op jit(solution)/shard_map/ppermute | solution.py:372
  26.3 2.7 %collective-permute-start.7 = (bf16[320,128]{1,0:T(8,128)(2,1)S(1)}, bf16[320,128]{1,0:T(8,128)(2,1)S(1)}, u32[]{:S(2)}, u32[]{:S(2)}) collective-permute-start(bf16[320,128]{1,0:T(8,128)(2,1)S(1)} %collective-permute-done.3.refs_4_), channel_id=1, source_target_pairs={{0,2},{1,3},{2,0},{3,1},{4,6},{5,7},{6,4},{7,5},{8,10},{9,11},{10,... | collective-permute-start | bytes 245768 | tf_op jit(solution)/shard_map/ppermute | solution.py:372
  29.5 2.0 %collective-permute-done.7.refs_8_ = bf16[320,128]{1,0:T(8,128)(2,1)S(1)} collective-permute-done((bf16[320,128]{1,0:T(8,128)(2,1)S(1)}, bf16[320,128]{1,0:T(8,128)(2,1)S(1)}, u32[]{:S(2)}, u32[]{:S(2)}) %collective-permute-start.7) | collective-permute-done | bytes 81952 | tf_op jit(solution)/shard_map/ppermute | solution.py:372
  31.5 2.0 %collective-permute-done.8.refs_9_ = bf16[320,128]{1,0:T(8,128)(2,1)S(1)} collective-permute-done((bf16[320,128]{1,0:T(8,128)(2,1)S(1)}, bf16[320,128]{1,0:T(8,128)(2,1)S(1)}, u32[]{:S(2)}, u32[]{:S(2)}) %collective-permute-start.8) | collective-permute-done | bytes 81952 | tf_op jit(solution)/shard_map/ppermute | solution.py:372
  33.5 7.0 %attend.1 = (bf16[128,1536]{1,0:T(8,128)(2,1)}, bf16[128,1024]{1,0:T(8,128)(2,1)S(1)}, f32[4,320,128]{2,1,0:T(8,128)S(1)}, bf16[4,320,128]{2,1,0:T(8,128)(2,1)S(1)}) custom-call(bf16[128,1024]{1,0:T(8,128)(2,1)S(1)} %queries.1.refs_0_, bf16[128,1536]{1,0:T(8,128)(2,1)S(1)} %bitcast.11, bf16[320,128]{1,0:T(8,128)(2,1)S(1)} %get-tuple-element.35.refs_2_, ...), custom_call_target="tpu_custom_call" | custom-call | flops 2013265920 | bytes 2949120 | tf_op jit(solution)/shard_map/attend/pallas_call | solution.py:30
  41.4 1.2 collective-permute-start.16
  42.6 7.8 %collective-permute-done.9.far = bf16[4,320,128]{2,1,0:T(8,128)(2,1)S(1)} collective-permute-done((bf16[4,320,128]{2,1,0:T(8,128)(2,1)S(1)}, bf16[4,320,128]{2,1,0:T(8,128)(2,1)S(1)}, u32[]{:S(2)}, u32[]{:S(2)}) %collective-permute-start.9) | collective-permute-done | bytes 327712 | tf_op jit(solution)/shard_map/ppermute | solution.py:372
  50.9 2.9 %collective-permute-start.11 = (bf16[320,128]{1,0:T(8,128)(2,1)S(1)}, bf16[320,128]{1,0:T(8,128)(2,1)S(1)}, u32[]{:S(2)}, u32[]{:S(2)}) collective-permute-start(bf16[320,128]{1,0:T(8,128)(2,1)S(1)} %get-tuple-element.41), channel_id=1, source_target_pairs={{0,8},{1,9},{2,10},{3,11},{4,12},{5,13},{6,14},{7,15},{8,0},{9,1},... | collective-permute-start | bytes 245768 | tf_op jit(solution)/shard_map/ppermute | solution.py:372
  53.8 1.1 collective-permute-start.12
  56.3 3.8 %collective-permute-done.12.refs_3_ = bf16[320,128]{1,0:T(8,128)(2,1)S(1)} collective-permute-done((bf16[320,128]{1,0:T(8,128)(2,1)S(1)}, bf16[320,128]{1,0:T(8,128)(2,1)S(1)}, u32[]{:S(2)}, u32[]{:S(2)}) %collective-permute-start.12) | collective-permute-done | bytes 81952 | tf_op jit(solution)/shard_map/ppermute | solution.py:372
  60.5 1.4 %collective-permute-start.13 = (bf16[208,768]{1,0:T(8,128)(2,1)S(1)}, bf16[208,768]{1,0:T(8,128)(2,1)S(1)}, u32[]{:S(2)}, u32[]{:S(2)}) collective-permute-start(bf16[208,768]{1,0:T(8,128)(2,1)S(1)} %get-tuple-element.45.cc.refs_2_), channel_id=1, source_target_pairs={{0,2},{1,3},{2,0},{3,1},{4,6},{5,7},{6,4},{7,5},{8,10},{9,11},{10,... | collective-permute-start | bytes 958472 | tf_op jit(solution)/shard_map/ppermute | solution.py:372
  63.1 7.0 %collective-permute-done.13.pair_cc.refs_4_ = bf16[208,768]{1,0:T(8,128)(2,1)S(1)} collective-permute-done((bf16[208,768]{1,0:T(8,128)(2,1)S(1)}, bf16[208,768]{1,0:T(8,128)(2,1)S(1)}, u32[]{:S(2)}, u32[]{:S(2)}) %collective-permute-start.13) | collective-permute-done | bytes 319520 | tf_op jit(solution)/shard_map/ppermute | solution.py:372
  70.7 2.5 %collective-permute-done.24.refs_3_ = bf16[128,1024]{1,0:T(8,128)(2,1)S(1)} collective-permute-done((bf16[128,1024]{1,0:T(8,128)(2,1)S(1)}, bf16[128,1024]{1,0:T(8,128)(2,1)S(1)}, u32[]{:S(2)}, u32[]{:S(2)}) %collective-permute-start.24) | collective-permute-done | bytes 262176 | tf_op jit(solution)/shard_map/ppermute | solution.py:372
  73.2 2.9 %select.1 = (bf16[512,1024]{1,0:T(8,128)(2,1)S(1)}, bf16[192,512]{1,0:T(8,128)(2,1)S(1)}) custom-call(bf16[544,384]{1,0:T(8,128)(2,1)S(1)} %get-tuple-element.34.e.refs_0_, bf16[544,384]{1,0:T(8,128)(2,1)S(1)} %collective-permute-done.15.refs_1_, bf16[544,384]{1,0:T(8,128)(2,1)S(1)} %collective-permute-done.16.refs_2_, ...), custom_call_target="tpu_custom_call" | custom-call | flops 2013265920 | bytes 2916352 | tf_op jit(solution)/shard_map/select/pallas_call | solution.py:30
  76.1 1.2 %conv_grad.1 = (f32[160,768]{1,0:T(8,128)S(1)}, bf16[160,768]{1,0:T(8,128)(2,1)S(1)}, bf16[160,768]{1,0:T(8,128)(2,1)S(1)}, bf16[160,768]{1,0:T(8,128)(2,1)S(1)}) custom-call(bf16[512,1024]{1,0:T(8,128)(2,1)S(1)} %get-tuple-element.47.refs_0_, bf16[192,512]{1,0:T(8,128)(2,1)S(1)} %get-tuple-element.48.refs_1_.refs_0_, ...), custom_call_target="tpu_custom_call" | custom-call | flops 805306368 | bytes 3751936 | tf_op jit(solution)/shard_map/conv_grad/pallas_call | solution.py:30
  77.5 1.7 %collective-permute-start.21 = (bf16[160,768]{1,0:T(8,128)(2,1)S(1)}, bf16[160,768]{1,0:T(8,128)(2,1)S(1)}, u32[]{:S(2)}, u32[]{:S(2)}) collective-permute-start(bf16[160,768]{1,0:T(8,128)(2,1)S(1)} %get-tuple-element.51), channel_id=1, source_target_pairs={{0,8},{1,9},{2,10},{3,11},{4,12},{5,13},{6,14},{7,15},{8,0},{9,1},... | collective-permute-start | bytes 737288 | tf_op jit(solution)/shard_map/ppermute | solution.py:372
  79.2 2.6 %collective-permute-start.22 = (bf16[160,768]{1,0:T(8,128)(2,1)S(1)}, bf16[160,768]{1,0:T(8,128)(2,1)S(1)}, u32[]{:S(2)}, u32[]{:S(2)}) collective-permute-start(bf16[160,768]{1,0:T(8,128)(2,1)S(1)} %get-tuple-element.52), channel_id=1, source_target_pairs={{0,12},{1,13},{2,14},{3,15},{4,8},{5,9},{6,10},{7,11},{8,4},{9,5},... | collective-permute-start | bytes 737288 | tf_op jit(solution)/shard_map/ppermute | solution.py:372
  83.4 24.0 %collective-permute-start.27 = (bf16[48,1024]{1,0:T(8,128)(2,1)S(1)}, bf16[48,1024]{1,0:T(8,128)(2,1)S(1)}, u32[]{:S(2)}, u32[]{:S(2)}) collective-permute-start(bf16[48,1024]{1,0:T(8,128)(2,1)S(1)} %get-tuple-element.56), channel_id=1, source_target_pairs={{0,8},{1,9},{2,10},{3,11},{4,12},{5,13},{6,14},{7,15},{8,0},{9,1},... | collective-permute-start | bytes 294920 | tf_op jit(solution)/shard_map/ppermute | solution.py:372
  107.5 2.0 %input_grad.1 = bf16[256,384]{1,0:T(8,128)(2,1)} custom-call(bf16[256,384]{1,0:T(8,128)(2,1)S(1)} %bitcast.10, bf16[208,768]{1,0:T(8,128)(2,1)S(1)} %get-tuple-element.45.cc.refs_2_, bf16[208,768]{1,0:T(8,128)(2,1)S(1)} %collective-permute-done.13.pair_cc.refs_4_, bf16[16,768]{1,0:T(8,128)(2,1)S(1)} %collective-permute-done.14.edge, ...), custom_call_target="tpu_custom_call" | custom-call | flops 754974720 | bytes 4005888 | tf_op jit(solution)/shard_map/input_grad/pallas_call | solution.py:30
  110.1 3.8 %collective-permute-done.28.refs_3_ = bf16[48,1024]{1,0:T(8,128)(2,1)S(1)} collective-permute-done((bf16[48,1024]{1,0:T(8,128)(2,1)S(1)}, bf16[48,1024]{1,0:T(8,128)(2,1)S(1)}, u32[]{:S(2)}, u32[]{:S(2)}) %collective-permute-start.28) | collective-permute-done | bytes 98336 | tf_op jit(solution)/shard_map/ppermute | solution.py:372
  114.6 0.9 conv_sum.1
  (55 shorter events, 10.4 us)
Async XLA Ops:
  1.3 8.0 %collective-permute-start = (bf16[2,384]{1,0:T(2,128)(2,1)S(1)}, bf16[2,384]{1,0:T(2,128)(2,1)S(1)}, u32[]{:S(2)}, u32[]{:S(2)}) collective-permute-start(bf16[2,384]{1,0:T(2,128)(2,1)S(1)} %get-tuple-element.62), channel_id=1, source_target_pairs={{0,2},{2,4},{4,6},{6,8},{8,10},{10,12},{12,14},{1,3},{3,5},{5,7},{... | collective-permute-start | bytes 4616 | tf_op jit(solution)/shard_map/ppermute | solution.py:381
  6.2 5.5 %collective-permute-start.1 = (bf16[2,384]{1,0:T(2,128)(2,1)S(1)}, bf16[2,384]{1,0:T(2,128)(2,1)S(1)}, u32[]{:S(2)}, u32[]{:S(2)}) collective-permute-start(bf16[2,384]{1,0:T(2,128)(2,1)S(1)} %get-tuple-element.61), channel_id=1, source_target_pairs={{2,0},{4,2},{6,4},{8,6},{10,8},{12,10},{14,12},{3,1},{5,3},{7,5},{... | collective-permute-start | bytes 4616 | tf_op jit(solution)/shard_map/ppermute | solution.py:382
  15.4 18.1 %copy-start.6 = (bf16[1,128,1536]{2,1,0:T(8,128)(2,1)S(1)}, bf16[1,128,1536]{2,1,0:T(8,128)(2,1)}, u32[]{:S(2)}) copy-start(bf16[1,128,1536]{2,1,0:T(8,128)(2,1)} %param.13) | copy-start | bytes 1179652
  17.2 6.9 %collective-permute-start.2 = (bf16[320,128]{1,0:T(8,128)(2,1)S(1)}, bf16[320,128]{1,0:T(8,128)(2,1)S(1)}, u32[]{:S(2)}, u32[]{:S(2)}) collective-permute-start(bf16[320,128]{1,0:T(8,128)(2,1)S(1)} %get-tuple-element.35.refs_2_), channel_id=1, source_target_pairs={{0,4},{1,5},{2,6},{3,7},{4,0},{5,1},{6,2},{7,3},{8,12},{9,13},{10,... | collective-permute-start | bytes 245768 | tf_op jit(solution)/shard_map/ppermute | solution.py:372
  18.9 7.5 %collective-permute-start.3 = (bf16[320,128]{1,0:T(8,128)(2,1)S(1)}, bf16[320,128]{1,0:T(8,128)(2,1)S(1)}, u32[]{:S(2)}, u32[]{:S(2)}) collective-permute-start(bf16[320,128]{1,0:T(8,128)(2,1)S(1)} %get-tuple-element.35.refs_2_), channel_id=1, source_target_pairs={{0,8},{1,9},{2,10},{3,11},{4,12},{5,13},{6,14},{7,15},{8,0},{9,1},... | collective-permute-start | bytes 245768 | tf_op jit(solution)/shard_map/ppermute | solution.py:372
  21.5 7.6 %collective-permute-start.4 = (bf16[320,128]{1,0:T(8,128)(2,1)S(1)}, bf16[320,128]{1,0:T(8,128)(2,1)S(1)}, u32[]{:S(2)}, u32[]{:S(2)}) collective-permute-start(bf16[320,128]{1,0:T(8,128)(2,1)S(1)} %get-tuple-element.35.refs_2_), channel_id=1, source_target_pairs={{0,12},{1,13},{2,14},{3,15},{4,8},{5,9},{6,10},{7,11},{8,4},{9,5},... | collective-permute-start | bytes 245768 | tf_op jit(solution)/shard_map/ppermute | solution.py:372
  21.7 7.8 %collective-permute-start.5 = (bf16[320,128]{1,0:T(8,128)(2,1)S(1)}, bf16[320,128]{1,0:T(8,128)(2,1)S(1)}, u32[]{:S(2)}, u32[]{:S(2)}) collective-permute-start(bf16[320,128]{1,0:T(8,128)(2,1)S(1)} %get-tuple-element.35.refs_2_), channel_id=1, source_target_pairs={{0,2},{1,3},{2,0},{3,1},{4,6},{5,7},{6,4},{7,5},{8,10},{9,11},{10,... | collective-permute-start | bytes 245768 | tf_op jit(solution)/shard_map/ppermute | solution.py:372
  24.1 5.4 %collective-permute-start.6 = (bf16[320,128]{1,0:T(8,128)(2,1)S(1)}, bf16[320,128]{1,0:T(8,128)(2,1)S(1)}, u32[]{:S(2)}, u32[]{:S(2)}) collective-permute-start(bf16[320,128]{1,0:T(8,128)(2,1)S(1)} %collective-permute-done.2.refs_3_), channel_id=1, source_target_pairs={{0,2},{1,3},{2,0},{3,1},{4,6},{5,7},{6,4},{7,5},{8,10},{9,11},{10,... | collective-permute-start | bytes 245768 | tf_op jit(solution)/shard_map/ppermute | solution.py:372
  26.3 5.1 %collective-permute-start.7 = (bf16[320,128]{1,0:T(8,128)(2,1)S(1)}, bf16[320,128]{1,0:T(8,128)(2,1)S(1)}, u32[]{:S(2)}, u32[]{:S(2)}) collective-permute-start(bf16[320,128]{1,0:T(8,128)(2,1)S(1)} %collective-permute-done.3.refs_4_), channel_id=1, source_target_pairs={{0,2},{1,3},{2,0},{3,1},{4,6},{5,7},{6,4},{7,5},{8,10},{9,11},{10,... | collective-permute-start | bytes 245768 | tf_op jit(solution)/shard_map/ppermute | solution.py:372
  29.1 4.4 %collective-permute-start.8 = (bf16[320,128]{1,0:T(8,128)(2,1)S(1)}, bf16[320,128]{1,0:T(8,128)(2,1)S(1)}, u32[]{:S(2)}, u32[]{:S(2)}) collective-permute-start(bf16[320,128]{1,0:T(8,128)(2,1)S(1)} %collective-permute-done.4.refs_5_), channel_id=1, source_target_pairs={{0,2},{1,3},{2,0},{3,1},{4,6},{5,7},{6,4},{7,5},{8,10},{9,11},{10,... | collective-permute-start | bytes 245768 | tf_op jit(solution)/shard_map/ppermute | solution.py:372
  40.6 9.9 %collective-permute-start.9 = (bf16[4,320,128]{2,1,0:T(8,128)(2,1)S(1)}, bf16[4,320,128]{2,1,0:T(8,128)(2,1)S(1)}, u32[]{:S(2)}, u32[]{:S(2)}) collective-permute-start(bf16[4,320,128]{2,1,0:T(8,128)(2,1)S(1)} %get-tuple-element.38), channel_id=1, source_target_pairs={{0,2},{1,3},{2,0},{3,1},{4,6},{5,7},{6,4},{7,5},{8,10},{9,11},{10,... | collective-permute-start | bytes 983048 | tf_op jit(solution)/shard_map/ppermute | solution.py:372
  41.4 20.5 %collective-permute-start.16 = (bf16[544,384]{1,0:T(8,128)(2,1)S(1)}, bf16[544,384]{1,0:T(8,128)(2,1)S(1)}, u32[]{:S(2)}, u32[]{:S(2)}) collective-permute-start(bf16[544,384]{1,0:T(8,128)(2,1)S(1)} %get-tuple-element.34.e.refs_0_), channel_id=1, source_target_pairs={{0,2},{1,3},{2,0},{3,1},{4,6},{5,7},{6,4},{7,5},{8,10},{9,11},{10,... | collective-permute-start | bytes 1253384 | tf_op jit(solution)/shard_map/ppermute | solution.py:372
  50.5 5.1 %collective-permute-start.10 = (bf16[320,128]{1,0:T(8,128)(2,1)S(1)}, bf16[320,128]{1,0:T(8,128)(2,1)S(1)}, u32[]{:S(2)}, u32[]{:S(2)}) collective-permute-start(bf16[320,128]{1,0:T(8,128)(2,1)S(1)} %get-tuple-element.40), channel_id=1, source_target_pairs={{0,4},{1,5},{2,6},{3,7},{4,0},{5,1},{6,2},{7,3},{8,12},{9,13},{10,... | collective-permute-start | bytes 245768 | tf_op jit(solution)/shard_map/ppermute | solution.py:372
  50.9 5.3 %collective-permute-start.11 = (bf16[320,128]{1,0:T(8,128)(2,1)S(1)}, bf16[320,128]{1,0:T(8,128)(2,1)S(1)}, u32[]{:S(2)}, u32[]{:S(2)}) collective-permute-start(bf16[320,128]{1,0:T(8,128)(2,1)S(1)} %get-tuple-element.41), channel_id=1, source_target_pairs={{0,8},{1,9},{2,10},{3,11},{4,12},{5,13},{6,14},{7,15},{8,0},{9,1},... | collective-permute-start | bytes 245768 | tf_op jit(solution)/shard_map/ppermute | solution.py:372
  53.8 6.2 %collective-permute-start.12 = (bf16[320,128]{1,0:T(8,128)(2,1)S(1)}, bf16[320,128]{1,0:T(8,128)(2,1)S(1)}, u32[]{:S(2)}, u32[]{:S(2)}) collective-permute-start(bf16[320,128]{1,0:T(8,128)(2,1)S(1)} %get-tuple-element.42), channel_id=1, source_target_pairs={{0,12},{1,13},{2,14},{3,15},{4,8},{5,9},{6,10},{7,11},{8,4},{9,5},... | collective-permute-start | bytes 245768 | tf_op jit(solution)/shard_map/ppermute | solution.py:372
  60.5 9.7 %collective-permute-start.13 = (bf16[208,768]{1,0:T(8,128)(2,1)S(1)}, bf16[208,768]{1,0:T(8,128)(2,1)S(1)}, u32[]{:S(2)}, u32[]{:S(2)}) collective-permute-start(bf16[208,768]{1,0:T(8,128)(2,1)S(1)} %get-tuple-element.45.cc.refs_2_), channel_id=1, source_target_pairs={{0,2},{1,3},{2,0},{3,1},{4,6},{5,7},{6,4},{7,5},{8,10},{9,11},{10,... | collective-permute-start | bytes 958472 | tf_op jit(solution)/shard_map/ppermute | solution.py:372
  61.9 8.3 %collective-permute-start.15 = (bf16[544,384]{1,0:T(8,128)(2,1)S(1)}, bf16[544,384]{1,0:T(8,128)(2,1)S(1)}, u32[]{:S(2)}, u32[]{:S(2)}) collective-permute-start(bf16[544,384]{1,0:T(8,128)(2,1)S(1)} %get-tuple-element.34.e.refs_0_), channel_id=1, source_target_pairs={{0,1},{1,0},{2,3},{3,2},{4,5},{5,4},{6,7},{7,6},{8,9},{9,8},{10,11... | collective-permute-start | bytes 1253384 | tf_op jit(solution)/shard_map/ppermute | solution.py:372
  61.9 11.3 %collective-permute-start.17 = (bf16[544,384]{1,0:T(8,128)(2,1)S(1)}, bf16[544,384]{1,0:T(8,128)(2,1)S(1)}, u32[]{:S(2)}, u32[]{:S(2)}) collective-permute-start(bf16[544,384]{1,0:T(8,128)(2,1)S(1)} %collective-permute-done.16.refs_2_), channel_id=1, source_target_pairs={{0,1},{1,0},{2,3},{3,2},{4,5},{5,4},{6,7},{7,6},{8,9},{9,8},{10,11... | collective-permute-start | bytes 1253384 | tf_op jit(solution)/shard_map/ppermute | solution.py:372
  62.4 10.8 %collective-permute-start.24 = (bf16[128,1024]{1,0:T(8,128)(2,1)S(1)}, bf16[128,1024]{1,0:T(8,128)(2,1)S(1)}, u32[]{:S(2)}, u32[]{:S(2)}) collective-permute-start(bf16[128,1024]{1,0:T(8,128)(2,1)S(1)} %get-tuple-element.43.dq.refs_1_), channel_id=1, source_target_pairs={{0,2},{1,3},{2,0},{3,1},{4,6},{5,7},{6,4},{7,5},{8,10},{9,11},{10,... | collective-permute-start | bytes 786440 | tf_op jit(solution)/shard_map/ppermute | solution.py:372
  63.1 13.0 %collective-permute-start.18 = (bf16[208,768]{1,0:T(8,128)(2,1)S(1)}, bf16[208,768]{1,0:T(8,128)(2,1)S(1)}, u32[]{:S(2)}, u32[]{:S(2)}) collective-permute-start(bf16[208,768]{1,0:T(8,128)(2,1)S(1)} %get-tuple-element.45.cc.refs_2_), channel_id=1, source_target_pairs={{0,1},{1,0},{2,3},{3,2},{4,5},{5,4},{6,7},{7,6},{8,9},{9,8},{10,11... | collective-permute-start | bytes 958472 | tf_op jit(solution)/shard_map/ppermute | solution.py:372
  70.2 6.0 %collective-permute-start.19 = (bf16[208,768]{1,0:T(8,128)(2,1)S(1)}, bf16[208,768]{1,0:T(8,128)(2,1)S(1)}, u32[]{:S(2)}, u32[]{:S(2)}) collective-permute-start(bf16[208,768]{1,0:T(8,128)(2,1)S(1)} %collective-permute-done.13.pair_cc.refs_4_), channel_id=1, source_target_pairs={{0,1},{1,0},{2,3},{3,2},{4,5},{5,4},{6,7},{7,6},{8,9},{9,8},{10,11... | collective-permute-start | bytes 958472 | tf_op jit(solution)/shard_map/ppermute | solution.py:372
  70.2 11.7 %collective-permute-start.23 = (bf16[128,1024]{1,0:T(8,128)(2,1)S(1)}, bf16[128,1024]{1,0:T(8,128)(2,1)S(1)}, u32[]{:S(2)}, u32[]{:S(2)}) collective-permute-start(bf16[128,1024]{1,0:T(8,128)(2,1)S(1)} %get-tuple-element.43.dq.refs_1_), channel_id=1, source_target_pairs={{0,1},{1,0},{2,3},{3,2},{4,5},{5,4},{6,7},{7,6},{8,9},{9,8},{10,11... | collective-permute-start | bytes 786440 | tf_op jit(solution)/shard_map/ppermute | solution.py:372
  73.2 8.7 %collective-permute-start.25 = (bf16[128,1024]{1,0:T(8,128)(2,1)S(1)}, bf16[128,1024]{1,0:T(8,128)(2,1)S(1)}, u32[]{:S(2)}, u32[]{:S(2)}) collective-permute-start(bf16[128,1024]{1,0:T(8,128)(2,1)S(1)} %collective-permute-done.24.refs_3_), channel_id=1, source_target_pairs={{0,1},{1,0},{2,3},{3,2},{4,5},{5,4},{6,7},{7,6},{8,9},{9,8},{10,11... | collective-permute-start | bytes 786440 | tf_op jit(solution)/shard_map/ppermute | solution.py:372
  76.1 31.4 %copy-start.1 = (bf16[5,384,768]{2,1,0:T(8,128)(2,1)S(1)}, bf16[5,384,768]{2,1,0:T(8,128)(2,1)}, u32[]{:S(2)}) copy-start(bf16[5,384,768]{2,1,0:T(8,128)(2,1)} %weight.3) | copy-start | bytes 8847364
  76.1 31.4 %copy-start.4 = (bf16[1,256,384]{2,1,0:T(8,128)(2,1)S(1)}, bf16[1,256,384]{2,1,0:T(8,128)(2,1)}, u32[]{:S(2)}) copy-start(bf16[1,256,384]{2,1,0:T(8,128)(2,1)} %param.7) | copy-start | bytes 589828
  77.4 37.2 %collective-permute-start.20 = (bf16[160,768]{1,0:T(8,128)(2,1)S(1)}, bf16[160,768]{1,0:T(8,128)(2,1)S(1)}, u32[]{:S(2)}, u32[]{:S(2)}) collective-permute-start(bf16[160,768]{1,0:T(8,128)(2,1)S(1)} %get-tuple-element.50), channel_id=1, source_target_pairs={{0,4},{1,5},{2,6},{3,7},{4,0},{5,1},{6,2},{7,3},{8,12},{9,13},{10,... | collective-permute-start | bytes 737288 | tf_op jit(solution)/shard_map/ppermute | solution.py:372
  77.5 37.1 %collective-permute-start.21 = (bf16[160,768]{1,0:T(8,128)(2,1)S(1)}, bf16[160,768]{1,0:T(8,128)(2,1)S(1)}, u32[]{:S(2)}, u32[]{:S(2)}) collective-permute-start(bf16[160,768]{1,0:T(8,128)(2,1)S(1)} %get-tuple-element.51), channel_id=1, source_target_pairs={{0,8},{1,9},{2,10},{3,11},{4,12},{5,13},{6,14},{7,15},{8,0},{9,1},... | collective-permute-start | bytes 737288 | tf_op jit(solution)/shard_map/ppermute | solution.py:372
  79.2 35.4 %collective-permute-start.22 = (bf16[160,768]{1,0:T(8,128)(2,1)S(1)}, bf16[160,768]{1,0:T(8,128)(2,1)S(1)}, u32[]{:S(2)}, u32[]{:S(2)}) collective-permute-start(bf16[160,768]{1,0:T(8,128)(2,1)S(1)} %get-tuple-element.52), channel_id=1, source_target_pairs={{0,12},{1,13},{2,14},{3,15},{4,8},{5,9},{6,10},{7,11},{8,4},{9,5},... | collective-permute-start | bytes 737288 | tf_op jit(solution)/shard_map/ppermute | solution.py:372
  82.7 24.8 %collective-permute-start.26 = (bf16[48,1024]{1,0:T(8,128)(2,1)S(1)}, bf16[48,1024]{1,0:T(8,128)(2,1)S(1)}, u32[]{:S(2)}, u32[]{:S(2)}) collective-permute-start(bf16[48,1024]{1,0:T(8,128)(2,1)S(1)} %get-tuple-element.55), channel_id=1, source_target_pairs={{0,4},{1,5},{2,6},{3,7},{4,0},{5,1},{6,2},{7,3},{8,12},{9,13},{10,... | collective-permute-start | bytes 294920 | tf_op jit(solution)/shard_map/ppermute | solution.py:372
  82.8 0.7 collective-permute-start.14
  83.4 26.7 %collective-permute-start.27 = (bf16[48,1024]{1,0:T(8,128)(2,1)S(1)}, bf16[48,1024]{1,0:T(8,128)(2,1)S(1)}, u32[]{:S(2)}, u32[]{:S(2)}) collective-permute-start(bf16[48,1024]{1,0:T(8,128)(2,1)S(1)} %get-tuple-element.56), channel_id=1, source_target_pairs={{0,8},{1,9},{2,10},{3,11},{4,12},{5,13},{6,14},{7,15},{8,0},{9,1},... | collective-permute-start | bytes 294920 | tf_op jit(solution)/shard_map/ppermute | solution.py:372
  107.5 6.4 %collective-permute-start.28 = (bf16[48,1024]{1,0:T(8,128)(2,1)S(1)}, bf16[48,1024]{1,0:T(8,128)(2,1)S(1)}, u32[]{:S(2)}, u32[]{:S(2)}) collective-permute-start(bf16[48,1024]{1,0:T(8,128)(2,1)S(1)} %get-tuple-element.57), channel_id=1, source_target_pairs={{0,12},{1,13},{2,14},{3,15},{4,8},{5,9},{6,10},{7,11},{8,4},{9,5},... | collective-permute-start | bytes 294920 | tf_op jit(solution)/shard_map/ppermute | solution.py:372
  (4 other events, 17.4 us)

commit v2 on v1

v2 whole, which is shorter than its diff:
```python
import math

import jax
import jax.numpy as jnp
from jax import lax
from jax.experimental import pallas as pl
from jax.experimental.pallas import tpu as pltpu
from jax.sharding import PartitionSpec as P

BF = jnp.bfloat16
F32 = jnp.float32
ROOT = math.sqrt(2.0 / math.pi)
EPS = 1e-06
LANES = 128
VMEM_BYTES = 40 * 2**20


def dot(a, b):
    return lax.dot_general(a, b, (((1,), (0,)), ((), ())), preferred_element_type=F32)


def dot_t(a, b):
    return lax.dot_general(a, b, (((1,), (1,)), ((), ())), preferred_element_type=F32)


def run(body, outs, args, scratch=(), flops=0, name=None, after=()):
    size = sum(math.prod(a.shape) * a.dtype.itemsize for a in args)
    size += sum(math.prod(s) * jnp.dtype(t).itemsize for s, t in outs)
    vmem = pl.BlockSpec(memory_space=pltpu.VMEM)
    rest = pl.BlockSpec(memory_space=pl.ANY)
    count, skip = len(args), len(args) + len(after)

    def whole(*refs):
        body(*refs[:count], *refs[skip:])

    return pl.pallas_call(
        whole,
        out_shape=[jax.ShapeDtypeStruct(s, t) for s, t in outs],
        in_specs=[vmem] * count + [rest] * len(after),
        out_specs=[vmem] * len(outs),
        scratch_shapes=list(scratch),
        compiler_params=pltpu.CompilerParams(vmem_limit_bytes=VMEM_BYTES),
        cost_estimate=pl.CostEstimate(flops=flops, bytes_accessed=size, transcendentals=0),
        name=name,
    )(*args, *after)


def gelu(v):
    return v * (0.5 * (1.0 + jnp.tanh(ROOT * (v + 0.044715 * (v * v * v)))))


def gelu_slope(v):
    tangent = jnp.tanh(ROOT * (v + 0.044715 * v * v * v))
    return 0.5 * (1.0 + tangent) + 0.5 * v * (1.0 - tangent * tangent) * ROOT * (
        1.0 + 3.0 * 0.044715 * v * v
    )


def round_up(value, step):
    return -(-value // step) * step


def pack_kv(keys, values):
    tokens, size = keys.shape
    rest = values[:, size:]
    half = tokens // 2
    tail = jnp.concatenate([rest[:half], rest[half:]], axis=1)
    return jnp.concatenate([keys, values[:, :size], tail], axis=0)


def unpack_values(packed, tokens, size):
    tail = packed[2 * tokens :]
    width = tail.shape[1] // 2
    rest = jnp.concatenate([tail[:, :width], tail[:, width:]], axis=0)
    return jnp.concatenate([packed[tokens : 2 * tokens], rest], axis=1)


def put(ref, start, rows):
    for c in range(ref.shape[0]):
        ref[c, start : start + rows.shape[0]] = rows[:, c * LANES : (c + 1) * LANES]


def every_second(ref, start, count):
    parts = [ref[c, pl.ds(start, count, stride=2)] for c in range(ref.shape[0])]
    return jnp.concatenate(parts, axis=1)


def prepare_kernel(x, pad):
    positions, channels = x.shape
    put(pad, 0, jnp.zeros((8, channels), F32))
    put(pad, 8, gelu(x[...].astype(F32)).astype(BF).astype(F32))
    put(pad, 8 + positions, jnp.zeros((pad.shape[1] - 8 - positions, channels), F32))


def front_kernel(ready, before, after, weight, gain, wk, wv, kv_out, early, normed_out, pooled_out, pad):
    channels = before.shape[1]
    tokens = pooled_out.shape[0]
    ext = early.shape[0] // 2
    pad[...] = ready[...]
    put(pad, 6, gelu(before[...].astype(F32)).astype(BF).astype(F32))
    put(pad, 8 + 2 * tokens, gelu(after[...].astype(F32)).astype(BF).astype(F32))
    pieces = [every_second(pad, 6 + u, tokens).astype(BF) for u in range(6)]
    total = None
    for tap in range(5):
        rows = jnp.concatenate([pieces[tap], pieces[tap + 1]], axis=0)
        term = dot(rows, weight[tap])
        total = term if total is None else total + term
    pooled = 0.5 * (total[:tokens] + total[tokens:])
    inv = lax.rsqrt(jnp.mean(pooled * pooled, axis=-1, keepdims=True) + EPS)
    normed = (pooled * inv * gain[...]).astype(BF)
    pooled_out[...] = pooled
    normed_out[...] = normed
    kv_out[...] = pack_kv(dot(normed, wk[...]), dot_t(normed, wv[...])).astype(BF)
    early[0:ext] = every_second(pad, 6, ext).astype(BF)
    early[ext : 2 * ext] = every_second(pad, 7, ext).astype(BF)


def query_kernel(normed, wq, early, out, early_out, *picks, groups, rows, padded, scale):
    width = normed.shape[1]
    value = normed[...]
    out[...] = (dot(value, wq[...]) * scale).astype(BF)
    for i in range(4):
        block_of = place(i)
        pick = [chosen(rows, padded, width, block_of(k)) for k in range(groups)]
        picks[i][...] = dot_t(jnp.concatenate(pick, axis=0), value).astype(BF)
    early_out[...] = early[...]


def attend_pair(index, q, cot, ks, vs, kt, vt, dk, dv, att, dq, key_size, value_size, scale, first):
    tokens = q.shape[0]
    ql, cl = 2 * index * key_size, 2 * index * value_size
    qs = jnp.concatenate(
        [q[:, ql : ql + key_size], q[:, ql + key_size : ql + 2 * key_size]], axis=0
    )
    both = cot[:, cl : cl + 2 * value_size]
    cs = jnp.concatenate([both[:, :value_size], both[:, value_size:]], axis=0)
    scores = dot_t(ks[...], qs)
    raised = jnp.exp(scores - jnp.max(scores, axis=0, keepdims=True))
    probs = raised * (1.0 / jnp.sum(raised, axis=0, keepdims=True))
    weights = probs.astype(BF)
    out_t = dot(vt[...], weights).astype(BF).astype(F32)
    delta = jnp.sum(cs.astype(F32).T * out_t, axis=0, keepdims=True)
    prob_cot = dot_t(vs[...], cs)
    score_cot = (probs * (prob_cot - delta)).astype(BF)
    dq_t = dot(kt[...], score_cot) * scale
    dk_term = dot(score_cot, qs)
    dv_term = dot(weights, cs)
    if first:
        dk[...] = dk_term
        dv[...] = dv_term
    else:
        dk[...] += dk_term
        dv[...] += dv_term
    out_rows = jnp.concatenate([out_t[:, :tokens].T, out_t[:, tokens:].T], axis=1)
    att[:, cl : cl + 2 * value_size] = out_rows.astype(BF)
    dq_rows = jnp.concatenate([dq_t[:, :tokens].T, dq_t[:, tokens:].T], axis=1)
    dq[:, ql % dq.shape[1] : ql % dq.shape[1] + 2 * key_size] = dq_rows.astype(BF)


def attend_first_kernel(*refs, blocks, heads, key_size, value_size, scale):
    q, cot = refs[:2]
    parts = refs[2 : 2 + blocks]
    att, dq, ks, vs, kt, vt, dk, dv = refs[2 + blocks :]
    tokens = q.shape[0]
    half = tokens // 2
    wide = value_size - key_size
    for i, part in enumerate(parts):
        at = i * tokens
        ks[at : at + tokens] = part[:tokens]
        vs[at : at + tokens, :key_size] = part[tokens : 2 * tokens]
        vs[at : at + half, key_size:] = part[2 * tokens :, :wide]
        vs[at + half : at + tokens, key_size:] = part[2 * tokens :, wide:]
        kt[:, at : at + tokens] = ks[at : at + tokens].astype(F32).T.astype(BF)
        vt[:, at : at + tokens] = vs[at : at + tokens].astype(F32).T.astype(BF)
    for pair in range(heads // 4):
        attend_pair(
            pair, q, cot, ks, vs, kt, vt, dk, dv, att, dq, key_size, value_size, scale, pair == 0
        )


def attend_second_kernel(*refs, blocks, heads, key_size, value_size, scale):
    q, cot, att_in, ks, vs, kt, vt, dk_in, dv_in = refs[:9]
    att, dq, near, far_first, far_last, dk, dv = refs[9:]
    tokens = q.shape[0]
    att[:, : att_in.shape[1]] = att_in[...]
    for pair in range(heads // 4, heads // 2):
        if pair == heads // 4:
            dk[...] = dk_in[...]
            dv[...] = dv_in[...]
        attend_pair(
            pair, q, cot, ks, vs, kt, vt, dk, dv, att, dq, key_size, value_size, scale, False
        )
    count = blocks // 2
    half = count // 2
    for i in range(blocks):
        at = slice(i * tokens, (i + 1) * tokens)
        packed = pack_kv(dk[at], dv[at])
        k = i - count
        if k < 0:
            near[i] = packed
        elif k < half:
            far_last[k] = packed.astype(BF)
        else:
            far_first[k - half] = packed.astype(BF)


def add_kernel(near, far, *outs, start):
    for k, out in enumerate(outs):
        out[...] = (near[start + k] + far[k].astype(F32)).astype(out.dtype)


def add_near_kernel(near, far, left, right, both, *outs):
    both[:, : left.shape[1]] = left[...]
    both[:, left.shape[1] :] = right[...]
    add_kernel(near, far, *outs, start=0)


def query_cot_kernel(dq, wq, out):
    out[...] = dot_t(dq[...], wq[...])


def make_middle(count):
    def middle(*refs):
        own, others = refs[0], refs[1:count]
        part, pooled_in, gain_in, wk, wv, message, edge = refs[count:]
        size = own.shape[1]
        tokens, width = pooled_in.shape
        total = own[...]
        for other in others:
            total = total + other[...].astype(F32)
        total = total.astype(BF).astype(F32)
        key_cot = total[:tokens]
        value_cot = unpack_values(total, tokens, size)
        normed_cot = part[...] + dot_t(key_cot.astype(BF), wk[...])
        normed_cot = normed_cot + dot(value_cot.astype(BF), wv[...])
        pooled, gain = pooled_in[...], gain_in[...]
        inv = lax.rsqrt(jnp.mean(pooled * pooled, axis=-1, keepdims=True) + EPS)
        gain_term = jnp.sum(normed_cot * pooled * inv, axis=0, keepdims=True)
        gained = gain * normed_cot
        pooled_cot = inv * gained - pooled * (inv * inv * inv) * (
            jnp.sum(gained * pooled, axis=-1, keepdims=True) / width
        )
        conv_cot = 0.5 * pooled_cot
        high = gain_term.astype(BF).astype(F32)
        low = gain_term - high
        row = lax.broadcasted_iota(jnp.int32, (16, width), 0)
        gains = jnp.where(row == 0, high, jnp.where(row == 1, low, 0.0))
        both = jnp.concatenate([key_cot, value_cot], axis=1)
        fill = width // 2 - both.shape[1]
        both = jnp.concatenate([both, jnp.zeros((tokens, fill), F32)], axis=1)
        side = jnp.concatenate([both[: tokens // 2], both[tokens // 2 :]], axis=1)
        message[:tokens] = conv_cot.astype(BF)
        message[tokens : tokens + 16] = gains.astype(BF)
        message[tokens + 16 :] = side.astype(BF)
        ends = jnp.where(row == 0, conv_cot[:1], jnp.where(row == 1, conv_cot[tokens - 1 :], 0.0))
        edge[...] = ends.astype(BF)

    return middle


def place(other=0):
    seq, dp = lax.axis_index("seq"), lax.axis_index("dp") ^ (other % 2)
    high, low = seq // 2, (seq % 2) ^ (other // 2)
    return lambda k: ((high ^ k) * 2 + low) * 2 + dp


def chosen(rows, padded, columns, block):
    row = lax.broadcasted_iota(jnp.int32, (padded, columns), 0)
    column = lax.broadcasted_iota(jnp.int32, (padded, columns), 1)
    hit = (column == row + block * rows) & (row < rows)
    return jnp.where(hit, 1.0, 0.0).astype(BF)


def relay_kernel(value, out):
    out[...] = value[...]


def select_kernel(*refs, groups, rows, padded):
    blocks = refs[:4]
    out, even, odd = refs[4:]
    ext, channels = even.shape
    tokens = out.shape[1] // 8
    block_of = place()
    pick = jnp.concatenate(
        [chosen(rows, padded, 5 * channels, block_of(k)) for k in range(groups)], axis=0
    )
    for i, block in enumerate(blocks):
        even[...] = block[:ext].astype(F32)
        odd[...] = block[ext : 2 * ext].astype(F32)
        pieces = []
        for shift in range(3):
            pieces += [even[shift : shift + tokens].astype(BF), odd[shift : shift + tokens].astype(BF)]
        shifted = jnp.concatenate(
            [jnp.concatenate(pieces[:5], axis=1), jnp.concatenate(pieces[1:], axis=1)], axis=0
        )
        out[:, 2 * i * tokens : 2 * (i + 1) * tokens] = dot_t(pick, shifted).astype(BF)


def query_grad_kernel(*refs, pad):
    picks, blocks = refs[:4], refs[4:8]
    outs, right = refs[8:-1], refs[-1]
    tokens = blocks[0].shape[0]
    for i, block in enumerate(blocks):
        right[i * tokens : (i + 1) * tokens] = block[...]
    pick = jnp.concatenate([part[...] for part in picks], axis=1)
    for k, out in enumerate(outs):
        out[...] = dot(pick[k * pad : (k + 1) * pad], right[...]).astype(out.dtype)


def query_sum_kernel(*refs):
    parts, out = refs[:-1], refs[-1]
    total = parts[0][...]
    for part in parts[1:]:
        total = total + part[...].astype(F32)
    out[...] = total[: out.shape[0]]


def chunk_layout(conv_rows, norm_rows, width, key_size, value_size):
    key_rows = norm_rows * key_size // width
    value_rows = norm_rows * value_size // width
    return conv_rows, conv_rows + key_rows, conv_rows + key_rows + value_rows


def conv_grad_kernel(*refs, conv_rows, conv_pad, norm_rows, norm_pad, key_size, value_size):
    pick, picks, blocks = refs[0], refs[1:5], refs[5:9]
    outs, right, side, stage = refs[9:-3], refs[-3], refs[-2], refs[-1]
    norm_pick = jnp.concatenate([part[...] for part in picks], axis=1)
    width = right.shape[1]
    tokens = side.shape[0] // 4
    half = tokens // 2
    gain = None
    for i, block in enumerate(blocks):
        piece = block[:tokens]
        right[2 * i * tokens : (2 * i + 1) * tokens] = piece
        right[(2 * i + 1) * tokens : (2 * i + 2) * tokens] = piece
        side[i * tokens : i * tokens + half] = block[tokens + 16 :, : width // 2]
        side[i * tokens + half : (i + 1) * tokens] = block[tokens + 16 :, width // 2 :]
        two = block[tokens : tokens + 16].astype(F32)
        term = two[0:1] + two[1:2]
        gain = term if gain is None else gain + term
    high = gain.astype(BF).astype(F32)
    key_at, value_at, gain_at = chunk_layout(conv_rows, norm_rows, width, key_size, value_size)
    stage[...] = jnp.zeros(stage.shape, F32)
    stage[gain_at : gain_at + 1] = high
    stage[gain_at + 1 : gain_at + 2] = gain - high
    for k, out in enumerate(outs):
        conv = dot(pick[k * conv_pad : (k + 1) * conv_pad], right[...])
        stage[:conv_rows] = conv[:conv_rows]
        both = dot(norm_pick[k * norm_pad : (k + 1) * norm_pad], side[...])
        key, value = both[:, :key_size], both[:, key_size : key_size + value_size]
        for part, at, end in ((key, key_at, value_at), (value, value_at, gain_at)):
            count = end - at
            pieces = [part[i : i + count] for i in range(0, norm_rows, count)]
            stage[at:end] = jnp.concatenate(pieces, axis=1)
        out[...] = stage[...].astype(out.dtype)


def final_kernel(*refs):
    parts = refs[:-5]
    conv, key, value, gain, stage = refs[-5:]
    total = parts[0][...]
    for part in parts[1:]:
        total = total + part[...].astype(F32)
    rows, width = conv.shape
    count = key.shape[0]
    stage[...] = total
    conv[...] = stage[:rows]
    key_at, value_at, gain_at = chunk_layout(
        rows, count, width, key.shape[1], value.shape[1]
    )
    for part, at, end in ((key, key_at, value_at), (value, value_at, gain_at)):
        size, step = part.shape[1], end - at
        packed = stage[at:end]
        for i in range(count // step):
            part[i * step : (i + 1) * step] = packed[:, i * size : (i + 1) * size]
    line = stage[gain_at : gain_at + 1] + stage[gain_at + 1 : gain_at + 2]
    line = jnp.broadcast_to(line, (8, width))
    start = place()(0) * count
    gain[...] = pltpu.roll(line, lax.rem(width - start, width), 1)[:1, :count]


def input_kernel(x, cc, pair_cc, edge, weight, out, ext, mixed):
    tokens = x.shape[0] // 2
    low = lax.axis_index("seq") % 2
    ext[8 : 8 + tokens] = cc[:tokens].astype(F32)
    pair_first = pair_cc[0:16].astype(F32)[0:1]
    pair_last = pair_cc[tokens - 16 : tokens].astype(F32)[15:16]
    ends = edge[...].astype(F32)
    ext[7:8] = jnp.where(low == 0, ends[1:2], pair_last)
    ext[8 + tokens : 9 + tokens] = jnp.where(low == 0, pair_first, ends[0:1])
    back = ext[7 : 7 + tokens].astype(BF)
    here = ext[8 : 8 + tokens].astype(BF)
    ahead = ext[9 : 9 + tokens].astype(BF)
    evens = (ahead, here, here, back, back)
    odds = (ahead, ahead, here, here, back)
    total = None
    for tap in range(5):
        term = dot_t(jnp.concatenate([evens[tap], odds[tap]], axis=0), weight[tap])
        total = term if total is None else total + term
    for c in range(mixed.shape[0]):
        lanes = slice(c * LANES, (c + 1) * LANES)
        mixed[c, pl.ds(0, tokens, stride=2)] = total[:tokens, lanes]
        mixed[c, pl.ds(1, tokens, stride=2)] = total[tokens:, lanes]
        out[:, lanes] = (mixed[c] * gelu_slope(x[:, lanes].astype(F32))).astype(BF)


def on_device(x, conv_weight, norm_gain, wq, wk, wv, cotangent):
    devices = lax.axis_size("seq")
    both_axes = ("seq", "dp")
    x, cotangent = x[0], cotangent[0]
    positions, channels = x.shape
    tokens = positions // 2
    taps, _, width = conv_weight.shape
    key_size, value_size = wk.shape[1], wv.shape[1]
    heads = cotangent.shape[1] // value_size
    scale = key_size ** (-0.5)
    groups = devices // 2
    owners = devices * 2
    conv_rows, norm_rows = taps * channels // owners, width // owners
    conv_pad, norm_pad = round_up(conv_rows, 16), round_up(norm_rows, 16)
    ext = tokens + 16
    gain = norm_gain.reshape(1, width)

    def swap(value, seq_bits, dp_bit=0):
        mask = 2 * seq_bits + dp_bit
        return lax.ppermute(value, both_axes, [(i, i ^ mask) for i in range(owners)])

    def quad(value):
        core = swap(value, 0, 1)
        near = swap(value, 1)
        return [value, core, near, swap(near, 0, 1)]

    up = [(i, i + 1) for i in range(devices - 1)]
    down = [(j, i) for i, j in up]
    before = lax.ppermute(x[positions - 2 :], "seq", up)
    after = lax.ppermute(x[:2], "seq", down)
    pad_shape = (channels // LANES, 8 + 2 * ext + 8, LANES)
    wv = wv.T
    (ready,) = run(prepare_kernel, [(pad_shape, F32)], [x], flops=4 * 10**9, name="gelu")
    kv, early, normed, pooled = run(
        front_kernel,
        [
            ((5 * tokens // 2, key_size), BF),
            ((2 * ext, channels), BF),
            ((tokens, width), BF),
            ((tokens, width), F32),
        ],
        [ready, before, after, conv_weight, gain, wk, wv],
        [pltpu.VMEM(pad_shape, F32)],
        flops=2 * positions * taps * channels * width,
        name="front",
    )
    near_kv = [kv] + [swap(kv, 2 * k) for k in range(1, groups)]
    far_kv = [swap(block, 1) for block in near_kv]
    queries, early, *picks = run(
        lambda *refs: query_kernel(
            *refs, groups=groups, rows=norm_rows, padded=norm_pad, scale=scale
        ),
        [
            ((tokens, heads * key_size), BF),
            (early.shape, BF),
        ]
        + [((groups * norm_pad, tokens), BF)] * 4,
        [normed, wq, early],
        flops=4 * tokens * width * heads * key_size,
        name="queries",
    )
    length = devices * tokens
    sizes = dict(
        blocks=devices, heads=heads, key_size=key_size, value_size=value_size, scale=scale
    )
    attend_flops = 3 * tokens * heads * length * (key_size + value_size)
    half_att = heads // 2 * value_size
    half_query = heads // 2 * key_size
    totals = [((length, key_size), F32), ((length, value_size), F32)]
    att_first, dq_first, *held = run(
        lambda *refs: attend_first_kernel(*refs, **sizes),
        [
            ((tokens, half_att), BF),
            ((tokens, half_query), BF),
            ((length, key_size), BF),
            ((length, value_size), BF),
            ((key_size, length), BF),
            ((value_size, length), BF),
        ]
        + totals,
        [queries, cotangent] + near_kv + far_kv,
        flops=attend_flops,
        name="attend_first",
    )
    early_near, early_core = swap(early, 1), swap(early, 0, 1)
    norm_picks = [picks[0], swap(picks[1], 0, 1), swap(picks[2], 1), swap(picks[3], 1, 1)]
    block_shape = (5 * tokens // 2, key_size)
    split = groups // 2
    attended, dq_second, near_cot, far_first, far_last = run(
        lambda *refs: attend_second_kernel(*refs, **sizes),
        [
            ((tokens, heads * value_size), BF),
            ((tokens, half_query), BF),
            ((groups,) + block_shape, F32),
            ((groups - split,) + block_shape, BF),
            ((split,) + block_shape, BF),
        ],
        [queries, cotangent, att_first] + held,
        [pltpu.VMEM(s, t) for s, t in totals],
        flops=attend_flops,
        name="attend_second",
        after=[early_near, early_core] + norm_picks[1:],
    )
    far_first = swap(far_first, 1)
    far_last = swap(far_last, 1)
    early_blocks = [early, early_core, early_near, swap(early_near, 0, 1)]
    (conv_pick,) = run(
        lambda *refs: select_kernel(*refs, groups=groups, rows=conv_rows, padded=conv_pad),
        [((groups * conv_pad, 8 * tokens), BF)],
        early_blocks,
        [pltpu.VMEM((ext, channels), F32), pltpu.VMEM((ext, channels), F32)],
        flops=2 * groups * conv_pad * taps * channels * 8 * tokens,
        name="select",
    )
    last = run(
        lambda *refs: add_kernel(*refs, start=split),
        [(block_shape, BF)] * (groups - split),
        [near_cot, far_first],
        name="kv_cot_far",
        after=[conv_pick],
    )
    query_cot, own, *others = run(
        add_near_kernel,
        [((tokens, heads * key_size), BF), (block_shape, F32)] + [(block_shape, BF)] * (split - 1),
        [near_cot, far_last, dq_first, dq_second],
        name="kv_cot_near",
        after=[last[0]],
    )
    others = others + list(last)
    arrived = [swap(other, 2 * (k + 1)) for k, other in enumerate(others)]
    (normed_cot,) = run(
        query_cot_kernel,
        [((tokens, width), F32)],
        [query_cot, wq],
        flops=2 * tokens * width * heads * key_size,
        name="query_part",
    )
    query_blocks = quad(query_cot)
    query_parts = run(
        lambda *refs: query_grad_kernel(*refs, pad=norm_pad),
        [((norm_pad, heads * key_size), F32 if k == 0 else BF) for k in range(groups)],
        norm_picks + query_blocks,
        [pltpu.VMEM((4 * tokens, heads * key_size), BF)],
        flops=2 * groups * norm_pad * 4 * tokens * heads * key_size,
        name="query_grad",
    )
    message, edge = run(
        make_middle(groups),
        [((tokens + 16 + tokens // 2, width), BF), ((16, width), BF)],
        [own] + arrived + [normed_cot, pooled, gain, wk, wv],
        flops=2 * tokens * width * (key_size + value_size),
        name="conv_cot",
        after=[query_blocks[2]],
    )
    near_message = swap(message, 1)
    (relay,) = run(
        relay_kernel,
        [(message.shape, BF)],
        [near_message],
        name="relay",
        after=[query_parts[0]],
    )
    blocks = [message, swap(message, 0, 1), near_message, swap(relay, 0, 1)]
    crossing = [(i, i + 1) for i in range(1, devices - 1, 2)]
    crossing = crossing + [(j, i) for i, j in crossing]
    edge_in = lax.ppermute(edge, "seq", crossing)
    query_in = [swap(part, 2 * (k + 1)) for k, part in enumerate(query_parts[1:])]
    _, _, gain_at = chunk_layout(conv_rows, norm_rows, width, key_size, value_size)
    chunk = (round_up(gain_at + 2, 16), width)
    conv_parts = run(
        lambda *refs: conv_grad_kernel(
            *refs,
            conv_rows=conv_rows,
            conv_pad=conv_pad,
            norm_rows=norm_rows,
            norm_pad=norm_pad,
            key_size=key_size,
            value_size=value_size,
        ),
        [(chunk, F32 if k == 0 else BF) for k in range(groups)],
        [conv_pick] + norm_picks + blocks,
        [
            pltpu.VMEM((8 * tokens, width), BF),
            pltpu.VMEM((4 * tokens, width // 2), BF),
            pltpu.VMEM(chunk, F32),
        ],
        flops=2 * groups * conv_pad * 8 * tokens * width,
        name="conv_grad",
        after=[edge_in] + query_in,
    )
    conv_in = [swap(part, 2 * (k + 1)) for k, part in enumerate(conv_parts[1:])]
    (input_grad,) = run(
        input_kernel,
        [((positions, channels), BF)],
        [x, message, blocks[2], edge_in, conv_weight],
        [
            pltpu.VMEM((tokens + 16, width), F32),
            pltpu.VMEM((channels // LANES, positions, LANES), F32),
        ],
        flops=2 * positions * taps * channels * width,
        name="input_grad",
        after=[conv_parts[0]],
    )
    (query_grad,) = run(
        query_sum_kernel,
        [((norm_rows, heads * key_size), F32)],
        [query_parts[0]] + query_in,
        name="query_sum",
        after=[conv_parts[0]],
    )
    conv_grad, key_grad, value_grad, gain_grad = run(
        final_kernel,
        [
            ((conv_rows, width), F32),
            ((norm_rows, key_size), F32),
            ((norm_rows, value_size), F32),
            ((1, norm_rows), F32),
        ],
        [conv_parts[0]] + conv_in,
        [pltpu.VMEM(chunk, F32)],
        name="conv_sum",
    )
    return (
        attended[None],
        input_grad[None],
        conv_grad,
        query_grad,
        key_grad,
        value_grad,
        gain_grad.reshape(norm_rows),
    )


def solution(mesh):
    placed = (
        P(("groups", "dp"), "seq", None),
        P(),
        P(),
        P(),
        P(),
        P(),
        P(("groups", "dp"), "seq", None),
    )
    return jax.shard_map(
        on_device,
        mesh=mesh,
        in_specs=placed,
        out_specs=(
            P(("groups", "dp"), "seq", None),
            P(("groups", "dp"), "seq", None),
            P(("groups", "seq", "dp"), None),
            P(("groups", "seq", "dp"), None),
            P(("groups", "seq", "dp"), None),
            P(("groups", "seq", "dp"), None),
            P(("groups", "seq", "dp")),
        ),
        check_vma=False,
    )
```

time: 116 us -> 109 us (0.940)
  starting transfers between devices: 55.1 us -> 39.1 us
  waiting for transfers between devices: 34.3 us -> 46.2 us
  local copies, waits for them, and re-layouts: 6.24 us -> 2.18 us
    ppermute x26 -> x30, starting transfers between devices: 48.2 us -> 32.3 us  [swap(): lax.ppermute(value, both_axes, [(i, i ^ mask) for i in range(owners)])]
    ppermute x26 -> x30, waiting for transfers between devices: 32 us -> 43.7 us  [swap(): lax.ppermute(value, both_axes, [(i, i ^ mask) for i in range(owners)])]
    unnamed x15 -> x16, local copies, waits for them, and re-layouts: 4.83 us -> 1.46 us
    pallas_call x12 -> x16, Pallas kernels: 19.1 us -> 19.6 us  [run(): pl.pallas_call(whole, out_shape=[jax.ShapeDtypeStruct(s, t) for s, t in o...]
  transfers between devices with their start and end apart: 29 -> 33, of which waited for: 11 -> 17; matrix products, arithmetic and copies ran while one was open for 2% -> 0% of each run, Pallas kernels for 8% -> 13%
where the time goes in v2:
time: 109 us; the launch traced here: 108 us
  waiting for transfers between devices  46.2 us (42%)
  starting transfers between devices  39.1 us (36%)
  Pallas kernels  19.6 us (18%)
  local copies, waits for them, and re-layouts  2.18 us (2%)
    ppermute x30, waiting for transfers between devices, swap(): lax.ppermute(value, both_axes, [(i, i ^ mask) for i in range(owners)])  43.7 us
    ppermute x30, starting transfers between devices, swap(): lax.ppermute(value, both_axes, [(i, i ^ mask) for i in range(owners)])  32.3 us
    pallas_call x16, Pallas kernels, run(): pl.pallas_call(whole, out_shape=[jax.ShapeDtypeStruct(s, t) for s, t in o...  19.6 us
    ppermute x1, starting transfers between devices, on_device(): before = lax.ppermute(x[positions - 2:], 'seq', up)  4.86 us
    ppermute x1, waiting for transfers between devices, on_device(): after = lax.ppermute(x[:2], 'seq', down)  2.54 us
  transfers between devices with their start and end apart: 33, of which 17 were waited for; matrix products, arithmetic and copies ran while one was open for 0% of the time, Pallas kernels for 13%

profile of v2, /device:TPU:0, one launch (start us, length us, event | category | flops | bytes accessed | tf_op | source)
XLA Modules:
  0.0 108.0 jit_solution(15095689949246565126)
XLA Ops:
  1.3 4.9 %collective-permute-start = (bf16[2,384]{1,0:T(2,128)(2,1)S(1)}, bf16[2,384]{1,0:T(2,128)(2,1)S(1)}, u32[]{:S(2)}, u32[]{:S(2)}) collective-permute-start(bf16[2,384]{1,0:T(2,128)(2,1)S(1)} %get-tuple-element.92), channel_id=1, source_target_pairs={{0,2},{2,4},{4,6},{6,8},{8,10},{10,12},{12,14},{1,3},{3,5},{5,7},{... | collective-permute-start | bytes 4616 | tf_op jit(solution)/shard_map/ppermute | solution.py:435
  6.2 1.3 %collective-permute-start.1 = (bf16[2,384]{1,0:T(2,128)(2,1)S(1)}, bf16[2,384]{1,0:T(2,128)(2,1)S(1)}, u32[]{:S(2)}, u32[]{:S(2)}) collective-permute-start(bf16[2,384]{1,0:T(2,128)(2,1)S(1)} %get-tuple-element.91), channel_id=1, source_target_pairs={{2,0},{4,2},{6,4},{8,6},{10,8},{12,10},{14,12},{3,1},{5,3},{7,5},{... | collective-permute-start | bytes 4616 | tf_op jit(solution)/shard_map/ppermute | solution.py:436
  9.1 2.5 %collective-permute-done.1.refs_2_ = bf16[2,384]{1,0:T(2,128)(2,1)S(1)} collective-permute-done((bf16[2,384]{1,0:T(2,128)(2,1)S(1)}, bf16[2,384]{1,0:T(2,128)(2,1)S(1)}, u32[]{:S(2)}, u32[]{:S(2)}) %collective-permute-start.1) | collective-permute-done | bytes 1568 | tf_op jit(solution)/shard_map/ppermute | solution.py:436
  11.7 1.8 %front.1 = (bf16[320,128]{1,0:T(8,128)(2,1)S(1)}, bf16[288,384]{1,0:T(8,128)(2,1)S(1)}, bf16[128,768]{1,0:T(8,128)(2,1)S(1)}, f32[128,768]{1,0:T(8,128)S(1)}) custom-call(f32[3,304,128]{2,1,0:T(8,128)S(1)} %gelu.1.refs_0_, bf16[2,384]{1,0:T(2,128)(2,1)S(1)} %collective-permute-done.refs_1_, bf16[2,384]{1,0:T(2,128)(2,1)S(1)} %collective-permute-done.1.refs_2_, ...), custom_call_target="tpu_custom_call" | custom-call | flops 754974720 | bytes 4806656 | tf_op jit(solution)/shard_map/front/pallas_call | solution.py:36
  14.3 2.5 %collective-permute-start.9 = (bf16[288,384]{1,0:T(8,128)(2,1)S(1)}, bf16[288,384]{1,0:T(8,128)(2,1)S(1)}, u32[]{:S(2)}, u32[]{:S(2)}) collective-permute-start(bf16[288,384]{1,0:T(8,128)(2,1)S(1)} %get-tuple-element.60.refs_0_), channel_id=1, source_target_pairs={{0,2},{1,3},{2,0},{3,1},{4,6},{5,7},{6,4},{7,5},{8,10},{9,11},{10,... | collective-permute-start | bytes 663560 | tf_op jit(solution)/shard_map/ppermute | solution.py:426
  16.8 1.6 %collective-permute-start.2 = (bf16[320,128]{1,0:T(8,128)(2,1)S(1)}, bf16[320,128]{1,0:T(8,128)(2,1)S(1)}, u32[]{:S(2)}, u32[]{:S(2)}) collective-permute-start(bf16[320,128]{1,0:T(8,128)(2,1)S(1)} %get-tuple-element.52.refs_2_), channel_id=1, source_target_pairs={{0,4},{1,5},{2,6},{3,7},{4,0},{5,1},{6,2},{7,3},{8,12},{9,13},{10,... | collective-permute-start | bytes 245768 | tf_op jit(solution)/shard_map/ppermute | solution.py:426
  18.3 1.5 %collective-permute-start.3 = (bf16[320,128]{1,0:T(8,128)(2,1)S(1)}, bf16[320,128]{1,0:T(8,128)(2,1)S(1)}, u32[]{:S(2)}, u32[]{:S(2)}) collective-permute-start(bf16[320,128]{1,0:T(8,128)(2,1)S(1)} %get-tuple-element.52.refs_2_), channel_id=1, source_target_pairs={{0,8},{1,9},{2,10},{3,11},{4,12},{5,13},{6,14},{7,15},{8,0},{9,1},... | collective-permute-start | bytes 245768 | tf_op jit(solution)/shard_map/ppermute | solution.py:426
  19.8 1.3 %collective-permute-start.4 = (bf16[320,128]{1,0:T(8,128)(2,1)S(1)}, bf16[320,128]{1,0:T(8,128)(2,1)S(1)}, u32[]{:S(2)}, u32[]{:S(2)}) collective-permute-start(bf16[320,128]{1,0:T(8,128)(2,1)S(1)} %get-tuple-element.52.refs_2_), channel_id=1, source_target_pairs={{0,12},{1,13},{2,14},{3,15},{4,8},{5,9},{6,10},{7,11},{8,4},{9,5},... | collective-permute-start | bytes 245768 | tf_op jit(solution)/shard_map/ppermute | solution.py:426
  21.4 4.9 %collective-permute-done.3.refs_4_ = bf16[320,128]{1,0:T(8,128)(2,1)S(1)} collective-permute-done((bf16[320,128]{1,0:T(8,128)(2,1)S(1)}, bf16[320,128]{1,0:T(8,128)(2,1)S(1)}, u32[]{:S(2)}, u32[]{:S(2)}) %collective-permute-start.3) | collective-permute-done | bytes 81952 | tf_op jit(solution)/shard_map/ppermute | solution.py:426
  26.2 2.0 %collective-permute-start.7 = (bf16[320,128]{1,0:T(8,128)(2,1)S(1)}, bf16[320,128]{1,0:T(8,128)(2,1)S(1)}, u32[]{:S(2)}, u32[]{:S(2)}) collective-permute-start(bf16[320,128]{1,0:T(8,128)(2,1)S(1)} %collective-permute-done.3.refs_4_), channel_id=1, source_target_pairs={{0,2},{1,3},{2,0},{3,1},{4,6},{5,7},{6,4},{7,5},{8,10},{9,11},{10,... | collective-permute-start | bytes 245768 | tf_op jit(solution)/shard_map/ppermute | solution.py:426
  28.3 2.3 %collective-permute-done.6.refs_7_ = bf16[320,128]{1,0:T(8,128)(2,1)S(1)} collective-permute-done((bf16[320,128]{1,0:T(8,128)(2,1)S(1)}, bf16[320,128]{1,0:T(8,128)(2,1)S(1)}, u32[]{:S(2)}, u32[]{:S(2)}) %collective-permute-start.6) | collective-permute-done | bytes 81952 | tf_op jit(solution)/shard_map/ppermute | solution.py:426
  32.7 3.3 %attend_first.1 = (bf16[128,768]{1,0:T(8,128)(2,1)S(1)}, bf16[128,512]{1,0:T(8,128)(2,1)S(1)}, bf16[1024,128]{1,0:T(8,128)(2,1)S(1)}, bf16[1024,192]{1,0:T(8,128...) custom-call(bf16[128,1024]{1,0:T(8,128)(2,1)S(1)} %get-tuple-element, ...), custom_call_target="tpu_custom_call" | custom-call | flops 1006632960 | bytes 4259840 | tf_op jit(solution)/shard_map/attend_first/pallas_call | solution.py:36
  36.7 4.0 %attend_second.1 = (bf16[128,1536]{1,0:T(8,128)(2,1)}, bf16[128,512]{1,0:T(8,128)(2,1)S(1)}, f32[4,320,128]{2,1,0:T(8,128)S(1)}, bf16[2,320,128]{2,1,0:T(8,128)(2,1)S(1)}, bf16[2,320,128]{2,1,0:T(8,128)(2,1)S(1)}) custom-call(bf16[128,1024]{1,0:T(8,128)(2,1)S(1)} %get-tuple-element.51.refs_0_, bf16[128,1536]{1,0:T(8,128)(2,1)S(1)} %bitcast.13, ...), custom_call_target="tpu_custom_call" | custom-call | flops 1006632960 | bytes 4980736 | tf_op jit(solution)/shard_map/attend_second/pallas_call | solution.py:36
  42.7 2.4 %select.1.refs_2_.refs_0_ = bf16[512,1024]{1,0:T(8,128)(2,1)S(1)} custom-call(bf16[288,384]{1,0:T(8,128)(2,1)S(1)} %get-tuple-element.60.refs_0_, bf16[288,384]{1,0:T(8,128)(2,1)S(1)} %collective-permute-done.10.refs_10_.refs_1_, bf16[288,384]{1,0:T(8,128)(2,1)S(1)} %collective-permute-done.9.refs_9_.refs_2_, ...), custom_call_target="tpu_custom_call" | custom-call | flops 2013265920 | bytes 1933312 | tf_op jit(solution)/shard_map/select/pallas_call | solution.py:36
  45.2 2.6 %collective-permute-done.15.refs_1_ = bf16[2,320,128]{2,1,0:T(8,128)(2,1)S(1)} collective-permute-done((bf16[2,320,128]{2,1,0:T(8,128)(2,1)S(1)}, bf16[2,320,128]{2,1,0:T(8,128)(2,1)S(1)}, u32[]{:S(2)}, u32[]{:S(2)}) %collective-permute-start.15) | collective-permute-done | bytes 163872 | tf_op jit(solution)/shard_map/ppermute | solution.py:426
  47.8 2.9 %collective-permute-done.14.refs_1_ = bf16[2,320,128]{2,1,0:T(8,128)(2,1)S(1)} collective-permute-done((bf16[2,320,128]{2,1,0:T(8,128)(2,1)S(1)}, bf16[2,320,128]{2,1,0:T(8,128)(2,1)S(1)}, u32[]{:S(2)}, u32[]{:S(2)}) %collective-permute-start.14) | collective-permute-done | bytes 163872 | tf_op jit(solution)/shard_map/ppermute | solution.py:426
  50.7 1.2 %collective-permute-start.20 = (bf16[128,1024]{1,0:T(8,128)(2,1)S(1)}, bf16[128,1024]{1,0:T(8,128)(2,1)S(1)}, u32[]{:S(2)}, u32[]{:S(2)}) collective-permute-start(bf16[128,1024]{1,0:T(8,128)(2,1)S(1)} %get-tuple-element.74.refs_0_.refs_4_), channel_id=1, source_target_pairs={{0,2},{1,3},{2,0},{3,1},{4,6},{5,7},{6,4},{7,5},{8,10},{9,11},{10,... | collective-permute-start | bytes 786440 | tf_op jit(solution)/shard_map/ppermute | solution.py:426
  53.1 1.5 %collective-permute-start.17 = (bf16[320,128]{1,0:T(8,128)(2,1)S(1)}, bf16[320,128]{1,0:T(8,128)(2,1)S(1)}, u32[]{:S(2)}, u32[]{:S(2)}) collective-permute-start(bf16[320,128]{1,0:T(8,128)(2,1)S(1)} %get-tuple-element.72), channel_id=1, source_target_pairs={{0,4},{1,5},{2,6},{3,7},{4,0},{5,1},{6,2},{7,3},{8,12},{9,13},{10,... | collective-permute-start | bytes 245768 | tf_op jit(solution)/shard_map/ppermute | solution.py:426
  54.6 1.8 %collective-permute-start.19 = (bf16[320,128]{1,0:T(8,128)(2,1)S(1)}, bf16[320,128]{1,0:T(8,128)(2,1)S(1)}, u32[]{:S(2)}, u32[]{:S(2)}) collective-permute-start(bf16[320,128]{1,0:T(8,128)(2,1)S(1)} %get-tuple-element.73), channel_id=1, source_target_pairs={{0,12},{1,13},{2,14},{3,15},{4,8},{5,9},{6,10},{7,11},{8,4},{9,5},... | collective-permute-start | bytes 245768 | tf_op jit(solution)/shard_map/ppermute | solution.py:426
  57.8 2.0 %collective-permute-done.18.refs_2_ = bf16[320,128]{1,0:T(8,128)(2,1)S(1)} collective-permute-done((bf16[320,128]{1,0:T(8,128)(2,1)S(1)}, bf16[320,128]{1,0:T(8,128)(2,1)S(1)}, u32[]{:S(2)}, u32[]{:S(2)}) %collective-permute-start.18) | collective-permute-done | bytes 81952 | tf_op jit(solution)/shard_map/ppermute | solution.py:426
  61.5 1.2 %collective-permute-start.21 = (bf16[208,768]{1,0:T(8,128)(2,1)S(1)}, bf16[208,768]{1,0:T(8,128)(2,1)S(1)}, u32[]{:S(2)}, u32[]{:S(2)}) collective-permute-start(bf16[208,768]{1,0:T(8,128)(2,1)S(1)} %get-tuple-element.76.refs_5_.refs_1_), channel_id=1, source_target_pairs={{0,2},{1,3},{2,0},{3,1},{4,6},{5,7},{6,4},{7,5},{8,10},{9,11},{10,... | collective-permute-start | bytes 958472 | tf_op jit(solution)/shard_map/ppermute | solution.py:426
  65.5 4.1 %collective-permute-done.21.refs_0_.refs_7_.refs_2_ = bf16[208,768]{1,0:T(8,128)(2,1)S(1)} collective-permute-done((bf16[208,768]{1,0:T(8,128)(2,1)S(1)}, bf16[208,768]{1,0:T(8,128)(2,1)S(1)}, u32[]{:S(2)}, u32[]{:S(2)}) %collective-permute-start.21) | collective-permute-done | bytes 319520 | tf_op jit(solution)/shard_map/ppermute | solution.py:426
  70.3 3.7 %collective-permute-start.27 = (bf16[48,1024]{1,0:T(8,128)(2,1)S(1)}, bf16[48,1024]{1,0:T(8,128)(2,1)S(1)}, u32[]{:S(2)}, u32[]{:S(2)}) collective-permute-start(bf16[48,1024]{1,0:T(8,128)(2,1)S(1)} %get-tuple-element.80), channel_id=1, source_target_pairs={{0,4},{1,5},{2,6},{3,7},{4,0},{5,1},{6,2},{7,3},{8,12},{9,13},{10,... | collective-permute-start | bytes 294920 | tf_op jit(solution)/shard_map/ppermute | solution.py:426
  74.1 3.0 %collective-permute-start.28 = (bf16[48,1024]{1,0:T(8,128)(2,1)S(1)}, bf16[48,1024]{1,0:T(8,128)(2,1)S(1)}, u32[]{:S(2)}, u32[]{:S(2)}) collective-permute-start(bf16[48,1024]{1,0:T(8,128)(2,1)S(1)} %get-tuple-element.81), channel_id=1, source_target_pairs={{0,8},{1,9},{2,10},{3,11},{4,12},{5,13},{6,14},{7,15},{8,0},{9,1},... | collective-permute-start | bytes 294920 | tf_op jit(solution)/shard_map/ppermute | solution.py:426
  77.1 1.4 %collective-permute-start.29 = (bf16[48,1024]{1,0:T(8,128)(2,1)S(1)}, bf16[48,1024]{1,0:T(8,128)(2,1)S(1)}, u32[]{:S(2)}, u32[]{:S(2)}) collective-permute-start(bf16[48,1024]{1,0:T(8,128)(2,1)S(1)} %get-tuple-element.82), channel_id=1, source_target_pairs={{0,12},{1,13},{2,14},{3,15},{4,8},{5,9},{6,10},{7,11},{8,4},{9,5},... | collective-permute-start | bytes 294920 | tf_op jit(solution)/shard_map/ppermute | solution.py:426
  78.5 6.4 %collective-permute-done.28.refs_11_.refs_2_ = bf16[48,1024]{1,0:T(8,128)(2,1)S(1)} collective-permute-done((bf16[48,1024]{1,0:T(8,128)(2,1)S(1)}, bf16[48,1024]{1,0:T(8,128)(2,1)S(1)}, u32[]{:S(2)}, u32[]{:S(2)}) %collective-permute-start.28) | collective-permute-done | bytes 98336 | tf_op jit(solution)/shard_map/ppermute | solution.py:426
  84.9 1.4 %conv_grad.1 = (f32[144,768]{1,0:T(8,128)S(1)}, bf16[144,768]{1,0:T(8,128)(2,1)S(1)}, bf16[144,768]{1,0:T(8,128)(2,1)S(1)}, bf16[144,768]{1,0:T(8,128)(2,1)S(1)}) custom-call(bf16[512,1024]{1,0:T(8,128)(2,1)S(1)} %select.1.refs_2_.refs_0_, bf16[192,128]{1,0:T(8,128)(2,1)S(1)} %get-tuple-element.78.refs_0_.refs_1_, ...), custom_call_target="tpu_custom_call" | custom-call | flops 805306368 | bytes 3629056 | tf_op jit(solution)/shard_map/conv_grad/pallas_call | solution.py:36
  86.4 2.0 %collective-permute-start.30 = (bf16[144,768]{1,0:T(8,128)(2,1)S(1)}, bf16[144,768]{1,0:T(8,128)(2,1)S(1)}, u32[]{:S(2)}, u32[]{:S(2)}) collective-permute-start(bf16[144,768]{1,0:T(8,128)(2,1)S(1)} %get-tuple-element.84), channel_id=1, source_target_pairs={{0,4},{1,5},{2,6},{3,7},{4,0},{5,1},{6,2},{7,3},{8,12},{9,13},{10,... | collective-permute-start | bytes 663560 | tf_op jit(solution)/shard_map/ppermute | solution.py:426
  89.5 1.4 %collective-permute-start.32 = (bf16[144,768]{1,0:T(8,128)(2,1)S(1)}, bf16[144,768]{1,0:T(8,128)(2,1)S(1)}, u32[]{:S(2)}, u32[]{:S(2)}) collective-permute-start(bf16[144,768]{1,0:T(8,128)(2,1)S(1)} %get-tuple-element.86), channel_id=1, source_target_pairs={{0,12},{1,13},{2,14},{3,15},{4,8},{5,9},{6,10},{7,11},{8,4},{9,5},... | collective-permute-start | bytes 663560 | tf_op jit(solution)/shard_map/ppermute | solution.py:426
  91.6 2.0 %input_grad.1 = bf16[256,384]{1,0:T(8,128)(2,1)} custom-call(bf16[256,384]{1,0:T(8,128)(2,1)S(1)} %bitcast.15, bf16[208,768]{1,0:T(8,128)(2,1)S(1)} %get-tuple-element.76.refs_5_.refs_1_, bf16[208,768]{1,0:T(8,128)(2,1)S(1)} %collective-permute-done.21.refs_0_.refs_7_.refs_2_, bf16[16,768]{1,0:T(8,128)(2,1)S(1)} %collective-permute-done.22.refs_9_.refs_3_, ...), custom_call_target="tpu_custom_call" | custom-call | flops 754974720 | bytes 4005888 | tf_op jit(solution)/shard_map/input_grad/pallas_call | solution.py:36
  93.6 3.4 %collective-permute-done.30.refs_1_ = bf16[144,768]{1,0:T(8,128)(2,1)S(1)} collective-permute-done((bf16[144,768]{1,0:T(8,128)(2,1)S(1)}, bf16[144,768]{1,0:T(8,128)(2,1)S(1)}, u32[]{:S(2)}, u32[]{:S(2)}) %collective-permute-start.30) | collective-permute-done | bytes 221216 | tf_op jit(solution)/shard_map/ppermute | solution.py:426
  97.0 10.1 %collective-permute-done.31.refs_2_ = bf16[144,768]{1,0:T(8,128)(2,1)S(1)} collective-permute-done((bf16[144,768]{1,0:T(8,128)(2,1)S(1)}, bf16[144,768]{1,0:T(8,128)(2,1)S(1)}, u32[]{:S(2)}, u32[]{:S(2)}) %collective-permute-start.31) | collective-permute-done | bytes 221216 | tf_op jit(solution)/shard_map/ppermute | solution.py:426
  (68 shorter events, 18.8 us)
Async XLA Ops:
  1.3 7.8 %collective-permute-start = (bf16[2,384]{1,0:T(2,128)(2,1)S(1)}, bf16[2,384]{1,0:T(2,128)(2,1)S(1)}, u32[]{:S(2)}, u32[]{:S(2)}) collective-permute-start(bf16[2,384]{1,0:T(2,128)(2,1)S(1)} %get-tuple-element.92), channel_id=1, source_target_pairs={{0,2},{2,4},{4,6},{6,8},{8,10},{10,12},{12,14},{1,3},{3,5},{5,7},{... | collective-permute-start | bytes 4616 | tf_op jit(solution)/shard_map/ppermute | solution.py:435
  6.2 5.5 %collective-permute-start.1 = (bf16[2,384]{1,0:T(2,128)(2,1)S(1)}, bf16[2,384]{1,0:T(2,128)(2,1)S(1)}, u32[]{:S(2)}, u32[]{:S(2)}) collective-permute-start(bf16[2,384]{1,0:T(2,128)(2,1)S(1)} %get-tuple-element.91), channel_id=1, source_target_pairs={{2,0},{4,2},{6,4},{8,6},{10,8},{12,10},{14,12},{3,1},{5,3},{7,5},{... | collective-permute-start | bytes 4616 | tf_op jit(solution)/shard_map/ppermute | solution.py:436
  14.3 14.1 %collective-permute-start.9 = (bf16[288,384]{1,0:T(8,128)(2,1)S(1)}, bf16[288,384]{1,0:T(8,128)(2,1)S(1)}, u32[]{:S(2)}, u32[]{:S(2)}) collective-permute-start(bf16[288,384]{1,0:T(8,128)(2,1)S(1)} %get-tuple-element.60.refs_0_), channel_id=1, source_target_pairs={{0,2},{1,3},{2,0},{3,1},{4,6},{5,7},{6,4},{7,5},{8,10},{9,11},{10,... | collective-permute-start | bytes 663560 | tf_op jit(solution)/shard_map/ppermute | solution.py:426
  16.8 4.6 %collective-permute-start.2 = (bf16[320,128]{1,0:T(8,128)(2,1)S(1)}, bf16[320,128]{1,0:T(8,128)(2,1)S(1)}, u32[]{:S(2)}, u32[]{:S(2)}) collective-permute-start(bf16[320,128]{1,0:T(8,128)(2,1)S(1)} %get-tuple-element.52.refs_2_), channel_id=1, source_target_pairs={{0,4},{1,5},{2,6},{3,7},{4,0},{5,1},{6,2},{7,3},{8,12},{9,13},{10,... | collective-permute-start | bytes 245768 | tf_op jit(solution)/shard_map/ppermute | solution.py:426
  18.3 7.9 %collective-permute-start.3 = (bf16[320,128]{1,0:T(8,128)(2,1)S(1)}, bf16[320,128]{1,0:T(8,128)(2,1)S(1)}, u32[]{:S(2)}, u32[]{:S(2)}) collective-permute-start(bf16[320,128]{1,0:T(8,128)(2,1)S(1)} %get-tuple-element.52.refs_2_), channel_id=1, source_target_pairs={{0,8},{1,9},{2,10},{3,11},{4,12},{5,13},{6,14},{7,15},{8,0},{9,1},... | collective-permute-start | bytes 245768 | tf_op jit(solution)/shard_map/ppermute | solution.py:426
  19.8 6.4 %collective-permute-start.4 = (bf16[320,128]{1,0:T(8,128)(2,1)S(1)}, bf16[320,128]{1,0:T(8,128)(2,1)S(1)}, u32[]{:S(2)}, u32[]{:S(2)}) collective-permute-start(bf16[320,128]{1,0:T(8,128)(2,1)S(1)} %get-tuple-element.52.refs_2_), channel_id=1, source_target_pairs={{0,12},{1,13},{2,14},{3,15},{4,8},{5,9},{6,10},{7,11},{8,4},{9,5},... | collective-permute-start | bytes 245768 | tf_op jit(solution)/shard_map/ppermute | solution.py:426
  21.2 7.1 %collective-permute-start.5 = (bf16[320,128]{1,0:T(8,128)(2,1)S(1)}, bf16[320,128]{1,0:T(8,128)(2,1)S(1)}, u32[]{:S(2)}, u32[]{:S(2)}) collective-permute-start(bf16[320,128]{1,0:T(8,128)(2,1)S(1)} %get-tuple-element.52.refs_2_), channel_id=1, source_target_pairs={{0,2},{1,3},{2,0},{3,1},{4,6},{5,7},{6,4},{7,5},{8,10},{9,11},{10,... | collective-permute-start | bytes 245768 | tf_op jit(solution)/shard_map/ppermute | solution.py:426
  21.4 15.3 %collective-permute-start.10 = (bf16[288,384]{1,0:T(8,128)(2,1)S(1)}, bf16[288,384]{1,0:T(8,128)(2,1)S(1)}, u32[]{:S(2)}, u32[]{:S(2)}) collective-permute-start(bf16[288,384]{1,0:T(8,128)(2,1)S(1)} %get-tuple-element.60.refs_0_), channel_id=1, source_target_pairs={{0,1},{1,0},{2,3},{3,2},{4,5},{5,4},{6,7},{7,6},{8,9},{9,8},{10,11... | collective-permute-start | bytes 663560 | tf_op jit(solution)/shard_map/ppermute | solution.py:426
  26.2 4.4 %collective-permute-start.6 = (bf16[320,128]{1,0:T(8,128)(2,1)S(1)}, bf16[320,128]{1,0:T(8,128)(2,1)S(1)}, u32[]{:S(2)}, u32[]{:S(2)}) collective-permute-start(bf16[320,128]{1,0:T(8,128)(2,1)S(1)} %collective-permute-done.2.refs_3_), channel_id=1, source_target_pairs={{0,2},{1,3},{2,0},{3,1},{4,6},{5,7},{6,4},{7,5},{8,10},{9,11},{10,... | collective-permute-start | bytes 245768 | tf_op jit(solution)/shard_map/ppermute | solution.py:426
  26.2 5.3 %collective-permute-start.7 = (bf16[320,128]{1,0:T(8,128)(2,1)S(1)}, bf16[320,128]{1,0:T(8,128)(2,1)S(1)}, u32[]{:S(2)}, u32[]{:S(2)}) collective-permute-start(bf16[320,128]{1,0:T(8,128)(2,1)S(1)} %collective-permute-done.3.refs_4_), channel_id=1, source_target_pairs={{0,2},{1,3},{2,0},{3,1},{4,6},{5,7},{6,4},{7,5},{8,10},{9,11},{10,... | collective-permute-start | bytes 245768 | tf_op jit(solution)/shard_map/ppermute | solution.py:426
  28.3 4.4 %collective-permute-start.8 = (bf16[320,128]{1,0:T(8,128)(2,1)S(1)}, bf16[320,128]{1,0:T(8,128)(2,1)S(1)}, u32[]{:S(2)}, u32[]{:S(2)}) collective-permute-start(bf16[320,128]{1,0:T(8,128)(2,1)S(1)} %collective-permute-done.4.refs_5_), channel_id=1, source_target_pairs={{0,2},{1,3},{2,0},{3,1},{4,6},{5,7},{6,4},{7,5},{8,10},{9,11},{10,... | collective-permute-start | bytes 245768 | tf_op jit(solution)/shard_map/ppermute | solution.py:426
  28.3 14.4 %collective-permute-start.16 = (bf16[288,384]{1,0:T(8,128)(2,1)S(1)}, bf16[288,384]{1,0:T(8,128)(2,1)S(1)}, u32[]{:S(2)}, u32[]{:S(2)}) collective-permute-start(bf16[288,384]{1,0:T(8,128)(2,1)S(1)} %collective-permute-done.9.refs_9_.refs_2_), channel_id=1, source_target_pairs={{0,1},{1,0},{2,3},{3,2},{4,5},{5,4},{6,7},{7,6},{8,9},{9,8},{10,11... | collective-permute-start | bytes 663560 | tf_op jit(solution)/shard_map/ppermute | solution.py:426
  30.7 5.3 %collective-permute-start.11 = (bf16[192,128]{1,0:T(8,128)(2,1)S(1)}, bf16[192,128]{1,0:T(8,128)(2,1)S(1)}, u32[]{:S(2)}, u32[]{:S(2)}) collective-permute-start(bf16[192,128]{1,0:T(8,128)(2,1)S(1)} %get-tuple-element.61), channel_id=1, source_target_pairs={{0,1},{1,0},{2,3},{3,2},{4,5},{5,4},{6,7},{7,6},{8,9},{9,8},{10,11... | collective-permute-start | bytes 147464 | tf_op jit(solution)/shard_map/ppermute | solution.py:426
  31.5 4.5 %collective-permute-start.12 = (bf16[192,128]{1,0:T(8,128)(2,1)S(1)}, bf16[192,128]{1,0:T(8,128)(2,1)S(1)}, u32[]{:S(2)}, u32[]{:S(2)}) collective-permute-start(bf16[192,128]{1,0:T(8,128)(2,1)S(1)} %get-tuple-element.62), channel_id=1, source_target_pairs={{0,2},{1,3},{2,0},{3,1},{4,6},{5,7},{6,4},{7,5},{8,10},{9,11},{10,... | collective-permute-start | bytes 147464 | tf_op jit(solution)/shard_map/ppermute | solution.py:426
  32.7 4.0 %collective-permute-start.13 = (bf16[192,128]{1,0:T(8,128)(2,1)S(1)}, bf16[192,128]{1,0:T(8,128)(2,1)S(1)}, u32[]{:S(2)}, u32[]{:S(2)}) collective-permute-start(bf16[192,128]{1,0:T(8,128)(2,1)S(1)} %get-tuple-element.63), channel_id=1, source_target_pairs={{0,3},{1,2},{2,1},{3,0},{4,7},{5,6},{6,5},{7,4},{8,11},{9,10},{10,... | collective-permute-start | bytes 147464 | tf_op jit(solution)/shard_map/ppermute | solution.py:426
  40.7 7.0 %collective-permute-start.15 = (bf16[2,320,128]{2,1,0:T(8,128)(2,1)S(1)}, bf16[2,320,128]{2,1,0:T(8,128)(2,1)S(1)}, u32[]{:S(2)}, u32[]{:S(2)}) collective-permute-start(bf16[2,320,128]{2,1,0:T(8,128)(2,1)S(1)} %get-tuple-element.69), channel_id=1, source_target_pairs={{0,2},{1,3},{2,0},{3,1},{4,6},{5,7},{6,4},{7,5},{8,10},{9,11},{10,... | collective-permute-start | bytes 491528 | tf_op jit(solution)/shard_map/ppermute | solution.py:426
  41.6 9.0 %collective-permute-start.14 = (bf16[2,320,128]{2,1,0:T(8,128)(2,1)S(1)}, bf16[2,320,128]{2,1,0:T(8,128)(2,1)S(1)}, u32[]{:S(2)}, u32[]{:S(2)}) collective-permute-start(bf16[2,320,128]{2,1,0:T(8,128)(2,1)S(1)} %get-tuple-element.66), channel_id=1, source_target_pairs={{0,2},{1,3},{2,0},{3,1},{4,6},{5,7},{6,4},{7,5},{8,10},{9,11},{10,... | collective-permute-start | bytes 491528 | tf_op jit(solution)/shard_map/ppermute | solution.py:426
  50.7 10.2 %collective-permute-start.20 = (bf16[128,1024]{1,0:T(8,128)(2,1)S(1)}, bf16[128,1024]{1,0:T(8,128)(2,1)S(1)}, u32[]{:S(2)}, u32[]{:S(2)}) collective-permute-start(bf16[128,1024]{1,0:T(8,128)(2,1)S(1)} %get-tuple-element.74.refs_0_.refs_4_), channel_id=1, source_target_pairs={{0,2},{1,3},{2,0},{3,1},{4,6},{5,7},{6,4},{7,5},{8,10},{9,11},{10,... | collective-permute-start | bytes 786440 | tf_op jit(solution)/shard_map/ppermute | solution.py:426
  51.9 7.9 %collective-permute-start.18 = (bf16[320,128]{1,0:T(8,128)(2,1)S(1)}, bf16[320,128]{1,0:T(8,128)(2,1)S(1)}, u32[]{:S(2)}, u32[]{:S(2)}) collective-permute-start(bf16[320,128]{1,0:T(8,128)(2,1)S(1)} %get-tuple-element.70.refs_4_), channel_id=1, source_target_pairs={{0,8},{1,9},{2,10},{3,11},{4,12},{5,13},{6,14},{7,15},{8,0},{9,1},... | collective-permute-start | bytes 245768 | tf_op jit(solution)/shard_map/ppermute | solution.py:426
  53.1 4.7 %collective-permute-start.17 = (bf16[320,128]{1,0:T(8,128)(2,1)S(1)}, bf16[320,128]{1,0:T(8,128)(2,1)S(1)}, u32[]{:S(2)}, u32[]{:S(2)}) collective-permute-start(bf16[320,128]{1,0:T(8,128)(2,1)S(1)} %get-tuple-element.72), channel_id=1, source_target_pairs={{0,4},{1,5},{2,6},{3,7},{4,0},{5,1},{6,2},{7,3},{8,12},{9,13},{10,... | collective-permute-start | bytes 245768 | tf_op jit(solution)/shard_map/ppermute | solution.py:426
  54.6 6.3 %collective-permute-start.19 = (bf16[320,128]{1,0:T(8,128)(2,1)S(1)}, bf16[320,128]{1,0:T(8,128)(2,1)S(1)}, u32[]{:S(2)}, u32[]{:S(2)}) collective-permute-start(bf16[320,128]{1,0:T(8,128)(2,1)S(1)} %get-tuple-element.73), channel_id=1, source_target_pairs={{0,12},{1,13},{2,14},{3,15},{4,8},{5,9},{6,10},{7,11},{8,4},{9,5},... | collective-permute-start | bytes 245768 | tf_op jit(solution)/shard_map/ppermute | solution.py:426
  61.5 8.0 %collective-permute-start.21 = (bf16[208,768]{1,0:T(8,128)(2,1)S(1)}, bf16[208,768]{1,0:T(8,128)(2,1)S(1)}, u32[]{:S(2)}, u32[]{:S(2)}) collective-permute-start(bf16[208,768]{1,0:T(8,128)(2,1)S(1)} %get-tuple-element.76.refs_5_.refs_1_), channel_id=1, source_target_pairs={{0,2},{1,3},{2,0},{3,1},{4,6},{5,7},{6,4},{7,5},{8,10},{9,11},{10,... | collective-permute-start | bytes 958472 | tf_op jit(solution)/shard_map/ppermute | solution.py:426
  62.7 1.9 %collective-permute-start.25 = (bf16[128,1024]{1,0:T(8,128)(2,1)S(1)}, bf16[128,1024]{1,0:T(8,128)(2,1)S(1)}, u32[]{:S(2)}, u32[]{:S(2)}) collective-permute-start(bf16[128,1024]{1,0:T(8,128)(2,1)S(1)} %collective-permute-done.20.refs_9_.refs_6_), channel_id=1, source_target_pairs={{0,1},{1,0},{2,3},{3,2},{4,5},{5,4},{6,7},{7,6},{8,9},{9,8},{10,11... | collective-permute-start | bytes 786440 | tf_op jit(solution)/shard_map/ppermute | solution.py:426
  63.2 15.3 %collective-permute-start.23 = (bf16[208,768]{1,0:T(8,128)(2,1)S(1)}, bf16[208,768]{1,0:T(8,128)(2,1)S(1)}, u32[]{:S(2)}, u32[]{:S(2)}) collective-permute-start(bf16[208,768]{1,0:T(8,128)(2,1)S(1)} %get-tuple-element.76.refs_5_.refs_1_), channel_id=1, source_target_pairs={{0,1},{1,0},{2,3},{3,2},{4,5},{5,4},{6,7},{7,6},{8,9},{9,8},{10,11... | collective-permute-start | bytes 958472 | tf_op jit(solution)/shard_map/ppermute | solution.py:426
  69.6 15.4 %collective-permute-start.26 = (bf16[208,768]{1,0:T(8,128)(2,1)S(1)}, bf16[208,768]{1,0:T(8,128)(2,1)S(1)}, u32[]{:S(2)}, u32[]{:S(2)}) collective-permute-start(bf16[208,768]{1,0:T(8,128)(2,1)S(1)} %relay.1), channel_id=1, source_target_pairs={{0,1},{1,0},{2,3},{3,2},{4,5},{5,4},{6,7},{7,6},{8,9},{9,8},{10,11... | collective-permute-start | bytes 958472 | tf_op jit(solution)/shard_map/ppermute | solution.py:426
  69.7 7.4 %collective-permute-start.22 = (bf16[16,768]{1,0:T(8,128)(2,1)S(1)}, bf16[16,768]{1,0:T(8,128)(2,1)S(1)}, u32[]{:S(2)}, u32[]{:S(2)}) collective-permute-start(bf16[16,768]{1,0:T(8,128)(2,1)S(1)} %get-tuple-element.77), channel_id=1, source_target_pairs={{2,4},{6,8},{10,12},{4,2},{8,6},{12,10},{3,5},{7,9},{11,13},{5,3},... | collective-permute-start | bytes 73736 | tf_op jit(solution)/shard_map/ppermute | solution.py:572
  70.3 8.2 %collective-permute-start.27 = (bf16[48,1024]{1,0:T(8,128)(2,1)S(1)}, bf16[48,1024]{1,0:T(8,128)(2,1)S(1)}, u32[]{:S(2)}, u32[]{:S(2)}) collective-permute-start(bf16[48,1024]{1,0:T(8,128)(2,1)S(1)} %get-tuple-element.80), channel_id=1, source_target_pairs={{0,4},{1,5},{2,6},{3,7},{4,0},{5,1},{6,2},{7,3},{8,12},{9,13},{10,... | collective-permute-start | bytes 294920 | tf_op jit(solution)/shard_map/ppermute | solution.py:426
  74.1 10.9 %collective-permute-start.28 = (bf16[48,1024]{1,0:T(8,128)(2,1)S(1)}, bf16[48,1024]{1,0:T(8,128)(2,1)S(1)}, u32[]{:S(2)}, u32[]{:S(2)}) collective-permute-start(bf16[48,1024]{1,0:T(8,128)(2,1)S(1)} %get-tuple-element.81), channel_id=1, source_target_pairs={{0,8},{1,9},{2,10},{3,11},{4,12},{5,13},{6,14},{7,15},{8,0},{9,1},... | collective-permute-start | bytes 294920 | tf_op jit(solution)/shard_map/ppermute | solution.py:426
  77.1 7.8 %collective-permute-start.29 = (bf16[48,1024]{1,0:T(8,128)(2,1)S(1)}, bf16[48,1024]{1,0:T(8,128)(2,1)S(1)}, u32[]{:S(2)}, u32[]{:S(2)}) collective-permute-start(bf16[48,1024]{1,0:T(8,128)(2,1)S(1)} %get-tuple-element.82), channel_id=1, source_target_pairs={{0,12},{1,13},{2,14},{3,15},{4,8},{5,9},{6,10},{7,11},{8,4},{9,5},... | collective-permute-start | bytes 294920 | tf_op jit(solution)/shard_map/ppermute | solution.py:426
  86.4 10.6 %collective-permute-start.30 = (bf16[144,768]{1,0:T(8,128)(2,1)S(1)}, bf16[144,768]{1,0:T(8,128)(2,1)S(1)}, u32[]{:S(2)}, u32[]{:S(2)}) collective-permute-start(bf16[144,768]{1,0:T(8,128)(2,1)S(1)} %get-tuple-element.84), channel_id=1, source_target_pairs={{0,4},{1,5},{2,6},{3,7},{4,0},{5,1},{6,2},{7,3},{8,12},{9,13},{10,... | collective-permute-start | bytes 663560 | tf_op jit(solution)/shard_map/ppermute | solution.py:426
  88.3 18.7 %collective-permute-start.31 = (bf16[144,768]{1,0:T(8,128)(2,1)S(1)}, bf16[144,768]{1,0:T(8,128)(2,1)S(1)}, u32[]{:S(2)}, u32[]{:S(2)}) collective-permute-start(bf16[144,768]{1,0:T(8,128)(2,1)S(1)} %get-tuple-element.85), channel_id=1, source_target_pairs={{0,8},{1,9},{2,10},{3,11},{4,12},{5,13},{6,14},{7,15},{8,0},{9,1},... | collective-permute-start | bytes 663560 | tf_op jit(solution)/shard_map/ppermute | solution.py:426
  89.5 17.6 %collective-permute-start.32 = (bf16[144,768]{1,0:T(8,128)(2,1)S(1)}, bf16[144,768]{1,0:T(8,128)(2,1)S(1)}, u32[]{:S(2)}, u32[]{:S(2)}) collective-permute-start(bf16[144,768]{1,0:T(8,128)(2,1)S(1)} %get-tuple-element.86), channel_id=1, source_target_pairs={{0,12},{1,13},{2,14},{3,15},{4,8},{5,9},{6,10},{7,11},{8,4},{9,5},... | collective-permute-start | bytes 663560 | tf_op jit(solution)/shard_map/ppermute | solution.py:426
  (9 other events, 65.2 us)

commit v3 on v2

--- a/solution.py
+++ b/solution.py
@@ -110,7 +110,9 @@
     normed = (pooled * inv * gain[...]).astype(BF)
     pooled_out[...] = pooled
     normed_out[...] = normed
-    kv_out[...] = pack_kv(dot(normed, wk[...]), dot_t(normed, wv[...])).astype(BF)
+    packed = pack_kv(dot(normed, wk[...]), dot_t(normed, wv[...])).astype(BF)
+    for i in range(kv_out.shape[0]):
+        kv_out[i] = packed
     early[0:ext] = every_second(pad, 6, ext).astype(BF)
     early[ext : 2 * ext] = every_second(pad, 7, ext).astype(BF)
 
@@ -158,13 +160,12 @@
 
 
 def attend_first_kernel(*refs, blocks, heads, key_size, value_size, scale):
-    q, cot = refs[:2]
-    parts = refs[2 : 2 + blocks]
-    att, dq, ks, vs, kt, vt, dk, dv = refs[2 + blocks :]
+    q, cot, parts, att, dq, ks, vs, kt, vt, dk, dv = refs
     tokens = q.shape[0]
     half = tokens // 2
     wide = value_size - key_size
-    for i, part in enumerate(parts):
+    for i in range(blocks):
+        part = parts[i]
         at = i * tokens
         ks[at : at + tokens] = part[:tokens]
         vs[at : at + tokens, :key_size] = part[tokens : 2 * tokens]
@@ -180,7 +181,7 @@
 
 def attend_second_kernel(*refs, blocks, heads, key_size, value_size, scale):
     q, cot, att_in, ks, vs, kt, vt, dk_in, dv_in = refs[:9]
-    att, dq, near, far_first, far_last, dk, dv = refs[9:]
+    att, dq, terms, dk, dv = refs[9:]
     tokens = q.shape[0]
     att[:, : att_in.shape[1]] = att_in[...]
     for pair in range(heads // 4, heads // 2):
@@ -190,72 +191,50 @@
         attend_pair(
             pair, q, cot, ks, vs, kt, vt, dk, dv, att, dq, key_size, value_size, scale, False
         )
-    count = blocks // 2
-    half = count // 2
     for i in range(blocks):
         at = slice(i * tokens, (i + 1) * tokens)
-        packed = pack_kv(dk[at], dv[at])
-        k = i - count
-        if k < 0:
-            near[i] = packed
-        elif k < half:
-            far_last[k] = packed.astype(BF)
-        else:
-            far_first[k - half] = packed.astype(BF)
-
-
-def add_kernel(near, far, *outs, start):
-    for k, out in enumerate(outs):
-        out[...] = (near[start + k] + far[k].astype(F32)).astype(out.dtype)
-
-
-def add_near_kernel(near, far, left, right, both, *outs):
+        terms[i] = pack_kv(dk[at], dv[at]).astype(BF)
+
+
+def query_cot_kernel(left, right, wq, both, out):
     both[:, : left.shape[1]] = left[...]
     both[:, left.shape[1] :] = right[...]
-    add_kernel(near, far, *outs, start=0)
-
-
-def query_cot_kernel(dq, wq, out):
-    out[...] = dot_t(dq[...], wq[...])
-
-
-def make_middle(count):
-    def middle(*refs):
-        own, others = refs[0], refs[1:count]
-        part, pooled_in, gain_in, wk, wv, message, edge = refs[count:]
-        size = own.shape[1]
-        tokens, width = pooled_in.shape
-        total = own[...]
-        for other in others:
-            total = total + other[...].astype(F32)
-        total = total.astype(BF).astype(F32)
-        key_cot = total[:tokens]
-        value_cot = unpack_values(total, tokens, size)
-        normed_cot = part[...] + dot_t(key_cot.astype(BF), wk[...])
-        normed_cot = normed_cot + dot(value_cot.astype(BF), wv[...])
-        pooled, gain = pooled_in[...], gain_in[...]
-        inv = lax.rsqrt(jnp.mean(pooled * pooled, axis=-1, keepdims=True) + EPS)
-        gain_term = jnp.sum(normed_cot * pooled * inv, axis=0, keepdims=True)
-        gained = gain * normed_cot
-        pooled_cot = inv * gained - pooled * (inv * inv * inv) * (
-            jnp.sum(gained * pooled, axis=-1, keepdims=True) / width
-        )
-        conv_cot = 0.5 * pooled_cot
-        high = gain_term.astype(BF).astype(F32)
-        low = gain_term - high
-        row = lax.broadcasted_iota(jnp.int32, (16, width), 0)
-        gains = jnp.where(row == 0, high, jnp.where(row == 1, low, 0.0))
-        both = jnp.concatenate([key_cot, value_cot], axis=1)
-        fill = width // 2 - both.shape[1]
-        both = jnp.concatenate([both, jnp.zeros((tokens, fill), F32)], axis=1)
-        side = jnp.concatenate([both[: tokens // 2], both[tokens // 2 :]], axis=1)
-        message[:tokens] = conv_cot.astype(BF)
-        message[tokens : tokens + 16] = gains.astype(BF)
-        message[tokens + 16 :] = side.astype(BF)
-        ends = jnp.where(row == 0, conv_cot[:1], jnp.where(row == 1, conv_cot[tokens - 1 :], 0.0))
-        edge[...] = ends.astype(BF)
-
-    return middle
+    out[...] = dot_t(both[...], wq[...])
+
+
+def middle_kernel(terms, part, pooled_in, gain_in, wk, wv, near, message, edge, near_out):
+    near_out[...] = near[...]
+    size = terms.shape[2]
+    tokens, width = pooled_in.shape
+    total = terms[0].astype(F32)
+    for i in range(1, terms.shape[0]):
+        total = total + terms[i].astype(F32)
+    total = total.astype(BF).astype(F32)
+    key_cot = total[:tokens]
+    value_cot = unpack_values(total, tokens, size)
+    normed_cot = part[...] + dot_t(key_cot.astype(BF), wk[...])
+    normed_cot = normed_cot + dot(value_cot.astype(BF), wv[...])
+    pooled, gain = pooled_in[...], gain_in[...]
+    inv = lax.rsqrt(jnp.mean(pooled * pooled, axis=-1, keepdims=True) + EPS)
+    gain_term = jnp.sum(normed_cot * pooled * inv, axis=0, keepdims=True)
+    gained = gain * normed_cot
+    pooled_cot = inv * gained - pooled * (inv * inv * inv) * (
+        jnp.sum(gained * pooled, axis=-1, keepdims=True) / width
+    )
+    conv_cot = 0.5 * pooled_cot
+    high = gain_term.astype(BF).astype(F32)
+    low = gain_term - high
+    row = lax.broadcasted_iota(jnp.int32, (16, width), 0)
+    gains = jnp.where(row == 0, high, jnp.where(row == 1, low, 0.0))
+    both = jnp.concatenate([key_cot, value_cot], axis=1)
+    fill = width // 2 - both.shape[1]
+    both = jnp.concatenate([both, jnp.zeros((tokens, fill), F32)], axis=1)
+    side = jnp.concatenate([both[: tokens // 2], both[tokens // 2 :]], axis=1)
+    message[:tokens] = conv_cot.astype(BF)
+    message[tokens : tokens + 16] = gains.astype(BF)
+    message[tokens + 16 :] = side.astype(BF)
+    ends = jnp.where(row == 0, conv_cot[:1], jnp.where(row == 1, conv_cot[tokens - 1 :], 0.0))
+    edge[...] = ends.astype(BF)
 
 
 def place(other=0):
@@ -305,14 +284,6 @@
     pick = jnp.concatenate([part[...] for part in picks], axis=1)
     for k, out in enumerate(outs):
         out[...] = dot(pick[k * pad : (k + 1) * pad], right[...]).astype(out.dtype)
-
-
-def query_sum_kernel(*refs):
-    parts, out = refs[:-1], refs[-1]
-    total = parts[0][...]
-    for part in parts[1:]:
-        total = total + part[...].astype(F32)
-    out[...] = total[: out.shape[0]]
 
 
 def chunk_layout(conv_rows, norm_rows, width, key_size, value_size):
@@ -355,12 +326,18 @@
         out[...] = stage[...].astype(out.dtype)
 
 
-def final_kernel(*refs):
-    parts = refs[:-5]
-    conv, key, value, gain, stage = refs[-5:]
+def summed(parts):
     total = parts[0][...]
     for part in parts[1:]:
         total = total + part[...].astype(F32)
+    return total
+
+
+def final_kernel(*refs):
+    conv, query, key, value, gain, stage = refs[-6:]
+    count = len(refs[:-6]) // 2
+    total = summed(refs[:count])
+    query[...] = summed(refs[count : 2 * count])[: query.shape[0]]
     rows, width = conv.shape
     count = key.shape[0]
     stage[...] = total
@@ -440,7 +417,7 @@
     kv, early, normed, pooled = run(
         front_kernel,
         [
-            ((5 * tokens // 2, key_size), BF),
+            ((devices, 5 * tokens // 2, key_size), BF),
             ((2 * ext, channels), BF),
             ((tokens, width), BF),
             ((tokens, width), F32),
@@ -450,8 +427,7 @@
         flops=2 * positions * taps * channels * width,
         name="front",
     )
-    near_kv = [kv] + [swap(kv, 2 * k) for k in range(1, groups)]
-    far_kv = [swap(block, 1) for block in near_kv]
+    kv = lax.all_to_all(kv, "seq", 0, 0, tiled=True)
     queries, early, *picks = run(
         lambda *refs: query_kernel(
             *refs, groups=groups, rows=norm_rows, padded=norm_pad, scale=scale
@@ -484,22 +460,18 @@
             ((value_size, length), BF),
         ]
         + totals,
-        [queries, cotangent] + near_kv + far_kv,
+        [queries, cotangent, kv],
         flops=attend_flops,
         name="attend_first",
     )
     early_near, early_core = swap(early, 1), swap(early, 0, 1)
     norm_picks = [picks[0], swap(picks[1], 0, 1), swap(picks[2], 1), swap(picks[3], 1, 1)]
-    block_shape = (5 * tokens // 2, key_size)
-    split = groups // 2
-    attended, dq_second, near_cot, far_first, far_last = run(
+    attended, dq_second, terms = run(
         lambda *refs: attend_second_kernel(*refs, **sizes),
         [
             ((tokens, heads * value_size), BF),
             ((tokens, half_query), BF),
-            ((groups,) + block_shape, F32),
-            ((groups - split,) + block_shape, BF),
-            ((split,) + block_shape, BF),
+            (kv.shape, BF),
         ],
         [queries, cotangent, att_first] + held,
         [pltpu.VMEM(s, t) for s, t in totals],
@@ -507,8 +479,6 @@
         name="attend_second",
         after=[early_near, early_core] + norm_picks[1:],
     )
-    far_first = swap(far_first, 1)
-    far_last = swap(far_last, 1)
     early_blocks = [early, early_core, early_near, swap(early_near, 0, 1)]
     (conv_pick,) = run(
         lambda *refs: select_kernel(*refs, groups=groups, rows=conv_rows, padded=conv_pad),
@@ -518,30 +488,27 @@
         flops=2 * groups * conv_pad * taps * channels * 8 * tokens,
         name="select",
     )
-    last = run(
-        lambda *refs: add_kernel(*refs, start=split),
-        [(block_shape, BF)] * (groups - split),
-        [near_cot, far_first],
-        name="kv_cot_far",
-        after=[conv_pick],
-    )
-    query_cot, own, *others = run(
-        add_near_kernel,
-        [((tokens, heads * key_size), BF), (block_shape, F32)] + [(block_shape, BF)] * (split - 1),
-        [near_cot, far_last, dq_first, dq_second],
-        name="kv_cot_near",
-        after=[last[0]],
-    )
-    others = others + list(last)
-    arrived = [swap(other, 2 * (k + 1)) for k, other in enumerate(others)]
-    (normed_cot,) = run(
+    query_cot, normed_cot = run(
         query_cot_kernel,
-        [((tokens, width), F32)],
-        [query_cot, wq],
+        [((tokens, heads * key_size), BF), ((tokens, width), F32)],
+        [dq_first, dq_second, wq],
         flops=2 * tokens * width * heads * key_size,
         name="query_part",
     )
-    query_blocks = quad(query_cot)
+    terms = lax.all_to_all(terms, "seq", 0, 0, tiled=True)
+    query_near = swap(query_cot, 1)
+    message, edge, query_relay = run(
+        middle_kernel,
+        [
+            ((tokens + 16 + tokens // 2, width), BF),
+            ((16, width), BF),
+            (query_near.shape, BF),
+        ],
+        [terms, normed_cot, pooled, gain, wk, wv, query_near],
+        flops=2 * tokens * width * (key_size + value_size),
+        name="conv_cot",
+    )
+    query_blocks = [query_cot, swap(query_cot, 0, 1), query_near, swap(query_relay, 0, 1)]
     query_parts = run(
         lambda *refs: query_grad_kernel(*refs, pad=norm_pad),
         [((norm_pad, heads * key_size), F32 if k == 0 else BF) for k in range(groups)],
@@ -550,27 +517,19 @@
         flops=2 * groups * norm_pad * 4 * tokens * heads * key_size,
         name="query_grad",
     )
-    message, edge = run(
-        make_middle(groups),
-        [((tokens + 16 + tokens // 2, width), BF), ((16, width), BF)],
-        [own] + arrived + [normed_cot, pooled, gain, wk, wv],
-        flops=2 * tokens * width * (key_size + value_size),
-        name="conv_cot",
-        after=[query_blocks[2]],
-    )
+    query_in = [swap(part, 2 * (k + 1)) for k, part in enumerate(query_parts[1:])]
     near_message = swap(message, 1)
     (relay,) = run(
         relay_kernel,
         [(message.shape, BF)],
         [near_message],
         name="relay",
-        after=[query_parts[0]],
+        after=[query_in[1], conv_pick],
     )
     blocks = [message, swap(message, 0, 1), near_message, swap(relay, 0, 1)]
     crossing = [(i, i + 1) for i in range(1, devices - 1, 2)]
     crossing = crossing + [(j, i) for i, j in crossing]
     edge_in = lax.ppermute(edge, "seq", crossing)
-    query_in = [swap(part, 2 * (k + 1)) for k, part in enumerate(query_parts[1:])]
     _, _, gain_at = chunk_layout(conv_rows, norm_rows, width, key_size, value_size)
     chunk = (round_up(gain_at + 2, 16), width)
     conv_parts = run(
@@ -592,7 +551,7 @@
         ],
         flops=2 * groups * conv_pad * 8 * tokens * width,
         name="conv_grad",
-        after=[edge_in] + query_in,
+        after=[edge_in, query_in[0]],
     )
     conv_in = [swap(part, 2 * (k + 1)) for k, part in enumerate(conv_parts[1:])]
     (input_grad,) = run(
@@ -607,24 +566,18 @@
         name="input_grad",
         after=[conv_parts[0]],
     )
-    (query_grad,) = run(
-        query_sum_kernel,
-        [((norm_rows, heads * key_size), F32)],
-        [query_parts[0]] + query_in,
-        name="query_sum",
-        after=[conv_parts[0]],
-    )
-    conv_grad, key_grad, value_grad, gain_grad = run(
+    conv_grad, query_grad, key_grad, value_grad, gain_grad = run(
         final_kernel,
         [
             ((conv_rows, width), F32),
+            ((norm_rows, heads * key_size), F32),
             ((norm_rows, key_size), F32),
             ((norm_rows, value_size), F32),
             ((1, norm_rows), F32),
         ],
-        [conv_parts[0]] + conv_in,
+        [conv_parts[0]] + conv_in + [query_parts[0]] + query_in,
         [pltpu.VMEM(chunk, F32)],
-        name="conv_sum",
+        name="final_sum",
     )
     return (
         attended[None],

time: 109 us -> 125 us (1.15)
  the two profiles are of different devices: /device:TPU:0 before, /device:TPU:10 now
where the time goes in v3:
time: 125 us; the launch traced here: 124 us
  waiting for transfers between devices  42.2 us (34%)
  starting transfers between devices  34.8 us (28%)
  Pallas kernels  25.1 us (20%)
  local copies, waits for them, and re-layouts  20.6 us (16%)
    ppermute x18, waiting for transfers between devices, swap(): lax.ppermute(value, both_axes, [(i, i ^ mask) for i in range(owners)])  30.6 us
    pallas_call x13, Pallas kernels, run(): pl.pallas_call(whole, out_shape=[jax.ShapeDtypeStruct(s, t) for s, t in o...  25.1 us
    unnamed x58, local copies, waits for them, and re-layouts  19.9 us
    ppermute x18, starting transfers between devices, swap(): lax.ppermute(value, both_axes, [(i, i ^ mask) for i in range(owners)])  14.9 us
    all_to_all x1, waiting for transfers between devices, on_device(): kv = lax.all_to_all(kv, 'seq', 0, 0, tiled=True)  6.85 us
    all_to_all x1, starting transfers between devices, on_device(): kv = lax.all_to_all(kv, 'seq', 0, 0, tiled=True)  5.48 us
    all_to_all x1, starting transfers between devices, on_device(): terms = lax.all_to_all(terms, 'seq', 0, 0, tiled=True)  5.47 us
    ppermute x1, waiting for transfers between devices, on_device(): edge_in = lax.ppermute(edge, 'seq', crossing)  4.31 us
  transfers between devices with their start and end apart: 23, of which 8 were waited for; matrix products, arithmetic and copies ran while one was open for 0% of the time, Pallas kernels for 13%

profile of v3, /device:TPU:10, one launch (start us, length us, event | category | flops | bytes accessed | tf_op | source)
XLA Modules:
  0.0 123.7 jit_solution(1634273870942256409)
XLA Ops:
  1.3 3.4 %collective-permute-start = (bf16[2,384]{1,0:T(2,128)(2,1)S(1)}, bf16[2,384]{1,0:T(2,128)(2,1)S(1)}, u32[]{:S(2)}, u32[]{:S(2)}) collective-permute-start(bf16[2,384]{1,0:T(2,128)(2,1)S(1)} %get-tuple-element.86), channel_id=1, source_target_pairs={{0,2},{2,4},{4,6},{6,8},{8,10},{10,12},{12,14},{1,3},{3,5},{5,7},{... | collective-permute-start | bytes 4616 | tf_op jit(solution)/shard_map/ppermute | solution.py:412
  4.8 3.3 %collective-permute-start.1 = (bf16[2,384]{1,0:T(2,128)(2,1)S(1)}, bf16[2,384]{1,0:T(2,128)(2,1)S(1)}, u32[]{:S(2)}, u32[]{:S(2)}) collective-permute-start(bf16[2,384]{1,0:T(2,128)(2,1)S(1)} %get-tuple-element.85), channel_id=1, source_target_pairs={{2,0},{4,2},{6,4},{8,6},{10,8},{12,10},{14,12},{3,1},{5,3},{7,5},{... | collective-permute-start | bytes 4616 | tf_op jit(solution)/shard_map/ppermute | solution.py:413
  10.9 1.8 %front.1 = (bf16[8,320,128]{2,1,0:T(8,128)(2,1)S(1)}, bf16[288,384]{1,0:T(8,128)(2,1)S(1)}, bf16[128,768]{1,0:T(8,128)(2,1)S(1)}, f32[128,768]{1,0:T(8,128)S(1)}) custom-call(f32[3,304,128]{2,1,0:T(8,128)S(1)} %gelu.1.refs_0_, bf16[2,384]{1,0:T(2,128)(2,1)S(1)} %collective-permute-done.refs_1_, bf16[2,384]{1,0:T(2,128)(2,1)S(1)} %collective-permute-done.1.refs_2_, ...), custom_call_target="tpu_custom_call" | custom-call | flops 754974720 | bytes 5380096 | tf_op jit(solution)/shard_map/front/pallas_call | solution.py:36
  15.8 5.5 %all-to-all-start = ((bf16[8,320,128]{2,1,0:T(8,128)(2,1)}), bf16[8,320,128]{2,1,0:T(8,128)(2,1)}, u32[]{:S(2)}, u32[]{:S(2)}) async-start(bf16[8,320,128]{2,1,0:T(8,128)(2,1)} %copy-done.6), calls=%async_computation | async-start | bytes 1310720 | tf_op jit(solution)/shard_map/all_to_all | solution.py:430
  21.3 1.4 %copy-done.1 = bf16[768,1024]{1,0:T(8,128)(2,1)S(1)} copy-done((bf16[768,1024]{1,0:T(8,128)(2,1)S(1)}, bf16[768,1024]{1,0:T(8,128)(2,1)}, u32[]{:S(2)}) %copy-start.1) | copy-done | bytes 1572888
  24.5 1.3 %queries.1 = (bf16[128,1024]{1,0:T(8,128)(2,1)S(1)}, bf16[288,384]{1,0:T(8,128)(2,1)}, bf16[192,128]{1,0:T(8,128)(2,1)S(1)}, bf16[192,128]{1,0:T(8,128)(2,1)}, b...) custom-call(bf16[128,768]{1,0:T(8,128)(2,1)S(1)} %copy-done.18, bf16[768,1024]{1,0:T(8,128)(2,1)S(1)} %copy-done.1, ...), custom_call_target="tpu_custom_call" | custom-call | flops 402653184 | bytes 2670592 | tf_op jit(solution)/shard_map/queries/pallas_call | solution.py:36
  26.5 1.5 %collective-permute-start.2 = (bf16[288,384]{1,0:T(8,128)(2,1)}, bf16[288,384]{1,0:T(8,128)(2,1)}, u32[]{:S(2)}, u32[]{:S(2)}) collective-permute-start(bf16[288,384]{1,0:T(8,128)(2,1)} %get-tuple-element.57.refs_0_), channel_id=1, source_target_pairs={{0,2},{1,3},{2,0},{3,1},{4,6},{5,7},{6,4},{7,5},{8,10},{9,11},{10,... | collective-permute-start | bytes 663560 | tf_op jit(solution)/shard_map/ppermute | solution.py:403
  29.8 6.8 %all-to-all-done.refs_2_ = bf16[8,320,128]{2,1,0:T(8,128)(2,1)} async-done(((bf16[8,320,128]{2,1,0:T(8,128)(2,1)}), bf16[8,320,128]{2,1,0:T(8,128)(2,1)}, u32[]{:S(2)}, u32[]{:S(2)}) %all-to-all-start) | async-done | bytes 655392 | tf_op jit(solution)/shard_map/all_to_all | solution.py:430
  36.7 1.0 copy-done.8
  37.7 4.4 %attend_first.1 = (bf16[128,768]{1,0:T(8,128)(2,1)S(1)}, bf16[128,512]{1,0:T(8,128)(2,1)S(1)}, bf16[1024,128]{1,0:T(8,128)(2,1)S(1)}, bf16[1024,192]{1,0:T(8,128...) custom-call(bf16[128,1024]{1,0:T(8,128)(2,1)S(1)} %get-tuple-element, ...), custom_call_target="tpu_custom_call" | custom-call | flops 1006632960 | bytes 4259840 | tf_op jit(solution)/shard_map/attend_first/pallas_call | solution.py:36
  42.1 4.0 %attend_second.1 = (bf16[128,1536]{1,0:T(8,128)(2,1)}, bf16[128,512]{1,0:T(8,128)(2,1)S(1)}, bf16[8,320,128]{2,1,0:T(8,128)(2,1)S(1)}) custom-call(bf16[128,1024]{1,0:T(8,128)(2,1)S(1)} %get-tuple-element.48.refs_0_, bf16[128,1536]{1,0:T(8,128)(2,1)S(1)} %bitcast.13, bf16[128,768]{1,0:T(8,128)(2,1)S(1)} %get-tuple-element.50.refs_2_, ...), custom_call_target="tpu_custom_call" | custom-call | flops 1006632960 | bytes 4653056 | tf_op jit(solution)/shard_map/attend_second/pallas_call | solution.py:36
  47.6 5.5 %all-to-all-start.1 = ((bf16[8,320,128]{2,1,0:T(8,128)(2,1)}), bf16[8,320,128]{2,1,0:T(8,128)(2,1)}, u32[]{:S(2)}, u32[]{:S(2)}) async-start(bf16[8,320,128]{2,1,0:T(8,128)(2,1)} %copy-done.7), calls=%async_computation.1 | async-start | bytes 1310720 | tf_op jit(solution)/shard_map/all_to_all | solution.py:498
  53.1 1.4 %copy-done.2 = bf16[768,1024]{1,0:T(8,128)(2,1)S(1)} copy-done((bf16[768,1024]{1,0:T(8,128)(2,1)S(1)}, bf16[768,1024]{1,0:T(8,128)(2,1)}, u32[]{:S(2)}) %copy-start.2) | copy-done | bytes 1572888
  56.3 1.2 query_part.1
  58.2 1.5 %collective-permute-start.7 = (bf16[128,1024]{1,0:T(8,128)(2,1)}, bf16[128,1024]{1,0:T(8,128)(2,1)S(1)}, u32[]{:S(2)}, u32[]{:S(2)}) collective-permute-start(bf16[128,1024]{1,0:T(8,128)(2,1)} %get-tuple-element.67.refs_4_), channel_id=1, source_target_pairs={{0,2},{1,3},{2,0},{3,1},{4,6},{5,7},{6,4},{7,5},{8,10},{9,11},{10,... | collective-permute-start | bytes 786440 | tf_op jit(solution)/shard_map/ppermute | solution.py:403
  59.7 9.3 %collective-permute-done.7.refs_6_ = bf16[128,1024]{1,0:T(8,128)(2,1)S(1)} collective-permute-done((bf16[128,1024]{1,0:T(8,128)(2,1)}, bf16[128,1024]{1,0:T(8,128)(2,1)S(1)}, u32[]{:S(2)}, u32[]{:S(2)}) %collective-permute-start.7) | collective-permute-done | bytes 262176 | tf_op jit(solution)/shard_map/ppermute | solution.py:403
  69.9 1.0 copy-done.10
  70.9 1.0 copy-done.12
  72.6 1.5 %conv_cot.1 = (bf16[208,768]{1,0:T(8,128)(2,1)S(1)}, bf16[16,768]{1,0:T(8,128)(2,1)S(1)}, bf16[128,1024]{1,0:T(8,128)(2,1)S(1)}) custom-call(bf16[8,320,128]{2,1,0:T(8,128)(2,1)} %all-to-all-done.1.refs_0_, f32[128,768]{1,0:T(8,128)S(1)} %copy-done.12, f32[128,768]{1,0:T(8,128)S(1)} %copy-done.10, f32[1,768]{1,0:T(1,128)S(1)} %copy-done.27, ...), custom_call_target="tpu_custom_call" | custom-call | flops 62914560 | bytes 2804736 | tf_op jit(solution)/shard_map/conv_cot/pallas_call | solution.py:36
  74.7 1.0 collective-permute-done.13.refs_7_
  76.5 1.9 %query_grad.1 = (f32[48,1024]{1,0:T(8,128)S(1)}, bf16[48,1024]{1,0:T(8,128)(2,1)S(1)}, bf16[48,1024]{1,0:T(8,128)(2,1)S(1)}, bf16[48,1024]{1,0:T(8,128)(2,1)S(1)}) custom-call(bf16[192,128]{1,0:T(8,128)(2,1)S(1)} %copy-done.24, bf16[192,128]{1,0:T(8,128)(2,1)S(1)} %collective-permute-done.4.refs_11_.refs_1_.refs_2_, ...), custom_call_target="tpu_custom_call" | custom-call | flops 201326592 | bytes 1736704 | tf_op jit(solution)/shard_map/query_grad/pallas_call | solution.py:36
  78.5 1.8 %collective-permute-start.14 = (bf16[48,1024]{1,0:T(8,128)(2,1)S(1)}, bf16[48,1024]{1,0:T(8,128)(2,1)S(1)}, u32[]{:S(2)}, u32[]{:S(2)}) collective-permute-start(bf16[48,1024]{1,0:T(8,128)(2,1)S(1)} %get-tuple-element.72), channel_id=1, source_target_pairs={{0,8},{1,9},{2,10},{3,11},{4,12},{5,13},{6,14},{7,15},{8,0},{9,1},... | collective-permute-start | bytes 294920 | tf_op jit(solution)/shard_map/ppermute | solution.py:403
  80.3 3.5 %select.1.refs_2_.refs_0_ = bf16[512,1024]{1,0:T(8,128)(2,1)S(1)} custom-call(bf16[288,384]{1,0:T(8,128)(2,1)} %get-tuple-element.57.refs_0_, bf16[288,384]{1,0:T(8,128)(2,1)} %collective-permute-done.3.refs_10_.refs_1_, bf16[288,384]{1,0:T(8,128)(2,1)} %collective-permute-done.2.refs_9_.refs_2_, bf16[288,384]{1,0:T(8,128)(2,1)S(1)} %collective-permute-done.10.refs_3_), custom_call_target="tpu_custom_call" | custom-call | flops 2013265920 | bytes 1933312 | tf_op jit(solution)/shard_map/select/pallas_call | solution.py:36
  84.8 2.9 %collective-permute-start.16 = (bf16[48,1024]{1,0:T(8,128)(2,1)S(1)}, bf16[48,1024]{1,0:T(8,128)(2,1)S(1)}, u32[]{:S(2)}, u32[]{:S(2)}) collective-permute-start(bf16[48,1024]{1,0:T(8,128)(2,1)S(1)} %get-tuple-element.73), channel_id=1, source_target_pairs={{0,4},{1,5},{2,6},{3,7},{4,0},{5,1},{6,2},{7,3},{8,12},{9,13},{10,... | collective-permute-start | bytes 294920 | tf_op jit(solution)/shard_map/ppermute | solution.py:403
  87.7 2.3 %collective-permute-start.9 = (bf16[16,768]{1,0:T(8,128)(2,1)S(1)}, bf16[16,768]{1,0:T(8,128)(2,1)S(1)}, u32[]{:S(2)}, u32[]{:S(2)}) collective-permute-start(bf16[16,768]{1,0:T(8,128)(2,1)S(1)} %get-tuple-element.69), channel_id=1, source_target_pairs={{2,4},{6,8},{10,12},{4,2},{8,6},{12,10},{3,5},{7,9},{11,13},{5,3},... | collective-permute-start | bytes 73736 | tf_op jit(solution)/shard_map/ppermute | solution.py:532
  90.0 4.3 %collective-permute-done.9.refs_9_.refs_3_ = bf16[16,768]{1,0:T(8,128)(2,1)S(1)} collective-permute-done((bf16[16,768]{1,0:T(8,128)(2,1)S(1)}, bf16[16,768]{1,0:T(8,128)(2,1)S(1)}, u32[]{:S(2)}, u32[]{:S(2)}) %collective-permute-start.9) | collective-permute-done | bytes 24608 | tf_op jit(solution)/shard_map/ppermute | solution.py:532
  94.4 2.3 %conv_grad.1 = (f32[144,768]{1,0:T(8,128)S(1)}, bf16[144,768]{1,0:T(8,128)(2,1)S(1)}, bf16[144,768]{1,0:T(8,128)(2,1)S(1)}, bf16[144,768]{1,0:T(8,128)(2,1)S(1)}) custom-call(bf16[512,1024]{1,0:T(8,128)(2,1)S(1)} %select.1.refs_2_.refs_0_, bf16[192,128]{1,0:T(8,128)(2,1)S(1)} %copy-done.25, ...), custom_call_target="tpu_custom_call" | custom-call | flops 805306368 | bytes 3629056 | tf_op jit(solution)/shard_map/conv_grad/pallas_call | solution.py:36
  96.7 2.5 %collective-permute-start.18 = (bf16[144,768]{1,0:T(8,128)(2,1)S(1)}, bf16[144,768]{1,0:T(8,128)(2,1)S(1)}, u32[]{:S(2)}, u32[]{:S(2)}) collective-permute-start(bf16[144,768]{1,0:T(8,128)(2,1)S(1)} %get-tuple-element.76), channel_id=1, source_target_pairs={{0,8},{1,9},{2,10},{3,11},{4,12},{5,13},{6,14},{7,15},{8,0},{9,1},... | collective-permute-start | bytes 663560 | tf_op jit(solution)/shard_map/ppermute | solution.py:403
  100.2 1.1 collective-permute-start.20
  101.3 2.0 %input_grad.1 = bf16[256,384]{1,0:T(8,128)(2,1)} custom-call(bf16[256,384]{1,0:T(8,128)(2,1)S(1)} %bitcast.15, bf16[208,768]{1,0:T(8,128)(2,1)S(1)} %get-tuple-element.68.refs_5_.refs_1_, bf16[208,768]{1,0:T(8,128)(2,1)S(1)} %collective-permute-done.8.refs_0_.refs_7_.refs_2_, bf16[16,768]{1,0:T(8,128)(2,1)S(1)} %collective-permute-done.9.refs_9_.refs_3_, ...), custom_call_target="tpu_custom_call" | custom-call | flops 754974720 | bytes 4005888 | tf_op jit(solution)/shard_map/input_grad/pallas_call | solution.py:36
  103.3 19.4 %collective-permute-done.20.refs_7_ = bf16[48,1024]{1,0:T(8,128)(2,1)S(1)} collective-permute-done((bf16[48,1024]{1,0:T(8,128)(2,1)S(1)}, bf16[48,1024]{1,0:T(8,128)(2,1)S(1)}, u32[]{:S(2)}, u32[]{:S(2)}) %collective-permute-start.20) | collective-permute-done | bytes 98336 | tf_op jit(solution)/shard_map/ppermute | solution.py:403
  122.7 1.0 final_sum.1
  (87 shorter events, 19.9 us)
Async XLA Ops:
  1.3 8.4 %collective-permute-start = (bf16[2,384]{1,0:T(2,128)(2,1)S(1)}, bf16[2,384]{1,0:T(2,128)(2,1)S(1)}, u32[]{:S(2)}, u32[]{:S(2)}) collective-permute-start(bf16[2,384]{1,0:T(2,128)(2,1)S(1)} %get-tuple-element.86), channel_id=1, source_target_pairs={{0,2},{2,4},{4,6},{6,8},{8,10},{10,12},{12,14},{1,3},{3,5},{5,7},{... | collective-permute-start | bytes 4616 | tf_op jit(solution)/shard_map/ppermute | solution.py:412
  4.8 5.5 %collective-permute-start.1 = (bf16[2,384]{1,0:T(2,128)(2,1)S(1)}, bf16[2,384]{1,0:T(2,128)(2,1)S(1)}, u32[]{:S(2)}, u32[]{:S(2)}) collective-permute-start(bf16[2,384]{1,0:T(2,128)(2,1)S(1)} %get-tuple-element.85), channel_id=1, source_target_pairs={{2,0},{4,2},{6,4},{8,6},{10,8},{12,10},{14,12},{3,1},{5,3},{7,5},{... | collective-permute-start | bytes 4616 | tf_op jit(solution)/shard_map/ppermute | solution.py:413
  9.0 1.8 %copy-start = (bf16[5,384,768]{2,1,0:T(8,128)(2,1)S(1)}, bf16[5,384,768]{2,1,0:T(8,128)(2,1)}, u32[]{:S(2)}) copy-start(bf16[5,384,768]{2,1,0:T(8,128)(2,1)} %refs_4_.3) | copy-start | bytes 8847364
  9.0 1.9 %copy-start.3 = (bf16[768,192]{0,1:T(8,128)(2,1)S(1)}, bf16[768,192]{0,1:T(8,128)(2,1)}, u32[]{:S(2)}) copy-start(bf16[768,192]{0,1:T(8,128)(2,1)} %param.12) | copy-start | bytes 884740
  9.0 1.9 %copy-start.4 = (bf16[768,128]{1,0:T(8,128)(2,1)S(1)}, bf16[768,128]{1,0:T(8,128)(2,1)}, u32[]{:S(2)}) copy-start(bf16[768,128]{1,0:T(8,128)(2,1)} %refs_4_.2) | copy-start | bytes 589828
  9.7 3.1 %copy-start.26 = (f32[1,768]{1,0:T(1,128)}, f32[1,768]{1,0:T(1,128)S(1)}, u32[]{:S(2)}) copy-start(f32[1,768]{1,0:T(1,128)S(1)} %reshape.22.refs_4_.refs_3_) | copy-start | bytes 9220
  15.8 20.9 %all-to-all-start = ((bf16[8,320,128]{2,1,0:T(8,128)(2,1)}), bf16[8,320,128]{2,1,0:T(8,128)(2,1)}, u32[]{:S(2)}, u32[]{:S(2)}) async-start(bf16[8,320,128]{2,1,0:T(8,128)(2,1)} %copy-done.6), calls=%async_computation | async-start | bytes 1310720 | tf_op jit(solution)/shard_map/all_to_all | solution.py:430
  21.3 1.4 %copy-start.1 = (bf16[768,1024]{1,0:T(8,128)(2,1)S(1)}, bf16[768,1024]{1,0:T(8,128)(2,1)}, u32[]{:S(2)}) copy-start(bf16[768,1024]{1,0:T(8,128)(2,1)} %refs_2_.1) | copy-start | bytes 4718596
  26.5 15.6 %collective-permute-start.2 = (bf16[288,384]{1,0:T(8,128)(2,1)}, bf16[288,384]{1,0:T(8,128)(2,1)}, u32[]{:S(2)}, u32[]{:S(2)}) collective-permute-start(bf16[288,384]{1,0:T(8,128)(2,1)} %get-tuple-element.57.refs_0_), channel_id=1, source_target_pairs={{0,2},{1,3},{2,0},{3,1},{4,6},{5,7},{6,4},{7,5},{8,10},{9,11},{10,... | collective-permute-start | bytes 663560 | tf_op jit(solution)/shard_map/ppermute | solution.py:403
  27.9 14.1 %collective-permute-start.3 = (bf16[288,384]{1,0:T(8,128)(2,1)}, bf16[288,384]{1,0:T(8,128)(2,1)}, u32[]{:S(2)}, u32[]{:S(2)}) collective-permute-start(bf16[288,384]{1,0:T(8,128)(2,1)} %get-tuple-element.57.refs_0_), channel_id=1, source_target_pairs={{0,1},{1,0},{2,3},{3,2},{4,5},{5,4},{6,7},{7,6},{8,9},{9,8},{10,11... | collective-permute-start | bytes 663560 | tf_op jit(solution)/shard_map/ppermute | solution.py:403
  27.9 14.1 %collective-permute-start.4 = (bf16[192,128]{1,0:T(8,128)(2,1)}, bf16[192,128]{1,0:T(8,128)(2,1)S(1)}, u32[]{:S(2)}, u32[]{:S(2)}) collective-permute-start(bf16[192,128]{1,0:T(8,128)(2,1)} %get-tuple-element.58), channel_id=1, source_target_pairs={{0,1},{1,0},{2,3},{3,2},{4,5},{5,4},{6,7},{7,6},{8,9},{9,8},{10,11... | collective-permute-start | bytes 147464 | tf_op jit(solution)/shard_map/ppermute | solution.py:403
  28.5 13.6 %collective-permute-start.5 = (bf16[192,128]{1,0:T(8,128)(2,1)}, bf16[192,128]{1,0:T(8,128)(2,1)}, u32[]{:S(2)}, u32[]{:S(2)}) collective-permute-start(bf16[192,128]{1,0:T(8,128)(2,1)} %get-tuple-element.59), channel_id=1, source_target_pairs={{0,2},{1,3},{2,0},{3,1},{4,6},{5,7},{6,4},{7,5},{8,10},{9,11},{10,... | collective-permute-start | bytes 147464 | tf_op jit(solution)/shard_map/ppermute | solution.py:403
  29.0 13.0 %collective-permute-start.6 = (bf16[192,128]{1,0:T(8,128)(2,1)}, bf16[192,128]{1,0:T(8,128)(2,1)}, u32[]{:S(2)}, u32[]{:S(2)}) collective-permute-start(bf16[192,128]{1,0:T(8,128)(2,1)} %get-tuple-element.60), channel_id=1, source_target_pairs={{0,3},{1,2},{2,1},{3,0},{4,7},{5,6},{6,5},{7,4},{8,11},{9,10},{10,... | collective-permute-start | bytes 147464 | tf_op jit(solution)/shard_map/ppermute | solution.py:403
  42.0 4.1 %copy-start.19 = (bf16[128,512]{1,0:T(8,128)(2,1)}, bf16[128,512]{1,0:T(8,128)(2,1)S(1)}, u32[]{:S(2)}) copy-start(bf16[128,512]{1,0:T(8,128)(2,1)S(1)} %get-tuple-element.63.refs_0_) | copy-start | bytes 393220
  47.6 21.4 %all-to-all-start.1 = ((bf16[8,320,128]{2,1,0:T(8,128)(2,1)}), bf16[8,320,128]{2,1,0:T(8,128)(2,1)}, u32[]{:S(2)}, u32[]{:S(2)}) async-start(bf16[8,320,128]{2,1,0:T(8,128)(2,1)} %copy-done.7), calls=%async_computation.1 | async-start | bytes 1310720 | tf_op jit(solution)/shard_map/all_to_all | solution.py:498
  53.1 1.4 %copy-start.2 = (bf16[768,1024]{1,0:T(8,128)(2,1)S(1)}, bf16[768,1024]{1,0:T(8,128)(2,1)}, u32[]{:S(2)}) copy-start(bf16[768,1024]{1,0:T(8,128)(2,1)} %refs_2_.1) | copy-start | bytes 4718596
  58.2 10.8 %collective-permute-start.7 = (bf16[128,1024]{1,0:T(8,128)(2,1)}, bf16[128,1024]{1,0:T(8,128)(2,1)S(1)}, u32[]{:S(2)}, u32[]{:S(2)}) collective-permute-start(bf16[128,1024]{1,0:T(8,128)(2,1)} %get-tuple-element.67.refs_4_), channel_id=1, source_target_pairs={{0,2},{1,3},{2,0},{3,1},{4,6},{5,7},{6,4},{7,5},{8,10},{9,11},{10,... | collective-permute-start | bytes 786440 | tf_op jit(solution)/shard_map/ppermute | solution.py:403
  59.7 15.0 %collective-permute-start.12 = (bf16[128,1024]{1,0:T(8,128)(2,1)}, bf16[128,1024]{1,0:T(8,128)(2,1)}, u32[]{:S(2)}, u32[]{:S(2)}) collective-permute-start(bf16[128,1024]{1,0:T(8,128)(2,1)} %get-tuple-element.67.refs_4_), channel_id=1, source_target_pairs={{0,1},{1,0},{2,3},{3,2},{4,5},{5,4},{6,7},{7,6},{8,9},{9,8},{10,11... | collective-permute-start | bytes 786440 | tf_op jit(solution)/shard_map/ppermute | solution.py:403
  74.1 1.6 %collective-permute-start.13 = (bf16[128,1024]{1,0:T(8,128)(2,1)S(1)}, bf16[128,1024]{1,0:T(8,128)(2,1)S(1)}, u32[]{:S(2)}, u32[]{:S(2)}) collective-permute-start(bf16[128,1024]{1,0:T(8,128)(2,1)S(1)} %get-tuple-element.71), channel_id=1, source_target_pairs={{0,1},{1,0},{2,3},{3,2},{4,5},{5,4},{6,7},{7,6},{8,9},{9,8},{10,11... | collective-permute-start | bytes 786440 | tf_op jit(solution)/shard_map/ppermute | solution.py:403
  74.2 6.0 %collective-permute-start.10 = (bf16[288,384]{1,0:T(8,128)(2,1)}, bf16[288,384]{1,0:T(8,128)(2,1)S(1)}, u32[]{:S(2)}, u32[]{:S(2)}) collective-permute-start(bf16[288,384]{1,0:T(8,128)(2,1)} %collective-permute-done.2.refs_9_.refs_2_), channel_id=1, source_target_pairs={{0,1},{1,0},{2,3},{3,2},{4,5},{5,4},{6,7},{7,6},{8,9},{9,8},{10,11... | collective-permute-start | bytes 663560 | tf_op jit(solution)/shard_map/ppermute | solution.py:403
  74.7 9.5 %collective-permute-start.8 = (bf16[208,768]{1,0:T(8,128)(2,1)S(1)}, bf16[208,768]{1,0:T(8,128)(2,1)S(1)}, u32[]{:S(2)}, u32[]{:S(2)}) collective-permute-start(bf16[208,768]{1,0:T(8,128)(2,1)S(1)} %get-tuple-element.68.refs_5_.refs_1_), channel_id=1, source_target_pairs={{0,2},{1,3},{2,0},{3,1},{4,6},{5,7},{6,4},{7,5},{8,10},{9,11},{10,... | collective-permute-start | bytes 958472 | tf_op jit(solution)/shard_map/ppermute | solution.py:403
  78.5 15.9 %copy-start.25 = (bf16[192,128]{1,0:T(8,128)(2,1)S(1)}, bf16[192,128]{1,0:T(8,128)(2,1)}, u32[]{:S(2)}) copy-start(bf16[192,128]{1,0:T(8,128)(2,1)} %copy-done.23) | copy-start | bytes 147460
  78.5 6.2 %collective-permute-start.14 = (bf16[48,1024]{1,0:T(8,128)(2,1)S(1)}, bf16[48,1024]{1,0:T(8,128)(2,1)S(1)}, u32[]{:S(2)}, u32[]{:S(2)}) collective-permute-start(bf16[48,1024]{1,0:T(8,128)(2,1)S(1)} %get-tuple-element.72), channel_id=1, source_target_pairs={{0,8},{1,9},{2,10},{3,11},{4,12},{5,13},{6,14},{7,15},{8,0},{9,1},... | collective-permute-start | bytes 294920 | tf_op jit(solution)/shard_map/ppermute | solution.py:403
  83.8 17.5 %copy-start.16 = (bf16[1,256,384]{2,1,0:T(8,128)(2,1)S(1)}, bf16[1,256,384]{2,1,0:T(8,128)(2,1)}, u32[]{:S(2)}) copy-start(bf16[1,256,384]{2,1,0:T(8,128)(2,1)} %param.7) | copy-start | bytes 589828
  83.8 10.5 %collective-permute-start.11 = (bf16[208,768]{1,0:T(8,128)(2,1)S(1)}, bf16[208,768]{1,0:T(8,128)(2,1)S(1)}, u32[]{:S(2)}, u32[]{:S(2)}) collective-permute-start(bf16[208,768]{1,0:T(8,128)(2,1)S(1)} %get-tuple-element.68.refs_5_.refs_1_), channel_id=1, source_target_pairs={{0,1},{1,0},{2,3},{3,2},{4,5},{5,4},{6,7},{7,6},{8,9},{9,8},{10,11... | collective-permute-start | bytes 958472 | tf_op jit(solution)/shard_map/ppermute | solution.py:403
  84.7 9.6 %collective-permute-start.15 = (bf16[208,768]{1,0:T(8,128)(2,1)S(1)}, bf16[208,768]{1,0:T(8,128)(2,1)S(1)}, u32[]{:S(2)}, u32[]{:S(2)}) collective-permute-start(bf16[208,768]{1,0:T(8,128)(2,1)S(1)} %relay.1), channel_id=1, source_target_pairs={{0,1},{1,0},{2,3},{3,2},{4,5},{5,4},{6,7},{7,6},{8,9},{9,8},{10,11... | collective-permute-start | bytes 958472 | tf_op jit(solution)/shard_map/ppermute | solution.py:403
  84.8 9.5 %collective-permute-start.16 = (bf16[48,1024]{1,0:T(8,128)(2,1)S(1)}, bf16[48,1024]{1,0:T(8,128)(2,1)S(1)}, u32[]{:S(2)}, u32[]{:S(2)}) collective-permute-start(bf16[48,1024]{1,0:T(8,128)(2,1)S(1)} %get-tuple-element.73), channel_id=1, source_target_pairs={{0,4},{1,5},{2,6},{3,7},{4,0},{5,1},{6,2},{7,3},{8,12},{9,13},{10,... | collective-permute-start | bytes 294920 | tf_op jit(solution)/shard_map/ppermute | solution.py:403
  87.7 6.6 %collective-permute-start.9 = (bf16[16,768]{1,0:T(8,128)(2,1)S(1)}, bf16[16,768]{1,0:T(8,128)(2,1)S(1)}, u32[]{:S(2)}, u32[]{:S(2)}) collective-permute-start(bf16[16,768]{1,0:T(8,128)(2,1)S(1)} %get-tuple-element.69), channel_id=1, source_target_pairs={{2,4},{6,8},{10,12},{4,2},{8,6},{12,10},{3,5},{7,9},{11,13},{5,3},... | collective-permute-start | bytes 73736 | tf_op jit(solution)/shard_map/ppermute | solution.py:532
  96.6 26.1 %collective-permute-start.17 = (bf16[144,768]{1,0:T(8,128)(2,1)S(1)}, bf16[144,768]{1,0:T(8,128)(2,1)S(1)}, u32[]{:S(2)}, u32[]{:S(2)}) collective-permute-start(bf16[144,768]{1,0:T(8,128)(2,1)S(1)} %get-tuple-element.75), channel_id=1, source_target_pairs={{0,4},{1,5},{2,6},{3,7},{4,0},{5,1},{6,2},{7,3},{8,12},{9,13},{10,... | collective-permute-start | bytes 663560 | tf_op jit(solution)/shard_map/ppermute | solution.py:403
  96.7 26.0 %collective-permute-start.18 = (bf16[144,768]{1,0:T(8,128)(2,1)S(1)}, bf16[144,768]{1,0:T(8,128)(2,1)S(1)}, u32[]{:S(2)}, u32[]{:S(2)}) collective-permute-start(bf16[144,768]{1,0:T(8,128)(2,1)S(1)} %get-tuple-element.76), channel_id=1, source_target_pairs={{0,8},{1,9},{2,10},{3,11},{4,12},{5,13},{6,14},{7,15},{8,0},{9,1},... | collective-permute-start | bytes 663560 | tf_op jit(solution)/shard_map/ppermute | solution.py:403
  99.2 23.5 %collective-permute-start.19 = (bf16[144,768]{1,0:T(8,128)(2,1)S(1)}, bf16[144,768]{1,0:T(8,128)(2,1)S(1)}, u32[]{:S(2)}, u32[]{:S(2)}) collective-permute-start(bf16[144,768]{1,0:T(8,128)(2,1)S(1)} %get-tuple-element.77), channel_id=1, source_target_pairs={{0,12},{1,13},{2,14},{3,15},{4,8},{5,9},{6,10},{7,11},{8,4},{9,5},... | collective-permute-start | bytes 663560 | tf_op jit(solution)/shard_map/ppermute | solution.py:403
  100.2 22.5 %collective-permute-start.20 = (bf16[48,1024]{1,0:T(8,128)(2,1)S(1)}, bf16[48,1024]{1,0:T(8,128)(2,1)S(1)}, u32[]{:S(2)}, u32[]{:S(2)}) collective-permute-start(bf16[48,1024]{1,0:T(8,128)(2,1)S(1)} %get-tuple-element.79), channel_id=1, source_target_pairs={{0,12},{1,13},{2,14},{3,15},{4,8},{5,9},{6,10},{7,11},{8,4},{9,5},... | collective-permute-start | bytes 294920 | tf_op jit(solution)/shard_map/ppermute | solution.py:403
  (20 other events, 16.5 us)

commit v4 on v3

--- a/solution.py
+++ b/solution.py
@@ -85,8 +85,10 @@
     return jnp.concatenate(parts, axis=1)
 
 
-def prepare_kernel(x, pad):
+def open_kernel(x, pad, first, last):
     positions, channels = x.shape
+    first[...] = x[:16][:2]
+    last[...] = x[positions - 16 :][14:]
     put(pad, 0, jnp.zeros((8, channels), F32))
     put(pad, 8, gelu(x[...].astype(F32)).astype(BF).astype(F32))
     put(pad, 8 + positions, jnp.zeros((pad.shape[1] - 8 - positions, channels), F32))
@@ -110,62 +112,52 @@
     normed = (pooled * inv * gain[...]).astype(BF)
     pooled_out[...] = pooled
     normed_out[...] = normed
-    packed = pack_kv(dot(normed, wk[...]), dot_t(normed, wv[...])).astype(BF)
-    for i in range(kv_out.shape[0]):
-        kv_out[i] = packed
+    kv_out[...] = pack_kv(dot(normed, wk[...]), dot_t(normed, wv[...])).astype(BF)
     early[0:ext] = every_second(pad, 6, ext).astype(BF)
     early[ext : 2 * ext] = every_second(pad, 7, ext).astype(BF)
 
 
-def query_kernel(normed, wq, early, out, early_out, *picks, groups, rows, padded, scale):
+def ordered(bits):
+    masks = [0]
+    for bit in reversed(bits):
+        masks = masks + [mask | (1 << bit) for mask in masks]
+    return masks
+
+
+def split_rows(rows, columns):
+    return round_up(-(-rows * LANES // columns), 16)
+
+
+def query_kernel(normed, wq, early, out, message, own, *, order, rows, padded, scale):
     width = normed.shape[1]
     value = normed[...]
     out[...] = (dot(value, wq[...]) * scale).astype(BF)
+    at, channels = early.shape
+    message[:at] = early[...]
+    count = len(order) * padded
+    step = split_rows(count, channels)
     for i in range(4):
         block_of = place(i)
-        pick = [chosen(rows, padded, width, block_of(k)) for k in range(groups)]
-        picks[i][...] = dot_t(jnp.concatenate(pick, axis=0), value).astype(BF)
-    early_out[...] = early[...]
-
-
-def attend_pair(index, q, cot, ks, vs, kt, vt, dk, dv, att, dq, key_size, value_size, scale, first):
-    tokens = q.shape[0]
-    ql, cl = 2 * index * key_size, 2 * index * value_size
-    qs = jnp.concatenate(
-        [q[:, ql : ql + key_size], q[:, ql + key_size : ql + 2 * key_size]], axis=0
-    )
-    both = cot[:, cl : cl + 2 * value_size]
-    cs = jnp.concatenate([both[:, :value_size], both[:, value_size:]], axis=0)
-    scores = dot_t(ks[...], qs)
-    raised = jnp.exp(scores - jnp.max(scores, axis=0, keepdims=True))
-    probs = raised * (1.0 / jnp.sum(raised, axis=0, keepdims=True))
-    weights = probs.astype(BF)
-    out_t = dot(vt[...], weights).astype(BF).astype(F32)
-    delta = jnp.sum(cs.astype(F32).T * out_t, axis=0, keepdims=True)
-    prob_cot = dot_t(vs[...], cs)
-    score_cot = (probs * (prob_cot - delta)).astype(BF)
-    dq_t = dot(kt[...], score_cot) * scale
-    dk_term = dot(score_cot, qs)
-    dv_term = dot(weights, cs)
-    if first:
-        dk[...] = dk_term
-        dv[...] = dv_term
-    else:
-        dk[...] += dk_term
-        dv[...] += dv_term
-    out_rows = jnp.concatenate([out_t[:, :tokens].T, out_t[:, tokens:].T], axis=1)
-    att[:, cl : cl + 2 * value_size] = out_rows.astype(BF)
-    dq_rows = jnp.concatenate([dq_t[:, :tokens].T, dq_t[:, tokens:].T], axis=1)
-    dq[:, ql % dq.shape[1] : ql % dq.shape[1] + 2 * key_size] = dq_rows.astype(BF)
-
-
-def attend_first_kernel(*refs, blocks, heads, key_size, value_size, scale):
-    q, cot, parts, att, dq, ks, vs, kt, vt, dk, dv = refs
+        pick = [chosen(rows, padded, width, block_of(k)) for k in order]
+        part = dot_t(jnp.concatenate(pick, axis=0), value).astype(BF)
+        if i == 0:
+            own[...] = part
+            continue
+        for c in range(channels // LANES):
+            piece = part[c * step : min((c + 1) * step, count)]
+            message[at : at + piece.shape[0], c * LANES : (c + 1) * LANES] = piece
+        at += step
+
+
+def attend_kernel(*refs, blocks, masks, heads, key_size, value_size, scale):
+    q, cot = refs[:2]
+    parts = refs[2 : 2 + blocks]
+    att, dq, keep_a, send_a, keep_b, send_b = refs[2 + blocks : 8 + blocks]
+    ks, vs, kt, vt, qs, cs, weights, score_cots = refs[8 + blocks :]
     tokens = q.shape[0]
     half = tokens // 2
     wide = value_size - key_size
-    for i in range(blocks):
-        part = parts[i]
+    for i, part in enumerate(parts):
         at = i * tokens
         ks[at : at + tokens] = part[:tokens]
         vs[at : at + tokens, :key_size] = part[tokens : 2 * tokens]
@@ -173,43 +165,79 @@
         vs[at + half : at + tokens, key_size:] = part[2 * tokens :, wide:]
         kt[:, at : at + tokens] = ks[at : at + tokens].astype(F32).T.astype(BF)
         vt[:, at : at + tokens] = vs[at : at + tokens].astype(F32).T.astype(BF)
-    for pair in range(heads // 4):
-        attend_pair(
-            pair, q, cot, ks, vs, kt, vt, dk, dv, att, dq, key_size, value_size, scale, pair == 0
+    for pair in range(heads // 2):
+        ql, cl = 2 * pair * key_size, 2 * pair * value_size
+        rows = slice(2 * pair * tokens, 2 * (pair + 1) * tokens)
+        both = cot[:, cl : cl + 2 * value_size]
+        qs[rows] = jnp.concatenate(
+            [q[:, ql : ql + key_size], q[:, ql + key_size : ql + 2 * key_size]], axis=0
         )
-
-
-def attend_second_kernel(*refs, blocks, heads, key_size, value_size, scale):
-    q, cot, att_in, ks, vs, kt, vt, dk_in, dv_in = refs[:9]
-    att, dq, terms, dk, dv = refs[9:]
-    tokens = q.shape[0]
-    att[:, : att_in.shape[1]] = att_in[...]
-    for pair in range(heads // 4, heads // 2):
-        if pair == heads // 4:
-            dk[...] = dk_in[...]
-            dv[...] = dv_in[...]
-        attend_pair(
-            pair, q, cot, ks, vs, kt, vt, dk, dv, att, dq, key_size, value_size, scale, False
-        )
+        cs[rows] = jnp.concatenate([both[:, :value_size], both[:, value_size:]], axis=0)
+        scores = dot_t(ks[...], qs[rows])
+        raised = jnp.exp(scores - jnp.max(scores, axis=0, keepdims=True))
+        probs = raised * (1.0 / jnp.sum(raised, axis=0, keepdims=True))
+        weights[:, rows] = probs.astype(BF)
+        out_t = dot(vt[...], weights[:, rows]).astype(BF).astype(F32)
+        delta = jnp.sum(cs[rows].astype(F32).T * out_t, axis=0, keepdims=True)
+        score_cots[:, rows] = (probs * (dot_t(vs[...], cs[rows]) - delta)).astype(BF)
+        dq_t = dot(kt[...], score_cots[:, rows]) * scale
+        out_rows = jnp.concatenate([out_t[:, :tokens].T, out_t[:, tokens:].T], axis=1)
+        att[:, cl : cl + 2 * value_size] = out_rows.astype(BF)
+        dq_rows = jnp.concatenate([dq_t[:, :tokens].T, dq_t[:, tokens:].T], axis=1)
+        dq[:, ql : ql + 2 * key_size] = dq_rows.astype(BF)
+    edge = keep_a.shape[1]
+    count = blocks // 2
     for i in range(blocks):
         at = slice(i * tokens, (i + 1) * tokens)
-        terms[i] = pack_kv(dk[at], dv[at]).astype(BF)
-
-
-def query_cot_kernel(left, right, wq, both, out):
-    both[:, : left.shape[1]] = left[...]
-    both[:, left.shape[1] :] = right[...]
-    out[...] = dot_t(both[...], wq[...])
-
-
-def middle_kernel(terms, part, pooled_in, gain_in, wk, wv, near, message, edge, near_out):
-    near_out[...] = near[...]
-    size = terms.shape[2]
+        packed = pack_kv(dot(score_cots[at], qs[...]), dot(weights[at], cs[...]))
+        for order, keep, send, part in (
+            (masks[0], keep_a, send_a, packed[:edge]),
+            (masks[1], keep_b, send_b, packed[edge:]),
+        ):
+            k = order.index(i)
+            if k < count:
+                keep[k] = part
+            else:
+                send[k - count] = part.astype(BF)
+
+
+def total_of(parts):
+    total = parts[0][...]
+    for part in parts[1:]:
+        total = total + part[...].astype(F32)
+    return total
+
+
+def fold_kernel(*refs):
+    keep, send = refs[-2:]
+    total = total_of(refs[:-2])
+    keep[...] = total[: keep.shape[0]]
+    send[...] = total[keep.shape[0] :].astype(BF)
+
+
+def fold_two_kernel(*refs):
+    fold_kernel(refs[0], refs[1], refs[4], refs[5])
+    fold_kernel(refs[2], refs[3], refs[6], refs[7])
+
+
+def merge_kernel(keep_a, in_a, keep_b, in_b, keep, send):
+    total = jnp.concatenate([total_of((keep_a, in_a)), total_of((keep_b, in_b))], axis=1)
+    keep[...] = total[: keep.shape[0]]
+    send[...] = total[keep.shape[0] :].astype(BF)
+
+
+def send_on_kernel(keep, came, out):
+    out[...] = (keep[...] + came[...].astype(F32)).astype(BF)
+
+
+def query_cot_kernel(dq, wq, out):
+    out[...] = dot_t(dq[...], wq[...])
+
+
+def middle_kernel(own, came, part, pooled_in, gain_in, wk, wv, message, edge):
+    size = own.shape[2]
     tokens, width = pooled_in.shape
-    total = terms[0].astype(F32)
-    for i in range(1, terms.shape[0]):
-        total = total + terms[i].astype(F32)
-    total = total.astype(BF).astype(F32)
+    total = (own[0] + came[0].astype(F32)).astype(BF).astype(F32)
     key_cot = total[:tokens]
     value_cot = unpack_values(total, tokens, size)
     normed_cot = part[...] + dot_t(key_cot.astype(BF), wk[...])
@@ -250,18 +278,28 @@
     return jnp.where(hit, 1.0, 0.0).astype(BF)
 
 
-def relay_kernel(value, out):
+def relay_kernel(value, keep_in, came, out, keep, send):
     out[...] = value[...]
-
-
-def select_kernel(*refs, groups, rows, padded):
-    blocks = refs[:4]
-    out, even, odd = refs[4:]
+    fold_kernel(keep_in, came, keep, send)
+
+
+def select_kernel(*refs, order, rows, padded):
+    own, blocks = refs[0], refs[1:5]
+    out, norm_out, even, odd = refs[5:]
     ext, channels = even.shape
-    tokens = out.shape[1] // 8
+    tokens = own.shape[1]
+    count = own.shape[0]
+    step = split_rows(count, channels)
+    norm_out[:, :tokens] = own[...]
+    for i in range(1, 4):
+        at = 2 * ext + (i - 1) * step
+        for c in range(channels // LANES):
+            end = min((c + 1) * step, count)
+            piece = blocks[i][at : at + end - c * step, c * LANES : (c + 1) * LANES]
+            norm_out[c * step : end, i * tokens : (i + 1) * tokens] = piece
     block_of = place()
     pick = jnp.concatenate(
-        [chosen(rows, padded, 5 * channels, block_of(k)) for k in range(groups)], axis=0
+        [chosen(rows, padded, 5 * channels, block_of(k)) for k in order], axis=0
     )
     for i, block in enumerate(blocks):
         even[...] = block[:ext].astype(F32)
@@ -275,15 +313,17 @@
         out[:, 2 * i * tokens : 2 * (i + 1) * tokens] = dot_t(pick, shifted).astype(BF)
 
 
-def query_grad_kernel(*refs, pad):
-    picks, blocks = refs[:4], refs[4:8]
-    outs, right = refs[8:-1], refs[-1]
-    tokens = blocks[0].shape[0]
-    for i, block in enumerate(blocks):
+def query_grad_kernel(pick, first, second, third, fourth, keep, send, right):
+    tokens = first.shape[0]
+    for i, block in enumerate((first, second, third, fourth)):
         right[i * tokens : (i + 1) * tokens] = block[...]
-    pick = jnp.concatenate([part[...] for part in picks], axis=1)
-    for k, out in enumerate(outs):
-        out[...] = dot(pick[k * pad : (k + 1) * pad], right[...]).astype(out.dtype)
+    count, pad = keep.shape[:2]
+    for k in range(2 * count):
+        term = dot(pick[k * pad : (k + 1) * pad], right[...])
+        if k < count:
+            keep[k] = term
+        else:
+            send[k - count] = term.astype(BF)
 
 
 def chunk_layout(conv_rows, norm_rows, width, key_size, value_size):
@@ -293,9 +333,8 @@
 
 
 def conv_grad_kernel(*refs, conv_rows, conv_pad, norm_rows, norm_pad, key_size, value_size):
-    pick, picks, blocks = refs[0], refs[1:5], refs[5:9]
-    outs, right, side, stage = refs[9:-3], refs[-3], refs[-2], refs[-1]
-    norm_pick = jnp.concatenate([part[...] for part in picks], axis=1)
+    pick, norm_pick, blocks = refs[0], refs[1], refs[2:6]
+    outs, right, side, stage = refs[6:-3], refs[-3], refs[-2], refs[-1]
     width = right.shape[1]
     tokens = side.shape[0] // 4
     half = tokens // 2
@@ -314,30 +353,24 @@
     stage[...] = jnp.zeros(stage.shape, F32)
     stage[gain_at : gain_at + 1] = high
     stage[gain_at + 1 : gain_at + 2] = gain - high
-    for k, out in enumerate(outs):
+    count = outs[0].shape[0]
+    for k in range(4 * count):
+        out = outs[k // count]
         conv = dot(pick[k * conv_pad : (k + 1) * conv_pad], right[...])
         stage[:conv_rows] = conv[:conv_rows]
         both = dot(norm_pick[k * norm_pad : (k + 1) * norm_pad], side[...])
         key, value = both[:, :key_size], both[:, key_size : key_size + value_size]
         for part, at, end in ((key, key_at, value_at), (value, value_at, gain_at)):
-            count = end - at
-            pieces = [part[i : i + count] for i in range(0, norm_rows, count)]
+            step = end - at
+            pieces = [part[i : i + step] for i in range(0, norm_rows, step)]
             stage[at:end] = jnp.concatenate(pieces, axis=1)
-        out[...] = stage[...].astype(out.dtype)
-
-
-def summed(parts):
-    total = parts[0][...]
-    for part in parts[1:]:
-        total = total + part[...].astype(F32)
-    return total
-
-
-def final_kernel(*refs):
+        out[k % count] = stage[...].astype(out.dtype)
+
+
+def final_kernel(*refs, conv_parts):
     conv, query, key, value, gain, stage = refs[-6:]
-    count = len(refs[:-6]) // 2
-    total = summed(refs[:count])
-    query[...] = summed(refs[count : 2 * count])[: query.shape[0]]
+    total = total_of(refs[:conv_parts])[0]
+    query[...] = total_of(refs[conv_parts:-6])[0, : query.shape[0]]
     rows, width = conv.shape
     count = key.shape[0]
     stage[...] = total
@@ -402,22 +435,42 @@
         mask = 2 * seq_bits + dp_bit
         return lax.ppermute(value, both_axes, [(i, i ^ mask) for i in range(owners)])
 
-    def quad(value):
+    def held(value, *until):
+        return lax.optimization_barrier((value,) + until)[0]
+
+    def quad(value, *until):
         core = swap(value, 0, 1)
         near = swap(value, 1)
-        return [value, core, near, swap(near, 0, 1)]
-
+        return [value, core, near, swap(held(near, *until), 0, 1)]
+
+    def fold(parts, name):
+        shape = (parts[0].shape[0] // 2,) + parts[0].shape[1:]
+        return run(fold_kernel, [(shape, F32), (shape, BF)], parts, name=name)
+
+    def halved(keep, send, bits, name):
+        for bit in bits[:-1]:
+            keep, send = fold([keep, swap(send, 1 << bit)], name)
+        return [keep, swap(send, 1 << bits[-1])]
+
+    bits = list(range(devices.bit_length() - 1))
+    order = [mask // 2 for mask in ordered(bits[1:])]
     up = [(i, i + 1) for i in range(devices - 1)]
     down = [(j, i) for i, j in up]
-    before = lax.ppermute(x[positions - 2 :], "seq", up)
-    after = lax.ppermute(x[:2], "seq", down)
     pad_shape = (channels // LANES, 8 + 2 * ext + 8, LANES)
+    ready, first, last = run(
+        open_kernel,
+        [(pad_shape, F32), ((2, channels), BF), ((2, channels), BF)],
+        [x],
+        flops=4 * 10**9,
+        name="gelu",
+    )
+    before = lax.ppermute(last, "seq", up)
+    after = lax.ppermute(first, "seq", down)
     wv = wv.T
-    (ready,) = run(prepare_kernel, [(pad_shape, F32)], [x], flops=4 * 10**9, name="gelu")
     kv, early, normed, pooled = run(
         front_kernel,
         [
-            ((devices, 5 * tokens // 2, key_size), BF),
+            ((5 * tokens // 2, key_size), BF),
             ((2 * ext, channels), BF),
             ((tokens, width), BF),
             ((tokens, width), F32),
@@ -427,112 +480,123 @@
         flops=2 * positions * taps * channels * width,
         name="front",
     )
-    kv = lax.all_to_all(kv, "seq", 0, 0, tiled=True)
-    queries, early, *picks = run(
+    near_kv = [kv] + [swap(kv, 2 * k) for k in range(1, groups)]
+    far_kv = [swap(block, 1) for block in near_kv]
+    picked = (groups * norm_pad, tokens)
+    rows = 2 * ext + 3 * split_rows(picked[0], channels)
+    queries, early, pick_own = run(
         lambda *refs: query_kernel(
-            *refs, groups=groups, rows=norm_rows, padded=norm_pad, scale=scale
+            *refs, order=order, rows=norm_rows, padded=norm_pad, scale=scale
         ),
-        [
-            ((tokens, heads * key_size), BF),
-            (early.shape, BF),
-        ]
-        + [((groups * norm_pad, tokens), BF)] * 4,
+        [((tokens, heads * key_size), BF), ((rows, channels), BF), (picked, BF)],
         [normed, wq, early],
         flops=4 * tokens * width * heads * key_size,
         name="queries",
-    )
+        after=near_kv[1:],
+    )
+    early = held(early, *far_kv)
     length = devices * tokens
-    sizes = dict(
-        blocks=devices, heads=heads, key_size=key_size, value_size=value_size, scale=scale
-    )
-    attend_flops = 3 * tokens * heads * length * (key_size + value_size)
-    half_att = heads // 2 * value_size
-    half_query = heads // 2 * key_size
-    totals = [((length, key_size), F32), ((length, value_size), F32)]
-    att_first, dq_first, *held = run(
-        lambda *refs: attend_first_kernel(*refs, **sizes),
+    masks = [2 * k for k in range(groups)] + [2 * k + 1 for k in range(groups)]
+    half_block = (groups, 5 * tokens // 4, key_size)
+    attended, query_cot, keep_a, send_a, keep_b, send_b = run(
+        lambda *refs: attend_kernel(
+            *refs,
+            blocks=devices,
+            masks=[
+                [masks.index(m) for m in ordered(way)] for way in (bits, [1, 0] + bits[2:])
+            ],
+            heads=heads,
+            key_size=key_size,
+            value_size=value_size,
+            scale=scale,
+        ),
+        [((tokens, heads * value_size), BF), ((tokens, heads * key_size), BF)]
+        + [(half_block, F32), (half_block, BF)] * 2,
+        [queries, cotangent] + near_kv + far_kv,
         [
-            ((tokens, half_att), BF),
-            ((tokens, half_query), BF),
-            ((length, key_size), BF),
-            ((length, value_size), BF),
-            ((key_size, length), BF),
-            ((value_size, length), BF),
-        ]
-        + totals,
-        [queries, cotangent, kv],
-        flops=attend_flops,
-        name="attend_first",
-    )
-    early_near, early_core = swap(early, 1), swap(early, 0, 1)
-    norm_picks = [picks[0], swap(picks[1], 0, 1), swap(picks[2], 1), swap(picks[3], 1, 1)]
-    attended, dq_second, terms = run(
-        lambda *refs: attend_second_kernel(*refs, **sizes),
-        [
-            ((tokens, heads * value_size), BF),
-            ((tokens, half_query), BF),
-            (kv.shape, BF),
+            pltpu.VMEM((length, key_size), BF),
+            pltpu.VMEM((length, value_size), BF),
+            pltpu.VMEM((key_size, length), BF),
+            pltpu.VMEM((value_size, length), BF),
+            pltpu.VMEM((heads * tokens, key_size), BF),
+            pltpu.VMEM((heads * tokens, value_size), BF),
+            pltpu.VMEM((length, heads * tokens), BF),
+            pltpu.VMEM((length, heads * tokens), BF),
         ],
-        [queries, cotangent, att_first] + held,
-        [pltpu.VMEM(s, t) for s, t in totals],
-        flops=attend_flops,
-        name="attend_second",
-        after=[early_near, early_core] + norm_picks[1:],
-    )
-    early_blocks = [early, early_core, early_near, swap(early_near, 0, 1)]
-    (conv_pick,) = run(
-        lambda *refs: select_kernel(*refs, groups=groups, rows=conv_rows, padded=conv_pad),
-        [((groups * conv_pad, 8 * tokens), BF)],
-        early_blocks,
+        flops=6 * tokens * heads * length * (key_size + value_size),
+        name="attend",
+    )
+    early_blocks = quad(early, send_a)
+    in_a, in_b = swap(send_a, 1), swap(send_b, 2)
+    conv_pick, norm_pick = run(
+        lambda *refs: select_kernel(*refs, order=order, rows=conv_rows, padded=conv_pad),
+        [((groups * conv_pad, 8 * tokens), BF), ((groups * norm_pad, 4 * tokens), BF)],
+        [pick_own] + early_blocks,
         [pltpu.VMEM((ext, channels), F32), pltpu.VMEM((ext, channels), F32)],
         flops=2 * groups * conv_pad * taps * channels * 8 * tokens,
         name="select",
     )
-    query_cot, normed_cot = run(
+    fourth = (groups // 2,) + half_block[1:]
+    keep_a, send_a, keep_b, send_b = run(
+        fold_two_kernel,
+        [(fourth, F32), (fourth, BF)] * 2,
+        [keep_a, in_a, keep_b, in_b],
+        name="kv_cot_fold",
+        after=[conv_pick],
+    )
+    in_a, in_b = swap(send_a, 2), swap(send_b, 1)
+    block = (groups // 4, 5 * tokens // 2, key_size)
+    keep, send = run(
+        merge_kernel,
+        [(block, F32), (block, BF)],
+        [keep_a, in_a, keep_b, in_b],
+        name="kv_cot_merge",
+    )
+    query_cot = held(query_cot, keep)
+    query_near, query_core = swap(query_cot, 1), swap(query_cot, 0, 1)
+    pooled = held(pooled, query_near, query_core)
+    kv_cot = halved(keep, send, bits[2:], "kv_cot_fold")
+    (normed_cot,) = run(
         query_cot_kernel,
-        [((tokens, heads * key_size), BF), ((tokens, width), F32)],
-        [dq_first, dq_second, wq],
+        [((tokens, width), F32)],
+        [query_cot, wq],
         flops=2 * tokens * width * heads * key_size,
         name="query_part",
     )
-    terms = lax.all_to_all(terms, "seq", 0, 0, tiled=True)
-    query_near = swap(query_cot, 1)
-    message, edge, query_relay = run(
+    message, edge = run(
         middle_kernel,
-        [
-            ((tokens + 16 + tokens // 2, width), BF),
-            ((16, width), BF),
-            (query_near.shape, BF),
-        ],
-        [terms, normed_cot, pooled, gain, wk, wv, query_near],
+        [((tokens + 16 + tokens // 2, width), BF), ((16, width), BF)],
+        kv_cot + [normed_cot, pooled, gain, wk, wv],
         flops=2 * tokens * width * (key_size + value_size),
         name="conv_cot",
     )
-    query_blocks = [query_cot, swap(query_cot, 0, 1), query_near, swap(query_relay, 0, 1)]
-    query_parts = run(
-        lambda *refs: query_grad_kernel(*refs, pad=norm_pad),
-        [((norm_pad, heads * key_size), F32 if k == 0 else BF) for k in range(groups)],
-        norm_picks + query_blocks,
+    near_message, core_message = swap(message, 1), swap(message, 0, 1)
+    crossing = [(i, i + 1) for i in range(1, devices - 1, 2)]
+    crossing = crossing + [(j, i) for i, j in crossing]
+    edge_in = lax.ppermute(edge, "seq", crossing)
+    query_half = (groups // 2, norm_pad, heads * key_size)
+    keep, send = run(
+        query_grad_kernel,
+        [(query_half, F32), (query_half, BF)],
+        [norm_pick, query_cot, query_core, query_near, swap(held(query_near, message), 0, 1)],
         [pltpu.VMEM((4 * tokens, heads * key_size), BF)],
         flops=2 * groups * norm_pad * 4 * tokens * heads * key_size,
         name="query_grad",
     )
-    query_in = [swap(part, 2 * (k + 1)) for k, part in enumerate(query_parts[1:])]
-    near_message = swap(message, 1)
-    (relay,) = run(
+    query_fourth = (groups // 4,) + query_half[1:]
+    relay, keep, send = run(
         relay_kernel,
-        [(message.shape, BF)],
-        [near_message],
+        [(message.shape, BF), (query_fourth, F32), (query_fourth, BF)],
+        [near_message, keep, swap(send, 2)],
         name="relay",
-        after=[query_in[1], conv_pick],
-    )
-    blocks = [message, swap(message, 0, 1), near_message, swap(relay, 0, 1)]
-    crossing = [(i, i + 1) for i in range(1, devices - 1, 2)]
-    crossing = crossing + [(j, i) for i, j in crossing]
-    edge_in = lax.ppermute(edge, "seq", crossing)
+        after=[edge_in],
+    )
+    query_parts = halved(keep, send, bits[2:], "query_fold")
+    blocks = [message, core_message, near_message, swap(relay, 0, 1)]
     _, _, gain_at = chunk_layout(conv_rows, norm_rows, width, key_size, value_size)
     chunk = (round_up(gain_at + 2, 16), width)
-    conv_parts = run(
+    chunks = (groups // 4,) + chunk
+    near_keep, far_keep, near_send, far_send = run(
         lambda *refs: conv_grad_kernel(
             *refs,
             conv_rows=conv_rows,
@@ -542,8 +606,8 @@
             key_size=key_size,
             value_size=value_size,
         ),
-        [(chunk, F32 if k == 0 else BF) for k in range(groups)],
-        [conv_pick] + norm_picks + blocks,
+        [(chunks, F32), (chunks, F32), (chunks, BF), (chunks, BF)],
+        [conv_pick, norm_pick] + blocks,
         [
             pltpu.VMEM((8 * tokens, width), BF),
             pltpu.VMEM((4 * tokens, width // 2), BF),
@@ -551,23 +615,28 @@
         ],
         flops=2 * groups * conv_pad * 8 * tokens * width,
         name="conv_grad",
-        after=[edge_in, query_in[0]],
-    )
-    conv_in = [swap(part, 2 * (k + 1)) for k, part in enumerate(conv_parts[1:])]
+    )
+    far_in = swap(far_send, 2)
+    near_in = swap(near_send, 2)
+    (far_sum,) = run(send_on_kernel, [(chunks, BF)], [far_keep, far_in], name="conv_send_on")
+    conv_parts = [near_keep, near_in, swap(far_sum, 4)]
+    if len(bits) > 3:
+        keep, send = fold(conv_parts, "conv_fold")
+        conv_parts = halved(keep, send, bits[3:], "conv_fold")
     (input_grad,) = run(
         input_kernel,
         [((positions, channels), BF)],
-        [x, message, blocks[2], edge_in, conv_weight],
+        [x, message, near_message, edge_in, conv_weight],
         [
             pltpu.VMEM((tokens + 16, width), F32),
             pltpu.VMEM((channels // LANES, positions, LANES), F32),
         ],
         flops=2 * positions * taps * channels * width,
         name="input_grad",
-        after=[conv_parts[0]],
+        after=[far_sum],
     )
     conv_grad, query_grad, key_grad, value_grad, gain_grad = run(
-        final_kernel,
+        lambda *refs: final_kernel(*refs, conv_parts=len(conv_parts)),
         [
             ((conv_rows, width), F32),
             ((norm_rows, heads * key_size), F32),
@@ -575,7 +644,7 @@
             ((norm_rows, value_size), F32),
             ((1, norm_rows), F32),
         ],
-        [conv_parts[0]] + conv_in + [query_parts[0]] + query_in,
+        conv_parts + query_parts,
         [pltpu.VMEM(chunk, F32)],
         name="final_sum",
     )

time: 125 us -> 99.3 us (0.79)
  the two profiles are of different devices: /device:TPU:10 before, /device:TPU:0 now
where the time goes in v4:
time: 99.3 us; the launch traced here: 99.1 us
  waiting for transfers between devices  44.6 us (45%)
  starting transfers between devices  34.5 us (35%)
  Pallas kernels  18.1 us (18%)
    ppermute x26, waiting for transfers between devices, swap(): lax.ppermute(value, both_axes, [(i, i ^ mask) for i in range(owners)])  40.5 us
    ppermute x26, starting transfers between devices, swap(): lax.ppermute(value, both_axes, [(i, i ^ mask) for i in range(owners)])  27.3 us
    pallas_call x15, Pallas kernels, run(): pl.pallas_call(whole, out_shape=[jax.ShapeDtypeStruct(s, t) for s, t in o...  18.1 us
    ppermute x1, starting transfers between devices, on_device(): before = lax.ppermute(last, 'seq', up)  5.13 us
    ppermute x1, waiting for transfers between devices, on_device(): after = lax.ppermute(first, 'seq', down)  4.14 us
  transfers between devices with their start and end apart: 29, of which 15 were waited for; matrix products, arithmetic and copies ran while one was open for 0% of the time, Pallas kernels for 13%

profile of v4, /device:TPU:0, one launch (start us, length us, event | category | flops | bytes accessed | tf_op | source)
XLA Modules:
  0.0 99.1 jit_solution(200318917837353945)
XLA Ops:
  1.8 5.1 %collective-permute-start = (bf16[2,384]{1,0:T(2,128)(2,1)S(1)}, bf16[2,384]{1,0:T(2,128)(2,1)S(1)}, u32[]{:S(2)}, u32[]{:S(2)}) collective-permute-start(bf16[2,384]{1,0:T(2,128)(2,1)S(1)} %get-tuple-element.53), channel_id=1, source_target_pairs={{0,2},{2,4},{4,6},{6,8},{8,10},{10,12},{12,14},{1,3},{3,5},{5,7},{... | collective-permute-start | bytes 4616 | tf_op jit(solution)/shard_map/ppermute | solution.py:467
  6.9 1.3 %collective-permute-start.1 = (bf16[2,384]{1,0:T(2,128)(2,1)S(1)}, bf16[2,384]{1,0:T(2,128)(2,1)S(1)}, u32[]{:S(2)}, u32[]{:S(2)}) collective-permute-start(bf16[2,384]{1,0:T(2,128)(2,1)S(1)} %get-tuple-element.54), channel_id=1, source_target_pairs={{2,0},{4,2},{6,4},{8,6},{10,8},{12,10},{14,12},{3,1},{5,3},{7,5},{... | collective-permute-start | bytes 4616 | tf_op jit(solution)/shard_map/ppermute | solution.py:468
  8.2 4.1 %collective-permute-done.1.refs_2_ = bf16[2,384]{1,0:T(2,128)(2,1)S(1)} collective-permute-done((bf16[2,384]{1,0:T(2,128)(2,1)S(1)}, bf16[2,384]{1,0:T(2,128)(2,1)S(1)}, u32[]{:S(2)}, u32[]{:S(2)}) %collective-permute-start.1) | collective-permute-done | bytes 1568 | tf_op jit(solution)/shard_map/ppermute | solution.py:468
  12.4 1.9 %front.1 = (bf16[320,128]{1,0:T(8,128)(2,1)S(1)}, bf16[288,384]{1,0:T(8,128)(2,1)S(1)}, bf16[128,768]{1,0:T(8,128)(2,1)S(1)}, f32[128,768]{1,0:T(8,128)S(1)}) custom-call(f32[3,304,128]{2,1,0:T(8,128)S(1)} %get-tuple-element.52.refs_0_, bf16[2,384]{1,0:T(2,128)(2,1)S(1)} %collective-permute-done.refs_1_, bf16[2,384]{1,0:T(2,128)(2,1)S(1)} %collective-permute-done.1.refs_2_, ...), custom_call_target="tpu_custom_call" | custom-call | flops 754974720 | bytes 4806656 | tf_op jit(solution)/shard_map/front/pallas_call | solution.py:36
  14.2 3.7 %collective-permute-start.4 = (bf16[320,128]{1,0:T(8,128)(2,1)S(1)}, bf16[320,128]{1,0:T(8,128)(2,1)S(1)}, u32[]{:S(2)}, u32[]{:S(2)}) collective-permute-start(bf16[320,128]{1,0:T(8,128)(2,1)S(1)} %get-tuple-element.57.refs_2_), channel_id=1, source_target_pairs={{0,12},{1,13},{2,14},{3,15},{4,8},{5,9},{6,10},{7,11},{8,4},{9,5},... | collective-permute-start | bytes 245768 | tf_op jit(solution)/shard_map/ppermute | solution.py:436
  18.7 2.4 %collective-permute-start.5 = (bf16[320,128]{1,0:T(8,128)(2,1)S(1)}, bf16[320,128]{1,0:T(8,128)(2,1)S(1)}, u32[]{:S(2)}, u32[]{:S(2)}) collective-permute-start(bf16[320,128]{1,0:T(8,128)(2,1)S(1)} %get-tuple-element.57.refs_2_), channel_id=1, source_target_pairs={{0,2},{1,3},{2,0},{3,1},{4,6},{5,7},{6,4},{7,5},{8,10},{9,11},{10,... | collective-permute-start | bytes 245768 | tf_op jit(solution)/shard_map/ppermute | solution.py:436
  21.1 2.5 %collective-permute-start.8 = (bf16[320,128]{1,0:T(8,128)(2,1)S(1)}, bf16[320,128]{1,0:T(8,128)(2,1)S(1)}, u32[]{:S(2)}, u32[]{:S(2)}) collective-permute-start(bf16[320,128]{1,0:T(8,128)(2,1)S(1)} %collective-permute-done.4.refs_5_), channel_id=1, source_target_pairs={{0,2},{1,3},{2,0},{3,1},{4,6},{5,7},{6,4},{7,5},{8,10},{9,11},{10,... | collective-permute-start | bytes 245768 | tf_op jit(solution)/shard_map/ppermute | solution.py:436
  23.8 2.0 %collective-permute-start.7 = (bf16[320,128]{1,0:T(8,128)(2,1)S(1)}, bf16[320,128]{1,0:T(8,128)(2,1)S(1)}, u32[]{:S(2)}, u32[]{:S(2)}) collective-permute-start(bf16[320,128]{1,0:T(8,128)(2,1)S(1)} %collective-permute-done.3.refs_4_), channel_id=1, source_target_pairs={{0,2},{1,3},{2,0},{3,1},{4,6},{5,7},{6,4},{7,5},{8,10},{9,11},{10,... | collective-permute-start | bytes 245768 | tf_op jit(solution)/shard_map/ppermute | solution.py:436
  26.6 2.1 %collective-permute-done.7.refs_8_ = bf16[320,128]{1,0:T(8,128)(2,1)S(1)} collective-permute-done((bf16[320,128]{1,0:T(8,128)(2,1)S(1)}, bf16[320,128]{1,0:T(8,128)(2,1)S(1)}, u32[]{:S(2)}, u32[]{:S(2)}) %collective-permute-start.7) | collective-permute-done | bytes 81952 | tf_op jit(solution)/shard_map/ppermute | solution.py:436
  28.7 1.5 %collective-permute-done.6.refs_7_ = bf16[320,128]{1,0:T(8,128)(2,1)S(1)} collective-permute-done((bf16[320,128]{1,0:T(8,128)(2,1)S(1)}, bf16[320,128]{1,0:T(8,128)(2,1)S(1)}, u32[]{:S(2)}, u32[]{:S(2)}) %collective-permute-start.6) | collective-permute-done | bytes 81952 | tf_op jit(solution)/shard_map/ppermute | solution.py:436
  31.1 6.5 %attend.1 = (bf16[128,1536]{1,0:T(8,128)(2,1)}, bf16[128,1024]{1,0:T(8,128)(2,1)S(1)}, f32[4,160,128]{2,1,0:T(8,128)S(1)}, bf16[4,160,128]{2,1,0:T(8,128)(2,1)S(...) custom-call(bf16[128,1024]{1,0:T(8,128)(2,1)S(1)} %get-tuple-element.58.refs_0_, ...), custom_call_target="tpu_custom_call" | custom-call | flops 2013265920 | bytes 2949120 | tf_op jit(solution)/shard_map/attend/pallas_call | solution.py:36
  37.6 1.1 %collective-permute-done.12.refs_3_ = bf16[480,384]{1,0:T(8,128)(2,1)S(1)} collective-permute-done((bf16[480,384]{1,0:T(8,128)(2,1)S(1)}, bf16[480,384]{1,0:T(8,128)(2,1)S(1)}, u32[]{:S(2)}, u32[]{:S(2)}) %collective-permute-start.12) | collective-permute-done | bytes 368672 | tf_op jit(solution)/shard_map/ppermute | solution.py:436
  39.3 1.0 %collective-permute-start.10 = (bf16[4,160,128]{2,1,0:T(8,128)(2,1)S(1)}, bf16[4,160,128]{2,1,0:T(8,128)(2,1)S(1)}, u32[]{:S(2)}, u32[]{:S(2)}) collective-permute-start(bf16[4,160,128]{2,1,0:T(8,128)(2,1)S(1)} %get-tuple-element.63), channel_id=1, source_target_pairs={{0,4},{1,5},{2,6},{3,7},{4,0},{5,1},{6,2},{7,3},{8,12},{9,13},{10,... | collective-permute-start | bytes 491528 | tf_op jit(solution)/shard_map/ppermute | solution.py:436
  40.4 2.4 %select.1 = (bf16[512,1024]{1,0:T(8,128)(2,1)S(1)}, bf16[192,512]{1,0:T(8,128)(2,1)S(1)}) custom-call(bf16[192,128]{1,0:T(8,128)(2,1)S(1)} %get-tuple-element.64.refs_0_, bf16[480,384]{1,0:T(8,128)(2,1)S(1)} %get-tuple-element.66.refs_1_, bf16[480,384]{1,0:T(8,128)(2,1)S(1)} %collective-permute-done.11.refs_2_, ...), custom_call_target="tpu_custom_call" | custom-call | flops 2013265920 | bytes 2768896 | tf_op jit(solution)/shard_map/select/pallas_call | solution.py:36
  42.9 2.7 %collective-permute-done.10.refs_3_ = bf16[4,160,128]{2,1,0:T(8,128)(2,1)S(1)} collective-permute-done((bf16[4,160,128]{2,1,0:T(8,128)(2,1)S(1)}, bf16[4,160,128]{2,1,0:T(8,128)(2,1)S(1)}, u32[]{:S(2)}, u32[]{:S(2)}) %collective-permute-start.10) | collective-permute-done | bytes 163872 | tf_op jit(solution)/shard_map/ppermute | solution.py:436
  45.7 1.1 %collective-permute-start.14 = (bf16[2,160,128]{2,1,0:T(8,128)(2,1)S(1)}, bf16[2,160,128]{2,1,0:T(8,128)(2,1)S(1)}, u32[]{:S(2)}, u32[]{:S(2)}) collective-permute-start(bf16[2,160,128]{2,1,0:T(8,128)(2,1)S(1)} %get-tuple-element.70), channel_id=1, source_target_pairs={{0,4},{1,5},{2,6},{3,7},{4,0},{5,1},{6,2},{7,3},{8,12},{9,13},{10,... | collective-permute-start | bytes 245768 | tf_op jit(solution)/shard_map/ppermute | solution.py:436
  46.8 1.1 %collective-permute-start.15 = (bf16[2,160,128]{2,1,0:T(8,128)(2,1)S(1)}, bf16[2,160,128]{2,1,0:T(8,128)(2,1)S(1)}, u32[]{:S(2)}, u32[]{:S(2)}) collective-permute-start(bf16[2,160,128]{2,1,0:T(8,128)(2,1)S(1)} %get-tuple-element.72), channel_id=1, source_target_pairs={{0,2},{1,3},{2,0},{3,1},{4,6},{5,7},{6,4},{7,5},{8,10},{9,11},{10,... | collective-permute-start | bytes 245768 | tf_op jit(solution)/shard_map/ppermute | solution.py:436
  47.9 2.3 %collective-permute-done.14.refs_1_ = bf16[2,160,128]{2,1,0:T(8,128)(2,1)S(1)} collective-permute-done((bf16[2,160,128]{2,1,0:T(8,128)(2,1)S(1)}, bf16[2,160,128]{2,1,0:T(8,128)(2,1)S(1)}, u32[]{:S(2)}, u32[]{:S(2)}) %collective-permute-start.14) | collective-permute-done | bytes 81952 | tf_op jit(solution)/shard_map/ppermute | solution.py:436
  50.2 1.1 %collective-permute-done.15.refs_3_ = bf16[2,160,128]{2,1,0:T(8,128)(2,1)S(1)} collective-permute-done((bf16[2,160,128]{2,1,0:T(8,128)(2,1)S(1)}, bf16[2,160,128]{2,1,0:T(8,128)(2,1)S(1)}, u32[]{:S(2)}, u32[]{:S(2)}) %collective-permute-start.15) | collective-permute-done | bytes 81952 | tf_op jit(solution)/shard_map/ppermute | solution.py:436
  51.4 1.1 %collective-permute-start.17 = (bf16[128,1024]{1,0:T(8,128)(2,1)S(1)}, bf16[128,1024]{1,0:T(8,128)(2,1)S(1)}, u32[]{:S(2)}, u32[]{:S(2)}) collective-permute-start(bf16[128,1024]{1,0:T(8,128)(2,1)S(1)} %get-tuple-element.76.refs_0_.refs_1_), channel_id=1, source_target_pairs={{0,2},{1,3},{2,0},{3,1},{4,6},{5,7},{6,4},{7,5},{8,10},{9,11},{10,... | collective-permute-start | bytes 786440 | tf_op jit(solution)/shard_map/ppermute | solution.py:436
  52.5 2.5 %collective-permute-start.16 = (bf16[1,320,128]{2,1,0:T(8,128)(2,1)S(1)}, bf16[1,320,128]{2,1,0:T(8,128)(2,1)S(1)}, u32[]{:S(2)}, u32[]{:S(2)}) collective-permute-start(bf16[1,320,128]{2,1,0:T(8,128)(2,1)S(1)} %get-tuple-element.74), channel_id=1, source_target_pairs={{0,8},{1,9},{2,10},{3,11},{4,12},{5,13},{6,14},{7,15},{8,0},{9,1},... | collective-permute-start | bytes 245768 | tf_op jit(solution)/shard_map/ppermute | solution.py:436
  55.6 4.4 %collective-permute-done.17.refs_3_ = bf16[128,1024]{1,0:T(8,128)(2,1)S(1)} collective-permute-done((bf16[128,1024]{1,0:T(8,128)(2,1)S(1)}, bf16[128,1024]{1,0:T(8,128)(2,1)S(1)}, u32[]{:S(2)}, u32[]{:S(2)}) %collective-permute-start.17) | collective-permute-done | bytes 262176 | tf_op jit(solution)/shard_map/ppermute | solution.py:436
  60.6 1.1 %collective-permute-start.19 = (bf16[208,768]{1,0:T(8,128)(2,1)S(1)}, bf16[208,768]{1,0:T(8,128)(2,1)S(1)}, u32[]{:S(2)}, u32[]{:S(2)}) collective-permute-start(bf16[208,768]{1,0:T(8,128)(2,1)S(1)} %get-tuple-element.79.refs_2_.refs_1_), channel_id=1, source_target_pairs={{0,2},{1,3},{2,0},{3,1},{4,6},{5,7},{6,4},{7,5},{8,10},{9,11},{10,... | collective-permute-start | bytes 958472 | tf_op jit(solution)/shard_map/ppermute | solution.py:436
  63.0 1.1 %collective-permute-start.23 = (bf16[2,48,1024]{2,1,0:T(8,128)(2,1)S(1)}, bf16[2,48,1024]{2,1,0:T(8,128)(2,1)S(1)}, u32[]{:S(2)}, u32[]{:S(2)}) collective-permute-start(bf16[2,48,1024]{2,1,0:T(8,128)(2,1)S(1)} %get-tuple-element.84), channel_id=1, source_target_pairs={{0,4},{1,5},{2,6},{3,7},{4,0},{5,1},{6,2},{7,3},{8,12},{9,13},{10,... | collective-permute-start | bytes 589832 | tf_op jit(solution)/shard_map/ppermute | solution.py:436
  65.0 5.6 %collective-permute-done.19.refs_0_.refs_4_.refs_2_ = bf16[208,768]{1,0:T(8,128)(2,1)S(1)} collective-permute-done((bf16[208,768]{1,0:T(8,128)(2,1)S(1)}, bf16[208,768]{1,0:T(8,128)(2,1)S(1)}, u32[]{:S(2)}, u32[]{:S(2)}) %collective-permute-start.19) | collective-permute-done | bytes 319520 | tf_op jit(solution)/shard_map/ppermute | solution.py:436
  70.7 1.6 %collective-permute-done.24.refs_5_ = bf16[208,768]{1,0:T(8,128)(2,1)S(1)} collective-permute-done((bf16[208,768]{1,0:T(8,128)(2,1)S(1)}, bf16[208,768]{1,0:T(8,128)(2,1)S(1)}, u32[]{:S(2)}, u32[]{:S(2)}) %collective-permute-start.24) | collective-permute-done | bytes 319520 | tf_op jit(solution)/shard_map/ppermute | solution.py:436
  72.3 1.4 %conv_grad.1 = (f32[1,144,768]{2,1,0:T(8,128)S(1)}, f32[1,144,768]{2,1,0:T(8,128)S(1)}, bf16[1,144,768]{2,1,0:T(8,128)(2,1)S(1)}, bf16[1,144,768]{2,1,0:T(8,128)(2,1)S(1)}) custom-call(bf16[512,1024]{1,0:T(8,128)(2,1)S(1)} %get-tuple-element.68.refs_4_.refs_0_, bf16[192,512]{1,0:T(8,128)(2,1)S(1)} %get-tuple-element.81.refs_0_.refs_1_, ...), custom_call_target="tpu_custom_call" | custom-call | flops 805306368 | bytes 3850240 | tf_op jit(solution)/shard_map/conv_grad/pallas_call | solution.py:36
  73.7 1.9 %collective-permute-start.25 = (bf16[1,144,768]{2,1,0:T(8,128)(2,1)S(1)}, bf16[1,144,768]{2,1,0:T(8,128)(2,1)S(1)}, u32[]{:S(2)}, u32[]{:S(2)}) collective-permute-start(bf16[1,144,768]{2,1,0:T(8,128)(2,1)S(1)} %get-tuple-element.87), channel_id=1, source_target_pairs={{0,4},{1,5},{2,6},{3,7},{4,0},{5,1},{6,2},{7,3},{8,12},{9,13},{10,... | collective-permute-start | bytes 663560 | tf_op jit(solution)/shard_map/ppermute | solution.py:436
  75.8 6.2 %collective-permute-done.25.refs_1_ = bf16[1,144,768]{2,1,0:T(8,128)(2,1)S(1)} collective-permute-done((bf16[1,144,768]{2,1,0:T(8,128)(2,1)S(1)}, bf16[1,144,768]{2,1,0:T(8,128)(2,1)S(1)}, u32[]{:S(2)}, u32[]{:S(2)}) %collective-permute-start.25) | collective-permute-done | bytes 221216 | tf_op jit(solution)/shard_map/ppermute | solution.py:436
  82.1 2.5 %collective-permute-start.27 = (bf16[1,144,768]{2,1,0:T(8,128)(2,1)S(1)}, bf16[1,144,768]{2,1,0:T(8,128)(2,1)S(1)}, u32[]{:S(2)}, u32[]{:S(2)}) collective-permute-start(bf16[1,144,768]{2,1,0:T(8,128)(2,1)S(1)} %conv_send_on.1.refs_5_), channel_id=1, source_target_pairs={{0,8},{1,9},{2,10},{3,11},{4,12},{5,13},{6,14},{7,15},{8,0},{9,1},... | collective-permute-start | bytes 663560 | tf_op jit(solution)/shard_map/ppermute | solution.py:436
  85.1 2.0 %input_grad.1 = bf16[256,384]{1,0:T(8,128)(2,1)} custom-call(bf16[256,384]{1,0:T(8,128)(2,1)S(1)} %bitcast.9, bf16[208,768]{1,0:T(8,128)(2,1)S(1)} %get-tuple-element.79.refs_2_.refs_1_, bf16[208,768]{1,0:T(8,128)(2,1)S(1)} %collective-permute-done.19.refs_0_.refs_4_.refs_2_, bf16[16,768]{1,0:T(8,128)(2,1)S(1)} %collective-permute-done.20.refs_3_, ...), custom_call_target="tpu_custom_call" | custom-call | flops 754974720 | bytes 4005888 | tf_op jit(solution)/shard_map/input_grad/pallas_call | solution.py:36
  87.1 11.1 %collective-permute-done.28.refs_4_ = bf16[1,48,1024]{2,1,0:T(8,128)(2,1)S(1)} collective-permute-done((bf16[1,48,1024]{2,1,0:T(8,128)(2,1)S(1)}, bf16[1,48,1024]{2,1,0:T(8,128)(2,1)S(1)}, u32[]{:S(2)}, u32[]{:S(2)}) %collective-permute-start.28) | collective-permute-done | bytes 98336 | tf_op jit(solution)/shard_map/ppermute | solution.py:436
  (58 shorter events, 9.5 us)
Async XLA Ops:
  1.7 24.1 %copy-start.1 = (bf16[768,1024]{1,0:T(8,128)(2,1)S(1)}, bf16[768,1024]{1,0:T(8,128)(2,1)}, u32[]{:S(2)}) copy-start(bf16[768,1024]{1,0:T(8,128)(2,1)} %refs_1_.3) | copy-start | bytes 4718596
  1.8 6.5 %collective-permute-start = (bf16[2,384]{1,0:T(2,128)(2,1)S(1)}, bf16[2,384]{1,0:T(2,128)(2,1)S(1)}, u32[]{:S(2)}, u32[]{:S(2)}) collective-permute-start(bf16[2,384]{1,0:T(2,128)(2,1)S(1)} %get-tuple-element.53), channel_id=1, source_target_pairs={{0,2},{2,4},{4,6},{6,8},{8,10},{10,12},{12,14},{1,3},{3,5},{5,7},{... | collective-permute-start | bytes 4616 | tf_op jit(solution)/shard_map/ppermute | solution.py:467
  6.9 5.5 %collective-permute-start.1 = (bf16[2,384]{1,0:T(2,128)(2,1)S(1)}, bf16[2,384]{1,0:T(2,128)(2,1)S(1)}, u32[]{:S(2)}, u32[]{:S(2)}) collective-permute-start(bf16[2,384]{1,0:T(2,128)(2,1)S(1)} %get-tuple-element.54), channel_id=1, source_target_pairs={{2,0},{4,2},{6,4},{8,6},{10,8},{12,10},{14,12},{3,1},{5,3},{7,5},{... | collective-permute-start | bytes 4616 | tf_op jit(solution)/shard_map/ppermute | solution.py:468
  12.4 18.7 %copy-start.6 = (bf16[1,128,1536]{2,1,0:T(8,128)(2,1)S(1)}, bf16[1,128,1536]{2,1,0:T(8,128)(2,1)}, u32[]{:S(2)}) copy-start(bf16[1,128,1536]{2,1,0:T(8,128)(2,1)} %param.13) | copy-start | bytes 1179652
  14.2 6.9 %collective-permute-start.4 = (bf16[320,128]{1,0:T(8,128)(2,1)S(1)}, bf16[320,128]{1,0:T(8,128)(2,1)S(1)}, u32[]{:S(2)}, u32[]{:S(2)}) collective-permute-start(bf16[320,128]{1,0:T(8,128)(2,1)S(1)} %get-tuple-element.57.refs_2_), channel_id=1, source_target_pairs={{0,12},{1,13},{2,14},{3,15},{4,8},{5,9},{6,10},{7,11},{8,4},{9,5},... | collective-permute-start | bytes 245768 | tf_op jit(solution)/shard_map/ppermute | solution.py:436
  17.9 5.9 %collective-permute-start.3 = (bf16[320,128]{1,0:T(8,128)(2,1)S(1)}, bf16[320,128]{1,0:T(8,128)(2,1)S(1)}, u32[]{:S(2)}, u32[]{:S(2)}) collective-permute-start(bf16[320,128]{1,0:T(8,128)(2,1)S(1)} %get-tuple-element.57.refs_2_), channel_id=1, source_target_pairs={{0,8},{1,9},{2,10},{3,11},{4,12},{5,13},{6,14},{7,15},{8,0},{9,1},... | collective-permute-start | bytes 245768 | tf_op jit(solution)/shard_map/ppermute | solution.py:436
  17.9 7.9 %collective-permute-start.2 = (bf16[320,128]{1,0:T(8,128)(2,1)S(1)}, bf16[320,128]{1,0:T(8,128)(2,1)S(1)}, u32[]{:S(2)}, u32[]{:S(2)}) collective-permute-start(bf16[320,128]{1,0:T(8,128)(2,1)S(1)} %get-tuple-element.57.refs_2_), channel_id=1, source_target_pairs={{0,4},{1,5},{2,6},{3,7},{4,0},{5,1},{6,2},{7,3},{8,12},{9,13},{10,... | collective-permute-start | bytes 245768 | tf_op jit(solution)/shard_map/ppermute | solution.py:436
  18.7 7.8 %collective-permute-start.5 = (bf16[320,128]{1,0:T(8,128)(2,1)S(1)}, bf16[320,128]{1,0:T(8,128)(2,1)S(1)}, u32[]{:S(2)}, u32[]{:S(2)}) collective-permute-start(bf16[320,128]{1,0:T(8,128)(2,1)S(1)} %get-tuple-element.57.refs_2_), channel_id=1, source_target_pairs={{0,2},{1,3},{2,0},{3,1},{4,6},{5,7},{6,4},{7,5},{8,10},{9,11},{10,... | collective-permute-start | bytes 245768 | tf_op jit(solution)/shard_map/ppermute | solution.py:436
  21.1 5.4 %collective-permute-start.8 = (bf16[320,128]{1,0:T(8,128)(2,1)S(1)}, bf16[320,128]{1,0:T(8,128)(2,1)S(1)}, u32[]{:S(2)}, u32[]{:S(2)}) collective-permute-start(bf16[320,128]{1,0:T(8,128)(2,1)S(1)} %collective-permute-done.4.refs_5_), channel_id=1, source_target_pairs={{0,2},{1,3},{2,0},{3,1},{4,6},{5,7},{6,4},{7,5},{8,10},{9,11},{10,... | collective-permute-start | bytes 245768 | tf_op jit(solution)/shard_map/ppermute | solution.py:436
  23.8 4.9 %collective-permute-start.7 = (bf16[320,128]{1,0:T(8,128)(2,1)S(1)}, bf16[320,128]{1,0:T(8,128)(2,1)S(1)}, u32[]{:S(2)}, u32[]{:S(2)}) collective-permute-start(bf16[320,128]{1,0:T(8,128)(2,1)S(1)} %collective-permute-done.3.refs_4_), channel_id=1, source_target_pairs={{0,2},{1,3},{2,0},{3,1},{4,6},{5,7},{6,4},{7,5},{8,10},{9,11},{10,... | collective-permute-start | bytes 245768 | tf_op jit(solution)/shard_map/ppermute | solution.py:436
  25.8 4.4 %collective-permute-start.6 = (bf16[320,128]{1,0:T(8,128)(2,1)S(1)}, bf16[320,128]{1,0:T(8,128)(2,1)S(1)}, u32[]{:S(2)}, u32[]{:S(2)}) collective-permute-start(bf16[320,128]{1,0:T(8,128)(2,1)S(1)} %collective-permute-done.2.refs_3_), channel_id=1, source_target_pairs={{0,2},{1,3},{2,0},{3,1},{4,6},{5,7},{6,4},{7,5},{8,10},{9,11},{10,... | collective-permute-start | bytes 245768 | tf_op jit(solution)/shard_map/ppermute | solution.py:436
  30.2 8.5 %collective-permute-start.12 = (bf16[480,384]{1,0:T(8,128)(2,1)S(1)}, bf16[480,384]{1,0:T(8,128)(2,1)S(1)}, u32[]{:S(2)}, u32[]{:S(2)}) collective-permute-start(bf16[480,384]{1,0:T(8,128)(2,1)S(1)} %get-tuple-element.66.refs_1_), channel_id=1, source_target_pairs={{0,2},{1,3},{2,0},{3,1},{4,6},{5,7},{6,4},{7,5},{8,10},{9,11},{10,... | collective-permute-start | bytes 1105928 | tf_op jit(solution)/shard_map/ppermute | solution.py:436
  31.1 9.2 %collective-permute-start.11 = (bf16[480,384]{1,0:T(8,128)(2,1)S(1)}, bf16[480,384]{1,0:T(8,128)(2,1)S(1)}, u32[]{:S(2)}, u32[]{:S(2)}) collective-permute-start(bf16[480,384]{1,0:T(8,128)(2,1)S(1)} %get-tuple-element.66.refs_1_), channel_id=1, source_target_pairs={{0,1},{1,0},{2,3},{3,2},{4,5},{5,4},{6,7},{7,6},{8,9},{9,8},{10,11... | collective-permute-start | bytes 1105928 | tf_op jit(solution)/shard_map/ppermute | solution.py:436
  38.8 1.7 %collective-permute-start.13 = (bf16[480,384]{1,0:T(8,128)(2,1)S(1)}, bf16[480,384]{1,0:T(8,128)(2,1)S(1)}, u32[]{:S(2)}, u32[]{:S(2)}) collective-permute-start(bf16[480,384]{1,0:T(8,128)(2,1)S(1)} %collective-permute-done.12.refs_3_), channel_id=1, source_target_pairs={{0,1},{1,0},{2,3},{3,2},{4,5},{5,4},{6,7},{7,6},{8,9},{9,8},{10,11... | collective-permute-start | bytes 1105928 | tf_op jit(solution)/shard_map/ppermute | solution.py:436
  38.8 6.8 %collective-permute-start.9 = (bf16[4,160,128]{2,1,0:T(8,128)(2,1)S(1)}, bf16[4,160,128]{2,1,0:T(8,128)(2,1)S(1)}, u32[]{:S(2)}, u32[]{:S(2)}) collective-permute-start(bf16[4,160,128]{2,1,0:T(8,128)(2,1)S(1)} %get-tuple-element.61), channel_id=1, source_target_pairs={{0,2},{1,3},{2,0},{3,1},{4,6},{5,7},{6,4},{7,5},{8,10},{9,11},{10,... | collective-permute-start | bytes 491528 | tf_op jit(solution)/shard_map/ppermute | solution.py:436
  39.3 6.3 %collective-permute-start.10 = (bf16[4,160,128]{2,1,0:T(8,128)(2,1)S(1)}, bf16[4,160,128]{2,1,0:T(8,128)(2,1)S(1)}, u32[]{:S(2)}, u32[]{:S(2)}) collective-permute-start(bf16[4,160,128]{2,1,0:T(8,128)(2,1)S(1)} %get-tuple-element.63), channel_id=1, source_target_pairs={{0,4},{1,5},{2,6},{3,7},{4,0},{5,1},{6,2},{7,3},{8,12},{9,13},{10,... | collective-permute-start | bytes 491528 | tf_op jit(solution)/shard_map/ppermute | solution.py:436
  45.7 4.5 %collective-permute-start.14 = (bf16[2,160,128]{2,1,0:T(8,128)(2,1)S(1)}, bf16[2,160,128]{2,1,0:T(8,128)(2,1)S(1)}, u32[]{:S(2)}, u32[]{:S(2)}) collective-permute-start(bf16[2,160,128]{2,1,0:T(8,128)(2,1)S(1)} %get-tuple-element.70), channel_id=1, source_target_pairs={{0,4},{1,5},{2,6},{3,7},{4,0},{5,1},{6,2},{7,3},{8,12},{9,13},{10,... | collective-permute-start | bytes 245768 | tf_op jit(solution)/shard_map/ppermute | solution.py:436
  46.8 4.4 %collective-permute-start.15 = (bf16[2,160,128]{2,1,0:T(8,128)(2,1)S(1)}, bf16[2,160,128]{2,1,0:T(8,128)(2,1)S(1)}, u32[]{:S(2)}, u32[]{:S(2)}) collective-permute-start(bf16[2,160,128]{2,1,0:T(8,128)(2,1)S(1)} %get-tuple-element.72), channel_id=1, source_target_pairs={{0,2},{1,3},{2,0},{3,1},{4,6},{5,7},{6,4},{7,5},{8,10},{9,11},{10,... | collective-permute-start | bytes 245768 | tf_op jit(solution)/shard_map/ppermute | solution.py:436
  51.3 4.4 %collective-permute-start.18 = (bf16[128,1024]{1,0:T(8,128)(2,1)S(1)}, bf16[128,1024]{1,0:T(8,128)(2,1)S(1)}, u32[]{:S(2)}, u32[]{:S(2)}) collective-permute-start(bf16[128,1024]{1,0:T(8,128)(2,1)S(1)} %get-tuple-element.76.refs_0_.refs_1_), channel_id=1, source_target_pairs={{0,1},{1,0},{2,3},{3,2},{4,5},{5,4},{6,7},{7,6},{8,9},{9,8},{10,11... | collective-permute-start | bytes 786440 | tf_op jit(solution)/shard_map/ppermute | solution.py:436
  51.4 8.7 %collective-permute-start.17 = (bf16[128,1024]{1,0:T(8,128)(2,1)S(1)}, bf16[128,1024]{1,0:T(8,128)(2,1)S(1)}, u32[]{:S(2)}, u32[]{:S(2)}) collective-permute-start(bf16[128,1024]{1,0:T(8,128)(2,1)S(1)} %get-tuple-element.76.refs_0_.refs_1_), channel_id=1, source_target_pairs={{0,2},{1,3},{2,0},{3,1},{4,6},{5,7},{6,4},{7,5},{8,10},{9,11},{10,... | collective-permute-start | bytes 786440 | tf_op jit(solution)/shard_map/ppermute | solution.py:436
  52.5 7.6 %collective-permute-start.16 = (bf16[1,320,128]{2,1,0:T(8,128)(2,1)S(1)}, bf16[1,320,128]{2,1,0:T(8,128)(2,1)S(1)}, u32[]{:S(2)}, u32[]{:S(2)}) collective-permute-start(bf16[1,320,128]{2,1,0:T(8,128)(2,1)S(1)} %get-tuple-element.74), channel_id=1, source_target_pairs={{0,8},{1,9},{2,10},{3,11},{4,12},{5,13},{6,14},{7,15},{8,0},{9,1},... | collective-permute-start | bytes 245768 | tf_op jit(solution)/shard_map/ppermute | solution.py:436
  60.5 1.6 %collective-permute-start.22 = (bf16[128,1024]{1,0:T(8,128)(2,1)S(1)}, bf16[128,1024]{1,0:T(8,128)(2,1)S(1)}, u32[]{:S(2)}, u32[]{:S(2)}) collective-permute-start(bf16[128,1024]{1,0:T(8,128)(2,1)S(1)} %collective-permute-done.17.refs_3_), channel_id=1, source_target_pairs={{0,1},{1,0},{2,3},{3,2},{4,5},{5,4},{6,7},{7,6},{8,9},{9,8},{10,11... | collective-permute-start | bytes 786440 | tf_op jit(solution)/shard_map/ppermute | solution.py:436
  60.6 10.0 %collective-permute-start.19 = (bf16[208,768]{1,0:T(8,128)(2,1)S(1)}, bf16[208,768]{1,0:T(8,128)(2,1)S(1)}, u32[]{:S(2)}, u32[]{:S(2)}) collective-permute-start(bf16[208,768]{1,0:T(8,128)(2,1)S(1)} %get-tuple-element.79.refs_2_.refs_1_), channel_id=1, source_target_pairs={{0,2},{1,3},{2,0},{3,1},{4,6},{5,7},{6,4},{7,5},{8,10},{9,11},{10,... | collective-permute-start | bytes 958472 | tf_op jit(solution)/shard_map/ppermute | solution.py:436
  62.1 23.0 %copy-start.5 = (bf16[1,256,384]{2,1,0:T(8,128)(2,1)S(1)}, bf16[1,256,384]{2,1,0:T(8,128)(2,1)}, u32[]{:S(2)}) copy-start(bf16[1,256,384]{2,1,0:T(8,128)(2,1)} %param.7) | copy-start | bytes 589828
  63.0 7.6 %collective-permute-start.23 = (bf16[2,48,1024]{2,1,0:T(8,128)(2,1)S(1)}, bf16[2,48,1024]{2,1,0:T(8,128)(2,1)S(1)}, u32[]{:S(2)}, u32[]{:S(2)}) collective-permute-start(bf16[2,48,1024]{2,1,0:T(8,128)(2,1)S(1)} %get-tuple-element.84), channel_id=1, source_target_pairs={{0,4},{1,5},{2,6},{3,7},{4,0},{5,1},{6,2},{7,3},{8,12},{9,13},{10,... | collective-permute-start | bytes 589832 | tf_op jit(solution)/shard_map/ppermute | solution.py:436
  64.1 0.9 collective-permute-start.20
  64.9 5.8 %collective-permute-start.21 = (bf16[208,768]{1,0:T(8,128)(2,1)S(1)}, bf16[208,768]{1,0:T(8,128)(2,1)S(1)}, u32[]{:S(2)}, u32[]{:S(2)}) collective-permute-start(bf16[208,768]{1,0:T(8,128)(2,1)S(1)} %get-tuple-element.79.refs_2_.refs_1_), channel_id=1, source_target_pairs={{0,1},{1,0},{2,3},{3,2},{4,5},{5,4},{6,7},{7,6},{8,9},{9,8},{10,11... | collective-permute-start | bytes 958472 | tf_op jit(solution)/shard_map/ppermute | solution.py:436
  70.6 1.7 %collective-permute-start.24 = (bf16[208,768]{1,0:T(8,128)(2,1)S(1)}, bf16[208,768]{1,0:T(8,128)(2,1)S(1)}, u32[]{:S(2)}, u32[]{:S(2)}) collective-permute-start(bf16[208,768]{1,0:T(8,128)(2,1)S(1)} %get-tuple-element.85), channel_id=1, source_target_pairs={{0,1},{1,0},{2,3},{3,2},{4,5},{5,4},{6,7},{7,6},{8,9},{9,8},{10,11... | collective-permute-start | bytes 958472 | tf_op jit(solution)/shard_map/ppermute | solution.py:436
  73.7 8.3 %collective-permute-start.25 = (bf16[1,144,768]{2,1,0:T(8,128)(2,1)S(1)}, bf16[1,144,768]{2,1,0:T(8,128)(2,1)S(1)}, u32[]{:S(2)}, u32[]{:S(2)}) collective-permute-start(bf16[1,144,768]{2,1,0:T(8,128)(2,1)S(1)} %get-tuple-element.87), channel_id=1, source_target_pairs={{0,4},{1,5},{2,6},{3,7},{4,0},{5,1},{6,2},{7,3},{8,12},{9,13},{10,... | collective-permute-start | bytes 663560 | tf_op jit(solution)/shard_map/ppermute | solution.py:436
  75.7 22.5 %collective-permute-start.26 = (bf16[1,144,768]{2,1,0:T(8,128)(2,1)S(1)}, bf16[1,144,768]{2,1,0:T(8,128)(2,1)S(1)}, u32[]{:S(2)}, u32[]{:S(2)}) collective-permute-start(bf16[1,144,768]{2,1,0:T(8,128)(2,1)S(1)} %get-tuple-element.89), channel_id=1, source_target_pairs={{0,4},{1,5},{2,6},{3,7},{4,0},{5,1},{6,2},{7,3},{8,12},{9,13},{10,... | collective-permute-start | bytes 663560 | tf_op jit(solution)/shard_map/ppermute | solution.py:436
  82.1 16.1 %collective-permute-start.27 = (bf16[1,144,768]{2,1,0:T(8,128)(2,1)S(1)}, bf16[1,144,768]{2,1,0:T(8,128)(2,1)S(1)}, u32[]{:S(2)}, u32[]{:S(2)}) collective-permute-start(bf16[1,144,768]{2,1,0:T(8,128)(2,1)S(1)} %conv_send_on.1.refs_5_), channel_id=1, source_target_pairs={{0,8},{1,9},{2,10},{3,11},{4,12},{5,13},{6,14},{7,15},{8,0},{9,1},... | collective-permute-start | bytes 663560 | tf_op jit(solution)/shard_map/ppermute | solution.py:436
  84.6 13.6 %collective-permute-start.28 = (bf16[1,48,1024]{2,1,0:T(8,128)(2,1)S(1)}, bf16[1,48,1024]{2,1,0:T(8,128)(2,1)S(1)}, u32[]{:S(2)}, u32[]{:S(2)}) collective-permute-start(bf16[1,48,1024]{2,1,0:T(8,128)(2,1)S(1)} %get-tuple-element.91), channel_id=1, source_target_pairs={{0,8},{1,9},{2,10},{3,11},{4,12},{5,13},{6,14},{7,15},{8,0},{9,1},... | collective-permute-start | bytes 294920 | tf_op jit(solution)/shard_map/ppermute | solution.py:436
  (5 other events, 40.0 us)

commit v5 on v4

--- a/solution.py
+++ b/solution.py
@@ -85,22 +85,25 @@
     return jnp.concatenate(parts, axis=1)
 
 
-def open_kernel(x, pad, first, last):
+def open_kernel(x, pad, ends):
     positions, channels = x.shape
-    first[...] = x[:16][:2]
-    last[...] = x[positions - 16 :][14:]
+    ends[:16] = x[:16]
+    ends[16:] = x[positions - 16 :]
     put(pad, 0, jnp.zeros((8, channels), F32))
     put(pad, 8, gelu(x[...].astype(F32)).astype(BF).astype(F32))
     put(pad, 8 + positions, jnp.zeros((pad.shape[1] - 8 - positions, channels), F32))
 
 
-def front_kernel(ready, before, after, weight, gain, wk, wv, kv_out, early, normed_out, pooled_out, pad):
-    channels = before.shape[1]
+def front_kernel(ready, pair, across, weight, gain, wk, wv, kv_out, early, normed_out, pooled_out, pad):
     tokens = pooled_out.shape[0]
     ext = early.shape[0] // 2
+    even = lax.axis_index("seq") % 2 == 0
+    pair_wide, across_wide = pair[...].astype(F32), across[...].astype(F32)
+    before = jnp.where(even, across_wide[16:], pair_wide[16:])[14:]
+    after = jnp.where(even, pair_wide[:16], across_wide[:16])[:2]
     pad[...] = ready[...]
-    put(pad, 6, gelu(before[...].astype(F32)).astype(BF).astype(F32))
-    put(pad, 8 + 2 * tokens, gelu(after[...].astype(F32)).astype(BF).astype(F32))
+    put(pad, 6, gelu(before).astype(BF).astype(F32))
+    put(pad, 8 + 2 * tokens, gelu(after).astype(BF).astype(F32))
     pieces = [every_second(pad, 6 + u, tokens).astype(BF) for u in range(6)]
     total = None
     for tap in range(5):
@@ -454,18 +457,17 @@
 
     bits = list(range(devices.bit_length() - 1))
     order = [mask // 2 for mask in ordered(bits[1:])]
-    up = [(i, i + 1) for i in range(devices - 1)]
-    down = [(j, i) for i, j in up]
+    crossing = [(i, i + 1) for i in range(1, devices - 1, 2)]
+    crossing = crossing + [(j, i) for i, j in crossing]
     pad_shape = (channels // LANES, 8 + 2 * ext + 8, LANES)
-    ready, first, last = run(
+    ready, ends = run(
         open_kernel,
-        [(pad_shape, F32), ((2, channels), BF), ((2, channels), BF)],
+        [(pad_shape, F32), ((32, channels), BF)],
         [x],
         flops=4 * 10**9,
         name="gelu",
     )
-    before = lax.ppermute(last, "seq", up)
-    after = lax.ppermute(first, "seq", down)
+    pair, across = swap(ends, 1), lax.ppermute(ends, "seq", crossing)
     wv = wv.T
     kv, early, normed, pooled = run(
         front_kernel,
@@ -475,7 +477,7 @@
             ((tokens, width), BF),
             ((tokens, width), F32),
         ],
-        [ready, before, after, conv_weight, gain, wk, wv],
+        [ready, pair, across, conv_weight, gain, wk, wv],
         [pltpu.VMEM(pad_shape, F32)],
         flops=2 * positions * taps * channels * width,
         name="front",
@@ -552,10 +554,6 @@
         [keep_a, in_a, keep_b, in_b],
         name="kv_cot_merge",
     )
-    query_cot = held(query_cot, keep)
-    query_near, query_core = swap(query_cot, 1), swap(query_cot, 0, 1)
-    pooled = held(pooled, query_near, query_core)
-    kv_cot = halved(keep, send, bits[2:], "kv_cot_fold")
     (normed_cot,) = run(
         query_cot_kernel,
         [((tokens, width), F32)],
@@ -563,6 +561,9 @@
         flops=2 * tokens * width * heads * key_size,
         name="query_part",
     )
+    query_cot = held(query_cot, keep)
+    query_near, query_core = swap(query_cot, 1), swap(query_cot, 0, 1)
+    kv_cot = halved(keep, send, bits[2:], "kv_cot_fold")
     message, edge = run(
         middle_kernel,
         [((tokens + 16 + tokens // 2, width), BF), ((16, width), BF)],
@@ -571,8 +572,6 @@
         name="conv_cot",
     )
     near_message, core_message = swap(message, 1), swap(message, 0, 1)
-    crossing = [(i, i + 1) for i in range(1, devices - 1, 2)]
-    crossing = crossing + [(j, i) for i, j in crossing]
     edge_in = lax.ppermute(edge, "seq", crossing)
     query_half = (groups // 2, norm_pad, heads * key_size)
     keep, send = run(
@@ -618,7 +617,7 @@
     )
     far_in = swap(far_send, 2)
     near_in = swap(near_send, 2)
-    (far_sum,) = run(send_on_kernel, [(chunks, BF)], [far_keep, far_in], name="conv_send_on")
+    (far_sum,) = run(send_on_kernel, [(chunks, BF)], [held(far_keep, query_parts[1]), far_in], name="conv_send_on")
     conv_parts = [near_keep, near_in, swap(far_sum, 4)]
     if len(bits) > 3:
         keep, send = fold(conv_parts, "conv_fold")

time: 99.3 us -> 95.2 us (0.959)
  waiting for transfers between devices: 44.6 us -> 36.7 us
  starting transfers between devices: 34.5 us -> 38.4 us
    ppermute x26 -> x27, starting transfers between devices: 27.3 us -> 36.8 us  [swap(): lax.ppermute(value, both_axes, [(i, i ^ mask) for i in range(owners)])]
    ppermute x2 -> x1, starting transfers between devices: 6.43 us -> 0.79 us  [on_device(): pair, across = (swap(ends, 1), lax.ppermute(ends, 'seq', crossing))]
    ppermute x2 -> x1, waiting for transfers between devices: 4.14 us -> 0.01 us  [on_device(): pair, across = (swap(ends, 1), lax.ppermute(ends, 'seq', crossing))]
    ppermute x26 -> x27, waiting for transfers between devices: 40.5 us -> 36.7 us  [swap(): lax.ppermute(value, both_axes, [(i, i ^ mask) for i in range(owners)])]
  transfers between devices with their start and end apart: 29 -> 29, of which waited for: 15 -> 17; matrix products, arithmetic and copies ran while one was open for 0% -> 0% of each run, Pallas kernels for 13% -> 14%
where the time goes in v5:
time: 95.2 us; the launch traced here: 95.1 us
  starting transfers between devices  38.4 us (40%)
  waiting for transfers between devices  36.7 us (39%)
  Pallas kernels  18.1 us (19%)
  local copies, waits for them, and re-layouts  0.96 us (1%)
    ppermute x27, starting transfers between devices, swap(): lax.ppermute(value, both_axes, [(i, i ^ mask) for i in range(owners)])  36.8 us
    ppermute x27, waiting for transfers between devices, swap(): lax.ppermute(value, both_axes, [(i, i ^ mask) for i in range(owners)])  36.7 us
    pallas_call x15, Pallas kernels, run(): pl.pallas_call(whole, out_shape=[jax.ShapeDtypeStruct(s, t) for s, t in o...  18.1 us
  transfers between devices with their start and end apart: 29, of which 17 were waited for; matrix products, arithmetic and copies ran while one was open for 0% of the time, Pallas kernels for 14%

profile of v5, /device:TPU:0, one launch (start us, length us, event | category | flops | bytes accessed | tf_op | source)
XLA Modules:
  0.0 95.1 jit_solution(11036925207363932066)
XLA Ops:
  0.6 0.9 copy-done.4
  2.6 5.9 %collective-permute-start = (bf16[32,384]{1,0:T(8,128)(2,1)S(1)}, bf16[32,384]{1,0:T(8,128)(2,1)S(1)}, u32[]{:S(2)}, u32[]{:S(2)}) collective-permute-start(bf16[32,384]{1,0:T(8,128)(2,1)S(1)} %get-tuple-element.52), channel_id=1, source_target_pairs={{0,2},{1,3},{2,0},{3,1},{4,6},{5,7},{6,4},{7,5},{8,10},{9,11},{10,... | collective-permute-start | bytes 73736 | tf_op jit(solution)/shard_map/ppermute | solution.py:439
  8.5 1.8 %collective-permute-done.refs_1_ = bf16[32,384]{1,0:T(8,128)(2,1)S(1)} collective-permute-done((bf16[32,384]{1,0:T(8,128)(2,1)S(1)}, bf16[32,384]{1,0:T(8,128)(2,1)S(1)}, u32[]{:S(2)}, u32[]{:S(2)}) %collective-permute-start) | collective-permute-done | bytes 24608 | tf_op jit(solution)/shard_map/ppermute | solution.py:439
  10.3 1.9 %front.1 = (bf16[320,128]{1,0:T(8,128)(2,1)S(1)}, bf16[288,384]{1,0:T(8,128)(2,1)S(1)}, bf16[128,768]{1,0:T(8,128)(2,1)S(1)}, f32[128,768]{1,0:T(8,128)S(1)}) custom-call(f32[3,304,128]{2,1,0:T(8,128)S(1)} %get-tuple-element.51.refs_0_, bf16[32,384]{1,0:T(8,128)(2,1)S(1)} %collective-permute-done.refs_1_, ...), custom_call_target="tpu_custom_call" | custom-call | flops 754974720 | bytes 4852736 | tf_op jit(solution)/shard_map/front/pallas_call | solution.py:36
  12.2 4.1 %collective-permute-start.4 = (bf16[320,128]{1,0:T(8,128)(2,1)S(1)}, bf16[320,128]{1,0:T(8,128)(2,1)S(1)}, u32[]{:S(2)}, u32[]{:S(2)}) collective-permute-start(bf16[320,128]{1,0:T(8,128)(2,1)S(1)} %get-tuple-element.55.refs_2_), channel_id=1, source_target_pairs={{0,12},{1,13},{2,14},{3,15},{4,8},{5,9},{6,10},{7,11},{8,4},{9,5},... | collective-permute-start | bytes 245768 | tf_op jit(solution)/shard_map/ppermute | solution.py:439
  16.9 1.8 %collective-permute-start.5 = (bf16[320,128]{1,0:T(8,128)(2,1)S(1)}, bf16[320,128]{1,0:T(8,128)(2,1)S(1)}, u32[]{:S(2)}, u32[]{:S(2)}) collective-permute-start(bf16[320,128]{1,0:T(8,128)(2,1)S(1)} %get-tuple-element.55.refs_2_), channel_id=1, source_target_pairs={{0,2},{1,3},{2,0},{3,1},{4,6},{5,7},{6,4},{7,5},{8,10},{9,11},{10,... | collective-permute-start | bytes 245768 | tf_op jit(solution)/shard_map/ppermute | solution.py:439
  18.7 2.4 %collective-permute-start.8 = (bf16[320,128]{1,0:T(8,128)(2,1)S(1)}, bf16[320,128]{1,0:T(8,128)(2,1)S(1)}, u32[]{:S(2)}, u32[]{:S(2)}) collective-permute-start(bf16[320,128]{1,0:T(8,128)(2,1)S(1)} %collective-permute-done.4.refs_5_), channel_id=1, source_target_pairs={{0,2},{1,3},{2,0},{3,1},{4,6},{5,7},{6,4},{7,5},{8,10},{9,11},{10,... | collective-permute-start | bytes 245768 | tf_op jit(solution)/shard_map/ppermute | solution.py:439
  21.1 1.0 %collective-permute-done.3.refs_4_ = bf16[320,128]{1,0:T(8,128)(2,1)S(1)} collective-permute-done((bf16[320,128]{1,0:T(8,128)(2,1)S(1)}, bf16[320,128]{1,0:T(8,128)(2,1)S(1)}, u32[]{:S(2)}, u32[]{:S(2)}) %collective-permute-start.3) | collective-permute-done | bytes 81952 | tf_op jit(solution)/shard_map/ppermute | solution.py:439
  22.1 1.3 %collective-permute-start.7 = (bf16[320,128]{1,0:T(8,128)(2,1)S(1)}, bf16[320,128]{1,0:T(8,128)(2,1)S(1)}, u32[]{:S(2)}, u32[]{:S(2)}) collective-permute-start(bf16[320,128]{1,0:T(8,128)(2,1)S(1)} %collective-permute-done.3.refs_4_), channel_id=1, source_target_pairs={{0,2},{1,3},{2,0},{3,1},{4,6},{5,7},{6,4},{7,5},{8,10},{9,11},{10,... | collective-permute-start | bytes 245768 | tf_op jit(solution)/shard_map/ppermute | solution.py:439
  24.9 1.8 %collective-permute-done.7.refs_8_ = bf16[320,128]{1,0:T(8,128)(2,1)S(1)} collective-permute-done((bf16[320,128]{1,0:T(8,128)(2,1)S(1)}, bf16[320,128]{1,0:T(8,128)(2,1)S(1)}, u32[]{:S(2)}, u32[]{:S(2)}) %collective-permute-start.7) | collective-permute-done | bytes 81952 | tf_op jit(solution)/shard_map/ppermute | solution.py:439
  26.6 1.2 %collective-permute-done.6.refs_7_ = bf16[320,128]{1,0:T(8,128)(2,1)S(1)} collective-permute-done((bf16[320,128]{1,0:T(8,128)(2,1)S(1)}, bf16[320,128]{1,0:T(8,128)(2,1)S(1)}, u32[]{:S(2)}, u32[]{:S(2)}) %collective-permute-start.6) | collective-permute-done | bytes 81952 | tf_op jit(solution)/shard_map/ppermute | solution.py:439
  28.7 6.5 %attend.1 = (bf16[128,1536]{1,0:T(8,128)(2,1)}, bf16[128,1024]{1,0:T(8,128)(2,1)S(1)}, f32[4,160,128]{2,1,0:T(8,128)S(1)}, bf16[4,160,128]{2,1,0:T(8,128)(2,1)S(...) custom-call(bf16[128,1024]{1,0:T(8,128)(2,1)S(1)} %get-tuple-element.56.refs_0_, ...), custom_call_target="tpu_custom_call" | custom-call | flops 2013265920 | bytes 2949120 | tf_op jit(solution)/shard_map/attend/pallas_call | solution.py:36
  35.3 1.1 %collective-permute-done.12.refs_3_ = bf16[480,384]{1,0:T(8,128)(2,1)S(1)} collective-permute-done((bf16[480,384]{1,0:T(8,128)(2,1)S(1)}, bf16[480,384]{1,0:T(8,128)(2,1)S(1)}, u32[]{:S(2)}, u32[]{:S(2)}) %collective-permute-start.12) | collective-permute-done | bytes 368672 | tf_op jit(solution)/shard_map/ppermute | solution.py:439
  38.1 2.4 %select.1 = (bf16[512,1024]{1,0:T(8,128)(2,1)S(1)}, bf16[192,512]{1,0:T(8,128)(2,1)S(1)}) custom-call(bf16[192,128]{1,0:T(8,128)(2,1)S(1)} %get-tuple-element.62.refs_0_, bf16[480,384]{1,0:T(8,128)(2,1)S(1)} %get-tuple-element.64.refs_1_, bf16[480,384]{1,0:T(8,128)(2,1)S(1)} %collective-permute-done.11.refs_2_, ...), custom_call_target="tpu_custom_call" | custom-call | flops 2013265920 | bytes 2768896 | tf_op jit(solution)/shard_map/select/pallas_call | solution.py:36
  40.5 3.1 %collective-permute-done.10.refs_3_ = bf16[4,160,128]{2,1,0:T(8,128)(2,1)S(1)} collective-permute-done((bf16[4,160,128]{2,1,0:T(8,128)(2,1)S(1)}, bf16[4,160,128]{2,1,0:T(8,128)(2,1)S(1)}, u32[]{:S(2)}, u32[]{:S(2)}) %collective-permute-start.10) | collective-permute-done | bytes 163872 | tf_op jit(solution)/shard_map/ppermute | solution.py:439
  44.2 1.1 %collective-permute-start.15 = (bf16[2,160,128]{2,1,0:T(8,128)(2,1)S(1)}, bf16[2,160,128]{2,1,0:T(8,128)(2,1)S(1)}, u32[]{:S(2)}, u32[]{:S(2)}) collective-permute-start(bf16[2,160,128]{2,1,0:T(8,128)(2,1)S(1)} %get-tuple-element.70), channel_id=1, source_target_pairs={{0,2},{1,3},{2,0},{3,1},{4,6},{5,7},{6,4},{7,5},{8,10},{9,11},{10,... | collective-permute-start | bytes 245768 | tf_op jit(solution)/shard_map/ppermute | solution.py:439
  45.2 2.9 %collective-permute-done.14.refs_1_ = bf16[2,160,128]{2,1,0:T(8,128)(2,1)S(1)} collective-permute-done((bf16[2,160,128]{2,1,0:T(8,128)(2,1)S(1)}, bf16[2,160,128]{2,1,0:T(8,128)(2,1)S(1)}, u32[]{:S(2)}, u32[]{:S(2)}) %collective-permute-start.14) | collective-permute-done | bytes 81952 | tf_op jit(solution)/shard_map/ppermute | solution.py:439
  48.6 1.1 %collective-permute-start.21 = (bf16[128,1024]{1,0:T(8,128)(2,1)S(1)}, bf16[128,1024]{1,0:T(8,128)(2,1)S(1)}, u32[]{:S(2)}, u32[]{:S(2)}) collective-permute-start(bf16[128,1024]{1,0:T(8,128)(2,1)S(1)} %get-tuple-element.78.refs_0_.refs_1_), channel_id=1, source_target_pairs={{0,2},{1,3},{2,0},{3,1},{4,6},{5,7},{6,4},{7,5},{8,10},{9,11},{10,... | collective-permute-start | bytes 786440 | tf_op jit(solution)/shard_map/ppermute | solution.py:439
  49.8 2.9 %collective-permute-start.16 = (bf16[1,320,128]{2,1,0:T(8,128)(2,1)S(1)}, bf16[1,320,128]{2,1,0:T(8,128)(2,1)S(1)}, u32[]{:S(2)}, u32[]{:S(2)}) collective-permute-start(bf16[1,320,128]{2,1,0:T(8,128)(2,1)S(1)} %get-tuple-element.72), channel_id=1, source_target_pairs={{0,8},{1,9},{2,10},{3,11},{4,12},{5,13},{6,14},{7,15},{8,0},{9,1},... | collective-permute-start | bytes 245768 | tf_op jit(solution)/shard_map/ppermute | solution.py:439
  53.4 1.7 %collective-permute-done.16.refs_1_ = bf16[1,320,128]{2,1,0:T(8,128)(2,1)S(1)} collective-permute-done((bf16[1,320,128]{2,1,0:T(8,128)(2,1)S(1)}, bf16[1,320,128]{2,1,0:T(8,128)(2,1)S(1)}, u32[]{:S(2)}, u32[]{:S(2)}) %collective-permute-start.16) | collective-permute-done | bytes 81952 | tf_op jit(solution)/shard_map/ppermute | solution.py:439
  55.6 1.0 %collective-permute-start.17 = (bf16[208,768]{1,0:T(8,128)(2,1)S(1)}, bf16[208,768]{1,0:T(8,128)(2,1)S(1)}, u32[]{:S(2)}, u32[]{:S(2)}) collective-permute-start(bf16[208,768]{1,0:T(8,128)(2,1)S(1)} %get-tuple-element.75.refs_2_.refs_1_), channel_id=1, source_target_pairs={{0,2},{1,3},{2,0},{3,1},{4,6},{5,7},{6,4},{7,5},{8,10},{9,11},{10,... | collective-permute-start | bytes 958472 | tf_op jit(solution)/shard_map/ppermute | solution.py:439
  58.0 1.7 %collective-permute-start.23 = (bf16[2,48,1024]{2,1,0:T(8,128)(2,1)S(1)}, bf16[2,48,1024]{2,1,0:T(8,128)(2,1)S(1)}, u32[]{:S(2)}, u32[]{:S(2)}) collective-permute-start(bf16[2,48,1024]{2,1,0:T(8,128)(2,1)S(1)} %get-tuple-element.81), channel_id=1, source_target_pairs={{0,4},{1,5},{2,6},{3,7},{4,0},{5,1},{6,2},{7,3},{8,12},{9,13},{10,... | collective-permute-start | bytes 589832 | tf_op jit(solution)/shard_map/ppermute | solution.py:439
  60.7 4.9 %collective-permute-done.17.refs_0_.refs_4_.refs_2_ = bf16[208,768]{1,0:T(8,128)(2,1)S(1)} collective-permute-done((bf16[208,768]{1,0:T(8,128)(2,1)S(1)}, bf16[208,768]{1,0:T(8,128)(2,1)S(1)}, u32[]{:S(2)}, u32[]{:S(2)}) %collective-permute-start.17) | collective-permute-done | bytes 319520 | tf_op jit(solution)/shard_map/ppermute | solution.py:439
  65.8 1.6 %collective-permute-done.24.refs_5_ = bf16[208,768]{1,0:T(8,128)(2,1)S(1)} collective-permute-done((bf16[208,768]{1,0:T(8,128)(2,1)S(1)}, bf16[208,768]{1,0:T(8,128)(2,1)S(1)}, u32[]{:S(2)}, u32[]{:S(2)}) %collective-permute-start.24) | collective-permute-done | bytes 319520 | tf_op jit(solution)/shard_map/ppermute | solution.py:439
  67.4 1.4 %conv_grad.1 = (f32[1,144,768]{2,1,0:T(8,128)S(1)}, f32[1,144,768]{2,1,0:T(8,128)S(1)}, bf16[1,144,768]{2,1,0:T(8,128)(2,1)S(1)}, bf16[1,144,768]{2,1,0:T(8,128)(2,1)S(1)}) custom-call(bf16[512,1024]{1,0:T(8,128)(2,1)S(1)} %get-tuple-element.66.refs_4_.refs_0_, bf16[192,512]{1,0:T(8,128)(2,1)S(1)} %get-tuple-element.77.refs_0_.refs_1_, ...), custom_call_target="tpu_custom_call" | custom-call | flops 805306368 | bytes 3850240 | tf_op jit(solution)/shard_map/conv_grad/pallas_call | solution.py:36
  68.8 2.2 %collective-permute-start.26 = (bf16[1,144,768]{2,1,0:T(8,128)(2,1)S(1)}, bf16[1,144,768]{2,1,0:T(8,128)(2,1)S(1)}, u32[]{:S(2)}, u32[]{:S(2)}) collective-permute-start(bf16[1,144,768]{2,1,0:T(8,128)(2,1)S(1)} %get-tuple-element.86), channel_id=1, source_target_pairs={{0,4},{1,5},{2,6},{3,7},{4,0},{5,1},{6,2},{7,3},{8,12},{9,13},{10,... | collective-permute-start | bytes 663560 | tf_op jit(solution)/shard_map/ppermute | solution.py:439
  71.0 2.9 %collective-permute-start.25 = (bf16[1,48,1024]{2,1,0:T(8,128)(2,1)S(1)}, bf16[1,48,1024]{2,1,0:T(8,128)(2,1)S(1)}, u32[]{:S(2)}, u32[]{:S(2)}) collective-permute-start(bf16[1,48,1024]{2,1,0:T(8,128)(2,1)S(1)} %get-tuple-element.84), channel_id=1, source_target_pairs={{0,8},{1,9},{2,10},{3,11},{4,12},{5,13},{6,14},{7,15},{8,0},{9,1},... | collective-permute-start | bytes 294920 | tf_op jit(solution)/shard_map/ppermute | solution.py:439
  73.9 4.2 %collective-permute-done.25.refs_4_ = bf16[1,48,1024]{2,1,0:T(8,128)(2,1)S(1)} collective-permute-done((bf16[1,48,1024]{2,1,0:T(8,128)(2,1)S(1)}, bf16[1,48,1024]{2,1,0:T(8,128)(2,1)S(1)}, u32[]{:S(2)}, u32[]{:S(2)}) %collective-permute-start.25) | collective-permute-done | bytes 98336 | tf_op jit(solution)/shard_map/ppermute | solution.py:439
  78.1 3.9 %collective-permute-start.27 = (bf16[1,144,768]{2,1,0:T(8,128)(2,1)S(1)}, bf16[1,144,768]{2,1,0:T(8,128)(2,1)S(1)}, u32[]{:S(2)}, u32[]{:S(2)}) collective-permute-start(bf16[1,144,768]{2,1,0:T(8,128)(2,1)S(1)} %get-tuple-element.88), channel_id=1, source_target_pairs={{0,4},{1,5},{2,6},{3,7},{4,0},{5,1},{6,2},{7,3},{8,12},{9,13},{10,... | collective-permute-start | bytes 663560 | tf_op jit(solution)/shard_map/ppermute | solution.py:439
  82.2 2.0 %input_grad.1 = bf16[256,384]{1,0:T(8,128)(2,1)} custom-call(bf16[256,384]{1,0:T(8,128)(2,1)S(1)} %bitcast.9, bf16[208,768]{1,0:T(8,128)(2,1)S(1)} %get-tuple-element.75.refs_2_.refs_1_, bf16[208,768]{1,0:T(8,128)(2,1)S(1)} %collective-permute-done.17.refs_0_.refs_4_.refs_2_, bf16[16,768]{1,0:T(8,128)(2,1)S(1)} %collective-permute-done.18.refs_3_, ...), custom_call_target="tpu_custom_call" | custom-call | flops 754974720 | bytes 4005888 | tf_op jit(solution)/shard_map/input_grad/pallas_call | solution.py:36
  84.2 5.7 %collective-permute-done.27.refs_1_ = bf16[1,144,768]{2,1,0:T(8,128)(2,1)S(1)} collective-permute-done((bf16[1,144,768]{2,1,0:T(8,128)(2,1)S(1)}, bf16[1,144,768]{2,1,0:T(8,128)(2,1)S(1)}, u32[]{:S(2)}, u32[]{:S(2)}) %collective-permute-start.27) | collective-permute-done | bytes 221216 | tf_op jit(solution)/shard_map/ppermute | solution.py:439
  89.9 4.3 %collective-permute-done.28.refs_2_ = bf16[1,144,768]{2,1,0:T(8,128)(2,1)S(1)} collective-permute-done((bf16[1,144,768]{2,1,0:T(8,128)(2,1)S(1)}, bf16[1,144,768]{2,1,0:T(8,128)(2,1)S(1)}, u32[]{:S(2)}, u32[]{:S(2)}) %collective-permute-start.28) | collective-permute-done | bytes 221216 | tf_op jit(solution)/shard_map/ppermute | solution.py:439
  (58 shorter events, 11.4 us)
Async XLA Ops:
  1.7 22.4 %copy-start.1 = (bf16[768,1024]{1,0:T(8,128)(2,1)S(1)}, bf16[768,1024]{1,0:T(8,128)(2,1)}, u32[]{:S(2)}) copy-start(bf16[768,1024]{1,0:T(8,128)(2,1)} %refs_1_.3) | copy-start | bytes 4718596
  1.8 6.7 %collective-permute-start.1 = (bf16[32,384]{1,0:T(8,128)(2,1)S(1)}, bf16[32,384]{1,0:T(8,128)(2,1)S(1)}, u32[]{:S(2)}, u32[]{:S(2)}) collective-permute-start(bf16[32,384]{1,0:T(8,128)(2,1)S(1)} %get-tuple-element.52), channel_id=1, source_target_pairs={{2,4},{6,8},{10,12},{4,2},{8,6},{12,10},{3,5},{7,9},{11,13},{5,3},... | collective-permute-start | bytes 73736 | tf_op jit(solution)/shard_map/ppermute | solution.py:470
  2.6 7.7 %collective-permute-start = (bf16[32,384]{1,0:T(8,128)(2,1)S(1)}, bf16[32,384]{1,0:T(8,128)(2,1)S(1)}, u32[]{:S(2)}, u32[]{:S(2)}) collective-permute-start(bf16[32,384]{1,0:T(8,128)(2,1)S(1)} %get-tuple-element.52), channel_id=1, source_target_pairs={{0,2},{1,3},{2,0},{3,1},{4,6},{5,7},{6,4},{7,5},{8,10},{9,11},{10,... | collective-permute-start | bytes 73736 | tf_op jit(solution)/shard_map/ppermute | solution.py:439
  10.3 18.4 %copy-start.6 = (bf16[1,128,1536]{2,1,0:T(8,128)(2,1)S(1)}, bf16[1,128,1536]{2,1,0:T(8,128)(2,1)}, u32[]{:S(2)}) copy-start(bf16[1,128,1536]{2,1,0:T(8,128)(2,1)} %param.13) | copy-start | bytes 1179652
  12.2 6.5 %collective-permute-start.4 = (bf16[320,128]{1,0:T(8,128)(2,1)S(1)}, bf16[320,128]{1,0:T(8,128)(2,1)S(1)}, u32[]{:S(2)}, u32[]{:S(2)}) collective-permute-start(bf16[320,128]{1,0:T(8,128)(2,1)S(1)} %get-tuple-element.55.refs_2_), channel_id=1, source_target_pairs={{0,12},{1,13},{2,14},{3,15},{4,8},{5,9},{6,10},{7,11},{8,4},{9,5},... | collective-permute-start | bytes 245768 | tf_op jit(solution)/shard_map/ppermute | solution.py:439
  16.2 5.9 %collective-permute-start.3 = (bf16[320,128]{1,0:T(8,128)(2,1)S(1)}, bf16[320,128]{1,0:T(8,128)(2,1)S(1)}, u32[]{:S(2)}, u32[]{:S(2)}) collective-permute-start(bf16[320,128]{1,0:T(8,128)(2,1)S(1)} %get-tuple-element.55.refs_2_), channel_id=1, source_target_pairs={{0,8},{1,9},{2,10},{3,11},{4,12},{5,13},{6,14},{7,15},{8,0},{9,1},... | collective-permute-start | bytes 245768 | tf_op jit(solution)/shard_map/ppermute | solution.py:439
  16.2 7.2 %collective-permute-start.2 = (bf16[320,128]{1,0:T(8,128)(2,1)S(1)}, bf16[320,128]{1,0:T(8,128)(2,1)S(1)}, u32[]{:S(2)}, u32[]{:S(2)}) collective-permute-start(bf16[320,128]{1,0:T(8,128)(2,1)S(1)} %get-tuple-element.55.refs_2_), channel_id=1, source_target_pairs={{0,4},{1,5},{2,6},{3,7},{4,0},{5,1},{6,2},{7,3},{8,12},{9,13},{10,... | collective-permute-start | bytes 245768 | tf_op jit(solution)/shard_map/ppermute | solution.py:439
  16.9 8.0 %collective-permute-start.5 = (bf16[320,128]{1,0:T(8,128)(2,1)S(1)}, bf16[320,128]{1,0:T(8,128)(2,1)S(1)}, u32[]{:S(2)}, u32[]{:S(2)}) collective-permute-start(bf16[320,128]{1,0:T(8,128)(2,1)S(1)} %get-tuple-element.55.refs_2_), channel_id=1, source_target_pairs={{0,2},{1,3},{2,0},{3,1},{4,6},{5,7},{6,4},{7,5},{8,10},{9,11},{10,... | collective-permute-start | bytes 245768 | tf_op jit(solution)/shard_map/ppermute | solution.py:439
  18.7 6.2 %collective-permute-start.8 = (bf16[320,128]{1,0:T(8,128)(2,1)S(1)}, bf16[320,128]{1,0:T(8,128)(2,1)S(1)}, u32[]{:S(2)}, u32[]{:S(2)}) collective-permute-start(bf16[320,128]{1,0:T(8,128)(2,1)S(1)} %collective-permute-done.4.refs_5_), channel_id=1, source_target_pairs={{0,2},{1,3},{2,0},{3,1},{4,6},{5,7},{6,4},{7,5},{8,10},{9,11},{10,... | collective-permute-start | bytes 245768 | tf_op jit(solution)/shard_map/ppermute | solution.py:439
  22.1 4.5 %collective-permute-start.7 = (bf16[320,128]{1,0:T(8,128)(2,1)S(1)}, bf16[320,128]{1,0:T(8,128)(2,1)S(1)}, u32[]{:S(2)}, u32[]{:S(2)}) collective-permute-start(bf16[320,128]{1,0:T(8,128)(2,1)S(1)} %collective-permute-done.3.refs_4_), channel_id=1, source_target_pairs={{0,2},{1,3},{2,0},{3,1},{4,6},{5,7},{6,4},{7,5},{8,10},{9,11},{10,... | collective-permute-start | bytes 245768 | tf_op jit(solution)/shard_map/ppermute | solution.py:439
  23.4 4.4 %collective-permute-start.6 = (bf16[320,128]{1,0:T(8,128)(2,1)S(1)}, bf16[320,128]{1,0:T(8,128)(2,1)S(1)}, u32[]{:S(2)}, u32[]{:S(2)}) collective-permute-start(bf16[320,128]{1,0:T(8,128)(2,1)S(1)} %collective-permute-done.2.refs_3_), channel_id=1, source_target_pairs={{0,2},{1,3},{2,0},{3,1},{4,6},{5,7},{6,4},{7,5},{8,10},{9,11},{10,... | collective-permute-start | bytes 245768 | tf_op jit(solution)/shard_map/ppermute | solution.py:439
  27.8 8.5 %collective-permute-start.12 = (bf16[480,384]{1,0:T(8,128)(2,1)S(1)}, bf16[480,384]{1,0:T(8,128)(2,1)S(1)}, u32[]{:S(2)}, u32[]{:S(2)}) collective-permute-start(bf16[480,384]{1,0:T(8,128)(2,1)S(1)} %get-tuple-element.64.refs_1_), channel_id=1, source_target_pairs={{0,2},{1,3},{2,0},{3,1},{4,6},{5,7},{6,4},{7,5},{8,10},{9,11},{10,... | collective-permute-start | bytes 1105928 | tf_op jit(solution)/shard_map/ppermute | solution.py:439
  28.7 9.0 %collective-permute-start.11 = (bf16[480,384]{1,0:T(8,128)(2,1)S(1)}, bf16[480,384]{1,0:T(8,128)(2,1)S(1)}, u32[]{:S(2)}, u32[]{:S(2)}) collective-permute-start(bf16[480,384]{1,0:T(8,128)(2,1)S(1)} %get-tuple-element.64.refs_1_), channel_id=1, source_target_pairs={{0,1},{1,0},{2,3},{3,2},{4,5},{5,4},{6,7},{7,6},{8,9},{9,8},{10,11... | collective-permute-start | bytes 1105928 | tf_op jit(solution)/shard_map/ppermute | solution.py:439
  36.4 1.7 %collective-permute-start.13 = (bf16[480,384]{1,0:T(8,128)(2,1)S(1)}, bf16[480,384]{1,0:T(8,128)(2,1)S(1)}, u32[]{:S(2)}, u32[]{:S(2)}) collective-permute-start(bf16[480,384]{1,0:T(8,128)(2,1)S(1)} %collective-permute-done.12.refs_3_), channel_id=1, source_target_pairs={{0,1},{1,0},{2,3},{3,2},{4,5},{5,4},{6,7},{7,6},{8,9},{9,8},{10,11... | collective-permute-start | bytes 1105928 | tf_op jit(solution)/shard_map/ppermute | solution.py:439
  36.4 7.2 %collective-permute-start.9 = (bf16[4,160,128]{2,1,0:T(8,128)(2,1)S(1)}, bf16[4,160,128]{2,1,0:T(8,128)(2,1)S(1)}, u32[]{:S(2)}, u32[]{:S(2)}) collective-permute-start(bf16[4,160,128]{2,1,0:T(8,128)(2,1)S(1)} %get-tuple-element.59), channel_id=1, source_target_pairs={{0,2},{1,3},{2,0},{3,1},{4,6},{5,7},{6,4},{7,5},{8,10},{9,11},{10,... | collective-permute-start | bytes 491528 | tf_op jit(solution)/shard_map/ppermute | solution.py:439
  37.2 6.3 %collective-permute-start.10 = (bf16[4,160,128]{2,1,0:T(8,128)(2,1)S(1)}, bf16[4,160,128]{2,1,0:T(8,128)(2,1)S(1)}, u32[]{:S(2)}, u32[]{:S(2)}) collective-permute-start(bf16[4,160,128]{2,1,0:T(8,128)(2,1)S(1)} %get-tuple-element.61), channel_id=1, source_target_pairs={{0,4},{1,5},{2,6},{3,7},{4,0},{5,1},{6,2},{7,3},{8,12},{9,13},{10,... | collective-permute-start | bytes 491528 | tf_op jit(solution)/shard_map/ppermute | solution.py:439
  43.6 4.5 %collective-permute-start.14 = (bf16[2,160,128]{2,1,0:T(8,128)(2,1)S(1)}, bf16[2,160,128]{2,1,0:T(8,128)(2,1)S(1)}, u32[]{:S(2)}, u32[]{:S(2)}) collective-permute-start(bf16[2,160,128]{2,1,0:T(8,128)(2,1)S(1)} %get-tuple-element.68), channel_id=1, source_target_pairs={{0,4},{1,5},{2,6},{3,7},{4,0},{5,1},{6,2},{7,3},{8,12},{9,13},{10,... | collective-permute-start | bytes 245768 | tf_op jit(solution)/shard_map/ppermute | solution.py:439
  44.2 4.4 %collective-permute-start.15 = (bf16[2,160,128]{2,1,0:T(8,128)(2,1)S(1)}, bf16[2,160,128]{2,1,0:T(8,128)(2,1)S(1)}, u32[]{:S(2)}, u32[]{:S(2)}) collective-permute-start(bf16[2,160,128]{2,1,0:T(8,128)(2,1)S(1)} %get-tuple-element.70), channel_id=1, source_target_pairs={{0,2},{1,3},{2,0},{3,1},{4,6},{5,7},{6,4},{7,5},{8,10},{9,11},{10,... | collective-permute-start | bytes 245768 | tf_op jit(solution)/shard_map/ppermute | solution.py:439
  48.6 6.9 %collective-permute-start.21 = (bf16[128,1024]{1,0:T(8,128)(2,1)S(1)}, bf16[128,1024]{1,0:T(8,128)(2,1)S(1)}, u32[]{:S(2)}, u32[]{:S(2)}) collective-permute-start(bf16[128,1024]{1,0:T(8,128)(2,1)S(1)} %get-tuple-element.78.refs_0_.refs_1_), channel_id=1, source_target_pairs={{0,2},{1,3},{2,0},{3,1},{4,6},{5,7},{6,4},{7,5},{8,10},{9,11},{10,... | collective-permute-start | bytes 786440 | tf_op jit(solution)/shard_map/ppermute | solution.py:439
  49.8 5.4 %collective-permute-start.16 = (bf16[1,320,128]{2,1,0:T(8,128)(2,1)S(1)}, bf16[1,320,128]{2,1,0:T(8,128)(2,1)S(1)}, u32[]{:S(2)}, u32[]{:S(2)}) collective-permute-start(bf16[1,320,128]{2,1,0:T(8,128)(2,1)S(1)} %get-tuple-element.72), channel_id=1, source_target_pairs={{0,8},{1,9},{2,10},{3,11},{4,12},{5,13},{6,14},{7,15},{8,0},{9,1},... | collective-permute-start | bytes 245768 | tf_op jit(solution)/shard_map/ppermute | solution.py:439
  53.4 3.3 %collective-permute-start.20 = (bf16[128,1024]{1,0:T(8,128)(2,1)S(1)}, bf16[128,1024]{1,0:T(8,128)(2,1)S(1)}, u32[]{:S(2)}, u32[]{:S(2)}) collective-permute-start(bf16[128,1024]{1,0:T(8,128)(2,1)S(1)} %get-tuple-element.78.refs_0_.refs_1_), channel_id=1, source_target_pairs={{0,1},{1,0},{2,3},{3,2},{4,5},{5,4},{6,7},{7,6},{8,9},{9,8},{10,11... | collective-permute-start | bytes 786440 | tf_op jit(solution)/shard_map/ppermute | solution.py:439
  55.6 1.6 %collective-permute-start.22 = (bf16[128,1024]{1,0:T(8,128)(2,1)S(1)}, bf16[128,1024]{1,0:T(8,128)(2,1)S(1)}, u32[]{:S(2)}, u32[]{:S(2)}) collective-permute-start(bf16[128,1024]{1,0:T(8,128)(2,1)S(1)} %collective-permute-done.21.refs_3_), channel_id=1, source_target_pairs={{0,1},{1,0},{2,3},{3,2},{4,5},{5,4},{6,7},{7,6},{8,9},{9,8},{10,11... | collective-permute-start | bytes 786440 | tf_op jit(solution)/shard_map/ppermute | solution.py:439
  55.6 10.0 %collective-permute-start.17 = (bf16[208,768]{1,0:T(8,128)(2,1)S(1)}, bf16[208,768]{1,0:T(8,128)(2,1)S(1)}, u32[]{:S(2)}, u32[]{:S(2)}) collective-permute-start(bf16[208,768]{1,0:T(8,128)(2,1)S(1)} %get-tuple-element.75.refs_2_.refs_1_), channel_id=1, source_target_pairs={{0,2},{1,3},{2,0},{3,1},{4,6},{5,7},{6,4},{7,5},{8,10},{9,11},{10,... | collective-permute-start | bytes 958472 | tf_op jit(solution)/shard_map/ppermute | solution.py:439
  57.2 25.0 %copy-start.5 = (bf16[1,256,384]{2,1,0:T(8,128)(2,1)S(1)}, bf16[1,256,384]{2,1,0:T(8,128)(2,1)}, u32[]{:S(2)}) copy-start(bf16[1,256,384]{2,1,0:T(8,128)(2,1)} %param.7) | copy-start | bytes 589828
  58.0 7.6 %collective-permute-start.23 = (bf16[2,48,1024]{2,1,0:T(8,128)(2,1)S(1)}, bf16[2,48,1024]{2,1,0:T(8,128)(2,1)S(1)}, u32[]{:S(2)}, u32[]{:S(2)}) collective-permute-start(bf16[2,48,1024]{2,1,0:T(8,128)(2,1)S(1)} %get-tuple-element.81), channel_id=1, source_target_pairs={{0,4},{1,5},{2,6},{3,7},{4,0},{5,1},{6,2},{7,3},{8,12},{9,13},{10,... | collective-permute-start | bytes 589832 | tf_op jit(solution)/shard_map/ppermute | solution.py:439
  59.7 0.9 collective-permute-start.18
  60.6 5.2 %collective-permute-start.19 = (bf16[208,768]{1,0:T(8,128)(2,1)S(1)}, bf16[208,768]{1,0:T(8,128)(2,1)S(1)}, u32[]{:S(2)}, u32[]{:S(2)}) collective-permute-start(bf16[208,768]{1,0:T(8,128)(2,1)S(1)} %get-tuple-element.75.refs_2_.refs_1_), channel_id=1, source_target_pairs={{0,1},{1,0},{2,3},{3,2},{4,5},{5,4},{6,7},{7,6},{8,9},{9,8},{10,11... | collective-permute-start | bytes 958472 | tf_op jit(solution)/shard_map/ppermute | solution.py:439
  65.7 1.7 %collective-permute-start.24 = (bf16[208,768]{1,0:T(8,128)(2,1)S(1)}, bf16[208,768]{1,0:T(8,128)(2,1)S(1)}, u32[]{:S(2)}, u32[]{:S(2)}) collective-permute-start(bf16[208,768]{1,0:T(8,128)(2,1)S(1)} %get-tuple-element.82), channel_id=1, source_target_pairs={{0,1},{1,0},{2,3},{3,2},{4,5},{5,4},{6,7},{7,6},{8,9},{9,8},{10,11... | collective-permute-start | bytes 958472 | tf_op jit(solution)/shard_map/ppermute | solution.py:439
  68.8 13.2 %collective-permute-start.26 = (bf16[1,144,768]{2,1,0:T(8,128)(2,1)S(1)}, bf16[1,144,768]{2,1,0:T(8,128)(2,1)S(1)}, u32[]{:S(2)}, u32[]{:S(2)}) collective-permute-start(bf16[1,144,768]{2,1,0:T(8,128)(2,1)S(1)} %get-tuple-element.86), channel_id=1, source_target_pairs={{0,4},{1,5},{2,6},{3,7},{4,0},{5,1},{6,2},{7,3},{8,12},{9,13},{10,... | collective-permute-start | bytes 663560 | tf_op jit(solution)/shard_map/ppermute | solution.py:439
  71.0 7.1 %collective-permute-start.25 = (bf16[1,48,1024]{2,1,0:T(8,128)(2,1)S(1)}, bf16[1,48,1024]{2,1,0:T(8,128)(2,1)S(1)}, u32[]{:S(2)}, u32[]{:S(2)}) collective-permute-start(bf16[1,48,1024]{2,1,0:T(8,128)(2,1)S(1)} %get-tuple-element.84), channel_id=1, source_target_pairs={{0,8},{1,9},{2,10},{3,11},{4,12},{5,13},{6,14},{7,15},{8,0},{9,1},... | collective-permute-start | bytes 294920 | tf_op jit(solution)/shard_map/ppermute | solution.py:439
  78.1 11.8 %collective-permute-start.27 = (bf16[1,144,768]{2,1,0:T(8,128)(2,1)S(1)}, bf16[1,144,768]{2,1,0:T(8,128)(2,1)S(1)}, u32[]{:S(2)}, u32[]{:S(2)}) collective-permute-start(bf16[1,144,768]{2,1,0:T(8,128)(2,1)S(1)} %get-tuple-element.88), channel_id=1, source_target_pairs={{0,4},{1,5},{2,6},{3,7},{4,0},{5,1},{6,2},{7,3},{8,12},{9,13},{10,... | collective-permute-start | bytes 663560 | tf_op jit(solution)/shard_map/ppermute | solution.py:439
  82.1 12.1 %collective-permute-start.28 = (bf16[1,144,768]{2,1,0:T(8,128)(2,1)S(1)}, bf16[1,144,768]{2,1,0:T(8,128)(2,1)S(1)}, u32[]{:S(2)}, u32[]{:S(2)}) collective-permute-start(bf16[1,144,768]{2,1,0:T(8,128)(2,1)S(1)} %conv_send_on.1.refs_5_), channel_id=1, source_target_pairs={{0,8},{1,9},{2,10},{3,11},{4,12},{5,13},{6,14},{7,15},{8,0},{9,1},... | collective-permute-start | bytes 663560 | tf_op jit(solution)/shard_map/ppermute | solution.py:439
  (5 other events, 34.0 us)

commit v6 on v5

--- a/solution.py
+++ b/solution.py
@@ -237,7 +237,7 @@
     out[...] = dot_t(dq[...], wq[...])
 
 
-def middle_kernel(own, came, part, pooled_in, gain_in, wk, wv, message, edge):
+def middle_kernel(own, came, part, pooled_in, gain_in, wk, wv, first, second, edge):
     size = own.shape[2]
     tokens, width = pooled_in.shape
     total = (own[0] + came[0].astype(F32)).astype(BF).astype(F32)
@@ -256,14 +256,17 @@
     high = gain_term.astype(BF).astype(F32)
     low = gain_term - high
     row = lax.broadcasted_iota(jnp.int32, (16, width), 0)
-    gains = jnp.where(row == 0, high, jnp.where(row == 1, low, 0.0))
-    both = jnp.concatenate([key_cot, value_cot], axis=1)
-    fill = width // 2 - both.shape[1]
-    both = jnp.concatenate([both, jnp.zeros((tokens, fill), F32)], axis=1)
-    side = jnp.concatenate([both[: tokens // 2], both[tokens // 2 :]], axis=1)
-    message[:tokens] = conv_cot.astype(BF)
-    message[tokens : tokens + 16] = gains.astype(BF)
-    message[tokens + 16 :] = side.astype(BF)
+    split = width // 2
+    lines = (high[:, :split], low[:, :split], high[:, split:], low[:, split:])
+    gains = jnp.zeros((16, split), F32)
+    for i, line in enumerate(lines):
+        gains = jnp.where(row[:, :split] == i, line, gains)
+    fill = split - size - value_cot.shape[1]
+    side = jnp.concatenate([key_cot, value_cot, jnp.zeros((tokens, fill), F32)], axis=1)
+    first[:tokens] = conv_cot[:, :split].astype(BF)
+    first[tokens:] = gains.astype(BF)
+    second[:tokens] = conv_cot[:, split:].astype(BF)
+    second[tokens:] = side.astype(BF)
     ends = jnp.where(row == 0, conv_cot[:1], jnp.where(row == 1, conv_cot[tokens - 1 :], 0.0))
     edge[...] = ends.astype(BF)
 
@@ -279,11 +282,6 @@
     column = lax.broadcasted_iota(jnp.int32, (padded, columns), 1)
     hit = (column == row + block * rows) & (row < rows)
     return jnp.where(hit, 1.0, 0.0).astype(BF)
-
-
-def relay_kernel(value, keep_in, came, out, keep, send):
-    out[...] = value[...]
-    fold_kernel(keep_in, came, keep, send)
 
 
 def select_kernel(*refs, order, rows, padded):
@@ -329,78 +327,125 @@
             send[k - count] = term.astype(BF)
 
 
-def chunk_layout(conv_rows, norm_rows, width, key_size, value_size):
-    key_rows = norm_rows * key_size // width
-    value_rows = norm_rows * value_size // width
-    return conv_rows, conv_rows + key_rows, conv_rows + key_rows + value_rows
-
-
-def conv_grad_kernel(*refs, conv_rows, conv_pad, norm_rows, norm_pad, key_size, value_size):
-    pick, norm_pick, blocks = refs[0], refs[1], refs[2:6]
-    outs, right, side, stage = refs[6:-3], refs[-3], refs[-2], refs[-1]
-    width = right.shape[1]
-    tokens = side.shape[0] // 4
-    half = tokens // 2
-    gain = None
+def side_rows(norm_rows, size, width):
+    return norm_rows * size // width
+
+
+def put_side(stage, at, part, rows):
+    pieces = [part[i : i + rows] for i in range(0, part.shape[0], rows)]
+    stage[at : at + rows] = jnp.concatenate(pieces, axis=1)
+
+
+def get_side(packed, part, rows):
+    size = part.shape[1]
+    for i in range(part.shape[0] // rows):
+        part[i * rows : (i + 1) * rows] = packed[:, i * size : (i + 1) * size]
+
+
+def stack_cots(blocks, right, tokens):
     for i, block in enumerate(blocks):
         piece = block[:tokens]
         right[2 * i * tokens : (2 * i + 1) * tokens] = piece
         right[(2 * i + 1) * tokens : (2 * i + 2) * tokens] = piece
-        side[i * tokens : i * tokens + half] = block[tokens + 16 :, : width // 2]
-        side[i * tokens + half : (i + 1) * tokens] = block[tokens + 16 :, width // 2 :]
-        two = block[tokens : tokens + 16].astype(F32)
-        term = two[0:1] + two[1:2]
-        gain = term if gain is None else gain + term
-    high = gain.astype(BF).astype(F32)
-    key_at, value_at, gain_at = chunk_layout(conv_rows, norm_rows, width, key_size, value_size)
+
+
+def conv_first_kernel(*refs, conv_rows, conv_pad):
+    pick, blocks, outs, right, stage = refs[0], refs[1:5], refs[5:9], refs[9], refs[10]
+    tokens = right.shape[0] // 8
+    stack_cots(blocks, right, tokens)
     stage[...] = jnp.zeros(stage.shape, F32)
-    stage[gain_at : gain_at + 1] = high
-    stage[gain_at + 1 : gain_at + 2] = gain - high
+    for half in range(2):
+        gain = None
+        for block in blocks:
+            lines = block[tokens : tokens + 16].astype(F32)[2 * half : 2 * half + 2]
+            term = lines[0:1] + lines[1:2]
+            gain = term if gain is None else gain + term
+        high = gain.astype(BF).astype(F32)
+        at = conv_rows + 2 * half
+        stage[at : at + 1] = high
+        stage[at + 1 : at + 2] = gain - high
     count = outs[0].shape[0]
     for k in range(4 * count):
+        conv = dot(pick[k * conv_pad : (k + 1) * conv_pad], right[...])
+        stage[:conv_rows] = conv[:conv_rows]
         out = outs[k // count]
+        out[k % count] = stage[...].astype(out.dtype)
+
+
+def conv_second_kernel(*refs, conv_rows, conv_pad, norm_rows, norm_pad, key_size, value_size):
+    pick, norm_pick, blocks, first_send = refs[0], refs[1], refs[2:6], refs[6]
+    near_keep, far_keep, near_send, far_send, right, side, stage = refs[7:]
+    tokens, width = right.shape[0] // 8, right.shape[1]
+    stack_cots(blocks, right, tokens)
+    for i, block in enumerate(blocks):
+        side[i * tokens : (i + 1) * tokens] = block[tokens:]
+    key_rows = side_rows(norm_rows, key_size, width)
+    value_rows = side_rows(norm_rows, value_size, width)
+    stage[...] = jnp.zeros(stage.shape, F32)
+    count, above = first_send.shape[:2]
+    near_send[:, :above] = first_send[...]
+    for k in range(4 * count):
         conv = dot(pick[k * conv_pad : (k + 1) * conv_pad], right[...])
         stage[:conv_rows] = conv[:conv_rows]
         both = dot(norm_pick[k * norm_pad : (k + 1) * norm_pad], side[...])
-        key, value = both[:, :key_size], both[:, key_size : key_size + value_size]
-        for part, at, end in ((key, key_at, value_at), (value, value_at, gain_at)):
-            step = end - at
-            pieces = [part[i : i + step] for i in range(0, norm_rows, step)]
-            stage[at:end] = jnp.concatenate(pieces, axis=1)
-        out[k % count] = stage[...].astype(out.dtype)
-
-
-def final_kernel(*refs, conv_parts):
+        put_side(stage, conv_rows, both[:norm_rows, :key_size], key_rows)
+        value = both[:norm_rows, key_size : key_size + value_size]
+        put_side(stage, conv_rows + key_rows, value, value_rows)
+        if k < 2 * count:
+            (near_keep, far_keep)[k // count][k % count] = stage[...]
+        elif k < 3 * count:
+            near_send[k % count, above:] = stage[...].astype(BF)
+        else:
+            far_send[k % count] = stage[...].astype(BF)
+
+
+def first_sum_kernel(keep, near, far, out):
+    above = keep.shape[1]
+    out[...] = keep[...] + near[:, :above].astype(F32) + far[...].astype(F32)
+
+
+def combine_kernel(first, second, near, far, out):
+    above = first.shape[1]
+    out[:, :above] = first[...]
+    out[:, above:] = second[...] + near[:, above:].astype(F32) + far[...].astype(F32)
+
+
+def final_kernel(*refs, conv_parts, above):
     conv, query, key, value, gain, stage = refs[-6:]
-    total = total_of(refs[:conv_parts])[0]
+    rows, width = conv.shape
+    split = width // 2
+    count = key.shape[0]
+    if conv_parts == 4:
+        combine_kernel(*refs[:4], stage)
+    else:
+        stage[...] = total_of(refs[:conv_parts])
     query[...] = total_of(refs[conv_parts:-6])[0, : query.shape[0]]
-    rows, width = conv.shape
-    count = key.shape[0]
-    stage[...] = total
-    conv[...] = stage[:rows]
-    key_at, value_at, gain_at = chunk_layout(
-        rows, count, width, key.shape[1], value.shape[1]
-    )
-    for part, at, end in ((key, key_at, value_at), (value, value_at, gain_at)):
-        size, step = part.shape[1], end - at
-        packed = stage[at:end]
-        for i in range(count // step):
-            part[i * step : (i + 1) * step] = packed[:, i * size : (i + 1) * size]
-    line = stage[gain_at : gain_at + 1] + stage[gain_at + 1 : gain_at + 2]
+    conv[:, :split] = stage[0, :rows]
+    conv[:, split:] = stage[0, above : above + rows]
+    at = above + rows
+    for part in (key, value):
+        step = side_rows(count, part.shape[1], split)
+        get_side(stage[0, at : at + step], part, step)
+        at += step
+    lines = stage[0, rows : rows + 4]
+    line = jnp.concatenate([lines[0:1] + lines[1:2], lines[2:3] + lines[3:4]], axis=1)
     line = jnp.broadcast_to(line, (8, width))
     start = place()(0) * count
     gain[...] = pltpu.roll(line, lax.rem(width - start, width), 1)[:1, :count]
 
 
-def input_kernel(x, cc, pair_cc, edge, weight, out, ext, mixed):
+def input_kernel(x, first, second, pair_first, pair_second, edge, weight, out, ext, mixed):
     tokens = x.shape[0] // 2
     low = lax.axis_index("seq") % 2
-    ext[8 : 8 + tokens] = cc[:tokens].astype(F32)
-    pair_first = pair_cc[0:16].astype(F32)[0:1]
-    pair_last = pair_cc[tokens - 16 : tokens].astype(F32)[15:16]
-    ends = edge[...].astype(F32)
-    ext[7:8] = jnp.where(low == 0, ends[1:2], pair_last)
-    ext[8 + tokens : 9 + tokens] = jnp.where(low == 0, pair_first, ends[0:1])
+    split = first.shape[1]
+    for half, own, pair in ((0, first, pair_first), (1, second, pair_second)):
+        lanes = slice(half * split, (half + 1) * split)
+        ends = edge[:, lanes].astype(F32)
+        top = pair[0:16].astype(F32)[0:1]
+        bottom = pair[tokens - 16 : tokens].astype(F32)[15:16]
+        ext[8 : 8 + tokens, lanes] = own[:tokens].astype(F32)
+        ext[7:8, lanes] = jnp.where(low == 0, ends[1:2], bottom)
+        ext[8 + tokens : 9 + tokens, lanes] = jnp.where(low == 0, top, ends[0:1])
     back = ext[7 : 7 + tokens].astype(BF)
     here = ext[8 : 8 + tokens].astype(BF)
     ahead = ext[9 : 9 + tokens].astype(BF)
@@ -547,6 +592,10 @@
         after=[conv_pick],
     )
     in_a, in_b = swap(send_a, 2), swap(send_b, 1)
+    query_cot = held(query_cot, early_blocks[3])
+    query_near, query_core = swap(query_cot, 1), swap(query_cot, 0, 1)
+    query_last = swap(held(query_near, in_a, in_b), 0, 1)
+    keep_a = held(keep_a, query_near)
     block = (groups // 4, 5 * tokens // 2, key_size)
     keep, send = run(
         merge_kernel,
@@ -561,42 +610,46 @@
         flops=2 * tokens * width * heads * key_size,
         name="query_part",
     )
-    query_cot = held(query_cot, keep)
-    query_near, query_core = swap(query_cot, 1), swap(query_cot, 0, 1)
     kv_cot = halved(keep, send, bits[2:], "kv_cot_fold")
-    message, edge = run(
-        middle_kernel,
-        [((tokens + 16 + tokens // 2, width), BF), ((16, width), BF)],
-        kv_cot + [normed_cot, pooled, gain, wk, wv],
-        flops=2 * tokens * width * (key_size + value_size),
-        name="conv_cot",
-    )
-    near_message, core_message = swap(message, 1), swap(message, 0, 1)
-    edge_in = lax.ppermute(edge, "seq", crossing)
     query_half = (groups // 2, norm_pad, heads * key_size)
-    keep, send = run(
+    query_keep, query_send = run(
         query_grad_kernel,
         [(query_half, F32), (query_half, BF)],
-        [norm_pick, query_cot, query_core, query_near, swap(held(query_near, message), 0, 1)],
+        [norm_pick, query_cot, query_core, query_near, query_last],
         [pltpu.VMEM((4 * tokens, heads * key_size), BF)],
         flops=2 * groups * norm_pad * 4 * tokens * heads * key_size,
         name="query_grad",
     )
-    query_fourth = (groups // 4,) + query_half[1:]
-    relay, keep, send = run(
-        relay_kernel,
-        [(message.shape, BF), (query_fourth, F32), (query_fourth, BF)],
-        [near_message, keep, swap(send, 2)],
-        name="relay",
-        after=[edge_in],
-    )
-    query_parts = halved(keep, send, bits[2:], "query_fold")
-    blocks = [message, core_message, near_message, swap(relay, 0, 1)]
-    _, _, gain_at = chunk_layout(conv_rows, norm_rows, width, key_size, value_size)
-    chunk = (round_up(gain_at + 2, 16), width)
-    chunks = (groups // 4,) + chunk
+    query_parts = halved(query_keep, query_send, bits[1:], "query_fold")
+    first, second, edge = run(
+        middle_kernel,
+        [
+            ((tokens + 16, width // 2), BF),
+            ((2 * tokens, width // 2), BF),
+            ((16, width), BF),
+        ],
+        kv_cot + [normed_cot, held(pooled, query_keep), gain, wk, wv],
+        flops=2 * tokens * width * (key_size + value_size),
+        name="conv_cot",
+    )
+    near_first, near_second = swap(first, 1), swap(second, 1)
+    core_first, core_second = swap(first, 0, 1), swap(second, 0, 1)
+    split = width // 2
+    side = side_rows(norm_rows, key_size, split) + side_rows(norm_rows, value_size, split)
+    above, below = round_up(conv_rows + 4, 16), round_up(conv_rows + side, 16)
+    count = groups // 4
     near_keep, far_keep, near_send, far_send = run(
-        lambda *refs: conv_grad_kernel(
+        lambda *refs: conv_first_kernel(*refs, conv_rows=conv_rows, conv_pad=conv_pad),
+        [((count, above, split), t) for t in (F32, F32, BF, BF)],
+        [conv_pick, first, core_first, near_first, swap(near_first, 0, 1)],
+        [pltpu.VMEM((8 * tokens, split), BF), pltpu.VMEM((above, split), F32)],
+        flops=groups * conv_pad * 8 * tokens * width,
+        name="conv_grad_first",
+    )
+    far_in = swap(far_send, 2)
+    last_second = swap(held(near_second, near_keep), 0, 1)
+    near_keep_second, far_keep_second, near_send, far_send = run(
+        lambda *refs: conv_second_kernel(
             *refs,
             conv_rows=conv_rows,
             conv_pad=conv_pad,
@@ -605,37 +658,65 @@
             key_size=key_size,
             value_size=value_size,
         ),
-        [(chunks, F32), (chunks, F32), (chunks, BF), (chunks, BF)],
-        [conv_pick, norm_pick] + blocks,
         [
-            pltpu.VMEM((8 * tokens, width), BF),
-            pltpu.VMEM((4 * tokens, width // 2), BF),
-            pltpu.VMEM(chunk, F32),
+            ((count, below, split), F32),
+            ((count, below, split), F32),
+            ((count, above + below, split), BF),
+            ((count, below, split), BF),
         ],
-        flops=2 * groups * conv_pad * 8 * tokens * width,
-        name="conv_grad",
-    )
-    far_in = swap(far_send, 2)
+        [conv_pick, norm_pick, second, core_second, near_second, last_second, near_send],
+        [
+            pltpu.VMEM((8 * tokens, split), BF),
+            pltpu.VMEM((4 * tokens, split), BF),
+            pltpu.VMEM((below, split), F32),
+        ],
+        flops=groups * conv_pad * 8 * tokens * width,
+        name="conv_grad_second",
+    )
+    edge_in = lax.ppermute(held(edge, near_keep), "seq", crossing)
+    far_in_second = swap(far_send, 2)
     near_in = swap(near_send, 2)
-    (far_sum,) = run(send_on_kernel, [(chunks, BF)], [held(far_keep, query_parts[1]), far_in], name="conv_send_on")
-    conv_parts = [near_keep, near_in, swap(far_sum, 4)]
-    if len(bits) > 3:
-        keep, send = fold(conv_parts, "conv_fold")
-        conv_parts = halved(keep, send, bits[3:], "conv_fold")
+    (far_sum,) = run(
+        send_on_kernel,
+        [((count, above, split), BF)],
+        [far_keep, far_in],
+        name="conv_send_on",
+    )
+    far_last = swap(far_sum, 4)
     (input_grad,) = run(
         input_kernel,
         [((positions, channels), BF)],
-        [x, message, near_message, edge_in, conv_weight],
+        [x, first, second, near_first, near_second, edge_in, conv_weight],
         [
             pltpu.VMEM((tokens + 16, width), F32),
             pltpu.VMEM((channels // LANES, positions, LANES), F32),
         ],
-        flops=2 * positions * taps * channels * width,
+        flops=20 * positions * taps * channels * width,
         name="input_grad",
         after=[far_sum],
     )
+    (far_sum,) = run(
+        send_on_kernel,
+        [((count, below, split), BF)],
+        [held(far_keep_second, input_grad), far_in_second],
+        name="conv_send_on",
+    )
+    (first_sum,) = run(
+        first_sum_kernel,
+        [((count, above, split), F32)],
+        [near_keep, near_in, far_last],
+        flops=5 * 10**9,
+        name="conv_first_sum",
+    )
+    conv_parts = [first_sum, near_keep_second, near_in, swap(far_sum, 4)]
+    chunk = (count, above + below, split)
+    if len(bits) > 3:
+        keep = run(combine_kernel, [(chunk, F32)], conv_parts, name="conv_combine")[0]
+        half = (count // 2,) + chunk[1:]
+        keep, send = run(fold_kernel, [(half, F32), (half, BF)], [keep], name="conv_fold")
+        conv_parts = halved(keep, send, bits[3:], "conv_fold")
     conv_grad, query_grad, key_grad, value_grad, gain_grad = run(
-        lambda *refs: final_kernel(*refs, conv_parts=len(conv_parts)),
+        lambda *refs: final_kernel(*refs, conv_parts=len(conv_parts), above=above),
         [
             ((conv_rows, width), F32),
             ((norm_rows, heads * key_size), F32),
@@ -644,7 +725,7 @@
             ((1, norm_rows), F32),
         ],
         conv_parts + query_parts,
-        [pltpu.VMEM(chunk, F32)],
+        [pltpu.VMEM((1,) + chunk[1:], F32)],
         name="final_sum",
     )
     return (

time: 95.2 us -> 94.6 us (level)
  starting transfers between devices: 38.4 us -> 36.6 us
    ppermute x27 -> x32, starting transfers between devices: 36.8 us -> 35.2 us  [swap(): lax.ppermute(value, both_axes, [(i, i ^ mask) for i in range(owners)])]
    ppermute x27 -> x32, waiting for transfers between devices: 36.7 us -> 37.5 us  [swap(): lax.ppermute(value, both_axes, [(i, i ^ mask) for i in range(owners)])]
    pallas_call x15 -> x18, Pallas kernels: 18.1 us -> 18.5 us  [run(): pl.pallas_call(whole, out_shape=[jax.ShapeDtypeStruct(s, t) for s, t in o...]
  transfers between devices with their start and end apart: 29 -> 34, of which waited for: 17 -> 18; matrix products, arithmetic and copies ran while one was open for 0% -> 0% of each run, Pallas kernels for 14% -> 16%
where the time goes in v6:
time: 94.6 us; the launch traced here: 94.5 us
  waiting for transfers between devices  37.5 us (40%)
  starting transfers between devices  36.6 us (39%)
  Pallas kernels  18.5 us (20%)
  local copies, waits for them, and re-layouts  0.96 us (1%)
    ppermute x32, waiting for transfers between devices, swap(): lax.ppermute(value, both_axes, [(i, i ^ mask) for i in range(owners)])  37.5 us
    ppermute x32, starting transfers between devices, swap(): lax.ppermute(value, both_axes, [(i, i ^ mask) for i in range(owners)])  35.2 us
    pallas_call x18, Pallas kernels, run(): pl.pallas_call(whole, out_shape=[jax.ShapeDtypeStruct(s, t) for s, t in o...  18.5 us
  transfers between devices with their start and end apart: 34, of which 18 were waited for; matrix products, arithmetic and copies ran while one was open for 0% of the time, Pallas kernels for 16%

profile of v6, /device:TPU:0, one launch (start us, length us, event | category | flops | bytes accessed | tf_op | source)
XLA Modules:
  0.0 94.5 jit_solution(2723659666974660604)
XLA Ops:
  2.6 5.9 %collective-permute-start = (bf16[32,384]{1,0:T(8,128)(2,1)S(1)}, bf16[32,384]{1,0:T(8,128)(2,1)S(1)}, u32[]{:S(2)}, u32[]{:S(2)}) collective-permute-start(bf16[32,384]{1,0:T(8,128)(2,1)S(1)} %get-tuple-element.60), channel_id=1, source_target_pairs={{0,2},{1,3},{2,0},{3,1},{4,6},{5,7},{6,4},{7,5},{8,10},{9,11},{10,... | collective-permute-start | bytes 73736 | tf_op jit(solution)/shard_map/ppermute | solution.py:484
  8.5 1.8 %collective-permute-done.refs_1_ = bf16[32,384]{1,0:T(8,128)(2,1)S(1)} collective-permute-done((bf16[32,384]{1,0:T(8,128)(2,1)S(1)}, bf16[32,384]{1,0:T(8,128)(2,1)S(1)}, u32[]{:S(2)}, u32[]{:S(2)}) %collective-permute-start) | collective-permute-done | bytes 24608 | tf_op jit(solution)/shard_map/ppermute | solution.py:484
  10.3 1.9 %front.1 = (bf16[320,128]{1,0:T(8,128)(2,1)S(1)}, bf16[288,384]{1,0:T(8,128)(2,1)S(1)}, bf16[128,768]{1,0:T(8,128)(2,1)S(1)}, f32[128,768]{1,0:T(8,128)S(1)}) custom-call(f32[3,304,128]{2,1,0:T(8,128)S(1)} %get-tuple-element.59.refs_0_, bf16[32,384]{1,0:T(8,128)(2,1)S(1)} %collective-permute-done.refs_1_, ...), custom_call_target="tpu_custom_call" | custom-call | flops 754974720 | bytes 4852736 | tf_op jit(solution)/shard_map/front/pallas_call | solution.py:36
  12.2 4.0 %collective-permute-start.4 = (bf16[320,128]{1,0:T(8,128)(2,1)S(1)}, bf16[320,128]{1,0:T(8,128)(2,1)S(1)}, u32[]{:S(2)}, u32[]{:S(2)}) collective-permute-start(bf16[320,128]{1,0:T(8,128)(2,1)S(1)} %get-tuple-element.63.refs_2_), channel_id=1, source_target_pairs={{0,12},{1,13},{2,14},{3,15},{4,8},{5,9},{6,10},{7,11},{8,4},{9,5},... | collective-permute-start | bytes 245768 | tf_op jit(solution)/shard_map/ppermute | solution.py:484
  16.9 1.8 %collective-permute-start.5 = (bf16[320,128]{1,0:T(8,128)(2,1)S(1)}, bf16[320,128]{1,0:T(8,128)(2,1)S(1)}, u32[]{:S(2)}, u32[]{:S(2)}) collective-permute-start(bf16[320,128]{1,0:T(8,128)(2,1)S(1)} %get-tuple-element.63.refs_2_), channel_id=1, source_target_pairs={{0,2},{1,3},{2,0},{3,1},{4,6},{5,7},{6,4},{7,5},{8,10},{9,11},{10,... | collective-permute-start | bytes 245768 | tf_op jit(solution)/shard_map/ppermute | solution.py:484
  18.7 2.4 %collective-permute-start.8 = (bf16[320,128]{1,0:T(8,128)(2,1)S(1)}, bf16[320,128]{1,0:T(8,128)(2,1)S(1)}, u32[]{:S(2)}, u32[]{:S(2)}) collective-permute-start(bf16[320,128]{1,0:T(8,128)(2,1)S(1)} %collective-permute-done.4.refs_5_), channel_id=1, source_target_pairs={{0,2},{1,3},{2,0},{3,1},{4,6},{5,7},{6,4},{7,5},{8,10},{9,11},{10,... | collective-permute-start | bytes 245768 | tf_op jit(solution)/shard_map/ppermute | solution.py:484
  21.1 1.0 %collective-permute-done.3.refs_4_ = bf16[320,128]{1,0:T(8,128)(2,1)S(1)} collective-permute-done((bf16[320,128]{1,0:T(8,128)(2,1)S(1)}, bf16[320,128]{1,0:T(8,128)(2,1)S(1)}, u32[]{:S(2)}, u32[]{:S(2)}) %collective-permute-start.3) | collective-permute-done | bytes 81952 | tf_op jit(solution)/shard_map/ppermute | solution.py:484
  22.1 1.3 %collective-permute-start.7 = (bf16[320,128]{1,0:T(8,128)(2,1)S(1)}, bf16[320,128]{1,0:T(8,128)(2,1)S(1)}, u32[]{:S(2)}, u32[]{:S(2)}) collective-permute-start(bf16[320,128]{1,0:T(8,128)(2,1)S(1)} %collective-permute-done.3.refs_4_), channel_id=1, source_target_pairs={{0,2},{1,3},{2,0},{3,1},{4,6},{5,7},{6,4},{7,5},{8,10},{9,11},{10,... | collective-permute-start | bytes 245768 | tf_op jit(solution)/shard_map/ppermute | solution.py:484
  24.9 1.8 %collective-permute-done.7.refs_8_ = bf16[320,128]{1,0:T(8,128)(2,1)S(1)} collective-permute-done((bf16[320,128]{1,0:T(8,128)(2,1)S(1)}, bf16[320,128]{1,0:T(8,128)(2,1)S(1)}, u32[]{:S(2)}, u32[]{:S(2)}) %collective-permute-start.7) | collective-permute-done | bytes 81952 | tf_op jit(solution)/shard_map/ppermute | solution.py:484
  26.6 1.2 %collective-permute-done.6.refs_7_ = bf16[320,128]{1,0:T(8,128)(2,1)S(1)} collective-permute-done((bf16[320,128]{1,0:T(8,128)(2,1)S(1)}, bf16[320,128]{1,0:T(8,128)(2,1)S(1)}, u32[]{:S(2)}, u32[]{:S(2)}) %collective-permute-start.6) | collective-permute-done | bytes 81952 | tf_op jit(solution)/shard_map/ppermute | solution.py:484
  28.7 6.5 %attend.1 = (bf16[128,1536]{1,0:T(8,128)(2,1)}, bf16[128,1024]{1,0:T(8,128)(2,1)S(1)}, f32[4,160,128]{2,1,0:T(8,128)S(1)}, bf16[4,160,128]{2,1,0:T(8,128)(2,1)S(...) custom-call(bf16[128,1024]{1,0:T(8,128)(2,1)S(1)} %get-tuple-element.64.refs_0_, ...), custom_call_target="tpu_custom_call" | custom-call | flops 2013265920 | bytes 2949120 | tf_op jit(solution)/shard_map/attend/pallas_call | solution.py:36
  35.3 1.1 %collective-permute-done.12.refs_3_ = bf16[480,384]{1,0:T(8,128)(2,1)S(1)} collective-permute-done((bf16[480,384]{1,0:T(8,128)(2,1)S(1)}, bf16[480,384]{1,0:T(8,128)(2,1)S(1)}, u32[]{:S(2)}, u32[]{:S(2)}) %collective-permute-start.12) | collective-permute-done | bytes 368672 | tf_op jit(solution)/shard_map/ppermute | solution.py:484
  38.2 1.1 %collective-permute-start.14 = (bf16[128,1024]{1,0:T(8,128)(2,1)S(1)}, bf16[128,1024]{1,0:T(8,128)(2,1)S(1)}, u32[]{:S(2)}, u32[]{:S(2)}) collective-permute-start(bf16[128,1024]{1,0:T(8,128)(2,1)S(1)} %get-tuple-element.77.refs_0_.refs_1_), channel_id=1, source_target_pairs={{0,2},{1,3},{2,0},{3,1},{4,6},{5,7},{6,4},{7,5},{8,10},{9,11},{10,... | collective-permute-start | bytes 786440 | tf_op jit(solution)/shard_map/ppermute | solution.py:484
  39.3 2.4 %select.1 = (bf16[512,1024]{1,0:T(8,128)(2,1)S(1)}, bf16[192,512]{1,0:T(8,128)(2,1)S(1)}) custom-call(bf16[192,128]{1,0:T(8,128)(2,1)S(1)} %get-tuple-element.70.refs_0_, bf16[480,384]{1,0:T(8,128)(2,1)S(1)} %get-tuple-element.72.refs_1_, bf16[480,384]{1,0:T(8,128)(2,1)S(1)} %collective-permute-done.11.refs_2_, ...), custom_call_target="tpu_custom_call" | custom-call | flops 2013265920 | bytes 2768896 | tf_op jit(solution)/shard_map/select/pallas_call | solution.py:36
  41.7 1.9 %collective-permute-done.10.refs_3_ = bf16[4,160,128]{2,1,0:T(8,128)(2,1)S(1)} collective-permute-done((bf16[4,160,128]{2,1,0:T(8,128)(2,1)S(1)}, bf16[4,160,128]{2,1,0:T(8,128)(2,1)S(1)}, u32[]{:S(2)}, u32[]{:S(2)}) %collective-permute-start.10) | collective-permute-done | bytes 163872 | tf_op jit(solution)/shard_map/ppermute | solution.py:484
  44.4 1.0 %collective-permute-start.16 = (bf16[2,160,128]{2,1,0:T(8,128)(2,1)S(1)}, bf16[2,160,128]{2,1,0:T(8,128)(2,1)S(1)}, u32[]{:S(2)}, u32[]{:S(2)}) collective-permute-start(bf16[2,160,128]{2,1,0:T(8,128)(2,1)S(1)} %get-tuple-element.81), channel_id=1, source_target_pairs={{0,2},{1,3},{2,0},{3,1},{4,6},{5,7},{6,4},{7,5},{8,10},{9,11},{10,... | collective-permute-start | bytes 245768 | tf_op jit(solution)/shard_map/ppermute | solution.py:484
  45.4 3.1 %collective-permute-done.15.refs_1_ = bf16[2,160,128]{2,1,0:T(8,128)(2,1)S(1)} collective-permute-done((bf16[2,160,128]{2,1,0:T(8,128)(2,1)S(1)}, bf16[2,160,128]{2,1,0:T(8,128)(2,1)S(1)}, u32[]{:S(2)}, u32[]{:S(2)}) %collective-permute-start.15) | collective-permute-done | bytes 81952 | tf_op jit(solution)/shard_map/ppermute | solution.py:484
  48.5 1.8 %collective-permute-done.16.refs_3_ = bf16[2,160,128]{2,1,0:T(8,128)(2,1)S(1)} collective-permute-done((bf16[2,160,128]{2,1,0:T(8,128)(2,1)S(1)}, bf16[2,160,128]{2,1,0:T(8,128)(2,1)S(1)}, u32[]{:S(2)}, u32[]{:S(2)}) %collective-permute-start.16) | collective-permute-done | bytes 81952 | tf_op jit(solution)/shard_map/ppermute | solution.py:484
  50.4 2.1 %collective-permute-start.17 = (bf16[1,320,128]{2,1,0:T(8,128)(2,1)S(1)}, bf16[1,320,128]{2,1,0:T(8,128)(2,1)S(1)}, u32[]{:S(2)}, u32[]{:S(2)}) collective-permute-start(bf16[1,320,128]{2,1,0:T(8,128)(2,1)S(1)} %get-tuple-element.83), channel_id=1, source_target_pairs={{0,8},{1,9},{2,10},{3,11},{4,12},{5,13},{6,14},{7,15},{8,0},{9,1},... | collective-permute-start | bytes 245768 | tf_op jit(solution)/shard_map/ppermute | solution.py:484
  54.0 4.0 %collective-permute-done.17.refs_1_ = bf16[1,320,128]{2,1,0:T(8,128)(2,1)S(1)} collective-permute-done((bf16[1,320,128]{2,1,0:T(8,128)(2,1)S(1)}, bf16[1,320,128]{2,1,0:T(8,128)(2,1)S(1)}, u32[]{:S(2)}, u32[]{:S(2)}) %collective-permute-start.17) | collective-permute-done | bytes 81952 | tf_op jit(solution)/shard_map/ppermute | solution.py:484
  59.2 1.3 %collective-permute-start.21 = (bf16[256,384]{1,0:T(8,128)(2,1)S(1)}, bf16[256,384]{1,0:T(8,128)(2,1)S(1)}, u32[]{:S(2)}, u32[]{:S(2)}) collective-permute-start(bf16[256,384]{1,0:T(8,128)(2,1)S(1)} %get-tuple-element.90.refs_2_), channel_id=1, source_target_pairs={{0,2},{1,3},{2,0},{3,1},{4,6},{5,7},{6,4},{7,5},{8,10},{9,11},{10,... | collective-permute-start | bytes 589832 | tf_op jit(solution)/shard_map/ppermute | solution.py:484
  60.5 3.9 %collective-permute-done.20.refs_3_ = bf16[144,384]{1,0:T(8,128)(2,1)S(1)} collective-permute-done((bf16[144,384]{1,0:T(8,128)(2,1)S(1)}, bf16[144,384]{1,0:T(8,128)(2,1)S(1)}, u32[]{:S(2)}, u32[]{:S(2)}) %collective-permute-start.20) | collective-permute-done | bytes 110624 | tf_op jit(solution)/shard_map/ppermute | solution.py:484
  66.5 1.1 %collective-permute-done.21.refs_4_ = bf16[256,384]{1,0:T(8,128)(2,1)S(1)} collective-permute-done((bf16[256,384]{1,0:T(8,128)(2,1)S(1)}, bf16[256,384]{1,0:T(8,128)(2,1)S(1)}, u32[]{:S(2)}, u32[]{:S(2)}) %collective-permute-start.21) | collective-permute-done | bytes 196640 | tf_op jit(solution)/shard_map/ppermute | solution.py:484
  67.9 4.8 %collective-permute-done.32.refs_1_ = bf16[2,48,1024]{2,1,0:T(8,128)(2,1)S(1)} collective-permute-done((bf16[2,48,1024]{2,1,0:T(8,128)(2,1)S(1)}, bf16[2,48,1024]{2,1,0:T(8,128)(2,1)S(1)}, u32[]{:S(2)}, u32[]{:S(2)}) %collective-permute-start.32) | collective-permute-done | bytes 196640 | tf_op jit(solution)/shard_map/ppermute | solution.py:484
  72.8 1.3 %collective-permute-start.33 = (bf16[1,48,1024]{2,1,0:T(8,128)(2,1)S(1)}, bf16[1,48,1024]{2,1,0:T(8,128)(2,1)S(1)}, u32[]{:S(2)}, u32[]{:S(2)}) collective-permute-start(bf16[1,48,1024]{2,1,0:T(8,128)(2,1)S(1)} %get-tuple-element.105), channel_id=1, source_target_pairs={{0,8},{1,9},{2,10},{3,11},{4,12},{5,13},{6,14},{7,15},{8,0},{9,1},... | collective-permute-start | bytes 294920 | tf_op jit(solution)/shard_map/ppermute | solution.py:484
  74.8 4.3 %collective-permute-start.29 = (bf16[1,128,384]{2,1,0:T(8,128)(2,1)S(1)}, bf16[1,128,384]{2,1,0:T(8,128)(2,1)S(1)}, u32[]{:S(2)}, u32[]{:S(2)}) collective-permute-start(bf16[1,128,384]{2,1,0:T(8,128)(2,1)S(1)} %conv_send_on.2.refs_7_), channel_id=1, source_target_pairs={{0,8},{1,9},{2,10},{3,11},{4,12},{5,13},{6,14},{7,15},{8,0},{9,1},... | collective-permute-start | bytes 294920 | tf_op jit(solution)/shard_map/ppermute | solution.py:484
  79.1 1.0 %conv_grad_second.1 = (f32[1,160,384]{2,1,0:T(8,128)S(1)}, f32[1,160,384]{2,1,0:T(8,128)S(1)}, bf16[1,288,384]{2,1,0:T(8,128)(2,1)S(1)}, bf16[1,160,384]{2,1,0:T(8,128)(2,1)S(1)}) custom-call(bf16[512,1024]{1,0:T(8,128)(2,1)S(1)} %get-tuple-element.74.refs_4_.refs_0_, bf16[192,512]{1,0:T(8,128)(2,1)S(1)} %get-tuple-element.85.refs_0_.refs_1_, ...), custom_call_target="tpu_custom_call" | custom-call | flops 402653184 | bytes 2965504 | tf_op jit(solution)/shard_map/conv_grad_second/pallas_call | solution.py:36
  80.8 1.3 %collective-permute-start.28 = (bf16[1,288,384]{2,1,0:T(8,128)(2,1)S(1)}, bf16[1,288,384]{2,1,0:T(8,128)(2,1)S(1)}, u32[]{:S(2)}, u32[]{:S(2)}) collective-permute-start(bf16[1,288,384]{2,1,0:T(8,128)(2,1)S(1)} %get-tuple-element.98), channel_id=1, source_target_pairs={{0,4},{1,5},{2,6},{3,7},{4,0},{5,1},{6,2},{7,3},{8,12},{9,13},{10,... | collective-permute-start | bytes 663560 | tf_op jit(solution)/shard_map/ppermute | solution.py:484
  82.1 2.0 %input_grad.1 = bf16[256,384]{1,0:T(8,128)(2,1)} custom-call(bf16[256,384]{1,0:T(8,128)(2,1)S(1)} %bitcast.10, bf16[144,384]{1,0:T(8,128)(2,1)S(1)} %get-tuple-element.89.refs_1_, bf16[256,384]{1,0:T(8,128)(2,1)S(1)} %get-tuple-element.90.refs_2_, bf16[144,384]{1,0:T(8,128)(2,1)S(1)} %collective-permute-done.20.refs_3_, ...), custom_call_target="tpu_custom_call" | custom-call | flops 7549747200 | bytes 3981312 | tf_op jit(solution)/shard_map/input_grad/pallas_call | solution.py:36
  84.2 2.2 %collective-permute-done.30.refs_1_ = bf16[1,160,384]{2,1,0:T(8,128)(2,1)S(1)} collective-permute-done((bf16[1,160,384]{2,1,0:T(8,128)(2,1)S(1)}, bf16[1,160,384]{2,1,0:T(8,128)(2,1)S(1)}, u32[]{:S(2)}, u32[]{:S(2)}) %collective-permute-start.30) | collective-permute-done | bytes 122912 | tf_op jit(solution)/shard_map/ppermute | solution.py:484
  87.1 4.3 %collective-permute-done.28.refs_1_.refs_2_ = bf16[1,288,384]{2,1,0:T(8,128)(2,1)S(1)} collective-permute-done((bf16[1,288,384]{2,1,0:T(8,128)(2,1)S(1)}, bf16[1,288,384]{2,1,0:T(8,128)(2,1)S(1)}, u32[]{:S(2)}, u32[]{:S(2)}) %collective-permute-start.28) | collective-permute-done | bytes 221216 | tf_op jit(solution)/shard_map/ppermute | solution.py:484
  91.4 2.2 %collective-permute-done.31.refs_3_ = bf16[1,160,384]{2,1,0:T(8,128)(2,1)S(1)} collective-permute-done((bf16[1,160,384]{2,1,0:T(8,128)(2,1)S(1)}, bf16[1,160,384]{2,1,0:T(8,128)(2,1)S(1)}, u32[]{:S(2)}, u32[]{:S(2)}) %collective-permute-start.31) | collective-permute-done | bytes 122912 | tf_op jit(solution)/shard_map/ppermute | solution.py:484
  (71 shorter events, 15.7 us)
Async XLA Ops:
  1.8 6.7 %collective-permute-start.1 = (bf16[32,384]{1,0:T(8,128)(2,1)S(1)}, bf16[32,384]{1,0:T(8,128)(2,1)S(1)}, u32[]{:S(2)}, u32[]{:S(2)}) collective-permute-start(bf16[32,384]{1,0:T(8,128)(2,1)S(1)} %get-tuple-element.60), channel_id=1, source_target_pairs={{2,4},{6,8},{10,12},{4,2},{8,6},{12,10},{3,5},{7,9},{11,13},{5,3},... | collective-permute-start | bytes 73736 | tf_op jit(solution)/shard_map/ppermute | solution.py:515
  2.6 7.7 %collective-permute-start = (bf16[32,384]{1,0:T(8,128)(2,1)S(1)}, bf16[32,384]{1,0:T(8,128)(2,1)S(1)}, u32[]{:S(2)}, u32[]{:S(2)}) collective-permute-start(bf16[32,384]{1,0:T(8,128)(2,1)S(1)} %get-tuple-element.60), channel_id=1, source_target_pairs={{0,2},{1,3},{2,0},{3,1},{4,6},{5,7},{6,4},{7,5},{8,10},{9,11},{10,... | collective-permute-start | bytes 73736 | tf_op jit(solution)/shard_map/ppermute | solution.py:484
  12.2 6.5 %collective-permute-start.4 = (bf16[320,128]{1,0:T(8,128)(2,1)S(1)}, bf16[320,128]{1,0:T(8,128)(2,1)S(1)}, u32[]{:S(2)}, u32[]{:S(2)}) collective-permute-start(bf16[320,128]{1,0:T(8,128)(2,1)S(1)} %get-tuple-element.63.refs_2_), channel_id=1, source_target_pairs={{0,12},{1,13},{2,14},{3,15},{4,8},{5,9},{6,10},{7,11},{8,4},{9,5},... | collective-permute-start | bytes 245768 | tf_op jit(solution)/shard_map/ppermute | solution.py:484
  16.2 5.9 %collective-permute-start.3 = (bf16[320,128]{1,0:T(8,128)(2,1)S(1)}, bf16[320,128]{1,0:T(8,128)(2,1)S(1)}, u32[]{:S(2)}, u32[]{:S(2)}) collective-permute-start(bf16[320,128]{1,0:T(8,128)(2,1)S(1)} %get-tuple-element.63.refs_2_), channel_id=1, source_target_pairs={{0,8},{1,9},{2,10},{3,11},{4,12},{5,13},{6,14},{7,15},{8,0},{9,1},... | collective-permute-start | bytes 245768 | tf_op jit(solution)/shard_map/ppermute | solution.py:484
  16.2 7.2 %collective-permute-start.2 = (bf16[320,128]{1,0:T(8,128)(2,1)S(1)}, bf16[320,128]{1,0:T(8,128)(2,1)S(1)}, u32[]{:S(2)}, u32[]{:S(2)}) collective-permute-start(bf16[320,128]{1,0:T(8,128)(2,1)S(1)} %get-tuple-element.63.refs_2_), channel_id=1, source_target_pairs={{0,4},{1,5},{2,6},{3,7},{4,0},{5,1},{6,2},{7,3},{8,12},{9,13},{10,... | collective-permute-start | bytes 245768 | tf_op jit(solution)/shard_map/ppermute | solution.py:484
  16.9 8.0 %collective-permute-start.5 = (bf16[320,128]{1,0:T(8,128)(2,1)S(1)}, bf16[320,128]{1,0:T(8,128)(2,1)S(1)}, u32[]{:S(2)}, u32[]{:S(2)}) collective-permute-start(bf16[320,128]{1,0:T(8,128)(2,1)S(1)} %get-tuple-element.63.refs_2_), channel_id=1, source_target_pairs={{0,2},{1,3},{2,0},{3,1},{4,6},{5,7},{6,4},{7,5},{8,10},{9,11},{10,... | collective-permute-start | bytes 245768 | tf_op jit(solution)/shard_map/ppermute | solution.py:484
  18.7 6.1 %collective-permute-start.8 = (bf16[320,128]{1,0:T(8,128)(2,1)S(1)}, bf16[320,128]{1,0:T(8,128)(2,1)S(1)}, u32[]{:S(2)}, u32[]{:S(2)}) collective-permute-start(bf16[320,128]{1,0:T(8,128)(2,1)S(1)} %collective-permute-done.4.refs_5_), channel_id=1, source_target_pairs={{0,2},{1,3},{2,0},{3,1},{4,6},{5,7},{6,4},{7,5},{8,10},{9,11},{10,... | collective-permute-start | bytes 245768 | tf_op jit(solution)/shard_map/ppermute | solution.py:484
  22.1 4.5 %collective-permute-start.7 = (bf16[320,128]{1,0:T(8,128)(2,1)S(1)}, bf16[320,128]{1,0:T(8,128)(2,1)S(1)}, u32[]{:S(2)}, u32[]{:S(2)}) collective-permute-start(bf16[320,128]{1,0:T(8,128)(2,1)S(1)} %collective-permute-done.3.refs_4_), channel_id=1, source_target_pairs={{0,2},{1,3},{2,0},{3,1},{4,6},{5,7},{6,4},{7,5},{8,10},{9,11},{10,... | collective-permute-start | bytes 245768 | tf_op jit(solution)/shard_map/ppermute | solution.py:484
  23.4 4.4 %collective-permute-start.6 = (bf16[320,128]{1,0:T(8,128)(2,1)S(1)}, bf16[320,128]{1,0:T(8,128)(2,1)S(1)}, u32[]{:S(2)}, u32[]{:S(2)}) collective-permute-start(bf16[320,128]{1,0:T(8,128)(2,1)S(1)} %collective-permute-done.2.refs_3_), channel_id=1, source_target_pairs={{0,2},{1,3},{2,0},{3,1},{4,6},{5,7},{6,4},{7,5},{8,10},{9,11},{10,... | collective-permute-start | bytes 245768 | tf_op jit(solution)/shard_map/ppermute | solution.py:484
  27.9 8.5 %collective-permute-start.12 = (bf16[480,384]{1,0:T(8,128)(2,1)S(1)}, bf16[480,384]{1,0:T(8,128)(2,1)S(1)}, u32[]{:S(2)}, u32[]{:S(2)}) collective-permute-start(bf16[480,384]{1,0:T(8,128)(2,1)S(1)} %get-tuple-element.72.refs_1_), channel_id=1, source_target_pairs={{0,2},{1,3},{2,0},{3,1},{4,6},{5,7},{6,4},{7,5},{8,10},{9,11},{10,... | collective-permute-start | bytes 1105928 | tf_op jit(solution)/shard_map/ppermute | solution.py:484
  36.4 2.9 %collective-permute-start.11 = (bf16[480,384]{1,0:T(8,128)(2,1)S(1)}, bf16[480,384]{1,0:T(8,128)(2,1)S(1)}, u32[]{:S(2)}, u32[]{:S(2)}) collective-permute-start(bf16[480,384]{1,0:T(8,128)(2,1)S(1)} %get-tuple-element.72.refs_1_), channel_id=1, source_target_pairs={{0,1},{1,0},{2,3},{3,2},{4,5},{5,4},{6,7},{7,6},{8,9},{9,8},{10,11... | collective-permute-start | bytes 1105928 | tf_op jit(solution)/shard_map/ppermute | solution.py:484
  36.9 7.1 %collective-permute-start.9 = (bf16[4,160,128]{2,1,0:T(8,128)(2,1)S(1)}, bf16[4,160,128]{2,1,0:T(8,128)(2,1)S(1)}, u32[]{:S(2)}, u32[]{:S(2)}) collective-permute-start(bf16[4,160,128]{2,1,0:T(8,128)(2,1)S(1)} %get-tuple-element.67), channel_id=1, source_target_pairs={{0,2},{1,3},{2,0},{3,1},{4,6},{5,7},{6,4},{7,5},{8,10},{9,11},{10,... | collective-permute-start | bytes 491528 | tf_op jit(solution)/shard_map/ppermute | solution.py:484
  37.7 5.8 %collective-permute-start.10 = (bf16[4,160,128]{2,1,0:T(8,128)(2,1)S(1)}, bf16[4,160,128]{2,1,0:T(8,128)(2,1)S(1)}, u32[]{:S(2)}, u32[]{:S(2)}) collective-permute-start(bf16[4,160,128]{2,1,0:T(8,128)(2,1)S(1)} %get-tuple-element.69), channel_id=1, source_target_pairs={{0,4},{1,5},{2,6},{3,7},{4,0},{5,1},{6,2},{7,3},{8,12},{9,13},{10,... | collective-permute-start | bytes 491528 | tf_op jit(solution)/shard_map/ppermute | solution.py:484
  38.2 12.2 %collective-permute-start.14 = (bf16[128,1024]{1,0:T(8,128)(2,1)S(1)}, bf16[128,1024]{1,0:T(8,128)(2,1)S(1)}, u32[]{:S(2)}, u32[]{:S(2)}) collective-permute-start(bf16[128,1024]{1,0:T(8,128)(2,1)S(1)} %get-tuple-element.77.refs_0_.refs_1_), channel_id=1, source_target_pairs={{0,2},{1,3},{2,0},{3,1},{4,6},{5,7},{6,4},{7,5},{8,10},{9,11},{10,... | collective-permute-start | bytes 786440 | tf_op jit(solution)/shard_map/ppermute | solution.py:484
  44.0 4.5 %collective-permute-start.15 = (bf16[2,160,128]{2,1,0:T(8,128)(2,1)S(1)}, bf16[2,160,128]{2,1,0:T(8,128)(2,1)S(1)}, u32[]{:S(2)}, u32[]{:S(2)}) collective-permute-start(bf16[2,160,128]{2,1,0:T(8,128)(2,1)S(1)} %get-tuple-element.79), channel_id=1, source_target_pairs={{0,4},{1,5},{2,6},{3,7},{4,0},{5,1},{6,2},{7,3},{8,12},{9,13},{10,... | collective-permute-start | bytes 245768 | tf_op jit(solution)/shard_map/ppermute | solution.py:484
  44.4 5.9 %collective-permute-start.16 = (bf16[2,160,128]{2,1,0:T(8,128)(2,1)S(1)}, bf16[2,160,128]{2,1,0:T(8,128)(2,1)S(1)}, u32[]{:S(2)}, u32[]{:S(2)}) collective-permute-start(bf16[2,160,128]{2,1,0:T(8,128)(2,1)S(1)} %get-tuple-element.81), channel_id=1, source_target_pairs={{0,2},{1,3},{2,0},{3,1},{4,6},{5,7},{6,4},{7,5},{8,10},{9,11},{10,... | collective-permute-start | bytes 245768 | tf_op jit(solution)/shard_map/ppermute | solution.py:484
  45.4 7.7 %collective-permute-start.18 = (bf16[128,1024]{1,0:T(8,128)(2,1)S(1)}, bf16[128,1024]{1,0:T(8,128)(2,1)S(1)}, u32[]{:S(2)}, u32[]{:S(2)}) collective-permute-start(bf16[128,1024]{1,0:T(8,128)(2,1)S(1)} %get-tuple-element.77.refs_0_.refs_1_), channel_id=1, source_target_pairs={{0,1},{1,0},{2,3},{3,2},{4,5},{5,4},{6,7},{7,6},{8,9},{9,8},{10,11... | collective-permute-start | bytes 786440 | tf_op jit(solution)/shard_map/ppermute | solution.py:484
  50.4 2.8 %collective-permute-start.19 = (bf16[128,1024]{1,0:T(8,128)(2,1)S(1)}, bf16[128,1024]{1,0:T(8,128)(2,1)S(1)}, u32[]{:S(2)}, u32[]{:S(2)}) collective-permute-start(bf16[128,1024]{1,0:T(8,128)(2,1)S(1)} %collective-permute-done.14.refs_3_), channel_id=1, source_target_pairs={{0,1},{1,0},{2,3},{3,2},{4,5},{5,4},{6,7},{7,6},{8,9},{9,8},{10,11... | collective-permute-start | bytes 786440 | tf_op jit(solution)/shard_map/ppermute | solution.py:484
  50.4 7.6 %collective-permute-start.17 = (bf16[1,320,128]{2,1,0:T(8,128)(2,1)S(1)}, bf16[1,320,128]{2,1,0:T(8,128)(2,1)S(1)}, u32[]{:S(2)}, u32[]{:S(2)}) collective-permute-start(bf16[1,320,128]{2,1,0:T(8,128)(2,1)S(1)} %get-tuple-element.83), channel_id=1, source_target_pairs={{0,8},{1,9},{2,10},{3,11},{4,12},{5,13},{6,14},{7,15},{8,0},{9,1},... | collective-permute-start | bytes 245768 | tf_op jit(solution)/shard_map/ppermute | solution.py:484
  58.4 6.0 %collective-permute-start.20 = (bf16[144,384]{1,0:T(8,128)(2,1)S(1)}, bf16[144,384]{1,0:T(8,128)(2,1)S(1)}, u32[]{:S(2)}, u32[]{:S(2)}) collective-permute-start(bf16[144,384]{1,0:T(8,128)(2,1)S(1)} %get-tuple-element.89.refs_1_), channel_id=1, source_target_pairs={{0,2},{1,3},{2,0},{3,1},{4,6},{5,7},{6,4},{7,5},{8,10},{9,11},{10,... | collective-permute-start | bytes 331784 | tf_op jit(solution)/shard_map/ppermute | solution.py:484
  59.2 8.4 %collective-permute-start.21 = (bf16[256,384]{1,0:T(8,128)(2,1)S(1)}, bf16[256,384]{1,0:T(8,128)(2,1)S(1)}, u32[]{:S(2)}, u32[]{:S(2)}) collective-permute-start(bf16[256,384]{1,0:T(8,128)(2,1)S(1)} %get-tuple-element.90.refs_2_), channel_id=1, source_target_pairs={{0,2},{1,3},{2,0},{3,1},{4,6},{5,7},{6,4},{7,5},{8,10},{9,11},{10,... | collective-permute-start | bytes 589832 | tf_op jit(solution)/shard_map/ppermute | solution.py:484
  60.5 4.4 %collective-permute-start.22 = (bf16[144,384]{1,0:T(8,128)(2,1)S(1)}, bf16[144,384]{1,0:T(8,128)(2,1)S(1)}, u32[]{:S(2)}, u32[]{:S(2)}) collective-permute-start(bf16[144,384]{1,0:T(8,128)(2,1)S(1)} %get-tuple-element.89.refs_1_), channel_id=1, source_target_pairs={{0,1},{1,0},{2,3},{3,2},{4,5},{5,4},{6,7},{7,6},{8,9},{9,8},{10,11... | collective-permute-start | bytes 331784 | tf_op jit(solution)/shard_map/ppermute | solution.py:484
  64.4 14.6 %collective-permute-start.26 = (bf16[256,384]{1,0:T(8,128)(2,1)S(1)}, bf16[256,384]{1,0:T(8,128)(2,1)S(1)}, u32[]{:S(2)}, u32[]{:S(2)}) collective-permute-start(bf16[256,384]{1,0:T(8,128)(2,1)S(1)} %get-tuple-element.90.refs_2_), channel_id=1, source_target_pairs={{0,1},{1,0},{2,3},{3,2},{4,5},{5,4},{6,7},{7,6},{8,9},{9,8},{10,11... | collective-permute-start | bytes 589832 | tf_op jit(solution)/shard_map/ppermute | solution.py:484
  64.9 7.8 %collective-permute-start.32 = (bf16[2,48,1024]{2,1,0:T(8,128)(2,1)S(1)}, bf16[2,48,1024]{2,1,0:T(8,128)(2,1)S(1)}, u32[]{:S(2)}, u32[]{:S(2)}) collective-permute-start(bf16[2,48,1024]{2,1,0:T(8,128)(2,1)S(1)} %get-tuple-element.103), channel_id=1, source_target_pairs={{0,4},{1,5},{2,6},{3,7},{4,0},{5,1},{6,2},{7,3},{8,12},{9,13},{10,... | collective-permute-start | bytes 589832 | tf_op jit(solution)/shard_map/ppermute | solution.py:484
  67.6 11.5 %collective-permute-start.27 = (bf16[256,384]{1,0:T(8,128)(2,1)S(1)}, bf16[256,384]{1,0:T(8,128)(2,1)S(1)}, u32[]{:S(2)}, u32[]{:S(2)}) collective-permute-start(bf16[256,384]{1,0:T(8,128)(2,1)S(1)} %collective-permute-done.21.refs_4_), channel_id=1, source_target_pairs={{0,1},{1,0},{2,3},{3,2},{4,5},{5,4},{6,7},{7,6},{8,9},{9,8},{10,11... | collective-permute-start | bytes 589832 | tf_op jit(solution)/shard_map/ppermute | solution.py:484
  67.6 7.1 %collective-permute-start.25 = (bf16[1,128,384]{2,1,0:T(8,128)(2,1)S(1)}, bf16[1,128,384]{2,1,0:T(8,128)(2,1)S(1)}, u32[]{:S(2)}, u32[]{:S(2)}) collective-permute-start(bf16[1,128,384]{2,1,0:T(8,128)(2,1)S(1)} %get-tuple-element.95), channel_id=1, source_target_pairs={{0,4},{1,5},{2,6},{3,7},{4,0},{5,1},{6,2},{7,3},{8,12},{9,13},{10,... | collective-permute-start | bytes 294920 | tf_op jit(solution)/shard_map/ppermute | solution.py:484
  72.8 18.6 %collective-permute-start.33 = (bf16[1,48,1024]{2,1,0:T(8,128)(2,1)S(1)}, bf16[1,48,1024]{2,1,0:T(8,128)(2,1)S(1)}, u32[]{:S(2)}, u32[]{:S(2)}) collective-permute-start(bf16[1,48,1024]{2,1,0:T(8,128)(2,1)S(1)} %get-tuple-element.105), channel_id=1, source_target_pairs={{0,8},{1,9},{2,10},{3,11},{4,12},{5,13},{6,14},{7,15},{8,0},{9,1},... | collective-permute-start | bytes 294920 | tf_op jit(solution)/shard_map/ppermute | solution.py:484
  74.1 8.1 %collective-permute-start.24 = (bf16[16,768]{1,0:T(8,128)(2,1)S(1)}, bf16[16,768]{1,0:T(8,128)(2,1)S(1)}, u32[]{:S(2)}, u32[]{:S(2)}) collective-permute-start(bf16[16,768]{1,0:T(8,128)(2,1)S(1)} %get-tuple-element.93), channel_id=1, source_target_pairs={{2,4},{6,8},{10,12},{4,2},{8,6},{12,10},{3,5},{7,9},{11,13},{5,3},... | collective-permute-start | bytes 73736 | tf_op jit(solution)/shard_map/ppermute | solution.py:676
  74.8 12.3 %collective-permute-start.29 = (bf16[1,128,384]{2,1,0:T(8,128)(2,1)S(1)}, bf16[1,128,384]{2,1,0:T(8,128)(2,1)S(1)}, u32[]{:S(2)}, u32[]{:S(2)}) collective-permute-start(bf16[1,128,384]{2,1,0:T(8,128)(2,1)S(1)} %conv_send_on.2.refs_7_), channel_id=1, source_target_pairs={{0,8},{1,9},{2,10},{3,11},{4,12},{5,13},{6,14},{7,15},{8,0},{9,1},... | collective-permute-start | bytes 294920 | tf_op jit(solution)/shard_map/ppermute | solution.py:484
  80.1 6.3 %collective-permute-start.30 = (bf16[1,160,384]{2,1,0:T(8,128)(2,1)S(1)}, bf16[1,160,384]{2,1,0:T(8,128)(2,1)S(1)}, u32[]{:S(2)}, u32[]{:S(2)}) collective-permute-start(bf16[1,160,384]{2,1,0:T(8,128)(2,1)S(1)} %get-tuple-element.102), channel_id=1, source_target_pairs={{0,4},{1,5},{2,6},{3,7},{4,0},{5,1},{6,2},{7,3},{8,12},{9,13},{10,... | collective-permute-start | bytes 368648 | tf_op jit(solution)/shard_map/ppermute | solution.py:484
  80.8 10.5 %collective-permute-start.28 = (bf16[1,288,384]{2,1,0:T(8,128)(2,1)S(1)}, bf16[1,288,384]{2,1,0:T(8,128)(2,1)S(1)}, u32[]{:S(2)}, u32[]{:S(2)}) collective-permute-start(bf16[1,288,384]{2,1,0:T(8,128)(2,1)S(1)} %get-tuple-element.98), channel_id=1, source_target_pairs={{0,4},{1,5},{2,6},{3,7},{4,0},{5,1},{6,2},{7,3},{8,12},{9,13},{10,... | collective-permute-start | bytes 663560 | tf_op jit(solution)/shard_map/ppermute | solution.py:484
  86.4 7.2 %collective-permute-start.31 = (bf16[1,160,384]{2,1,0:T(8,128)(2,1)S(1)}, bf16[1,160,384]{2,1,0:T(8,128)(2,1)S(1)}, u32[]{:S(2)}, u32[]{:S(2)}) collective-permute-start(bf16[1,160,384]{2,1,0:T(8,128)(2,1)S(1)} %conv_send_on.3), channel_id=1, source_target_pairs={{0,8},{1,9},{2,10},{3,11},{4,12},{5,13},{6,14},{7,15},{8,0},{9,1},... | collective-permute-start | bytes 368648 | tf_op jit(solution)/shard_map/ppermute | solution.py:484
  (10 other events, 102.1 us)

commit v7 on v6

--- a/solution.py
+++ b/solution.py
@@ -258,6 +258,7 @@
     row = lax.broadcasted_iota(jnp.int32, (16, width), 0)
     split = width // 2
     lines = (high[:, :split], low[:, :split], high[:, split:], low[:, split:])
+    lines += (conv_cot[:1, split:], conv_cot[tokens - 1 :, split:])
     gains = jnp.zeros((16, split), F32)
     for i, line in enumerate(lines):
         gains = jnp.where(row[:, :split] == i, line, gains)
@@ -364,10 +365,20 @@
         at = conv_rows + 2 * half
         stage[at : at + 1] = high
         stage[at + 1 : at + 2] = gain - high
-    count = outs[0].shape[0]
+    count, above = outs[0].shape[:2]
+    even = lax.axis_index("seq") % 2 == 0
+    own, pair = blocks[0], blocks[2]
+    tops = [b[0:16].astype(F32)[0:1] for b in (own, pair)]
+    bottoms = [b[tokens - 16 : tokens].astype(F32)[15:16] for b in (own, pair)]
+    rests = [b[tokens : tokens + 16].astype(F32)[4:6] for b in (own, pair)]
     for k in range(4 * count):
         conv = dot(pick[k * conv_pad : (k + 1) * conv_pad], right[...])
         stage[:conv_rows] = conv[:conv_rows]
+        if k == 3 * count:
+            stage[above - 4 : above - 3] = jnp.where(even, tops[0], tops[1])
+            stage[above - 3 : above - 2] = jnp.where(even, rests[0][0:1], rests[1][0:1])
+            stage[above - 2 : above - 1] = jnp.where(even, bottoms[1], bottoms[0])
+            stage[above - 1 : above] = jnp.where(even, rests[1][1:2], rests[0][1:2])
         out = outs[k // count]
         out[k % count] = stage[...].astype(out.dtype)
 
@@ -434,18 +445,26 @@
     gain[...] = pltpu.roll(line, lax.rem(width - start, width), 1)[:1, :count]
 
 
-def input_kernel(x, first, second, pair_first, pair_second, edge, weight, out, ext, mixed):
+def input_kernel(*refs):
+    x, first, second, pair_first, pair_second, one, three, weight, out, ext, mixed = refs
     tokens = x.shape[0] // 2
-    low = lax.axis_index("seq") % 2
+    seq, devices = lax.axis_index("seq"), lax.axis_size("seq")
+    low, high = seq % 2, seq // 2
     split = first.shape[1]
+    above = one.shape[1]
+    one_rows = one[0, above - 16 :].astype(F32)[12:]
+    three_rows = three[0, above - 16 :].astype(F32)[12:]
+    heads = jnp.where(high % 2 == 0, one_rows[:2], three_rows[:2])
+    tails = jnp.where(high % 2 == 0, three_rows[2:], one_rows[2:])
+    heads = jnp.where(seq == devices - 1, 0.0, heads)
+    tails = jnp.where(seq == 0, 0.0, tails)
     for half, own, pair in ((0, first, pair_first), (1, second, pair_second)):
         lanes = slice(half * split, (half + 1) * split)
-        ends = edge[:, lanes].astype(F32)
         top = pair[0:16].astype(F32)[0:1]
         bottom = pair[tokens - 16 : tokens].astype(F32)[15:16]
         ext[8 : 8 + tokens, lanes] = own[:tokens].astype(F32)
-        ext[7:8, lanes] = jnp.where(low == 0, ends[1:2], bottom)
-        ext[8 + tokens : 9 + tokens, lanes] = jnp.where(low == 0, top, ends[0:1])
+        ext[7:8, lanes] = jnp.where(low == 0, tails[half : half + 1], bottom)
+        ext[8 + tokens : 9 + tokens, lanes] = jnp.where(low == 0, top, heads[half : half + 1])
     back = ext[7 : 7 + tokens].astype(BF)
     here = ext[8 : 8 + tokens].astype(BF)
     ahead = ext[9 : 9 + tokens].astype(BF)
@@ -573,8 +592,8 @@
         flops=6 * tokens * heads * length * (key_size + value_size),
         name="attend",
     )
+    in_a, in_b = swap(send_a, 1), swap(send_b, 2)
     early_blocks = quad(early, send_a)
-    in_a, in_b = swap(send_a, 1), swap(send_b, 2)
     conv_pick, norm_pick = run(
         lambda *refs: select_kernel(*refs, order=order, rows=conv_rows, padded=conv_pad),
         [((groups * conv_pad, 8 * tokens), BF), ((groups * norm_pad, 4 * tokens), BF)],
@@ -592,10 +611,6 @@
         after=[conv_pick],
     )
     in_a, in_b = swap(send_a, 2), swap(send_b, 1)
-    query_cot = held(query_cot, early_blocks[3])
-    query_near, query_core = swap(query_cot, 1), swap(query_cot, 0, 1)
-    query_last = swap(held(query_near, in_a, in_b), 0, 1)
-    keep_a = held(keep_a, query_near)
     block = (groups // 4, 5 * tokens // 2, key_size)
     keep, send = run(
         merge_kernel,
@@ -610,7 +625,22 @@
         flops=2 * tokens * width * heads * key_size,
         name="query_part",
     )
+    query_cot = held(query_cot, keep)
+    query_near, query_core = swap(query_cot, 1), swap(query_cot, 0, 1)
     kv_cot = halved(keep, send, bits[2:], "kv_cot_fold")
+    first, second, edge = run(
+        middle_kernel,
+        [
+            ((tokens + 16, width // 2), BF),
+            ((2 * tokens, width // 2), BF),
+            ((16, width), BF),
+        ],
+        kv_cot + [normed_cot, pooled, gain, wk, wv],
+        flops=2 * tokens * width * (key_size + value_size),
+        name="conv_cot",
+    )
+    near_first, near_second = swap(first, 1), swap(second, 1)
+    query_last = swap(held(query_near, first), 0, 1)
     query_half = (groups // 2, norm_pad, heads * key_size)
     query_keep, query_send = run(
         query_grad_kernel,
@@ -621,27 +651,16 @@
         name="query_grad",
     )
     query_parts = halved(query_keep, query_send, bits[1:], "query_fold")
-    first, second, edge = run(
-        middle_kernel,
-        [
-            ((tokens + 16, width // 2), BF),
-            ((2 * tokens, width // 2), BF),
-            ((16, width), BF),
-        ],
-        kv_cot + [normed_cot, held(pooled, query_keep), gain, wk, wv],
-        flops=2 * tokens * width * (key_size + value_size),
-        name="conv_cot",
-    )
-    near_first, near_second = swap(first, 1), swap(second, 1)
     core_first, core_second = swap(first, 0, 1), swap(second, 0, 1)
     split = width // 2
     side = side_rows(norm_rows, key_size, split) + side_rows(norm_rows, value_size, split)
-    above, below = round_up(conv_rows + 4, 16), round_up(conv_rows + side, 16)
+    above, below = round_up(conv_rows + 8, 16), round_up(conv_rows + side, 16)
     count = groups // 4
+    last_first = swap(held(near_first, query_keep), 0, 1)
     near_keep, far_keep, near_send, far_send = run(
         lambda *refs: conv_first_kernel(*refs, conv_rows=conv_rows, conv_pad=conv_pad),
         [((count, above, split), t) for t in (F32, F32, BF, BF)],
-        [conv_pick, first, core_first, near_first, swap(near_first, 0, 1)],
+        [conv_pick, first, core_first, near_first, last_first],
         [pltpu.VMEM((8 * tokens, split), BF), pltpu.VMEM((above, split), F32)],
         flops=groups * conv_pad * 8 * tokens * width,
         name="conv_grad_first",
@@ -664,7 +683,7 @@
             ((count, above + below, split), BF),
             ((count, below, split), BF),
         ],
-        [conv_pick, norm_pick, second, core_second, near_second, last_second, near_send],
+        [held(conv_pick, query_parts[0]), norm_pick, second, core_second, near_second, last_second, near_send],
         [
             pltpu.VMEM((8 * tokens, split), BF),
             pltpu.VMEM((4 * tokens, split), BF),
@@ -673,7 +692,6 @@
         flops=groups * conv_pad * 8 * tokens * width,
         name="conv_grad_second",
     )
-    edge_in = lax.ppermute(held(edge, near_keep), "seq", crossing)
     far_in_second = swap(far_send, 2)
     near_in = swap(near_send, 2)
     (far_sum,) = run(
@@ -683,22 +701,26 @@
         name="conv_send_on",
     )
     far_last = swap(far_sum, 4)
+    edges = [far_in, far_last]
+    if len(bits) > 3:
+        came = lax.ppermute(edge, "seq", crossing)
+        rows = jnp.concatenate([came[:1, :split], came[:1, split:], came[1:2, :split], came[1:2, split:]])
+        edges = [jnp.pad(rows, ((above - 4, 0), (0, 0)))[None]] * 2
     (input_grad,) = run(
         input_kernel,
         [((positions, channels), BF)],
-        [x, first, second, near_first, near_second, edge_in, conv_weight],
+        [x, first, second, near_first, near_second] + edges + [conv_weight],
         [
             pltpu.VMEM((tokens + 16, width), F32),
             pltpu.VMEM((channels // LANES, positions, LANES), F32),
         ],
         flops=20 * positions * taps * channels * width,
         name="input_grad",
-        after=[far_sum],
     )
     (far_sum,) = run(
         send_on_kernel,
         [((count, below, split), BF)],
-        [held(far_keep_second, input_grad), far_in_second],
+        [far_keep_second, far_in_second],
         name="conv_send_on",
     )
     (first_sum,) = run(

time: 94.6 us -> 94.5 us (level)
  waiting for transfers between devices: 37.5 us -> 35.5 us
  starting transfers between devices: 36.6 us -> 37.9 us
    ppermute x32, waiting for transfers between devices: 37.5 us -> 35.5 us  [swap(): lax.ppermute(value, both_axes, [(i, i ^ mask) for i in range(owners)])]
    ppermute x32, starting transfers between devices: 35.2 us -> 37.1 us  [swap(): lax.ppermute(value, both_axes, [(i, i ^ mask) for i in range(owners)])]
  transfers between devices with their start and end apart: 34 -> 33, of which waited for: 18 -> 18; matrix products, arithmetic and copies ran while one was open for 0% -> 0% of each run, Pallas kernels for 16% -> 17%
where the time goes in v7:
time: 94.5 us; the launch traced here: 94.4 us
  starting transfers between devices  37.9 us (40%)
  waiting for transfers between devices  35.5 us (38%)
  Pallas kernels  19.2 us (20%)
  local copies, waits for them, and re-layouts  0.96 us (1%)
    ppermute x32, starting transfers between devices, swap(): lax.ppermute(value, both_axes, [(i, i ^ mask) for i in range(owners)])  37.1 us
    ppermute x32, waiting for transfers between devices, swap(): lax.ppermute(value, both_axes, [(i, i ^ mask) for i in range(owners)])  35.5 us
    pallas_call x18, Pallas kernels, run(): pl.pallas_call(whole, out_shape=[jax.ShapeDtypeStruct(s, t) for s, t in o...  19.2 us
  transfers between devices with their start and end apart: 33, of which 18 were waited for; matrix products, arithmetic and copies ran while one was open for 0% of the time, Pallas kernels for 17%

profile of v7, /device:TPU:0, one launch (start us, length us, event | category | flops | bytes accessed | tf_op | source)
XLA Modules:
  0.0 94.4 jit_solution(3434455447165563038)
XLA Ops:
  2.6 5.9 %collective-permute-start = (bf16[32,384]{1,0:T(8,128)(2,1)S(1)}, bf16[32,384]{1,0:T(8,128)(2,1)S(1)}, u32[]{:S(2)}, u32[]{:S(2)}) collective-permute-start(bf16[32,384]{1,0:T(8,128)(2,1)S(1)} %get-tuple-element.57), channel_id=1, source_target_pairs={{0,2},{1,3},{2,0},{3,1},{4,6},{5,7},{6,4},{7,5},{8,10},{9,11},{10,... | collective-permute-start | bytes 73736 | tf_op jit(solution)/shard_map/ppermute | solution.py:503
  8.5 1.8 %collective-permute-done.refs_1_ = bf16[32,384]{1,0:T(8,128)(2,1)S(1)} collective-permute-done((bf16[32,384]{1,0:T(8,128)(2,1)S(1)}, bf16[32,384]{1,0:T(8,128)(2,1)S(1)}, u32[]{:S(2)}, u32[]{:S(2)}) %collective-permute-start) | collective-permute-done | bytes 24608 | tf_op jit(solution)/shard_map/ppermute | solution.py:503
  10.3 1.9 %front.1 = (bf16[320,128]{1,0:T(8,128)(2,1)S(1)}, bf16[288,384]{1,0:T(8,128)(2,1)S(1)}, bf16[128,768]{1,0:T(8,128)(2,1)S(1)}, f32[128,768]{1,0:T(8,128)S(1)}) custom-call(f32[3,304,128]{2,1,0:T(8,128)S(1)} %get-tuple-element.56.refs_0_, bf16[32,384]{1,0:T(8,128)(2,1)S(1)} %collective-permute-done.refs_1_, ...), custom_call_target="tpu_custom_call" | custom-call | flops 754974720 | bytes 4852736 | tf_op jit(solution)/shard_map/front/pallas_call | solution.py:36
  12.2 4.0 %collective-permute-start.4 = (bf16[320,128]{1,0:T(8,128)(2,1)S(1)}, bf16[320,128]{1,0:T(8,128)(2,1)S(1)}, u32[]{:S(2)}, u32[]{:S(2)}) collective-permute-start(bf16[320,128]{1,0:T(8,128)(2,1)S(1)} %get-tuple-element.60.refs_2_), channel_id=1, source_target_pairs={{0,12},{1,13},{2,14},{3,15},{4,8},{5,9},{6,10},{7,11},{8,4},{9,5},... | collective-permute-start | bytes 245768 | tf_op jit(solution)/shard_map/ppermute | solution.py:503
  16.9 1.8 %collective-permute-start.5 = (bf16[320,128]{1,0:T(8,128)(2,1)S(1)}, bf16[320,128]{1,0:T(8,128)(2,1)S(1)}, u32[]{:S(2)}, u32[]{:S(2)}) collective-permute-start(bf16[320,128]{1,0:T(8,128)(2,1)S(1)} %get-tuple-element.60.refs_2_), channel_id=1, source_target_pairs={{0,2},{1,3},{2,0},{3,1},{4,6},{5,7},{6,4},{7,5},{8,10},{9,11},{10,... | collective-permute-start | bytes 245768 | tf_op jit(solution)/shard_map/ppermute | solution.py:503
  18.7 2.4 %collective-permute-start.8 = (bf16[320,128]{1,0:T(8,128)(2,1)S(1)}, bf16[320,128]{1,0:T(8,128)(2,1)S(1)}, u32[]{:S(2)}, u32[]{:S(2)}) collective-permute-start(bf16[320,128]{1,0:T(8,128)(2,1)S(1)} %collective-permute-done.4.refs_5_), channel_id=1, source_target_pairs={{0,2},{1,3},{2,0},{3,1},{4,6},{5,7},{6,4},{7,5},{8,10},{9,11},{10,... | collective-permute-start | bytes 245768 | tf_op jit(solution)/shard_map/ppermute | solution.py:503
  22.1 1.3 %collective-permute-start.7 = (bf16[320,128]{1,0:T(8,128)(2,1)S(1)}, bf16[320,128]{1,0:T(8,128)(2,1)S(1)}, u32[]{:S(2)}, u32[]{:S(2)}) collective-permute-start(bf16[320,128]{1,0:T(8,128)(2,1)S(1)} %collective-permute-done.3.refs_4_), channel_id=1, source_target_pairs={{0,2},{1,3},{2,0},{3,1},{4,6},{5,7},{6,4},{7,5},{8,10},{9,11},{10,... | collective-permute-start | bytes 245768 | tf_op jit(solution)/shard_map/ppermute | solution.py:503
  24.9 1.7 %collective-permute-done.7.refs_8_ = bf16[320,128]{1,0:T(8,128)(2,1)S(1)} collective-permute-done((bf16[320,128]{1,0:T(8,128)(2,1)S(1)}, bf16[320,128]{1,0:T(8,128)(2,1)S(1)}, u32[]{:S(2)}, u32[]{:S(2)}) %collective-permute-start.7) | collective-permute-done | bytes 81952 | tf_op jit(solution)/shard_map/ppermute | solution.py:503
  26.6 1.2 %collective-permute-done.6.refs_7_ = bf16[320,128]{1,0:T(8,128)(2,1)S(1)} collective-permute-done((bf16[320,128]{1,0:T(8,128)(2,1)S(1)}, bf16[320,128]{1,0:T(8,128)(2,1)S(1)}, u32[]{:S(2)}, u32[]{:S(2)}) %collective-permute-start.6) | collective-permute-done | bytes 81952 | tf_op jit(solution)/shard_map/ppermute | solution.py:503
  28.7 6.5 %attend.1 = (bf16[128,1536]{1,0:T(8,128)(2,1)}, bf16[128,1024]{1,0:T(8,128)(2,1)S(1)}, f32[4,160,128]{2,1,0:T(8,128)S(1)}, bf16[4,160,128]{2,1,0:T(8,128)(2,1)S(...) custom-call(bf16[128,1024]{1,0:T(8,128)(2,1)S(1)} %get-tuple-element.61.refs_0_, ...), custom_call_target="tpu_custom_call" | custom-call | flops 2013265920 | bytes 2949120 | tf_op jit(solution)/shard_map/attend/pallas_call | solution.py:36
  35.3 1.1 %collective-permute-done.12.refs_3_ = bf16[480,384]{1,0:T(8,128)(2,1)S(1)} collective-permute-done((bf16[480,384]{1,0:T(8,128)(2,1)S(1)}, bf16[480,384]{1,0:T(8,128)(2,1)S(1)}, u32[]{:S(2)}, u32[]{:S(2)}) %collective-permute-start.12) | collective-permute-done | bytes 368672 | tf_op jit(solution)/shard_map/ppermute | solution.py:503
  38.1 2.4 %select.1 = (bf16[512,1024]{1,0:T(8,128)(2,1)S(1)}, bf16[192,512]{1,0:T(8,128)(2,1)S(1)}) custom-call(bf16[192,128]{1,0:T(8,128)(2,1)S(1)} %get-tuple-element.67.refs_0_, bf16[480,384]{1,0:T(8,128)(2,1)S(1)} %get-tuple-element.69.refs_1_, bf16[480,384]{1,0:T(8,128)(2,1)S(1)} %collective-permute-done.11.refs_2_, ...), custom_call_target="tpu_custom_call" | custom-call | flops 2013265920 | bytes 2768896 | tf_op jit(solution)/shard_map/select/pallas_call | solution.py:36
  40.5 3.1 %collective-permute-done.10.refs_3_ = bf16[4,160,128]{2,1,0:T(8,128)(2,1)S(1)} collective-permute-done((bf16[4,160,128]{2,1,0:T(8,128)(2,1)S(1)}, bf16[4,160,128]{2,1,0:T(8,128)(2,1)S(1)}, u32[]{:S(2)}, u32[]{:S(2)}) %collective-permute-start.10) | collective-permute-done | bytes 163872 | tf_op jit(solution)/shard_map/ppermute | solution.py:503
  44.1 1.1 %collective-permute-start.15 = (bf16[2,160,128]{2,1,0:T(8,128)(2,1)S(1)}, bf16[2,160,128]{2,1,0:T(8,128)(2,1)S(1)}, u32[]{:S(2)}, u32[]{:S(2)}) collective-permute-start(bf16[2,160,128]{2,1,0:T(8,128)(2,1)S(1)} %get-tuple-element.75), channel_id=1, source_target_pairs={{0,2},{1,3},{2,0},{3,1},{4,6},{5,7},{6,4},{7,5},{8,10},{9,11},{10,... | collective-permute-start | bytes 245768 | tf_op jit(solution)/shard_map/ppermute | solution.py:503
  45.2 2.9 %collective-permute-done.14.refs_1_ = bf16[2,160,128]{2,1,0:T(8,128)(2,1)S(1)} collective-permute-done((bf16[2,160,128]{2,1,0:T(8,128)(2,1)S(1)}, bf16[2,160,128]{2,1,0:T(8,128)(2,1)S(1)}, u32[]{:S(2)}, u32[]{:S(2)}) %collective-permute-start.14) | collective-permute-done | bytes 81952 | tf_op jit(solution)/shard_map/ppermute | solution.py:503
  48.6 1.1 %collective-permute-start.21 = (bf16[128,1024]{1,0:T(8,128)(2,1)S(1)}, bf16[128,1024]{1,0:T(8,128)(2,1)S(1)}, u32[]{:S(2)}, u32[]{:S(2)}) collective-permute-start(bf16[128,1024]{1,0:T(8,128)(2,1)S(1)} %get-tuple-element.83.refs_0_.refs_1_), channel_id=1, source_target_pairs={{0,2},{1,3},{2,0},{3,1},{4,6},{5,7},{6,4},{7,5},{8,10},{9,11},{10,... | collective-permute-start | bytes 786440 | tf_op jit(solution)/shard_map/ppermute | solution.py:503
  49.8 2.9 %collective-permute-start.16 = (bf16[1,320,128]{2,1,0:T(8,128)(2,1)S(1)}, bf16[1,320,128]{2,1,0:T(8,128)(2,1)S(1)}, u32[]{:S(2)}, u32[]{:S(2)}) collective-permute-start(bf16[1,320,128]{2,1,0:T(8,128)(2,1)S(1)} %get-tuple-element.77), channel_id=1, source_target_pairs={{0,8},{1,9},{2,10},{3,11},{4,12},{5,13},{6,14},{7,15},{8,0},{9,1},... | collective-permute-start | bytes 245768 | tf_op jit(solution)/shard_map/ppermute | solution.py:503
  53.4 1.7 %collective-permute-done.16.refs_1_ = bf16[1,320,128]{2,1,0:T(8,128)(2,1)S(1)} collective-permute-done((bf16[1,320,128]{2,1,0:T(8,128)(2,1)S(1)}, bf16[1,320,128]{2,1,0:T(8,128)(2,1)S(1)}, u32[]{:S(2)}, u32[]{:S(2)}) %collective-permute-start.16) | collective-permute-done | bytes 81952 | tf_op jit(solution)/shard_map/ppermute | solution.py:503
  55.1 1.0 %conv_cot.1 = (bf16[144,384]{1,0:T(8,128)(2,1)S(1)}, bf16[256,384]{1,0:T(8,128)(2,1)S(1)}, bf16[16,768]{1,0:T(8,128)(2,1)}) custom-call(f32[1,320,128]{2,1,0:T(8,128)S(1)} %get-tuple-element.76.refs_0_, bf16[1,320,128]{2,1,0:T(8,128)(2,1)S(1)} %collective-permute-done.16.refs_1_, f32[128,768]{1,0:T(8,128)S(1)} %query_part.1.refs_2_, ...), custom_call_target="tpu_custom_call" | custom-call | flops 62914560 | bytes 1858560 | tf_op jit(solution)/shard_map/conv_cot/pallas_call | solution.py:36
  57.2 1.1 %collective-permute-start.18 = (bf16[256,384]{1,0:T(8,128)(2,1)S(1)}, bf16[256,384]{1,0:T(8,128)(2,1)S(1)}, u32[]{:S(2)}, u32[]{:S(2)}) collective-permute-start(bf16[256,384]{1,0:T(8,128)(2,1)S(1)} %get-tuple-element.81.refs_2_), channel_id=1, source_target_pairs={{0,2},{1,3},{2,0},{3,1},{4,6},{5,7},{6,4},{7,5},{8,10},{9,11},{10,... | collective-permute-start | bytes 589832 | tf_op jit(solution)/shard_map/ppermute | solution.py:503
  59.2 2.9 %collective-permute-done.17.refs_3_ = bf16[144,384]{1,0:T(8,128)(2,1)S(1)} collective-permute-done((bf16[144,384]{1,0:T(8,128)(2,1)S(1)}, bf16[144,384]{1,0:T(8,128)(2,1)S(1)}, u32[]{:S(2)}, u32[]{:S(2)}) %collective-permute-start.17) | collective-permute-done | bytes 110624 | tf_op jit(solution)/shard_map/ppermute | solution.py:503
  62.6 1.7 %collective-permute-start.26 = (bf16[2,48,1024]{2,1,0:T(8,128)(2,1)S(1)}, bf16[2,48,1024]{2,1,0:T(8,128)(2,1)S(1)}, u32[]{:S(2)}, u32[]{:S(2)}) collective-permute-start(bf16[2,48,1024]{2,1,0:T(8,128)(2,1)S(1)} %get-tuple-element.90), channel_id=1, source_target_pairs={{0,4},{1,5},{2,6},{3,7},{4,0},{5,1},{6,2},{7,3},{8,12},{9,13},{10,... | collective-permute-start | bytes 589832 | tf_op jit(solution)/shard_map/ppermute | solution.py:503
  65.8 1.7 %collective-permute-start.24 = (bf16[1,128,384]{2,1,0:T(8,128)(2,1)S(1)}, bf16[1,128,384]{2,1,0:T(8,128)(2,1)S(1)}, u32[]{:S(2)}, u32[]{:S(2)}) collective-permute-start(bf16[1,128,384]{2,1,0:T(8,128)(2,1)S(1)} %get-tuple-element.87), channel_id=1, source_target_pairs={{0,4},{1,5},{2,6},{3,7},{4,0},{5,1},{6,2},{7,3},{8,12},{9,13},{10,... | collective-permute-start | bytes 294920 | tf_op jit(solution)/shard_map/ppermute | solution.py:503
  67.5 4.0 %collective-permute-done.24.refs_1_.refs_5_ = bf16[1,128,384]{2,1,0:T(8,128)(2,1)S(1)} collective-permute-done((bf16[1,128,384]{2,1,0:T(8,128)(2,1)S(1)}, bf16[1,128,384]{2,1,0:T(8,128)(2,1)S(1)}, u32[]{:S(2)}, u32[]{:S(2)}) %collective-permute-start.24) | collective-permute-done | bytes 98336 | tf_op jit(solution)/shard_map/ppermute | solution.py:503
  71.6 3.1 %collective-permute-start.25 = (bf16[1,128,384]{2,1,0:T(8,128)(2,1)S(1)}, bf16[1,128,384]{2,1,0:T(8,128)(2,1)S(1)}, u32[]{:S(2)}, u32[]{:S(2)}) collective-permute-start(bf16[1,128,384]{2,1,0:T(8,128)(2,1)S(1)} %conv_send_on.2), channel_id=1, source_target_pairs={{0,8},{1,9},{2,10},{3,11},{4,12},{5,13},{6,14},{7,15},{8,0},{9,1},... | collective-permute-start | bytes 294920 | tf_op jit(solution)/shard_map/ppermute | solution.py:503
  75.8 1.5 %collective-permute-start.30 = (bf16[1,160,384]{2,1,0:T(8,128)(2,1)S(1)}, bf16[1,160,384]{2,1,0:T(8,128)(2,1)S(1)}, u32[]{:S(2)}, u32[]{:S(2)}) collective-permute-start(bf16[1,160,384]{2,1,0:T(8,128)(2,1)S(1)} %get-tuple-element.98), channel_id=1, source_target_pairs={{0,4},{1,5},{2,6},{3,7},{4,0},{5,1},{6,2},{7,3},{8,12},{9,13},{10,... | collective-permute-start | bytes 368648 | tf_op jit(solution)/shard_map/ppermute | solution.py:503
  77.8 4.7 %collective-permute-done.25.refs_6_.refs_2_ = bf16[1,128,384]{2,1,0:T(8,128)(2,1)S(1)} collective-permute-done((bf16[1,128,384]{2,1,0:T(8,128)(2,1)S(1)}, bf16[1,128,384]{2,1,0:T(8,128)(2,1)S(1)}, u32[]{:S(2)}, u32[]{:S(2)}) %collective-permute-start.25) | collective-permute-done | bytes 98336 | tf_op jit(solution)/shard_map/ppermute | solution.py:503
  82.5 2.1 %input_grad.1 = bf16[256,384]{1,0:T(8,128)(2,1)} custom-call(bf16[256,384]{1,0:T(8,128)(2,1)S(1)} %bitcast.10, bf16[144,384]{1,0:T(8,128)(2,1)S(1)} %get-tuple-element.80.refs_1_, bf16[256,384]{1,0:T(8,128)(2,1)S(1)} %get-tuple-element.81.refs_2_, bf16[144,384]{1,0:T(8,128)(2,1)S(1)} %collective-permute-done.17.refs_3_, ...), custom_call_target="tpu_custom_call" | custom-call | flops 7549747200 | bytes 4153344 | tf_op jit(solution)/shard_map/input_grad/pallas_call | solution.py:36
  84.6 1.7 %collective-permute-done.30.refs_1_ = bf16[1,160,384]{2,1,0:T(8,128)(2,1)S(1)} collective-permute-done((bf16[1,160,384]{2,1,0:T(8,128)(2,1)S(1)}, bf16[1,160,384]{2,1,0:T(8,128)(2,1)S(1)}, u32[]{:S(2)}, u32[]{:S(2)}) %collective-permute-start.30) | collective-permute-done | bytes 122912 | tf_op jit(solution)/shard_map/ppermute | solution.py:503
  86.3 1.2 %collective-permute-start.31 = (bf16[1,160,384]{2,1,0:T(8,128)(2,1)S(1)}, bf16[1,160,384]{2,1,0:T(8,128)(2,1)S(1)}, u32[]{:S(2)}, u32[]{:S(2)}) collective-permute-start(bf16[1,160,384]{2,1,0:T(8,128)(2,1)S(1)} %conv_send_on.3), channel_id=1, source_target_pairs={{0,8},{1,9},{2,10},{3,11},{4,12},{5,13},{6,14},{7,15},{8,0},{9,1},... | collective-permute-start | bytes 368648 | tf_op jit(solution)/shard_map/ppermute | solution.py:503
  87.5 2.2 %collective-permute-done.29.refs_1_.refs_2_ = bf16[1,288,384]{2,1,0:T(8,128)(2,1)S(1)} collective-permute-done((bf16[1,288,384]{2,1,0:T(8,128)(2,1)S(1)}, bf16[1,288,384]{2,1,0:T(8,128)(2,1)S(1)}, u32[]{:S(2)}, u32[]{:S(2)}) %collective-permute-start.29) | collective-permute-done | bytes 221216 | tf_op jit(solution)/shard_map/ppermute | solution.py:503
  89.8 3.7 %collective-permute-done.31.refs_3_ = bf16[1,160,384]{2,1,0:T(8,128)(2,1)S(1)} collective-permute-done((bf16[1,160,384]{2,1,0:T(8,128)(2,1)S(1)}, bf16[1,160,384]{2,1,0:T(8,128)(2,1)S(1)}, u32[]{:S(2)}, u32[]{:S(2)}) %collective-permute-start.31) | collective-permute-done | bytes 122912 | tf_op jit(solution)/shard_map/ppermute | solution.py:503
  (69 shorter events, 16.0 us)
Async XLA Ops:
  1.8 6.7 %collective-permute-start.1 = (bf16[32,384]{1,0:T(8,128)(2,1)S(1)}, bf16[32,384]{1,0:T(8,128)(2,1)S(1)}, u32[]{:S(2)}, u32[]{:S(2)}) collective-permute-start(bf16[32,384]{1,0:T(8,128)(2,1)S(1)} %get-tuple-element.57), channel_id=1, source_target_pairs={{2,4},{6,8},{10,12},{4,2},{8,6},{12,10},{3,5},{7,9},{11,13},{5,3},... | collective-permute-start | bytes 73736 | tf_op jit(solution)/shard_map/ppermute | solution.py:534
  2.6 7.7 %collective-permute-start = (bf16[32,384]{1,0:T(8,128)(2,1)S(1)}, bf16[32,384]{1,0:T(8,128)(2,1)S(1)}, u32[]{:S(2)}, u32[]{:S(2)}) collective-permute-start(bf16[32,384]{1,0:T(8,128)(2,1)S(1)} %get-tuple-element.57), channel_id=1, source_target_pairs={{0,2},{1,3},{2,0},{3,1},{4,6},{5,7},{6,4},{7,5},{8,10},{9,11},{10,... | collective-permute-start | bytes 73736 | tf_op jit(solution)/shard_map/ppermute | solution.py:503
  12.2 6.5 %collective-permute-start.4 = (bf16[320,128]{1,0:T(8,128)(2,1)S(1)}, bf16[320,128]{1,0:T(8,128)(2,1)S(1)}, u32[]{:S(2)}, u32[]{:S(2)}) collective-permute-start(bf16[320,128]{1,0:T(8,128)(2,1)S(1)} %get-tuple-element.60.refs_2_), channel_id=1, source_target_pairs={{0,12},{1,13},{2,14},{3,15},{4,8},{5,9},{6,10},{7,11},{8,4},{9,5},... | collective-permute-start | bytes 245768 | tf_op jit(solution)/shard_map/ppermute | solution.py:503
  16.2 5.9 %collective-permute-start.3 = (bf16[320,128]{1,0:T(8,128)(2,1)S(1)}, bf16[320,128]{1,0:T(8,128)(2,1)S(1)}, u32[]{:S(2)}, u32[]{:S(2)}) collective-permute-start(bf16[320,128]{1,0:T(8,128)(2,1)S(1)} %get-tuple-element.60.refs_2_), channel_id=1, source_target_pairs={{0,8},{1,9},{2,10},{3,11},{4,12},{5,13},{6,14},{7,15},{8,0},{9,1},... | collective-permute-start | bytes 245768 | tf_op jit(solution)/shard_map/ppermute | solution.py:503
  16.2 7.2 %collective-permute-start.2 = (bf16[320,128]{1,0:T(8,128)(2,1)S(1)}, bf16[320,128]{1,0:T(8,128)(2,1)S(1)}, u32[]{:S(2)}, u32[]{:S(2)}) collective-permute-start(bf16[320,128]{1,0:T(8,128)(2,1)S(1)} %get-tuple-element.60.refs_2_), channel_id=1, source_target_pairs={{0,4},{1,5},{2,6},{3,7},{4,0},{5,1},{6,2},{7,3},{8,12},{9,13},{10,... | collective-permute-start | bytes 245768 | tf_op jit(solution)/shard_map/ppermute | solution.py:503
  16.9 8.0 %collective-permute-start.5 = (bf16[320,128]{1,0:T(8,128)(2,1)S(1)}, bf16[320,128]{1,0:T(8,128)(2,1)S(1)}, u32[]{:S(2)}, u32[]{:S(2)}) collective-permute-start(bf16[320,128]{1,0:T(8,128)(2,1)S(1)} %get-tuple-element.60.refs_2_), channel_id=1, source_target_pairs={{0,2},{1,3},{2,0},{3,1},{4,6},{5,7},{6,4},{7,5},{8,10},{9,11},{10,... | collective-permute-start | bytes 245768 | tf_op jit(solution)/shard_map/ppermute | solution.py:503
  18.7 6.2 %collective-permute-start.8 = (bf16[320,128]{1,0:T(8,128)(2,1)S(1)}, bf16[320,128]{1,0:T(8,128)(2,1)S(1)}, u32[]{:S(2)}, u32[]{:S(2)}) collective-permute-start(bf16[320,128]{1,0:T(8,128)(2,1)S(1)} %collective-permute-done.4.refs_5_), channel_id=1, source_target_pairs={{0,2},{1,3},{2,0},{3,1},{4,6},{5,7},{6,4},{7,5},{8,10},{9,11},{10,... | collective-permute-start | bytes 245768 | tf_op jit(solution)/shard_map/ppermute | solution.py:503
  22.1 4.5 %collective-permute-start.7 = (bf16[320,128]{1,0:T(8,128)(2,1)S(1)}, bf16[320,128]{1,0:T(8,128)(2,1)S(1)}, u32[]{:S(2)}, u32[]{:S(2)}) collective-permute-start(bf16[320,128]{1,0:T(8,128)(2,1)S(1)} %collective-permute-done.3.refs_4_), channel_id=1, source_target_pairs={{0,2},{1,3},{2,0},{3,1},{4,6},{5,7},{6,4},{7,5},{8,10},{9,11},{10,... | collective-permute-start | bytes 245768 | tf_op jit(solution)/shard_map/ppermute | solution.py:503
  23.4 4.4 %collective-permute-start.6 = (bf16[320,128]{1,0:T(8,128)(2,1)S(1)}, bf16[320,128]{1,0:T(8,128)(2,1)S(1)}, u32[]{:S(2)}, u32[]{:S(2)}) collective-permute-start(bf16[320,128]{1,0:T(8,128)(2,1)S(1)} %collective-permute-done.2.refs_3_), channel_id=1, source_target_pairs={{0,2},{1,3},{2,0},{3,1},{4,6},{5,7},{6,4},{7,5},{8,10},{9,11},{10,... | collective-permute-start | bytes 245768 | tf_op jit(solution)/shard_map/ppermute | solution.py:503
  27.9 8.5 %collective-permute-start.12 = (bf16[480,384]{1,0:T(8,128)(2,1)S(1)}, bf16[480,384]{1,0:T(8,128)(2,1)S(1)}, u32[]{:S(2)}, u32[]{:S(2)}) collective-permute-start(bf16[480,384]{1,0:T(8,128)(2,1)S(1)} %get-tuple-element.69.refs_1_), channel_id=1, source_target_pairs={{0,2},{1,3},{2,0},{3,1},{4,6},{5,7},{6,4},{7,5},{8,10},{9,11},{10,... | collective-permute-start | bytes 1105928 | tf_op jit(solution)/shard_map/ppermute | solution.py:503
  28.7 9.0 %collective-permute-start.11 = (bf16[480,384]{1,0:T(8,128)(2,1)S(1)}, bf16[480,384]{1,0:T(8,128)(2,1)S(1)}, u32[]{:S(2)}, u32[]{:S(2)}) collective-permute-start(bf16[480,384]{1,0:T(8,128)(2,1)S(1)} %get-tuple-element.69.refs_1_), channel_id=1, source_target_pairs={{0,1},{1,0},{2,3},{3,2},{4,5},{5,4},{6,7},{7,6},{8,9},{9,8},{10,11... | collective-permute-start | bytes 1105928 | tf_op jit(solution)/shard_map/ppermute | solution.py:503
  36.4 7.2 %collective-permute-start.9 = (bf16[4,160,128]{2,1,0:T(8,128)(2,1)S(1)}, bf16[4,160,128]{2,1,0:T(8,128)(2,1)S(1)}, u32[]{:S(2)}, u32[]{:S(2)}) collective-permute-start(bf16[4,160,128]{2,1,0:T(8,128)(2,1)S(1)} %get-tuple-element.64), channel_id=1, source_target_pairs={{0,2},{1,3},{2,0},{3,1},{4,6},{5,7},{6,4},{7,5},{8,10},{9,11},{10,... | collective-permute-start | bytes 491528 | tf_op jit(solution)/shard_map/ppermute | solution.py:503
  37.2 6.3 %collective-permute-start.10 = (bf16[4,160,128]{2,1,0:T(8,128)(2,1)S(1)}, bf16[4,160,128]{2,1,0:T(8,128)(2,1)S(1)}, u32[]{:S(2)}, u32[]{:S(2)}) collective-permute-start(bf16[4,160,128]{2,1,0:T(8,128)(2,1)S(1)} %get-tuple-element.66), channel_id=1, source_target_pairs={{0,4},{1,5},{2,6},{3,7},{4,0},{5,1},{6,2},{7,3},{8,12},{9,13},{10,... | collective-permute-start | bytes 491528 | tf_op jit(solution)/shard_map/ppermute | solution.py:503
  43.6 4.5 %collective-permute-start.14 = (bf16[2,160,128]{2,1,0:T(8,128)(2,1)S(1)}, bf16[2,160,128]{2,1,0:T(8,128)(2,1)S(1)}, u32[]{:S(2)}, u32[]{:S(2)}) collective-permute-start(bf16[2,160,128]{2,1,0:T(8,128)(2,1)S(1)} %get-tuple-element.73), channel_id=1, source_target_pairs={{0,4},{1,5},{2,6},{3,7},{4,0},{5,1},{6,2},{7,3},{8,12},{9,13},{10,... | collective-permute-start | bytes 245768 | tf_op jit(solution)/shard_map/ppermute | solution.py:503
  44.1 4.4 %collective-permute-start.15 = (bf16[2,160,128]{2,1,0:T(8,128)(2,1)S(1)}, bf16[2,160,128]{2,1,0:T(8,128)(2,1)S(1)}, u32[]{:S(2)}, u32[]{:S(2)}) collective-permute-start(bf16[2,160,128]{2,1,0:T(8,128)(2,1)S(1)} %get-tuple-element.75), channel_id=1, source_target_pairs={{0,2},{1,3},{2,0},{3,1},{4,6},{5,7},{6,4},{7,5},{8,10},{9,11},{10,... | collective-permute-start | bytes 245768 | tf_op jit(solution)/shard_map/ppermute | solution.py:503
  48.6 7.5 %collective-permute-start.21 = (bf16[128,1024]{1,0:T(8,128)(2,1)S(1)}, bf16[128,1024]{1,0:T(8,128)(2,1)S(1)}, u32[]{:S(2)}, u32[]{:S(2)}) collective-permute-start(bf16[128,1024]{1,0:T(8,128)(2,1)S(1)} %get-tuple-element.83.refs_0_.refs_1_), channel_id=1, source_target_pairs={{0,2},{1,3},{2,0},{3,1},{4,6},{5,7},{6,4},{7,5},{8,10},{9,11},{10,... | collective-permute-start | bytes 786440 | tf_op jit(solution)/shard_map/ppermute | solution.py:503
  49.8 5.4 %collective-permute-start.16 = (bf16[1,320,128]{2,1,0:T(8,128)(2,1)S(1)}, bf16[1,320,128]{2,1,0:T(8,128)(2,1)S(1)}, u32[]{:S(2)}, u32[]{:S(2)}) collective-permute-start(bf16[1,320,128]{2,1,0:T(8,128)(2,1)S(1)} %get-tuple-element.77), channel_id=1, source_target_pairs={{0,8},{1,9},{2,10},{3,11},{4,12},{5,13},{6,14},{7,15},{8,0},{9,1},... | collective-permute-start | bytes 245768 | tf_op jit(solution)/shard_map/ppermute | solution.py:503
  53.3 4.9 %collective-permute-start.20 = (bf16[128,1024]{1,0:T(8,128)(2,1)S(1)}, bf16[128,1024]{1,0:T(8,128)(2,1)S(1)}, u32[]{:S(2)}, u32[]{:S(2)}) collective-permute-start(bf16[128,1024]{1,0:T(8,128)(2,1)S(1)} %get-tuple-element.83.refs_0_.refs_1_), channel_id=1, source_target_pairs={{0,1},{1,0},{2,3},{3,2},{4,5},{5,4},{6,7},{7,6},{8,9},{9,8},{10,11... | collective-permute-start | bytes 786440 | tf_op jit(solution)/shard_map/ppermute | solution.py:503
  56.2 2.1 %collective-permute-start.22 = (bf16[128,1024]{1,0:T(8,128)(2,1)S(1)}, bf16[128,1024]{1,0:T(8,128)(2,1)S(1)}, u32[]{:S(2)}, u32[]{:S(2)}) collective-permute-start(bf16[128,1024]{1,0:T(8,128)(2,1)S(1)} %collective-permute-done.21.refs_3_), channel_id=1, source_target_pairs={{0,1},{1,0},{2,3},{3,2},{4,5},{5,4},{6,7},{7,6},{8,9},{9,8},{10,11... | collective-permute-start | bytes 786440 | tf_op jit(solution)/shard_map/ppermute | solution.py:503
  56.2 5.9 %collective-permute-start.17 = (bf16[144,384]{1,0:T(8,128)(2,1)S(1)}, bf16[144,384]{1,0:T(8,128)(2,1)S(1)}, u32[]{:S(2)}, u32[]{:S(2)}) collective-permute-start(bf16[144,384]{1,0:T(8,128)(2,1)S(1)} %get-tuple-element.80.refs_1_), channel_id=1, source_target_pairs={{0,2},{1,3},{2,0},{3,1},{4,6},{5,7},{6,4},{7,5},{8,10},{9,11},{10,... | collective-permute-start | bytes 331784 | tf_op jit(solution)/shard_map/ppermute | solution.py:503
  57.2 8.7 %collective-permute-start.18 = (bf16[256,384]{1,0:T(8,128)(2,1)S(1)}, bf16[256,384]{1,0:T(8,128)(2,1)S(1)}, u32[]{:S(2)}, u32[]{:S(2)}) collective-permute-start(bf16[256,384]{1,0:T(8,128)(2,1)S(1)} %get-tuple-element.81.refs_2_), channel_id=1, source_target_pairs={{0,2},{1,3},{2,0},{3,1},{4,6},{5,7},{6,4},{7,5},{8,10},{9,11},{10,... | collective-permute-start | bytes 589832 | tf_op jit(solution)/shard_map/ppermute | solution.py:503
  58.3 6.0 %collective-permute-start.19 = (bf16[144,384]{1,0:T(8,128)(2,1)S(1)}, bf16[144,384]{1,0:T(8,128)(2,1)S(1)}, u32[]{:S(2)}, u32[]{:S(2)}) collective-permute-start(bf16[144,384]{1,0:T(8,128)(2,1)S(1)} %get-tuple-element.80.refs_1_), channel_id=1, source_target_pairs={{0,1},{1,0},{2,3},{3,2},{4,5},{5,4},{6,7},{7,6},{8,9},{9,8},{10,11... | collective-permute-start | bytes 331784 | tf_op jit(solution)/shard_map/ppermute | solution.py:503
  62.1 2.2 %collective-permute-start.23 = (bf16[144,384]{1,0:T(8,128)(2,1)S(1)}, bf16[144,384]{1,0:T(8,128)(2,1)S(1)}, u32[]{:S(2)}, u32[]{:S(2)}) collective-permute-start(bf16[144,384]{1,0:T(8,128)(2,1)S(1)} %collective-permute-done.17.refs_3_), channel_id=1, source_target_pairs={{0,1},{1,0},{2,3},{3,2},{4,5},{5,4},{6,7},{7,6},{8,9},{9,8},{10,11... | collective-permute-start | bytes 331784 | tf_op jit(solution)/shard_map/ppermute | solution.py:503
  62.1 12.7 %collective-permute-start.27 = (bf16[256,384]{1,0:T(8,128)(2,1)S(1)}, bf16[256,384]{1,0:T(8,128)(2,1)S(1)}, u32[]{:S(2)}, u32[]{:S(2)}) collective-permute-start(bf16[256,384]{1,0:T(8,128)(2,1)S(1)} %get-tuple-element.81.refs_2_), channel_id=1, source_target_pairs={{0,1},{1,0},{2,3},{3,2},{4,5},{5,4},{6,7},{7,6},{8,9},{9,8},{10,11... | collective-permute-start | bytes 589832 | tf_op jit(solution)/shard_map/ppermute | solution.py:503
  62.6 12.0 %collective-permute-start.26 = (bf16[2,48,1024]{2,1,0:T(8,128)(2,1)S(1)}, bf16[2,48,1024]{2,1,0:T(8,128)(2,1)S(1)}, u32[]{:S(2)}, u32[]{:S(2)}) collective-permute-start(bf16[2,48,1024]{2,1,0:T(8,128)(2,1)S(1)} %get-tuple-element.90), channel_id=1, source_target_pairs={{0,4},{1,5},{2,6},{3,7},{4,0},{5,1},{6,2},{7,3},{8,12},{9,13},{10,... | collective-permute-start | bytes 589832 | tf_op jit(solution)/shard_map/ppermute | solution.py:503
  65.8 8.9 %collective-permute-start.28 = (bf16[256,384]{1,0:T(8,128)(2,1)S(1)}, bf16[256,384]{1,0:T(8,128)(2,1)S(1)}, u32[]{:S(2)}, u32[]{:S(2)}) collective-permute-start(bf16[256,384]{1,0:T(8,128)(2,1)S(1)} %collective-permute-done.18.refs_4_), channel_id=1, source_target_pairs={{0,1},{1,0},{2,3},{3,2},{4,5},{5,4},{6,7},{7,6},{8,9},{9,8},{10,11... | collective-permute-start | bytes 589832 | tf_op jit(solution)/shard_map/ppermute | solution.py:503
  65.8 5.7 %collective-permute-start.24 = (bf16[1,128,384]{2,1,0:T(8,128)(2,1)S(1)}, bf16[1,128,384]{2,1,0:T(8,128)(2,1)S(1)}, u32[]{:S(2)}, u32[]{:S(2)}) collective-permute-start(bf16[1,128,384]{2,1,0:T(8,128)(2,1)S(1)} %get-tuple-element.87), channel_id=1, source_target_pairs={{0,4},{1,5},{2,6},{3,7},{4,0},{5,1},{6,2},{7,3},{8,12},{9,13},{10,... | collective-permute-start | bytes 294920 | tf_op jit(solution)/shard_map/ppermute | solution.py:503
  71.6 11.0 %collective-permute-start.25 = (bf16[1,128,384]{2,1,0:T(8,128)(2,1)S(1)}, bf16[1,128,384]{2,1,0:T(8,128)(2,1)S(1)}, u32[]{:S(2)}, u32[]{:S(2)}) collective-permute-start(bf16[1,128,384]{2,1,0:T(8,128)(2,1)S(1)} %conv_send_on.2), channel_id=1, source_target_pairs={{0,8},{1,9},{2,10},{3,11},{4,12},{5,13},{6,14},{7,15},{8,0},{9,1},... | collective-permute-start | bytes 294920 | tf_op jit(solution)/shard_map/ppermute | solution.py:503
  74.7 15.1 %collective-permute-start.32 = (bf16[1,48,1024]{2,1,0:T(8,128)(2,1)S(1)}, bf16[1,48,1024]{2,1,0:T(8,128)(2,1)S(1)}, u32[]{:S(2)}, u32[]{:S(2)}) collective-permute-start(bf16[1,48,1024]{2,1,0:T(8,128)(2,1)S(1)} %get-tuple-element.99), channel_id=1, source_target_pairs={{0,8},{1,9},{2,10},{3,11},{4,12},{5,13},{6,14},{7,15},{8,0},{9,1},... | collective-permute-start | bytes 294920 | tf_op jit(solution)/shard_map/ppermute | solution.py:503
  75.8 10.5 %collective-permute-start.30 = (bf16[1,160,384]{2,1,0:T(8,128)(2,1)S(1)}, bf16[1,160,384]{2,1,0:T(8,128)(2,1)S(1)}, u32[]{:S(2)}, u32[]{:S(2)}) collective-permute-start(bf16[1,160,384]{2,1,0:T(8,128)(2,1)S(1)} %get-tuple-element.98), channel_id=1, source_target_pairs={{0,4},{1,5},{2,6},{3,7},{4,0},{5,1},{6,2},{7,3},{8,12},{9,13},{10,... | collective-permute-start | bytes 368648 | tf_op jit(solution)/shard_map/ppermute | solution.py:503
  77.3 12.4 %collective-permute-start.29 = (bf16[1,288,384]{2,1,0:T(8,128)(2,1)S(1)}, bf16[1,288,384]{2,1,0:T(8,128)(2,1)S(1)}, u32[]{:S(2)}, u32[]{:S(2)}) collective-permute-start(bf16[1,288,384]{2,1,0:T(8,128)(2,1)S(1)} %get-tuple-element.95), channel_id=1, source_target_pairs={{0,4},{1,5},{2,6},{3,7},{4,0},{5,1},{6,2},{7,3},{8,12},{9,13},{10,... | collective-permute-start | bytes 663560 | tf_op jit(solution)/shard_map/ppermute | solution.py:503
  86.3 7.2 %collective-permute-start.31 = (bf16[1,160,384]{2,1,0:T(8,128)(2,1)S(1)}, bf16[1,160,384]{2,1,0:T(8,128)(2,1)S(1)}, u32[]{:S(2)}, u32[]{:S(2)}) collective-permute-start(bf16[1,160,384]{2,1,0:T(8,128)(2,1)S(1)} %conv_send_on.3), channel_id=1, source_target_pairs={{0,8},{1,9},{2,10},{3,11},{4,12},{5,13},{6,14},{7,15},{8,0},{9,1},... | collective-permute-start | bytes 368648 | tf_op jit(solution)/shard_map/ppermute | solution.py:503
  (9 other events, 102.9 us)

commit v8 on v7

--- a/solution.py
+++ b/solution.py
@@ -237,7 +237,7 @@
     out[...] = dot_t(dq[...], wq[...])
 
 
-def middle_kernel(own, came, part, pooled_in, gain_in, wk, wv, first, second, edge):
+def middle_kernel(own, came, part, pooled_in, gain_in, wk, wv, first, second, *edges):
     size = own.shape[2]
     tokens, width = pooled_in.shape
     total = (own[0] + came[0].astype(F32)).astype(BF).astype(F32)
@@ -268,8 +268,9 @@
     first[tokens:] = gains.astype(BF)
     second[:tokens] = conv_cot[:, split:].astype(BF)
     second[tokens:] = side.astype(BF)
-    ends = jnp.where(row == 0, conv_cot[:1], jnp.where(row == 1, conv_cot[tokens - 1 :], 0.0))
-    edge[...] = ends.astype(BF)
+    for edge in edges:
+        ends = jnp.where(row == 0, conv_cot[:1], jnp.where(row == 1, conv_cot[tokens - 1 :], 0.0))
+        edge[...] = ends.astype(BF)
 
 
 def place(other=0):
@@ -628,13 +629,13 @@
     query_cot = held(query_cot, keep)
     query_near, query_core = swap(query_cot, 1), swap(query_cot, 0, 1)
     kv_cot = halved(keep, send, bits[2:], "kv_cot_fold")
-    first, second, edge = run(
+    first, second, *edge = run(
         middle_kernel,
         [
             ((tokens + 16, width // 2), BF),
             ((2 * tokens, width // 2), BF),
-            ((16, width), BF),
-        ],
+        ]
+        + [((16, width), BF)] * (len(bits) > 3),
         kv_cot + [normed_cot, pooled, gain, wk, wv],
         flops=2 * tokens * width * (key_size + value_size),
         name="conv_cot",
@@ -701,27 +702,27 @@
         name="conv_send_on",
     )
     far_last = swap(far_sum, 4)
+    (far_sum,) = run(
+        send_on_kernel,
+        [((count, below, split), BF)],
+        [far_keep_second, far_in_second],
+        name="conv_send_on",
+    )
     edges = [far_in, far_last]
     if len(bits) > 3:
-        came = lax.ppermute(edge, "seq", crossing)
+        came = lax.ppermute(edge[0], "seq", crossing)
         rows = jnp.concatenate([came[:1, :split], came[:1, split:], came[1:2, :split], came[1:2, split:]])
         edges = [jnp.pad(rows, ((above - 4, 0), (0, 0)))[None]] * 2
     (input_grad,) = run(
         input_kernel,
         [((positions, channels), BF)],
-        [x, first, second, near_first, near_second] + edges + [conv_weight],
+        [held(x, far_sum), first, second, near_first, near_second] + edges + [conv_weight],
         [
             pltpu.VMEM((tokens + 16, width), F32),
             pltpu.VMEM((channels // LANES, positions, LANES), F32),
         ],
         flops=20 * positions * taps * channels * width,
         name="input_grad",
-    )
-    (far_sum,) = run(
-        send_on_kernel,
-        [((count, below, split), BF)],
-        [far_keep_second, far_in_second],
-        name="conv_send_on",
     )
     (first_sum,) = run(
         first_sum_kernel,

time: 94.5 us -> 88 us (0.931)
  waiting for transfers between devices: 35.5 us -> 28.1 us
  starting transfers between devices: 37.9 us -> 39.2 us
    ppermute x32, waiting for transfers between devices: 35.5 us -> 28.1 us  [swap(): lax.ppermute(value, both_axes, [(i, i ^ mask) for i in range(owners)])]
    ppermute x32, starting transfers between devices: 37.1 us -> 38.5 us  [swap(): lax.ppermute(value, both_axes, [(i, i ^ mask) for i in range(owners)])]
  transfers between devices with their start and end apart: 33 -> 33, of which waited for: 18 -> 17; matrix products, arithmetic and copies ran while one was open for 0% -> 0% of each run, Pallas kernels for 17% -> 18%
where the time goes in v8:
time: 88 us; the launch traced here: 87.8 us
  starting transfers between devices  39.2 us (45%)
  waiting for transfers between devices  28.1 us (32%)
  Pallas kernels  18.6 us (21%)
  local copies, waits for them, and re-layouts  0.96 us (1%)
    ppermute x32, starting transfers between devices, swap(): lax.ppermute(value, both_axes, [(i, i ^ mask) for i in range(owners)])  38.5 us
    ppermute x32, waiting for transfers between devices, swap(): lax.ppermute(value, both_axes, [(i, i ^ mask) for i in range(owners)])  28.1 us
    pallas_call x18, Pallas kernels, run(): pl.pallas_call(whole, out_shape=[jax.ShapeDtypeStruct(s, t) for s, t in o...  18.6 us
  transfers between devices with their start and end apart: 33, of which 17 were waited for; matrix products, arithmetic and copies ran while one was open for 0% of the time, Pallas kernels for 18%

profile of v8, /device:TPU:0, one launch (start us, length us, event | category | flops | bytes accessed | tf_op | source)
XLA Modules:
  0.0 87.8 jit_solution(7521426847818956547)
XLA Ops:
  2.6 5.9 %collective-permute-start = (bf16[32,384]{1,0:T(8,128)(2,1)S(1)}, bf16[32,384]{1,0:T(8,128)(2,1)S(1)}, u32[]{:S(2)}, u32[]{:S(2)}) collective-permute-start(bf16[32,384]{1,0:T(8,128)(2,1)S(1)} %get-tuple-element.58), channel_id=1, source_target_pairs={{0,2},{1,3},{2,0},{3,1},{4,6},{5,7},{6,4},{7,5},{8,10},{9,11},{10,... | collective-permute-start | bytes 73736 | tf_op jit(solution)/shard_map/ppermute | solution.py:504
  8.5 1.8 %collective-permute-done.refs_1_ = bf16[32,384]{1,0:T(8,128)(2,1)S(1)} collective-permute-done((bf16[32,384]{1,0:T(8,128)(2,1)S(1)}, bf16[32,384]{1,0:T(8,128)(2,1)S(1)}, u32[]{:S(2)}, u32[]{:S(2)}) %collective-permute-start) | collective-permute-done | bytes 24608 | tf_op jit(solution)/shard_map/ppermute | solution.py:504
  10.3 1.9 %front.1 = (bf16[320,128]{1,0:T(8,128)(2,1)S(1)}, bf16[288,384]{1,0:T(8,128)(2,1)S(1)}, bf16[128,768]{1,0:T(8,128)(2,1)S(1)}, f32[128,768]{1,0:T(8,128)S(1)}) custom-call(f32[3,304,128]{2,1,0:T(8,128)S(1)} %get-tuple-element.57.refs_0_, bf16[32,384]{1,0:T(8,128)(2,1)S(1)} %collective-permute-done.refs_1_, ...), custom_call_target="tpu_custom_call" | custom-call | flops 754974720 | bytes 4852736 | tf_op jit(solution)/shard_map/front/pallas_call | solution.py:36
  12.2 4.0 %collective-permute-start.4 = (bf16[320,128]{1,0:T(8,128)(2,1)S(1)}, bf16[320,128]{1,0:T(8,128)(2,1)S(1)}, u32[]{:S(2)}, u32[]{:S(2)}) collective-permute-start(bf16[320,128]{1,0:T(8,128)(2,1)S(1)} %get-tuple-element.61.refs_2_), channel_id=1, source_target_pairs={{0,12},{1,13},{2,14},{3,15},{4,8},{5,9},{6,10},{7,11},{8,4},{9,5},... | collective-permute-start | bytes 245768 | tf_op jit(solution)/shard_map/ppermute | solution.py:504
  16.9 1.8 %collective-permute-start.5 = (bf16[320,128]{1,0:T(8,128)(2,1)S(1)}, bf16[320,128]{1,0:T(8,128)(2,1)S(1)}, u32[]{:S(2)}, u32[]{:S(2)}) collective-permute-start(bf16[320,128]{1,0:T(8,128)(2,1)S(1)} %get-tuple-element.61.refs_2_), channel_id=1, source_target_pairs={{0,2},{1,3},{2,0},{3,1},{4,6},{5,7},{6,4},{7,5},{8,10},{9,11},{10,... | collective-permute-start | bytes 245768 | tf_op jit(solution)/shard_map/ppermute | solution.py:504
  18.7 2.4 %collective-permute-start.8 = (bf16[320,128]{1,0:T(8,128)(2,1)S(1)}, bf16[320,128]{1,0:T(8,128)(2,1)S(1)}, u32[]{:S(2)}, u32[]{:S(2)}) collective-permute-start(bf16[320,128]{1,0:T(8,128)(2,1)S(1)} %collective-permute-done.4.refs_5_), channel_id=1, source_target_pairs={{0,2},{1,3},{2,0},{3,1},{4,6},{5,7},{6,4},{7,5},{8,10},{9,11},{10,... | collective-permute-start | bytes 245768 | tf_op jit(solution)/shard_map/ppermute | solution.py:504
  21.1 1.0 %collective-permute-done.3.refs_4_ = bf16[320,128]{1,0:T(8,128)(2,1)S(1)} collective-permute-done((bf16[320,128]{1,0:T(8,128)(2,1)S(1)}, bf16[320,128]{1,0:T(8,128)(2,1)S(1)}, u32[]{:S(2)}, u32[]{:S(2)}) %collective-permute-start.3) | collective-permute-done | bytes 81952 | tf_op jit(solution)/shard_map/ppermute | solution.py:504
  22.1 1.3 %collective-permute-start.7 = (bf16[320,128]{1,0:T(8,128)(2,1)S(1)}, bf16[320,128]{1,0:T(8,128)(2,1)S(1)}, u32[]{:S(2)}, u32[]{:S(2)}) collective-permute-start(bf16[320,128]{1,0:T(8,128)(2,1)S(1)} %collective-permute-done.3.refs_4_), channel_id=1, source_target_pairs={{0,2},{1,3},{2,0},{3,1},{4,6},{5,7},{6,4},{7,5},{8,10},{9,11},{10,... | collective-permute-start | bytes 245768 | tf_op jit(solution)/shard_map/ppermute | solution.py:504
  24.9 1.7 %collective-permute-done.7.refs_8_ = bf16[320,128]{1,0:T(8,128)(2,1)S(1)} collective-permute-done((bf16[320,128]{1,0:T(8,128)(2,1)S(1)}, bf16[320,128]{1,0:T(8,128)(2,1)S(1)}, u32[]{:S(2)}, u32[]{:S(2)}) %collective-permute-start.7) | collective-permute-done | bytes 81952 | tf_op jit(solution)/shard_map/ppermute | solution.py:504
  26.6 1.2 %collective-permute-done.6.refs_7_ = bf16[320,128]{1,0:T(8,128)(2,1)S(1)} collective-permute-done((bf16[320,128]{1,0:T(8,128)(2,1)S(1)}, bf16[320,128]{1,0:T(8,128)(2,1)S(1)}, u32[]{:S(2)}, u32[]{:S(2)}) %collective-permute-start.6) | collective-permute-done | bytes 81952 | tf_op jit(solution)/shard_map/ppermute | solution.py:504
  28.7 6.5 %attend.1 = (bf16[128,1536]{1,0:T(8,128)(2,1)}, bf16[128,1024]{1,0:T(8,128)(2,1)S(1)}, f32[4,160,128]{2,1,0:T(8,128)S(1)}, bf16[4,160,128]{2,1,0:T(8,128)(2,1)S(...) custom-call(bf16[128,1024]{1,0:T(8,128)(2,1)S(1)} %get-tuple-element.62.refs_0_, ...), custom_call_target="tpu_custom_call" | custom-call | flops 2013265920 | bytes 2949120 | tf_op jit(solution)/shard_map/attend/pallas_call | solution.py:36
  35.3 1.1 %collective-permute-done.10.refs_3_ = bf16[480,384]{1,0:T(8,128)(2,1)S(1)} collective-permute-done((bf16[480,384]{1,0:T(8,128)(2,1)S(1)}, bf16[480,384]{1,0:T(8,128)(2,1)S(1)}, u32[]{:S(2)}, u32[]{:S(2)}) %collective-permute-start.10) | collective-permute-done | bytes 368672 | tf_op jit(solution)/shard_map/ppermute | solution.py:504
  38.1 2.4 %select.1 = (bf16[512,1024]{1,0:T(8,128)(2,1)S(1)}, bf16[192,512]{1,0:T(8,128)(2,1)S(1)}) custom-call(bf16[192,128]{1,0:T(8,128)(2,1)S(1)} %get-tuple-element.64.refs_0_, bf16[480,384]{1,0:T(8,128)(2,1)S(1)} %get-tuple-element.66.refs_1_, bf16[480,384]{1,0:T(8,128)(2,1)S(1)} %collective-permute-done.9.refs_2_, ...), custom_call_target="tpu_custom_call" | custom-call | flops 2013265920 | bytes 2768896 | tf_op jit(solution)/shard_map/select/pallas_call | solution.py:36
  40.5 3.1 %collective-permute-done.13.refs_3_ = bf16[4,160,128]{2,1,0:T(8,128)(2,1)S(1)} collective-permute-done((bf16[4,160,128]{2,1,0:T(8,128)(2,1)S(1)}, bf16[4,160,128]{2,1,0:T(8,128)(2,1)S(1)}, u32[]{:S(2)}, u32[]{:S(2)}) %collective-permute-start.13) | collective-permute-done | bytes 163872 | tf_op jit(solution)/shard_map/ppermute | solution.py:504
  44.1 1.1 %collective-permute-start.15 = (bf16[2,160,128]{2,1,0:T(8,128)(2,1)S(1)}, bf16[2,160,128]{2,1,0:T(8,128)(2,1)S(1)}, u32[]{:S(2)}, u32[]{:S(2)}) collective-permute-start(bf16[2,160,128]{2,1,0:T(8,128)(2,1)S(1)} %get-tuple-element.78), channel_id=1, source_target_pairs={{0,2},{1,3},{2,0},{3,1},{4,6},{5,7},{6,4},{7,5},{8,10},{9,11},{10,... | collective-permute-start | bytes 245768 | tf_op jit(solution)/shard_map/ppermute | solution.py:504
  45.2 2.9 %collective-permute-done.14.refs_1_ = bf16[2,160,128]{2,1,0:T(8,128)(2,1)S(1)} collective-permute-done((bf16[2,160,128]{2,1,0:T(8,128)(2,1)S(1)}, bf16[2,160,128]{2,1,0:T(8,128)(2,1)S(1)}, u32[]{:S(2)}, u32[]{:S(2)}) %collective-permute-start.14) | collective-permute-done | bytes 81952 | tf_op jit(solution)/shard_map/ppermute | solution.py:504
  48.6 1.1 %collective-permute-start.17 = (bf16[128,1024]{1,0:T(8,128)(2,1)S(1)}, bf16[128,1024]{1,0:T(8,128)(2,1)S(1)}, u32[]{:S(2)}, u32[]{:S(2)}) collective-permute-start(bf16[128,1024]{1,0:T(8,128)(2,1)S(1)} %get-tuple-element.80.refs_0_.refs_1_), channel_id=1, source_target_pairs={{0,2},{1,3},{2,0},{3,1},{4,6},{5,7},{6,4},{7,5},{8,10},{9,11},{10,... | collective-permute-start | bytes 786440 | tf_op jit(solution)/shard_map/ppermute | solution.py:504
  49.8 2.9 %collective-permute-start.18 = (bf16[1,320,128]{2,1,0:T(8,128)(2,1)S(1)}, bf16[1,320,128]{2,1,0:T(8,128)(2,1)S(1)}, u32[]{:S(2)}, u32[]{:S(2)}) collective-permute-start(bf16[1,320,128]{2,1,0:T(8,128)(2,1)S(1)} %get-tuple-element.81), channel_id=1, source_target_pairs={{0,8},{1,9},{2,10},{3,11},{4,12},{5,13},{6,14},{7,15},{8,0},{9,1},... | collective-permute-start | bytes 245768 | tf_op jit(solution)/shard_map/ppermute | solution.py:504
  53.4 1.7 %collective-permute-done.18.refs_1_ = bf16[1,320,128]{2,1,0:T(8,128)(2,1)S(1)} collective-permute-done((bf16[1,320,128]{2,1,0:T(8,128)(2,1)S(1)}, bf16[1,320,128]{2,1,0:T(8,128)(2,1)S(1)}, u32[]{:S(2)}, u32[]{:S(2)}) %collective-permute-start.18) | collective-permute-done | bytes 81952 | tf_op jit(solution)/shard_map/ppermute | solution.py:504
  55.6 1.0 %collective-permute-start.24 = (bf16[144,384]{1,0:T(8,128)(2,1)S(1)}, bf16[144,384]{1,0:T(8,128)(2,1)S(1)}, u32[]{:S(2)}, u32[]{:S(2)}) collective-permute-start(bf16[144,384]{1,0:T(8,128)(2,1)S(1)} %get-tuple-element.83.refs_1_), channel_id=1, source_target_pairs={{0,2},{1,3},{2,0},{3,1},{4,6},{5,7},{6,4},{7,5},{8,10},{9,11},{10,... | collective-permute-start | bytes 331784 | tf_op jit(solution)/shard_map/ppermute | solution.py:504
  56.6 1.1 %collective-permute-start.22 = (bf16[256,384]{1,0:T(8,128)(2,1)S(1)}, bf16[256,384]{1,0:T(8,128)(2,1)S(1)}, u32[]{:S(2)}, u32[]{:S(2)}) collective-permute-start(bf16[256,384]{1,0:T(8,128)(2,1)S(1)} %get-tuple-element.89.refs_2_), channel_id=1, source_target_pairs={{0,2},{1,3},{2,0},{3,1},{4,6},{5,7},{6,4},{7,5},{8,10},{9,11},{10,... | collective-permute-start | bytes 589832 | tf_op jit(solution)/shard_map/ppermute | solution.py:504
  58.7 2.9 %collective-permute-done.24.refs_3_ = bf16[144,384]{1,0:T(8,128)(2,1)S(1)} collective-permute-done((bf16[144,384]{1,0:T(8,128)(2,1)S(1)}, bf16[144,384]{1,0:T(8,128)(2,1)S(1)}, u32[]{:S(2)}, u32[]{:S(2)}) %collective-permute-start.24) | collective-permute-done | bytes 110624 | tf_op jit(solution)/shard_map/ppermute | solution.py:504
  62.1 1.7 %collective-permute-start.20 = (bf16[2,48,1024]{2,1,0:T(8,128)(2,1)S(1)}, bf16[2,48,1024]{2,1,0:T(8,128)(2,1)S(1)}, u32[]{:S(2)}, u32[]{:S(2)}) collective-permute-start(bf16[2,48,1024]{2,1,0:T(8,128)(2,1)S(1)} %get-tuple-element.86), channel_id=1, source_target_pairs={{0,4},{1,5},{2,6},{3,7},{4,0},{5,1},{6,2},{7,3},{8,12},{9,13},{10,... | collective-permute-start | bytes 589832 | tf_op jit(solution)/shard_map/ppermute | solution.py:504
  65.3 1.7 %collective-permute-start.28 = (bf16[1,128,384]{2,1,0:T(8,128)(2,1)S(1)}, bf16[1,128,384]{2,1,0:T(8,128)(2,1)S(1)}, u32[]{:S(2)}, u32[]{:S(2)}) collective-permute-start(bf16[1,128,384]{2,1,0:T(8,128)(2,1)S(1)} %get-tuple-element.97), channel_id=1, source_target_pairs={{0,4},{1,5},{2,6},{3,7},{4,0},{5,1},{6,2},{7,3},{8,12},{9,13},{10,... | collective-permute-start | bytes 294920 | tf_op jit(solution)/shard_map/ppermute | solution.py:504
  67.0 2.3 %collective-permute-done.20.refs_1_ = bf16[2,48,1024]{2,1,0:T(8,128)(2,1)S(1)} collective-permute-done((bf16[2,48,1024]{2,1,0:T(8,128)(2,1)S(1)}, bf16[2,48,1024]{2,1,0:T(8,128)(2,1)S(1)}, u32[]{:S(2)}, u32[]{:S(2)}) %collective-permute-start.20) | collective-permute-done | bytes 196640 | tf_op jit(solution)/shard_map/ppermute | solution.py:504
  69.3 1.0 %conv_grad_second.1 = (f32[1,160,384]{2,1,0:T(8,128)S(1)}, f32[1,160,384]{2,1,0:T(8,128)S(1)}, bf16[1,288,384]{2,1,0:T(8,128)(2,1)S(1)}, bf16[1,160,384]{2,1,0:T(8,128)(2,1)S(1)}) custom-call(bf16[512,1024]{1,0:T(8,128)(2,1)S(1)} %get-tuple-element.88.refs_4_.refs_0_, bf16[192,512]{1,0:T(8,128)(2,1)S(1)} %get-tuple-element.70.refs_0_.refs_1_, ...), custom_call_target="tpu_custom_call" | custom-call | flops 402653184 | bytes 2965504 | tf_op jit(solution)/shard_map/conv_grad_second/pallas_call | solution.py:36
  70.3 1.7 %collective-permute-start.27 = (bf16[1,160,384]{2,1,0:T(8,128)(2,1)S(1)}, bf16[1,160,384]{2,1,0:T(8,128)(2,1)S(1)}, u32[]{:S(2)}, u32[]{:S(2)}) collective-permute-start(bf16[1,160,384]{2,1,0:T(8,128)(2,1)S(1)} %get-tuple-element.95), channel_id=1, source_target_pairs={{0,4},{1,5},{2,6},{3,7},{4,0},{5,1},{6,2},{7,3},{8,12},{9,13},{10,... | collective-permute-start | bytes 368648 | tf_op jit(solution)/shard_map/ppermute | solution.py:504
  72.0 2.9 %collective-permute-start.29 = (bf16[1,128,384]{2,1,0:T(8,128)(2,1)S(1)}, bf16[1,128,384]{2,1,0:T(8,128)(2,1)S(1)}, u32[]{:S(2)}, u32[]{:S(2)}) collective-permute-start(bf16[1,128,384]{2,1,0:T(8,128)(2,1)S(1)} %conv_send_on.3), channel_id=1, source_target_pairs={{0,8},{1,9},{2,10},{3,11},{4,12},{5,13},{6,14},{7,15},{8,0},{9,1},... | collective-permute-start | bytes 294920 | tf_op jit(solution)/shard_map/ppermute | solution.py:504
  76.3 2.4 %collective-permute-start.31 = (bf16[1,160,384]{2,1,0:T(8,128)(2,1)S(1)}, bf16[1,160,384]{2,1,0:T(8,128)(2,1)S(1)}, u32[]{:S(2)}, u32[]{:S(2)}) collective-permute-start(bf16[1,160,384]{2,1,0:T(8,128)(2,1)S(1)} %conv_send_on.2), channel_id=1, source_target_pairs={{0,8},{1,9},{2,10},{3,11},{4,12},{5,13},{6,14},{7,15},{8,0},{9,1},... | collective-permute-start | bytes 368648 | tf_op jit(solution)/shard_map/ppermute | solution.py:504
  78.7 2.8 %collective-permute-done.29.refs_6_.refs_2_ = bf16[1,128,384]{2,1,0:T(8,128)(2,1)S(1)} collective-permute-done((bf16[1,128,384]{2,1,0:T(8,128)(2,1)S(1)}, bf16[1,128,384]{2,1,0:T(8,128)(2,1)S(1)}, u32[]{:S(2)}, u32[]{:S(2)}) %collective-permute-start.29) | collective-permute-done | bytes 98336 | tf_op jit(solution)/shard_map/ppermute | solution.py:504
  81.4 2.0 %input_grad.1 = bf16[256,384]{1,0:T(8,128)(2,1)} custom-call(bf16[256,384]{1,0:T(8,128)(2,1)S(1)} %bitcast.10, bf16[144,384]{1,0:T(8,128)(2,1)S(1)} %get-tuple-element.83.refs_1_, bf16[256,384]{1,0:T(8,128)(2,1)S(1)} %get-tuple-element.89.refs_2_, bf16[144,384]{1,0:T(8,128)(2,1)S(1)} %collective-permute-done.24.refs_3_, ...), custom_call_target="tpu_custom_call" | custom-call | flops 7549747200 | bytes 4153344 | tf_op jit(solution)/shard_map/input_grad/pallas_call | solution.py:36
  83.5 3.3 %collective-permute-done.30.refs_1_.refs_2_ = bf16[1,288,384]{2,1,0:T(8,128)(2,1)S(1)} collective-permute-done((bf16[1,288,384]{2,1,0:T(8,128)(2,1)S(1)}, bf16[1,288,384]{2,1,0:T(8,128)(2,1)S(1)}, u32[]{:S(2)}, u32[]{:S(2)}) %collective-permute-start.30) | collective-permute-done | bytes 221216 | tf_op jit(solution)/shard_map/ppermute | solution.py:504
  (69 shorter events, 14.2 us)
Async XLA Ops:
  1.8 6.7 %collective-permute-start.1 = (bf16[32,384]{1,0:T(8,128)(2,1)S(1)}, bf16[32,384]{1,0:T(8,128)(2,1)S(1)}, u32[]{:S(2)}, u32[]{:S(2)}) collective-permute-start(bf16[32,384]{1,0:T(8,128)(2,1)S(1)} %get-tuple-element.58), channel_id=1, source_target_pairs={{2,4},{6,8},{10,12},{4,2},{8,6},{12,10},{3,5},{7,9},{11,13},{5,3},... | collective-permute-start | bytes 73736 | tf_op jit(solution)/shard_map/ppermute | solution.py:535
  2.6 7.7 %collective-permute-start = (bf16[32,384]{1,0:T(8,128)(2,1)S(1)}, bf16[32,384]{1,0:T(8,128)(2,1)S(1)}, u32[]{:S(2)}, u32[]{:S(2)}) collective-permute-start(bf16[32,384]{1,0:T(8,128)(2,1)S(1)} %get-tuple-element.58), channel_id=1, source_target_pairs={{0,2},{1,3},{2,0},{3,1},{4,6},{5,7},{6,4},{7,5},{8,10},{9,11},{10,... | collective-permute-start | bytes 73736 | tf_op jit(solution)/shard_map/ppermute | solution.py:504
  12.2 6.5 %collective-permute-start.4 = (bf16[320,128]{1,0:T(8,128)(2,1)S(1)}, bf16[320,128]{1,0:T(8,128)(2,1)S(1)}, u32[]{:S(2)}, u32[]{:S(2)}) collective-permute-start(bf16[320,128]{1,0:T(8,128)(2,1)S(1)} %get-tuple-element.61.refs_2_), channel_id=1, source_target_pairs={{0,12},{1,13},{2,14},{3,15},{4,8},{5,9},{6,10},{7,11},{8,4},{9,5},... | collective-permute-start | bytes 245768 | tf_op jit(solution)/shard_map/ppermute | solution.py:504
  16.2 5.9 %collective-permute-start.3 = (bf16[320,128]{1,0:T(8,128)(2,1)S(1)}, bf16[320,128]{1,0:T(8,128)(2,1)S(1)}, u32[]{:S(2)}, u32[]{:S(2)}) collective-permute-start(bf16[320,128]{1,0:T(8,128)(2,1)S(1)} %get-tuple-element.61.refs_2_), channel_id=1, source_target_pairs={{0,8},{1,9},{2,10},{3,11},{4,12},{5,13},{6,14},{7,15},{8,0},{9,1},... | collective-permute-start | bytes 245768 | tf_op jit(solution)/shard_map/ppermute | solution.py:504
  16.2 7.2 %collective-permute-start.2 = (bf16[320,128]{1,0:T(8,128)(2,1)S(1)}, bf16[320,128]{1,0:T(8,128)(2,1)S(1)}, u32[]{:S(2)}, u32[]{:S(2)}) collective-permute-start(bf16[320,128]{1,0:T(8,128)(2,1)S(1)} %get-tuple-element.61.refs_2_), channel_id=1, source_target_pairs={{0,4},{1,5},{2,6},{3,7},{4,0},{5,1},{6,2},{7,3},{8,12},{9,13},{10,... | collective-permute-start | bytes 245768 | tf_op jit(solution)/shard_map/ppermute | solution.py:504
  16.9 8.0 %collective-permute-start.5 = (bf16[320,128]{1,0:T(8,128)(2,1)S(1)}, bf16[320,128]{1,0:T(8,128)(2,1)S(1)}, u32[]{:S(2)}, u32[]{:S(2)}) collective-permute-start(bf16[320,128]{1,0:T(8,128)(2,1)S(1)} %get-tuple-element.61.refs_2_), channel_id=1, source_target_pairs={{0,2},{1,3},{2,0},{3,1},{4,6},{5,7},{6,4},{7,5},{8,10},{9,11},{10,... | collective-permute-start | bytes 245768 | tf_op jit(solution)/shard_map/ppermute | solution.py:504
  18.7 6.2 %collective-permute-start.8 = (bf16[320,128]{1,0:T(8,128)(2,1)S(1)}, bf16[320,128]{1,0:T(8,128)(2,1)S(1)}, u32[]{:S(2)}, u32[]{:S(2)}) collective-permute-start(bf16[320,128]{1,0:T(8,128)(2,1)S(1)} %collective-permute-done.4.refs_5_), channel_id=1, source_target_pairs={{0,2},{1,3},{2,0},{3,1},{4,6},{5,7},{6,4},{7,5},{8,10},{9,11},{10,... | collective-permute-start | bytes 245768 | tf_op jit(solution)/shard_map/ppermute | solution.py:504
  22.1 4.5 %collective-permute-start.7 = (bf16[320,128]{1,0:T(8,128)(2,1)S(1)}, bf16[320,128]{1,0:T(8,128)(2,1)S(1)}, u32[]{:S(2)}, u32[]{:S(2)}) collective-permute-start(bf16[320,128]{1,0:T(8,128)(2,1)S(1)} %collective-permute-done.3.refs_4_), channel_id=1, source_target_pairs={{0,2},{1,3},{2,0},{3,1},{4,6},{5,7},{6,4},{7,5},{8,10},{9,11},{10,... | collective-permute-start | bytes 245768 | tf_op jit(solution)/shard_map/ppermute | solution.py:504
  23.4 4.4 %collective-permute-start.6 = (bf16[320,128]{1,0:T(8,128)(2,1)S(1)}, bf16[320,128]{1,0:T(8,128)(2,1)S(1)}, u32[]{:S(2)}, u32[]{:S(2)}) collective-permute-start(bf16[320,128]{1,0:T(8,128)(2,1)S(1)} %collective-permute-done.2.refs_3_), channel_id=1, source_target_pairs={{0,2},{1,3},{2,0},{3,1},{4,6},{5,7},{6,4},{7,5},{8,10},{9,11},{10,... | collective-permute-start | bytes 245768 | tf_op jit(solution)/shard_map/ppermute | solution.py:504
  27.9 8.5 %collective-permute-start.10 = (bf16[480,384]{1,0:T(8,128)(2,1)S(1)}, bf16[480,384]{1,0:T(8,128)(2,1)S(1)}, u32[]{:S(2)}, u32[]{:S(2)}) collective-permute-start(bf16[480,384]{1,0:T(8,128)(2,1)S(1)} %get-tuple-element.66.refs_1_), channel_id=1, source_target_pairs={{0,2},{1,3},{2,0},{3,1},{4,6},{5,7},{6,4},{7,5},{8,10},{9,11},{10,... | collective-permute-start | bytes 1105928 | tf_op jit(solution)/shard_map/ppermute | solution.py:504
  28.7 9.0 %collective-permute-start.9 = (bf16[480,384]{1,0:T(8,128)(2,1)S(1)}, bf16[480,384]{1,0:T(8,128)(2,1)S(1)}, u32[]{:S(2)}, u32[]{:S(2)}) collective-permute-start(bf16[480,384]{1,0:T(8,128)(2,1)S(1)} %get-tuple-element.66.refs_1_), channel_id=1, source_target_pairs={{0,1},{1,0},{2,3},{3,2},{4,5},{5,4},{6,7},{7,6},{8,9},{9,8},{10,11... | collective-permute-start | bytes 1105928 | tf_op jit(solution)/shard_map/ppermute | solution.py:504
  36.4 7.2 %collective-permute-start.12 = (bf16[4,160,128]{2,1,0:T(8,128)(2,1)S(1)}, bf16[4,160,128]{2,1,0:T(8,128)(2,1)S(1)}, u32[]{:S(2)}, u32[]{:S(2)}) collective-permute-start(bf16[4,160,128]{2,1,0:T(8,128)(2,1)S(1)} %get-tuple-element.67), channel_id=1, source_target_pairs={{0,2},{1,3},{2,0},{3,1},{4,6},{5,7},{6,4},{7,5},{8,10},{9,11},{10,... | collective-permute-start | bytes 491528 | tf_op jit(solution)/shard_map/ppermute | solution.py:504
  37.2 6.3 %collective-permute-start.13 = (bf16[4,160,128]{2,1,0:T(8,128)(2,1)S(1)}, bf16[4,160,128]{2,1,0:T(8,128)(2,1)S(1)}, u32[]{:S(2)}, u32[]{:S(2)}) collective-permute-start(bf16[4,160,128]{2,1,0:T(8,128)(2,1)S(1)} %get-tuple-element.74), channel_id=1, source_target_pairs={{0,4},{1,5},{2,6},{3,7},{4,0},{5,1},{6,2},{7,3},{8,12},{9,13},{10,... | collective-permute-start | bytes 491528 | tf_op jit(solution)/shard_map/ppermute | solution.py:504
  43.6 4.5 %collective-permute-start.14 = (bf16[2,160,128]{2,1,0:T(8,128)(2,1)S(1)}, bf16[2,160,128]{2,1,0:T(8,128)(2,1)S(1)}, u32[]{:S(2)}, u32[]{:S(2)}) collective-permute-start(bf16[2,160,128]{2,1,0:T(8,128)(2,1)S(1)} %get-tuple-element.76), channel_id=1, source_target_pairs={{0,4},{1,5},{2,6},{3,7},{4,0},{5,1},{6,2},{7,3},{8,12},{9,13},{10,... | collective-permute-start | bytes 245768 | tf_op jit(solution)/shard_map/ppermute | solution.py:504
  44.1 4.4 %collective-permute-start.15 = (bf16[2,160,128]{2,1,0:T(8,128)(2,1)S(1)}, bf16[2,160,128]{2,1,0:T(8,128)(2,1)S(1)}, u32[]{:S(2)}, u32[]{:S(2)}) collective-permute-start(bf16[2,160,128]{2,1,0:T(8,128)(2,1)S(1)} %get-tuple-element.78), channel_id=1, source_target_pairs={{0,2},{1,3},{2,0},{3,1},{4,6},{5,7},{6,4},{7,5},{8,10},{9,11},{10,... | collective-permute-start | bytes 245768 | tf_op jit(solution)/shard_map/ppermute | solution.py:504
  48.6 6.9 %collective-permute-start.17 = (bf16[128,1024]{1,0:T(8,128)(2,1)S(1)}, bf16[128,1024]{1,0:T(8,128)(2,1)S(1)}, u32[]{:S(2)}, u32[]{:S(2)}) collective-permute-start(bf16[128,1024]{1,0:T(8,128)(2,1)S(1)} %get-tuple-element.80.refs_0_.refs_1_), channel_id=1, source_target_pairs={{0,2},{1,3},{2,0},{3,1},{4,6},{5,7},{6,4},{7,5},{8,10},{9,11},{10,... | collective-permute-start | bytes 786440 | tf_op jit(solution)/shard_map/ppermute | solution.py:504
  49.8 5.4 %collective-permute-start.18 = (bf16[1,320,128]{2,1,0:T(8,128)(2,1)S(1)}, bf16[1,320,128]{2,1,0:T(8,128)(2,1)S(1)}, u32[]{:S(2)}, u32[]{:S(2)}) collective-permute-start(bf16[1,320,128]{2,1,0:T(8,128)(2,1)S(1)} %get-tuple-element.81), channel_id=1, source_target_pairs={{0,8},{1,9},{2,10},{3,11},{4,12},{5,13},{6,14},{7,15},{8,0},{9,1},... | collective-permute-start | bytes 245768 | tf_op jit(solution)/shard_map/ppermute | solution.py:504
  53.3 4.4 %collective-permute-start.16 = (bf16[128,1024]{1,0:T(8,128)(2,1)S(1)}, bf16[128,1024]{1,0:T(8,128)(2,1)S(1)}, u32[]{:S(2)}, u32[]{:S(2)}) collective-permute-start(bf16[128,1024]{1,0:T(8,128)(2,1)S(1)} %get-tuple-element.80.refs_0_.refs_1_), channel_id=1, source_target_pairs={{0,1},{1,0},{2,3},{3,2},{4,5},{5,4},{6,7},{7,6},{8,9},{9,8},{10,11... | collective-permute-start | bytes 786440 | tf_op jit(solution)/shard_map/ppermute | solution.py:504
  55.6 2.2 %collective-permute-start.19 = (bf16[128,1024]{1,0:T(8,128)(2,1)S(1)}, bf16[128,1024]{1,0:T(8,128)(2,1)S(1)}, u32[]{:S(2)}, u32[]{:S(2)}) collective-permute-start(bf16[128,1024]{1,0:T(8,128)(2,1)S(1)} %collective-permute-done.17.refs_3_), channel_id=1, source_target_pairs={{0,1},{1,0},{2,3},{3,2},{4,5},{5,4},{6,7},{7,6},{8,9},{9,8},{10,11... | collective-permute-start | bytes 786440 | tf_op jit(solution)/shard_map/ppermute | solution.py:504
  55.6 5.9 %collective-permute-start.24 = (bf16[144,384]{1,0:T(8,128)(2,1)S(1)}, bf16[144,384]{1,0:T(8,128)(2,1)S(1)}, u32[]{:S(2)}, u32[]{:S(2)}) collective-permute-start(bf16[144,384]{1,0:T(8,128)(2,1)S(1)} %get-tuple-element.83.refs_1_), channel_id=1, source_target_pairs={{0,2},{1,3},{2,0},{3,1},{4,6},{5,7},{6,4},{7,5},{8,10},{9,11},{10,... | collective-permute-start | bytes 331784 | tf_op jit(solution)/shard_map/ppermute | solution.py:504
  56.6 8.7 %collective-permute-start.22 = (bf16[256,384]{1,0:T(8,128)(2,1)S(1)}, bf16[256,384]{1,0:T(8,128)(2,1)S(1)}, u32[]{:S(2)}, u32[]{:S(2)}) collective-permute-start(bf16[256,384]{1,0:T(8,128)(2,1)S(1)} %get-tuple-element.89.refs_2_), channel_id=1, source_target_pairs={{0,2},{1,3},{2,0},{3,1},{4,6},{5,7},{6,4},{7,5},{8,10},{9,11},{10,... | collective-permute-start | bytes 589832 | tf_op jit(solution)/shard_map/ppermute | solution.py:504
  57.7 6.0 %collective-permute-start.23 = (bf16[144,384]{1,0:T(8,128)(2,1)S(1)}, bf16[144,384]{1,0:T(8,128)(2,1)S(1)}, u32[]{:S(2)}, u32[]{:S(2)}) collective-permute-start(bf16[144,384]{1,0:T(8,128)(2,1)S(1)} %get-tuple-element.83.refs_1_), channel_id=1, source_target_pairs={{0,1},{1,0},{2,3},{3,2},{4,5},{5,4},{6,7},{7,6},{8,9},{9,8},{10,11... | collective-permute-start | bytes 331784 | tf_op jit(solution)/shard_map/ppermute | solution.py:504
  61.6 2.2 %collective-permute-start.25 = (bf16[144,384]{1,0:T(8,128)(2,1)S(1)}, bf16[144,384]{1,0:T(8,128)(2,1)S(1)}, u32[]{:S(2)}, u32[]{:S(2)}) collective-permute-start(bf16[144,384]{1,0:T(8,128)(2,1)S(1)} %collective-permute-done.24.refs_3_), channel_id=1, source_target_pairs={{0,1},{1,0},{2,3},{3,2},{4,5},{5,4},{6,7},{7,6},{8,9},{9,8},{10,11... | collective-permute-start | bytes 331784 | tf_op jit(solution)/shard_map/ppermute | solution.py:504
  61.6 7.7 %collective-permute-start.21 = (bf16[256,384]{1,0:T(8,128)(2,1)S(1)}, bf16[256,384]{1,0:T(8,128)(2,1)S(1)}, u32[]{:S(2)}, u32[]{:S(2)}) collective-permute-start(bf16[256,384]{1,0:T(8,128)(2,1)S(1)} %get-tuple-element.89.refs_2_), channel_id=1, source_target_pairs={{0,1},{1,0},{2,3},{3,2},{4,5},{5,4},{6,7},{7,6},{8,9},{9,8},{10,11... | collective-permute-start | bytes 589832 | tf_op jit(solution)/shard_map/ppermute | solution.py:504
  62.1 7.2 %collective-permute-start.20 = (bf16[2,48,1024]{2,1,0:T(8,128)(2,1)S(1)}, bf16[2,48,1024]{2,1,0:T(8,128)(2,1)S(1)}, u32[]{:S(2)}, u32[]{:S(2)}) collective-permute-start(bf16[2,48,1024]{2,1,0:T(8,128)(2,1)S(1)} %get-tuple-element.86), channel_id=1, source_target_pairs={{0,4},{1,5},{2,6},{3,7},{4,0},{5,1},{6,2},{7,3},{8,12},{9,13},{10,... | collective-permute-start | bytes 589832 | tf_op jit(solution)/shard_map/ppermute | solution.py:504
  65.3 4.0 %collective-permute-start.26 = (bf16[256,384]{1,0:T(8,128)(2,1)S(1)}, bf16[256,384]{1,0:T(8,128)(2,1)S(1)}, u32[]{:S(2)}, u32[]{:S(2)}) collective-permute-start(bf16[256,384]{1,0:T(8,128)(2,1)S(1)} %collective-permute-done.22.refs_4_), channel_id=1, source_target_pairs={{0,1},{1,0},{2,3},{3,2},{4,5},{5,4},{6,7},{7,6},{8,9},{9,8},{10,11... | collective-permute-start | bytes 589832 | tf_op jit(solution)/shard_map/ppermute | solution.py:504
  65.3 6.7 %collective-permute-start.28 = (bf16[1,128,384]{2,1,0:T(8,128)(2,1)S(1)}, bf16[1,128,384]{2,1,0:T(8,128)(2,1)S(1)}, u32[]{:S(2)}, u32[]{:S(2)}) collective-permute-start(bf16[1,128,384]{2,1,0:T(8,128)(2,1)S(1)} %get-tuple-element.97), channel_id=1, source_target_pairs={{0,4},{1,5},{2,6},{3,7},{4,0},{5,1},{6,2},{7,3},{8,12},{9,13},{10,... | collective-permute-start | bytes 294920 | tf_op jit(solution)/shard_map/ppermute | solution.py:504
  70.3 5.9 %collective-permute-start.27 = (bf16[1,160,384]{2,1,0:T(8,128)(2,1)S(1)}, bf16[1,160,384]{2,1,0:T(8,128)(2,1)S(1)}, u32[]{:S(2)}, u32[]{:S(2)}) collective-permute-start(bf16[1,160,384]{2,1,0:T(8,128)(2,1)S(1)} %get-tuple-element.95), channel_id=1, source_target_pairs={{0,4},{1,5},{2,6},{3,7},{4,0},{5,1},{6,2},{7,3},{8,12},{9,13},{10,... | collective-permute-start | bytes 368648 | tf_op jit(solution)/shard_map/ppermute | solution.py:504
  72.0 9.4 %collective-permute-start.29 = (bf16[1,128,384]{2,1,0:T(8,128)(2,1)S(1)}, bf16[1,128,384]{2,1,0:T(8,128)(2,1)S(1)}, u32[]{:S(2)}, u32[]{:S(2)}) collective-permute-start(bf16[1,128,384]{2,1,0:T(8,128)(2,1)S(1)} %conv_send_on.3), channel_id=1, source_target_pairs={{0,8},{1,9},{2,10},{3,11},{4,12},{5,13},{6,14},{7,15},{8,0},{9,1},... | collective-permute-start | bytes 294920 | tf_op jit(solution)/shard_map/ppermute | solution.py:504
  75.0 11.9 %collective-permute-start.32 = (bf16[1,48,1024]{2,1,0:T(8,128)(2,1)S(1)}, bf16[1,48,1024]{2,1,0:T(8,128)(2,1)S(1)}, u32[]{:S(2)}, u32[]{:S(2)}) collective-permute-start(bf16[1,48,1024]{2,1,0:T(8,128)(2,1)S(1)} %get-tuple-element.101), channel_id=1, source_target_pairs={{0,8},{1,9},{2,10},{3,11},{4,12},{5,13},{6,14},{7,15},{8,0},{9,1},... | collective-permute-start | bytes 294920 | tf_op jit(solution)/shard_map/ppermute | solution.py:504
  75.1 11.8 %collective-permute-start.30 = (bf16[1,288,384]{2,1,0:T(8,128)(2,1)S(1)}, bf16[1,288,384]{2,1,0:T(8,128)(2,1)S(1)}, u32[]{:S(2)}, u32[]{:S(2)}) collective-permute-start(bf16[1,288,384]{2,1,0:T(8,128)(2,1)S(1)} %get-tuple-element.99), channel_id=1, source_target_pairs={{0,4},{1,5},{2,6},{3,7},{4,0},{5,1},{6,2},{7,3},{8,12},{9,13},{10,... | collective-permute-start | bytes 663560 | tf_op jit(solution)/shard_map/ppermute | solution.py:504
  76.3 10.6 %collective-permute-start.31 = (bf16[1,160,384]{2,1,0:T(8,128)(2,1)S(1)}, bf16[1,160,384]{2,1,0:T(8,128)(2,1)S(1)}, u32[]{:S(2)}, u32[]{:S(2)}) collective-permute-start(bf16[1,160,384]{2,1,0:T(8,128)(2,1)S(1)} %conv_send_on.2), channel_id=1, source_target_pairs={{0,8},{1,9},{2,10},{3,11},{4,12},{5,13},{6,14},{7,15},{8,0},{9,1},... | collective-permute-start | bytes 368648 | tf_op jit(solution)/shard_map/ppermute | solution.py:504
  (9 other events, 100.2 us)

commit v9 on v8

--- a/solution.py
+++ b/solution.py
@@ -1,3 +1,4 @@
+import functools
 import math
 
 import jax
@@ -152,11 +153,15 @@
         at += step
 
 
+def by_eight(rows):
+    return rows.reshape(rows.shape[0] // 8, 8, rows.shape[1])
+
+
 def attend_kernel(*refs, blocks, masks, heads, key_size, value_size, scale):
     q, cot = refs[:2]
     parts = refs[2 : 2 + blocks]
     att, dq, keep_a, send_a, keep_b, send_b = refs[2 + blocks : 8 + blocks]
-    ks, vs, kt, vt, qs, cs, weights, score_cots = refs[8 + blocks :]
+    ks, vs, kt, vt, qs, cs, weights, score_cots, scores, prob_cots = refs[8 + blocks :]
     tokens = q.shape[0]
     half = tokens // 2
     wide = value_size - key_size
@@ -176,23 +181,36 @@
             [q[:, ql : ql + key_size], q[:, ql + key_size : ql + 2 * key_size]], axis=0
         )
         cs[rows] = jnp.concatenate([both[:, :value_size], both[:, value_size:]], axis=0)
-        scores = dot_t(ks[...], qs[rows])
-        raised = jnp.exp(scores - jnp.max(scores, axis=0, keepdims=True))
-        probs = raised * (1.0 / jnp.sum(raised, axis=0, keepdims=True))
-        weights[:, rows] = probs.astype(BF)
+        slot = pair % scores.shape[0]
+        parts_of = [slice(i * tokens, (i + 1) * tokens) for i in range(blocks)]
+        scores[slot] = dot_t(ks[...], qs[rows])
+        prob_cots[slot] = dot_t(vs[...], cs[rows])
+        top = functools.reduce(jnp.maximum, [by_eight(scores[slot, at]).max(0) for at in parts_of])
+        top = jnp.max(top, axis=0, keepdims=True)
+        sums = 0.0
+        for at in parts_of:
+            raised = jnp.exp(scores[slot, at] - top)
+            sums = sums + by_eight(raised).sum(0)
+            scores[slot, at] = raised
+        inverse = 1.0 / jnp.sum(sums, axis=0, keepdims=True)
+        for at in parts_of:
+            weights[at, rows] = (scores[slot, at] * inverse).astype(BF)
         out_t = dot(vt[...], weights[:, rows]).astype(BF).astype(F32)
         delta = jnp.sum(cs[rows].astype(F32).T * out_t, axis=0, keepdims=True)
-        score_cots[:, rows] = (probs * (dot_t(vs[...], cs[rows]) - delta)).astype(BF)
+        for at in parts_of:
+            probs = scores[slot, at] * inverse
+            score_cots[at, rows] = (probs * (prob_cots[slot, at] - delta)).astype(BF)
         dq_t = dot(kt[...], score_cots[:, rows]) * scale
         out_rows = jnp.concatenate([out_t[:, :tokens].T, out_t[:, tokens:].T], axis=1)
         att[:, cl : cl + 2 * value_size] = out_rows.astype(BF)
         dq_rows = jnp.concatenate([dq_t[:, :tokens].T, dq_t[:, tokens:].T], axis=1)
         dq[:, ql : ql + 2 * key_size] = dq_rows.astype(BF)
+    key_cots, value_cots = dot(score_cots[...], qs[...]), dot(weights[...], cs[...])
     edge = keep_a.shape[1]
     count = blocks // 2
     for i in range(blocks):
         at = slice(i * tokens, (i + 1) * tokens)
-        packed = pack_kv(dot(score_cots[at], qs[...]), dot(weights[at], cs[...]))
+        packed = pack_kv(key_cots[at], value_cots[at])
         for order, keep, send, part in (
             (masks[0], keep_a, send_a, packed[:edge]),
             (masks[1], keep_b, send_b, packed[edge:]),
@@ -385,8 +403,8 @@
 
 
 def conv_second_kernel(*refs, conv_rows, conv_pad, norm_rows, norm_pad, key_size, value_size):
-    pick, norm_pick, blocks, first_send = refs[0], refs[1], refs[2:6], refs[6]
-    near_keep, far_keep, near_send, far_send, right, side, stage = refs[7:]
+    pick, norm_pick, blocks, outs = refs[0], refs[1], refs[2:6], refs[6:10]
+    right, side, stage = refs[10:]
     tokens, width = right.shape[0] // 8, right.shape[1]
     stack_cots(blocks, right, tokens)
     for i, block in enumerate(blocks):
@@ -394,8 +412,7 @@
     key_rows = side_rows(norm_rows, key_size, width)
     value_rows = side_rows(norm_rows, value_size, width)
     stage[...] = jnp.zeros(stage.shape, F32)
-    count, above = first_send.shape[:2]
-    near_send[:, :above] = first_send[...]
+    count = outs[0].shape[0]
     for k in range(4 * count):
         conv = dot(pick[k * conv_pad : (k + 1) * conv_pad], right[...])
         stage[:conv_rows] = conv[:conv_rows]
@@ -403,23 +420,18 @@
         put_side(stage, conv_rows, both[:norm_rows, :key_size], key_rows)
         value = both[:norm_rows, key_size : key_size + value_size]
         put_side(stage, conv_rows + key_rows, value, value_rows)
-        if k < 2 * count:
-            (near_keep, far_keep)[k // count][k % count] = stage[...]
-        elif k < 3 * count:
-            near_send[k % count, above:] = stage[...].astype(BF)
-        else:
-            far_send[k % count] = stage[...].astype(BF)
+        out = outs[k // count]
+        out[k % count] = stage[...].astype(out.dtype)
 
 
 def first_sum_kernel(keep, near, far, out):
-    above = keep.shape[1]
-    out[...] = keep[...] + near[:, :above].astype(F32) + far[...].astype(F32)
+    out[...] = total_of((keep, near, far))
 
 
 def combine_kernel(first, second, near, far, out):
     above = first.shape[1]
     out[:, :above] = first[...]
-    out[:, above:] = second[...] + near[:, above:].astype(F32) + far[...].astype(F32)
+    out[:, above:] = total_of((second, near, far))
 
 
 def final_kernel(*refs, conv_parts, above):
@@ -565,6 +577,7 @@
     length = devices * tokens
     masks = [2 * k for k in range(groups)] + [2 * k + 1 for k in range(groups)]
     half_block = (groups, 5 * tokens // 4, key_size)
+    slots = 2 if length <= 2048 else 1
     attended, query_cot, keep_a, send_a, keep_b, send_b = run(
         lambda *refs: attend_kernel(
             *refs,
@@ -589,6 +602,8 @@
             pltpu.VMEM((heads * tokens, value_size), BF),
             pltpu.VMEM((length, heads * tokens), BF),
             pltpu.VMEM((length, heads * tokens), BF),
+            pltpu.VMEM((slots, length, 2 * tokens), F32),
+            pltpu.VMEM((slots, length, 2 * tokens), F32),
         ],
         flops=6 * tokens * heads * length * (key_size + value_size),
         name="attend",
@@ -661,14 +676,14 @@
     near_keep, far_keep, near_send, far_send = run(
         lambda *refs: conv_first_kernel(*refs, conv_rows=conv_rows, conv_pad=conv_pad),
         [((count, above, split), t) for t in (F32, F32, BF, BF)],
-        [conv_pick, first, core_first, near_first, last_first],
+        [held(conv_pick, query_parts[0]), first, core_first, near_first, last_first],
         [pltpu.VMEM((8 * tokens, split), BF), pltpu.VMEM((above, split), F32)],
         flops=groups * conv_pad * 8 * tokens * width,
         name="conv_grad_first",
     )
-    far_in = swap(far_send, 2)
+    far_in, near_in = swap(far_send, 2), swap(held(near_send, query_parts[1]), 2)
     last_second = swap(held(near_second, near_keep), 0, 1)
-    near_keep_second, far_keep_second, near_send, far_send = run(
+    near_keep_second, far_keep_second, near_send_second, far_send_second = run(
         lambda *refs: conv_second_kernel(
             *refs,
             conv_rows=conv_rows,
@@ -681,10 +696,10 @@
         [
             ((count, below, split), F32),
             ((count, below, split), F32),
-            ((count, above + below, split), BF),
+            ((count, below, split), BF),
             ((count, below, split), BF),
         ],
-        [held(conv_pick, query_parts[0]), norm_pick, second, core_second, near_second, last_second, near_send],
+        [conv_pick, norm_pick, second, core_second, near_second, last_second],
         [
             pltpu.VMEM((8 * tokens, split), BF),
             pltpu.VMEM((4 * tokens, split), BF),
@@ -693,8 +708,7 @@
         flops=groups * conv_pad * 8 * tokens * width,
         name="conv_grad_second",
     )
-    far_in_second = swap(far_send, 2)
-    near_in = swap(near_send, 2)
+    far_in_second, near_in_second = swap(far_send_second, 2), swap(near_send_second, 2)
     (far_sum,) = run(
         send_on_kernel,
         [((count, above, split), BF)],
@@ -727,11 +741,11 @@
     (first_sum,) = run(
         first_sum_kernel,
         [((count, above, split), F32)],
-        [near_keep, near_in, far_last],
+        [held(near_keep, input_grad), near_in, far_last],
         flops=5 * 10**9,
         name="conv_first_sum",
     )
-    conv_parts = [first_sum, near_keep_second, near_in, swap(far_sum, 4)]
+    conv_parts = [first_sum, near_keep_second, near_in_second, swap(far_sum, 4)]
     chunk = (count, above + below, split)
     if len(bits) > 3:
         keep = run(combine_kernel, [(chunk, F32)], conv_parts, name="conv_combine")[0]

time: 88 us -> 89.7 us (1.019)
  starting transfers between devices: 39.2 us -> 45.1 us
  waiting for transfers between devices: 28.1 us -> 24.1 us
    ppermute x32 -> x33, starting transfers between devices: 38.5 us -> 44.3 us  [swap(): lax.ppermute(value, both_axes, [(i, i ^ mask) for i in range(owners)])]
    ppermute x32 -> x33, waiting for transfers between devices: 28.1 us -> 24.1 us  [swap(): lax.ppermute(value, both_axes, [(i, i ^ mask) for i in range(owners)])]
  transfers between devices with their start and end apart: 33 -> 34, of which waited for: 17 -> 17; matrix products, arithmetic and copies ran while one was open for 0% -> 0% of each run, Pallas kernels for 18% -> 17%
where the time goes in v9:
time: 89.7 us; the launch traced here: 89.6 us
  starting transfers between devices  45.1 us (50%)
  waiting for transfers between devices  24.1 us (27%)
  Pallas kernels  18.6 us (21%)
  local copies, waits for them, and re-layouts  0.96 us (1%)
    ppermute x33, starting transfers between devices, swap(): lax.ppermute(value, both_axes, [(i, i ^ mask) for i in range(owners)])  44.3 us
    ppermute x33, waiting for transfers between devices, swap(): lax.ppermute(value, both_axes, [(i, i ^ mask) for i in range(owners)])  24.1 us
    pallas_call x18, Pallas kernels, run(): pl.pallas_call(whole, out_shape=[jax.ShapeDtypeStruct(s, t) for s, t in o...  18.6 us
  transfers between devices with their start and end apart: 34, of which 17 were waited for; matrix products, arithmetic and copies ran while one was open for 0% of the time, Pallas kernels for 17%

profile of v9, /device:TPU:0, one launch (start us, length us, event | category | flops | bytes accessed | tf_op | source)
XLA Modules:
  0.0 89.6 jit_solution(10364387895783409349)
XLA Ops:
  2.6 5.9 %collective-permute-start = (bf16[32,384]{1,0:T(8,128)(2,1)S(1)}, bf16[32,384]{1,0:T(8,128)(2,1)S(1)}, u32[]{:S(2)}, u32[]{:S(2)}) collective-permute-start(bf16[32,384]{1,0:T(8,128)(2,1)S(1)} %get-tuple-element.60), channel_id=1, source_target_pairs={{0,2},{1,3},{2,0},{3,1},{4,6},{5,7},{6,4},{7,5},{8,10},{9,11},{10,... | collective-permute-start | bytes 73736 | tf_op jit(solution)/shard_map/ppermute | solution.py:516
  8.5 1.8 %collective-permute-done.refs_1_ = bf16[32,384]{1,0:T(8,128)(2,1)S(1)} collective-permute-done((bf16[32,384]{1,0:T(8,128)(2,1)S(1)}, bf16[32,384]{1,0:T(8,128)(2,1)S(1)}, u32[]{:S(2)}, u32[]{:S(2)}) %collective-permute-start) | collective-permute-done | bytes 24608 | tf_op jit(solution)/shard_map/ppermute | solution.py:516
  10.3 1.9 %front.1 = (bf16[320,128]{1,0:T(8,128)(2,1)S(1)}, bf16[288,384]{1,0:T(8,128)(2,1)S(1)}, bf16[128,768]{1,0:T(8,128)(2,1)S(1)}, f32[128,768]{1,0:T(8,128)S(1)}) custom-call(f32[3,304,128]{2,1,0:T(8,128)S(1)} %get-tuple-element.59.refs_0_, bf16[32,384]{1,0:T(8,128)(2,1)S(1)} %collective-permute-done.refs_1_, ...), custom_call_target="tpu_custom_call" | custom-call | flops 754974720 | bytes 4852736 | tf_op jit(solution)/shard_map/front/pallas_call | solution.py:37
  12.2 4.0 %collective-permute-start.4 = (bf16[320,128]{1,0:T(8,128)(2,1)S(1)}, bf16[320,128]{1,0:T(8,128)(2,1)S(1)}, u32[]{:S(2)}, u32[]{:S(2)}) collective-permute-start(bf16[320,128]{1,0:T(8,128)(2,1)S(1)} %get-tuple-element.63.refs_2_), channel_id=1, source_target_pairs={{0,12},{1,13},{2,14},{3,15},{4,8},{5,9},{6,10},{7,11},{8,4},{9,5},... | collective-permute-start | bytes 245768 | tf_op jit(solution)/shard_map/ppermute | solution.py:516
  16.9 1.8 %collective-permute-start.5 = (bf16[320,128]{1,0:T(8,128)(2,1)S(1)}, bf16[320,128]{1,0:T(8,128)(2,1)S(1)}, u32[]{:S(2)}, u32[]{:S(2)}) collective-permute-start(bf16[320,128]{1,0:T(8,128)(2,1)S(1)} %get-tuple-element.63.refs_2_), channel_id=1, source_target_pairs={{0,2},{1,3},{2,0},{3,1},{4,6},{5,7},{6,4},{7,5},{8,10},{9,11},{10,... | collective-permute-start | bytes 245768 | tf_op jit(solution)/shard_map/ppermute | solution.py:516
  18.7 2.4 %collective-permute-start.8 = (bf16[320,128]{1,0:T(8,128)(2,1)S(1)}, bf16[320,128]{1,0:T(8,128)(2,1)S(1)}, u32[]{:S(2)}, u32[]{:S(2)}) collective-permute-start(bf16[320,128]{1,0:T(8,128)(2,1)S(1)} %collective-permute-done.4.refs_5_), channel_id=1, source_target_pairs={{0,2},{1,3},{2,0},{3,1},{4,6},{5,7},{6,4},{7,5},{8,10},{9,11},{10,... | collective-permute-start | bytes 245768 | tf_op jit(solution)/shard_map/ppermute | solution.py:516
  21.1 1.0 %collective-permute-done.3.refs_4_ = bf16[320,128]{1,0:T(8,128)(2,1)S(1)} collective-permute-done((bf16[320,128]{1,0:T(8,128)(2,1)S(1)}, bf16[320,128]{1,0:T(8,128)(2,1)S(1)}, u32[]{:S(2)}, u32[]{:S(2)}) %collective-permute-start.3) | collective-permute-done | bytes 81952 | tf_op jit(solution)/shard_map/ppermute | solution.py:516
  22.1 1.3 %collective-permute-start.7 = (bf16[320,128]{1,0:T(8,128)(2,1)S(1)}, bf16[320,128]{1,0:T(8,128)(2,1)S(1)}, u32[]{:S(2)}, u32[]{:S(2)}) collective-permute-start(bf16[320,128]{1,0:T(8,128)(2,1)S(1)} %collective-permute-done.3.refs_4_), channel_id=1, source_target_pairs={{0,2},{1,3},{2,0},{3,1},{4,6},{5,7},{6,4},{7,5},{8,10},{9,11},{10,... | collective-permute-start | bytes 245768 | tf_op jit(solution)/shard_map/ppermute | solution.py:516
  24.9 1.7 %collective-permute-done.7.refs_8_ = bf16[320,128]{1,0:T(8,128)(2,1)S(1)} collective-permute-done((bf16[320,128]{1,0:T(8,128)(2,1)S(1)}, bf16[320,128]{1,0:T(8,128)(2,1)S(1)}, u32[]{:S(2)}, u32[]{:S(2)}) %collective-permute-start.7) | collective-permute-done | bytes 81952 | tf_op jit(solution)/shard_map/ppermute | solution.py:516
  26.6 1.2 %collective-permute-done.6.refs_7_ = bf16[320,128]{1,0:T(8,128)(2,1)S(1)} collective-permute-done((bf16[320,128]{1,0:T(8,128)(2,1)S(1)}, bf16[320,128]{1,0:T(8,128)(2,1)S(1)}, u32[]{:S(2)}, u32[]{:S(2)}) %collective-permute-start.6) | collective-permute-done | bytes 81952 | tf_op jit(solution)/shard_map/ppermute | solution.py:516
  28.7 6.4 %attend.1 = (bf16[128,1536]{1,0:T(8,128)(2,1)}, bf16[128,1024]{1,0:T(8,128)(2,1)S(1)}, f32[4,160,128]{2,1,0:T(8,128)S(1)}, bf16[4,160,128]{2,1,0:T(8,128)(2,1)S(...) custom-call(bf16[128,1024]{1,0:T(8,128)(2,1)S(1)} %get-tuple-element.64.refs_0_, ...), custom_call_target="tpu_custom_call" | custom-call | flops 2013265920 | bytes 2949120 | tf_op jit(solution)/shard_map/attend/pallas_call | solution.py:37
  35.1 1.2 %collective-permute-done.10.refs_3_ = bf16[480,384]{1,0:T(8,128)(2,1)S(1)} collective-permute-done((bf16[480,384]{1,0:T(8,128)(2,1)S(1)}, bf16[480,384]{1,0:T(8,128)(2,1)S(1)}, u32[]{:S(2)}, u32[]{:S(2)}) %collective-permute-start.10) | collective-permute-done | bytes 368672 | tf_op jit(solution)/shard_map/ppermute | solution.py:516
  38.1 2.4 %select.1 = (bf16[512,1024]{1,0:T(8,128)(2,1)S(1)}, bf16[192,512]{1,0:T(8,128)(2,1)S(1)}) custom-call(bf16[192,128]{1,0:T(8,128)(2,1)S(1)} %get-tuple-element.66.refs_0_, bf16[480,384]{1,0:T(8,128)(2,1)S(1)} %get-tuple-element.68.refs_1_, bf16[480,384]{1,0:T(8,128)(2,1)S(1)} %collective-permute-done.9.refs_2_, ...), custom_call_target="tpu_custom_call" | custom-call | flops 2013265920 | bytes 2768896 | tf_op jit(solution)/shard_map/select/pallas_call | solution.py:37
  40.5 3.1 %collective-permute-done.13.refs_3_ = bf16[4,160,128]{2,1,0:T(8,128)(2,1)S(1)} collective-permute-done((bf16[4,160,128]{2,1,0:T(8,128)(2,1)S(1)}, bf16[4,160,128]{2,1,0:T(8,128)(2,1)S(1)}, u32[]{:S(2)}, u32[]{:S(2)}) %collective-permute-start.13) | collective-permute-done | bytes 163872 | tf_op jit(solution)/shard_map/ppermute | solution.py:516
  44.2 1.0 %collective-permute-start.15 = (bf16[2,160,128]{2,1,0:T(8,128)(2,1)S(1)}, bf16[2,160,128]{2,1,0:T(8,128)(2,1)S(1)}, u32[]{:S(2)}, u32[]{:S(2)}) collective-permute-start(bf16[2,160,128]{2,1,0:T(8,128)(2,1)S(1)} %get-tuple-element.79), channel_id=1, source_target_pairs={{0,2},{1,3},{2,0},{3,1},{4,6},{5,7},{6,4},{7,5},{8,10},{9,11},{10,... | collective-permute-start | bytes 245768 | tf_op jit(solution)/shard_map/ppermute | solution.py:516
  45.2 3.0 %collective-permute-done.14.refs_1_ = bf16[2,160,128]{2,1,0:T(8,128)(2,1)S(1)} collective-permute-done((bf16[2,160,128]{2,1,0:T(8,128)(2,1)S(1)}, bf16[2,160,128]{2,1,0:T(8,128)(2,1)S(1)}, u32[]{:S(2)}, u32[]{:S(2)}) %collective-permute-start.14) | collective-permute-done | bytes 81952 | tf_op jit(solution)/shard_map/ppermute | solution.py:516
  48.6 1.1 %collective-permute-start.20 = (bf16[128,1024]{1,0:T(8,128)(2,1)S(1)}, bf16[128,1024]{1,0:T(8,128)(2,1)S(1)}, u32[]{:S(2)}, u32[]{:S(2)}) collective-permute-start(bf16[128,1024]{1,0:T(8,128)(2,1)S(1)} %get-tuple-element.85.refs_0_.refs_1_), channel_id=1, source_target_pairs={{0,2},{1,3},{2,0},{3,1},{4,6},{5,7},{6,4},{7,5},{8,10},{9,11},{10,... | collective-permute-start | bytes 786440 | tf_op jit(solution)/shard_map/ppermute | solution.py:516
  49.7 3.0 %collective-permute-start.16 = (bf16[1,320,128]{2,1,0:T(8,128)(2,1)S(1)}, bf16[1,320,128]{2,1,0:T(8,128)(2,1)S(1)}, u32[]{:S(2)}, u32[]{:S(2)}) collective-permute-start(bf16[1,320,128]{2,1,0:T(8,128)(2,1)S(1)} %get-tuple-element.81), channel_id=1, source_target_pairs={{0,8},{1,9},{2,10},{3,11},{4,12},{5,13},{6,14},{7,15},{8,0},{9,1},... | collective-permute-start | bytes 245768 | tf_op jit(solution)/shard_map/ppermute | solution.py:516
  53.4 1.7 %collective-permute-done.16.refs_1_ = bf16[1,320,128]{2,1,0:T(8,128)(2,1)S(1)} collective-permute-done((bf16[1,320,128]{2,1,0:T(8,128)(2,1)S(1)}, bf16[1,320,128]{2,1,0:T(8,128)(2,1)S(1)}, u32[]{:S(2)}, u32[]{:S(2)}) %collective-permute-start.16) | collective-permute-done | bytes 81952 | tf_op jit(solution)/shard_map/ppermute | solution.py:516
  55.6 1.0 %collective-permute-start.24 = (bf16[144,384]{1,0:T(8,128)(2,1)S(1)}, bf16[144,384]{1,0:T(8,128)(2,1)S(1)}, u32[]{:S(2)}, u32[]{:S(2)}) collective-permute-start(bf16[144,384]{1,0:T(8,128)(2,1)S(1)} %get-tuple-element.86.refs_1_), channel_id=1, source_target_pairs={{0,2},{1,3},{2,0},{3,1},{4,6},{5,7},{6,4},{7,5},{8,10},{9,11},{10,... | collective-permute-start | bytes 331784 | tf_op jit(solution)/shard_map/ppermute | solution.py:516
  58.0 1.7 %collective-permute-start.22 = (bf16[2,48,1024]{2,1,0:T(8,128)(2,1)S(1)}, bf16[2,48,1024]{2,1,0:T(8,128)(2,1)S(1)}, u32[]{:S(2)}, u32[]{:S(2)}) collective-permute-start(bf16[2,48,1024]{2,1,0:T(8,128)(2,1)S(1)} %get-tuple-element.89), channel_id=1, source_target_pairs={{0,4},{1,5},{2,6},{3,7},{4,0},{5,1},{6,2},{7,3},{8,12},{9,13},{10,... | collective-permute-start | bytes 589832 | tf_op jit(solution)/shard_map/ppermute | solution.py:516
  61.6 3.4 %collective-permute-done.22.refs_1_ = bf16[2,48,1024]{2,1,0:T(8,128)(2,1)S(1)} collective-permute-done((bf16[2,48,1024]{2,1,0:T(8,128)(2,1)S(1)}, bf16[2,48,1024]{2,1,0:T(8,128)(2,1)S(1)}, u32[]{:S(2)}, u32[]{:S(2)}) %collective-permute-start.22) | collective-permute-done | bytes 196640 | tf_op jit(solution)/shard_map/ppermute | solution.py:516
  66.4 1.5 %collective-permute-start.28 = (bf16[1,128,384]{2,1,0:T(8,128)(2,1)S(1)}, bf16[1,128,384]{2,1,0:T(8,128)(2,1)S(1)}, u32[]{:S(2)}, u32[]{:S(2)}) collective-permute-start(bf16[1,128,384]{2,1,0:T(8,128)(2,1)S(1)} %get-tuple-element.98), channel_id=1, source_target_pairs={{0,4},{1,5},{2,6},{3,7},{4,0},{5,1},{6,2},{7,3},{8,12},{9,13},{10,... | collective-permute-start | bytes 294920 | tf_op jit(solution)/shard_map/ppermute | solution.py:516
  67.9 1.0 %conv_grad_second.1 = (f32[1,160,384]{2,1,0:T(8,128)S(1)}, f32[1,160,384]{2,1,0:T(8,128)S(1)}, bf16[1,160,384]{2,1,0:T(8,128)(2,1)S(1)}, bf16[1,160,384]{2,1,0:T(8,128)(2,1)S(1)}) custom-call(bf16[512,1024]{1,0:T(8,128)(2,1)S(1)} %get-tuple-element.91.refs_4_.refs_0_, bf16[192,512]{1,0:T(8,128)(2,1)S(1)} %get-tuple-element.72.refs_0_.refs_1_, ...), custom_call_target="tpu_custom_call" | custom-call | flops 402653184 | bytes 2768896 | tf_op jit(solution)/shard_map/conv_grad_second/pallas_call | solution.py:37
  68.9 1.4 %collective-permute-start.27 = (bf16[1,160,384]{2,1,0:T(8,128)(2,1)S(1)}, bf16[1,160,384]{2,1,0:T(8,128)(2,1)S(1)}, u32[]{:S(2)}, u32[]{:S(2)}) collective-permute-start(bf16[1,160,384]{2,1,0:T(8,128)(2,1)S(1)} %get-tuple-element.96), channel_id=1, source_target_pairs={{0,4},{1,5},{2,6},{3,7},{4,0},{5,1},{6,2},{7,3},{8,12},{9,13},{10,... | collective-permute-start | bytes 368648 | tf_op jit(solution)/shard_map/ppermute | solution.py:516
  70.2 2.9 %collective-permute-start.30 = (bf16[1,48,1024]{2,1,0:T(8,128)(2,1)S(1)}, bf16[1,48,1024]{2,1,0:T(8,128)(2,1)S(1)}, u32[]{:S(2)}, u32[]{:S(2)}) collective-permute-start(bf16[1,48,1024]{2,1,0:T(8,128)(2,1)S(1)} %get-tuple-element.102), channel_id=1, source_target_pairs={{0,8},{1,9},{2,10},{3,11},{4,12},{5,13},{6,14},{7,15},{8,0},{9,1},... | collective-permute-start | bytes 294920 | tf_op jit(solution)/shard_map/ppermute | solution.py:516
  73.1 1.4 %collective-permute-start.29 = (bf16[1,128,384]{2,1,0:T(8,128)(2,1)S(1)}, bf16[1,128,384]{2,1,0:T(8,128)(2,1)S(1)}, u32[]{:S(2)}, u32[]{:S(2)}) collective-permute-start(bf16[1,128,384]{2,1,0:T(8,128)(2,1)S(1)} %conv_send_on.3), channel_id=1, source_target_pairs={{0,8},{1,9},{2,10},{3,11},{4,12},{5,13},{6,14},{7,15},{8,0},{9,1},... | collective-permute-start | bytes 294920 | tf_op jit(solution)/shard_map/ppermute | solution.py:516
  74.6 1.7 %collective-permute-done.30.refs_5_ = bf16[1,48,1024]{2,1,0:T(8,128)(2,1)S(1)} collective-permute-done((bf16[1,48,1024]{2,1,0:T(8,128)(2,1)S(1)}, bf16[1,48,1024]{2,1,0:T(8,128)(2,1)S(1)}, u32[]{:S(2)}, u32[]{:S(2)}) %collective-permute-start.30) | collective-permute-done | bytes 98336 | tf_op jit(solution)/shard_map/ppermute | solution.py:516
  76.2 4.8 %collective-permute-start.31 = (bf16[1,128,384]{2,1,0:T(8,128)(2,1)S(1)}, bf16[1,128,384]{2,1,0:T(8,128)(2,1)S(1)}, u32[]{:S(2)}, u32[]{:S(2)}) collective-permute-start(bf16[1,128,384]{2,1,0:T(8,128)(2,1)S(1)} %get-tuple-element.103), channel_id=1, source_target_pairs={{0,4},{1,5},{2,6},{3,7},{4,0},{5,1},{6,2},{7,3},{8,12},{9,13},{10,... | collective-permute-start | bytes 294920 | tf_op jit(solution)/shard_map/ppermute | solution.py:516
  81.1 3.4 %collective-permute-start.33 = (bf16[1,160,384]{2,1,0:T(8,128)(2,1)S(1)}, bf16[1,160,384]{2,1,0:T(8,128)(2,1)S(1)}, u32[]{:S(2)}, u32[]{:S(2)}) collective-permute-start(bf16[1,160,384]{2,1,0:T(8,128)(2,1)S(1)} %conv_send_on.2), channel_id=1, source_target_pairs={{0,8},{1,9},{2,10},{3,11},{4,12},{5,13},{6,14},{7,15},{8,0},{9,1},... | collective-permute-start | bytes 368648 | tf_op jit(solution)/shard_map/ppermute | solution.py:516
  84.6 2.0 %input_grad.1 = bf16[256,384]{1,0:T(8,128)(2,1)} custom-call(bf16[256,384]{1,0:T(8,128)(2,1)S(1)} %bitcast.10, bf16[144,384]{1,0:T(8,128)(2,1)S(1)} %get-tuple-element.86.refs_1_, bf16[256,384]{1,0:T(8,128)(2,1)S(1)} %get-tuple-element.84.refs_2_, bf16[144,384]{1,0:T(8,128)(2,1)S(1)} %collective-permute-done.24.refs_3_, ...), custom_call_target="tpu_custom_call" | custom-call | flops 7549747200 | bytes 4153344 | tf_op jit(solution)/shard_map/input_grad/pallas_call | solution.py:37
  86.7 2.1 %collective-permute-done.32.refs_2_ = bf16[1,160,384]{2,1,0:T(8,128)(2,1)S(1)} collective-permute-done((bf16[1,160,384]{2,1,0:T(8,128)(2,1)S(1)}, bf16[1,160,384]{2,1,0:T(8,128)(2,1)S(1)}, u32[]{:S(2)}, u32[]{:S(2)}) %collective-permute-start.32) | collective-permute-done | bytes 122912 | tf_op jit(solution)/shard_map/ppermute | solution.py:516
  (71 shorter events, 14.5 us)
Async XLA Ops:
  1.8 6.7 %collective-permute-start.1 = (bf16[32,384]{1,0:T(8,128)(2,1)S(1)}, bf16[32,384]{1,0:T(8,128)(2,1)S(1)}, u32[]{:S(2)}, u32[]{:S(2)}) collective-permute-start(bf16[32,384]{1,0:T(8,128)(2,1)S(1)} %get-tuple-element.60), channel_id=1, source_target_pairs={{2,4},{6,8},{10,12},{4,2},{8,6},{12,10},{3,5},{7,9},{11,13},{5,3},... | collective-permute-start | bytes 73736 | tf_op jit(solution)/shard_map/ppermute | solution.py:547
  2.6 7.7 %collective-permute-start = (bf16[32,384]{1,0:T(8,128)(2,1)S(1)}, bf16[32,384]{1,0:T(8,128)(2,1)S(1)}, u32[]{:S(2)}, u32[]{:S(2)}) collective-permute-start(bf16[32,384]{1,0:T(8,128)(2,1)S(1)} %get-tuple-element.60), channel_id=1, source_target_pairs={{0,2},{1,3},{2,0},{3,1},{4,6},{5,7},{6,4},{7,5},{8,10},{9,11},{10,... | collective-permute-start | bytes 73736 | tf_op jit(solution)/shard_map/ppermute | solution.py:516
  12.2 6.5 %collective-permute-start.4 = (bf16[320,128]{1,0:T(8,128)(2,1)S(1)}, bf16[320,128]{1,0:T(8,128)(2,1)S(1)}, u32[]{:S(2)}, u32[]{:S(2)}) collective-permute-start(bf16[320,128]{1,0:T(8,128)(2,1)S(1)} %get-tuple-element.63.refs_2_), channel_id=1, source_target_pairs={{0,12},{1,13},{2,14},{3,15},{4,8},{5,9},{6,10},{7,11},{8,4},{9,5},... | collective-permute-start | bytes 245768 | tf_op jit(solution)/shard_map/ppermute | solution.py:516
  16.2 5.9 %collective-permute-start.3 = (bf16[320,128]{1,0:T(8,128)(2,1)S(1)}, bf16[320,128]{1,0:T(8,128)(2,1)S(1)}, u32[]{:S(2)}, u32[]{:S(2)}) collective-permute-start(bf16[320,128]{1,0:T(8,128)(2,1)S(1)} %get-tuple-element.63.refs_2_), channel_id=1, source_target_pairs={{0,8},{1,9},{2,10},{3,11},{4,12},{5,13},{6,14},{7,15},{8,0},{9,1},... | collective-permute-start | bytes 245768 | tf_op jit(solution)/shard_map/ppermute | solution.py:516
  16.2 7.2 %collective-permute-start.2 = (bf16[320,128]{1,0:T(8,128)(2,1)S(1)}, bf16[320,128]{1,0:T(8,128)(2,1)S(1)}, u32[]{:S(2)}, u32[]{:S(2)}) collective-permute-start(bf16[320,128]{1,0:T(8,128)(2,1)S(1)} %get-tuple-element.63.refs_2_), channel_id=1, source_target_pairs={{0,4},{1,5},{2,6},{3,7},{4,0},{5,1},{6,2},{7,3},{8,12},{9,13},{10,... | collective-permute-start | bytes 245768 | tf_op jit(solution)/shard_map/ppermute | solution.py:516
  16.9 8.0 %collective-permute-start.5 = (bf16[320,128]{1,0:T(8,128)(2,1)S(1)}, bf16[320,128]{1,0:T(8,128)(2,1)S(1)}, u32[]{:S(2)}, u32[]{:S(2)}) collective-permute-start(bf16[320,128]{1,0:T(8,128)(2,1)S(1)} %get-tuple-element.63.refs_2_), channel_id=1, source_target_pairs={{0,2},{1,3},{2,0},{3,1},{4,6},{5,7},{6,4},{7,5},{8,10},{9,11},{10,... | collective-permute-start | bytes 245768 | tf_op jit(solution)/shard_map/ppermute | solution.py:516
  18.7 6.2 %collective-permute-start.8 = (bf16[320,128]{1,0:T(8,128)(2,1)S(1)}, bf16[320,128]{1,0:T(8,128)(2,1)S(1)}, u32[]{:S(2)}, u32[]{:S(2)}) collective-permute-start(bf16[320,128]{1,0:T(8,128)(2,1)S(1)} %collective-permute-done.4.refs_5_), channel_id=1, source_target_pairs={{0,2},{1,3},{2,0},{3,1},{4,6},{5,7},{6,4},{7,5},{8,10},{9,11},{10,... | collective-permute-start | bytes 245768 | tf_op jit(solution)/shard_map/ppermute | solution.py:516
  22.1 4.5 %collective-permute-start.7 = (bf16[320,128]{1,0:T(8,128)(2,1)S(1)}, bf16[320,128]{1,0:T(8,128)(2,1)S(1)}, u32[]{:S(2)}, u32[]{:S(2)}) collective-permute-start(bf16[320,128]{1,0:T(8,128)(2,1)S(1)} %collective-permute-done.3.refs_4_), channel_id=1, source_target_pairs={{0,2},{1,3},{2,0},{3,1},{4,6},{5,7},{6,4},{7,5},{8,10},{9,11},{10,... | collective-permute-start | bytes 245768 | tf_op jit(solution)/shard_map/ppermute | solution.py:516
  23.4 4.4 %collective-permute-start.6 = (bf16[320,128]{1,0:T(8,128)(2,1)S(1)}, bf16[320,128]{1,0:T(8,128)(2,1)S(1)}, u32[]{:S(2)}, u32[]{:S(2)}) collective-permute-start(bf16[320,128]{1,0:T(8,128)(2,1)S(1)} %collective-permute-done.2.refs_3_), channel_id=1, source_target_pairs={{0,2},{1,3},{2,0},{3,1},{4,6},{5,7},{6,4},{7,5},{8,10},{9,11},{10,... | collective-permute-start | bytes 245768 | tf_op jit(solution)/shard_map/ppermute | solution.py:516
  27.9 8.5 %collective-permute-start.10 = (bf16[480,384]{1,0:T(8,128)(2,1)S(1)}, bf16[480,384]{1,0:T(8,128)(2,1)S(1)}, u32[]{:S(2)}, u32[]{:S(2)}) collective-permute-start(bf16[480,384]{1,0:T(8,128)(2,1)S(1)} %get-tuple-element.68.refs_1_), channel_id=1, source_target_pairs={{0,2},{1,3},{2,0},{3,1},{4,6},{5,7},{6,4},{7,5},{8,10},{9,11},{10,... | collective-permute-start | bytes 1105928 | tf_op jit(solution)/shard_map/ppermute | solution.py:516
  28.7 9.0 %collective-permute-start.9 = (bf16[480,384]{1,0:T(8,128)(2,1)S(1)}, bf16[480,384]{1,0:T(8,128)(2,1)S(1)}, u32[]{:S(2)}, u32[]{:S(2)}) collective-permute-start(bf16[480,384]{1,0:T(8,128)(2,1)S(1)} %get-tuple-element.68.refs_1_), channel_id=1, source_target_pairs={{0,1},{1,0},{2,3},{3,2},{4,5},{5,4},{6,7},{7,6},{8,9},{9,8},{10,11... | collective-permute-start | bytes 1105928 | tf_op jit(solution)/shard_map/ppermute | solution.py:516
  36.4 1.7 %collective-permute-start.11 = (bf16[480,384]{1,0:T(8,128)(2,1)S(1)}, bf16[480,384]{1,0:T(8,128)(2,1)S(1)}, u32[]{:S(2)}, u32[]{:S(2)}) collective-permute-start(bf16[480,384]{1,0:T(8,128)(2,1)S(1)} %collective-permute-done.10.refs_3_), channel_id=1, source_target_pairs={{0,1},{1,0},{2,3},{3,2},{4,5},{5,4},{6,7},{7,6},{8,9},{9,8},{10,11... | collective-permute-start | bytes 1105928 | tf_op jit(solution)/shard_map/ppermute | solution.py:516
  36.4 7.2 %collective-permute-start.12 = (bf16[4,160,128]{2,1,0:T(8,128)(2,1)S(1)}, bf16[4,160,128]{2,1,0:T(8,128)(2,1)S(1)}, u32[]{:S(2)}, u32[]{:S(2)}) collective-permute-start(bf16[4,160,128]{2,1,0:T(8,128)(2,1)S(1)} %get-tuple-element.69), channel_id=1, source_target_pairs={{0,2},{1,3},{2,0},{3,1},{4,6},{5,7},{6,4},{7,5},{8,10},{9,11},{10,... | collective-permute-start | bytes 491528 | tf_op jit(solution)/shard_map/ppermute | solution.py:516
  37.2 6.3 %collective-permute-start.13 = (bf16[4,160,128]{2,1,0:T(8,128)(2,1)S(1)}, bf16[4,160,128]{2,1,0:T(8,128)(2,1)S(1)}, u32[]{:S(2)}, u32[]{:S(2)}) collective-permute-start(bf16[4,160,128]{2,1,0:T(8,128)(2,1)S(1)} %get-tuple-element.75), channel_id=1, source_target_pairs={{0,4},{1,5},{2,6},{3,7},{4,0},{5,1},{6,2},{7,3},{8,12},{9,13},{10,... | collective-permute-start | bytes 491528 | tf_op jit(solution)/shard_map/ppermute | solution.py:516
  43.6 4.5 %collective-permute-start.14 = (bf16[2,160,128]{2,1,0:T(8,128)(2,1)S(1)}, bf16[2,160,128]{2,1,0:T(8,128)(2,1)S(1)}, u32[]{:S(2)}, u32[]{:S(2)}) collective-permute-start(bf16[2,160,128]{2,1,0:T(8,128)(2,1)S(1)} %get-tuple-element.77), channel_id=1, source_target_pairs={{0,4},{1,5},{2,6},{3,7},{4,0},{5,1},{6,2},{7,3},{8,12},{9,13},{10,... | collective-permute-start | bytes 245768 | tf_op jit(solution)/shard_map/ppermute | solution.py:516
  44.2 4.4 %collective-permute-start.15 = (bf16[2,160,128]{2,1,0:T(8,128)(2,1)S(1)}, bf16[2,160,128]{2,1,0:T(8,128)(2,1)S(1)}, u32[]{:S(2)}, u32[]{:S(2)}) collective-permute-start(bf16[2,160,128]{2,1,0:T(8,128)(2,1)S(1)} %get-tuple-element.79), channel_id=1, source_target_pairs={{0,2},{1,3},{2,0},{3,1},{4,6},{5,7},{6,4},{7,5},{8,10},{9,11},{10,... | collective-permute-start | bytes 245768 | tf_op jit(solution)/shard_map/ppermute | solution.py:516
  48.6 6.9 %collective-permute-start.20 = (bf16[128,1024]{1,0:T(8,128)(2,1)S(1)}, bf16[128,1024]{1,0:T(8,128)(2,1)S(1)}, u32[]{:S(2)}, u32[]{:S(2)}) collective-permute-start(bf16[128,1024]{1,0:T(8,128)(2,1)S(1)} %get-tuple-element.85.refs_0_.refs_1_), channel_id=1, source_target_pairs={{0,2},{1,3},{2,0},{3,1},{4,6},{5,7},{6,4},{7,5},{8,10},{9,11},{10,... | collective-permute-start | bytes 786440 | tf_op jit(solution)/shard_map/ppermute | solution.py:516
  49.7 5.4 %collective-permute-start.16 = (bf16[1,320,128]{2,1,0:T(8,128)(2,1)S(1)}, bf16[1,320,128]{2,1,0:T(8,128)(2,1)S(1)}, u32[]{:S(2)}, u32[]{:S(2)}) collective-permute-start(bf16[1,320,128]{2,1,0:T(8,128)(2,1)S(1)} %get-tuple-element.81), channel_id=1, source_target_pairs={{0,8},{1,9},{2,10},{3,11},{4,12},{5,13},{6,14},{7,15},{8,0},{9,1},... | collective-permute-start | bytes 245768 | tf_op jit(solution)/shard_map/ppermute | solution.py:516
  53.4 3.3 %collective-permute-start.19 = (bf16[128,1024]{1,0:T(8,128)(2,1)S(1)}, bf16[128,1024]{1,0:T(8,128)(2,1)S(1)}, u32[]{:S(2)}, u32[]{:S(2)}) collective-permute-start(bf16[128,1024]{1,0:T(8,128)(2,1)S(1)} %get-tuple-element.85.refs_0_.refs_1_), channel_id=1, source_target_pairs={{0,1},{1,0},{2,3},{3,2},{4,5},{5,4},{6,7},{7,6},{8,9},{9,8},{10,11... | collective-permute-start | bytes 786440 | tf_op jit(solution)/shard_map/ppermute | solution.py:516
  55.6 5.5 %collective-permute-start.24 = (bf16[144,384]{1,0:T(8,128)(2,1)S(1)}, bf16[144,384]{1,0:T(8,128)(2,1)S(1)}, u32[]{:S(2)}, u32[]{:S(2)}) collective-permute-start(bf16[144,384]{1,0:T(8,128)(2,1)S(1)} %get-tuple-element.86.refs_1_), channel_id=1, source_target_pairs={{0,2},{1,3},{2,0},{3,1},{4,6},{5,7},{6,4},{7,5},{8,10},{9,11},{10,... | collective-permute-start | bytes 331784 | tf_op jit(solution)/shard_map/ppermute | solution.py:516
  58.0 7.0 %collective-permute-start.22 = (bf16[2,48,1024]{2,1,0:T(8,128)(2,1)S(1)}, bf16[2,48,1024]{2,1,0:T(8,128)(2,1)S(1)}, u32[]{:S(2)}, u32[]{:S(2)}) collective-permute-start(bf16[2,48,1024]{2,1,0:T(8,128)(2,1)S(1)} %get-tuple-element.89), channel_id=1, source_target_pairs={{0,4},{1,5},{2,6},{3,7},{4,0},{5,1},{6,2},{7,3},{8,12},{9,13},{10,... | collective-permute-start | bytes 589832 | tf_op jit(solution)/shard_map/ppermute | solution.py:516
  59.7 6.7 %collective-permute-start.18 = (bf16[256,384]{1,0:T(8,128)(2,1)S(1)}, bf16[256,384]{1,0:T(8,128)(2,1)S(1)}, u32[]{:S(2)}, u32[]{:S(2)}) collective-permute-start(bf16[256,384]{1,0:T(8,128)(2,1)S(1)} %get-tuple-element.84.refs_2_), channel_id=1, source_target_pairs={{0,2},{1,3},{2,0},{3,1},{4,6},{5,7},{6,4},{7,5},{8,10},{9,11},{10,... | collective-permute-start | bytes 589832 | tf_op jit(solution)/shard_map/ppermute | solution.py:516
  60.6 4.5 %collective-permute-start.23 = (bf16[144,384]{1,0:T(8,128)(2,1)S(1)}, bf16[144,384]{1,0:T(8,128)(2,1)S(1)}, u32[]{:S(2)}, u32[]{:S(2)}) collective-permute-start(bf16[144,384]{1,0:T(8,128)(2,1)S(1)} %get-tuple-element.86.refs_1_), channel_id=1, source_target_pairs={{0,1},{1,0},{2,3},{3,2},{4,5},{5,4},{6,7},{7,6},{8,9},{9,8},{10,11... | collective-permute-start | bytes 331784 | tf_op jit(solution)/shard_map/ppermute | solution.py:516
  61.1 3.9 %collective-permute-start.25 = (bf16[144,384]{1,0:T(8,128)(2,1)S(1)}, bf16[144,384]{1,0:T(8,128)(2,1)S(1)}, u32[]{:S(2)}, u32[]{:S(2)}) collective-permute-start(bf16[144,384]{1,0:T(8,128)(2,1)S(1)} %collective-permute-done.24.refs_3_), channel_id=1, source_target_pairs={{0,1},{1,0},{2,3},{3,2},{4,5},{5,4},{6,7},{7,6},{8,9},{9,8},{10,11... | collective-permute-start | bytes 331784 | tf_op jit(solution)/shard_map/ppermute | solution.py:516
  61.1 6.7 %collective-permute-start.17 = (bf16[256,384]{1,0:T(8,128)(2,1)S(1)}, bf16[256,384]{1,0:T(8,128)(2,1)S(1)}, u32[]{:S(2)}, u32[]{:S(2)}) collective-permute-start(bf16[256,384]{1,0:T(8,128)(2,1)S(1)} %get-tuple-element.84.refs_2_), channel_id=1, source_target_pairs={{0,1},{1,0},{2,3},{3,2},{4,5},{5,4},{6,7},{7,6},{8,9},{9,8},{10,11... | collective-permute-start | bytes 589832 | tf_op jit(solution)/shard_map/ppermute | solution.py:516
  66.4 6.7 %collective-permute-start.28 = (bf16[1,128,384]{2,1,0:T(8,128)(2,1)S(1)}, bf16[1,128,384]{2,1,0:T(8,128)(2,1)S(1)}, u32[]{:S(2)}, u32[]{:S(2)}) collective-permute-start(bf16[1,128,384]{2,1,0:T(8,128)(2,1)S(1)} %get-tuple-element.98), channel_id=1, source_target_pairs={{0,4},{1,5},{2,6},{3,7},{4,0},{5,1},{6,2},{7,3},{8,12},{9,13},{10,... | collective-permute-start | bytes 294920 | tf_op jit(solution)/shard_map/ppermute | solution.py:516
  68.9 12.2 %collective-permute-start.27 = (bf16[1,160,384]{2,1,0:T(8,128)(2,1)S(1)}, bf16[1,160,384]{2,1,0:T(8,128)(2,1)S(1)}, u32[]{:S(2)}, u32[]{:S(2)}) collective-permute-start(bf16[1,160,384]{2,1,0:T(8,128)(2,1)S(1)} %get-tuple-element.96), channel_id=1, source_target_pairs={{0,4},{1,5},{2,6},{3,7},{4,0},{5,1},{6,2},{7,3},{8,12},{9,13},{10,... | collective-permute-start | bytes 368648 | tf_op jit(solution)/shard_map/ppermute | solution.py:516
  70.2 6.0 %collective-permute-start.30 = (bf16[1,48,1024]{2,1,0:T(8,128)(2,1)S(1)}, bf16[1,48,1024]{2,1,0:T(8,128)(2,1)S(1)}, u32[]{:S(2)}, u32[]{:S(2)}) collective-permute-start(bf16[1,48,1024]{2,1,0:T(8,128)(2,1)S(1)} %get-tuple-element.102), channel_id=1, source_target_pairs={{0,8},{1,9},{2,10},{3,11},{4,12},{5,13},{6,14},{7,15},{8,0},{9,1},... | collective-permute-start | bytes 294920 | tf_op jit(solution)/shard_map/ppermute | solution.py:516
  73.1 11.4 %collective-permute-start.29 = (bf16[1,128,384]{2,1,0:T(8,128)(2,1)S(1)}, bf16[1,128,384]{2,1,0:T(8,128)(2,1)S(1)}, u32[]{:S(2)}, u32[]{:S(2)}) collective-permute-start(bf16[1,128,384]{2,1,0:T(8,128)(2,1)S(1)} %conv_send_on.3), channel_id=1, source_target_pairs={{0,8},{1,9},{2,10},{3,11},{4,12},{5,13},{6,14},{7,15},{8,0},{9,1},... | collective-permute-start | bytes 294920 | tf_op jit(solution)/shard_map/ppermute | solution.py:516
  76.2 10.4 %collective-permute-start.31 = (bf16[1,128,384]{2,1,0:T(8,128)(2,1)S(1)}, bf16[1,128,384]{2,1,0:T(8,128)(2,1)S(1)}, u32[]{:S(2)}, u32[]{:S(2)}) collective-permute-start(bf16[1,128,384]{2,1,0:T(8,128)(2,1)S(1)} %get-tuple-element.103), channel_id=1, source_target_pairs={{0,4},{1,5},{2,6},{3,7},{4,0},{5,1},{6,2},{7,3},{8,12},{9,13},{10,... | collective-permute-start | bytes 294920 | tf_op jit(solution)/shard_map/ppermute | solution.py:516
  81.0 7.7 %collective-permute-start.32 = (bf16[1,160,384]{2,1,0:T(8,128)(2,1)S(1)}, bf16[1,160,384]{2,1,0:T(8,128)(2,1)S(1)}, u32[]{:S(2)}, u32[]{:S(2)}) collective-permute-start(bf16[1,160,384]{2,1,0:T(8,128)(2,1)S(1)} %get-tuple-element.105), channel_id=1, source_target_pairs={{0,4},{1,5},{2,6},{3,7},{4,0},{5,1},{6,2},{7,3},{8,12},{9,13},{10,... | collective-permute-start | bytes 368648 | tf_op jit(solution)/shard_map/ppermute | solution.py:516
  81.1 7.6 %collective-permute-start.33 = (bf16[1,160,384]{2,1,0:T(8,128)(2,1)S(1)}, bf16[1,160,384]{2,1,0:T(8,128)(2,1)S(1)}, u32[]{:S(2)}, u32[]{:S(2)}) collective-permute-start(bf16[1,160,384]{2,1,0:T(8,128)(2,1)S(1)} %conv_send_on.2), channel_id=1, source_target_pairs={{0,8},{1,9},{2,10},{3,11},{4,12},{5,13},{6,14},{7,15},{8,0},{9,1},... | collective-permute-start | bytes 368648 | tf_op jit(solution)/shard_map/ppermute | solution.py:516
  (10 other events, 105.3 us)

commit v10 on v8

--- a/solution.py
+++ b/solution.py
@@ -1,3 +1,4 @@
+import functools
 import math
 
 import jax
@@ -152,11 +153,15 @@
         at += step
 
 
+def by_eight(rows):
+    return rows.reshape(rows.shape[0] // 8, 8, rows.shape[1])
+
+
 def attend_kernel(*refs, blocks, masks, heads, key_size, value_size, scale):
     q, cot = refs[:2]
     parts = refs[2 : 2 + blocks]
     att, dq, keep_a, send_a, keep_b, send_b = refs[2 + blocks : 8 + blocks]
-    ks, vs, kt, vt, qs, cs, weights, score_cots = refs[8 + blocks :]
+    ks, vs, kt, vt, qs, cs, weights, score_cots, scores, prob_cots = refs[8 + blocks :]
     tokens = q.shape[0]
     half = tokens // 2
     wide = value_size - key_size
@@ -176,23 +181,36 @@
             [q[:, ql : ql + key_size], q[:, ql + key_size : ql + 2 * key_size]], axis=0
         )
         cs[rows] = jnp.concatenate([both[:, :value_size], both[:, value_size:]], axis=0)
-        scores = dot_t(ks[...], qs[rows])
-        raised = jnp.exp(scores - jnp.max(scores, axis=0, keepdims=True))
-        probs = raised * (1.0 / jnp.sum(raised, axis=0, keepdims=True))
-        weights[:, rows] = probs.astype(BF)
+        slot = pair % scores.shape[0]
+        parts_of = [slice(i * tokens, (i + 1) * tokens) for i in range(blocks)]
+        scores[slot] = dot_t(ks[...], qs[rows])
+        prob_cots[slot] = dot_t(vs[...], cs[rows])
+        top = functools.reduce(jnp.maximum, [by_eight(scores[slot, at]).max(0) for at in parts_of])
+        top = jnp.max(top, axis=0, keepdims=True)
+        sums = 0.0
+        for at in parts_of:
+            raised = jnp.exp(scores[slot, at] - top)
+            sums = sums + by_eight(raised).sum(0)
+            scores[slot, at] = raised
+        inverse = 1.0 / jnp.sum(sums, axis=0, keepdims=True)
+        for at in parts_of:
+            weights[at, rows] = (scores[slot, at] * inverse).astype(BF)
         out_t = dot(vt[...], weights[:, rows]).astype(BF).astype(F32)
         delta = jnp.sum(cs[rows].astype(F32).T * out_t, axis=0, keepdims=True)
-        score_cots[:, rows] = (probs * (dot_t(vs[...], cs[rows]) - delta)).astype(BF)
+        for at in parts_of:
+            probs = scores[slot, at] * inverse
+            score_cots[at, rows] = (probs * (prob_cots[slot, at] - delta)).astype(BF)
         dq_t = dot(kt[...], score_cots[:, rows]) * scale
         out_rows = jnp.concatenate([out_t[:, :tokens].T, out_t[:, tokens:].T], axis=1)
         att[:, cl : cl + 2 * value_size] = out_rows.astype(BF)
         dq_rows = jnp.concatenate([dq_t[:, :tokens].T, dq_t[:, tokens:].T], axis=1)
         dq[:, ql : ql + 2 * key_size] = dq_rows.astype(BF)
+    key_cots, value_cots = dot(score_cots[...], qs[...]), dot(weights[...], cs[...])
     edge = keep_a.shape[1]
     count = blocks // 2
     for i in range(blocks):
         at = slice(i * tokens, (i + 1) * tokens)
-        packed = pack_kv(dot(score_cots[at], qs[...]), dot(weights[at], cs[...]))
+        packed = pack_kv(key_cots[at], value_cots[at])
         for order, keep, send, part in (
             (masks[0], keep_a, send_a, packed[:edge]),
             (masks[1], keep_b, send_b, packed[edge:]),
@@ -565,6 +583,7 @@
     length = devices * tokens
     masks = [2 * k for k in range(groups)] + [2 * k + 1 for k in range(groups)]
     half_block = (groups, 5 * tokens // 4, key_size)
+    slots = 2 if length <= 2048 else 1
     attended, query_cot, keep_a, send_a, keep_b, send_b = run(
         lambda *refs: attend_kernel(
             *refs,
@@ -589,6 +608,8 @@
             pltpu.VMEM((heads * tokens, value_size), BF),
             pltpu.VMEM((length, heads * tokens), BF),
             pltpu.VMEM((length, heads * tokens), BF),
+            pltpu.VMEM((slots, length, 2 * tokens), F32),
+            pltpu.VMEM((slots, length, 2 * tokens), F32),
         ],
         flops=6 * tokens * heads * length * (key_size + value_size),
         name="attend",
@@ -667,7 +688,7 @@
         name="conv_grad_first",
     )
     far_in = swap(far_send, 2)
-    last_second = swap(held(near_second, near_keep), 0, 1)
+    last_second = swap(held(near_second, near_keep, query_parts[0]), 0, 1)
     near_keep_second, far_keep_second, near_send, far_send = run(
         lambda *refs: conv_second_kernel(
             *refs,
@@ -684,7 +705,7 @@
             ((count, above + below, split), BF),
             ((count, below, split), BF),
         ],
-        [held(conv_pick, query_parts[0]), norm_pick, second, core_second, near_second, last_second, near_send],
+        [conv_pick, norm_pick, second, core_second, near_second, last_second, near_send],
         [
             pltpu.VMEM((8 * tokens, split), BF),
             pltpu.VMEM((4 * tokens, split), BF),
@@ -716,7 +737,7 @@
     (input_grad,) = run(
         input_kernel,
         [((positions, channels), BF)],
-        [held(x, far_sum), first, second, near_first, near_second] + edges + [conv_weight],
+        [held(x, far_sum, query_parts[1]), first, second, near_first, near_second] + edges + [conv_weight],
         [
             pltpu.VMEM((tokens + 16, width), F32),
             pltpu.VMEM((channels // LANES, positions, LANES), F32),

time: 88 us -> 86.9 us (0.988)
  starting transfers between devices: 39.2 us -> 36.8 us
  waiting for transfers between devices: 28.1 us -> 29.6 us
    ppermute x32, starting transfers between devices: 38.5 us -> 36 us  [swap(): lax.ppermute(value, both_axes, [(i, i ^ mask) for i in range(owners)])]
    ppermute x32, waiting for transfers between devices: 28.1 us -> 29.6 us  [swap(): lax.ppermute(value, both_axes, [(i, i ^ mask) for i in range(owners)])]
  transfers between devices with their start and end apart: 33 -> 33, of which waited for: 17 -> 21; matrix products, arithmetic and copies ran while one was open for 0% -> 0% of each run, Pallas kernels for 18% -> 18%
where the time goes in v10:
time: 86.9 us; the launch traced here: 86.7 us
  starting transfers between devices  36.8 us (42%)
  waiting for transfers between devices  29.6 us (34%)
  Pallas kernels  18.5 us (21%)
  local copies, waits for them, and re-layouts  0.96 us (1%)
    ppermute x32, starting transfers between devices, swap(): lax.ppermute(value, both_axes, [(i, i ^ mask) for i in range(owners)])  36 us
    ppermute x32, waiting for transfers between devices, swap(): lax.ppermute(value, both_axes, [(i, i ^ mask) for i in range(owners)])  29.6 us
    pallas_call x18, Pallas kernels, run(): pl.pallas_call(whole, out_shape=[jax.ShapeDtypeStruct(s, t) for s, t in o...  18.5 us
  transfers between devices with their start and end apart: 33, of which 21 were waited for; matrix products, arithmetic and copies ran while one was open for 0% of the time, Pallas kernels for 18%

profile of v10, /device:TPU:0, one launch (start us, length us, event | category | flops | bytes accessed | tf_op | source)
XLA Modules:
  0.0 86.7 jit_solution(13694008515282821766)
XLA Ops:
  0.6 0.9 %copy-done.5 = bf16[1,256,384]{2,1,0:T(8,128)(2,1)S(1)} copy-done((bf16[1,256,384]{2,1,0:T(8,128)(2,1)S(1)}, bf16[1,256,384]{2,1,0:T(8,128)(2,1)}, u32[]{:S(2)}) %copy-start.5) | copy-done | bytes 196632
  2.6 5.9 %collective-permute-start = (bf16[32,384]{1,0:T(8,128)(2,1)S(1)}, bf16[32,384]{1,0:T(8,128)(2,1)S(1)}, u32[]{:S(2)}, u32[]{:S(2)}) collective-permute-start(bf16[32,384]{1,0:T(8,128)(2,1)S(1)} %get-tuple-element.57), channel_id=1, source_target_pairs={{0,2},{1,3},{2,0},{3,1},{4,6},{5,7},{6,4},{7,5},{8,10},{9,11},{10,... | collective-permute-start | bytes 73736 | tf_op jit(solution)/shard_map/ppermute | solution.py:522
  8.5 1.8 %collective-permute-done.refs_1_ = bf16[32,384]{1,0:T(8,128)(2,1)S(1)} collective-permute-done((bf16[32,384]{1,0:T(8,128)(2,1)S(1)}, bf16[32,384]{1,0:T(8,128)(2,1)S(1)}, u32[]{:S(2)}, u32[]{:S(2)}) %collective-permute-start) | collective-permute-done | bytes 24608 | tf_op jit(solution)/shard_map/ppermute | solution.py:522
  10.3 1.9 %front.1 = (bf16[320,128]{1,0:T(8,128)(2,1)S(1)}, bf16[288,384]{1,0:T(8,128)(2,1)S(1)}, bf16[128,768]{1,0:T(8,128)(2,1)S(1)}, f32[128,768]{1,0:T(8,128)S(1)}) custom-call(f32[3,304,128]{2,1,0:T(8,128)S(1)} %get-tuple-element.56.refs_0_, bf16[32,384]{1,0:T(8,128)(2,1)S(1)} %collective-permute-done.refs_1_, ...), custom_call_target="tpu_custom_call" | custom-call | flops 754974720 | bytes 4852736 | tf_op jit(solution)/shard_map/front/pallas_call | solution.py:37
  12.2 4.0 %collective-permute-start.4 = (bf16[320,128]{1,0:T(8,128)(2,1)S(1)}, bf16[320,128]{1,0:T(8,128)(2,1)S(1)}, u32[]{:S(2)}, u32[]{:S(2)}) collective-permute-start(bf16[320,128]{1,0:T(8,128)(2,1)S(1)} %get-tuple-element.60.refs_2_), channel_id=1, source_target_pairs={{0,12},{1,13},{2,14},{3,15},{4,8},{5,9},{6,10},{7,11},{8,4},{9,5},... | collective-permute-start | bytes 245768 | tf_op jit(solution)/shard_map/ppermute | solution.py:522
  16.9 1.8 %collective-permute-start.5 = (bf16[320,128]{1,0:T(8,128)(2,1)S(1)}, bf16[320,128]{1,0:T(8,128)(2,1)S(1)}, u32[]{:S(2)}, u32[]{:S(2)}) collective-permute-start(bf16[320,128]{1,0:T(8,128)(2,1)S(1)} %get-tuple-element.60.refs_2_), channel_id=1, source_target_pairs={{0,2},{1,3},{2,0},{3,1},{4,6},{5,7},{6,4},{7,5},{8,10},{9,11},{10,... | collective-permute-start | bytes 245768 | tf_op jit(solution)/shard_map/ppermute | solution.py:522
  18.7 2.4 %collective-permute-start.8 = (bf16[320,128]{1,0:T(8,128)(2,1)S(1)}, bf16[320,128]{1,0:T(8,128)(2,1)S(1)}, u32[]{:S(2)}, u32[]{:S(2)}) collective-permute-start(bf16[320,128]{1,0:T(8,128)(2,1)S(1)} %collective-permute-done.4.refs_5_), channel_id=1, source_target_pairs={{0,2},{1,3},{2,0},{3,1},{4,6},{5,7},{6,4},{7,5},{8,10},{9,11},{10,... | collective-permute-start | bytes 245768 | tf_op jit(solution)/shard_map/ppermute | solution.py:522
  21.1 1.0 %collective-permute-done.3.refs_4_ = bf16[320,128]{1,0:T(8,128)(2,1)S(1)} collective-permute-done((bf16[320,128]{1,0:T(8,128)(2,1)S(1)}, bf16[320,128]{1,0:T(8,128)(2,1)S(1)}, u32[]{:S(2)}, u32[]{:S(2)}) %collective-permute-start.3) | collective-permute-done | bytes 81952 | tf_op jit(solution)/shard_map/ppermute | solution.py:522
  22.1 1.3 %collective-permute-start.7 = (bf16[320,128]{1,0:T(8,128)(2,1)S(1)}, bf16[320,128]{1,0:T(8,128)(2,1)S(1)}, u32[]{:S(2)}, u32[]{:S(2)}) collective-permute-start(bf16[320,128]{1,0:T(8,128)(2,1)S(1)} %collective-permute-done.3.refs_4_), channel_id=1, source_target_pairs={{0,2},{1,3},{2,0},{3,1},{4,6},{5,7},{6,4},{7,5},{8,10},{9,11},{10,... | collective-permute-start | bytes 245768 | tf_op jit(solution)/shard_map/ppermute | solution.py:522
  24.9 1.7 %collective-permute-done.7.refs_8_ = bf16[320,128]{1,0:T(8,128)(2,1)S(1)} collective-permute-done((bf16[320,128]{1,0:T(8,128)(2,1)S(1)}, bf16[320,128]{1,0:T(8,128)(2,1)S(1)}, u32[]{:S(2)}, u32[]{:S(2)}) %collective-permute-start.7) | collective-permute-done | bytes 81952 | tf_op jit(solution)/shard_map/ppermute | solution.py:522
  26.6 1.2 %collective-permute-done.6.refs_7_ = bf16[320,128]{1,0:T(8,128)(2,1)S(1)} collective-permute-done((bf16[320,128]{1,0:T(8,128)(2,1)S(1)}, bf16[320,128]{1,0:T(8,128)(2,1)S(1)}, u32[]{:S(2)}, u32[]{:S(2)}) %collective-permute-start.6) | collective-permute-done | bytes 81952 | tf_op jit(solution)/shard_map/ppermute | solution.py:522
  28.7 6.4 %attend.1 = (bf16[128,1536]{1,0:T(8,128)(2,1)}, bf16[128,1024]{1,0:T(8,128)(2,1)S(1)}, f32[4,160,128]{2,1,0:T(8,128)S(1)}, bf16[4,160,128]{2,1,0:T(8,128)(2,1)S(...) custom-call(bf16[128,1024]{1,0:T(8,128)(2,1)S(1)} %get-tuple-element.61.refs_0_, ...), custom_call_target="tpu_custom_call" | custom-call | flops 2013265920 | bytes 2949120 | tf_op jit(solution)/shard_map/attend/pallas_call | solution.py:37
  35.1 1.2 %collective-permute-done.10.refs_3_ = bf16[480,384]{1,0:T(8,128)(2,1)S(1)} collective-permute-done((bf16[480,384]{1,0:T(8,128)(2,1)S(1)}, bf16[480,384]{1,0:T(8,128)(2,1)S(1)}, u32[]{:S(2)}, u32[]{:S(2)}) %collective-permute-start.10) | collective-permute-done | bytes 368672 | tf_op jit(solution)/shard_map/ppermute | solution.py:522
  38.1 2.4 %select.1 = (bf16[512,1024]{1,0:T(8,128)(2,1)S(1)}, bf16[192,512]{1,0:T(8,128)(2,1)S(1)}) custom-call(bf16[192,128]{1,0:T(8,128)(2,1)S(1)} %get-tuple-element.63.refs_0_, bf16[480,384]{1,0:T(8,128)(2,1)S(1)} %get-tuple-element.65.refs_1_, bf16[480,384]{1,0:T(8,128)(2,1)S(1)} %collective-permute-done.9.refs_2_, ...), custom_call_target="tpu_custom_call" | custom-call | flops 2013265920 | bytes 2768896 | tf_op jit(solution)/shard_map/select/pallas_call | solution.py:37
  40.5 3.1 %collective-permute-done.13.refs_3_ = bf16[4,160,128]{2,1,0:T(8,128)(2,1)S(1)} collective-permute-done((bf16[4,160,128]{2,1,0:T(8,128)(2,1)S(1)}, bf16[4,160,128]{2,1,0:T(8,128)(2,1)S(1)}, u32[]{:S(2)}, u32[]{:S(2)}) %collective-permute-start.13) | collective-permute-done | bytes 163872 | tf_op jit(solution)/shard_map/ppermute | solution.py:522
  44.1 1.0 %collective-permute-start.15 = (bf16[2,160,128]{2,1,0:T(8,128)(2,1)S(1)}, bf16[2,160,128]{2,1,0:T(8,128)(2,1)S(1)}, u32[]{:S(2)}, u32[]{:S(2)}) collective-permute-start(bf16[2,160,128]{2,1,0:T(8,128)(2,1)S(1)} %get-tuple-element.76), channel_id=1, source_target_pairs={{0,2},{1,3},{2,0},{3,1},{4,6},{5,7},{6,4},{7,5},{8,10},{9,11},{10,... | collective-permute-start | bytes 245768 | tf_op jit(solution)/shard_map/ppermute | solution.py:522
  45.2 3.0 %collective-permute-done.14.refs_1_ = bf16[2,160,128]{2,1,0:T(8,128)(2,1)S(1)} collective-permute-done((bf16[2,160,128]{2,1,0:T(8,128)(2,1)S(1)}, bf16[2,160,128]{2,1,0:T(8,128)(2,1)S(1)}, u32[]{:S(2)}, u32[]{:S(2)}) %collective-permute-start.14) | collective-permute-done | bytes 81952 | tf_op jit(solution)/shard_map/ppermute | solution.py:522
  48.6 1.1 %collective-permute-start.22 = (bf16[128,1024]{1,0:T(8,128)(2,1)S(1)}, bf16[128,1024]{1,0:T(8,128)(2,1)S(1)}, u32[]{:S(2)}, u32[]{:S(2)}) collective-permute-start(bf16[128,1024]{1,0:T(8,128)(2,1)S(1)} %get-tuple-element.83.refs_0_.refs_1_), channel_id=1, source_target_pairs={{0,2},{1,3},{2,0},{3,1},{4,6},{5,7},{6,4},{7,5},{8,10},{9,11},{10,... | collective-permute-start | bytes 786440 | tf_op jit(solution)/shard_map/ppermute | solution.py:522
  49.7 3.0 %collective-permute-start.16 = (bf16[1,320,128]{2,1,0:T(8,128)(2,1)S(1)}, bf16[1,320,128]{2,1,0:T(8,128)(2,1)S(1)}, u32[]{:S(2)}, u32[]{:S(2)}) collective-permute-start(bf16[1,320,128]{2,1,0:T(8,128)(2,1)S(1)} %get-tuple-element.78), channel_id=1, source_target_pairs={{0,8},{1,9},{2,10},{3,11},{4,12},{5,13},{6,14},{7,15},{8,0},{9,1},... | collective-permute-start | bytes 245768 | tf_op jit(solution)/shard_map/ppermute | solution.py:522
  53.4 1.7 %collective-permute-done.16.refs_1_ = bf16[1,320,128]{2,1,0:T(8,128)(2,1)S(1)} collective-permute-done((bf16[1,320,128]{2,1,0:T(8,128)(2,1)S(1)}, bf16[1,320,128]{2,1,0:T(8,128)(2,1)S(1)}, u32[]{:S(2)}, u32[]{:S(2)}) %collective-permute-start.16) | collective-permute-done | bytes 81952 | tf_op jit(solution)/shard_map/ppermute | solution.py:522
  55.6 1.0 %collective-permute-start.20 = (bf16[144,384]{1,0:T(8,128)(2,1)S(1)}, bf16[144,384]{1,0:T(8,128)(2,1)S(1)}, u32[]{:S(2)}, u32[]{:S(2)}) collective-permute-start(bf16[144,384]{1,0:T(8,128)(2,1)S(1)} %get-tuple-element.82.refs_1_), channel_id=1, source_target_pairs={{0,2},{1,3},{2,0},{3,1},{4,6},{5,7},{6,4},{7,5},{8,10},{9,11},{10,... | collective-permute-start | bytes 331784 | tf_op jit(solution)/shard_map/ppermute | solution.py:522
  58.0 1.7 %collective-permute-start.25 = (bf16[2,48,1024]{2,1,0:T(8,128)(2,1)S(1)}, bf16[2,48,1024]{2,1,0:T(8,128)(2,1)S(1)}, u32[]{:S(2)}, u32[]{:S(2)}) collective-permute-start(bf16[2,48,1024]{2,1,0:T(8,128)(2,1)S(1)} %get-tuple-element.88), channel_id=1, source_target_pairs={{0,4},{1,5},{2,6},{3,7},{4,0},{5,1},{6,2},{7,3},{8,12},{9,13},{10,... | collective-permute-start | bytes 589832 | tf_op jit(solution)/shard_map/ppermute | solution.py:522
  62.4 1.0 %conv_grad_first.1 = (f32[1,128,384]{2,1,0:T(8,128)S(1)}, f32[1,128,384]{2,1,0:T(8,128)S(1)}, bf16[1,128,384]{2,1,0:T(8,128)(2,1)S(1)}, bf16[1,128,384]{2,1,0:T(8,128)(2,1)S(1)}) custom-call(bf16[512,1024]{1,0:T(8,128)(2,1)S(1)} %get-tuple-element.68.refs_4_.refs_0_, bf16[144,384]{1,0:T(8,128)(2,1)S(1)} %get-tuple-element.82.refs_1_, ...), custom_call_target="tpu_custom_call" | custom-call | flops 402653184 | bytes 2080768 | tf_op jit(solution)/shard_map/conv_grad_first/pallas_call | solution.py:37
  63.4 1.6 %collective-permute-done.25.refs_1_ = bf16[2,48,1024]{2,1,0:T(8,128)(2,1)S(1)} collective-permute-done((bf16[2,48,1024]{2,1,0:T(8,128)(2,1)S(1)}, bf16[2,48,1024]{2,1,0:T(8,128)(2,1)S(1)}, u32[]{:S(2)}, u32[]{:S(2)}) %collective-permute-start.25) | collective-permute-done | bytes 196640 | tf_op jit(solution)/shard_map/ppermute | solution.py:522
  65.0 1.3 %collective-permute-done.18.refs_4_ = bf16[256,384]{1,0:T(8,128)(2,1)S(1)} collective-permute-done((bf16[256,384]{1,0:T(8,128)(2,1)S(1)}, bf16[256,384]{1,0:T(8,128)(2,1)S(1)}, u32[]{:S(2)}, u32[]{:S(2)}) %collective-permute-start.18) | collective-permute-done | bytes 196640 | tf_op jit(solution)/shard_map/ppermute | solution.py:522
  67.8 1.0 %conv_grad_second.1 = (f32[1,160,384]{2,1,0:T(8,128)S(1)}, f32[1,160,384]{2,1,0:T(8,128)S(1)}, bf16[1,288,384]{2,1,0:T(8,128)(2,1)S(1)}, bf16[1,160,384]{2,1,0:T(8,128)(2,1)S(1)}) custom-call(bf16[512,1024]{1,0:T(8,128)(2,1)S(1)} %get-tuple-element.68.refs_4_.refs_0_, bf16[192,512]{1,0:T(8,128)(2,1)S(1)} %get-tuple-element.69.refs_0_.refs_1_, ...), custom_call_target="tpu_custom_call" | custom-call | flops 402653184 | bytes 2965504 | tf_op jit(solution)/shard_map/conv_grad_second/pallas_call | solution.py:37
  69.5 2.9 %collective-permute-start.28 = (bf16[1,48,1024]{2,1,0:T(8,128)(2,1)S(1)}, bf16[1,48,1024]{2,1,0:T(8,128)(2,1)S(1)}, u32[]{:S(2)}, u32[]{:S(2)}) collective-permute-start(bf16[1,48,1024]{2,1,0:T(8,128)(2,1)S(1)} %get-tuple-element.94), channel_id=1, source_target_pairs={{0,8},{1,9},{2,10},{3,11},{4,12},{5,13},{6,14},{7,15},{8,0},{9,1},... | collective-permute-start | bytes 294920 | tf_op jit(solution)/shard_map/ppermute | solution.py:522
  72.3 2.2 %collective-permute-start.30 = (bf16[1,128,384]{2,1,0:T(8,128)(2,1)S(1)}, bf16[1,128,384]{2,1,0:T(8,128)(2,1)S(1)}, u32[]{:S(2)}, u32[]{:S(2)}) collective-permute-start(bf16[1,128,384]{2,1,0:T(8,128)(2,1)S(1)} %conv_send_on.3), channel_id=1, source_target_pairs={{0,8},{1,9},{2,10},{3,11},{4,12},{5,13},{6,14},{7,15},{8,0},{9,1},... | collective-permute-start | bytes 294920 | tf_op jit(solution)/shard_map/ppermute | solution.py:522
  75.2 2.5 %collective-permute-done.27.refs_1_ = bf16[1,160,384]{2,1,0:T(8,128)(2,1)S(1)} collective-permute-done((bf16[1,160,384]{2,1,0:T(8,128)(2,1)S(1)}, bf16[1,160,384]{2,1,0:T(8,128)(2,1)S(1)}, u32[]{:S(2)}, u32[]{:S(2)}) %collective-permute-start.27) | collective-permute-done | bytes 122912 | tf_op jit(solution)/shard_map/ppermute | solution.py:522
  78.0 4.8 %collective-permute-done.30.refs_6_.refs_2_ = bf16[1,128,384]{2,1,0:T(8,128)(2,1)S(1)} collective-permute-done((bf16[1,128,384]{2,1,0:T(8,128)(2,1)S(1)}, bf16[1,128,384]{2,1,0:T(8,128)(2,1)S(1)}, u32[]{:S(2)}, u32[]{:S(2)}) %collective-permute-start.30) | collective-permute-done | bytes 98336 | tf_op jit(solution)/shard_map/ppermute | solution.py:522
  82.8 2.1 %input_grad.1 = bf16[256,384]{1,0:T(8,128)(2,1)} custom-call(bf16[256,384]{1,0:T(8,128)(2,1)S(1)} %bitcast.10, bf16[144,384]{1,0:T(8,128)(2,1)S(1)} %get-tuple-element.82.refs_1_, bf16[256,384]{1,0:T(8,128)(2,1)S(1)} %get-tuple-element.81.refs_2_, bf16[144,384]{1,0:T(8,128)(2,1)S(1)} %collective-permute-done.20.refs_3_, ...), custom_call_target="tpu_custom_call" | custom-call | flops 7549747200 | bytes 4153344 | tf_op jit(solution)/shard_map/input_grad/pallas_call | solution.py:37
  84.8 1.0 %collective-permute-done.31.refs_1_.refs_2_ = bf16[1,288,384]{2,1,0:T(8,128)(2,1)S(1)} collective-permute-done((bf16[1,288,384]{2,1,0:T(8,128)(2,1)S(1)}, bf16[1,288,384]{2,1,0:T(8,128)(2,1)S(1)}, u32[]{:S(2)}, u32[]{:S(2)}) %collective-permute-start.31) | collective-permute-done | bytes 221216 | tf_op jit(solution)/shard_map/ppermute | solution.py:522
  (69 shorter events, 16.0 us)
Async XLA Ops:
  1.8 6.7 %collective-permute-start.1 = (bf16[32,384]{1,0:T(8,128)(2,1)S(1)}, bf16[32,384]{1,0:T(8,128)(2,1)S(1)}, u32[]{:S(2)}, u32[]{:S(2)}) collective-permute-start(bf16[32,384]{1,0:T(8,128)(2,1)S(1)} %get-tuple-element.57), channel_id=1, source_target_pairs={{2,4},{6,8},{10,12},{4,2},{8,6},{12,10},{3,5},{7,9},{11,13},{5,3},... | collective-permute-start | bytes 73736 | tf_op jit(solution)/shard_map/ppermute | solution.py:553
  2.6 7.7 %collective-permute-start = (bf16[32,384]{1,0:T(8,128)(2,1)S(1)}, bf16[32,384]{1,0:T(8,128)(2,1)S(1)}, u32[]{:S(2)}, u32[]{:S(2)}) collective-permute-start(bf16[32,384]{1,0:T(8,128)(2,1)S(1)} %get-tuple-element.57), channel_id=1, source_target_pairs={{0,2},{1,3},{2,0},{3,1},{4,6},{5,7},{6,4},{7,5},{8,10},{9,11},{10,... | collective-permute-start | bytes 73736 | tf_op jit(solution)/shard_map/ppermute | solution.py:522
  12.2 6.5 %collective-permute-start.4 = (bf16[320,128]{1,0:T(8,128)(2,1)S(1)}, bf16[320,128]{1,0:T(8,128)(2,1)S(1)}, u32[]{:S(2)}, u32[]{:S(2)}) collective-permute-start(bf16[320,128]{1,0:T(8,128)(2,1)S(1)} %get-tuple-element.60.refs_2_), channel_id=1, source_target_pairs={{0,12},{1,13},{2,14},{3,15},{4,8},{5,9},{6,10},{7,11},{8,4},{9,5},... | collective-permute-start | bytes 245768 | tf_op jit(solution)/shard_map/ppermute | solution.py:522
  16.2 5.9 %collective-permute-start.3 = (bf16[320,128]{1,0:T(8,128)(2,1)S(1)}, bf16[320,128]{1,0:T(8,128)(2,1)S(1)}, u32[]{:S(2)}, u32[]{:S(2)}) collective-permute-start(bf16[320,128]{1,0:T(8,128)(2,1)S(1)} %get-tuple-element.60.refs_2_), channel_id=1, source_target_pairs={{0,8},{1,9},{2,10},{3,11},{4,12},{5,13},{6,14},{7,15},{8,0},{9,1},... | collective-permute-start | bytes 245768 | tf_op jit(solution)/shard_map/ppermute | solution.py:522
  16.2 7.2 %collective-permute-start.2 = (bf16[320,128]{1,0:T(8,128)(2,1)S(1)}, bf16[320,128]{1,0:T(8,128)(2,1)S(1)}, u32[]{:S(2)}, u32[]{:S(2)}) collective-permute-start(bf16[320,128]{1,0:T(8,128)(2,1)S(1)} %get-tuple-element.60.refs_2_), channel_id=1, source_target_pairs={{0,4},{1,5},{2,6},{3,7},{4,0},{5,1},{6,2},{7,3},{8,12},{9,13},{10,... | collective-permute-start | bytes 245768 | tf_op jit(solution)/shard_map/ppermute | solution.py:522
  16.9 8.0 %collective-permute-start.5 = (bf16[320,128]{1,0:T(8,128)(2,1)S(1)}, bf16[320,128]{1,0:T(8,128)(2,1)S(1)}, u32[]{:S(2)}, u32[]{:S(2)}) collective-permute-start(bf16[320,128]{1,0:T(8,128)(2,1)S(1)} %get-tuple-element.60.refs_2_), channel_id=1, source_target_pairs={{0,2},{1,3},{2,0},{3,1},{4,6},{5,7},{6,4},{7,5},{8,10},{9,11},{10,... | collective-permute-start | bytes 245768 | tf_op jit(solution)/shard_map/ppermute | solution.py:522
  18.7 6.2 %collective-permute-start.8 = (bf16[320,128]{1,0:T(8,128)(2,1)S(1)}, bf16[320,128]{1,0:T(8,128)(2,1)S(1)}, u32[]{:S(2)}, u32[]{:S(2)}) collective-permute-start(bf16[320,128]{1,0:T(8,128)(2,1)S(1)} %collective-permute-done.4.refs_5_), channel_id=1, source_target_pairs={{0,2},{1,3},{2,0},{3,1},{4,6},{5,7},{6,4},{7,5},{8,10},{9,11},{10,... | collective-permute-start | bytes 245768 | tf_op jit(solution)/shard_map/ppermute | solution.py:522
  22.1 4.5 %collective-permute-start.7 = (bf16[320,128]{1,0:T(8,128)(2,1)S(1)}, bf16[320,128]{1,0:T(8,128)(2,1)S(1)}, u32[]{:S(2)}, u32[]{:S(2)}) collective-permute-start(bf16[320,128]{1,0:T(8,128)(2,1)S(1)} %collective-permute-done.3.refs_4_), channel_id=1, source_target_pairs={{0,2},{1,3},{2,0},{3,1},{4,6},{5,7},{6,4},{7,5},{8,10},{9,11},{10,... | collective-permute-start | bytes 245768 | tf_op jit(solution)/shard_map/ppermute | solution.py:522
  23.4 4.4 %collective-permute-start.6 = (bf16[320,128]{1,0:T(8,128)(2,1)S(1)}, bf16[320,128]{1,0:T(8,128)(2,1)S(1)}, u32[]{:S(2)}, u32[]{:S(2)}) collective-permute-start(bf16[320,128]{1,0:T(8,128)(2,1)S(1)} %collective-permute-done.2.refs_3_), channel_id=1, source_target_pairs={{0,2},{1,3},{2,0},{3,1},{4,6},{5,7},{6,4},{7,5},{8,10},{9,11},{10,... | collective-permute-start | bytes 245768 | tf_op jit(solution)/shard_map/ppermute | solution.py:522
  27.9 8.5 %collective-permute-start.10 = (bf16[480,384]{1,0:T(8,128)(2,1)S(1)}, bf16[480,384]{1,0:T(8,128)(2,1)S(1)}, u32[]{:S(2)}, u32[]{:S(2)}) collective-permute-start(bf16[480,384]{1,0:T(8,128)(2,1)S(1)} %get-tuple-element.65.refs_1_), channel_id=1, source_target_pairs={{0,2},{1,3},{2,0},{3,1},{4,6},{5,7},{6,4},{7,5},{8,10},{9,11},{10,... | collective-permute-start | bytes 1105928 | tf_op jit(solution)/shard_map/ppermute | solution.py:522
  28.7 9.0 %collective-permute-start.9 = (bf16[480,384]{1,0:T(8,128)(2,1)S(1)}, bf16[480,384]{1,0:T(8,128)(2,1)S(1)}, u32[]{:S(2)}, u32[]{:S(2)}) collective-permute-start(bf16[480,384]{1,0:T(8,128)(2,1)S(1)} %get-tuple-element.65.refs_1_), channel_id=1, source_target_pairs={{0,1},{1,0},{2,3},{3,2},{4,5},{5,4},{6,7},{7,6},{8,9},{9,8},{10,11... | collective-permute-start | bytes 1105928 | tf_op jit(solution)/shard_map/ppermute | solution.py:522
  36.4 1.7 %collective-permute-start.11 = (bf16[480,384]{1,0:T(8,128)(2,1)S(1)}, bf16[480,384]{1,0:T(8,128)(2,1)S(1)}, u32[]{:S(2)}, u32[]{:S(2)}) collective-permute-start(bf16[480,384]{1,0:T(8,128)(2,1)S(1)} %collective-permute-done.10.refs_3_), channel_id=1, source_target_pairs={{0,1},{1,0},{2,3},{3,2},{4,5},{5,4},{6,7},{7,6},{8,9},{9,8},{10,11... | collective-permute-start | bytes 1105928 | tf_op jit(solution)/shard_map/ppermute | solution.py:522
  36.4 7.2 %collective-permute-start.12 = (bf16[4,160,128]{2,1,0:T(8,128)(2,1)S(1)}, bf16[4,160,128]{2,1,0:T(8,128)(2,1)S(1)}, u32[]{:S(2)}, u32[]{:S(2)}) collective-permute-start(bf16[4,160,128]{2,1,0:T(8,128)(2,1)S(1)} %get-tuple-element.66), channel_id=1, source_target_pairs={{0,2},{1,3},{2,0},{3,1},{4,6},{5,7},{6,4},{7,5},{8,10},{9,11},{10,... | collective-permute-start | bytes 491528 | tf_op jit(solution)/shard_map/ppermute | solution.py:522
  37.2 6.3 %collective-permute-start.13 = (bf16[4,160,128]{2,1,0:T(8,128)(2,1)S(1)}, bf16[4,160,128]{2,1,0:T(8,128)(2,1)S(1)}, u32[]{:S(2)}, u32[]{:S(2)}) collective-permute-start(bf16[4,160,128]{2,1,0:T(8,128)(2,1)S(1)} %get-tuple-element.72), channel_id=1, source_target_pairs={{0,4},{1,5},{2,6},{3,7},{4,0},{5,1},{6,2},{7,3},{8,12},{9,13},{10,... | collective-permute-start | bytes 491528 | tf_op jit(solution)/shard_map/ppermute | solution.py:522
  43.6 4.5 %collective-permute-start.14 = (bf16[2,160,128]{2,1,0:T(8,128)(2,1)S(1)}, bf16[2,160,128]{2,1,0:T(8,128)(2,1)S(1)}, u32[]{:S(2)}, u32[]{:S(2)}) collective-permute-start(bf16[2,160,128]{2,1,0:T(8,128)(2,1)S(1)} %get-tuple-element.74), channel_id=1, source_target_pairs={{0,4},{1,5},{2,6},{3,7},{4,0},{5,1},{6,2},{7,3},{8,12},{9,13},{10,... | collective-permute-start | bytes 245768 | tf_op jit(solution)/shard_map/ppermute | solution.py:522
  44.1 4.4 %collective-permute-start.15 = (bf16[2,160,128]{2,1,0:T(8,128)(2,1)S(1)}, bf16[2,160,128]{2,1,0:T(8,128)(2,1)S(1)}, u32[]{:S(2)}, u32[]{:S(2)}) collective-permute-start(bf16[2,160,128]{2,1,0:T(8,128)(2,1)S(1)} %get-tuple-element.76), channel_id=1, source_target_pairs={{0,2},{1,3},{2,0},{3,1},{4,6},{5,7},{6,4},{7,5},{8,10},{9,11},{10,... | collective-permute-start | bytes 245768 | tf_op jit(solution)/shard_map/ppermute | solution.py:522
  48.6 6.9 %collective-permute-start.22 = (bf16[128,1024]{1,0:T(8,128)(2,1)S(1)}, bf16[128,1024]{1,0:T(8,128)(2,1)S(1)}, u32[]{:S(2)}, u32[]{:S(2)}) collective-permute-start(bf16[128,1024]{1,0:T(8,128)(2,1)S(1)} %get-tuple-element.83.refs_0_.refs_1_), channel_id=1, source_target_pairs={{0,2},{1,3},{2,0},{3,1},{4,6},{5,7},{6,4},{7,5},{8,10},{9,11},{10,... | collective-permute-start | bytes 786440 | tf_op jit(solution)/shard_map/ppermute | solution.py:522
  49.7 5.4 %collective-permute-start.16 = (bf16[1,320,128]{2,1,0:T(8,128)(2,1)S(1)}, bf16[1,320,128]{2,1,0:T(8,128)(2,1)S(1)}, u32[]{:S(2)}, u32[]{:S(2)}) collective-permute-start(bf16[1,320,128]{2,1,0:T(8,128)(2,1)S(1)} %get-tuple-element.78), channel_id=1, source_target_pairs={{0,8},{1,9},{2,10},{3,11},{4,12},{5,13},{6,14},{7,15},{8,0},{9,1},... | collective-permute-start | bytes 245768 | tf_op jit(solution)/shard_map/ppermute | solution.py:522
  53.3 3.3 %collective-permute-start.21 = (bf16[128,1024]{1,0:T(8,128)(2,1)S(1)}, bf16[128,1024]{1,0:T(8,128)(2,1)S(1)}, u32[]{:S(2)}, u32[]{:S(2)}) collective-permute-start(bf16[128,1024]{1,0:T(8,128)(2,1)S(1)} %get-tuple-element.83.refs_0_.refs_1_), channel_id=1, source_target_pairs={{0,1},{1,0},{2,3},{3,2},{4,5},{5,4},{6,7},{7,6},{8,9},{9,8},{10,11... | collective-permute-start | bytes 786440 | tf_op jit(solution)/shard_map/ppermute | solution.py:522
  55.6 1.6 %collective-permute-start.23 = (bf16[128,1024]{1,0:T(8,128)(2,1)S(1)}, bf16[128,1024]{1,0:T(8,128)(2,1)S(1)}, u32[]{:S(2)}, u32[]{:S(2)}) collective-permute-start(bf16[128,1024]{1,0:T(8,128)(2,1)S(1)} %collective-permute-done.22.refs_3_), channel_id=1, source_target_pairs={{0,1},{1,0},{2,3},{3,2},{4,5},{5,4},{6,7},{7,6},{8,9},{9,8},{10,11... | collective-permute-start | bytes 786440 | tf_op jit(solution)/shard_map/ppermute | solution.py:522
  55.6 5.5 %collective-permute-start.20 = (bf16[144,384]{1,0:T(8,128)(2,1)S(1)}, bf16[144,384]{1,0:T(8,128)(2,1)S(1)}, u32[]{:S(2)}, u32[]{:S(2)}) collective-permute-start(bf16[144,384]{1,0:T(8,128)(2,1)S(1)} %get-tuple-element.82.refs_1_), channel_id=1, source_target_pairs={{0,2},{1,3},{2,0},{3,1},{4,6},{5,7},{6,4},{7,5},{8,10},{9,11},{10,... | collective-permute-start | bytes 331784 | tf_op jit(solution)/shard_map/ppermute | solution.py:522
  58.0 7.0 %collective-permute-start.25 = (bf16[2,48,1024]{2,1,0:T(8,128)(2,1)S(1)}, bf16[2,48,1024]{2,1,0:T(8,128)(2,1)S(1)}, u32[]{:S(2)}, u32[]{:S(2)}) collective-permute-start(bf16[2,48,1024]{2,1,0:T(8,128)(2,1)S(1)} %get-tuple-element.88), channel_id=1, source_target_pairs={{0,4},{1,5},{2,6},{3,7},{4,0},{5,1},{6,2},{7,3},{8,12},{9,13},{10,... | collective-permute-start | bytes 589832 | tf_op jit(solution)/shard_map/ppermute | solution.py:522
  59.7 6.7 %collective-permute-start.18 = (bf16[256,384]{1,0:T(8,128)(2,1)S(1)}, bf16[256,384]{1,0:T(8,128)(2,1)S(1)}, u32[]{:S(2)}, u32[]{:S(2)}) collective-permute-start(bf16[256,384]{1,0:T(8,128)(2,1)S(1)} %get-tuple-element.81.refs_2_), channel_id=1, source_target_pairs={{0,2},{1,3},{2,0},{3,1},{4,6},{5,7},{6,4},{7,5},{8,10},{9,11},{10,... | collective-permute-start | bytes 589832 | tf_op jit(solution)/shard_map/ppermute | solution.py:522
  61.1 1.3 %collective-permute-start.24 = (bf16[144,384]{1,0:T(8,128)(2,1)S(1)}, bf16[144,384]{1,0:T(8,128)(2,1)S(1)}, u32[]{:S(2)}, u32[]{:S(2)}) collective-permute-start(bf16[144,384]{1,0:T(8,128)(2,1)S(1)} %collective-permute-done.20.refs_3_), channel_id=1, source_target_pairs={{0,1},{1,0},{2,3},{3,2},{4,5},{5,4},{6,7},{7,6},{8,9},{9,8},{10,11... | collective-permute-start | bytes 331784 | tf_op jit(solution)/shard_map/ppermute | solution.py:522
  61.1 5.9 %collective-permute-start.17 = (bf16[256,384]{1,0:T(8,128)(2,1)S(1)}, bf16[256,384]{1,0:T(8,128)(2,1)S(1)}, u32[]{:S(2)}, u32[]{:S(2)}) collective-permute-start(bf16[256,384]{1,0:T(8,128)(2,1)S(1)} %get-tuple-element.81.refs_2_), channel_id=1, source_target_pairs={{0,1},{1,0},{2,3},{3,2},{4,5},{5,4},{6,7},{7,6},{8,9},{9,8},{10,11... | collective-permute-start | bytes 589832 | tf_op jit(solution)/shard_map/ppermute | solution.py:522
  66.4 1.4 %collective-permute-start.26 = (bf16[256,384]{1,0:T(8,128)(2,1)S(1)}, bf16[256,384]{1,0:T(8,128)(2,1)S(1)}, u32[]{:S(2)}, u32[]{:S(2)}) collective-permute-start(bf16[256,384]{1,0:T(8,128)(2,1)S(1)} %collective-permute-done.18.refs_4_), channel_id=1, source_target_pairs={{0,1},{1,0},{2,3},{3,2},{4,5},{5,4},{6,7},{7,6},{8,9},{9,8},{10,11... | collective-permute-start | bytes 589832 | tf_op jit(solution)/shard_map/ppermute | solution.py:522
  66.4 5.9 %collective-permute-start.29 = (bf16[1,128,384]{2,1,0:T(8,128)(2,1)S(1)}, bf16[1,128,384]{2,1,0:T(8,128)(2,1)S(1)}, u32[]{:S(2)}, u32[]{:S(2)}) collective-permute-start(bf16[1,128,384]{2,1,0:T(8,128)(2,1)S(1)} %get-tuple-element.96), channel_id=1, source_target_pairs={{0,4},{1,5},{2,6},{3,7},{4,0},{5,1},{6,2},{7,3},{8,12},{9,13},{10,... | collective-permute-start | bytes 294920 | tf_op jit(solution)/shard_map/ppermute | solution.py:522
  68.8 8.8 %collective-permute-start.27 = (bf16[1,160,384]{2,1,0:T(8,128)(2,1)S(1)}, bf16[1,160,384]{2,1,0:T(8,128)(2,1)S(1)}, u32[]{:S(2)}, u32[]{:S(2)}) collective-permute-start(bf16[1,160,384]{2,1,0:T(8,128)(2,1)S(1)} %get-tuple-element.93), channel_id=1, source_target_pairs={{0,4},{1,5},{2,6},{3,7},{4,0},{5,1},{6,2},{7,3},{8,12},{9,13},{10,... | collective-permute-start | bytes 368648 | tf_op jit(solution)/shard_map/ppermute | solution.py:522
  69.5 8.5 %collective-permute-start.28 = (bf16[1,48,1024]{2,1,0:T(8,128)(2,1)S(1)}, bf16[1,48,1024]{2,1,0:T(8,128)(2,1)S(1)}, u32[]{:S(2)}, u32[]{:S(2)}) collective-permute-start(bf16[1,48,1024]{2,1,0:T(8,128)(2,1)S(1)} %get-tuple-element.94), channel_id=1, source_target_pairs={{0,8},{1,9},{2,10},{3,11},{4,12},{5,13},{6,14},{7,15},{8,0},{9,1},... | collective-permute-start | bytes 294920 | tf_op jit(solution)/shard_map/ppermute | solution.py:522
  72.3 10.4 %collective-permute-start.30 = (bf16[1,128,384]{2,1,0:T(8,128)(2,1)S(1)}, bf16[1,128,384]{2,1,0:T(8,128)(2,1)S(1)}, u32[]{:S(2)}, u32[]{:S(2)}) collective-permute-start(bf16[1,128,384]{2,1,0:T(8,128)(2,1)S(1)} %conv_send_on.3), channel_id=1, source_target_pairs={{0,8},{1,9},{2,10},{3,11},{4,12},{5,13},{6,14},{7,15},{8,0},{9,1},... | collective-permute-start | bytes 294920 | tf_op jit(solution)/shard_map/ppermute | solution.py:522
  74.5 11.3 %collective-permute-start.31 = (bf16[1,288,384]{2,1,0:T(8,128)(2,1)S(1)}, bf16[1,288,384]{2,1,0:T(8,128)(2,1)S(1)}, u32[]{:S(2)}, u32[]{:S(2)}) collective-permute-start(bf16[1,288,384]{2,1,0:T(8,128)(2,1)S(1)} %get-tuple-element.98), channel_id=1, source_target_pairs={{0,4},{1,5},{2,6},{3,7},{4,0},{5,1},{6,2},{7,3},{8,12},{9,13},{10,... | collective-permute-start | bytes 663560 | tf_op jit(solution)/shard_map/ppermute | solution.py:522
  77.7 8.2 %collective-permute-start.32 = (bf16[1,160,384]{2,1,0:T(8,128)(2,1)S(1)}, bf16[1,160,384]{2,1,0:T(8,128)(2,1)S(1)}, u32[]{:S(2)}, u32[]{:S(2)}) collective-permute-start(bf16[1,160,384]{2,1,0:T(8,128)(2,1)S(1)} %conv_send_on.2), channel_id=1, source_target_pairs={{0,8},{1,9},{2,10},{3,11},{4,12},{5,13},{6,14},{7,15},{8,0},{9,1},... | collective-permute-start | bytes 368648 | tf_op jit(solution)/shard_map/ppermute | solution.py:522
  (9 other events, 101.8 us)

commit v11 on v10

--- a/solution.py
+++ b/solution.py
@@ -132,12 +132,13 @@
     return round_up(-(-rows * LANES // columns), 16)
 
 
-def query_kernel(normed, wq, early, out, message, own, *, order, rows, padded, scale):
+def query_kernel(normed, wq, early, out, near, core, own, *, order, rows, padded, scale):
     width = normed.shape[1]
     value = normed[...]
     out[...] = (dot(value, wq[...]) * scale).astype(BF)
-    at, channels = early.shape
-    message[:at] = early[...]
+    ext, channels = early.shape
+    near[:ext] = early[...]
+    core[:ext] = early[...]
     count = len(order) * padded
     step = split_rows(count, channels)
     for i in range(4):
@@ -147,10 +148,10 @@
         if i == 0:
             own[...] = part
             continue
+        message, at = ((core, ext), (near, ext), (near, ext + step))[i - 1]
         for c in range(channels // LANES):
             piece = part[c * step : min((c + 1) * step, count)]
             message[at : at + piece.shape[0], c * LANES : (c + 1) * LANES] = piece
-        at += step
 
 
 def by_eight(rows):
@@ -313,7 +314,7 @@
     step = split_rows(count, channels)
     norm_out[:, :tokens] = own[...]
     for i in range(1, 4):
-        at = 2 * ext + (i - 1) * step
+        at = 2 * ext + (i // 3) * step
         for c in range(channels // LANES):
             end = min((c + 1) * step, count)
             piece = blocks[i][at : at + end - c * step, c * LANES : (c + 1) * LANES]
@@ -565,23 +566,29 @@
         flops=2 * positions * taps * channels * width,
         name="front",
     )
-    near_kv = [kv] + [swap(kv, 2 * k) for k in range(1, groups)]
+    parts = [0, *range(2, groups), 1]
+    near_kv = [swap(kv, 2 * k) if k else kv for k in parts]
     far_kv = [swap(block, 1) for block in near_kv]
     picked = (groups * norm_pad, tokens)
-    rows = 2 * ext + 3 * split_rows(picked[0], channels)
-    queries, early, pick_own = run(
+    rows = split_rows(picked[0], channels)
+    queries, to_near, to_core, pick_own = run(
         lambda *refs: query_kernel(
             *refs, order=order, rows=norm_rows, padded=norm_pad, scale=scale
         ),
-        [((tokens, heads * key_size), BF), ((rows, channels), BF), (picked, BF)],
+        [
+            ((tokens, heads * key_size), BF),
+            ((2 * ext + 2 * rows, channels), BF),
+            ((2 * ext + rows, channels), BF),
+            (picked, BF),
+        ],
         [normed, wq, early],
         flops=4 * tokens * width * heads * key_size,
         name="queries",
         after=near_kv[1:],
     )
-    early = held(early, *far_kv)
+    to_near, to_core = held(to_near, *far_kv), held(to_core, *far_kv)
     length = devices * tokens
-    masks = [2 * k for k in range(groups)] + [2 * k + 1 for k in range(groups)]
+    masks = [2 * k for k in parts] + [2 * k + 1 for k in parts]
     half_block = (groups, 5 * tokens // 4, key_size)
     slots = 2 if length <= 2048 else 1
     attended, query_cot, keep_a, send_a, keep_b, send_b = run(
@@ -615,7 +622,8 @@
         name="attend",
     )
     in_a, in_b = swap(send_a, 1), swap(send_b, 2)
-    early_blocks = quad(early, send_a)
+    early_near = swap(to_near, 1)
+    early_blocks = [early, swap(to_core, 0, 1), early_near, swap(held(early_near, send_a), 0, 1)]
     conv_pick, norm_pick = run(
         lambda *refs: select_kernel(*refs, order=order, rows=conv_rows, padded=conv_pad),
         [((groups * conv_pad, 8 * tokens), BF), ((groups * norm_pad, 4 * tokens), BF)],

time: 86.9 us -> 86.3 us (level)
  waiting for transfers between devices: 29.6 us -> 28.7 us
  transfers between devices with their start and end apart: 33 -> 33, of which waited for: 21 -> 18; matrix products, arithmetic and copies ran while one was open for 0% -> 0% of each run, Pallas kernels for 18% -> 18%
where the time goes in v11:
time: 86.3 us; the launch traced here: 86.2 us
  starting transfers between devices  37.2 us (43%)
  waiting for transfers between devices  28.7 us (33%)
  Pallas kernels  18.5 us (21%)
  local copies, waits for them, and re-layouts  0.96 us (1%)
    ppermute x32, starting transfers between devices, swap(): lax.ppermute(value, both_axes, [(i, i ^ mask) for i in range(owners)])  36.4 us
    ppermute x32, waiting for transfers between devices, swap(): lax.ppermute(value, both_axes, [(i, i ^ mask) for i in range(owners)])  28.7 us
    pallas_call x18, Pallas kernels, run(): pl.pallas_call(whole, out_shape=[jax.ShapeDtypeStruct(s, t) for s, t in o...  18.5 us
  transfers between devices with their start and end apart: 33, of which 18 were waited for; matrix products, arithmetic and copies ran while one was open for 0% of the time, Pallas kernels for 18%

profile of v11, /device:TPU:0, one launch (start us, length us, event | category | flops | bytes accessed | tf_op | source)
XLA Modules:
  0.0 86.2 jit_solution(9544936143835699877)
XLA Ops:
  2.6 5.9 %collective-permute-start = (bf16[32,384]{1,0:T(8,128)(2,1)S(1)}, bf16[32,384]{1,0:T(8,128)(2,1)S(1)}, u32[]{:S(2)}, u32[]{:S(2)}) collective-permute-start(bf16[32,384]{1,0:T(8,128)(2,1)S(1)} %get-tuple-element.59), channel_id=1, source_target_pairs={{0,2},{1,3},{2,0},{3,1},{4,6},{5,7},{6,4},{7,5},{8,10},{9,11},{10,... | collective-permute-start | bytes 73736 | tf_op jit(solution)/shard_map/ppermute | solution.py:523
  8.5 1.8 %collective-permute-done.refs_1_ = bf16[32,384]{1,0:T(8,128)(2,1)S(1)} collective-permute-done((bf16[32,384]{1,0:T(8,128)(2,1)S(1)}, bf16[32,384]{1,0:T(8,128)(2,1)S(1)}, u32[]{:S(2)}, u32[]{:S(2)}) %collective-permute-start) | collective-permute-done | bytes 24608 | tf_op jit(solution)/shard_map/ppermute | solution.py:523
  10.3 1.9 %front.1 = (bf16[320,128]{1,0:T(8,128)(2,1)S(1)}, bf16[288,384]{1,0:T(8,128)(2,1)S(1)}, bf16[128,768]{1,0:T(8,128)(2,1)S(1)}, f32[128,768]{1,0:T(8,128)S(1)}) custom-call(f32[3,304,128]{2,1,0:T(8,128)S(1)} %get-tuple-element.58.refs_0_, bf16[32,384]{1,0:T(8,128)(2,1)S(1)} %collective-permute-done.refs_1_, ...), custom_call_target="tpu_custom_call" | custom-call | flops 754974720 | bytes 4852736 | tf_op jit(solution)/shard_map/front/pallas_call | solution.py:37
  12.2 2.0 %collective-permute-start.4 = (bf16[320,128]{1,0:T(8,128)(2,1)S(1)}, bf16[320,128]{1,0:T(8,128)(2,1)S(1)}, u32[]{:S(2)}, u32[]{:S(2)}) collective-permute-start(bf16[320,128]{1,0:T(8,128)(2,1)S(1)} %get-tuple-element.62.refs_2_), channel_id=1, source_target_pairs={{0,4},{1,5},{2,6},{3,7},{4,0},{5,1},{6,2},{7,3},{8,12},{9,13},{10,... | collective-permute-start | bytes 245768 | tf_op jit(solution)/shard_map/ppermute | solution.py:523
  14.2 2.5 %collective-permute-start.3 = (bf16[320,128]{1,0:T(8,128)(2,1)S(1)}, bf16[320,128]{1,0:T(8,128)(2,1)S(1)}, u32[]{:S(2)}, u32[]{:S(2)}) collective-permute-start(bf16[320,128]{1,0:T(8,128)(2,1)S(1)} %get-tuple-element.62.refs_2_), channel_id=1, source_target_pairs={{0,12},{1,13},{2,14},{3,15},{4,8},{5,9},{6,10},{7,11},{8,4},{9,5},... | collective-permute-start | bytes 245768 | tf_op jit(solution)/shard_map/ppermute | solution.py:523
  16.8 1.5 %collective-permute-start.5 = (bf16[320,128]{1,0:T(8,128)(2,1)S(1)}, bf16[320,128]{1,0:T(8,128)(2,1)S(1)}, u32[]{:S(2)}, u32[]{:S(2)}) collective-permute-start(bf16[320,128]{1,0:T(8,128)(2,1)S(1)} %get-tuple-element.62.refs_2_), channel_id=1, source_target_pairs={{0,2},{1,3},{2,0},{3,1},{4,6},{5,7},{6,4},{7,5},{8,10},{9,11},{10,... | collective-permute-start | bytes 245768 | tf_op jit(solution)/shard_map/ppermute | solution.py:523
  18.3 1.3 %collective-permute-start.8 = (bf16[320,128]{1,0:T(8,128)(2,1)S(1)}, bf16[320,128]{1,0:T(8,128)(2,1)S(1)}, u32[]{:S(2)}, u32[]{:S(2)}) collective-permute-start(bf16[320,128]{1,0:T(8,128)(2,1)S(1)} %collective-permute-done.4.refs_5_), channel_id=1, source_target_pairs={{0,2},{1,3},{2,0},{3,1},{4,6},{5,7},{6,4},{7,5},{8,10},{9,11},{10,... | collective-permute-start | bytes 245768 | tf_op jit(solution)/shard_map/ppermute | solution.py:523
  19.6 1.2 %collective-permute-done.3.refs_4_ = bf16[320,128]{1,0:T(8,128)(2,1)S(1)} collective-permute-done((bf16[320,128]{1,0:T(8,128)(2,1)S(1)}, bf16[320,128]{1,0:T(8,128)(2,1)S(1)}, u32[]{:S(2)}, u32[]{:S(2)}) %collective-permute-start.3) | collective-permute-done | bytes 81952 | tf_op jit(solution)/shard_map/ppermute | solution.py:523
  20.8 1.4 %collective-permute-start.7 = (bf16[320,128]{1,0:T(8,128)(2,1)S(1)}, bf16[320,128]{1,0:T(8,128)(2,1)S(1)}, u32[]{:S(2)}, u32[]{:S(2)}) collective-permute-start(bf16[320,128]{1,0:T(8,128)(2,1)S(1)} %collective-permute-done.3.refs_4_), channel_id=1, source_target_pairs={{0,2},{1,3},{2,0},{3,1},{4,6},{5,7},{6,4},{7,5},{8,10},{9,11},{10,... | collective-permute-start | bytes 245768 | tf_op jit(solution)/shard_map/ppermute | solution.py:523
  22.2 1.1 %collective-permute-done.2.refs_3_ = bf16[320,128]{1,0:T(8,128)(2,1)S(1)} collective-permute-done((bf16[320,128]{1,0:T(8,128)(2,1)S(1)}, bf16[320,128]{1,0:T(8,128)(2,1)S(1)}, u32[]{:S(2)}, u32[]{:S(2)}) %collective-permute-start.2) | collective-permute-done | bytes 81952 | tf_op jit(solution)/shard_map/ppermute | solution.py:523
  23.3 1.2 %collective-permute-start.6 = (bf16[320,128]{1,0:T(8,128)(2,1)S(1)}, bf16[320,128]{1,0:T(8,128)(2,1)S(1)}, u32[]{:S(2)}, u32[]{:S(2)}) collective-permute-start(bf16[320,128]{1,0:T(8,128)(2,1)S(1)} %collective-permute-done.2.refs_3_), channel_id=1, source_target_pairs={{0,2},{1,3},{2,0},{3,1},{4,6},{5,7},{6,4},{7,5},{8,10},{9,11},{10,... | collective-permute-start | bytes 245768 | tf_op jit(solution)/shard_map/ppermute | solution.py:523
  25.8 1.9 %collective-permute-done.6.refs_7_ = bf16[320,128]{1,0:T(8,128)(2,1)S(1)} collective-permute-done((bf16[320,128]{1,0:T(8,128)(2,1)S(1)}, bf16[320,128]{1,0:T(8,128)(2,1)S(1)}, u32[]{:S(2)}, u32[]{:S(2)}) %collective-permute-start.6) | collective-permute-done | bytes 81952 | tf_op jit(solution)/shard_map/ppermute | solution.py:523
  27.7 1.2 %collective-permute-start.10 = (bf16[416,384]{1,0:T(8,128)(2,1)S(1)}, bf16[416,384]{1,0:T(8,128)(2,1)S(1)}, u32[]{:S(2)}, u32[]{:S(2)}) collective-permute-start(bf16[416,384]{1,0:T(8,128)(2,1)S(1)} %get-tuple-element.69), channel_id=1, source_target_pairs={{0,2},{1,3},{2,0},{3,1},{4,6},{5,7},{6,4},{7,5},{8,10},{9,11},{10,... | collective-permute-start | bytes 958472 | tf_op jit(solution)/shard_map/ppermute | solution.py:523
  28.9 6.4 %attend.1 = (bf16[128,1536]{1,0:T(8,128)(2,1)}, bf16[128,1024]{1,0:T(8,128)(2,1)S(1)}, f32[4,160,128]{2,1,0:T(8,128)S(1)}, bf16[4,160,128]{2,1,0:T(8,128)(2,1)S(...) custom-call(bf16[128,1024]{1,0:T(8,128)(2,1)S(1)} %get-tuple-element.63.refs_0_, ...), custom_call_target="tpu_custom_call" | custom-call | flops 2013265920 | bytes 2949120 | tf_op jit(solution)/shard_map/attend/pallas_call | solution.py:37
  35.9 1.4 %collective-permute-start.12 = (bf16[4,160,128]{2,1,0:T(8,128)(2,1)S(1)}, bf16[4,160,128]{2,1,0:T(8,128)(2,1)S(1)}, u32[]{:S(2)}, u32[]{:S(2)}) collective-permute-start(bf16[4,160,128]{2,1,0:T(8,128)(2,1)S(1)} %get-tuple-element.70), channel_id=1, source_target_pairs={{0,2},{1,3},{2,0},{3,1},{4,6},{5,7},{6,4},{7,5},{8,10},{9,11},{10,... | collective-permute-start | bytes 491528 | tf_op jit(solution)/shard_map/ppermute | solution.py:523
  38.1 2.4 %select.1 = (bf16[512,1024]{1,0:T(8,128)(2,1)S(1)}, bf16[192,512]{1,0:T(8,128)(2,1)S(1)}) custom-call(bf16[192,128]{1,0:T(8,128)(2,1)S(1)} %get-tuple-element.65.refs_0_, bf16[288,384]{1,0:T(8,128)(2,1)S(1)} %get-tuple-element.61.refs_2_.refs_1_, bf16[352,384]{1,0:T(8,128)(2,1)S(1)} %collective-permute-done.9.refs_2_, ...), custom_call_target="tpu_custom_call" | custom-call | flops 2013265920 | bytes 2424832 | tf_op jit(solution)/shard_map/select/pallas_call | solution.py:37
  40.6 2.5 %collective-permute-done.13.refs_3_ = bf16[4,160,128]{2,1,0:T(8,128)(2,1)S(1)} collective-permute-done((bf16[4,160,128]{2,1,0:T(8,128)(2,1)S(1)}, bf16[4,160,128]{2,1,0:T(8,128)(2,1)S(1)}, u32[]{:S(2)}, u32[]{:S(2)}) %collective-permute-start.13) | collective-permute-done | bytes 163872 | tf_op jit(solution)/shard_map/ppermute | solution.py:523
  44.8 2.9 %collective-permute-done.14.refs_1_ = bf16[2,160,128]{2,1,0:T(8,128)(2,1)S(1)} collective-permute-done((bf16[2,160,128]{2,1,0:T(8,128)(2,1)S(1)}, bf16[2,160,128]{2,1,0:T(8,128)(2,1)S(1)}, u32[]{:S(2)}, u32[]{:S(2)}) %collective-permute-start.14) | collective-permute-done | bytes 81952 | tf_op jit(solution)/shard_map/ppermute | solution.py:523
  49.4 2.1 %collective-permute-start.16 = (bf16[1,320,128]{2,1,0:T(8,128)(2,1)S(1)}, bf16[1,320,128]{2,1,0:T(8,128)(2,1)S(1)}, u32[]{:S(2)}, u32[]{:S(2)}) collective-permute-start(bf16[1,320,128]{2,1,0:T(8,128)(2,1)S(1)} %get-tuple-element.82), channel_id=1, source_target_pairs={{0,8},{1,9},{2,10},{3,11},{4,12},{5,13},{6,14},{7,15},{8,0},{9,1},... | collective-permute-start | bytes 245768 | tf_op jit(solution)/shard_map/ppermute | solution.py:523
  52.1 3.4 %collective-permute-done.16.refs_1_ = bf16[1,320,128]{2,1,0:T(8,128)(2,1)S(1)} collective-permute-done((bf16[1,320,128]{2,1,0:T(8,128)(2,1)S(1)}, bf16[1,320,128]{2,1,0:T(8,128)(2,1)S(1)}, u32[]{:S(2)}, u32[]{:S(2)}) %collective-permute-start.16) | collective-permute-done | bytes 81952 | tf_op jit(solution)/shard_map/ppermute | solution.py:523
  56.1 1.4 %collective-permute-start.20 = (bf16[144,384]{1,0:T(8,128)(2,1)S(1)}, bf16[144,384]{1,0:T(8,128)(2,1)S(1)}, u32[]{:S(2)}, u32[]{:S(2)}) collective-permute-start(bf16[144,384]{1,0:T(8,128)(2,1)S(1)} %get-tuple-element.86.refs_1_), channel_id=1, source_target_pairs={{0,2},{1,3},{2,0},{3,1},{4,6},{5,7},{6,4},{7,5},{8,10},{9,11},{10,... | collective-permute-start | bytes 331784 | tf_op jit(solution)/shard_map/ppermute | solution.py:523
  58.8 1.4 %collective-permute-start.18 = (bf16[256,384]{1,0:T(8,128)(2,1)S(1)}, bf16[256,384]{1,0:T(8,128)(2,1)S(1)}, u32[]{:S(2)}, u32[]{:S(2)}) collective-permute-start(bf16[256,384]{1,0:T(8,128)(2,1)S(1)} %get-tuple-element.85.refs_2_), channel_id=1, source_target_pairs={{0,2},{1,3},{2,0},{3,1},{4,6},{5,7},{6,4},{7,5},{8,10},{9,11},{10,... | collective-permute-start | bytes 589832 | tf_op jit(solution)/shard_map/ppermute | solution.py:523
  60.2 1.5 %collective-permute-done.20.refs_3_ = bf16[144,384]{1,0:T(8,128)(2,1)S(1)} collective-permute-done((bf16[144,384]{1,0:T(8,128)(2,1)S(1)}, bf16[144,384]{1,0:T(8,128)(2,1)S(1)}, u32[]{:S(2)}, u32[]{:S(2)}) %collective-permute-start.20) | collective-permute-done | bytes 110624 | tf_op jit(solution)/shard_map/ppermute | solution.py:523
  64.0 1.4 %collective-permute-done.25.refs_1_ = bf16[2,48,1024]{2,1,0:T(8,128)(2,1)S(1)} collective-permute-done((bf16[2,48,1024]{2,1,0:T(8,128)(2,1)S(1)}, bf16[2,48,1024]{2,1,0:T(8,128)(2,1)S(1)}, u32[]{:S(2)}, u32[]{:S(2)}) %collective-permute-start.25) | collective-permute-done | bytes 196640 | tf_op jit(solution)/shard_map/ppermute | solution.py:523
  65.8 1.4 %collective-permute-start.29 = (bf16[1,128,384]{2,1,0:T(8,128)(2,1)S(1)}, bf16[1,128,384]{2,1,0:T(8,128)(2,1)S(1)}, u32[]{:S(2)}, u32[]{:S(2)}) collective-permute-start(bf16[1,128,384]{2,1,0:T(8,128)(2,1)S(1)} %get-tuple-element.100), channel_id=1, source_target_pairs={{0,4},{1,5},{2,6},{3,7},{4,0},{5,1},{6,2},{7,3},{8,12},{9,13},{10,... | collective-permute-start | bytes 294920 | tf_op jit(solution)/shard_map/ppermute | solution.py:523
  68.2 1.4 %collective-permute-start.27 = (bf16[1,160,384]{2,1,0:T(8,128)(2,1)S(1)}, bf16[1,160,384]{2,1,0:T(8,128)(2,1)S(1)}, u32[]{:S(2)}, u32[]{:S(2)}) collective-permute-start(bf16[1,160,384]{2,1,0:T(8,128)(2,1)S(1)} %get-tuple-element.97), channel_id=1, source_target_pairs={{0,4},{1,5},{2,6},{3,7},{4,0},{5,1},{6,2},{7,3},{8,12},{9,13},{10,... | collective-permute-start | bytes 368648 | tf_op jit(solution)/shard_map/ppermute | solution.py:523
  69.7 1.8 %collective-permute-start.28 = (bf16[1,48,1024]{2,1,0:T(8,128)(2,1)S(1)}, bf16[1,48,1024]{2,1,0:T(8,128)(2,1)S(1)}, u32[]{:S(2)}, u32[]{:S(2)}) collective-permute-start(bf16[1,48,1024]{2,1,0:T(8,128)(2,1)S(1)} %get-tuple-element.98), channel_id=1, source_target_pairs={{0,8},{1,9},{2,10},{3,11},{4,12},{5,13},{6,14},{7,15},{8,0},{9,1},... | collective-permute-start | bytes 294920 | tf_op jit(solution)/shard_map/ppermute | solution.py:523
  71.5 2.2 %collective-permute-start.30 = (bf16[1,128,384]{2,1,0:T(8,128)(2,1)S(1)}, bf16[1,128,384]{2,1,0:T(8,128)(2,1)S(1)}, u32[]{:S(2)}, u32[]{:S(2)}) collective-permute-start(bf16[1,128,384]{2,1,0:T(8,128)(2,1)S(1)} %conv_send_on.3), channel_id=1, source_target_pairs={{0,8},{1,9},{2,10},{3,11},{4,12},{5,13},{6,14},{7,15},{8,0},{9,1},... | collective-permute-start | bytes 294920 | tf_op jit(solution)/shard_map/ppermute | solution.py:523
  74.3 2.1 %collective-permute-done.27.refs_1_ = bf16[1,160,384]{2,1,0:T(8,128)(2,1)S(1)} collective-permute-done((bf16[1,160,384]{2,1,0:T(8,128)(2,1)S(1)}, bf16[1,160,384]{2,1,0:T(8,128)(2,1)S(1)}, u32[]{:S(2)}, u32[]{:S(2)}) %collective-permute-start.27) | collective-permute-done | bytes 122912 | tf_op jit(solution)/shard_map/ppermute | solution.py:523
  77.1 5.0 %collective-permute-done.30.refs_6_.refs_2_ = bf16[1,128,384]{2,1,0:T(8,128)(2,1)S(1)} collective-permute-done((bf16[1,128,384]{2,1,0:T(8,128)(2,1)S(1)}, bf16[1,128,384]{2,1,0:T(8,128)(2,1)S(1)}, u32[]{:S(2)}, u32[]{:S(2)}) %collective-permute-start.30) | collective-permute-done | bytes 98336 | tf_op jit(solution)/shard_map/ppermute | solution.py:523
  82.1 2.1 %input_grad.1 = bf16[256,384]{1,0:T(8,128)(2,1)} custom-call(bf16[256,384]{1,0:T(8,128)(2,1)S(1)} %bitcast.10, bf16[144,384]{1,0:T(8,128)(2,1)S(1)} %get-tuple-element.86.refs_1_, bf16[256,384]{1,0:T(8,128)(2,1)S(1)} %get-tuple-element.85.refs_2_, bf16[144,384]{1,0:T(8,128)(2,1)S(1)} %collective-permute-done.20.refs_3_, ...), custom_call_target="tpu_custom_call" | custom-call | flops 7549747200 | bytes 4153344 | tf_op jit(solution)/shard_map/input_grad/pallas_call | solution.py:37
  84.2 1.1 %collective-permute-done.31.refs_1_.refs_2_ = bf16[1,288,384]{2,1,0:T(8,128)(2,1)S(1)} collective-permute-done((bf16[1,288,384]{2,1,0:T(8,128)(2,1)S(1)}, bf16[1,288,384]{2,1,0:T(8,128)(2,1)S(1)}, u32[]{:S(2)}, u32[]{:S(2)}) %collective-permute-start.31) | collective-permute-done | bytes 221216 | tf_op jit(solution)/shard_map/ppermute | solution.py:523
  (69 shorter events, 16.6 us)
Async XLA Ops:
  1.8 6.7 %collective-permute-start.1 = (bf16[32,384]{1,0:T(8,128)(2,1)S(1)}, bf16[32,384]{1,0:T(8,128)(2,1)S(1)}, u32[]{:S(2)}, u32[]{:S(2)}) collective-permute-start(bf16[32,384]{1,0:T(8,128)(2,1)S(1)} %get-tuple-element.59), channel_id=1, source_target_pairs={{2,4},{6,8},{10,12},{4,2},{8,6},{12,10},{3,5},{7,9},{11,13},{5,3},... | collective-permute-start | bytes 73736 | tf_op jit(solution)/shard_map/ppermute | solution.py:554
  2.6 7.7 %collective-permute-start = (bf16[32,384]{1,0:T(8,128)(2,1)S(1)}, bf16[32,384]{1,0:T(8,128)(2,1)S(1)}, u32[]{:S(2)}, u32[]{:S(2)}) collective-permute-start(bf16[32,384]{1,0:T(8,128)(2,1)S(1)} %get-tuple-element.59), channel_id=1, source_target_pairs={{0,2},{1,3},{2,0},{3,1},{4,6},{5,7},{6,4},{7,5},{8,10},{9,11},{10,... | collective-permute-start | bytes 73736 | tf_op jit(solution)/shard_map/ppermute | solution.py:523
  12.2 6.1 %collective-permute-start.4 = (bf16[320,128]{1,0:T(8,128)(2,1)S(1)}, bf16[320,128]{1,0:T(8,128)(2,1)S(1)}, u32[]{:S(2)}, u32[]{:S(2)}) collective-permute-start(bf16[320,128]{1,0:T(8,128)(2,1)S(1)} %get-tuple-element.62.refs_2_), channel_id=1, source_target_pairs={{0,4},{1,5},{2,6},{3,7},{4,0},{5,1},{6,2},{7,3},{8,12},{9,13},{10,... | collective-permute-start | bytes 245768 | tf_op jit(solution)/shard_map/ppermute | solution.py:523
  14.2 6.6 %collective-permute-start.3 = (bf16[320,128]{1,0:T(8,128)(2,1)S(1)}, bf16[320,128]{1,0:T(8,128)(2,1)S(1)}, u32[]{:S(2)}, u32[]{:S(2)}) collective-permute-start(bf16[320,128]{1,0:T(8,128)(2,1)S(1)} %get-tuple-element.62.refs_2_), channel_id=1, source_target_pairs={{0,12},{1,13},{2,14},{3,15},{4,8},{5,9},{6,10},{7,11},{8,4},{9,5},... | collective-permute-start | bytes 245768 | tf_op jit(solution)/shard_map/ppermute | solution.py:523
  16.7 6.6 %collective-permute-start.2 = (bf16[320,128]{1,0:T(8,128)(2,1)S(1)}, bf16[320,128]{1,0:T(8,128)(2,1)S(1)}, u32[]{:S(2)}, u32[]{:S(2)}) collective-permute-start(bf16[320,128]{1,0:T(8,128)(2,1)S(1)} %get-tuple-element.62.refs_2_), channel_id=1, source_target_pairs={{0,8},{1,9},{2,10},{3,11},{4,12},{5,13},{6,14},{7,15},{8,0},{9,1},... | collective-permute-start | bytes 245768 | tf_op jit(solution)/shard_map/ppermute | solution.py:523
  16.8 8.4 %collective-permute-start.5 = (bf16[320,128]{1,0:T(8,128)(2,1)S(1)}, bf16[320,128]{1,0:T(8,128)(2,1)S(1)}, u32[]{:S(2)}, u32[]{:S(2)}) collective-permute-start(bf16[320,128]{1,0:T(8,128)(2,1)S(1)} %get-tuple-element.62.refs_2_), channel_id=1, source_target_pairs={{0,2},{1,3},{2,0},{3,1},{4,6},{5,7},{6,4},{7,5},{8,10},{9,11},{10,... | collective-permute-start | bytes 245768 | tf_op jit(solution)/shard_map/ppermute | solution.py:523
  18.3 6.9 %collective-permute-start.8 = (bf16[320,128]{1,0:T(8,128)(2,1)S(1)}, bf16[320,128]{1,0:T(8,128)(2,1)S(1)}, u32[]{:S(2)}, u32[]{:S(2)}) collective-permute-start(bf16[320,128]{1,0:T(8,128)(2,1)S(1)} %collective-permute-done.4.refs_5_), channel_id=1, source_target_pairs={{0,2},{1,3},{2,0},{3,1},{4,6},{5,7},{6,4},{7,5},{8,10},{9,11},{10,... | collective-permute-start | bytes 245768 | tf_op jit(solution)/shard_map/ppermute | solution.py:523
  20.8 5.1 %collective-permute-start.7 = (bf16[320,128]{1,0:T(8,128)(2,1)S(1)}, bf16[320,128]{1,0:T(8,128)(2,1)S(1)}, u32[]{:S(2)}, u32[]{:S(2)}) collective-permute-start(bf16[320,128]{1,0:T(8,128)(2,1)S(1)} %collective-permute-done.3.refs_4_), channel_id=1, source_target_pairs={{0,2},{1,3},{2,0},{3,1},{4,6},{5,7},{6,4},{7,5},{8,10},{9,11},{10,... | collective-permute-start | bytes 245768 | tf_op jit(solution)/shard_map/ppermute | solution.py:523
  23.3 4.4 %collective-permute-start.6 = (bf16[320,128]{1,0:T(8,128)(2,1)S(1)}, bf16[320,128]{1,0:T(8,128)(2,1)S(1)}, u32[]{:S(2)}, u32[]{:S(2)}) collective-permute-start(bf16[320,128]{1,0:T(8,128)(2,1)S(1)} %collective-permute-done.2.refs_3_), channel_id=1, source_target_pairs={{0,2},{1,3},{2,0},{3,1},{4,6},{5,7},{6,4},{7,5},{8,10},{9,11},{10,... | collective-permute-start | bytes 245768 | tf_op jit(solution)/shard_map/ppermute | solution.py:523
  27.7 7.7 %collective-permute-start.10 = (bf16[416,384]{1,0:T(8,128)(2,1)S(1)}, bf16[416,384]{1,0:T(8,128)(2,1)S(1)}, u32[]{:S(2)}, u32[]{:S(2)}) collective-permute-start(bf16[416,384]{1,0:T(8,128)(2,1)S(1)} %get-tuple-element.69), channel_id=1, source_target_pairs={{0,2},{1,3},{2,0},{3,1},{4,6},{5,7},{6,4},{7,5},{8,10},{9,11},{10,... | collective-permute-start | bytes 958472 | tf_op jit(solution)/shard_map/ppermute | solution.py:523
  35.4 2.8 %collective-permute-start.11 = (bf16[416,384]{1,0:T(8,128)(2,1)S(1)}, bf16[416,384]{1,0:T(8,128)(2,1)S(1)}, u32[]{:S(2)}, u32[]{:S(2)}) collective-permute-start(bf16[416,384]{1,0:T(8,128)(2,1)S(1)} %collective-permute-done.10.refs_3_), channel_id=1, source_target_pairs={{0,1},{1,0},{2,3},{3,2},{4,5},{5,4},{6,7},{7,6},{8,9},{9,8},{10,11... | collective-permute-start | bytes 958472 | tf_op jit(solution)/shard_map/ppermute | solution.py:523
  35.4 2.7 %collective-permute-start.9 = (bf16[352,384]{1,0:T(8,128)(2,1)S(1)}, bf16[352,384]{1,0:T(8,128)(2,1)S(1)}, u32[]{:S(2)}, u32[]{:S(2)}) collective-permute-start(bf16[352,384]{1,0:T(8,128)(2,1)S(1)} %get-tuple-element.67), channel_id=1, source_target_pairs={{0,1},{1,0},{2,3},{3,2},{4,5},{5,4},{6,7},{7,6},{8,9},{9,8},{10,11... | collective-permute-start | bytes 811016 | tf_op jit(solution)/shard_map/ppermute | solution.py:523
  35.9 7.2 %collective-permute-start.12 = (bf16[4,160,128]{2,1,0:T(8,128)(2,1)S(1)}, bf16[4,160,128]{2,1,0:T(8,128)(2,1)S(1)}, u32[]{:S(2)}, u32[]{:S(2)}) collective-permute-start(bf16[4,160,128]{2,1,0:T(8,128)(2,1)S(1)} %get-tuple-element.70), channel_id=1, source_target_pairs={{0,2},{1,3},{2,0},{3,1},{4,6},{5,7},{6,4},{7,5},{8,10},{9,11},{10,... | collective-permute-start | bytes 491528 | tf_op jit(solution)/shard_map/ppermute | solution.py:523
  37.3 5.8 %collective-permute-start.13 = (bf16[4,160,128]{2,1,0:T(8,128)(2,1)S(1)}, bf16[4,160,128]{2,1,0:T(8,128)(2,1)S(1)}, u32[]{:S(2)}, u32[]{:S(2)}) collective-permute-start(bf16[4,160,128]{2,1,0:T(8,128)(2,1)S(1)} %get-tuple-element.76), channel_id=1, source_target_pairs={{0,4},{1,5},{2,6},{3,7},{4,0},{5,1},{6,2},{7,3},{8,12},{9,13},{10,... | collective-permute-start | bytes 491528 | tf_op jit(solution)/shard_map/ppermute | solution.py:523
  43.2 4.5 %collective-permute-start.14 = (bf16[2,160,128]{2,1,0:T(8,128)(2,1)S(1)}, bf16[2,160,128]{2,1,0:T(8,128)(2,1)S(1)}, u32[]{:S(2)}, u32[]{:S(2)}) collective-permute-start(bf16[2,160,128]{2,1,0:T(8,128)(2,1)S(1)} %get-tuple-element.78), channel_id=1, source_target_pairs={{0,4},{1,5},{2,6},{3,7},{4,0},{5,1},{6,2},{7,3},{8,12},{9,13},{10,... | collective-permute-start | bytes 245768 | tf_op jit(solution)/shard_map/ppermute | solution.py:523
  44.1 4.4 %collective-permute-start.15 = (bf16[2,160,128]{2,1,0:T(8,128)(2,1)S(1)}, bf16[2,160,128]{2,1,0:T(8,128)(2,1)S(1)}, u32[]{:S(2)}, u32[]{:S(2)}) collective-permute-start(bf16[2,160,128]{2,1,0:T(8,128)(2,1)S(1)} %get-tuple-element.80), channel_id=1, source_target_pairs={{0,2},{1,3},{2,0},{3,1},{4,6},{5,7},{6,4},{7,5},{8,10},{9,11},{10,... | collective-permute-start | bytes 245768 | tf_op jit(solution)/shard_map/ppermute | solution.py:523
  48.6 7.4 %collective-permute-start.22 = (bf16[128,1024]{1,0:T(8,128)(2,1)S(1)}, bf16[128,1024]{1,0:T(8,128)(2,1)S(1)}, u32[]{:S(2)}, u32[]{:S(2)}) collective-permute-start(bf16[128,1024]{1,0:T(8,128)(2,1)S(1)} %get-tuple-element.87.refs_0_.refs_1_), channel_id=1, source_target_pairs={{0,2},{1,3},{2,0},{3,1},{4,6},{5,7},{6,4},{7,5},{8,10},{9,11},{10,... | collective-permute-start | bytes 786440 | tf_op jit(solution)/shard_map/ppermute | solution.py:523
  49.4 6.2 %collective-permute-start.16 = (bf16[1,320,128]{2,1,0:T(8,128)(2,1)S(1)}, bf16[1,320,128]{2,1,0:T(8,128)(2,1)S(1)}, u32[]{:S(2)}, u32[]{:S(2)}) collective-permute-start(bf16[1,320,128]{2,1,0:T(8,128)(2,1)S(1)} %get-tuple-element.82), channel_id=1, source_target_pairs={{0,8},{1,9},{2,10},{3,11},{4,12},{5,13},{6,14},{7,15},{8,0},{9,1},... | collective-permute-start | bytes 245768 | tf_op jit(solution)/shard_map/ppermute | solution.py:523
  52.1 5.4 %collective-permute-start.21 = (bf16[128,1024]{1,0:T(8,128)(2,1)S(1)}, bf16[128,1024]{1,0:T(8,128)(2,1)S(1)}, u32[]{:S(2)}, u32[]{:S(2)}) collective-permute-start(bf16[128,1024]{1,0:T(8,128)(2,1)S(1)} %get-tuple-element.87.refs_0_.refs_1_), channel_id=1, source_target_pairs={{0,1},{1,0},{2,3},{3,2},{4,5},{5,4},{6,7},{7,6},{8,9},{9,8},{10,11... | collective-permute-start | bytes 786440 | tf_op jit(solution)/shard_map/ppermute | solution.py:523
  56.0 1.6 %collective-permute-start.23 = (bf16[128,1024]{1,0:T(8,128)(2,1)S(1)}, bf16[128,1024]{1,0:T(8,128)(2,1)S(1)}, u32[]{:S(2)}, u32[]{:S(2)}) collective-permute-start(bf16[128,1024]{1,0:T(8,128)(2,1)S(1)} %collective-permute-done.22.refs_3_), channel_id=1, source_target_pairs={{0,1},{1,0},{2,3},{3,2},{4,5},{5,4},{6,7},{7,6},{8,9},{9,8},{10,11... | collective-permute-start | bytes 786440 | tf_op jit(solution)/shard_map/ppermute | solution.py:523
  56.1 5.7 %collective-permute-start.20 = (bf16[144,384]{1,0:T(8,128)(2,1)S(1)}, bf16[144,384]{1,0:T(8,128)(2,1)S(1)}, u32[]{:S(2)}, u32[]{:S(2)}) collective-permute-start(bf16[144,384]{1,0:T(8,128)(2,1)S(1)} %get-tuple-element.86.refs_1_), channel_id=1, source_target_pairs={{0,2},{1,3},{2,0},{3,1},{4,6},{5,7},{6,4},{7,5},{8,10},{9,11},{10,... | collective-permute-start | bytes 331784 | tf_op jit(solution)/shard_map/ppermute | solution.py:523
  58.4 7.0 %collective-permute-start.25 = (bf16[2,48,1024]{2,1,0:T(8,128)(2,1)S(1)}, bf16[2,48,1024]{2,1,0:T(8,128)(2,1)S(1)}, u32[]{:S(2)}, u32[]{:S(2)}) collective-permute-start(bf16[2,48,1024]{2,1,0:T(8,128)(2,1)S(1)} %get-tuple-element.92), channel_id=1, source_target_pairs={{0,4},{1,5},{2,6},{3,7},{4,0},{5,1},{6,2},{7,3},{8,12},{9,13},{10,... | collective-permute-start | bytes 589832 | tf_op jit(solution)/shard_map/ppermute | solution.py:523
  58.8 6.9 %collective-permute-start.18 = (bf16[256,384]{1,0:T(8,128)(2,1)S(1)}, bf16[256,384]{1,0:T(8,128)(2,1)S(1)}, u32[]{:S(2)}, u32[]{:S(2)}) collective-permute-start(bf16[256,384]{1,0:T(8,128)(2,1)S(1)} %get-tuple-element.85.refs_2_), channel_id=1, source_target_pairs={{0,2},{1,3},{2,0},{3,1},{4,6},{5,7},{6,4},{7,5},{8,10},{9,11},{10,... | collective-permute-start | bytes 589832 | tf_op jit(solution)/shard_map/ppermute | solution.py:523
  60.2 2.1 %collective-permute-start.19 = (bf16[144,384]{1,0:T(8,128)(2,1)S(1)}, bf16[144,384]{1,0:T(8,128)(2,1)S(1)}, u32[]{:S(2)}, u32[]{:S(2)}) collective-permute-start(bf16[144,384]{1,0:T(8,128)(2,1)S(1)} %get-tuple-element.86.refs_1_), channel_id=1, source_target_pairs={{0,1},{1,0},{2,3},{3,2},{4,5},{5,4},{6,7},{7,6},{8,9},{9,8},{10,11... | collective-permute-start | bytes 331784 | tf_op jit(solution)/shard_map/ppermute | solution.py:523
  61.7 5.5 %collective-permute-start.17 = (bf16[256,384]{1,0:T(8,128)(2,1)S(1)}, bf16[256,384]{1,0:T(8,128)(2,1)S(1)}, u32[]{:S(2)}, u32[]{:S(2)}) collective-permute-start(bf16[256,384]{1,0:T(8,128)(2,1)S(1)} %get-tuple-element.85.refs_2_), channel_id=1, source_target_pairs={{0,1},{1,0},{2,3},{3,2},{4,5},{5,4},{6,7},{7,6},{8,9},{9,8},{10,11... | collective-permute-start | bytes 589832 | tf_op jit(solution)/shard_map/ppermute | solution.py:523
  65.8 1.4 %collective-permute-start.26 = (bf16[256,384]{1,0:T(8,128)(2,1)S(1)}, bf16[256,384]{1,0:T(8,128)(2,1)S(1)}, u32[]{:S(2)}, u32[]{:S(2)}) collective-permute-start(bf16[256,384]{1,0:T(8,128)(2,1)S(1)} %collective-permute-done.18.refs_4_), channel_id=1, source_target_pairs={{0,1},{1,0},{2,3},{3,2},{4,5},{5,4},{6,7},{7,6},{8,9},{9,8},{10,11... | collective-permute-start | bytes 589832 | tf_op jit(solution)/shard_map/ppermute | solution.py:523
  65.8 5.7 %collective-permute-start.29 = (bf16[1,128,384]{2,1,0:T(8,128)(2,1)S(1)}, bf16[1,128,384]{2,1,0:T(8,128)(2,1)S(1)}, u32[]{:S(2)}, u32[]{:S(2)}) collective-permute-start(bf16[1,128,384]{2,1,0:T(8,128)(2,1)S(1)} %get-tuple-element.100), channel_id=1, source_target_pairs={{0,4},{1,5},{2,6},{3,7},{4,0},{5,1},{6,2},{7,3},{8,12},{9,13},{10,... | collective-permute-start | bytes 294920 | tf_op jit(solution)/shard_map/ppermute | solution.py:523
  68.2 8.1 %collective-permute-start.27 = (bf16[1,160,384]{2,1,0:T(8,128)(2,1)S(1)}, bf16[1,160,384]{2,1,0:T(8,128)(2,1)S(1)}, u32[]{:S(2)}, u32[]{:S(2)}) collective-permute-start(bf16[1,160,384]{2,1,0:T(8,128)(2,1)S(1)} %get-tuple-element.97), channel_id=1, source_target_pairs={{0,4},{1,5},{2,6},{3,7},{4,0},{5,1},{6,2},{7,3},{8,12},{9,13},{10,... | collective-permute-start | bytes 368648 | tf_op jit(solution)/shard_map/ppermute | solution.py:523
  69.7 7.5 %collective-permute-start.28 = (bf16[1,48,1024]{2,1,0:T(8,128)(2,1)S(1)}, bf16[1,48,1024]{2,1,0:T(8,128)(2,1)S(1)}, u32[]{:S(2)}, u32[]{:S(2)}) collective-permute-start(bf16[1,48,1024]{2,1,0:T(8,128)(2,1)S(1)} %get-tuple-element.98), channel_id=1, source_target_pairs={{0,8},{1,9},{2,10},{3,11},{4,12},{5,13},{6,14},{7,15},{8,0},{9,1},... | collective-permute-start | bytes 294920 | tf_op jit(solution)/shard_map/ppermute | solution.py:523
  71.5 10.6 %collective-permute-start.30 = (bf16[1,128,384]{2,1,0:T(8,128)(2,1)S(1)}, bf16[1,128,384]{2,1,0:T(8,128)(2,1)S(1)}, u32[]{:S(2)}, u32[]{:S(2)}) collective-permute-start(bf16[1,128,384]{2,1,0:T(8,128)(2,1)S(1)} %conv_send_on.3), channel_id=1, source_target_pairs={{0,8},{1,9},{2,10},{3,11},{4,12},{5,13},{6,14},{7,15},{8,0},{9,1},... | collective-permute-start | bytes 294920 | tf_op jit(solution)/shard_map/ppermute | solution.py:523
  73.7 11.6 %collective-permute-start.31 = (bf16[1,288,384]{2,1,0:T(8,128)(2,1)S(1)}, bf16[1,288,384]{2,1,0:T(8,128)(2,1)S(1)}, u32[]{:S(2)}, u32[]{:S(2)}) collective-permute-start(bf16[1,288,384]{2,1,0:T(8,128)(2,1)S(1)} %get-tuple-element.102), channel_id=1, source_target_pairs={{0,4},{1,5},{2,6},{3,7},{4,0},{5,1},{6,2},{7,3},{8,12},{9,13},{10,... | collective-permute-start | bytes 663560 | tf_op jit(solution)/shard_map/ppermute | solution.py:523
  76.4 8.9 %collective-permute-start.32 = (bf16[1,160,384]{2,1,0:T(8,128)(2,1)S(1)}, bf16[1,160,384]{2,1,0:T(8,128)(2,1)S(1)}, u32[]{:S(2)}, u32[]{:S(2)}) collective-permute-start(bf16[1,160,384]{2,1,0:T(8,128)(2,1)S(1)} %conv_send_on.2), channel_id=1, source_target_pairs={{0,8},{1,9},{2,10},{3,11},{4,12},{5,13},{6,14},{7,15},{8,0},{9,1},... | collective-permute-start | bytes 368648 | tf_op jit(solution)/shard_map/ppermute | solution.py:523
  (9 other events, 101.3 us)

commit v12 on v11

--- a/solution.py
+++ b/solution.py
@@ -530,13 +530,13 @@
         near = swap(value, 1)
         return [value, core, near, swap(held(near, *until), 0, 1)]
 
-    def fold(parts, name):
+    def fold(parts, name, flops=0):
         shape = (parts[0].shape[0] // 2,) + parts[0].shape[1:]
-        return run(fold_kernel, [(shape, F32), (shape, BF)], parts, name=name)
-
-    def halved(keep, send, bits, name):
+        return run(fold_kernel, [(shape, F32), (shape, BF)], parts, flops=flops, name=name)
+
+    def halved(keep, send, bits, name, flops=0):
         for bit in bits[:-1]:
-            keep, send = fold([keep, swap(send, 1 << bit)], name)
+            keep, send = fold([keep, swap(send, 1 << bit)], name, flops)
         return [keep, swap(send, 1 << bits[-1])]
 
     bits = list(range(devices.bit_length() - 1))
@@ -680,7 +680,7 @@
         flops=2 * groups * norm_pad * 4 * tokens * heads * key_size,
         name="query_grad",
     )
-    query_parts = halved(query_keep, query_send, bits[1:], "query_fold")
+    query_parts = halved(query_keep, query_send, bits[1:], "query_fold", 5 * 10**9)
     core_first, core_second = swap(first, 0, 1), swap(second, 0, 1)
     split = width // 2
     side = side_rows(norm_rows, key_size, split) + side_rows(norm_rows, value_size, split)
@@ -696,7 +696,7 @@
         name="conv_grad_first",
     )
     far_in = swap(far_send, 2)
-    last_second = swap(held(near_second, near_keep, query_parts[0]), 0, 1)
+    last_second = swap(held(near_second, near_keep), 0, 1)
     near_keep_second, far_keep_second, near_send, far_send = run(
         lambda *refs: conv_second_kernel(
             *refs,
@@ -713,7 +713,7 @@
             ((count, above + below, split), BF),
             ((count, below, split), BF),
         ],
-        [conv_pick, norm_pick, second, core_second, near_second, last_second, near_send],
+        [held(conv_pick, query_parts[0]), norm_pick, second, core_second, near_second, last_second, near_send],
         [
             pltpu.VMEM((8 * tokens, split), BF),
             pltpu.VMEM((4 * tokens, split), BF),

time: 86.3 us -> 86.6 us (level)
  waiting for transfers between devices: 28.7 us -> 30.9 us
  starting transfers between devices: 37.2 us -> 35.2 us
    ppermute x32, waiting for transfers between devices: 28.7 us -> 30.9 us  [swap(): lax.ppermute(value, both_axes, [(i, i ^ mask) for i in range(owners)])]
    ppermute x32, starting transfers between devices: 36.4 us -> 34.4 us  [swap(): lax.ppermute(value, both_axes, [(i, i ^ mask) for i in range(owners)])]
where the time goes in v12:
time: 86.6 us; the launch traced here: 86.4 us
  starting transfers between devices  35.2 us (41%)
  waiting for transfers between devices  30.9 us (36%)
  Pallas kernels  18.5 us (21%)
  local copies, waits for them, and re-layouts  0.96 us (1%)
    ppermute x32, starting transfers between devices, swap(): lax.ppermute(value, both_axes, [(i, i ^ mask) for i in range(owners)])  34.4 us
    ppermute x32, waiting for transfers between devices, swap(): lax.ppermute(value, both_axes, [(i, i ^ mask) for i in range(owners)])  30.9 us
    pallas_call x18, Pallas kernels, run(): pl.pallas_call(whole, out_shape=[jax.ShapeDtypeStruct(s, t) for s, t in o...  18.5 us
  transfers between devices with their start and end apart: 33, of which 18 were waited for; matrix products, arithmetic and copies ran while one was open for 0% of the time, Pallas kernels for 18%

profile of v12, /device:TPU:0, one launch (start us, length us, event | category | flops | bytes accessed | tf_op | source)
XLA Modules:
  0.0 86.4 jit_solution(10338764887051423826)
XLA Ops:
  2.6 5.9 %collective-permute-start = (bf16[32,384]{1,0:T(8,128)(2,1)S(1)}, bf16[32,384]{1,0:T(8,128)(2,1)S(1)}, u32[]{:S(2)}, u32[]{:S(2)}) collective-permute-start(bf16[32,384]{1,0:T(8,128)(2,1)S(1)} %get-tuple-element.60), channel_id=1, source_target_pairs={{0,2},{1,3},{2,0},{3,1},{4,6},{5,7},{6,4},{7,5},{8,10},{9,11},{10,... | collective-permute-start | bytes 73736 | tf_op jit(solution)/shard_map/ppermute | solution.py:523
  8.5 1.8 %collective-permute-done.refs_1_ = bf16[32,384]{1,0:T(8,128)(2,1)S(1)} collective-permute-done((bf16[32,384]{1,0:T(8,128)(2,1)S(1)}, bf16[32,384]{1,0:T(8,128)(2,1)S(1)}, u32[]{:S(2)}, u32[]{:S(2)}) %collective-permute-start) | collective-permute-done | bytes 24608 | tf_op jit(solution)/shard_map/ppermute | solution.py:523
  10.3 1.9 %front.1 = (bf16[320,128]{1,0:T(8,128)(2,1)S(1)}, bf16[288,384]{1,0:T(8,128)(2,1)S(1)}, bf16[128,768]{1,0:T(8,128)(2,1)S(1)}, f32[128,768]{1,0:T(8,128)S(1)}) custom-call(f32[3,304,128]{2,1,0:T(8,128)S(1)} %get-tuple-element.59.refs_0_, bf16[32,384]{1,0:T(8,128)(2,1)S(1)} %collective-permute-done.refs_1_, ...), custom_call_target="tpu_custom_call" | custom-call | flops 754974720 | bytes 4852736 | tf_op jit(solution)/shard_map/front/pallas_call | solution.py:37
  12.2 2.0 %collective-permute-start.4 = (bf16[320,128]{1,0:T(8,128)(2,1)S(1)}, bf16[320,128]{1,0:T(8,128)(2,1)S(1)}, u32[]{:S(2)}, u32[]{:S(2)}) collective-permute-start(bf16[320,128]{1,0:T(8,128)(2,1)S(1)} %get-tuple-element.63.refs_2_), channel_id=1, source_target_pairs={{0,4},{1,5},{2,6},{3,7},{4,0},{5,1},{6,2},{7,3},{8,12},{9,13},{10,... | collective-permute-start | bytes 245768 | tf_op jit(solution)/shard_map/ppermute | solution.py:523
  14.2 2.5 %collective-permute-start.3 = (bf16[320,128]{1,0:T(8,128)(2,1)S(1)}, bf16[320,128]{1,0:T(8,128)(2,1)S(1)}, u32[]{:S(2)}, u32[]{:S(2)}) collective-permute-start(bf16[320,128]{1,0:T(8,128)(2,1)S(1)} %get-tuple-element.63.refs_2_), channel_id=1, source_target_pairs={{0,12},{1,13},{2,14},{3,15},{4,8},{5,9},{6,10},{7,11},{8,4},{9,5},... | collective-permute-start | bytes 245768 | tf_op jit(solution)/shard_map/ppermute | solution.py:523
  16.8 1.5 %collective-permute-start.5 = (bf16[320,128]{1,0:T(8,128)(2,1)S(1)}, bf16[320,128]{1,0:T(8,128)(2,1)S(1)}, u32[]{:S(2)}, u32[]{:S(2)}) collective-permute-start(bf16[320,128]{1,0:T(8,128)(2,1)S(1)} %get-tuple-element.63.refs_2_), channel_id=1, source_target_pairs={{0,2},{1,3},{2,0},{3,1},{4,6},{5,7},{6,4},{7,5},{8,10},{9,11},{10,... | collective-permute-start | bytes 245768 | tf_op jit(solution)/shard_map/ppermute | solution.py:523
  18.3 1.3 %collective-permute-start.8 = (bf16[320,128]{1,0:T(8,128)(2,1)S(1)}, bf16[320,128]{1,0:T(8,128)(2,1)S(1)}, u32[]{:S(2)}, u32[]{:S(2)}) collective-permute-start(bf16[320,128]{1,0:T(8,128)(2,1)S(1)} %collective-permute-done.4.refs_5_), channel_id=1, source_target_pairs={{0,2},{1,3},{2,0},{3,1},{4,6},{5,7},{6,4},{7,5},{8,10},{9,11},{10,... | collective-permute-start | bytes 245768 | tf_op jit(solution)/shard_map/ppermute | solution.py:523
  19.6 1.2 %collective-permute-done.3.refs_4_ = bf16[320,128]{1,0:T(8,128)(2,1)S(1)} collective-permute-done((bf16[320,128]{1,0:T(8,128)(2,1)S(1)}, bf16[320,128]{1,0:T(8,128)(2,1)S(1)}, u32[]{:S(2)}, u32[]{:S(2)}) %collective-permute-start.3) | collective-permute-done | bytes 81952 | tf_op jit(solution)/shard_map/ppermute | solution.py:523
  20.8 1.4 %collective-permute-start.7 = (bf16[320,128]{1,0:T(8,128)(2,1)S(1)}, bf16[320,128]{1,0:T(8,128)(2,1)S(1)}, u32[]{:S(2)}, u32[]{:S(2)}) collective-permute-start(bf16[320,128]{1,0:T(8,128)(2,1)S(1)} %collective-permute-done.3.refs_4_), channel_id=1, source_target_pairs={{0,2},{1,3},{2,0},{3,1},{4,6},{5,7},{6,4},{7,5},{8,10},{9,11},{10,... | collective-permute-start | bytes 245768 | tf_op jit(solution)/shard_map/ppermute | solution.py:523
  22.2 1.1 %collective-permute-done.2.refs_3_ = bf16[320,128]{1,0:T(8,128)(2,1)S(1)} collective-permute-done((bf16[320,128]{1,0:T(8,128)(2,1)S(1)}, bf16[320,128]{1,0:T(8,128)(2,1)S(1)}, u32[]{:S(2)}, u32[]{:S(2)}) %collective-permute-start.2) | collective-permute-done | bytes 81952 | tf_op jit(solution)/shard_map/ppermute | solution.py:523
  23.3 1.2 %collective-permute-start.6 = (bf16[320,128]{1,0:T(8,128)(2,1)S(1)}, bf16[320,128]{1,0:T(8,128)(2,1)S(1)}, u32[]{:S(2)}, u32[]{:S(2)}) collective-permute-start(bf16[320,128]{1,0:T(8,128)(2,1)S(1)} %collective-permute-done.2.refs_3_), channel_id=1, source_target_pairs={{0,2},{1,3},{2,0},{3,1},{4,6},{5,7},{6,4},{7,5},{8,10},{9,11},{10,... | collective-permute-start | bytes 245768 | tf_op jit(solution)/shard_map/ppermute | solution.py:523
  25.8 1.9 %collective-permute-done.6.refs_7_ = bf16[320,128]{1,0:T(8,128)(2,1)S(1)} collective-permute-done((bf16[320,128]{1,0:T(8,128)(2,1)S(1)}, bf16[320,128]{1,0:T(8,128)(2,1)S(1)}, u32[]{:S(2)}, u32[]{:S(2)}) %collective-permute-start.6) | collective-permute-done | bytes 81952 | tf_op jit(solution)/shard_map/ppermute | solution.py:523
  27.7 1.2 %collective-permute-start.10 = (bf16[416,384]{1,0:T(8,128)(2,1)S(1)}, bf16[416,384]{1,0:T(8,128)(2,1)S(1)}, u32[]{:S(2)}, u32[]{:S(2)}) collective-permute-start(bf16[416,384]{1,0:T(8,128)(2,1)S(1)} %get-tuple-element.70), channel_id=1, source_target_pairs={{0,2},{1,3},{2,0},{3,1},{4,6},{5,7},{6,4},{7,5},{8,10},{9,11},{10,... | collective-permute-start | bytes 958472 | tf_op jit(solution)/shard_map/ppermute | solution.py:523
  28.9 6.4 %attend.1 = (bf16[128,1536]{1,0:T(8,128)(2,1)}, bf16[128,1024]{1,0:T(8,128)(2,1)S(1)}, f32[4,160,128]{2,1,0:T(8,128)S(1)}, bf16[4,160,128]{2,1,0:T(8,128)(2,1)S(...) custom-call(bf16[128,1024]{1,0:T(8,128)(2,1)S(1)} %get-tuple-element.64.refs_0_, ...), custom_call_target="tpu_custom_call" | custom-call | flops 2013265920 | bytes 2949120 | tf_op jit(solution)/shard_map/attend/pallas_call | solution.py:37
  35.9 1.4 %collective-permute-start.12 = (bf16[4,160,128]{2,1,0:T(8,128)(2,1)S(1)}, bf16[4,160,128]{2,1,0:T(8,128)(2,1)S(1)}, u32[]{:S(2)}, u32[]{:S(2)}) collective-permute-start(bf16[4,160,128]{2,1,0:T(8,128)(2,1)S(1)} %get-tuple-element.71), channel_id=1, source_target_pairs={{0,2},{1,3},{2,0},{3,1},{4,6},{5,7},{6,4},{7,5},{8,10},{9,11},{10,... | collective-permute-start | bytes 491528 | tf_op jit(solution)/shard_map/ppermute | solution.py:523
  38.1 2.4 %select.1 = (bf16[512,1024]{1,0:T(8,128)(2,1)S(1)}, bf16[192,512]{1,0:T(8,128)(2,1)S(1)}) custom-call(bf16[192,128]{1,0:T(8,128)(2,1)S(1)} %get-tuple-element.66.refs_0_, bf16[288,384]{1,0:T(8,128)(2,1)S(1)} %get-tuple-element.62.refs_2_.refs_1_, bf16[352,384]{1,0:T(8,128)(2,1)S(1)} %collective-permute-done.9.refs_2_, ...), custom_call_target="tpu_custom_call" | custom-call | flops 2013265920 | bytes 2424832 | tf_op jit(solution)/shard_map/select/pallas_call | solution.py:37
  40.6 2.5 %collective-permute-done.13.refs_3_ = bf16[4,160,128]{2,1,0:T(8,128)(2,1)S(1)} collective-permute-done((bf16[4,160,128]{2,1,0:T(8,128)(2,1)S(1)}, bf16[4,160,128]{2,1,0:T(8,128)(2,1)S(1)}, u32[]{:S(2)}, u32[]{:S(2)}) %collective-permute-start.13) | collective-permute-done | bytes 163872 | tf_op jit(solution)/shard_map/ppermute | solution.py:523
  44.8 2.9 %collective-permute-done.14.refs_1_ = bf16[2,160,128]{2,1,0:T(8,128)(2,1)S(1)} collective-permute-done((bf16[2,160,128]{2,1,0:T(8,128)(2,1)S(1)}, bf16[2,160,128]{2,1,0:T(8,128)(2,1)S(1)}, u32[]{:S(2)}, u32[]{:S(2)}) %collective-permute-start.14) | collective-permute-done | bytes 81952 | tf_op jit(solution)/shard_map/ppermute | solution.py:523
  49.4 2.1 %collective-permute-start.18 = (bf16[1,320,128]{2,1,0:T(8,128)(2,1)S(1)}, bf16[1,320,128]{2,1,0:T(8,128)(2,1)S(1)}, u32[]{:S(2)}, u32[]{:S(2)}) collective-permute-start(bf16[1,320,128]{2,1,0:T(8,128)(2,1)S(1)} %get-tuple-element.85), channel_id=1, source_target_pairs={{0,8},{1,9},{2,10},{3,11},{4,12},{5,13},{6,14},{7,15},{8,0},{9,1},... | collective-permute-start | bytes 245768 | tf_op jit(solution)/shard_map/ppermute | solution.py:523
  52.1 3.4 %collective-permute-done.18.refs_1_ = bf16[1,320,128]{2,1,0:T(8,128)(2,1)S(1)} collective-permute-done((bf16[1,320,128]{2,1,0:T(8,128)(2,1)S(1)}, bf16[1,320,128]{2,1,0:T(8,128)(2,1)S(1)}, u32[]{:S(2)}, u32[]{:S(2)}) %collective-permute-start.18) | collective-permute-done | bytes 81952 | tf_op jit(solution)/shard_map/ppermute | solution.py:523
  56.1 1.4 %collective-permute-start.24 = (bf16[144,384]{1,0:T(8,128)(2,1)S(1)}, bf16[144,384]{1,0:T(8,128)(2,1)S(1)}, u32[]{:S(2)}, u32[]{:S(2)}) collective-permute-start(bf16[144,384]{1,0:T(8,128)(2,1)S(1)} %get-tuple-element.87.refs_1_), channel_id=1, source_target_pairs={{0,2},{1,3},{2,0},{3,1},{4,6},{5,7},{6,4},{7,5},{8,10},{9,11},{10,... | collective-permute-start | bytes 331784 | tf_op jit(solution)/shard_map/ppermute | solution.py:523
  59.4 2.6 %collective-permute-done.24.refs_3_ = bf16[144,384]{1,0:T(8,128)(2,1)S(1)} collective-permute-done((bf16[144,384]{1,0:T(8,128)(2,1)S(1)}, bf16[144,384]{1,0:T(8,128)(2,1)S(1)}, u32[]{:S(2)}, u32[]{:S(2)}) %collective-permute-start.24) | collective-permute-done | bytes 110624 | tf_op jit(solution)/shard_map/ppermute | solution.py:523
  64.3 1.5 %collective-permute-done.22.refs_4_ = bf16[256,384]{1,0:T(8,128)(2,1)S(1)} collective-permute-done((bf16[256,384]{1,0:T(8,128)(2,1)S(1)}, bf16[256,384]{1,0:T(8,128)(2,1)S(1)}, u32[]{:S(2)}, u32[]{:S(2)}) %collective-permute-start.22) | collective-permute-done | bytes 196640 | tf_op jit(solution)/shard_map/ppermute | solution.py:523
  66.2 1.4 %collective-permute-done.26.refs_5_ = bf16[256,384]{1,0:T(8,128)(2,1)S(1)} collective-permute-done((bf16[256,384]{1,0:T(8,128)(2,1)S(1)}, bf16[256,384]{1,0:T(8,128)(2,1)S(1)}, u32[]{:S(2)}, u32[]{:S(2)}) %collective-permute-start.26) | collective-permute-done | bytes 196640 | tf_op jit(solution)/shard_map/ppermute | solution.py:523
  68.6 1.7 %collective-permute-start.27 = (bf16[1,160,384]{2,1,0:T(8,128)(2,1)S(1)}, bf16[1,160,384]{2,1,0:T(8,128)(2,1)S(1)}, u32[]{:S(2)}, u32[]{:S(2)}) collective-permute-start(bf16[1,160,384]{2,1,0:T(8,128)(2,1)S(1)} %get-tuple-element.99), channel_id=1, source_target_pairs={{0,4},{1,5},{2,6},{3,7},{4,0},{5,1},{6,2},{7,3},{8,12},{9,13},{10,... | collective-permute-start | bytes 368648 | tf_op jit(solution)/shard_map/ppermute | solution.py:523
  70.3 1.3 %collective-permute-start.28 = (bf16[1,48,1024]{2,1,0:T(8,128)(2,1)S(1)}, bf16[1,48,1024]{2,1,0:T(8,128)(2,1)S(1)}, u32[]{:S(2)}, u32[]{:S(2)}) collective-permute-start(bf16[1,48,1024]{2,1,0:T(8,128)(2,1)S(1)} %get-tuple-element.100), channel_id=1, source_target_pairs={{0,8},{1,9},{2,10},{3,11},{4,12},{5,13},{6,14},{7,15},{8,0},{9,1},... | collective-permute-start | bytes 294920 | tf_op jit(solution)/shard_map/ppermute | solution.py:523
  71.6 1.7 %collective-permute-start.30 = (bf16[1,128,384]{2,1,0:T(8,128)(2,1)S(1)}, bf16[1,128,384]{2,1,0:T(8,128)(2,1)S(1)}, u32[]{:S(2)}, u32[]{:S(2)}) collective-permute-start(bf16[1,128,384]{2,1,0:T(8,128)(2,1)S(1)} %conv_send_on.3), channel_id=1, source_target_pairs={{0,8},{1,9},{2,10},{3,11},{4,12},{5,13},{6,14},{7,15},{8,0},{9,1},... | collective-permute-start | bytes 294920 | tf_op jit(solution)/shard_map/ppermute | solution.py:523
  73.7 2.6 %collective-permute-done.27.refs_1_ = bf16[1,160,384]{2,1,0:T(8,128)(2,1)S(1)} collective-permute-done((bf16[1,160,384]{2,1,0:T(8,128)(2,1)S(1)}, bf16[1,160,384]{2,1,0:T(8,128)(2,1)S(1)}, u32[]{:S(2)}, u32[]{:S(2)}) %collective-permute-start.27) | collective-permute-done | bytes 122912 | tf_op jit(solution)/shard_map/ppermute | solution.py:523
  76.3 1.4 %collective-permute-start.32 = (bf16[1,160,384]{2,1,0:T(8,128)(2,1)S(1)}, bf16[1,160,384]{2,1,0:T(8,128)(2,1)S(1)}, u32[]{:S(2)}, u32[]{:S(2)}) collective-permute-start(bf16[1,160,384]{2,1,0:T(8,128)(2,1)S(1)} %conv_send_on.2), channel_id=1, source_target_pairs={{0,8},{1,9},{2,10},{3,11},{4,12},{5,13},{6,14},{7,15},{8,0},{9,1},... | collective-permute-start | bytes 368648 | tf_op jit(solution)/shard_map/ppermute | solution.py:523
  77.7 2.5 %collective-permute-done.28.refs_5_ = bf16[1,48,1024]{2,1,0:T(8,128)(2,1)S(1)} collective-permute-done((bf16[1,48,1024]{2,1,0:T(8,128)(2,1)S(1)}, bf16[1,48,1024]{2,1,0:T(8,128)(2,1)S(1)}, u32[]{:S(2)}, u32[]{:S(2)}) %collective-permute-start.28) | collective-permute-done | bytes 98336 | tf_op jit(solution)/shard_map/ppermute | solution.py:523
  80.2 2.8 %collective-permute-done.30.refs_6_.refs_2_ = bf16[1,128,384]{2,1,0:T(8,128)(2,1)S(1)} collective-permute-done((bf16[1,128,384]{2,1,0:T(8,128)(2,1)S(1)}, bf16[1,128,384]{2,1,0:T(8,128)(2,1)S(1)}, u32[]{:S(2)}, u32[]{:S(2)}) %collective-permute-start.30) | collective-permute-done | bytes 98336 | tf_op jit(solution)/shard_map/ppermute | solution.py:523
  83.0 2.1 %input_grad.1 = bf16[256,384]{1,0:T(8,128)(2,1)} custom-call(bf16[256,384]{1,0:T(8,128)(2,1)S(1)} %bitcast.10, bf16[144,384]{1,0:T(8,128)(2,1)S(1)} %get-tuple-element.87.refs_1_, bf16[256,384]{1,0:T(8,128)(2,1)S(1)} %get-tuple-element.93.refs_2_, bf16[144,384]{1,0:T(8,128)(2,1)S(1)} %collective-permute-done.24.refs_3_, ...), custom_call_target="tpu_custom_call" | custom-call | flops 7549747200 | bytes 4153344 | tf_op jit(solution)/shard_map/input_grad/pallas_call | solution.py:37
  (69 shorter events, 16.8 us)
Async XLA Ops:
  1.8 6.7 %collective-permute-start.1 = (bf16[32,384]{1,0:T(8,128)(2,1)S(1)}, bf16[32,384]{1,0:T(8,128)(2,1)S(1)}, u32[]{:S(2)}, u32[]{:S(2)}) collective-permute-start(bf16[32,384]{1,0:T(8,128)(2,1)S(1)} %get-tuple-element.60), channel_id=1, source_target_pairs={{2,4},{6,8},{10,12},{4,2},{8,6},{12,10},{3,5},{7,9},{11,13},{5,3},... | collective-permute-start | bytes 73736 | tf_op jit(solution)/shard_map/ppermute | solution.py:554
  2.6 7.7 %collective-permute-start = (bf16[32,384]{1,0:T(8,128)(2,1)S(1)}, bf16[32,384]{1,0:T(8,128)(2,1)S(1)}, u32[]{:S(2)}, u32[]{:S(2)}) collective-permute-start(bf16[32,384]{1,0:T(8,128)(2,1)S(1)} %get-tuple-element.60), channel_id=1, source_target_pairs={{0,2},{1,3},{2,0},{3,1},{4,6},{5,7},{6,4},{7,5},{8,10},{9,11},{10,... | collective-permute-start | bytes 73736 | tf_op jit(solution)/shard_map/ppermute | solution.py:523
  12.2 6.1 %collective-permute-start.4 = (bf16[320,128]{1,0:T(8,128)(2,1)S(1)}, bf16[320,128]{1,0:T(8,128)(2,1)S(1)}, u32[]{:S(2)}, u32[]{:S(2)}) collective-permute-start(bf16[320,128]{1,0:T(8,128)(2,1)S(1)} %get-tuple-element.63.refs_2_), channel_id=1, source_target_pairs={{0,4},{1,5},{2,6},{3,7},{4,0},{5,1},{6,2},{7,3},{8,12},{9,13},{10,... | collective-permute-start | bytes 245768 | tf_op jit(solution)/shard_map/ppermute | solution.py:523
  14.2 6.6 %collective-permute-start.3 = (bf16[320,128]{1,0:T(8,128)(2,1)S(1)}, bf16[320,128]{1,0:T(8,128)(2,1)S(1)}, u32[]{:S(2)}, u32[]{:S(2)}) collective-permute-start(bf16[320,128]{1,0:T(8,128)(2,1)S(1)} %get-tuple-element.63.refs_2_), channel_id=1, source_target_pairs={{0,12},{1,13},{2,14},{3,15},{4,8},{5,9},{6,10},{7,11},{8,4},{9,5},... | collective-permute-start | bytes 245768 | tf_op jit(solution)/shard_map/ppermute | solution.py:523
  16.7 6.6 %collective-permute-start.2 = (bf16[320,128]{1,0:T(8,128)(2,1)S(1)}, bf16[320,128]{1,0:T(8,128)(2,1)S(1)}, u32[]{:S(2)}, u32[]{:S(2)}) collective-permute-start(bf16[320,128]{1,0:T(8,128)(2,1)S(1)} %get-tuple-element.63.refs_2_), channel_id=1, source_target_pairs={{0,8},{1,9},{2,10},{3,11},{4,12},{5,13},{6,14},{7,15},{8,0},{9,1},... | collective-permute-start | bytes 245768 | tf_op jit(solution)/shard_map/ppermute | solution.py:523
  16.8 8.4 %collective-permute-start.5 = (bf16[320,128]{1,0:T(8,128)(2,1)S(1)}, bf16[320,128]{1,0:T(8,128)(2,1)S(1)}, u32[]{:S(2)}, u32[]{:S(2)}) collective-permute-start(bf16[320,128]{1,0:T(8,128)(2,1)S(1)} %get-tuple-element.63.refs_2_), channel_id=1, source_target_pairs={{0,2},{1,3},{2,0},{3,1},{4,6},{5,7},{6,4},{7,5},{8,10},{9,11},{10,... | collective-permute-start | bytes 245768 | tf_op jit(solution)/shard_map/ppermute | solution.py:523
  18.3 6.9 %collective-permute-start.8 = (bf16[320,128]{1,0:T(8,128)(2,1)S(1)}, bf16[320,128]{1,0:T(8,128)(2,1)S(1)}, u32[]{:S(2)}, u32[]{:S(2)}) collective-permute-start(bf16[320,128]{1,0:T(8,128)(2,1)S(1)} %collective-permute-done.4.refs_5_), channel_id=1, source_target_pairs={{0,2},{1,3},{2,0},{3,1},{4,6},{5,7},{6,4},{7,5},{8,10},{9,11},{10,... | collective-permute-start | bytes 245768 | tf_op jit(solution)/shard_map/ppermute | solution.py:523
  20.8 5.1 %collective-permute-start.7 = (bf16[320,128]{1,0:T(8,128)(2,1)S(1)}, bf16[320,128]{1,0:T(8,128)(2,1)S(1)}, u32[]{:S(2)}, u32[]{:S(2)}) collective-permute-start(bf16[320,128]{1,0:T(8,128)(2,1)S(1)} %collective-permute-done.3.refs_4_), channel_id=1, source_target_pairs={{0,2},{1,3},{2,0},{3,1},{4,6},{5,7},{6,4},{7,5},{8,10},{9,11},{10,... | collective-permute-start | bytes 245768 | tf_op jit(solution)/shard_map/ppermute | solution.py:523
  23.3 4.4 %collective-permute-start.6 = (bf16[320,128]{1,0:T(8,128)(2,1)S(1)}, bf16[320,128]{1,0:T(8,128)(2,1)S(1)}, u32[]{:S(2)}, u32[]{:S(2)}) collective-permute-start(bf16[320,128]{1,0:T(8,128)(2,1)S(1)} %collective-permute-done.2.refs_3_), channel_id=1, source_target_pairs={{0,2},{1,3},{2,0},{3,1},{4,6},{5,7},{6,4},{7,5},{8,10},{9,11},{10,... | collective-permute-start | bytes 245768 | tf_op jit(solution)/shard_map/ppermute | solution.py:523
  27.7 7.7 %collective-permute-start.10 = (bf16[416,384]{1,0:T(8,128)(2,1)S(1)}, bf16[416,384]{1,0:T(8,128)(2,1)S(1)}, u32[]{:S(2)}, u32[]{:S(2)}) collective-permute-start(bf16[416,384]{1,0:T(8,128)(2,1)S(1)} %get-tuple-element.70), channel_id=1, source_target_pairs={{0,2},{1,3},{2,0},{3,1},{4,6},{5,7},{6,4},{7,5},{8,10},{9,11},{10,... | collective-permute-start | bytes 958472 | tf_op jit(solution)/shard_map/ppermute | solution.py:523
  35.4 2.8 %collective-permute-start.11 = (bf16[416,384]{1,0:T(8,128)(2,1)S(1)}, bf16[416,384]{1,0:T(8,128)(2,1)S(1)}, u32[]{:S(2)}, u32[]{:S(2)}) collective-permute-start(bf16[416,384]{1,0:T(8,128)(2,1)S(1)} %collective-permute-done.10.refs_3_), channel_id=1, source_target_pairs={{0,1},{1,0},{2,3},{3,2},{4,5},{5,4},{6,7},{7,6},{8,9},{9,8},{10,11... | collective-permute-start | bytes 958472 | tf_op jit(solution)/shard_map/ppermute | solution.py:523
  35.4 2.7 %collective-permute-start.9 = (bf16[352,384]{1,0:T(8,128)(2,1)S(1)}, bf16[352,384]{1,0:T(8,128)(2,1)S(1)}, u32[]{:S(2)}, u32[]{:S(2)}) collective-permute-start(bf16[352,384]{1,0:T(8,128)(2,1)S(1)} %get-tuple-element.68), channel_id=1, source_target_pairs={{0,1},{1,0},{2,3},{3,2},{4,5},{5,4},{6,7},{7,6},{8,9},{9,8},{10,11... | collective-permute-start | bytes 811016 | tf_op jit(solution)/shard_map/ppermute | solution.py:523
  35.9 7.2 %collective-permute-start.12 = (bf16[4,160,128]{2,1,0:T(8,128)(2,1)S(1)}, bf16[4,160,128]{2,1,0:T(8,128)(2,1)S(1)}, u32[]{:S(2)}, u32[]{:S(2)}) collective-permute-start(bf16[4,160,128]{2,1,0:T(8,128)(2,1)S(1)} %get-tuple-element.71), channel_id=1, source_target_pairs={{0,2},{1,3},{2,0},{3,1},{4,6},{5,7},{6,4},{7,5},{8,10},{9,11},{10,... | collective-permute-start | bytes 491528 | tf_op jit(solution)/shard_map/ppermute | solution.py:523
  37.3 5.8 %collective-permute-start.13 = (bf16[4,160,128]{2,1,0:T(8,128)(2,1)S(1)}, bf16[4,160,128]{2,1,0:T(8,128)(2,1)S(1)}, u32[]{:S(2)}, u32[]{:S(2)}) collective-permute-start(bf16[4,160,128]{2,1,0:T(8,128)(2,1)S(1)} %get-tuple-element.78), channel_id=1, source_target_pairs={{0,4},{1,5},{2,6},{3,7},{4,0},{5,1},{6,2},{7,3},{8,12},{9,13},{10,... | collective-permute-start | bytes 491528 | tf_op jit(solution)/shard_map/ppermute | solution.py:523
  43.2 4.5 %collective-permute-start.14 = (bf16[2,160,128]{2,1,0:T(8,128)(2,1)S(1)}, bf16[2,160,128]{2,1,0:T(8,128)(2,1)S(1)}, u32[]{:S(2)}, u32[]{:S(2)}) collective-permute-start(bf16[2,160,128]{2,1,0:T(8,128)(2,1)S(1)} %get-tuple-element.80), channel_id=1, source_target_pairs={{0,4},{1,5},{2,6},{3,7},{4,0},{5,1},{6,2},{7,3},{8,12},{9,13},{10,... | collective-permute-start | bytes 245768 | tf_op jit(solution)/shard_map/ppermute | solution.py:523
  44.1 4.4 %collective-permute-start.15 = (bf16[2,160,128]{2,1,0:T(8,128)(2,1)S(1)}, bf16[2,160,128]{2,1,0:T(8,128)(2,1)S(1)}, u32[]{:S(2)}, u32[]{:S(2)}) collective-permute-start(bf16[2,160,128]{2,1,0:T(8,128)(2,1)S(1)} %get-tuple-element.82), channel_id=1, source_target_pairs={{0,2},{1,3},{2,0},{3,1},{4,6},{5,7},{6,4},{7,5},{8,10},{9,11},{10,... | collective-permute-start | bytes 245768 | tf_op jit(solution)/shard_map/ppermute | solution.py:523
  48.6 7.4 %collective-permute-start.17 = (bf16[128,1024]{1,0:T(8,128)(2,1)S(1)}, bf16[128,1024]{1,0:T(8,128)(2,1)S(1)}, u32[]{:S(2)}, u32[]{:S(2)}) collective-permute-start(bf16[128,1024]{1,0:T(8,128)(2,1)S(1)} %get-tuple-element.84.refs_0_.refs_1_), channel_id=1, source_target_pairs={{0,2},{1,3},{2,0},{3,1},{4,6},{5,7},{6,4},{7,5},{8,10},{9,11},{10,... | collective-permute-start | bytes 786440 | tf_op jit(solution)/shard_map/ppermute | solution.py:523
  49.4 6.2 %collective-permute-start.18 = (bf16[1,320,128]{2,1,0:T(8,128)(2,1)S(1)}, bf16[1,320,128]{2,1,0:T(8,128)(2,1)S(1)}, u32[]{:S(2)}, u32[]{:S(2)}) collective-permute-start(bf16[1,320,128]{2,1,0:T(8,128)(2,1)S(1)} %get-tuple-element.85), channel_id=1, source_target_pairs={{0,8},{1,9},{2,10},{3,11},{4,12},{5,13},{6,14},{7,15},{8,0},{9,1},... | collective-permute-start | bytes 245768 | tf_op jit(solution)/shard_map/ppermute | solution.py:523
  52.1 6.1 %collective-permute-start.16 = (bf16[128,1024]{1,0:T(8,128)(2,1)S(1)}, bf16[128,1024]{1,0:T(8,128)(2,1)S(1)}, u32[]{:S(2)}, u32[]{:S(2)}) collective-permute-start(bf16[128,1024]{1,0:T(8,128)(2,1)S(1)} %get-tuple-element.84.refs_0_.refs_1_), channel_id=1, source_target_pairs={{0,1},{1,0},{2,3},{3,2},{4,5},{5,4},{6,7},{7,6},{8,9},{9,8},{10,11... | collective-permute-start | bytes 786440 | tf_op jit(solution)/shard_map/ppermute | solution.py:523
  56.0 2.2 %collective-permute-start.19 = (bf16[128,1024]{1,0:T(8,128)(2,1)S(1)}, bf16[128,1024]{1,0:T(8,128)(2,1)S(1)}, u32[]{:S(2)}, u32[]{:S(2)}) collective-permute-start(bf16[128,1024]{1,0:T(8,128)(2,1)S(1)} %collective-permute-done.17.refs_3_), channel_id=1, source_target_pairs={{0,1},{1,0},{2,3},{3,2},{4,5},{5,4},{6,7},{7,6},{8,9},{9,8},{10,11... | collective-permute-start | bytes 786440 | tf_op jit(solution)/shard_map/ppermute | solution.py:523
  56.1 5.9 %collective-permute-start.24 = (bf16[144,384]{1,0:T(8,128)(2,1)S(1)}, bf16[144,384]{1,0:T(8,128)(2,1)S(1)}, u32[]{:S(2)}, u32[]{:S(2)}) collective-permute-start(bf16[144,384]{1,0:T(8,128)(2,1)S(1)} %get-tuple-element.87.refs_1_), channel_id=1, source_target_pairs={{0,2},{1,3},{2,0},{3,1},{4,6},{5,7},{6,4},{7,5},{8,10},{9,11},{10,... | collective-permute-start | bytes 331784 | tf_op jit(solution)/shard_map/ppermute | solution.py:523
  57.5 8.3 %collective-permute-start.22 = (bf16[256,384]{1,0:T(8,128)(2,1)S(1)}, bf16[256,384]{1,0:T(8,128)(2,1)S(1)}, u32[]{:S(2)}, u32[]{:S(2)}) collective-permute-start(bf16[256,384]{1,0:T(8,128)(2,1)S(1)} %get-tuple-element.93.refs_2_), channel_id=1, source_target_pairs={{0,2},{1,3},{2,0},{3,1},{4,6},{5,7},{6,4},{7,5},{8,10},{9,11},{10,... | collective-permute-start | bytes 589832 | tf_op jit(solution)/shard_map/ppermute | solution.py:523
  59.0 7.1 %collective-permute-start.20 = (bf16[2,48,1024]{2,1,0:T(8,128)(2,1)S(1)}, bf16[2,48,1024]{2,1,0:T(8,128)(2,1)S(1)}, u32[]{:S(2)}, u32[]{:S(2)}) collective-permute-start(bf16[2,48,1024]{2,1,0:T(8,128)(2,1)S(1)} %get-tuple-element.90), channel_id=1, source_target_pairs={{0,4},{1,5},{2,6},{3,7},{4,0},{5,1},{6,2},{7,3},{8,12},{9,13},{10,... | collective-permute-start | bytes 589832 | tf_op jit(solution)/shard_map/ppermute | solution.py:523
  59.4 3.1 %collective-permute-start.23 = (bf16[144,384]{1,0:T(8,128)(2,1)S(1)}, bf16[144,384]{1,0:T(8,128)(2,1)S(1)}, u32[]{:S(2)}, u32[]{:S(2)}) collective-permute-start(bf16[144,384]{1,0:T(8,128)(2,1)S(1)} %get-tuple-element.87.refs_1_), channel_id=1, source_target_pairs={{0,1},{1,0},{2,3},{3,2},{4,5},{5,4},{6,7},{7,6},{8,9},{9,8},{10,11... | collective-permute-start | bytes 331784 | tf_op jit(solution)/shard_map/ppermute | solution.py:523
  62.0 4.2 %collective-permute-start.21 = (bf16[256,384]{1,0:T(8,128)(2,1)S(1)}, bf16[256,384]{1,0:T(8,128)(2,1)S(1)}, u32[]{:S(2)}, u32[]{:S(2)}) collective-permute-start(bf16[256,384]{1,0:T(8,128)(2,1)S(1)} %get-tuple-element.93.refs_2_), channel_id=1, source_target_pairs={{0,1},{1,0},{2,3},{3,2},{4,5},{5,4},{6,7},{7,6},{8,9},{9,8},{10,11... | collective-permute-start | bytes 589832 | tf_op jit(solution)/shard_map/ppermute | solution.py:523
  65.8 5.8 %collective-permute-start.29 = (bf16[1,128,384]{2,1,0:T(8,128)(2,1)S(1)}, bf16[1,128,384]{2,1,0:T(8,128)(2,1)S(1)}, u32[]{:S(2)}, u32[]{:S(2)}) collective-permute-start(bf16[1,128,384]{2,1,0:T(8,128)(2,1)S(1)} %get-tuple-element.102), channel_id=1, source_target_pairs={{0,4},{1,5},{2,6},{3,7},{4,0},{5,1},{6,2},{7,3},{8,12},{9,13},{10,... | collective-permute-start | bytes 294920 | tf_op jit(solution)/shard_map/ppermute | solution.py:523
  66.1 1.4 %collective-permute-start.26 = (bf16[256,384]{1,0:T(8,128)(2,1)S(1)}, bf16[256,384]{1,0:T(8,128)(2,1)S(1)}, u32[]{:S(2)}, u32[]{:S(2)}) collective-permute-start(bf16[256,384]{1,0:T(8,128)(2,1)S(1)} %collective-permute-done.22.refs_4_), channel_id=1, source_target_pairs={{0,1},{1,0},{2,3},{3,2},{4,5},{5,4},{6,7},{7,6},{8,9},{9,8},{10,11... | collective-permute-start | bytes 589832 | tf_op jit(solution)/shard_map/ppermute | solution.py:523
  68.6 7.7 %collective-permute-start.27 = (bf16[1,160,384]{2,1,0:T(8,128)(2,1)S(1)}, bf16[1,160,384]{2,1,0:T(8,128)(2,1)S(1)}, u32[]{:S(2)}, u32[]{:S(2)}) collective-permute-start(bf16[1,160,384]{2,1,0:T(8,128)(2,1)S(1)} %get-tuple-element.99), channel_id=1, source_target_pairs={{0,4},{1,5},{2,6},{3,7},{4,0},{5,1},{6,2},{7,3},{8,12},{9,13},{10,... | collective-permute-start | bytes 368648 | tf_op jit(solution)/shard_map/ppermute | solution.py:523
  70.3 10.0 %collective-permute-start.28 = (bf16[1,48,1024]{2,1,0:T(8,128)(2,1)S(1)}, bf16[1,48,1024]{2,1,0:T(8,128)(2,1)S(1)}, u32[]{:S(2)}, u32[]{:S(2)}) collective-permute-start(bf16[1,48,1024]{2,1,0:T(8,128)(2,1)S(1)} %get-tuple-element.100), channel_id=1, source_target_pairs={{0,8},{1,9},{2,10},{3,11},{4,12},{5,13},{6,14},{7,15},{8,0},{9,1},... | collective-permute-start | bytes 294920 | tf_op jit(solution)/shard_map/ppermute | solution.py:523
  71.6 11.4 %collective-permute-start.30 = (bf16[1,128,384]{2,1,0:T(8,128)(2,1)S(1)}, bf16[1,128,384]{2,1,0:T(8,128)(2,1)S(1)}, u32[]{:S(2)}, u32[]{:S(2)}) collective-permute-start(bf16[1,128,384]{2,1,0:T(8,128)(2,1)S(1)} %conv_send_on.3), channel_id=1, source_target_pairs={{0,8},{1,9},{2,10},{3,11},{4,12},{5,13},{6,14},{7,15},{8,0},{9,1},... | collective-permute-start | bytes 294920 | tf_op jit(solution)/shard_map/ppermute | solution.py:523
  73.3 12.2 %collective-permute-start.31 = (bf16[1,288,384]{2,1,0:T(8,128)(2,1)S(1)}, bf16[1,288,384]{2,1,0:T(8,128)(2,1)S(1)}, u32[]{:S(2)}, u32[]{:S(2)}) collective-permute-start(bf16[1,288,384]{2,1,0:T(8,128)(2,1)S(1)} %get-tuple-element.104), channel_id=1, source_target_pairs={{0,4},{1,5},{2,6},{3,7},{4,0},{5,1},{6,2},{7,3},{8,12},{9,13},{10,... | collective-permute-start | bytes 663560 | tf_op jit(solution)/shard_map/ppermute | solution.py:523
  76.3 9.3 %collective-permute-start.32 = (bf16[1,160,384]{2,1,0:T(8,128)(2,1)S(1)}, bf16[1,160,384]{2,1,0:T(8,128)(2,1)S(1)}, u32[]{:S(2)}, u32[]{:S(2)}) collective-permute-start(bf16[1,160,384]{2,1,0:T(8,128)(2,1)S(1)} %conv_send_on.2), channel_id=1, source_target_pairs={{0,8},{1,9},{2,10},{3,11},{4,12},{5,13},{6,14},{7,15},{8,0},{9,1},... | collective-permute-start | bytes 368648 | tf_op jit(solution)/shard_map/ppermute | solution.py:523
  (9 other events, 93.6 us)

commit v13 on v12

--- a/solution.py
+++ b/solution.py
@@ -237,15 +237,20 @@
     send[...] = total[keep.shape[0] :].astype(BF)
 
 
-def fold_two_kernel(*refs):
-    fold_kernel(refs[0], refs[1], refs[4], refs[5])
-    fold_kernel(refs[2], refs[3], refs[6], refs[7])
-
-
-def merge_kernel(keep_a, in_a, keep_b, in_b, keep, send):
-    total = jnp.concatenate([total_of((keep_a, in_a)), total_of((keep_b, in_b))], axis=1)
-    keep[...] = total[: keep.shape[0]]
-    send[...] = total[keep.shape[0] :].astype(BF)
+def share_kernel(keep_a, in_a, keep_b, in_b, *outs, masks_a, masks_b):
+    left = left_masks(masks_a, masks_b)
+    total_a, total_b = total_of((keep_a, in_a)), total_of((keep_b, in_b))
+    for out, mask in zip(outs, left):
+        parts = []
+        if mask in masks_a:
+            parts.append(total_a[masks_a.index(mask)])
+        if mask in masks_b:
+            parts.append(total_b[masks_b.index(mask)])
+        out[...] = jnp.concatenate(parts, axis=0).astype(out.dtype)
+
+
+def left_masks(masks_a, masks_b):
+    return sorted(set(masks_a) | set(masks_b))
 
 
 def send_on_kernel(keep, came, out):
@@ -256,10 +261,18 @@
     out[...] = dot_t(dq[...], wq[...])
 
 
-def middle_kernel(own, came, part, pooled_in, gain_in, wk, wv, first, second, *edges):
-    size = own.shape[2]
+def middle_kernel(*refs, masks_a, masks_b):
+    left = left_masks(masks_a, masks_b)
+    part, pooled_in, gain_in, wk, wv, first, second, *edges = refs[len(left) :]
+    size = refs[0].shape[1]
     tokens, width = pooled_in.shape
-    total = (own[0] + came[0].astype(F32)).astype(BF).astype(F32)
+    half = refs[0].shape[0] // 2
+    top, bottom = refs[0][:half], refs[0][half:]
+    for came, mask in zip(refs[1:], left[1:]):
+        came = came[...].astype(F32)
+        top = top + came[:half] if mask in masks_a else top
+        bottom = bottom + came[-half:] if mask in masks_b else bottom
+    total = jnp.concatenate([top, bottom], axis=0).astype(BF).astype(F32)
     key_cot = total[:tokens]
     value_cot = unpack_values(total, tokens, size)
     normed_cot = part[...] + dot_t(key_cot.astype(BF), wk[...])
@@ -632,22 +645,22 @@
         flops=2 * groups * conv_pad * taps * channels * 8 * tokens,
         name="select",
     )
-    fourth = (groups // 2,) + half_block[1:]
-    keep_a, send_a, keep_b, send_b = run(
-        fold_two_kernel,
-        [(fourth, F32), (fourth, BF)] * 2,
+    ways = dict(masks_a=ordered(bits[1:]), masks_b=ordered([0] + bits[2:]))
+    left = left_masks(**ways)
+    both = [(mask in ways["masks_a"]) + (mask in ways["masks_b"]) for mask in left]
+    sums = run(
+        lambda *refs: share_kernel(*refs, **ways),
+        [
+            ((half_block[1] * n, key_size), F32 if mask == 0 else BF)
+            for mask, n in zip(left, both)
+        ],
         [keep_a, in_a, keep_b, in_b],
-        name="kv_cot_fold",
+        name="kv_cot_share",
         after=[conv_pick],
     )
-    in_a, in_b = swap(send_a, 2), swap(send_b, 1)
-    block = (groups // 4, 5 * tokens // 2, key_size)
-    keep, send = run(
-        merge_kernel,
-        [(block, F32), (block, BF)],
-        [keep_a, in_a, keep_b, in_b],
-        name="kv_cot_merge",
-    )
+    query_cot = held(query_cot, sums[0])
+    query_near, query_core = swap(query_cot, 1), swap(query_cot, 0, 1)
+    kv_cot = [sums[0]] + [swap(part, mask) for part, mask in zip(sums[1:], left[1:])]
     (normed_cot,) = run(
         query_cot_kernel,
         [((tokens, width), F32)],
@@ -655,11 +668,8 @@
         flops=2 * tokens * width * heads * key_size,
         name="query_part",
     )
-    query_cot = held(query_cot, keep)
-    query_near, query_core = swap(query_cot, 1), swap(query_cot, 0, 1)
-    kv_cot = halved(keep, send, bits[2:], "kv_cot_fold")
     first, second, *edge = run(
-        middle_kernel,
+        lambda *refs: middle_kernel(*refs, **ways),
         [
             ((tokens + 16, width // 2), BF),
             ((2 * tokens, width // 2), BF),

time: 86.6 us -> 88.1 us (1.017)
  starting transfers between devices: 35.2 us -> 39.8 us
  waiting for transfers between devices: 30.9 us -> 27.7 us
    ppermute x32 -> x34, starting transfers between devices: 34.4 us -> 39 us  [swap(): lax.ppermute(value, both_axes, [(i, i ^ mask) for i in range(owners)])]
    ppermute x32 -> x34, waiting for transfers between devices: 30.9 us -> 27.7 us  [swap(): lax.ppermute(value, both_axes, [(i, i ^ mask) for i in range(owners)])]
    pallas_call x18 -> x17, Pallas kernels: 18.5 us -> 18.5 us  [run(): pl.pallas_call(whole, out_shape=[jax.ShapeDtypeStruct(s, t) for s, t in o...]
  transfers between devices with their start and end apart: 33 -> 35, of which waited for: 18 -> 17; matrix products, arithmetic and copies ran while one was open for 0% -> 0% of each run, Pallas kernels for 18% -> 18%
where the time goes in v13:
time: 88.1 us; the launch traced here: 87.8 us
  starting transfers between devices  39.8 us (45%)
  waiting for transfers between devices  27.7 us (31%)
  Pallas kernels  18.5 us (21%)
  local copies, waits for them, and re-layouts  0.96 us (1%)
    ppermute x34, starting transfers between devices, swap(): lax.ppermute(value, both_axes, [(i, i ^ mask) for i in range(owners)])  39 us
    ppermute x34, waiting for transfers between devices, swap(): lax.ppermute(value, both_axes, [(i, i ^ mask) for i in range(owners)])  27.7 us
    pallas_call x17, Pallas kernels, run(): pl.pallas_call(whole, out_shape=[jax.ShapeDtypeStruct(s, t) for s, t in o...  18.5 us
  transfers between devices with their start and end apart: 35, of which 17 were waited for; matrix products, arithmetic and copies ran while one was open for 0% of the time, Pallas kernels for 18%

profile of v13, /device:TPU:0, one launch (start us, length us, event | category | flops | bytes accessed | tf_op | source)
XLA Modules:
  0.0 87.8 jit_solution(9875749526804674778)
XLA Ops:
  2.6 5.9 %collective-permute-start = (bf16[32,384]{1,0:T(8,128)(2,1)S(1)}, bf16[32,384]{1,0:T(8,128)(2,1)S(1)}, u32[]{:S(2)}, u32[]{:S(2)}) collective-permute-start(bf16[32,384]{1,0:T(8,128)(2,1)S(1)} %get-tuple-element.60), channel_id=1, source_target_pairs={{0,2},{1,3},{2,0},{3,1},{4,6},{5,7},{6,4},{7,5},{8,10},{9,11},{10,... | collective-permute-start | bytes 73736 | tf_op jit(solution)/shard_map/ppermute | solution.py:536
  8.5 1.8 %collective-permute-done.refs_1_ = bf16[32,384]{1,0:T(8,128)(2,1)S(1)} collective-permute-done((bf16[32,384]{1,0:T(8,128)(2,1)S(1)}, bf16[32,384]{1,0:T(8,128)(2,1)S(1)}, u32[]{:S(2)}, u32[]{:S(2)}) %collective-permute-start) | collective-permute-done | bytes 24608 | tf_op jit(solution)/shard_map/ppermute | solution.py:536
  10.3 1.9 %front.1 = (bf16[320,128]{1,0:T(8,128)(2,1)S(1)}, bf16[288,384]{1,0:T(8,128)(2,1)S(1)}, bf16[128,768]{1,0:T(8,128)(2,1)S(1)}, f32[128,768]{1,0:T(8,128)S(1)}) custom-call(f32[3,304,128]{2,1,0:T(8,128)S(1)} %get-tuple-element.59.refs_0_, bf16[32,384]{1,0:T(8,128)(2,1)S(1)} %collective-permute-done.refs_1_, ...), custom_call_target="tpu_custom_call" | custom-call | flops 754974720 | bytes 4852736 | tf_op jit(solution)/shard_map/front/pallas_call | solution.py:37
  12.2 2.0 %collective-permute-start.4 = (bf16[320,128]{1,0:T(8,128)(2,1)S(1)}, bf16[320,128]{1,0:T(8,128)(2,1)S(1)}, u32[]{:S(2)}, u32[]{:S(2)}) collective-permute-start(bf16[320,128]{1,0:T(8,128)(2,1)S(1)} %get-tuple-element.63.refs_2_), channel_id=1, source_target_pairs={{0,4},{1,5},{2,6},{3,7},{4,0},{5,1},{6,2},{7,3},{8,12},{9,13},{10,... | collective-permute-start | bytes 245768 | tf_op jit(solution)/shard_map/ppermute | solution.py:536
  14.2 2.5 %collective-permute-start.3 = (bf16[320,128]{1,0:T(8,128)(2,1)S(1)}, bf16[320,128]{1,0:T(8,128)(2,1)S(1)}, u32[]{:S(2)}, u32[]{:S(2)}) collective-permute-start(bf16[320,128]{1,0:T(8,128)(2,1)S(1)} %get-tuple-element.63.refs_2_), channel_id=1, source_target_pairs={{0,12},{1,13},{2,14},{3,15},{4,8},{5,9},{6,10},{7,11},{8,4},{9,5},... | collective-permute-start | bytes 245768 | tf_op jit(solution)/shard_map/ppermute | solution.py:536
  16.8 1.5 %collective-permute-start.5 = (bf16[320,128]{1,0:T(8,128)(2,1)S(1)}, bf16[320,128]{1,0:T(8,128)(2,1)S(1)}, u32[]{:S(2)}, u32[]{:S(2)}) collective-permute-start(bf16[320,128]{1,0:T(8,128)(2,1)S(1)} %get-tuple-element.63.refs_2_), channel_id=1, source_target_pairs={{0,2},{1,3},{2,0},{3,1},{4,6},{5,7},{6,4},{7,5},{8,10},{9,11},{10,... | collective-permute-start | bytes 245768 | tf_op jit(solution)/shard_map/ppermute | solution.py:536
  18.3 1.3 %collective-permute-start.8 = (bf16[320,128]{1,0:T(8,128)(2,1)S(1)}, bf16[320,128]{1,0:T(8,128)(2,1)S(1)}, u32[]{:S(2)}, u32[]{:S(2)}) collective-permute-start(bf16[320,128]{1,0:T(8,128)(2,1)S(1)} %collective-permute-done.4.refs_5_), channel_id=1, source_target_pairs={{0,2},{1,3},{2,0},{3,1},{4,6},{5,7},{6,4},{7,5},{8,10},{9,11},{10,... | collective-permute-start | bytes 245768 | tf_op jit(solution)/shard_map/ppermute | solution.py:536
  19.6 1.2 %collective-permute-done.3.refs_4_ = bf16[320,128]{1,0:T(8,128)(2,1)S(1)} collective-permute-done((bf16[320,128]{1,0:T(8,128)(2,1)S(1)}, bf16[320,128]{1,0:T(8,128)(2,1)S(1)}, u32[]{:S(2)}, u32[]{:S(2)}) %collective-permute-start.3) | collective-permute-done | bytes 81952 | tf_op jit(solution)/shard_map/ppermute | solution.py:536
  20.8 1.4 %collective-permute-start.7 = (bf16[320,128]{1,0:T(8,128)(2,1)S(1)}, bf16[320,128]{1,0:T(8,128)(2,1)S(1)}, u32[]{:S(2)}, u32[]{:S(2)}) collective-permute-start(bf16[320,128]{1,0:T(8,128)(2,1)S(1)} %collective-permute-done.3.refs_4_), channel_id=1, source_target_pairs={{0,2},{1,3},{2,0},{3,1},{4,6},{5,7},{6,4},{7,5},{8,10},{9,11},{10,... | collective-permute-start | bytes 245768 | tf_op jit(solution)/shard_map/ppermute | solution.py:536
  22.2 1.1 %collective-permute-done.2.refs_3_ = bf16[320,128]{1,0:T(8,128)(2,1)S(1)} collective-permute-done((bf16[320,128]{1,0:T(8,128)(2,1)S(1)}, bf16[320,128]{1,0:T(8,128)(2,1)S(1)}, u32[]{:S(2)}, u32[]{:S(2)}) %collective-permute-start.2) | collective-permute-done | bytes 81952 | tf_op jit(solution)/shard_map/ppermute | solution.py:536
  23.3 1.2 %collective-permute-start.6 = (bf16[320,128]{1,0:T(8,128)(2,1)S(1)}, bf16[320,128]{1,0:T(8,128)(2,1)S(1)}, u32[]{:S(2)}, u32[]{:S(2)}) collective-permute-start(bf16[320,128]{1,0:T(8,128)(2,1)S(1)} %collective-permute-done.2.refs_3_), channel_id=1, source_target_pairs={{0,2},{1,3},{2,0},{3,1},{4,6},{5,7},{6,4},{7,5},{8,10},{9,11},{10,... | collective-permute-start | bytes 245768 | tf_op jit(solution)/shard_map/ppermute | solution.py:536
  25.8 1.9 %collective-permute-done.6.refs_7_ = bf16[320,128]{1,0:T(8,128)(2,1)S(1)} collective-permute-done((bf16[320,128]{1,0:T(8,128)(2,1)S(1)}, bf16[320,128]{1,0:T(8,128)(2,1)S(1)}, u32[]{:S(2)}, u32[]{:S(2)}) %collective-permute-start.6) | collective-permute-done | bytes 81952 | tf_op jit(solution)/shard_map/ppermute | solution.py:536
  27.7 1.2 %collective-permute-start.10 = (bf16[416,384]{1,0:T(8,128)(2,1)S(1)}, bf16[416,384]{1,0:T(8,128)(2,1)S(1)}, u32[]{:S(2)}, u32[]{:S(2)}) collective-permute-start(bf16[416,384]{1,0:T(8,128)(2,1)S(1)} %get-tuple-element.70), channel_id=1, source_target_pairs={{0,2},{1,3},{2,0},{3,1},{4,6},{5,7},{6,4},{7,5},{8,10},{9,11},{10,... | collective-permute-start | bytes 958472 | tf_op jit(solution)/shard_map/ppermute | solution.py:536
  28.9 6.4 %attend.1 = (bf16[128,1536]{1,0:T(8,128)(2,1)}, bf16[128,1024]{1,0:T(8,128)(2,1)S(1)}, f32[4,160,128]{2,1,0:T(8,128)S(1)}, bf16[4,160,128]{2,1,0:T(8,128)(2,1)S(...) custom-call(bf16[128,1024]{1,0:T(8,128)(2,1)S(1)} %get-tuple-element.64.refs_0_, ...), custom_call_target="tpu_custom_call" | custom-call | flops 2013265920 | bytes 2949120 | tf_op jit(solution)/shard_map/attend/pallas_call | solution.py:37
  35.9 1.4 %collective-permute-start.12 = (bf16[4,160,128]{2,1,0:T(8,128)(2,1)S(1)}, bf16[4,160,128]{2,1,0:T(8,128)(2,1)S(1)}, u32[]{:S(2)}, u32[]{:S(2)}) collective-permute-start(bf16[4,160,128]{2,1,0:T(8,128)(2,1)S(1)} %get-tuple-element.71), channel_id=1, source_target_pairs={{0,2},{1,3},{2,0},{3,1},{4,6},{5,7},{6,4},{7,5},{8,10},{9,11},{10,... | collective-permute-start | bytes 491528 | tf_op jit(solution)/shard_map/ppermute | solution.py:536
  38.1 2.4 %select.1 = (bf16[512,1024]{1,0:T(8,128)(2,1)S(1)}, bf16[192,512]{1,0:T(8,128)(2,1)S(1)}) custom-call(bf16[192,128]{1,0:T(8,128)(2,1)S(1)} %get-tuple-element.66.refs_0_, bf16[288,384]{1,0:T(8,128)(2,1)S(1)} %get-tuple-element.62.refs_2_.refs_1_, bf16[352,384]{1,0:T(8,128)(2,1)S(1)} %collective-permute-done.9.refs_2_, ...), custom_call_target="tpu_custom_call" | custom-call | flops 2013265920 | bytes 2424832 | tf_op jit(solution)/shard_map/select/pallas_call | solution.py:37
  40.6 2.5 %collective-permute-done.13.refs_3_ = bf16[4,160,128]{2,1,0:T(8,128)(2,1)S(1)} collective-permute-done((bf16[4,160,128]{2,1,0:T(8,128)(2,1)S(1)}, bf16[4,160,128]{2,1,0:T(8,128)(2,1)S(1)}, u32[]{:S(2)}, u32[]{:S(2)}) %collective-permute-start.13) | collective-permute-done | bytes 163872 | tf_op jit(solution)/shard_map/ppermute | solution.py:536
  43.9 1.4 %collective-permute-start.16 = (bf16[160,128]{1,0:T(8,128)(2,1)S(1)}, bf16[160,128]{1,0:T(8,128)(2,1)S(1)}, u32[]{:S(2)}, u32[]{:S(2)}) collective-permute-start(bf16[160,128]{1,0:T(8,128)(2,1)S(1)} %get-tuple-element.81), channel_id=1, source_target_pairs={{0,2},{1,3},{2,0},{3,1},{4,6},{5,7},{6,4},{7,5},{8,10},{9,11},{10,... | collective-permute-start | bytes 122888 | tf_op jit(solution)/shard_map/ppermute | solution.py:536
  45.3 2.1 %collective-permute-start.18 = (bf16[320,128]{1,0:T(8,128)(2,1)S(1)}, bf16[320,128]{1,0:T(8,128)(2,1)S(1)}, u32[]{:S(2)}, u32[]{:S(2)}) collective-permute-start(bf16[320,128]{1,0:T(8,128)(2,1)S(1)} %get-tuple-element.83), channel_id=1, source_target_pairs={{0,8},{1,9},{2,10},{3,11},{4,12},{5,13},{6,14},{7,15},{8,0},{9,1},... | collective-permute-start | bytes 245768 | tf_op jit(solution)/shard_map/ppermute | solution.py:536
  49.2 2.0 %collective-permute-done.16.refs_1_ = bf16[160,128]{1,0:T(8,128)(2,1)S(1)} collective-permute-done((bf16[160,128]{1,0:T(8,128)(2,1)S(1)}, bf16[160,128]{1,0:T(8,128)(2,1)S(1)}, u32[]{:S(2)}, u32[]{:S(2)}) %collective-permute-start.16) | collective-permute-done | bytes 40992 | tf_op jit(solution)/shard_map/ppermute | solution.py:536
  51.2 2.9 %collective-permute-start.20 = (bf16[160,128]{1,0:T(8,128)(2,1)S(1)}, bf16[160,128]{1,0:T(8,128)(2,1)S(1)}, u32[]{:S(2)}, u32[]{:S(2)}) collective-permute-start(bf16[160,128]{1,0:T(8,128)(2,1)S(1)} %get-tuple-element.85), channel_id=1, source_target_pairs={{0,12},{1,13},{2,14},{3,15},{4,8},{5,9},{6,10},{7,11},{8,4},{9,5},... | collective-permute-start | bytes 122888 | tf_op jit(solution)/shard_map/ppermute | solution.py:536
  54.9 2.1 %collective-permute-done.20.refs_5_ = bf16[160,128]{1,0:T(8,128)(2,1)S(1)} collective-permute-done((bf16[160,128]{1,0:T(8,128)(2,1)S(1)}, bf16[160,128]{1,0:T(8,128)(2,1)S(1)}, u32[]{:S(2)}, u32[]{:S(2)}) %collective-permute-start.20) | collective-permute-done | bytes 40992 | tf_op jit(solution)/shard_map/ppermute | solution.py:536
  60.6 2.8 %collective-permute-done.26.refs_3_ = bf16[144,384]{1,0:T(8,128)(2,1)S(1)} collective-permute-done((bf16[144,384]{1,0:T(8,128)(2,1)S(1)}, bf16[144,384]{1,0:T(8,128)(2,1)S(1)}, u32[]{:S(2)}, u32[]{:S(2)}) %collective-permute-start.26) | collective-permute-done | bytes 110624 | tf_op jit(solution)/shard_map/ppermute | solution.py:536
  65.7 1.5 %collective-permute-done.24.refs_4_ = bf16[256,384]{1,0:T(8,128)(2,1)S(1)} collective-permute-done((bf16[256,384]{1,0:T(8,128)(2,1)S(1)}, bf16[256,384]{1,0:T(8,128)(2,1)S(1)}, u32[]{:S(2)}, u32[]{:S(2)}) %collective-permute-start.24) | collective-permute-done | bytes 196640 | tf_op jit(solution)/shard_map/ppermute | solution.py:536
  67.3 1.4 %collective-permute-done.28.refs_5_ = bf16[256,384]{1,0:T(8,128)(2,1)S(1)} collective-permute-done((bf16[256,384]{1,0:T(8,128)(2,1)S(1)}, bf16[256,384]{1,0:T(8,128)(2,1)S(1)}, u32[]{:S(2)}, u32[]{:S(2)}) %collective-permute-start.28) | collective-permute-done | bytes 196640 | tf_op jit(solution)/shard_map/ppermute | solution.py:536
  69.6 2.0 %collective-permute-start.29 = (bf16[1,160,384]{2,1,0:T(8,128)(2,1)S(1)}, bf16[1,160,384]{2,1,0:T(8,128)(2,1)S(1)}, u32[]{:S(2)}, u32[]{:S(2)}) collective-permute-start(bf16[1,160,384]{2,1,0:T(8,128)(2,1)S(1)} %get-tuple-element.99), channel_id=1, source_target_pairs={{0,4},{1,5},{2,6},{3,7},{4,0},{5,1},{6,2},{7,3},{8,12},{9,13},{10,... | collective-permute-start | bytes 368648 | tf_op jit(solution)/shard_map/ppermute | solution.py:536
  71.7 1.5 %collective-permute-start.30 = (bf16[1,48,1024]{2,1,0:T(8,128)(2,1)S(1)}, bf16[1,48,1024]{2,1,0:T(8,128)(2,1)S(1)}, u32[]{:S(2)}, u32[]{:S(2)}) collective-permute-start(bf16[1,48,1024]{2,1,0:T(8,128)(2,1)S(1)} %get-tuple-element.100), channel_id=1, source_target_pairs={{0,8},{1,9},{2,10},{3,11},{4,12},{5,13},{6,14},{7,15},{8,0},{9,1},... | collective-permute-start | bytes 294920 | tf_op jit(solution)/shard_map/ppermute | solution.py:536
  73.2 1.5 %collective-permute-start.32 = (bf16[1,128,384]{2,1,0:T(8,128)(2,1)S(1)}, bf16[1,128,384]{2,1,0:T(8,128)(2,1)S(1)}, u32[]{:S(2)}, u32[]{:S(2)}) collective-permute-start(bf16[1,128,384]{2,1,0:T(8,128)(2,1)S(1)} %conv_send_on.3), channel_id=1, source_target_pairs={{0,8},{1,9},{2,10},{3,11},{4,12},{5,13},{6,14},{7,15},{8,0},{9,1},... | collective-permute-start | bytes 294920 | tf_op jit(solution)/shard_map/ppermute | solution.py:536
  75.3 2.4 %collective-permute-done.29.refs_1_ = bf16[1,160,384]{2,1,0:T(8,128)(2,1)S(1)} collective-permute-done((bf16[1,160,384]{2,1,0:T(8,128)(2,1)S(1)}, bf16[1,160,384]{2,1,0:T(8,128)(2,1)S(1)}, u32[]{:S(2)}, u32[]{:S(2)}) %collective-permute-start.29) | collective-permute-done | bytes 122912 | tf_op jit(solution)/shard_map/ppermute | solution.py:536
  77.7 1.6 %collective-permute-start.34 = (bf16[1,160,384]{2,1,0:T(8,128)(2,1)S(1)}, bf16[1,160,384]{2,1,0:T(8,128)(2,1)S(1)}, u32[]{:S(2)}, u32[]{:S(2)}) collective-permute-start(bf16[1,160,384]{2,1,0:T(8,128)(2,1)S(1)} %conv_send_on.2), channel_id=1, source_target_pairs={{0,8},{1,9},{2,10},{3,11},{4,12},{5,13},{6,14},{7,15},{8,0},{9,1},... | collective-permute-start | bytes 368648 | tf_op jit(solution)/shard_map/ppermute | solution.py:536
  79.3 4.9 %collective-permute-done.32.refs_6_.refs_2_ = bf16[1,128,384]{2,1,0:T(8,128)(2,1)S(1)} collective-permute-done((bf16[1,128,384]{2,1,0:T(8,128)(2,1)S(1)}, bf16[1,128,384]{2,1,0:T(8,128)(2,1)S(1)}, u32[]{:S(2)}, u32[]{:S(2)}) %collective-permute-start.32) | collective-permute-done | bytes 98336 | tf_op jit(solution)/shard_map/ppermute | solution.py:536
  84.3 2.1 %input_grad.1 = bf16[256,384]{1,0:T(8,128)(2,1)} custom-call(bf16[256,384]{1,0:T(8,128)(2,1)S(1)} %bitcast.10, bf16[144,384]{1,0:T(8,128)(2,1)S(1)} %get-tuple-element.87.refs_1_, bf16[256,384]{1,0:T(8,128)(2,1)S(1)} %get-tuple-element.93.refs_2_, bf16[144,384]{1,0:T(8,128)(2,1)S(1)} %collective-permute-done.26.refs_3_, ...), custom_call_target="tpu_custom_call" | custom-call | flops 7549747200 | bytes 4153344 | tf_op jit(solution)/shard_map/input_grad/pallas_call | solution.py:37
  (72 shorter events, 17.2 us)
Async XLA Ops:
  1.8 6.7 %collective-permute-start.1 = (bf16[32,384]{1,0:T(8,128)(2,1)S(1)}, bf16[32,384]{1,0:T(8,128)(2,1)S(1)}, u32[]{:S(2)}, u32[]{:S(2)}) collective-permute-start(bf16[32,384]{1,0:T(8,128)(2,1)S(1)} %get-tuple-element.60), channel_id=1, source_target_pairs={{2,4},{6,8},{10,12},{4,2},{8,6},{12,10},{3,5},{7,9},{11,13},{5,3},... | collective-permute-start | bytes 73736 | tf_op jit(solution)/shard_map/ppermute | solution.py:567
  2.6 7.7 %collective-permute-start = (bf16[32,384]{1,0:T(8,128)(2,1)S(1)}, bf16[32,384]{1,0:T(8,128)(2,1)S(1)}, u32[]{:S(2)}, u32[]{:S(2)}) collective-permute-start(bf16[32,384]{1,0:T(8,128)(2,1)S(1)} %get-tuple-element.60), channel_id=1, source_target_pairs={{0,2},{1,3},{2,0},{3,1},{4,6},{5,7},{6,4},{7,5},{8,10},{9,11},{10,... | collective-permute-start | bytes 73736 | tf_op jit(solution)/shard_map/ppermute | solution.py:536
  12.2 6.1 %collective-permute-start.4 = (bf16[320,128]{1,0:T(8,128)(2,1)S(1)}, bf16[320,128]{1,0:T(8,128)(2,1)S(1)}, u32[]{:S(2)}, u32[]{:S(2)}) collective-permute-start(bf16[320,128]{1,0:T(8,128)(2,1)S(1)} %get-tuple-element.63.refs_2_), channel_id=1, source_target_pairs={{0,4},{1,5},{2,6},{3,7},{4,0},{5,1},{6,2},{7,3},{8,12},{9,13},{10,... | collective-permute-start | bytes 245768 | tf_op jit(solution)/shard_map/ppermute | solution.py:536
  14.2 6.6 %collective-permute-start.3 = (bf16[320,128]{1,0:T(8,128)(2,1)S(1)}, bf16[320,128]{1,0:T(8,128)(2,1)S(1)}, u32[]{:S(2)}, u32[]{:S(2)}) collective-permute-start(bf16[320,128]{1,0:T(8,128)(2,1)S(1)} %get-tuple-element.63.refs_2_), channel_id=1, source_target_pairs={{0,12},{1,13},{2,14},{3,15},{4,8},{5,9},{6,10},{7,11},{8,4},{9,5},... | collective-permute-start | bytes 245768 | tf_op jit(solution)/shard_map/ppermute | solution.py:536
  16.7 6.6 %collective-permute-start.2 = (bf16[320,128]{1,0:T(8,128)(2,1)S(1)}, bf16[320,128]{1,0:T(8,128)(2,1)S(1)}, u32[]{:S(2)}, u32[]{:S(2)}) collective-permute-start(bf16[320,128]{1,0:T(8,128)(2,1)S(1)} %get-tuple-element.63.refs_2_), channel_id=1, source_target_pairs={{0,8},{1,9},{2,10},{3,11},{4,12},{5,13},{6,14},{7,15},{8,0},{9,1},... | collective-permute-start | bytes 245768 | tf_op jit(solution)/shard_map/ppermute | solution.py:536
  16.8 8.4 %collective-permute-start.5 = (bf16[320,128]{1,0:T(8,128)(2,1)S(1)}, bf16[320,128]{1,0:T(8,128)(2,1)S(1)}, u32[]{:S(2)}, u32[]{:S(2)}) collective-permute-start(bf16[320,128]{1,0:T(8,128)(2,1)S(1)} %get-tuple-element.63.refs_2_), channel_id=1, source_target_pairs={{0,2},{1,3},{2,0},{3,1},{4,6},{5,7},{6,4},{7,5},{8,10},{9,11},{10,... | collective-permute-start | bytes 245768 | tf_op jit(solution)/shard_map/ppermute | solution.py:536
  18.3 6.9 %collective-permute-start.8 = (bf16[320,128]{1,0:T(8,128)(2,1)S(1)}, bf16[320,128]{1,0:T(8,128)(2,1)S(1)}, u32[]{:S(2)}, u32[]{:S(2)}) collective-permute-start(bf16[320,128]{1,0:T(8,128)(2,1)S(1)} %collective-permute-done.4.refs_5_), channel_id=1, source_target_pairs={{0,2},{1,3},{2,0},{3,1},{4,6},{5,7},{6,4},{7,5},{8,10},{9,11},{10,... | collective-permute-start | bytes 245768 | tf_op jit(solution)/shard_map/ppermute | solution.py:536
  20.8 5.1 %collective-permute-start.7 = (bf16[320,128]{1,0:T(8,128)(2,1)S(1)}, bf16[320,128]{1,0:T(8,128)(2,1)S(1)}, u32[]{:S(2)}, u32[]{:S(2)}) collective-permute-start(bf16[320,128]{1,0:T(8,128)(2,1)S(1)} %collective-permute-done.3.refs_4_), channel_id=1, source_target_pairs={{0,2},{1,3},{2,0},{3,1},{4,6},{5,7},{6,4},{7,5},{8,10},{9,11},{10,... | collective-permute-start | bytes 245768 | tf_op jit(solution)/shard_map/ppermute | solution.py:536
  23.3 4.4 %collective-permute-start.6 = (bf16[320,128]{1,0:T(8,128)(2,1)S(1)}, bf16[320,128]{1,0:T(8,128)(2,1)S(1)}, u32[]{:S(2)}, u32[]{:S(2)}) collective-permute-start(bf16[320,128]{1,0:T(8,128)(2,1)S(1)} %collective-permute-done.2.refs_3_), channel_id=1, source_target_pairs={{0,2},{1,3},{2,0},{3,1},{4,6},{5,7},{6,4},{7,5},{8,10},{9,11},{10,... | collective-permute-start | bytes 245768 | tf_op jit(solution)/shard_map/ppermute | solution.py:536
  27.7 7.7 %collective-permute-start.10 = (bf16[416,384]{1,0:T(8,128)(2,1)S(1)}, bf16[416,384]{1,0:T(8,128)(2,1)S(1)}, u32[]{:S(2)}, u32[]{:S(2)}) collective-permute-start(bf16[416,384]{1,0:T(8,128)(2,1)S(1)} %get-tuple-element.70), channel_id=1, source_target_pairs={{0,2},{1,3},{2,0},{3,1},{4,6},{5,7},{6,4},{7,5},{8,10},{9,11},{10,... | collective-permute-start | bytes 958472 | tf_op jit(solution)/shard_map/ppermute | solution.py:536
  35.4 2.8 %collective-permute-start.11 = (bf16[416,384]{1,0:T(8,128)(2,1)S(1)}, bf16[416,384]{1,0:T(8,128)(2,1)S(1)}, u32[]{:S(2)}, u32[]{:S(2)}) collective-permute-start(bf16[416,384]{1,0:T(8,128)(2,1)S(1)} %collective-permute-done.10.refs_3_), channel_id=1, source_target_pairs={{0,1},{1,0},{2,3},{3,2},{4,5},{5,4},{6,7},{7,6},{8,9},{9,8},{10,11... | collective-permute-start | bytes 958472 | tf_op jit(solution)/shard_map/ppermute | solution.py:536
  35.4 2.7 %collective-permute-start.9 = (bf16[352,384]{1,0:T(8,128)(2,1)S(1)}, bf16[352,384]{1,0:T(8,128)(2,1)S(1)}, u32[]{:S(2)}, u32[]{:S(2)}) collective-permute-start(bf16[352,384]{1,0:T(8,128)(2,1)S(1)} %get-tuple-element.68), channel_id=1, source_target_pairs={{0,1},{1,0},{2,3},{3,2},{4,5},{5,4},{6,7},{7,6},{8,9},{9,8},{10,11... | collective-permute-start | bytes 811016 | tf_op jit(solution)/shard_map/ppermute | solution.py:536
  35.9 7.2 %collective-permute-start.12 = (bf16[4,160,128]{2,1,0:T(8,128)(2,1)S(1)}, bf16[4,160,128]{2,1,0:T(8,128)(2,1)S(1)}, u32[]{:S(2)}, u32[]{:S(2)}) collective-permute-start(bf16[4,160,128]{2,1,0:T(8,128)(2,1)S(1)} %get-tuple-element.71), channel_id=1, source_target_pairs={{0,2},{1,3},{2,0},{3,1},{4,6},{5,7},{6,4},{7,5},{8,10},{9,11},{10,... | collective-permute-start | bytes 491528 | tf_op jit(solution)/shard_map/ppermute | solution.py:536
  37.3 5.8 %collective-permute-start.13 = (bf16[4,160,128]{2,1,0:T(8,128)(2,1)S(1)}, bf16[4,160,128]{2,1,0:T(8,128)(2,1)S(1)}, u32[]{:S(2)}, u32[]{:S(2)}) collective-permute-start(bf16[4,160,128]{2,1,0:T(8,128)(2,1)S(1)} %get-tuple-element.78), channel_id=1, source_target_pairs={{0,4},{1,5},{2,6},{3,7},{4,0},{5,1},{6,2},{7,3},{8,12},{9,13},{10,... | collective-permute-start | bytes 491528 | tf_op jit(solution)/shard_map/ppermute | solution.py:536
  43.2 14.2 %collective-permute-start.15 = (bf16[128,1024]{1,0:T(8,128)(2,1)S(1)}, bf16[128,1024]{1,0:T(8,128)(2,1)S(1)}, u32[]{:S(2)}, u32[]{:S(2)}) collective-permute-start(bf16[128,1024]{1,0:T(8,128)(2,1)S(1)} %get-tuple-element.80.refs_0_.refs_1_), channel_id=1, source_target_pairs={{0,2},{1,3},{2,0},{3,1},{4,6},{5,7},{6,4},{7,5},{8,10},{9,11},{10,... | collective-permute-start | bytes 786440 | tf_op jit(solution)/shard_map/ppermute | solution.py:536
  43.9 7.3 %collective-permute-start.16 = (bf16[160,128]{1,0:T(8,128)(2,1)S(1)}, bf16[160,128]{1,0:T(8,128)(2,1)S(1)}, u32[]{:S(2)}, u32[]{:S(2)}) collective-permute-start(bf16[160,128]{1,0:T(8,128)(2,1)S(1)} %get-tuple-element.81), channel_id=1, source_target_pairs={{0,2},{1,3},{2,0},{3,1},{4,6},{5,7},{6,4},{7,5},{8,10},{9,11},{10,... | collective-permute-start | bytes 122888 | tf_op jit(solution)/shard_map/ppermute | solution.py:536
  45.3 11.7 %collective-permute-start.18 = (bf16[320,128]{1,0:T(8,128)(2,1)S(1)}, bf16[320,128]{1,0:T(8,128)(2,1)S(1)}, u32[]{:S(2)}, u32[]{:S(2)}) collective-permute-start(bf16[320,128]{1,0:T(8,128)(2,1)S(1)} %get-tuple-element.83), channel_id=1, source_target_pairs={{0,8},{1,9},{2,10},{3,11},{4,12},{5,13},{6,14},{7,15},{8,0},{9,1},... | collective-permute-start | bytes 245768 | tf_op jit(solution)/shard_map/ppermute | solution.py:536
  47.4 7.3 %collective-permute-start.17 = (bf16[160,128]{1,0:T(8,128)(2,1)S(1)}, bf16[160,128]{1,0:T(8,128)(2,1)S(1)}, u32[]{:S(2)}, u32[]{:S(2)}) collective-permute-start(bf16[160,128]{1,0:T(8,128)(2,1)S(1)} %get-tuple-element.82), channel_id=1, source_target_pairs={{0,4},{1,5},{2,6},{3,7},{4,0},{5,1},{6,2},{7,3},{8,12},{9,13},{10,... | collective-permute-start | bytes 122888 | tf_op jit(solution)/shard_map/ppermute | solution.py:536
  48.3 6.6 %collective-permute-start.19 = (bf16[160,128]{1,0:T(8,128)(2,1)S(1)}, bf16[160,128]{1,0:T(8,128)(2,1)S(1)}, u32[]{:S(2)}, u32[]{:S(2)}) collective-permute-start(bf16[160,128]{1,0:T(8,128)(2,1)S(1)} %get-tuple-element.84), channel_id=1, source_target_pairs={{0,10},{1,11},{2,8},{3,9},{4,14},{5,15},{6,12},{7,13},{8,2},{9,3},... | collective-permute-start | bytes 122888 | tf_op jit(solution)/shard_map/ppermute | solution.py:536
  51.2 5.8 %collective-permute-start.20 = (bf16[160,128]{1,0:T(8,128)(2,1)S(1)}, bf16[160,128]{1,0:T(8,128)(2,1)S(1)}, u32[]{:S(2)}, u32[]{:S(2)}) collective-permute-start(bf16[160,128]{1,0:T(8,128)(2,1)S(1)} %get-tuple-element.85), channel_id=1, source_target_pairs={{0,12},{1,13},{2,14},{3,15},{4,8},{5,9},{6,10},{7,11},{8,4},{9,5},... | collective-permute-start | bytes 122888 | tf_op jit(solution)/shard_map/ppermute | solution.py:536
  54.7 4.9 %collective-permute-start.14 = (bf16[128,1024]{1,0:T(8,128)(2,1)S(1)}, bf16[128,1024]{1,0:T(8,128)(2,1)S(1)}, u32[]{:S(2)}, u32[]{:S(2)}) collective-permute-start(bf16[128,1024]{1,0:T(8,128)(2,1)S(1)} %get-tuple-element.80.refs_0_.refs_1_), channel_id=1, source_target_pairs={{0,1},{1,0},{2,3},{3,2},{4,5},{5,4},{6,7},{7,6},{8,9},{9,8},{10,11... | collective-permute-start | bytes 786440 | tf_op jit(solution)/shard_map/ppermute | solution.py:536
  57.5 5.9 %collective-permute-start.26 = (bf16[144,384]{1,0:T(8,128)(2,1)S(1)}, bf16[144,384]{1,0:T(8,128)(2,1)S(1)}, u32[]{:S(2)}, u32[]{:S(2)}) collective-permute-start(bf16[144,384]{1,0:T(8,128)(2,1)S(1)} %get-tuple-element.87.refs_1_), channel_id=1, source_target_pairs={{0,2},{1,3},{2,0},{3,1},{4,6},{5,7},{6,4},{7,5},{8,10},{9,11},{10,... | collective-permute-start | bytes 331784 | tf_op jit(solution)/shard_map/ppermute | solution.py:536
  58.6 8.6 %collective-permute-start.24 = (bf16[256,384]{1,0:T(8,128)(2,1)S(1)}, bf16[256,384]{1,0:T(8,128)(2,1)S(1)}, u32[]{:S(2)}, u32[]{:S(2)}) collective-permute-start(bf16[256,384]{1,0:T(8,128)(2,1)S(1)} %get-tuple-element.93.refs_2_), channel_id=1, source_target_pairs={{0,2},{1,3},{2,0},{3,1},{4,6},{5,7},{6,4},{7,5},{8,10},{9,11},{10,... | collective-permute-start | bytes 589832 | tf_op jit(solution)/shard_map/ppermute | solution.py:536
  60.4 6.8 %collective-permute-start.22 = (bf16[2,48,1024]{2,1,0:T(8,128)(2,1)S(1)}, bf16[2,48,1024]{2,1,0:T(8,128)(2,1)S(1)}, u32[]{:S(2)}, u32[]{:S(2)}) collective-permute-start(bf16[2,48,1024]{2,1,0:T(8,128)(2,1)S(1)} %get-tuple-element.90), channel_id=1, source_target_pairs={{0,4},{1,5},{2,6},{3,7},{4,0},{5,1},{6,2},{7,3},{8,12},{9,13},{10,... | collective-permute-start | bytes 589832 | tf_op jit(solution)/shard_map/ppermute | solution.py:536
  60.5 3.4 %collective-permute-start.25 = (bf16[144,384]{1,0:T(8,128)(2,1)S(1)}, bf16[144,384]{1,0:T(8,128)(2,1)S(1)}, u32[]{:S(2)}, u32[]{:S(2)}) collective-permute-start(bf16[144,384]{1,0:T(8,128)(2,1)S(1)} %get-tuple-element.87.refs_1_), channel_id=1, source_target_pairs={{0,1},{1,0},{2,3},{3,2},{4,5},{5,4},{6,7},{7,6},{8,9},{9,8},{10,11... | collective-permute-start | bytes 331784 | tf_op jit(solution)/shard_map/ppermute | solution.py:536
  63.4 3.8 %collective-permute-start.23 = (bf16[256,384]{1,0:T(8,128)(2,1)S(1)}, bf16[256,384]{1,0:T(8,128)(2,1)S(1)}, u32[]{:S(2)}, u32[]{:S(2)}) collective-permute-start(bf16[256,384]{1,0:T(8,128)(2,1)S(1)} %get-tuple-element.93.refs_2_), channel_id=1, source_target_pairs={{0,1},{1,0},{2,3},{3,2},{4,5},{5,4},{6,7},{7,6},{8,9},{9,8},{10,11... | collective-permute-start | bytes 589832 | tf_op jit(solution)/shard_map/ppermute | solution.py:536
  67.2 6.0 %collective-permute-start.31 = (bf16[1,128,384]{2,1,0:T(8,128)(2,1)S(1)}, bf16[1,128,384]{2,1,0:T(8,128)(2,1)S(1)}, u32[]{:S(2)}, u32[]{:S(2)}) collective-permute-start(bf16[1,128,384]{2,1,0:T(8,128)(2,1)S(1)} %get-tuple-element.102), channel_id=1, source_target_pairs={{0,4},{1,5},{2,6},{3,7},{4,0},{5,1},{6,2},{7,3},{8,12},{9,13},{10,... | collective-permute-start | bytes 294920 | tf_op jit(solution)/shard_map/ppermute | solution.py:536
  69.6 8.0 %collective-permute-start.29 = (bf16[1,160,384]{2,1,0:T(8,128)(2,1)S(1)}, bf16[1,160,384]{2,1,0:T(8,128)(2,1)S(1)}, u32[]{:S(2)}, u32[]{:S(2)}) collective-permute-start(bf16[1,160,384]{2,1,0:T(8,128)(2,1)S(1)} %get-tuple-element.99), channel_id=1, source_target_pairs={{0,4},{1,5},{2,6},{3,7},{4,0},{5,1},{6,2},{7,3},{8,12},{9,13},{10,... | collective-permute-start | bytes 368648 | tf_op jit(solution)/shard_map/ppermute | solution.py:536
  71.7 7.7 %collective-permute-start.30 = (bf16[1,48,1024]{2,1,0:T(8,128)(2,1)S(1)}, bf16[1,48,1024]{2,1,0:T(8,128)(2,1)S(1)}, u32[]{:S(2)}, u32[]{:S(2)}) collective-permute-start(bf16[1,48,1024]{2,1,0:T(8,128)(2,1)S(1)} %get-tuple-element.100), channel_id=1, source_target_pairs={{0,8},{1,9},{2,10},{3,11},{4,12},{5,13},{6,14},{7,15},{8,0},{9,1},... | collective-permute-start | bytes 294920 | tf_op jit(solution)/shard_map/ppermute | solution.py:536
  73.2 11.1 %collective-permute-start.32 = (bf16[1,128,384]{2,1,0:T(8,128)(2,1)S(1)}, bf16[1,128,384]{2,1,0:T(8,128)(2,1)S(1)}, u32[]{:S(2)}, u32[]{:S(2)}) collective-permute-start(bf16[1,128,384]{2,1,0:T(8,128)(2,1)S(1)} %conv_send_on.3), channel_id=1, source_target_pairs={{0,8},{1,9},{2,10},{3,11},{4,12},{5,13},{6,14},{7,15},{8,0},{9,1},... | collective-permute-start | bytes 294920 | tf_op jit(solution)/shard_map/ppermute | solution.py:536
  74.7 12.2 %collective-permute-start.33 = (bf16[1,288,384]{2,1,0:T(8,128)(2,1)S(1)}, bf16[1,288,384]{2,1,0:T(8,128)(2,1)S(1)}, u32[]{:S(2)}, u32[]{:S(2)}) collective-permute-start(bf16[1,288,384]{2,1,0:T(8,128)(2,1)S(1)} %get-tuple-element.104), channel_id=1, source_target_pairs={{0,4},{1,5},{2,6},{3,7},{4,0},{5,1},{6,2},{7,3},{8,12},{9,13},{10,... | collective-permute-start | bytes 663560 | tf_op jit(solution)/shard_map/ppermute | solution.py:536
  77.7 9.2 %collective-permute-start.34 = (bf16[1,160,384]{2,1,0:T(8,128)(2,1)S(1)}, bf16[1,160,384]{2,1,0:T(8,128)(2,1)S(1)}, u32[]{:S(2)}, u32[]{:S(2)}) collective-permute-start(bf16[1,160,384]{2,1,0:T(8,128)(2,1)S(1)} %conv_send_on.2), channel_id=1, source_target_pairs={{0,8},{1,9},{2,10},{3,11},{4,12},{5,13},{6,14},{7,15},{8,0},{9,1},... | collective-permute-start | bytes 368648 | tf_op jit(solution)/shard_map/ppermute | solution.py:536
  (11 other events, 97.4 us)

commit v14 on v11

--- a/solution.py
+++ b/solution.py
@@ -174,7 +174,10 @@
         vs[at + half : at + tokens, key_size:] = part[2 * tokens :, wide:]
         kt[:, at : at + tokens] = ks[at : at + tokens].astype(F32).T.astype(BF)
         vt[:, at : at + tokens] = vs[at : at + tokens].astype(F32).T.astype(BF)
-    for pair in range(heads // 2):
+    slots = scores.shape[0]
+    parts_of = [slice(i * tokens, (i + 1) * tokens) for i in range(blocks)]
+
+    def products(pair):
         ql, cl = 2 * pair * key_size, 2 * pair * value_size
         rows = slice(2 * pair * tokens, 2 * (pair + 1) * tokens)
         both = cot[:, cl : cl + 2 * value_size]
@@ -182,10 +185,16 @@
             [q[:, ql : ql + key_size], q[:, ql + key_size : ql + 2 * key_size]], axis=0
         )
         cs[rows] = jnp.concatenate([both[:, :value_size], both[:, value_size:]], axis=0)
-        slot = pair % scores.shape[0]
-        parts_of = [slice(i * tokens, (i + 1) * tokens) for i in range(blocks)]
-        scores[slot] = dot_t(ks[...], qs[rows])
-        prob_cots[slot] = dot_t(vs[...], cs[rows])
+        scores[pair % slots] = dot_t(ks[...], qs[rows])
+        prob_cots[pair % slots] = dot_t(vs[...], cs[rows])
+
+    products(0)
+    for pair in range(heads // 2):
+        ql, cl = 2 * pair * key_size, 2 * pair * value_size
+        rows = slice(2 * pair * tokens, 2 * (pair + 1) * tokens)
+        slot = pair % slots
+        if slots > 1 and pair + 1 < heads // 2:
+            products(pair + 1)
         top = functools.reduce(jnp.maximum, [by_eight(scores[slot, at]).max(0) for at in parts_of])
         top = jnp.max(top, axis=0, keepdims=True)
         sums = 0.0
@@ -201,6 +210,8 @@
         for at in parts_of:
             probs = scores[slot, at] * inverse
             score_cots[at, rows] = (probs * (prob_cots[slot, at] - delta)).astype(BF)
+        if slots == 1 and pair + 1 < heads // 2:
+            products(pair + 1)
         dq_t = dot(kt[...], score_cots[:, rows]) * scale
         out_rows = jnp.concatenate([out_t[:, :tokens].T, out_t[:, tokens:].T], axis=1)
         att[:, cl : cl + 2 * value_size] = out_rows.astype(BF)

time: 86.3 us -> 86.4 us (level)
  waiting for transfers between devices: 28.7 us -> 31.5 us
  starting transfers between devices: 37.2 us -> 35.2 us
    ppermute x32, waiting for transfers between devices: 28.7 us -> 31.5 us  [swap(): lax.ppermute(value, both_axes, [(i, i ^ mask) for i in range(owners)])]
    ppermute x32, starting transfers between devices: 36.4 us -> 34.4 us  [swap(): lax.ppermute(value, both_axes, [(i, i ^ mask) for i in range(owners)])]
  transfers between devices with their start and end apart: 33 -> 33, of which waited for: 18 -> 18; matrix products, arithmetic and copies ran while one was open for 0% -> 0% of each run, Pallas kernels for 18% -> 17%
where the time goes in v14:
time: 86.4 us; the launch traced here: 86.2 us
  starting transfers between devices  35.2 us (41%)
  waiting for transfers between devices  31.5 us (36%)
  Pallas kernels  17.8 us (21%)
  local copies, waits for them, and re-layouts  0.96 us (1%)
    ppermute x32, starting transfers between devices, swap(): lax.ppermute(value, both_axes, [(i, i ^ mask) for i in range(owners)])  34.4 us
    ppermute x32, waiting for transfers between devices, swap(): lax.ppermute(value, both_axes, [(i, i ^ mask) for i in range(owners)])  31.5 us
    pallas_call x18, Pallas kernels, run(): pl.pallas_call(whole, out_shape=[jax.ShapeDtypeStruct(s, t) for s, t in o...  17.8 us
  transfers between devices with their start and end apart: 33, of which 18 were waited for; matrix products, arithmetic and copies ran while one was open for 0% of the time, Pallas kernels for 17%

profile of v14, /device:TPU:0, one launch (start us, length us, event | category | flops | bytes accessed | tf_op | source)
XLA Modules:
  0.0 86.2 jit_solution(5511029570623638841)
XLA Ops:
  2.6 5.9 %collective-permute-start = (bf16[32,384]{1,0:T(8,128)(2,1)S(1)}, bf16[32,384]{1,0:T(8,128)(2,1)S(1)}, u32[]{:S(2)}, u32[]{:S(2)}) collective-permute-start(bf16[32,384]{1,0:T(8,128)(2,1)S(1)} %get-tuple-element.59), channel_id=1, source_target_pairs={{0,2},{1,3},{2,0},{3,1},{4,6},{5,7},{6,4},{7,5},{8,10},{9,11},{10,... | collective-permute-start | bytes 73736 | tf_op jit(solution)/shard_map/ppermute | solution.py:534
  8.5 1.8 %collective-permute-done.refs_1_ = bf16[32,384]{1,0:T(8,128)(2,1)S(1)} collective-permute-done((bf16[32,384]{1,0:T(8,128)(2,1)S(1)}, bf16[32,384]{1,0:T(8,128)(2,1)S(1)}, u32[]{:S(2)}, u32[]{:S(2)}) %collective-permute-start) | collective-permute-done | bytes 24608 | tf_op jit(solution)/shard_map/ppermute | solution.py:534
  10.3 1.9 %front.1 = (bf16[320,128]{1,0:T(8,128)(2,1)S(1)}, bf16[288,384]{1,0:T(8,128)(2,1)S(1)}, bf16[128,768]{1,0:T(8,128)(2,1)S(1)}, f32[128,768]{1,0:T(8,128)S(1)}) custom-call(f32[3,304,128]{2,1,0:T(8,128)S(1)} %get-tuple-element.58.refs_0_, bf16[32,384]{1,0:T(8,128)(2,1)S(1)} %collective-permute-done.refs_1_, ...), custom_call_target="tpu_custom_call" | custom-call | flops 754974720 | bytes 4852736 | tf_op jit(solution)/shard_map/front/pallas_call | solution.py:37
  12.2 2.0 %collective-permute-start.4 = (bf16[320,128]{1,0:T(8,128)(2,1)S(1)}, bf16[320,128]{1,0:T(8,128)(2,1)S(1)}, u32[]{:S(2)}, u32[]{:S(2)}) collective-permute-start(bf16[320,128]{1,0:T(8,128)(2,1)S(1)} %get-tuple-element.62.refs_2_), channel_id=1, source_target_pairs={{0,4},{1,5},{2,6},{3,7},{4,0},{5,1},{6,2},{7,3},{8,12},{9,13},{10,... | collective-permute-start | bytes 245768 | tf_op jit(solution)/shard_map/ppermute | solution.py:534
  14.2 2.5 %collective-permute-start.3 = (bf16[320,128]{1,0:T(8,128)(2,1)S(1)}, bf16[320,128]{1,0:T(8,128)(2,1)S(1)}, u32[]{:S(2)}, u32[]{:S(2)}) collective-permute-start(bf16[320,128]{1,0:T(8,128)(2,1)S(1)} %get-tuple-element.62.refs_2_), channel_id=1, source_target_pairs={{0,12},{1,13},{2,14},{3,15},{4,8},{5,9},{6,10},{7,11},{8,4},{9,5},... | collective-permute-start | bytes 245768 | tf_op jit(solution)/shard_map/ppermute | solution.py:534
  16.8 1.5 %collective-permute-start.5 = (bf16[320,128]{1,0:T(8,128)(2,1)S(1)}, bf16[320,128]{1,0:T(8,128)(2,1)S(1)}, u32[]{:S(2)}, u32[]{:S(2)}) collective-permute-start(bf16[320,128]{1,0:T(8,128)(2,1)S(1)} %get-tuple-element.62.refs_2_), channel_id=1, source_target_pairs={{0,2},{1,3},{2,0},{3,1},{4,6},{5,7},{6,4},{7,5},{8,10},{9,11},{10,... | collective-permute-start | bytes 245768 | tf_op jit(solution)/shard_map/ppermute | solution.py:534
  18.3 1.3 %collective-permute-start.8 = (bf16[320,128]{1,0:T(8,128)(2,1)S(1)}, bf16[320,128]{1,0:T(8,128)(2,1)S(1)}, u32[]{:S(2)}, u32[]{:S(2)}) collective-permute-start(bf16[320,128]{1,0:T(8,128)(2,1)S(1)} %collective-permute-done.4.refs_5_), channel_id=1, source_target_pairs={{0,2},{1,3},{2,0},{3,1},{4,6},{5,7},{6,4},{7,5},{8,10},{9,11},{10,... | collective-permute-start | bytes 245768 | tf_op jit(solution)/shard_map/ppermute | solution.py:534
  19.6 1.2 %collective-permute-done.3.refs_4_ = bf16[320,128]{1,0:T(8,128)(2,1)S(1)} collective-permute-done((bf16[320,128]{1,0:T(8,128)(2,1)S(1)}, bf16[320,128]{1,0:T(8,128)(2,1)S(1)}, u32[]{:S(2)}, u32[]{:S(2)}) %collective-permute-start.3) | collective-permute-done | bytes 81952 | tf_op jit(solution)/shard_map/ppermute | solution.py:534
  20.8 1.4 %collective-permute-start.7 = (bf16[320,128]{1,0:T(8,128)(2,1)S(1)}, bf16[320,128]{1,0:T(8,128)(2,1)S(1)}, u32[]{:S(2)}, u32[]{:S(2)}) collective-permute-start(bf16[320,128]{1,0:T(8,128)(2,1)S(1)} %collective-permute-done.3.refs_4_), channel_id=1, source_target_pairs={{0,2},{1,3},{2,0},{3,1},{4,6},{5,7},{6,4},{7,5},{8,10},{9,11},{10,... | collective-permute-start | bytes 245768 | tf_op jit(solution)/shard_map/ppermute | solution.py:534
  23.3 1.2 %collective-permute-start.6 = (bf16[320,128]{1,0:T(8,128)(2,1)S(1)}, bf16[320,128]{1,0:T(8,128)(2,1)S(1)}, u32[]{:S(2)}, u32[]{:S(2)}) collective-permute-start(bf16[320,128]{1,0:T(8,128)(2,1)S(1)} %collective-permute-done.2.refs_3_), channel_id=1, source_target_pairs={{0,2},{1,3},{2,0},{3,1},{4,6},{5,7},{6,4},{7,5},{8,10},{9,11},{10,... | collective-permute-start | bytes 245768 | tf_op jit(solution)/shard_map/ppermute | solution.py:534
  25.8 1.9 %collective-permute-done.6.refs_7_ = bf16[320,128]{1,0:T(8,128)(2,1)S(1)} collective-permute-done((bf16[320,128]{1,0:T(8,128)(2,1)S(1)}, bf16[320,128]{1,0:T(8,128)(2,1)S(1)}, u32[]{:S(2)}, u32[]{:S(2)}) %collective-permute-start.6) | collective-permute-done | bytes 81952 | tf_op jit(solution)/shard_map/ppermute | solution.py:534
  27.7 1.2 %collective-permute-start.10 = (bf16[416,384]{1,0:T(8,128)(2,1)S(1)}, bf16[416,384]{1,0:T(8,128)(2,1)S(1)}, u32[]{:S(2)}, u32[]{:S(2)}) collective-permute-start(bf16[416,384]{1,0:T(8,128)(2,1)S(1)} %get-tuple-element.69), channel_id=1, source_target_pairs={{0,2},{1,3},{2,0},{3,1},{4,6},{5,7},{6,4},{7,5},{8,10},{9,11},{10,... | collective-permute-start | bytes 958472 | tf_op jit(solution)/shard_map/ppermute | solution.py:534
  28.9 5.7 %attend.1 = (bf16[128,1536]{1,0:T(8,128)(2,1)}, bf16[128,1024]{1,0:T(8,128)(2,1)S(1)}, f32[4,160,128]{2,1,0:T(8,128)S(1)}, bf16[4,160,128]{2,1,0:T(8,128)(2,1)S(...) custom-call(bf16[128,1024]{1,0:T(8,128)(2,1)S(1)} %get-tuple-element.63.refs_0_, ...), custom_call_target="tpu_custom_call" | custom-call | flops 2013265920 | bytes 2949120 | tf_op jit(solution)/shard_map/attend/pallas_call | solution.py:37
  35.9 1.4 %collective-permute-start.12 = (bf16[4,160,128]{2,1,0:T(8,128)(2,1)S(1)}, bf16[4,160,128]{2,1,0:T(8,128)(2,1)S(1)}, u32[]{:S(2)}, u32[]{:S(2)}) collective-permute-start(bf16[4,160,128]{2,1,0:T(8,128)(2,1)S(1)} %get-tuple-element.70), channel_id=1, source_target_pairs={{0,2},{1,3},{2,0},{3,1},{4,6},{5,7},{6,4},{7,5},{8,10},{9,11},{10,... | collective-permute-start | bytes 491528 | tf_op jit(solution)/shard_map/ppermute | solution.py:534
  37.4 2.4 %select.1 = (bf16[512,1024]{1,0:T(8,128)(2,1)S(1)}, bf16[192,512]{1,0:T(8,128)(2,1)S(1)}) custom-call(bf16[192,128]{1,0:T(8,128)(2,1)S(1)} %get-tuple-element.65.refs_0_, bf16[288,384]{1,0:T(8,128)(2,1)S(1)} %get-tuple-element.61.refs_2_.refs_1_, bf16[352,384]{1,0:T(8,128)(2,1)S(1)} %collective-permute-done.9.refs_2_, ...), custom_call_target="tpu_custom_call" | custom-call | flops 2013265920 | bytes 2424832 | tf_op jit(solution)/shard_map/select/pallas_call | solution.py:37
  39.9 3.2 %collective-permute-done.13.refs_3_ = bf16[4,160,128]{2,1,0:T(8,128)(2,1)S(1)} collective-permute-done((bf16[4,160,128]{2,1,0:T(8,128)(2,1)S(1)}, bf16[4,160,128]{2,1,0:T(8,128)(2,1)S(1)}, u32[]{:S(2)}, u32[]{:S(2)}) %collective-permute-start.13) | collective-permute-done | bytes 163872 | tf_op jit(solution)/shard_map/ppermute | solution.py:534
  44.7 3.0 %collective-permute-done.14.refs_1_ = bf16[2,160,128]{2,1,0:T(8,128)(2,1)S(1)} collective-permute-done((bf16[2,160,128]{2,1,0:T(8,128)(2,1)S(1)}, bf16[2,160,128]{2,1,0:T(8,128)(2,1)S(1)}, u32[]{:S(2)}, u32[]{:S(2)}) %collective-permute-start.14) | collective-permute-done | bytes 81952 | tf_op jit(solution)/shard_map/ppermute | solution.py:534
  48.0 1.2 %collective-permute-start.22 = (bf16[128,1024]{1,0:T(8,128)(2,1)S(1)}, bf16[128,1024]{1,0:T(8,128)(2,1)S(1)}, u32[]{:S(2)}, u32[]{:S(2)}) collective-permute-start(bf16[128,1024]{1,0:T(8,128)(2,1)S(1)} %get-tuple-element.87.refs_0_.refs_1_), channel_id=1, source_target_pairs={{0,2},{1,3},{2,0},{3,1},{4,6},{5,7},{6,4},{7,5},{8,10},{9,11},{10,... | collective-permute-start | bytes 786440 | tf_op jit(solution)/shard_map/ppermute | solution.py:534
  49.2 2.1 %collective-permute-start.16 = (bf16[1,320,128]{2,1,0:T(8,128)(2,1)S(1)}, bf16[1,320,128]{2,1,0:T(8,128)(2,1)S(1)}, u32[]{:S(2)}, u32[]{:S(2)}) collective-permute-start(bf16[1,320,128]{2,1,0:T(8,128)(2,1)S(1)} %get-tuple-element.82), channel_id=1, source_target_pairs={{0,8},{1,9},{2,10},{3,11},{4,12},{5,13},{6,14},{7,15},{8,0},{9,1},... | collective-permute-start | bytes 245768 | tf_op jit(solution)/shard_map/ppermute | solution.py:534
  52.1 3.4 %collective-permute-done.16.refs_1_ = bf16[1,320,128]{2,1,0:T(8,128)(2,1)S(1)} collective-permute-done((bf16[1,320,128]{2,1,0:T(8,128)(2,1)S(1)}, bf16[1,320,128]{2,1,0:T(8,128)(2,1)S(1)}, u32[]{:S(2)}, u32[]{:S(2)}) %collective-permute-start.16) | collective-permute-done | bytes 81952 | tf_op jit(solution)/shard_map/ppermute | solution.py:534
  56.0 1.4 %collective-permute-done.23.refs_4_ = bf16[128,1024]{1,0:T(8,128)(2,1)S(1)} collective-permute-done((bf16[128,1024]{1,0:T(8,128)(2,1)S(1)}, bf16[128,1024]{1,0:T(8,128)(2,1)S(1)}, u32[]{:S(2)}, u32[]{:S(2)}) %collective-permute-start.23) | collective-permute-done | bytes 262176 | tf_op jit(solution)/shard_map/ppermute | solution.py:534
  58.8 1.3 %collective-permute-start.18 = (bf16[256,384]{1,0:T(8,128)(2,1)S(1)}, bf16[256,384]{1,0:T(8,128)(2,1)S(1)}, u32[]{:S(2)}, u32[]{:S(2)}) collective-permute-start(bf16[256,384]{1,0:T(8,128)(2,1)S(1)} %get-tuple-element.85.refs_2_), channel_id=1, source_target_pairs={{0,2},{1,3},{2,0},{3,1},{4,6},{5,7},{6,4},{7,5},{8,10},{9,11},{10,... | collective-permute-start | bytes 589832 | tf_op jit(solution)/shard_map/ppermute | solution.py:534
  60.1 1.4 %collective-permute-done.20.refs_3_ = bf16[144,384]{1,0:T(8,128)(2,1)S(1)} collective-permute-done((bf16[144,384]{1,0:T(8,128)(2,1)S(1)}, bf16[144,384]{1,0:T(8,128)(2,1)S(1)}, u32[]{:S(2)}, u32[]{:S(2)}) %collective-permute-start.20) | collective-permute-done | bytes 110624 | tf_op jit(solution)/shard_map/ppermute | solution.py:534
  63.6 1.7 %collective-permute-done.25.refs_1_ = bf16[2,48,1024]{2,1,0:T(8,128)(2,1)S(1)} collective-permute-done((bf16[2,48,1024]{2,1,0:T(8,128)(2,1)S(1)}, bf16[2,48,1024]{2,1,0:T(8,128)(2,1)S(1)}, u32[]{:S(2)}, u32[]{:S(2)}) %collective-permute-start.25) | collective-permute-done | bytes 196640 | tf_op jit(solution)/shard_map/ppermute | solution.py:534
  65.7 1.4 %collective-permute-start.29 = (bf16[1,128,384]{2,1,0:T(8,128)(2,1)S(1)}, bf16[1,128,384]{2,1,0:T(8,128)(2,1)S(1)}, u32[]{:S(2)}, u32[]{:S(2)}) collective-permute-start(bf16[1,128,384]{2,1,0:T(8,128)(2,1)S(1)} %get-tuple-element.100), channel_id=1, source_target_pairs={{0,4},{1,5},{2,6},{3,7},{4,0},{5,1},{6,2},{7,3},{8,12},{9,13},{10,... | collective-permute-start | bytes 294920 | tf_op jit(solution)/shard_map/ppermute | solution.py:534
  67.1 1.2 %conv_grad_second.1 = (f32[1,160,384]{2,1,0:T(8,128)S(1)}, f32[1,160,384]{2,1,0:T(8,128)S(1)}, bf16[1,288,384]{2,1,0:T(8,128)(2,1)S(1)}, bf16[1,160,384]{2,1,0:T(8,128)(2,1)S(1)}) custom-call(bf16[512,1024]{1,0:T(8,128)(2,1)S(1)} %get-tuple-element.72.refs_4_.refs_0_, bf16[192,512]{1,0:T(8,128)(2,1)S(1)} %get-tuple-element.73.refs_0_.refs_1_, ...), custom_call_target="tpu_custom_call" | custom-call | flops 402653184 | bytes 2965504 | tf_op jit(solution)/shard_map/conv_grad_second/pallas_call | solution.py:37
  68.3 1.4 %collective-permute-start.27 = (bf16[1,160,384]{2,1,0:T(8,128)(2,1)S(1)}, bf16[1,160,384]{2,1,0:T(8,128)(2,1)S(1)}, u32[]{:S(2)}, u32[]{:S(2)}) collective-permute-start(bf16[1,160,384]{2,1,0:T(8,128)(2,1)S(1)} %get-tuple-element.97), channel_id=1, source_target_pairs={{0,4},{1,5},{2,6},{3,7},{4,0},{5,1},{6,2},{7,3},{8,12},{9,13},{10,... | collective-permute-start | bytes 368648 | tf_op jit(solution)/shard_map/ppermute | solution.py:534
  69.7 1.9 %collective-permute-start.28 = (bf16[1,48,1024]{2,1,0:T(8,128)(2,1)S(1)}, bf16[1,48,1024]{2,1,0:T(8,128)(2,1)S(1)}, u32[]{:S(2)}, u32[]{:S(2)}) collective-permute-start(bf16[1,48,1024]{2,1,0:T(8,128)(2,1)S(1)} %get-tuple-element.98), channel_id=1, source_target_pairs={{0,8},{1,9},{2,10},{3,11},{4,12},{5,13},{6,14},{7,15},{8,0},{9,1},... | collective-permute-start | bytes 294920 | tf_op jit(solution)/shard_map/ppermute | solution.py:534
  71.6 2.0 %collective-permute-start.30 = (bf16[1,128,384]{2,1,0:T(8,128)(2,1)S(1)}, bf16[1,128,384]{2,1,0:T(8,128)(2,1)S(1)}, u32[]{:S(2)}, u32[]{:S(2)}) collective-permute-start(bf16[1,128,384]{2,1,0:T(8,128)(2,1)S(1)} %conv_send_on.3), channel_id=1, source_target_pairs={{0,8},{1,9},{2,10},{3,11},{4,12},{5,13},{6,14},{7,15},{8,0},{9,1},... | collective-permute-start | bytes 294920 | tf_op jit(solution)/shard_map/ppermute | solution.py:534
  74.2 2.5 %collective-permute-done.27.refs_1_ = bf16[1,160,384]{2,1,0:T(8,128)(2,1)S(1)} collective-permute-done((bf16[1,160,384]{2,1,0:T(8,128)(2,1)S(1)}, bf16[1,160,384]{2,1,0:T(8,128)(2,1)S(1)}, u32[]{:S(2)}, u32[]{:S(2)}) %collective-permute-start.27) | collective-permute-done | bytes 122912 | tf_op jit(solution)/shard_map/ppermute | solution.py:534
  77.2 4.9 %collective-permute-done.30.refs_6_.refs_2_ = bf16[1,128,384]{2,1,0:T(8,128)(2,1)S(1)} collective-permute-done((bf16[1,128,384]{2,1,0:T(8,128)(2,1)S(1)}, bf16[1,128,384]{2,1,0:T(8,128)(2,1)S(1)}, u32[]{:S(2)}, u32[]{:S(2)}) %collective-permute-start.30) | collective-permute-done | bytes 98336 | tf_op jit(solution)/shard_map/ppermute | solution.py:534
  82.1 2.0 %input_grad.1 = bf16[256,384]{1,0:T(8,128)(2,1)} custom-call(bf16[256,384]{1,0:T(8,128)(2,1)S(1)} %bitcast.10, bf16[144,384]{1,0:T(8,128)(2,1)S(1)} %get-tuple-element.86.refs_1_, bf16[256,384]{1,0:T(8,128)(2,1)S(1)} %get-tuple-element.85.refs_2_, bf16[144,384]{1,0:T(8,128)(2,1)S(1)} %collective-permute-done.20.refs_3_, ...), custom_call_target="tpu_custom_call" | custom-call | flops 7549747200 | bytes 4153344 | tf_op jit(solution)/shard_map/input_grad/pallas_call | solution.py:37
  (69 shorter events, 16.0 us)
Async XLA Ops:
  1.8 6.7 %collective-permute-start.1 = (bf16[32,384]{1,0:T(8,128)(2,1)S(1)}, bf16[32,384]{1,0:T(8,128)(2,1)S(1)}, u32[]{:S(2)}, u32[]{:S(2)}) collective-permute-start(bf16[32,384]{1,0:T(8,128)(2,1)S(1)} %get-tuple-element.59), channel_id=1, source_target_pairs={{2,4},{6,8},{10,12},{4,2},{8,6},{12,10},{3,5},{7,9},{11,13},{5,3},... | collective-permute-start | bytes 73736 | tf_op jit(solution)/shard_map/ppermute | solution.py:565
  2.6 7.7 %collective-permute-start = (bf16[32,384]{1,0:T(8,128)(2,1)S(1)}, bf16[32,384]{1,0:T(8,128)(2,1)S(1)}, u32[]{:S(2)}, u32[]{:S(2)}) collective-permute-start(bf16[32,384]{1,0:T(8,128)(2,1)S(1)} %get-tuple-element.59), channel_id=1, source_target_pairs={{0,2},{1,3},{2,0},{3,1},{4,6},{5,7},{6,4},{7,5},{8,10},{9,11},{10,... | collective-permute-start | bytes 73736 | tf_op jit(solution)/shard_map/ppermute | solution.py:534
  12.2 6.1 %collective-permute-start.4 = (bf16[320,128]{1,0:T(8,128)(2,1)S(1)}, bf16[320,128]{1,0:T(8,128)(2,1)S(1)}, u32[]{:S(2)}, u32[]{:S(2)}) collective-permute-start(bf16[320,128]{1,0:T(8,128)(2,1)S(1)} %get-tuple-element.62.refs_2_), channel_id=1, source_target_pairs={{0,4},{1,5},{2,6},{3,7},{4,0},{5,1},{6,2},{7,3},{8,12},{9,13},{10,... | collective-permute-start | bytes 245768 | tf_op jit(solution)/shard_map/ppermute | solution.py:534
  14.2 6.6 %collective-permute-start.3 = (bf16[320,128]{1,0:T(8,128)(2,1)S(1)}, bf16[320,128]{1,0:T(8,128)(2,1)S(1)}, u32[]{:S(2)}, u32[]{:S(2)}) collective-permute-start(bf16[320,128]{1,0:T(8,128)(2,1)S(1)} %get-tuple-element.62.refs_2_), channel_id=1, source_target_pairs={{0,12},{1,13},{2,14},{3,15},{4,8},{5,9},{6,10},{7,11},{8,4},{9,5},... | collective-permute-start | bytes 245768 | tf_op jit(solution)/shard_map/ppermute | solution.py:534
  16.7 6.6 %collective-permute-start.2 = (bf16[320,128]{1,0:T(8,128)(2,1)S(1)}, bf16[320,128]{1,0:T(8,128)(2,1)S(1)}, u32[]{:S(2)}, u32[]{:S(2)}) collective-permute-start(bf16[320,128]{1,0:T(8,128)(2,1)S(1)} %get-tuple-element.62.refs_2_), channel_id=1, source_target_pairs={{0,8},{1,9},{2,10},{3,11},{4,12},{5,13},{6,14},{7,15},{8,0},{9,1},... | collective-permute-start | bytes 245768 | tf_op jit(solution)/shard_map/ppermute | solution.py:534
  16.8 8.4 %collective-permute-start.5 = (bf16[320,128]{1,0:T(8,128)(2,1)S(1)}, bf16[320,128]{1,0:T(8,128)(2,1)S(1)}, u32[]{:S(2)}, u32[]{:S(2)}) collective-permute-start(bf16[320,128]{1,0:T(8,128)(2,1)S(1)} %get-tuple-element.62.refs_2_), channel_id=1, source_target_pairs={{0,2},{1,3},{2,0},{3,1},{4,6},{5,7},{6,4},{7,5},{8,10},{9,11},{10,... | collective-permute-start | bytes 245768 | tf_op jit(solution)/shard_map/ppermute | solution.py:534
  18.3 6.9 %collective-permute-start.8 = (bf16[320,128]{1,0:T(8,128)(2,1)S(1)}, bf16[320,128]{1,0:T(8,128)(2,1)S(1)}, u32[]{:S(2)}, u32[]{:S(2)}) collective-permute-start(bf16[320,128]{1,0:T(8,128)(2,1)S(1)} %collective-permute-done.4.refs_5_), channel_id=1, source_target_pairs={{0,2},{1,3},{2,0},{3,1},{4,6},{5,7},{6,4},{7,5},{8,10},{9,11},{10,... | collective-permute-start | bytes 245768 | tf_op jit(solution)/shard_map/ppermute | solution.py:534
  20.8 5.1 %collective-permute-start.7 = (bf16[320,128]{1,0:T(8,128)(2,1)S(1)}, bf16[320,128]{1,0:T(8,128)(2,1)S(1)}, u32[]{:S(2)}, u32[]{:S(2)}) collective-permute-start(bf16[320,128]{1,0:T(8,128)(2,1)S(1)} %collective-permute-done.3.refs_4_), channel_id=1, source_target_pairs={{0,2},{1,3},{2,0},{3,1},{4,6},{5,7},{6,4},{7,5},{8,10},{9,11},{10,... | collective-permute-start | bytes 245768 | tf_op jit(solution)/shard_map/ppermute | solution.py:534
  23.3 4.4 %collective-permute-start.6 = (bf16[320,128]{1,0:T(8,128)(2,1)S(1)}, bf16[320,128]{1,0:T(8,128)(2,1)S(1)}, u32[]{:S(2)}, u32[]{:S(2)}) collective-permute-start(bf16[320,128]{1,0:T(8,128)(2,1)S(1)} %collective-permute-done.2.refs_3_), channel_id=1, source_target_pairs={{0,2},{1,3},{2,0},{3,1},{4,6},{5,7},{6,4},{7,5},{8,10},{9,11},{10,... | collective-permute-start | bytes 245768 | tf_op jit(solution)/shard_map/ppermute | solution.py:534
  27.7 7.7 %collective-permute-start.10 = (bf16[416,384]{1,0:T(8,128)(2,1)S(1)}, bf16[416,384]{1,0:T(8,128)(2,1)S(1)}, u32[]{:S(2)}, u32[]{:S(2)}) collective-permute-start(bf16[416,384]{1,0:T(8,128)(2,1)S(1)} %get-tuple-element.69), channel_id=1, source_target_pairs={{0,2},{1,3},{2,0},{3,1},{4,6},{5,7},{6,4},{7,5},{8,10},{9,11},{10,... | collective-permute-start | bytes 958472 | tf_op jit(solution)/shard_map/ppermute | solution.py:534
  35.4 2.0 %collective-permute-start.11 = (bf16[416,384]{1,0:T(8,128)(2,1)S(1)}, bf16[416,384]{1,0:T(8,128)(2,1)S(1)}, u32[]{:S(2)}, u32[]{:S(2)}) collective-permute-start(bf16[416,384]{1,0:T(8,128)(2,1)S(1)} %collective-permute-done.10.refs_3_), channel_id=1, source_target_pairs={{0,1},{1,0},{2,3},{3,2},{4,5},{5,4},{6,7},{7,6},{8,9},{9,8},{10,11... | collective-permute-start | bytes 958472 | tf_op jit(solution)/shard_map/ppermute | solution.py:534
  35.4 2.0 %collective-permute-start.9 = (bf16[352,384]{1,0:T(8,128)(2,1)S(1)}, bf16[352,384]{1,0:T(8,128)(2,1)S(1)}, u32[]{:S(2)}, u32[]{:S(2)}) collective-permute-start(bf16[352,384]{1,0:T(8,128)(2,1)S(1)} %get-tuple-element.67), channel_id=1, source_target_pairs={{0,1},{1,0},{2,3},{3,2},{4,5},{5,4},{6,7},{7,6},{8,9},{9,8},{10,11... | collective-permute-start | bytes 811016 | tf_op jit(solution)/shard_map/ppermute | solution.py:534
  35.9 7.2 %collective-permute-start.12 = (bf16[4,160,128]{2,1,0:T(8,128)(2,1)S(1)}, bf16[4,160,128]{2,1,0:T(8,128)(2,1)S(1)}, u32[]{:S(2)}, u32[]{:S(2)}) collective-permute-start(bf16[4,160,128]{2,1,0:T(8,128)(2,1)S(1)} %get-tuple-element.70), channel_id=1, source_target_pairs={{0,2},{1,3},{2,0},{3,1},{4,6},{5,7},{6,4},{7,5},{8,10},{9,11},{10,... | collective-permute-start | bytes 491528 | tf_op jit(solution)/shard_map/ppermute | solution.py:534
  37.3 5.8 %collective-permute-start.13 = (bf16[4,160,128]{2,1,0:T(8,128)(2,1)S(1)}, bf16[4,160,128]{2,1,0:T(8,128)(2,1)S(1)}, u32[]{:S(2)}, u32[]{:S(2)}) collective-permute-start(bf16[4,160,128]{2,1,0:T(8,128)(2,1)S(1)} %get-tuple-element.76), channel_id=1, source_target_pairs={{0,4},{1,5},{2,6},{3,7},{4,0},{5,1},{6,2},{7,3},{8,12},{9,13},{10,... | collective-permute-start | bytes 491528 | tf_op jit(solution)/shard_map/ppermute | solution.py:534
  43.2 4.5 %collective-permute-start.14 = (bf16[2,160,128]{2,1,0:T(8,128)(2,1)S(1)}, bf16[2,160,128]{2,1,0:T(8,128)(2,1)S(1)}, u32[]{:S(2)}, u32[]{:S(2)}) collective-permute-start(bf16[2,160,128]{2,1,0:T(8,128)(2,1)S(1)} %get-tuple-element.78), channel_id=1, source_target_pairs={{0,4},{1,5},{2,6},{3,7},{4,0},{5,1},{6,2},{7,3},{8,12},{9,13},{10,... | collective-permute-start | bytes 245768 | tf_op jit(solution)/shard_map/ppermute | solution.py:534
  43.5 4.4 %collective-permute-start.15 = (bf16[2,160,128]{2,1,0:T(8,128)(2,1)S(1)}, bf16[2,160,128]{2,1,0:T(8,128)(2,1)S(1)}, u32[]{:S(2)}, u32[]{:S(2)}) collective-permute-start(bf16[2,160,128]{2,1,0:T(8,128)(2,1)S(1)} %get-tuple-element.80), channel_id=1, source_target_pairs={{0,2},{1,3},{2,0},{3,1},{4,6},{5,7},{6,4},{7,5},{8,10},{9,11},{10,... | collective-permute-start | bytes 245768 | tf_op jit(solution)/shard_map/ppermute | solution.py:534
  48.0 7.9 %collective-permute-start.22 = (bf16[128,1024]{1,0:T(8,128)(2,1)S(1)}, bf16[128,1024]{1,0:T(8,128)(2,1)S(1)}, u32[]{:S(2)}, u32[]{:S(2)}) collective-permute-start(bf16[128,1024]{1,0:T(8,128)(2,1)S(1)} %get-tuple-element.87.refs_0_.refs_1_), channel_id=1, source_target_pairs={{0,2},{1,3},{2,0},{3,1},{4,6},{5,7},{6,4},{7,5},{8,10},{9,11},{10,... | collective-permute-start | bytes 786440 | tf_op jit(solution)/shard_map/ppermute | solution.py:534
  49.2 6.2 %collective-permute-start.16 = (bf16[1,320,128]{2,1,0:T(8,128)(2,1)S(1)}, bf16[1,320,128]{2,1,0:T(8,128)(2,1)S(1)}, u32[]{:S(2)}, u32[]{:S(2)}) collective-permute-start(bf16[1,320,128]{2,1,0:T(8,128)(2,1)S(1)} %get-tuple-element.82), channel_id=1, source_target_pairs={{0,8},{1,9},{2,10},{3,11},{4,12},{5,13},{6,14},{7,15},{8,0},{9,1},... | collective-permute-start | bytes 245768 | tf_op jit(solution)/shard_map/ppermute | solution.py:534
  52.0 4.0 %collective-permute-start.21 = (bf16[128,1024]{1,0:T(8,128)(2,1)S(1)}, bf16[128,1024]{1,0:T(8,128)(2,1)S(1)}, u32[]{:S(2)}, u32[]{:S(2)}) collective-permute-start(bf16[128,1024]{1,0:T(8,128)(2,1)S(1)} %get-tuple-element.87.refs_0_.refs_1_), channel_id=1, source_target_pairs={{0,1},{1,0},{2,3},{3,2},{4,5},{5,4},{6,7},{7,6},{8,9},{9,8},{10,11... | collective-permute-start | bytes 786440 | tf_op jit(solution)/shard_map/ppermute | solution.py:534
  55.9 1.6 %collective-permute-start.23 = (bf16[128,1024]{1,0:T(8,128)(2,1)S(1)}, bf16[128,1024]{1,0:T(8,128)(2,1)S(1)}, u32[]{:S(2)}, u32[]{:S(2)}) collective-permute-start(bf16[128,1024]{1,0:T(8,128)(2,1)S(1)} %collective-permute-done.22.refs_3_), channel_id=1, source_target_pairs={{0,1},{1,0},{2,3},{3,2},{4,5},{5,4},{6,7},{7,6},{8,9},{9,8},{10,11... | collective-permute-start | bytes 786440 | tf_op jit(solution)/shard_map/ppermute | solution.py:534
  56.0 5.6 %collective-permute-start.20 = (bf16[144,384]{1,0:T(8,128)(2,1)S(1)}, bf16[144,384]{1,0:T(8,128)(2,1)S(1)}, u32[]{:S(2)}, u32[]{:S(2)}) collective-permute-start(bf16[144,384]{1,0:T(8,128)(2,1)S(1)} %get-tuple-element.86.refs_1_), channel_id=1, source_target_pairs={{0,2},{1,3},{2,0},{3,1},{4,6},{5,7},{6,4},{7,5},{8,10},{9,11},{10,... | collective-permute-start | bytes 331784 | tf_op jit(solution)/shard_map/ppermute | solution.py:534
  58.3 7.0 %collective-permute-start.25 = (bf16[2,48,1024]{2,1,0:T(8,128)(2,1)S(1)}, bf16[2,48,1024]{2,1,0:T(8,128)(2,1)S(1)}, u32[]{:S(2)}, u32[]{:S(2)}) collective-permute-start(bf16[2,48,1024]{2,1,0:T(8,128)(2,1)S(1)} %get-tuple-element.92), channel_id=1, source_target_pairs={{0,4},{1,5},{2,6},{3,7},{4,0},{5,1},{6,2},{7,3},{8,12},{9,13},{10,... | collective-permute-start | bytes 589832 | tf_op jit(solution)/shard_map/ppermute | solution.py:534
  58.8 6.8 %collective-permute-start.18 = (bf16[256,384]{1,0:T(8,128)(2,1)S(1)}, bf16[256,384]{1,0:T(8,128)(2,1)S(1)}, u32[]{:S(2)}, u32[]{:S(2)}) collective-permute-start(bf16[256,384]{1,0:T(8,128)(2,1)S(1)} %get-tuple-element.85.refs_2_), channel_id=1, source_target_pairs={{0,2},{1,3},{2,0},{3,1},{4,6},{5,7},{6,4},{7,5},{8,10},{9,11},{10,... | collective-permute-start | bytes 589832 | tf_op jit(solution)/shard_map/ppermute | solution.py:534
  60.1 1.9 %collective-permute-start.19 = (bf16[144,384]{1,0:T(8,128)(2,1)S(1)}, bf16[144,384]{1,0:T(8,128)(2,1)S(1)}, u32[]{:S(2)}, u32[]{:S(2)}) collective-permute-start(bf16[144,384]{1,0:T(8,128)(2,1)S(1)} %get-tuple-element.86.refs_1_), channel_id=1, source_target_pairs={{0,1},{1,0},{2,3},{3,2},{4,5},{5,4},{6,7},{7,6},{8,9},{9,8},{10,11... | collective-permute-start | bytes 331784 | tf_op jit(solution)/shard_map/ppermute | solution.py:534
  61.5 5.6 %collective-permute-start.17 = (bf16[256,384]{1,0:T(8,128)(2,1)S(1)}, bf16[256,384]{1,0:T(8,128)(2,1)S(1)}, u32[]{:S(2)}, u32[]{:S(2)}) collective-permute-start(bf16[256,384]{1,0:T(8,128)(2,1)S(1)} %get-tuple-element.85.refs_2_), channel_id=1, source_target_pairs={{0,1},{1,0},{2,3},{3,2},{4,5},{5,4},{6,7},{7,6},{8,9},{9,8},{10,11... | collective-permute-start | bytes 589832 | tf_op jit(solution)/shard_map/ppermute | solution.py:534
  65.6 1.4 %collective-permute-start.26 = (bf16[256,384]{1,0:T(8,128)(2,1)S(1)}, bf16[256,384]{1,0:T(8,128)(2,1)S(1)}, u32[]{:S(2)}, u32[]{:S(2)}) collective-permute-start(bf16[256,384]{1,0:T(8,128)(2,1)S(1)} %collective-permute-done.18.refs_4_), channel_id=1, source_target_pairs={{0,1},{1,0},{2,3},{3,2},{4,5},{5,4},{6,7},{7,6},{8,9},{9,8},{10,11... | collective-permute-start | bytes 589832 | tf_op jit(solution)/shard_map/ppermute | solution.py:534
  65.7 5.9 %collective-permute-start.29 = (bf16[1,128,384]{2,1,0:T(8,128)(2,1)S(1)}, bf16[1,128,384]{2,1,0:T(8,128)(2,1)S(1)}, u32[]{:S(2)}, u32[]{:S(2)}) collective-permute-start(bf16[1,128,384]{2,1,0:T(8,128)(2,1)S(1)} %get-tuple-element.100), channel_id=1, source_target_pairs={{0,4},{1,5},{2,6},{3,7},{4,0},{5,1},{6,2},{7,3},{8,12},{9,13},{10,... | collective-permute-start | bytes 294920 | tf_op jit(solution)/shard_map/ppermute | solution.py:534
  68.3 8.4 %collective-permute-start.27 = (bf16[1,160,384]{2,1,0:T(8,128)(2,1)S(1)}, bf16[1,160,384]{2,1,0:T(8,128)(2,1)S(1)}, u32[]{:S(2)}, u32[]{:S(2)}) collective-permute-start(bf16[1,160,384]{2,1,0:T(8,128)(2,1)S(1)} %get-tuple-element.97), channel_id=1, source_target_pairs={{0,4},{1,5},{2,6},{3,7},{4,0},{5,1},{6,2},{7,3},{8,12},{9,13},{10,... | collective-permute-start | bytes 368648 | tf_op jit(solution)/shard_map/ppermute | solution.py:534
  69.7 7.5 %collective-permute-start.28 = (bf16[1,48,1024]{2,1,0:T(8,128)(2,1)S(1)}, bf16[1,48,1024]{2,1,0:T(8,128)(2,1)S(1)}, u32[]{:S(2)}, u32[]{:S(2)}) collective-permute-start(bf16[1,48,1024]{2,1,0:T(8,128)(2,1)S(1)} %get-tuple-element.98), channel_id=1, source_target_pairs={{0,8},{1,9},{2,10},{3,11},{4,12},{5,13},{6,14},{7,15},{8,0},{9,1},... | collective-permute-start | bytes 294920 | tf_op jit(solution)/shard_map/ppermute | solution.py:534
  71.6 10.5 %collective-permute-start.30 = (bf16[1,128,384]{2,1,0:T(8,128)(2,1)S(1)}, bf16[1,128,384]{2,1,0:T(8,128)(2,1)S(1)}, u32[]{:S(2)}, u32[]{:S(2)}) collective-permute-start(bf16[1,128,384]{2,1,0:T(8,128)(2,1)S(1)} %conv_send_on.3), channel_id=1, source_target_pairs={{0,8},{1,9},{2,10},{3,11},{4,12},{5,13},{6,14},{7,15},{8,0},{9,1},... | collective-permute-start | bytes 294920 | tf_op jit(solution)/shard_map/ppermute | solution.py:534
  73.6 11.7 %collective-permute-start.31 = (bf16[1,288,384]{2,1,0:T(8,128)(2,1)S(1)}, bf16[1,288,384]{2,1,0:T(8,128)(2,1)S(1)}, u32[]{:S(2)}, u32[]{:S(2)}) collective-permute-start(bf16[1,288,384]{2,1,0:T(8,128)(2,1)S(1)} %get-tuple-element.102), channel_id=1, source_target_pairs={{0,4},{1,5},{2,6},{3,7},{4,0},{5,1},{6,2},{7,3},{8,12},{9,13},{10,... | collective-permute-start | bytes 663560 | tf_op jit(solution)/shard_map/ppermute | solution.py:534
  76.7 8.6 %collective-permute-start.32 = (bf16[1,160,384]{2,1,0:T(8,128)(2,1)S(1)}, bf16[1,160,384]{2,1,0:T(8,128)(2,1)S(1)}, u32[]{:S(2)}, u32[]{:S(2)}) collective-permute-start(bf16[1,160,384]{2,1,0:T(8,128)(2,1)S(1)} %conv_send_on.2), channel_id=1, source_target_pairs={{0,8},{1,9},{2,10},{3,11},{4,12},{5,13},{6,14},{7,15},{8,0},{9,1},... | collective-permute-start | bytes 368648 | tf_op jit(solution)/shard_map/ppermute | solution.py:534
  (9 other events, 101.4 us)

commit v15 on v14

--- a/solution.py
+++ b/solution.py
@@ -634,14 +634,12 @@
     )
     in_a, in_b = swap(send_a, 1), swap(send_b, 2)
     early_near = swap(to_near, 1)
-    early_blocks = [early, swap(to_core, 0, 1), early_near, swap(held(early_near, send_a), 0, 1)]
-    conv_pick, norm_pick = run(
-        lambda *refs: select_kernel(*refs, order=order, rows=conv_rows, padded=conv_pad),
-        [((groups * conv_pad, 8 * tokens), BF), ((groups * norm_pad, 4 * tokens), BF)],
-        [pick_own] + early_blocks,
-        [pltpu.VMEM((ext, channels), F32), pltpu.VMEM((ext, channels), F32)],
-        flops=2 * groups * conv_pad * taps * channels * 8 * tokens,
-        name="select",
+    (normed_cot,) = run(
+        query_cot_kernel,
+        [((tokens, width), F32)],
+        [query_cot, wq],
+        flops=2 * tokens * width * heads * key_size,
+        name="query_part",
     )
     fourth = (groups // 2,) + half_block[1:]
     keep_a, send_a, keep_b, send_b = run(
@@ -649,8 +647,10 @@
         [(fourth, F32), (fourth, BF)] * 2,
         [keep_a, in_a, keep_b, in_b],
         name="kv_cot_fold",
-        after=[conv_pick],
-    )
+        after=[normed_cot],
+    )
+    early_core, early_last = swap(held(to_core, keep_a), 0, 1), swap(held(early_near, keep_a), 0, 1)
+    early_blocks = [early, early_core, early_near, early_last]
     in_a, in_b = swap(send_a, 2), swap(send_b, 1)
     block = (groups // 4, 5 * tokens // 2, key_size)
     keep, send = run(
@@ -659,12 +659,13 @@
         [keep_a, in_a, keep_b, in_b],
         name="kv_cot_merge",
     )
-    (normed_cot,) = run(
-        query_cot_kernel,
-        [((tokens, width), F32)],
-        [query_cot, wq],
-        flops=2 * tokens * width * heads * key_size,
-        name="query_part",
+    conv_pick, norm_pick = run(
+        lambda *refs: select_kernel(*refs, order=order, rows=conv_rows, padded=conv_pad),
+        [((groups * conv_pad, 8 * tokens), BF), ((groups * norm_pad, 4 * tokens), BF)],
+        [held(pick_own, keep)] + early_blocks,
+        [pltpu.VMEM((ext, channels), F32), pltpu.VMEM((ext, channels), F32)],
+        flops=2 * groups * conv_pad * taps * channels * 8 * tokens,
+        name="select",
     )
     query_cot = held(query_cot, keep)
     query_near, query_core = swap(query_cot, 1), swap(query_cot, 0, 1)
@@ -676,7 +677,7 @@
             ((2 * tokens, width // 2), BF),
         ]
         + [((16, width), BF)] * (len(bits) > 3),
-        kv_cot + [normed_cot, pooled, gain, wk, wv],
+        kv_cot + [normed_cot, held(pooled, conv_pick), gain, wk, wv],
         flops=2 * tokens * width * (key_size + value_size),
         name="conv_cot",
     )

time: 86.4 us -> 88.1 us (1.020)
  starting transfers between devices: 35.2 us -> 36.1 us
    ppermute x32, starting transfers between devices: 34.4 us -> 35.4 us  [swap(): lax.ppermute(value, both_axes, [(i, i ^ mask) for i in range(owners)])]
  transfers between devices with their start and end apart: 33 -> 33, of which waited for: 18 -> 19; matrix products, arithmetic and copies ran while one was open for 0% -> 0% of each run, Pallas kernels for 17% -> 17%
where the time goes in v15:
time: 88.1 us; the launch traced here: 87.9 us
  starting transfers between devices  36.1 us (41%)
  waiting for transfers between devices  32.2 us (37%)
  Pallas kernels  17.8 us (20%)
  local copies, waits for them, and re-layouts  0.96 us (1%)
    ppermute x32, starting transfers between devices, swap(): lax.ppermute(value, both_axes, [(i, i ^ mask) for i in range(owners)])  35.4 us
    ppermute x32, waiting for transfers between devices, swap(): lax.ppermute(value, both_axes, [(i, i ^ mask) for i in range(owners)])  32.2 us
    pallas_call x18, Pallas kernels, run(): pl.pallas_call(whole, out_shape=[jax.ShapeDtypeStruct(s, t) for s, t in o...  17.8 us
  transfers between devices with their start and end apart: 33, of which 19 were waited for; matrix products, arithmetic and copies ran while one was open for 0% of the time, Pallas kernels for 17%

profile of v15, /device:TPU:0, one launch (start us, length us, event | category | flops | bytes accessed | tf_op | source)
XLA Modules:
  0.0 87.9 jit_solution(5982331725260319812)
XLA Ops:
  1.8 3.0 %collective-permute-start = (bf16[32,384]{1,0:T(8,128)(2,1)S(1)}, bf16[32,384]{1,0:T(8,128)(2,1)S(1)}, u32[]{:S(2)}, u32[]{:S(2)}) collective-permute-start(bf16[32,384]{1,0:T(8,128)(2,1)S(1)} %get-tuple-element.62), channel_id=1, source_target_pairs={{0,2},{1,3},{2,0},{3,1},{4,6},{5,7},{6,4},{7,5},{8,10},{9,11},{10,... | collective-permute-start | bytes 73736 | tf_op jit(solution)/shard_map/ppermute | solution.py:534
  5.5 1.1 %collective-permute-done.refs_1_ = bf16[32,384]{1,0:T(8,128)(2,1)S(1)} collective-permute-done((bf16[32,384]{1,0:T(8,128)(2,1)S(1)}, bf16[32,384]{1,0:T(8,128)(2,1)S(1)}, u32[]{:S(2)}, u32[]{:S(2)}) %collective-permute-start) | collective-permute-done | bytes 24608 | tf_op jit(solution)/shard_map/ppermute | solution.py:534
  6.6 1.9 %front.1 = (bf16[320,128]{1,0:T(8,128)(2,1)S(1)}, bf16[288,384]{1,0:T(8,128)(2,1)S(1)}, bf16[128,768]{1,0:T(8,128)(2,1)S(1)}, f32[128,768]{1,0:T(8,128)S(1)}) custom-call(f32[3,304,128]{2,1,0:T(8,128)S(1)} %get-tuple-element.61.refs_0_, bf16[32,384]{1,0:T(8,128)(2,1)S(1)} %collective-permute-done.refs_1_, ...), custom_call_target="tpu_custom_call" | custom-call | flops 754974720 | bytes 4852736 | tf_op jit(solution)/shard_map/front/pallas_call | solution.py:37
  8.5 7.4 %collective-permute-start.2 = (bf16[320,128]{1,0:T(8,128)(2,1)S(1)}, bf16[320,128]{1,0:T(8,128)(2,1)S(1)}, u32[]{:S(2)}, u32[]{:S(2)}) collective-permute-start(bf16[320,128]{1,0:T(8,128)(2,1)S(1)} %get-tuple-element.65.refs_2_), channel_id=1, source_target_pairs={{0,8},{1,9},{2,10},{3,11},{4,12},{5,13},{6,14},{7,15},{8,0},{9,1},... | collective-permute-start | bytes 245768 | tf_op jit(solution)/shard_map/ppermute | solution.py:534
  15.9 1.3 %collective-permute-start.3 = (bf16[320,128]{1,0:T(8,128)(2,1)S(1)}, bf16[320,128]{1,0:T(8,128)(2,1)S(1)}, u32[]{:S(2)}, u32[]{:S(2)}) collective-permute-start(bf16[320,128]{1,0:T(8,128)(2,1)S(1)} %get-tuple-element.65.refs_2_), channel_id=1, source_target_pairs={{0,12},{1,13},{2,14},{3,15},{4,8},{5,9},{6,10},{7,11},{8,4},{9,5},... | collective-permute-start | bytes 245768 | tf_op jit(solution)/shard_map/ppermute | solution.py:534
  17.9 2.7 %collective-permute-done.2.refs_3_ = bf16[320,128]{1,0:T(8,128)(2,1)S(1)} collective-permute-done((bf16[320,128]{1,0:T(8,128)(2,1)S(1)}, bf16[320,128]{1,0:T(8,128)(2,1)S(1)}, u32[]{:S(2)}, u32[]{:S(2)}) %collective-permute-start.2) | collective-permute-done | bytes 81952 | tf_op jit(solution)/shard_map/ppermute | solution.py:534
  21.2 1.1 %collective-permute-done.3.refs_4_ = bf16[320,128]{1,0:T(8,128)(2,1)S(1)} collective-permute-done((bf16[320,128]{1,0:T(8,128)(2,1)S(1)}, bf16[320,128]{1,0:T(8,128)(2,1)S(1)}, u32[]{:S(2)}, u32[]{:S(2)}) %collective-permute-start.3) | collective-permute-done | bytes 81952 | tf_op jit(solution)/shard_map/ppermute | solution.py:534
  23.0 1.4 %collective-permute-start.8 = (bf16[320,128]{1,0:T(8,128)(2,1)S(1)}, bf16[320,128]{1,0:T(8,128)(2,1)S(1)}, u32[]{:S(2)}, u32[]{:S(2)}) collective-permute-start(bf16[320,128]{1,0:T(8,128)(2,1)S(1)} %collective-permute-done.4.refs_5_), channel_id=1, source_target_pairs={{0,2},{1,3},{2,0},{3,1},{4,6},{5,7},{6,4},{7,5},{8,10},{9,11},{10,... | collective-permute-start | bytes 245768 | tf_op jit(solution)/shard_map/ppermute | solution.py:534
  25.2 1.5 %collective-permute-done.7.refs_8_ = bf16[320,128]{1,0:T(8,128)(2,1)S(1)} collective-permute-done((bf16[320,128]{1,0:T(8,128)(2,1)S(1)}, bf16[320,128]{1,0:T(8,128)(2,1)S(1)}, u32[]{:S(2)}, u32[]{:S(2)}) %collective-permute-start.7) | collective-permute-done | bytes 81952 | tf_op jit(solution)/shard_map/ppermute | solution.py:534
  26.8 1.3 %collective-permute-done.8.refs_9_ = bf16[320,128]{1,0:T(8,128)(2,1)S(1)} collective-permute-done((bf16[320,128]{1,0:T(8,128)(2,1)S(1)}, bf16[320,128]{1,0:T(8,128)(2,1)S(1)}, u32[]{:S(2)}, u32[]{:S(2)}) %collective-permute-start.8) | collective-permute-done | bytes 81952 | tf_op jit(solution)/shard_map/ppermute | solution.py:534
  28.1 1.0 %collective-permute-start.14 = (bf16[416,384]{1,0:T(8,128)(2,1)S(1)}, bf16[416,384]{1,0:T(8,128)(2,1)S(1)}, u32[]{:S(2)}, u32[]{:S(2)}) collective-permute-start(bf16[416,384]{1,0:T(8,128)(2,1)S(1)} %get-tuple-element.84), channel_id=1, source_target_pairs={{0,2},{1,3},{2,0},{3,1},{4,6},{5,7},{6,4},{7,5},{8,10},{9,11},{10,... | collective-permute-start | bytes 958472 | tf_op jit(solution)/shard_map/ppermute | solution.py:534
  29.2 5.7 %attend.1 = (bf16[128,1536]{1,0:T(8,128)(2,1)}, bf16[128,1024]{1,0:T(8,128)(2,1)S(1)}, f32[4,160,128]{2,1,0:T(8,128)S(1)}, bf16[4,160,128]{2,1,0:T(8,128)(2,1)S(...) custom-call(bf16[128,1024]{1,0:T(8,128)(2,1)S(1)} %get-tuple-element.66.refs_0_, ...), custom_call_target="tpu_custom_call" | custom-call | flops 2013265920 | bytes 2949120 | tf_op jit(solution)/shard_map/attend/pallas_call | solution.py:37
  35.8 1.2 %collective-permute-start.10 = (bf16[4,160,128]{2,1,0:T(8,128)(2,1)S(1)}, bf16[4,160,128]{2,1,0:T(8,128)(2,1)S(1)}, u32[]{:S(2)}, u32[]{:S(2)}) collective-permute-start(bf16[4,160,128]{2,1,0:T(8,128)(2,1)S(1)} %get-tuple-element.72), channel_id=1, source_target_pairs={{0,4},{1,5},{2,6},{3,7},{4,0},{5,1},{6,2},{7,3},{8,12},{9,13},{10,... | collective-permute-start | bytes 491528 | tf_op jit(solution)/shard_map/ppermute | solution.py:534
  37.7 2.5 %collective-permute-done.9.refs_1_ = bf16[4,160,128]{2,1,0:T(8,128)(2,1)S(1)} collective-permute-done((bf16[4,160,128]{2,1,0:T(8,128)(2,1)S(1)}, bf16[4,160,128]{2,1,0:T(8,128)(2,1)S(1)}, u32[]{:S(2)}, u32[]{:S(2)}) %collective-permute-start.9) | collective-permute-done | bytes 163872 | tf_op jit(solution)/shard_map/ppermute | solution.py:534
  41.8 1.2 %collective-permute-start.11 = (bf16[2,160,128]{2,1,0:T(8,128)(2,1)S(1)}, bf16[2,160,128]{2,1,0:T(8,128)(2,1)S(1)}, u32[]{:S(2)}, u32[]{:S(2)}) collective-permute-start(bf16[2,160,128]{2,1,0:T(8,128)(2,1)S(1)} %get-tuple-element.75), channel_id=1, source_target_pairs={{0,4},{1,5},{2,6},{3,7},{4,0},{5,1},{6,2},{7,3},{8,12},{9,13},{10,... | collective-permute-start | bytes 245768 | tf_op jit(solution)/shard_map/ppermute | solution.py:534
  43.4 2.8 %collective-permute-done.11.refs_1_ = bf16[2,160,128]{2,1,0:T(8,128)(2,1)S(1)} collective-permute-done((bf16[2,160,128]{2,1,0:T(8,128)(2,1)S(1)}, bf16[2,160,128]{2,1,0:T(8,128)(2,1)S(1)}, u32[]{:S(2)}, u32[]{:S(2)}) %collective-permute-start.11) | collective-permute-done | bytes 81952 | tf_op jit(solution)/shard_map/ppermute | solution.py:534
  46.2 1.2 %collective-permute-done.12.refs_3_ = bf16[2,160,128]{2,1,0:T(8,128)(2,1)S(1)} collective-permute-done((bf16[2,160,128]{2,1,0:T(8,128)(2,1)S(1)}, bf16[2,160,128]{2,1,0:T(8,128)(2,1)S(1)}, u32[]{:S(2)}, u32[]{:S(2)}) %collective-permute-start.12) | collective-permute-done | bytes 81952 | tf_op jit(solution)/shard_map/ppermute | solution.py:534
  48.0 4.8 %collective-permute-start.16 = (bf16[1,320,128]{2,1,0:T(8,128)(2,1)S(1)}, bf16[1,320,128]{2,1,0:T(8,128)(2,1)S(1)}, u32[]{:S(2)}, u32[]{:S(2)}) collective-permute-start(bf16[1,320,128]{2,1,0:T(8,128)(2,1)S(1)} %get-tuple-element.88), channel_id=1, source_target_pairs={{0,8},{1,9},{2,10},{3,11},{4,12},{5,13},{6,14},{7,15},{8,0},{9,1},... | collective-permute-start | bytes 245768 | tf_op jit(solution)/shard_map/ppermute | solution.py:534
  52.8 2.4 %select.1 = (bf16[512,1024]{1,0:T(8,128)(2,1)S(1)}, bf16[192,512]{1,0:T(8,128)(2,1)S(1)}) custom-call(bf16[192,128]{1,0:T(8,128)(2,1)S(1)} %get-tuple-element.79.refs_0_, bf16[288,384]{1,0:T(8,128)(2,1)S(1)} %get-tuple-element.64.refs_2_.refs_1_, bf16[352,384]{1,0:T(8,128)(2,1)S(1)} %collective-permute-done.13.refs_2_, ...), custom_call_target="tpu_custom_call" | custom-call | flops 2013265920 | bytes 2424832 | tf_op jit(solution)/shard_map/select/pallas_call | solution.py:37
  55.3 1.9 %collective-permute-done.16.refs_1_ = bf16[1,320,128]{2,1,0:T(8,128)(2,1)S(1)} collective-permute-done((bf16[1,320,128]{2,1,0:T(8,128)(2,1)S(1)}, bf16[1,320,128]{2,1,0:T(8,128)(2,1)S(1)}, u32[]{:S(2)}, u32[]{:S(2)}) %collective-permute-start.16) | collective-permute-done | bytes 81952 | tf_op jit(solution)/shard_map/ppermute | solution.py:534
  58.0 1.1 %collective-permute-done.23.refs_4_ = bf16[128,1024]{1,0:T(8,128)(2,1)S(1)} collective-permute-done((bf16[128,1024]{1,0:T(8,128)(2,1)S(1)}, bf16[128,1024]{1,0:T(8,128)(2,1)S(1)}, u32[]{:S(2)}, u32[]{:S(2)}) %collective-permute-start.23) | collective-permute-done | bytes 262176 | tf_op jit(solution)/shard_map/ppermute | solution.py:534
  60.7 2.6 %collective-permute-done.20.refs_3_ = bf16[144,384]{1,0:T(8,128)(2,1)S(1)} collective-permute-done((bf16[144,384]{1,0:T(8,128)(2,1)S(1)}, bf16[144,384]{1,0:T(8,128)(2,1)S(1)}, u32[]{:S(2)}, u32[]{:S(2)}) %collective-permute-start.20) | collective-permute-done | bytes 110624 | tf_op jit(solution)/shard_map/ppermute | solution.py:534
  65.4 1.6 %collective-permute-done.25.refs_1_ = bf16[2,48,1024]{2,1,0:T(8,128)(2,1)S(1)} collective-permute-done((bf16[2,48,1024]{2,1,0:T(8,128)(2,1)S(1)}, bf16[2,48,1024]{2,1,0:T(8,128)(2,1)S(1)}, u32[]{:S(2)}, u32[]{:S(2)}) %collective-permute-start.25) | collective-permute-done | bytes 196640 | tf_op jit(solution)/shard_map/ppermute | solution.py:534
  67.3 1.4 %collective-permute-start.29 = (bf16[1,128,384]{2,1,0:T(8,128)(2,1)S(1)}, bf16[1,128,384]{2,1,0:T(8,128)(2,1)S(1)}, u32[]{:S(2)}, u32[]{:S(2)}) collective-permute-start(bf16[1,128,384]{2,1,0:T(8,128)(2,1)S(1)} %get-tuple-element.106), channel_id=1, source_target_pairs={{0,4},{1,5},{2,6},{3,7},{4,0},{5,1},{6,2},{7,3},{8,12},{9,13},{10,... | collective-permute-start | bytes 294920 | tf_op jit(solution)/shard_map/ppermute | solution.py:534
  68.8 1.2 %conv_grad_second.1 = (f32[1,160,384]{2,1,0:T(8,128)S(1)}, f32[1,160,384]{2,1,0:T(8,128)S(1)}, bf16[1,288,384]{2,1,0:T(8,128)(2,1)S(1)}, bf16[1,160,384]{2,1,0:T(8,128)(2,1)S(1)}) custom-call(bf16[512,1024]{1,0:T(8,128)(2,1)S(1)} %get-tuple-element.86.refs_0_, bf16[192,512]{1,0:T(8,128)(2,1)S(1)} %get-tuple-element.87.refs_0_.refs_1_, ...), custom_call_target="tpu_custom_call" | custom-call | flops 402653184 | bytes 2965504 | tf_op jit(solution)/shard_map/conv_grad_second/pallas_call | solution.py:37
  70.0 1.4 %collective-permute-start.27 = (bf16[1,160,384]{2,1,0:T(8,128)(2,1)S(1)}, bf16[1,160,384]{2,1,0:T(8,128)(2,1)S(1)}, u32[]{:S(2)}, u32[]{:S(2)}) collective-permute-start(bf16[1,160,384]{2,1,0:T(8,128)(2,1)S(1)} %get-tuple-element.103), channel_id=1, source_target_pairs={{0,4},{1,5},{2,6},{3,7},{4,0},{5,1},{6,2},{7,3},{8,12},{9,13},{10,... | collective-permute-start | bytes 368648 | tf_op jit(solution)/shard_map/ppermute | solution.py:534
  71.4 1.8 %collective-permute-start.28 = (bf16[1,48,1024]{2,1,0:T(8,128)(2,1)S(1)}, bf16[1,48,1024]{2,1,0:T(8,128)(2,1)S(1)}, u32[]{:S(2)}, u32[]{:S(2)}) collective-permute-start(bf16[1,48,1024]{2,1,0:T(8,128)(2,1)S(1)} %get-tuple-element.104), channel_id=1, source_target_pairs={{0,8},{1,9},{2,10},{3,11},{4,12},{5,13},{6,14},{7,15},{8,0},{9,1},... | collective-permute-start | bytes 294920 | tf_op jit(solution)/shard_map/ppermute | solution.py:534
  73.2 2.0 %collective-permute-start.30 = (bf16[1,128,384]{2,1,0:T(8,128)(2,1)S(1)}, bf16[1,128,384]{2,1,0:T(8,128)(2,1)S(1)}, u32[]{:S(2)}, u32[]{:S(2)}) collective-permute-start(bf16[1,128,384]{2,1,0:T(8,128)(2,1)S(1)} %conv_send_on.3), channel_id=1, source_target_pairs={{0,8},{1,9},{2,10},{3,11},{4,12},{5,13},{6,14},{7,15},{8,0},{9,1},... | collective-permute-start | bytes 294920 | tf_op jit(solution)/shard_map/ppermute | solution.py:534
  75.8 2.4 %collective-permute-done.27.refs_1_ = bf16[1,160,384]{2,1,0:T(8,128)(2,1)S(1)} collective-permute-done((bf16[1,160,384]{2,1,0:T(8,128)(2,1)S(1)}, bf16[1,160,384]{2,1,0:T(8,128)(2,1)S(1)}, u32[]{:S(2)}, u32[]{:S(2)}) %collective-permute-start.27) | collective-permute-done | bytes 122912 | tf_op jit(solution)/shard_map/ppermute | solution.py:534
  78.9 5.0 %collective-permute-done.30.refs_6_.refs_2_ = bf16[1,128,384]{2,1,0:T(8,128)(2,1)S(1)} collective-permute-done((bf16[1,128,384]{2,1,0:T(8,128)(2,1)S(1)}, bf16[1,128,384]{2,1,0:T(8,128)(2,1)S(1)}, u32[]{:S(2)}, u32[]{:S(2)}) %collective-permute-start.30) | collective-permute-done | bytes 98336 | tf_op jit(solution)/shard_map/ppermute | solution.py:534
  83.9 2.1 %input_grad.1 = bf16[256,384]{1,0:T(8,128)(2,1)} custom-call(bf16[256,384]{1,0:T(8,128)(2,1)S(1)} %bitcast.10, bf16[144,384]{1,0:T(8,128)(2,1)S(1)} %get-tuple-element.92.refs_1_, bf16[256,384]{1,0:T(8,128)(2,1)S(1)} %get-tuple-element.91.refs_2_, bf16[144,384]{1,0:T(8,128)(2,1)S(1)} %collective-permute-done.20.refs_3_, ...), custom_call_target="tpu_custom_call" | custom-call | flops 7549747200 | bytes 4153344 | tf_op jit(solution)/shard_map/input_grad/pallas_call | solution.py:37
  85.9 1.1 %collective-permute-done.31.refs_1_.refs_2_ = bf16[1,288,384]{2,1,0:T(8,128)(2,1)S(1)} collective-permute-done((bf16[1,288,384]{2,1,0:T(8,128)(2,1)S(1)}, bf16[1,288,384]{2,1,0:T(8,128)(2,1)S(1)}, u32[]{:S(2)}, u32[]{:S(2)}) %collective-permute-start.31) | collective-permute-done | bytes 221216 | tf_op jit(solution)/shard_map/ppermute | solution.py:534
  (69 shorter events, 15.7 us)
Async XLA Ops:
  1.8 4.8 %collective-permute-start = (bf16[32,384]{1,0:T(8,128)(2,1)S(1)}, bf16[32,384]{1,0:T(8,128)(2,1)S(1)}, u32[]{:S(2)}, u32[]{:S(2)}) collective-permute-start(bf16[32,384]{1,0:T(8,128)(2,1)S(1)} %get-tuple-element.62), channel_id=1, source_target_pairs={{0,2},{1,3},{2,0},{3,1},{4,6},{5,7},{6,4},{7,5},{8,10},{9,11},{10,... | collective-permute-start | bytes 73736 | tf_op jit(solution)/shard_map/ppermute | solution.py:534
  4.8 1.8 %collective-permute-start.1 = (bf16[32,384]{1,0:T(8,128)(2,1)S(1)}, bf16[32,384]{1,0:T(8,128)(2,1)S(1)}, u32[]{:S(2)}, u32[]{:S(2)}) collective-permute-start(bf16[32,384]{1,0:T(8,128)(2,1)S(1)} %get-tuple-element.62), channel_id=1, source_target_pairs={{2,4},{6,8},{10,12},{4,2},{8,6},{12,10},{3,5},{7,9},{11,13},{5,3},... | collective-permute-start | bytes 73736 | tf_op jit(solution)/shard_map/ppermute | solution.py:565
  8.5 12.2 %collective-permute-start.2 = (bf16[320,128]{1,0:T(8,128)(2,1)S(1)}, bf16[320,128]{1,0:T(8,128)(2,1)S(1)}, u32[]{:S(2)}, u32[]{:S(2)}) collective-permute-start(bf16[320,128]{1,0:T(8,128)(2,1)S(1)} %get-tuple-element.65.refs_2_), channel_id=1, source_target_pairs={{0,8},{1,9},{2,10},{3,11},{4,12},{5,13},{6,14},{7,15},{8,0},{9,1},... | collective-permute-start | bytes 245768 | tf_op jit(solution)/shard_map/ppermute | solution.py:534
  15.9 6.4 %collective-permute-start.3 = (bf16[320,128]{1,0:T(8,128)(2,1)S(1)}, bf16[320,128]{1,0:T(8,128)(2,1)S(1)}, u32[]{:S(2)}, u32[]{:S(2)}) collective-permute-start(bf16[320,128]{1,0:T(8,128)(2,1)S(1)} %get-tuple-element.65.refs_2_), channel_id=1, source_target_pairs={{0,12},{1,13},{2,14},{3,15},{4,8},{5,9},{6,10},{7,11},{8,4},{9,5},... | collective-permute-start | bytes 245768 | tf_op jit(solution)/shard_map/ppermute | solution.py:534
  17.3 5.7 %collective-permute-start.4 = (bf16[320,128]{1,0:T(8,128)(2,1)S(1)}, bf16[320,128]{1,0:T(8,128)(2,1)S(1)}, u32[]{:S(2)}, u32[]{:S(2)}) collective-permute-start(bf16[320,128]{1,0:T(8,128)(2,1)S(1)} %get-tuple-element.65.refs_2_), channel_id=1, source_target_pairs={{0,4},{1,5},{2,6},{3,7},{4,0},{5,1},{6,2},{7,3},{8,12},{9,13},{10,... | collective-permute-start | bytes 245768 | tf_op jit(solution)/shard_map/ppermute | solution.py:534
  17.5 7.6 %collective-permute-start.5 = (bf16[320,128]{1,0:T(8,128)(2,1)S(1)}, bf16[320,128]{1,0:T(8,128)(2,1)S(1)}, u32[]{:S(2)}, u32[]{:S(2)}) collective-permute-start(bf16[320,128]{1,0:T(8,128)(2,1)S(1)} %get-tuple-element.65.refs_2_), channel_id=1, source_target_pairs={{0,2},{1,3},{2,0},{3,1},{4,6},{5,7},{6,4},{7,5},{8,10},{9,11},{10,... | collective-permute-start | bytes 245768 | tf_op jit(solution)/shard_map/ppermute | solution.py:534
  20.7 4.6 %collective-permute-start.6 = (bf16[320,128]{1,0:T(8,128)(2,1)S(1)}, bf16[320,128]{1,0:T(8,128)(2,1)S(1)}, u32[]{:S(2)}, u32[]{:S(2)}) collective-permute-start(bf16[320,128]{1,0:T(8,128)(2,1)S(1)} %collective-permute-done.2.refs_3_), channel_id=1, source_target_pairs={{0,2},{1,3},{2,0},{3,1},{4,6},{5,7},{6,4},{7,5},{8,10},{9,11},{10,... | collective-permute-start | bytes 245768 | tf_op jit(solution)/shard_map/ppermute | solution.py:534
  22.3 4.4 %collective-permute-start.7 = (bf16[320,128]{1,0:T(8,128)(2,1)S(1)}, bf16[320,128]{1,0:T(8,128)(2,1)S(1)}, u32[]{:S(2)}, u32[]{:S(2)}) collective-permute-start(bf16[320,128]{1,0:T(8,128)(2,1)S(1)} %collective-permute-done.3.refs_4_), channel_id=1, source_target_pairs={{0,2},{1,3},{2,0},{3,1},{4,6},{5,7},{6,4},{7,5},{8,10},{9,11},{10,... | collective-permute-start | bytes 245768 | tf_op jit(solution)/shard_map/ppermute | solution.py:534
  23.0 5.1 %collective-permute-start.8 = (bf16[320,128]{1,0:T(8,128)(2,1)S(1)}, bf16[320,128]{1,0:T(8,128)(2,1)S(1)}, u32[]{:S(2)}, u32[]{:S(2)}) collective-permute-start(bf16[320,128]{1,0:T(8,128)(2,1)S(1)} %collective-permute-done.4.refs_5_), channel_id=1, source_target_pairs={{0,2},{1,3},{2,0},{3,1},{4,6},{5,7},{6,4},{7,5},{8,10},{9,11},{10,... | collective-permute-start | bytes 245768 | tf_op jit(solution)/shard_map/ppermute | solution.py:534
  28.1 13.1 %collective-permute-start.14 = (bf16[416,384]{1,0:T(8,128)(2,1)S(1)}, bf16[416,384]{1,0:T(8,128)(2,1)S(1)}, u32[]{:S(2)}, u32[]{:S(2)}) collective-permute-start(bf16[416,384]{1,0:T(8,128)(2,1)S(1)} %get-tuple-element.84), channel_id=1, source_target_pairs={{0,2},{1,3},{2,0},{3,1},{4,6},{5,7},{6,4},{7,5},{8,10},{9,11},{10,... | collective-permute-start | bytes 958472 | tf_op jit(solution)/shard_map/ppermute | solution.py:534
  34.8 5.3 %collective-permute-start.9 = (bf16[4,160,128]{2,1,0:T(8,128)(2,1)S(1)}, bf16[4,160,128]{2,1,0:T(8,128)(2,1)S(1)}, u32[]{:S(2)}, u32[]{:S(2)}) collective-permute-start(bf16[4,160,128]{2,1,0:T(8,128)(2,1)S(1)} %get-tuple-element.70), channel_id=1, source_target_pairs={{0,2},{1,3},{2,0},{3,1},{4,6},{5,7},{6,4},{7,5},{8,10},{9,11},{10,... | collective-permute-start | bytes 491528 | tf_op jit(solution)/shard_map/ppermute | solution.py:534
  35.8 5.3 %collective-permute-start.10 = (bf16[4,160,128]{2,1,0:T(8,128)(2,1)S(1)}, bf16[4,160,128]{2,1,0:T(8,128)(2,1)S(1)}, u32[]{:S(2)}, u32[]{:S(2)}) collective-permute-start(bf16[4,160,128]{2,1,0:T(8,128)(2,1)S(1)} %get-tuple-element.72), channel_id=1, source_target_pairs={{0,4},{1,5},{2,6},{3,7},{4,0},{5,1},{6,2},{7,3},{8,12},{9,13},{10,... | collective-permute-start | bytes 491528 | tf_op jit(solution)/shard_map/ppermute | solution.py:534
  41.2 11.6 %collective-permute-start.15 = (bf16[416,384]{1,0:T(8,128)(2,1)S(1)}, bf16[416,384]{1,0:T(8,128)(2,1)S(1)}, u32[]{:S(2)}, u32[]{:S(2)}) collective-permute-start(bf16[416,384]{1,0:T(8,128)(2,1)S(1)} %collective-permute-done.14.refs_3_), channel_id=1, source_target_pairs={{0,1},{1,0},{2,3},{3,2},{4,5},{5,4},{6,7},{7,6},{8,9},{9,8},{10,11... | collective-permute-start | bytes 958472 | tf_op jit(solution)/shard_map/ppermute | solution.py:534
  41.3 11.5 %collective-permute-start.13 = (bf16[352,384]{1,0:T(8,128)(2,1)S(1)}, bf16[352,384]{1,0:T(8,128)(2,1)S(1)}, u32[]{:S(2)}, u32[]{:S(2)}) collective-permute-start(bf16[352,384]{1,0:T(8,128)(2,1)S(1)} %get-tuple-element.82), channel_id=1, source_target_pairs={{0,1},{1,0},{2,3},{3,2},{4,5},{5,4},{6,7},{7,6},{8,9},{9,8},{10,11... | collective-permute-start | bytes 811016 | tf_op jit(solution)/shard_map/ppermute | solution.py:534
  41.8 4.4 %collective-permute-start.11 = (bf16[2,160,128]{2,1,0:T(8,128)(2,1)S(1)}, bf16[2,160,128]{2,1,0:T(8,128)(2,1)S(1)}, u32[]{:S(2)}, u32[]{:S(2)}) collective-permute-start(bf16[2,160,128]{2,1,0:T(8,128)(2,1)S(1)} %get-tuple-element.75), channel_id=1, source_target_pairs={{0,4},{1,5},{2,6},{3,7},{4,0},{5,1},{6,2},{7,3},{8,12},{9,13},{10,... | collective-permute-start | bytes 245768 | tf_op jit(solution)/shard_map/ppermute | solution.py:534
  43.0 4.4 %collective-permute-start.12 = (bf16[2,160,128]{2,1,0:T(8,128)(2,1)S(1)}, bf16[2,160,128]{2,1,0:T(8,128)(2,1)S(1)}, u32[]{:S(2)}, u32[]{:S(2)}) collective-permute-start(bf16[2,160,128]{2,1,0:T(8,128)(2,1)S(1)} %get-tuple-element.77), channel_id=1, source_target_pairs={{0,2},{1,3},{2,0},{3,1},{4,6},{5,7},{6,4},{7,5},{8,10},{9,11},{10,... | collective-permute-start | bytes 245768 | tf_op jit(solution)/shard_map/ppermute | solution.py:534
  47.5 10.1 %collective-permute-start.22 = (bf16[128,1024]{1,0:T(8,128)(2,1)S(1)}, bf16[128,1024]{1,0:T(8,128)(2,1)S(1)}, u32[]{:S(2)}, u32[]{:S(2)}) collective-permute-start(bf16[128,1024]{1,0:T(8,128)(2,1)S(1)} %get-tuple-element.93.refs_0_.refs_1_), channel_id=1, source_target_pairs={{0,2},{1,3},{2,0},{3,1},{4,6},{5,7},{6,4},{7,5},{8,10},{9,11},{10,... | collective-permute-start | bytes 786440 | tf_op jit(solution)/shard_map/ppermute | solution.py:534
  48.0 10.0 %collective-permute-start.21 = (bf16[128,1024]{1,0:T(8,128)(2,1)S(1)}, bf16[128,1024]{1,0:T(8,128)(2,1)S(1)}, u32[]{:S(2)}, u32[]{:S(2)}) collective-permute-start(bf16[128,1024]{1,0:T(8,128)(2,1)S(1)} %get-tuple-element.93.refs_0_.refs_1_), channel_id=1, source_target_pairs={{0,1},{1,0},{2,3},{3,2},{4,5},{5,4},{6,7},{7,6},{8,9},{9,8},{10,11... | collective-permute-start | bytes 786440 | tf_op jit(solution)/shard_map/ppermute | solution.py:534
  48.0 9.1 %collective-permute-start.16 = (bf16[1,320,128]{2,1,0:T(8,128)(2,1)S(1)}, bf16[1,320,128]{2,1,0:T(8,128)(2,1)S(1)}, u32[]{:S(2)}, u32[]{:S(2)}) collective-permute-start(bf16[1,320,128]{2,1,0:T(8,128)(2,1)S(1)} %get-tuple-element.88), channel_id=1, source_target_pairs={{0,8},{1,9},{2,10},{3,11},{4,12},{5,13},{6,14},{7,15},{8,0},{9,1},... | collective-permute-start | bytes 245768 | tf_op jit(solution)/shard_map/ppermute | solution.py:534
  57.6 1.6 %collective-permute-start.23 = (bf16[128,1024]{1,0:T(8,128)(2,1)S(1)}, bf16[128,1024]{1,0:T(8,128)(2,1)S(1)}, u32[]{:S(2)}, u32[]{:S(2)}) collective-permute-start(bf16[128,1024]{1,0:T(8,128)(2,1)S(1)} %collective-permute-done.22.refs_3_), channel_id=1, source_target_pairs={{0,1},{1,0},{2,3},{3,2},{4,5},{5,4},{6,7},{7,6},{8,9},{9,8},{10,11... | collective-permute-start | bytes 786440 | tf_op jit(solution)/shard_map/ppermute | solution.py:534
  57.7 5.6 %collective-permute-start.20 = (bf16[144,384]{1,0:T(8,128)(2,1)S(1)}, bf16[144,384]{1,0:T(8,128)(2,1)S(1)}, u32[]{:S(2)}, u32[]{:S(2)}) collective-permute-start(bf16[144,384]{1,0:T(8,128)(2,1)S(1)} %get-tuple-element.92.refs_1_), channel_id=1, source_target_pairs={{0,2},{1,3},{2,0},{3,1},{4,6},{5,7},{6,4},{7,5},{8,10},{9,11},{10,... | collective-permute-start | bytes 331784 | tf_op jit(solution)/shard_map/ppermute | solution.py:534
  60.0 7.0 %collective-permute-start.25 = (bf16[2,48,1024]{2,1,0:T(8,128)(2,1)S(1)}, bf16[2,48,1024]{2,1,0:T(8,128)(2,1)S(1)}, u32[]{:S(2)}, u32[]{:S(2)}) collective-permute-start(bf16[2,48,1024]{2,1,0:T(8,128)(2,1)S(1)} %get-tuple-element.98), channel_id=1, source_target_pairs={{0,4},{1,5},{2,6},{3,7},{4,0},{5,1},{6,2},{7,3},{8,12},{9,13},{10,... | collective-permute-start | bytes 589832 | tf_op jit(solution)/shard_map/ppermute | solution.py:534
  60.1 7.3 %collective-permute-start.18 = (bf16[256,384]{1,0:T(8,128)(2,1)S(1)}, bf16[256,384]{1,0:T(8,128)(2,1)S(1)}, u32[]{:S(2)}, u32[]{:S(2)}) collective-permute-start(bf16[256,384]{1,0:T(8,128)(2,1)S(1)} %get-tuple-element.91.refs_2_), channel_id=1, source_target_pairs={{0,2},{1,3},{2,0},{3,1},{4,6},{5,7},{6,4},{7,5},{8,10},{9,11},{10,... | collective-permute-start | bytes 589832 | tf_op jit(solution)/shard_map/ppermute | solution.py:534
  60.7 3.1 %collective-permute-start.19 = (bf16[144,384]{1,0:T(8,128)(2,1)S(1)}, bf16[144,384]{1,0:T(8,128)(2,1)S(1)}, u32[]{:S(2)}, u32[]{:S(2)}) collective-permute-start(bf16[144,384]{1,0:T(8,128)(2,1)S(1)} %get-tuple-element.92.refs_1_), channel_id=1, source_target_pairs={{0,1},{1,0},{2,3},{3,2},{4,5},{5,4},{6,7},{7,6},{8,9},{9,8},{10,11... | collective-permute-start | bytes 331784 | tf_op jit(solution)/shard_map/ppermute | solution.py:534
  63.3 5.4 %collective-permute-start.17 = (bf16[256,384]{1,0:T(8,128)(2,1)S(1)}, bf16[256,384]{1,0:T(8,128)(2,1)S(1)}, u32[]{:S(2)}, u32[]{:S(2)}) collective-permute-start(bf16[256,384]{1,0:T(8,128)(2,1)S(1)} %get-tuple-element.91.refs_2_), channel_id=1, source_target_pairs={{0,1},{1,0},{2,3},{3,2},{4,5},{5,4},{6,7},{7,6},{8,9},{9,8},{10,11... | collective-permute-start | bytes 589832 | tf_op jit(solution)/shard_map/ppermute | solution.py:534
  67.3 1.4 %collective-permute-start.26 = (bf16[256,384]{1,0:T(8,128)(2,1)S(1)}, bf16[256,384]{1,0:T(8,128)(2,1)S(1)}, u32[]{:S(2)}, u32[]{:S(2)}) collective-permute-start(bf16[256,384]{1,0:T(8,128)(2,1)S(1)} %collective-permute-done.18.refs_4_), channel_id=1, source_target_pairs={{0,1},{1,0},{2,3},{3,2},{4,5},{5,4},{6,7},{7,6},{8,9},{9,8},{10,11... | collective-permute-start | bytes 589832 | tf_op jit(solution)/shard_map/ppermute | solution.py:534
  67.3 5.9 %collective-permute-start.29 = (bf16[1,128,384]{2,1,0:T(8,128)(2,1)S(1)}, bf16[1,128,384]{2,1,0:T(8,128)(2,1)S(1)}, u32[]{:S(2)}, u32[]{:S(2)}) collective-permute-start(bf16[1,128,384]{2,1,0:T(8,128)(2,1)S(1)} %get-tuple-element.106), channel_id=1, source_target_pairs={{0,4},{1,5},{2,6},{3,7},{4,0},{5,1},{6,2},{7,3},{8,12},{9,13},{10,... | collective-permute-start | bytes 294920 | tf_op jit(solution)/shard_map/ppermute | solution.py:534
  70.0 8.2 %collective-permute-start.27 = (bf16[1,160,384]{2,1,0:T(8,128)(2,1)S(1)}, bf16[1,160,384]{2,1,0:T(8,128)(2,1)S(1)}, u32[]{:S(2)}, u32[]{:S(2)}) collective-permute-start(bf16[1,160,384]{2,1,0:T(8,128)(2,1)S(1)} %get-tuple-element.103), channel_id=1, source_target_pairs={{0,4},{1,5},{2,6},{3,7},{4,0},{5,1},{6,2},{7,3},{8,12},{9,13},{10,... | collective-permute-start | bytes 368648 | tf_op jit(solution)/shard_map/ppermute | solution.py:534
  71.4 7.5 %collective-permute-start.28 = (bf16[1,48,1024]{2,1,0:T(8,128)(2,1)S(1)}, bf16[1,48,1024]{2,1,0:T(8,128)(2,1)S(1)}, u32[]{:S(2)}, u32[]{:S(2)}) collective-permute-start(bf16[1,48,1024]{2,1,0:T(8,128)(2,1)S(1)} %get-tuple-element.104), channel_id=1, source_target_pairs={{0,8},{1,9},{2,10},{3,11},{4,12},{5,13},{6,14},{7,15},{8,0},{9,1},... | collective-permute-start | bytes 294920 | tf_op jit(solution)/shard_map/ppermute | solution.py:534
  73.2 10.6 %collective-permute-start.30 = (bf16[1,128,384]{2,1,0:T(8,128)(2,1)S(1)}, bf16[1,128,384]{2,1,0:T(8,128)(2,1)S(1)}, u32[]{:S(2)}, u32[]{:S(2)}) collective-permute-start(bf16[1,128,384]{2,1,0:T(8,128)(2,1)S(1)} %conv_send_on.3), channel_id=1, source_target_pairs={{0,8},{1,9},{2,10},{3,11},{4,12},{5,13},{6,14},{7,15},{8,0},{9,1},... | collective-permute-start | bytes 294920 | tf_op jit(solution)/shard_map/ppermute | solution.py:534
  75.2 11.8 %collective-permute-start.31 = (bf16[1,288,384]{2,1,0:T(8,128)(2,1)S(1)}, bf16[1,288,384]{2,1,0:T(8,128)(2,1)S(1)}, u32[]{:S(2)}, u32[]{:S(2)}) collective-permute-start(bf16[1,288,384]{2,1,0:T(8,128)(2,1)S(1)} %get-tuple-element.108), channel_id=1, source_target_pairs={{0,4},{1,5},{2,6},{3,7},{4,0},{5,1},{6,2},{7,3},{8,12},{9,13},{10,... | collective-permute-start | bytes 663560 | tf_op jit(solution)/shard_map/ppermute | solution.py:534
  78.2 8.8 %collective-permute-start.32 = (bf16[1,160,384]{2,1,0:T(8,128)(2,1)S(1)}, bf16[1,160,384]{2,1,0:T(8,128)(2,1)S(1)}, u32[]{:S(2)}, u32[]{:S(2)}) collective-permute-start(bf16[1,160,384]{2,1,0:T(8,128)(2,1)S(1)} %conv_send_on.2), channel_id=1, source_target_pairs={{0,8},{1,9},{2,10},{3,11},{4,12},{5,13},{6,14},{7,15},{8,0},{9,1},... | collective-permute-start | bytes 368648 | tf_op jit(solution)/shard_map/ppermute | solution.py:534
  (9 other events, 91.1 us)

commit v16 on v15

--- a/solution.py
+++ b/solution.py
@@ -668,7 +668,7 @@
         name="select",
     )
     query_cot = held(query_cot, keep)
-    query_near, query_core = swap(query_cot, 1), swap(query_cot, 0, 1)
+    query_near, query_core = swap(query_cot, 1), swap(held(query_cot, conv_pick), 0, 1)
     kv_cot = halved(keep, send, bits[2:], "kv_cot_fold")
     first, second, *edge = run(
         middle_kernel,

time: 88.1 us -> 86.7 us (0.984)
  waiting for transfers between devices: 32.2 us -> 29.5 us
  starting transfers between devices: 36.1 us -> 37.4 us
    ppermute x32, waiting for transfers between devices: 32.2 us -> 29.5 us  [swap(): lax.ppermute(value, both_axes, [(i, i ^ mask) for i in range(owners)])]
    ppermute x32, starting transfers between devices: 35.4 us -> 36.8 us  [swap(): lax.ppermute(value, both_axes, [(i, i ^ mask) for i in range(owners)])]
  transfers between devices with their start and end apart: 33 -> 33, of which waited for: 19 -> 20; matrix products, arithmetic and copies ran while one was open for 0% -> 0% of each run, Pallas kernels for 17% -> 17%
where the time goes in v16:
time: 86.7 us; the launch traced here: 86.5 us
  starting transfers between devices  37.4 us (43%)
  waiting for transfers between devices  29.5 us (34%)
  Pallas kernels  17.8 us (21%)
  local copies, waits for them, and re-layouts  0.96 us (1%)
    ppermute x32, starting transfers between devices, swap(): lax.ppermute(value, both_axes, [(i, i ^ mask) for i in range(owners)])  36.8 us
    ppermute x32, waiting for transfers between devices, swap(): lax.ppermute(value, both_axes, [(i, i ^ mask) for i in range(owners)])  29.5 us
    pallas_call x18, Pallas kernels, run(): pl.pallas_call(whole, out_shape=[jax.ShapeDtypeStruct(s, t) for s, t in o...  17.8 us
  transfers between devices with their start and end apart: 33, of which 20 were waited for; matrix products, arithmetic and copies ran while one was open for 0% of the time, Pallas kernels for 17%

profile of v16, /device:TPU:0, one launch (start us, length us, event | category | flops | bytes accessed | tf_op | source)
XLA Modules:
  0.0 86.5 jit_solution(17082823755648456753)
XLA Ops:
  1.8 3.0 %collective-permute-start = (bf16[32,384]{1,0:T(8,128)(2,1)S(1)}, bf16[32,384]{1,0:T(8,128)(2,1)S(1)}, u32[]{:S(2)}, u32[]{:S(2)}) collective-permute-start(bf16[32,384]{1,0:T(8,128)(2,1)S(1)} %get-tuple-element.63), channel_id=1, source_target_pairs={{0,2},{1,3},{2,0},{3,1},{4,6},{5,7},{6,4},{7,5},{8,10},{9,11},{10,... | collective-permute-start | bytes 73736 | tf_op jit(solution)/shard_map/ppermute | solution.py:534
  5.5 1.1 %collective-permute-done.refs_1_ = bf16[32,384]{1,0:T(8,128)(2,1)S(1)} collective-permute-done((bf16[32,384]{1,0:T(8,128)(2,1)S(1)}, bf16[32,384]{1,0:T(8,128)(2,1)S(1)}, u32[]{:S(2)}, u32[]{:S(2)}) %collective-permute-start) | collective-permute-done | bytes 24608 | tf_op jit(solution)/shard_map/ppermute | solution.py:534
  6.6 1.9 %front.1 = (bf16[320,128]{1,0:T(8,128)(2,1)S(1)}, bf16[288,384]{1,0:T(8,128)(2,1)S(1)}, bf16[128,768]{1,0:T(8,128)(2,1)S(1)}, f32[128,768]{1,0:T(8,128)S(1)}) custom-call(f32[3,304,128]{2,1,0:T(8,128)S(1)} %get-tuple-element.62.refs_0_, bf16[32,384]{1,0:T(8,128)(2,1)S(1)} %collective-permute-done.refs_1_, ...), custom_call_target="tpu_custom_call" | custom-call | flops 754974720 | bytes 4852736 | tf_op jit(solution)/shard_map/front/pallas_call | solution.py:37
  8.5 7.4 %collective-permute-start.2 = (bf16[320,128]{1,0:T(8,128)(2,1)S(1)}, bf16[320,128]{1,0:T(8,128)(2,1)S(1)}, u32[]{:S(2)}, u32[]{:S(2)}) collective-permute-start(bf16[320,128]{1,0:T(8,128)(2,1)S(1)} %get-tuple-element.66.refs_2_), channel_id=1, source_target_pairs={{0,8},{1,9},{2,10},{3,11},{4,12},{5,13},{6,14},{7,15},{8,0},{9,1},... | collective-permute-start | bytes 245768 | tf_op jit(solution)/shard_map/ppermute | solution.py:534
  15.9 1.3 %collective-permute-start.3 = (bf16[320,128]{1,0:T(8,128)(2,1)S(1)}, bf16[320,128]{1,0:T(8,128)(2,1)S(1)}, u32[]{:S(2)}, u32[]{:S(2)}) collective-permute-start(bf16[320,128]{1,0:T(8,128)(2,1)S(1)} %get-tuple-element.66.refs_2_), channel_id=1, source_target_pairs={{0,12},{1,13},{2,14},{3,15},{4,8},{5,9},{6,10},{7,11},{8,4},{9,5},... | collective-permute-start | bytes 245768 | tf_op jit(solution)/shard_map/ppermute | solution.py:534
  17.9 2.7 %collective-permute-done.2.refs_3_ = bf16[320,128]{1,0:T(8,128)(2,1)S(1)} collective-permute-done((bf16[320,128]{1,0:T(8,128)(2,1)S(1)}, bf16[320,128]{1,0:T(8,128)(2,1)S(1)}, u32[]{:S(2)}, u32[]{:S(2)}) %collective-permute-start.2) | collective-permute-done | bytes 81952 | tf_op jit(solution)/shard_map/ppermute | solution.py:534
  21.2 1.1 %collective-permute-done.3.refs_4_ = bf16[320,128]{1,0:T(8,128)(2,1)S(1)} collective-permute-done((bf16[320,128]{1,0:T(8,128)(2,1)S(1)}, bf16[320,128]{1,0:T(8,128)(2,1)S(1)}, u32[]{:S(2)}, u32[]{:S(2)}) %collective-permute-start.3) | collective-permute-done | bytes 81952 | tf_op jit(solution)/shard_map/ppermute | solution.py:534
  23.0 1.4 %collective-permute-start.8 = (bf16[320,128]{1,0:T(8,128)(2,1)S(1)}, bf16[320,128]{1,0:T(8,128)(2,1)S(1)}, u32[]{:S(2)}, u32[]{:S(2)}) collective-permute-start(bf16[320,128]{1,0:T(8,128)(2,1)S(1)} %collective-permute-done.4.refs_5_), channel_id=1, source_target_pairs={{0,2},{1,3},{2,0},{3,1},{4,6},{5,7},{6,4},{7,5},{8,10},{9,11},{10,... | collective-permute-start | bytes 245768 | tf_op jit(solution)/shard_map/ppermute | solution.py:534
  25.2 1.5 %collective-permute-done.7.refs_8_ = bf16[320,128]{1,0:T(8,128)(2,1)S(1)} collective-permute-done((bf16[320,128]{1,0:T(8,128)(2,1)S(1)}, bf16[320,128]{1,0:T(8,128)(2,1)S(1)}, u32[]{:S(2)}, u32[]{:S(2)}) %collective-permute-start.7) | collective-permute-done | bytes 81952 | tf_op jit(solution)/shard_map/ppermute | solution.py:534
  26.8 1.3 %collective-permute-done.8.refs_9_ = bf16[320,128]{1,0:T(8,128)(2,1)S(1)} collective-permute-done((bf16[320,128]{1,0:T(8,128)(2,1)S(1)}, bf16[320,128]{1,0:T(8,128)(2,1)S(1)}, u32[]{:S(2)}, u32[]{:S(2)}) %collective-permute-start.8) | collective-permute-done | bytes 81952 | tf_op jit(solution)/shard_map/ppermute | solution.py:534
  28.1 1.0 %collective-permute-start.14 = (bf16[416,384]{1,0:T(8,128)(2,1)S(1)}, bf16[416,384]{1,0:T(8,128)(2,1)S(1)}, u32[]{:S(2)}, u32[]{:S(2)}) collective-permute-start(bf16[416,384]{1,0:T(8,128)(2,1)S(1)} %get-tuple-element.85), channel_id=1, source_target_pairs={{0,2},{1,3},{2,0},{3,1},{4,6},{5,7},{6,4},{7,5},{8,10},{9,11},{10,... | collective-permute-start | bytes 958472 | tf_op jit(solution)/shard_map/ppermute | solution.py:534
  29.2 5.7 %attend.1 = (bf16[128,1536]{1,0:T(8,128)(2,1)}, bf16[128,1024]{1,0:T(8,128)(2,1)S(1)}, f32[4,160,128]{2,1,0:T(8,128)S(1)}, bf16[4,160,128]{2,1,0:T(8,128)(2,1)S(...) custom-call(bf16[128,1024]{1,0:T(8,128)(2,1)S(1)} %get-tuple-element.67.refs_0_, ...), custom_call_target="tpu_custom_call" | custom-call | flops 2013265920 | bytes 2949120 | tf_op jit(solution)/shard_map/attend/pallas_call | solution.py:37
  34.8 1.0 %collective-permute-start.9 = (bf16[4,160,128]{2,1,0:T(8,128)(2,1)S(1)}, bf16[4,160,128]{2,1,0:T(8,128)(2,1)S(1)}, u32[]{:S(2)}, u32[]{:S(2)}) collective-permute-start(bf16[4,160,128]{2,1,0:T(8,128)(2,1)S(1)} %get-tuple-element.71), channel_id=1, source_target_pairs={{0,2},{1,3},{2,0},{3,1},{4,6},{5,7},{6,4},{7,5},{8,10},{9,11},{10,... | collective-permute-start | bytes 491528 | tf_op jit(solution)/shard_map/ppermute | solution.py:534
  35.8 1.2 %collective-permute-start.10 = (bf16[4,160,128]{2,1,0:T(8,128)(2,1)S(1)}, bf16[4,160,128]{2,1,0:T(8,128)(2,1)S(1)}, u32[]{:S(2)}, u32[]{:S(2)}) collective-permute-start(bf16[4,160,128]{2,1,0:T(8,128)(2,1)S(1)} %get-tuple-element.73), channel_id=1, source_target_pairs={{0,4},{1,5},{2,6},{3,7},{4,0},{5,1},{6,2},{7,3},{8,12},{9,13},{10,... | collective-permute-start | bytes 491528 | tf_op jit(solution)/shard_map/ppermute | solution.py:534
  37.7 2.5 %collective-permute-done.9.refs_1_ = bf16[4,160,128]{2,1,0:T(8,128)(2,1)S(1)} collective-permute-done((bf16[4,160,128]{2,1,0:T(8,128)(2,1)S(1)}, bf16[4,160,128]{2,1,0:T(8,128)(2,1)S(1)}, u32[]{:S(2)}, u32[]{:S(2)}) %collective-permute-start.9) | collective-permute-done | bytes 163872 | tf_op jit(solution)/shard_map/ppermute | solution.py:534
  41.8 1.2 %collective-permute-start.11 = (bf16[2,160,128]{2,1,0:T(8,128)(2,1)S(1)}, bf16[2,160,128]{2,1,0:T(8,128)(2,1)S(1)}, u32[]{:S(2)}, u32[]{:S(2)}) collective-permute-start(bf16[2,160,128]{2,1,0:T(8,128)(2,1)S(1)} %get-tuple-element.76), channel_id=1, source_target_pairs={{0,4},{1,5},{2,6},{3,7},{4,0},{5,1},{6,2},{7,3},{8,12},{9,13},{10,... | collective-permute-start | bytes 245768 | tf_op jit(solution)/shard_map/ppermute | solution.py:534
  43.4 2.8 %collective-permute-done.11.refs_1_ = bf16[2,160,128]{2,1,0:T(8,128)(2,1)S(1)} collective-permute-done((bf16[2,160,128]{2,1,0:T(8,128)(2,1)S(1)}, bf16[2,160,128]{2,1,0:T(8,128)(2,1)S(1)}, u32[]{:S(2)}, u32[]{:S(2)}) %collective-permute-start.11) | collective-permute-done | bytes 81952 | tf_op jit(solution)/shard_map/ppermute | solution.py:534
  46.2 1.2 %collective-permute-done.12.refs_3_ = bf16[2,160,128]{2,1,0:T(8,128)(2,1)S(1)} collective-permute-done((bf16[2,160,128]{2,1,0:T(8,128)(2,1)S(1)}, bf16[2,160,128]{2,1,0:T(8,128)(2,1)S(1)}, u32[]{:S(2)}, u32[]{:S(2)}) %collective-permute-start.12) | collective-permute-done | bytes 81952 | tf_op jit(solution)/shard_map/ppermute | solution.py:534
  48.0 4.8 %collective-permute-start.16 = (bf16[1,320,128]{2,1,0:T(8,128)(2,1)S(1)}, bf16[1,320,128]{2,1,0:T(8,128)(2,1)S(1)}, u32[]{:S(2)}, u32[]{:S(2)}) collective-permute-start(bf16[1,320,128]{2,1,0:T(8,128)(2,1)S(1)} %get-tuple-element.89), channel_id=1, source_target_pairs={{0,8},{1,9},{2,10},{3,11},{4,12},{5,13},{6,14},{7,15},{8,0},{9,1},... | collective-permute-start | bytes 245768 | tf_op jit(solution)/shard_map/ppermute | solution.py:534
  52.8 2.4 %select.1 = (bf16[512,1024]{1,0:T(8,128)(2,1)S(1)}, bf16[192,512]{1,0:T(8,128)(2,1)S(1)}) custom-call(bf16[192,128]{1,0:T(8,128)(2,1)S(1)} %get-tuple-element.80.refs_0_, bf16[288,384]{1,0:T(8,128)(2,1)S(1)} %get-tuple-element.65.refs_2_.refs_1_, bf16[352,384]{1,0:T(8,128)(2,1)S(1)} %collective-permute-done.13.refs_2_, ...), custom_call_target="tpu_custom_call" | custom-call | flops 2013265920 | bytes 2424832 | tf_op jit(solution)/shard_map/select/pallas_call | solution.py:37
  59.4 2.2 %collective-permute-done.20.refs_3_ = bf16[144,384]{1,0:T(8,128)(2,1)S(1)} collective-permute-done((bf16[144,384]{1,0:T(8,128)(2,1)S(1)}, bf16[144,384]{1,0:T(8,128)(2,1)S(1)}, u32[]{:S(2)}, u32[]{:S(2)}) %collective-permute-start.20) | collective-permute-done | bytes 110624 | tf_op jit(solution)/shard_map/ppermute | solution.py:534
  63.6 2.0 %collective-permute-done.25.refs_1_ = bf16[2,48,1024]{2,1,0:T(8,128)(2,1)S(1)} collective-permute-done((bf16[2,48,1024]{2,1,0:T(8,128)(2,1)S(1)}, bf16[2,48,1024]{2,1,0:T(8,128)(2,1)S(1)}, u32[]{:S(2)}, u32[]{:S(2)}) %collective-permute-start.25) | collective-permute-done | bytes 196640 | tf_op jit(solution)/shard_map/ppermute | solution.py:534
  65.7 1.6 %collective-permute-start.29 = (bf16[1,128,384]{2,1,0:T(8,128)(2,1)S(1)}, bf16[1,128,384]{2,1,0:T(8,128)(2,1)S(1)}, u32[]{:S(2)}, u32[]{:S(2)}) collective-permute-start(bf16[1,128,384]{2,1,0:T(8,128)(2,1)S(1)} %get-tuple-element.108), channel_id=1, source_target_pairs={{0,4},{1,5},{2,6},{3,7},{4,0},{5,1},{6,2},{7,3},{8,12},{9,13},{10,... | collective-permute-start | bytes 294920 | tf_op jit(solution)/shard_map/ppermute | solution.py:534
  67.3 1.2 %conv_grad_second.1 = (f32[1,160,384]{2,1,0:T(8,128)S(1)}, f32[1,160,384]{2,1,0:T(8,128)S(1)}, bf16[1,288,384]{2,1,0:T(8,128)(2,1)S(1)}, bf16[1,160,384]{2,1,0:T(8,128)(2,1)S(1)}) custom-call(bf16[512,1024]{1,0:T(8,128)(2,1)S(1)} %get-tuple-element.87.refs_0_, bf16[192,512]{1,0:T(8,128)(2,1)S(1)} %get-tuple-element.88.refs_0_.refs_1_, ...), custom_call_target="tpu_custom_call" | custom-call | flops 402653184 | bytes 2965504 | tf_op jit(solution)/shard_map/conv_grad_second/pallas_call | solution.py:37
  68.5 1.4 %collective-permute-start.27 = (bf16[1,160,384]{2,1,0:T(8,128)(2,1)S(1)}, bf16[1,160,384]{2,1,0:T(8,128)(2,1)S(1)}, u32[]{:S(2)}, u32[]{:S(2)}) collective-permute-start(bf16[1,160,384]{2,1,0:T(8,128)(2,1)S(1)} %get-tuple-element.105), channel_id=1, source_target_pairs={{0,4},{1,5},{2,6},{3,7},{4,0},{5,1},{6,2},{7,3},{8,12},{9,13},{10,... | collective-permute-start | bytes 368648 | tf_op jit(solution)/shard_map/ppermute | solution.py:534
  70.0 2.5 %collective-permute-start.28 = (bf16[1,48,1024]{2,1,0:T(8,128)(2,1)S(1)}, bf16[1,48,1024]{2,1,0:T(8,128)(2,1)S(1)}, u32[]{:S(2)}, u32[]{:S(2)}) collective-permute-start(bf16[1,48,1024]{2,1,0:T(8,128)(2,1)S(1)} %get-tuple-element.106), channel_id=1, source_target_pairs={{0,8},{1,9},{2,10},{3,11},{4,12},{5,13},{6,14},{7,15},{8,0},{9,1},... | collective-permute-start | bytes 294920 | tf_op jit(solution)/shard_map/ppermute | solution.py:534
  72.5 1.2 %collective-permute-start.30 = (bf16[1,128,384]{2,1,0:T(8,128)(2,1)S(1)}, bf16[1,128,384]{2,1,0:T(8,128)(2,1)S(1)}, u32[]{:S(2)}, u32[]{:S(2)}) collective-permute-start(bf16[1,128,384]{2,1,0:T(8,128)(2,1)S(1)} %conv_send_on.3), channel_id=1, source_target_pairs={{0,8},{1,9},{2,10},{3,11},{4,12},{5,13},{6,14},{7,15},{8,0},{9,1},... | collective-permute-start | bytes 294920 | tf_op jit(solution)/shard_map/ppermute | solution.py:534
  73.7 1.4 %collective-permute-start.31 = (bf16[1,288,384]{2,1,0:T(8,128)(2,1)S(1)}, bf16[1,288,384]{2,1,0:T(8,128)(2,1)S(1)}, u32[]{:S(2)}, u32[]{:S(2)}) collective-permute-start(bf16[1,288,384]{2,1,0:T(8,128)(2,1)S(1)} %get-tuple-element.110), channel_id=1, source_target_pairs={{0,4},{1,5},{2,6},{3,7},{4,0},{5,1},{6,2},{7,3},{8,12},{9,13},{10,... | collective-permute-start | bytes 663560 | tf_op jit(solution)/shard_map/ppermute | solution.py:534
  75.1 1.8 %collective-permute-done.27.refs_1_ = bf16[1,160,384]{2,1,0:T(8,128)(2,1)S(1)} collective-permute-done((bf16[1,160,384]{2,1,0:T(8,128)(2,1)S(1)}, bf16[1,160,384]{2,1,0:T(8,128)(2,1)S(1)}, u32[]{:S(2)}, u32[]{:S(2)}) %collective-permute-start.27) | collective-permute-done | bytes 122912 | tf_op jit(solution)/shard_map/ppermute | solution.py:534
  77.6 4.9 %collective-permute-done.30.refs_6_.refs_2_ = bf16[1,128,384]{2,1,0:T(8,128)(2,1)S(1)} collective-permute-done((bf16[1,128,384]{2,1,0:T(8,128)(2,1)S(1)}, bf16[1,128,384]{2,1,0:T(8,128)(2,1)S(1)}, u32[]{:S(2)}, u32[]{:S(2)}) %collective-permute-start.30) | collective-permute-done | bytes 98336 | tf_op jit(solution)/shard_map/ppermute | solution.py:534
  82.5 2.1 %input_grad.1 = bf16[256,384]{1,0:T(8,128)(2,1)} custom-call(bf16[256,384]{1,0:T(8,128)(2,1)S(1)} %bitcast.10, bf16[144,384]{1,0:T(8,128)(2,1)S(1)} %get-tuple-element.93.refs_1_, bf16[256,384]{1,0:T(8,128)(2,1)S(1)} %get-tuple-element.92.refs_2_, bf16[144,384]{1,0:T(8,128)(2,1)S(1)} %collective-permute-done.20.refs_3_, ...), custom_call_target="tpu_custom_call" | custom-call | flops 7549747200 | bytes 4153344 | tf_op jit(solution)/shard_map/input_grad/pallas_call | solution.py:37
  84.5 1.1 %collective-permute-done.31.refs_1_.refs_2_ = bf16[1,288,384]{2,1,0:T(8,128)(2,1)S(1)} collective-permute-done((bf16[1,288,384]{2,1,0:T(8,128)(2,1)S(1)}, bf16[1,288,384]{2,1,0:T(8,128)(2,1)S(1)}, u32[]{:S(2)}, u32[]{:S(2)}) %collective-permute-start.31) | collective-permute-done | bytes 221216 | tf_op jit(solution)/shard_map/ppermute | solution.py:534
  (69 shorter events, 15.5 us)
Async XLA Ops:
  1.8 4.8 %collective-permute-start = (bf16[32,384]{1,0:T(8,128)(2,1)S(1)}, bf16[32,384]{1,0:T(8,128)(2,1)S(1)}, u32[]{:S(2)}, u32[]{:S(2)}) collective-permute-start(bf16[32,384]{1,0:T(8,128)(2,1)S(1)} %get-tuple-element.63), channel_id=1, source_target_pairs={{0,2},{1,3},{2,0},{3,1},{4,6},{5,7},{6,4},{7,5},{8,10},{9,11},{10,... | collective-permute-start | bytes 73736 | tf_op jit(solution)/shard_map/ppermute | solution.py:534
  4.8 1.8 %collective-permute-start.1 = (bf16[32,384]{1,0:T(8,128)(2,1)S(1)}, bf16[32,384]{1,0:T(8,128)(2,1)S(1)}, u32[]{:S(2)}, u32[]{:S(2)}) collective-permute-start(bf16[32,384]{1,0:T(8,128)(2,1)S(1)} %get-tuple-element.63), channel_id=1, source_target_pairs={{2,4},{6,8},{10,12},{4,2},{8,6},{12,10},{3,5},{7,9},{11,13},{5,3},... | collective-permute-start | bytes 73736 | tf_op jit(solution)/shard_map/ppermute | solution.py:565
  8.5 12.2 %collective-permute-start.2 = (bf16[320,128]{1,0:T(8,128)(2,1)S(1)}, bf16[320,128]{1,0:T(8,128)(2,1)S(1)}, u32[]{:S(2)}, u32[]{:S(2)}) collective-permute-start(bf16[320,128]{1,0:T(8,128)(2,1)S(1)} %get-tuple-element.66.refs_2_), channel_id=1, source_target_pairs={{0,8},{1,9},{2,10},{3,11},{4,12},{5,13},{6,14},{7,15},{8,0},{9,1},... | collective-permute-start | bytes 245768 | tf_op jit(solution)/shard_map/ppermute | solution.py:534
  15.9 6.4 %collective-permute-start.3 = (bf16[320,128]{1,0:T(8,128)(2,1)S(1)}, bf16[320,128]{1,0:T(8,128)(2,1)S(1)}, u32[]{:S(2)}, u32[]{:S(2)}) collective-permute-start(bf16[320,128]{1,0:T(8,128)(2,1)S(1)} %get-tuple-element.66.refs_2_), channel_id=1, source_target_pairs={{0,12},{1,13},{2,14},{3,15},{4,8},{5,9},{6,10},{7,11},{8,4},{9,5},... | collective-permute-start | bytes 245768 | tf_op jit(solution)/shard_map/ppermute | solution.py:534
  17.3 5.7 %collective-permute-start.4 = (bf16[320,128]{1,0:T(8,128)(2,1)S(1)}, bf16[320,128]{1,0:T(8,128)(2,1)S(1)}, u32[]{:S(2)}, u32[]{:S(2)}) collective-permute-start(bf16[320,128]{1,0:T(8,128)(2,1)S(1)} %get-tuple-element.66.refs_2_), channel_id=1, source_target_pairs={{0,4},{1,5},{2,6},{3,7},{4,0},{5,1},{6,2},{7,3},{8,12},{9,13},{10,... | collective-permute-start | bytes 245768 | tf_op jit(solution)/shard_map/ppermute | solution.py:534
  17.5 7.6 %collective-permute-start.5 = (bf16[320,128]{1,0:T(8,128)(2,1)S(1)}, bf16[320,128]{1,0:T(8,128)(2,1)S(1)}, u32[]{:S(2)}, u32[]{:S(2)}) collective-permute-start(bf16[320,128]{1,0:T(8,128)(2,1)S(1)} %get-tuple-element.66.refs_2_), channel_id=1, source_target_pairs={{0,2},{1,3},{2,0},{3,1},{4,6},{5,7},{6,4},{7,5},{8,10},{9,11},{10,... | collective-permute-start | bytes 245768 | tf_op jit(solution)/shard_map/ppermute | solution.py:534
  20.7 4.6 %collective-permute-start.6 = (bf16[320,128]{1,0:T(8,128)(2,1)S(1)}, bf16[320,128]{1,0:T(8,128)(2,1)S(1)}, u32[]{:S(2)}, u32[]{:S(2)}) collective-permute-start(bf16[320,128]{1,0:T(8,128)(2,1)S(1)} %collective-permute-done.2.refs_3_), channel_id=1, source_target_pairs={{0,2},{1,3},{2,0},{3,1},{4,6},{5,7},{6,4},{7,5},{8,10},{9,11},{10,... | collective-permute-start | bytes 245768 | tf_op jit(solution)/shard_map/ppermute | solution.py:534
  22.3 4.4 %collective-permute-start.7 = (bf16[320,128]{1,0:T(8,128)(2,1)S(1)}, bf16[320,128]{1,0:T(8,128)(2,1)S(1)}, u32[]{:S(2)}, u32[]{:S(2)}) collective-permute-start(bf16[320,128]{1,0:T(8,128)(2,1)S(1)} %collective-permute-done.3.refs_4_), channel_id=1, source_target_pairs={{0,2},{1,3},{2,0},{3,1},{4,6},{5,7},{6,4},{7,5},{8,10},{9,11},{10,... | collective-permute-start | bytes 245768 | tf_op jit(solution)/shard_map/ppermute | solution.py:534
  23.0 5.1 %collective-permute-start.8 = (bf16[320,128]{1,0:T(8,128)(2,1)S(1)}, bf16[320,128]{1,0:T(8,128)(2,1)S(1)}, u32[]{:S(2)}, u32[]{:S(2)}) collective-permute-start(bf16[320,128]{1,0:T(8,128)(2,1)S(1)} %collective-permute-done.4.refs_5_), channel_id=1, source_target_pairs={{0,2},{1,3},{2,0},{3,1},{4,6},{5,7},{6,4},{7,5},{8,10},{9,11},{10,... | collective-permute-start | bytes 245768 | tf_op jit(solution)/shard_map/ppermute | solution.py:534
  28.1 13.1 %collective-permute-start.14 = (bf16[416,384]{1,0:T(8,128)(2,1)S(1)}, bf16[416,384]{1,0:T(8,128)(2,1)S(1)}, u32[]{:S(2)}, u32[]{:S(2)}) collective-permute-start(bf16[416,384]{1,0:T(8,128)(2,1)S(1)} %get-tuple-element.85), channel_id=1, source_target_pairs={{0,2},{1,3},{2,0},{3,1},{4,6},{5,7},{6,4},{7,5},{8,10},{9,11},{10,... | collective-permute-start | bytes 958472 | tf_op jit(solution)/shard_map/ppermute | solution.py:534
  34.8 5.3 %collective-permute-start.9 = (bf16[4,160,128]{2,1,0:T(8,128)(2,1)S(1)}, bf16[4,160,128]{2,1,0:T(8,128)(2,1)S(1)}, u32[]{:S(2)}, u32[]{:S(2)}) collective-permute-start(bf16[4,160,128]{2,1,0:T(8,128)(2,1)S(1)} %get-tuple-element.71), channel_id=1, source_target_pairs={{0,2},{1,3},{2,0},{3,1},{4,6},{5,7},{6,4},{7,5},{8,10},{9,11},{10,... | collective-permute-start | bytes 491528 | tf_op jit(solution)/shard_map/ppermute | solution.py:534
  35.8 5.3 %collective-permute-start.10 = (bf16[4,160,128]{2,1,0:T(8,128)(2,1)S(1)}, bf16[4,160,128]{2,1,0:T(8,128)(2,1)S(1)}, u32[]{:S(2)}, u32[]{:S(2)}) collective-permute-start(bf16[4,160,128]{2,1,0:T(8,128)(2,1)S(1)} %get-tuple-element.73), channel_id=1, source_target_pairs={{0,4},{1,5},{2,6},{3,7},{4,0},{5,1},{6,2},{7,3},{8,12},{9,13},{10,... | collective-permute-start | bytes 491528 | tf_op jit(solution)/shard_map/ppermute | solution.py:534
  41.2 11.6 %collective-permute-start.15 = (bf16[416,384]{1,0:T(8,128)(2,1)S(1)}, bf16[416,384]{1,0:T(8,128)(2,1)S(1)}, u32[]{:S(2)}, u32[]{:S(2)}) collective-permute-start(bf16[416,384]{1,0:T(8,128)(2,1)S(1)} %collective-permute-done.14.refs_3_), channel_id=1, source_target_pairs={{0,1},{1,0},{2,3},{3,2},{4,5},{5,4},{6,7},{7,6},{8,9},{9,8},{10,11... | collective-permute-start | bytes 958472 | tf_op jit(solution)/shard_map/ppermute | solution.py:534
  41.3 11.5 %collective-permute-start.13 = (bf16[352,384]{1,0:T(8,128)(2,1)S(1)}, bf16[352,384]{1,0:T(8,128)(2,1)S(1)}, u32[]{:S(2)}, u32[]{:S(2)}) collective-permute-start(bf16[352,384]{1,0:T(8,128)(2,1)S(1)} %get-tuple-element.83), channel_id=1, source_target_pairs={{0,1},{1,0},{2,3},{3,2},{4,5},{5,4},{6,7},{7,6},{8,9},{9,8},{10,11... | collective-permute-start | bytes 811016 | tf_op jit(solution)/shard_map/ppermute | solution.py:534
  41.8 4.4 %collective-permute-start.11 = (bf16[2,160,128]{2,1,0:T(8,128)(2,1)S(1)}, bf16[2,160,128]{2,1,0:T(8,128)(2,1)S(1)}, u32[]{:S(2)}, u32[]{:S(2)}) collective-permute-start(bf16[2,160,128]{2,1,0:T(8,128)(2,1)S(1)} %get-tuple-element.76), channel_id=1, source_target_pairs={{0,4},{1,5},{2,6},{3,7},{4,0},{5,1},{6,2},{7,3},{8,12},{9,13},{10,... | collective-permute-start | bytes 245768 | tf_op jit(solution)/shard_map/ppermute | solution.py:534
  43.0 4.4 %collective-permute-start.12 = (bf16[2,160,128]{2,1,0:T(8,128)(2,1)S(1)}, bf16[2,160,128]{2,1,0:T(8,128)(2,1)S(1)}, u32[]{:S(2)}, u32[]{:S(2)}) collective-permute-start(bf16[2,160,128]{2,1,0:T(8,128)(2,1)S(1)} %get-tuple-element.78), channel_id=1, source_target_pairs={{0,2},{1,3},{2,0},{3,1},{4,6},{5,7},{6,4},{7,5},{8,10},{9,11},{10,... | collective-permute-start | bytes 245768 | tf_op jit(solution)/shard_map/ppermute | solution.py:534
  47.5 8.5 %collective-permute-start.22 = (bf16[128,1024]{1,0:T(8,128)(2,1)S(1)}, bf16[128,1024]{1,0:T(8,128)(2,1)S(1)}, u32[]{:S(2)}, u32[]{:S(2)}) collective-permute-start(bf16[128,1024]{1,0:T(8,128)(2,1)S(1)} %get-tuple-element.95.refs_0_.refs_1_), channel_id=1, source_target_pairs={{0,2},{1,3},{2,0},{3,1},{4,6},{5,7},{6,4},{7,5},{8,10},{9,11},{10,... | collective-permute-start | bytes 786440 | tf_op jit(solution)/shard_map/ppermute | solution.py:534
  48.0 7.6 %collective-permute-start.16 = (bf16[1,320,128]{2,1,0:T(8,128)(2,1)S(1)}, bf16[1,320,128]{2,1,0:T(8,128)(2,1)S(1)}, u32[]{:S(2)}, u32[]{:S(2)}) collective-permute-start(bf16[1,320,128]{2,1,0:T(8,128)(2,1)S(1)} %get-tuple-element.89), channel_id=1, source_target_pairs={{0,8},{1,9},{2,10},{3,11},{4,12},{5,13},{6,14},{7,15},{8,0},{9,1},... | collective-permute-start | bytes 245768 | tf_op jit(solution)/shard_map/ppermute | solution.py:534
  55.3 1.6 %collective-permute-start.21 = (bf16[128,1024]{1,0:T(8,128)(2,1)S(1)}, bf16[128,1024]{1,0:T(8,128)(2,1)S(1)}, u32[]{:S(2)}, u32[]{:S(2)}) collective-permute-start(bf16[128,1024]{1,0:T(8,128)(2,1)S(1)} %get-tuple-element.95.refs_0_.refs_1_), channel_id=1, source_target_pairs={{0,1},{1,0},{2,3},{3,2},{4,5},{5,4},{6,7},{7,6},{8,9},{9,8},{10,11... | collective-permute-start | bytes 786440 | tf_op jit(solution)/shard_map/ppermute | solution.py:534
  56.0 1.6 %collective-permute-start.23 = (bf16[128,1024]{1,0:T(8,128)(2,1)S(1)}, bf16[128,1024]{1,0:T(8,128)(2,1)S(1)}, u32[]{:S(2)}, u32[]{:S(2)}) collective-permute-start(bf16[128,1024]{1,0:T(8,128)(2,1)S(1)} %collective-permute-done.22.refs_3_), channel_id=1, source_target_pairs={{0,1},{1,0},{2,3},{3,2},{4,5},{5,4},{6,7},{7,6},{8,9},{9,8},{10,11... | collective-permute-start | bytes 786440 | tf_op jit(solution)/shard_map/ppermute | solution.py:534
  56.3 5.2 %collective-permute-start.20 = (bf16[144,384]{1,0:T(8,128)(2,1)S(1)}, bf16[144,384]{1,0:T(8,128)(2,1)S(1)}, u32[]{:S(2)}, u32[]{:S(2)}) collective-permute-start(bf16[144,384]{1,0:T(8,128)(2,1)S(1)} %get-tuple-element.93.refs_1_), channel_id=1, source_target_pairs={{0,2},{1,3},{2,0},{3,1},{4,6},{5,7},{6,4},{7,5},{8,10},{9,11},{10,... | collective-permute-start | bytes 331784 | tf_op jit(solution)/shard_map/ppermute | solution.py:534
  58.4 7.2 %collective-permute-start.25 = (bf16[2,48,1024]{2,1,0:T(8,128)(2,1)S(1)}, bf16[2,48,1024]{2,1,0:T(8,128)(2,1)S(1)}, u32[]{:S(2)}, u32[]{:S(2)}) collective-permute-start(bf16[2,48,1024]{2,1,0:T(8,128)(2,1)S(1)} %get-tuple-element.100), channel_id=1, source_target_pairs={{0,4},{1,5},{2,6},{3,7},{4,0},{5,1},{6,2},{7,3},{8,12},{9,13},{10,... | collective-permute-start | bytes 589832 | tf_op jit(solution)/shard_map/ppermute | solution.py:534
  58.5 7.2 %collective-permute-start.18 = (bf16[256,384]{1,0:T(8,128)(2,1)S(1)}, bf16[256,384]{1,0:T(8,128)(2,1)S(1)}, u32[]{:S(2)}, u32[]{:S(2)}) collective-permute-start(bf16[256,384]{1,0:T(8,128)(2,1)S(1)} %get-tuple-element.92.refs_2_), channel_id=1, source_target_pairs={{0,2},{1,3},{2,0},{3,1},{4,6},{5,7},{6,4},{7,5},{8,10},{9,11},{10,... | collective-permute-start | bytes 589832 | tf_op jit(solution)/shard_map/ppermute | solution.py:534
  59.4 2.7 %collective-permute-start.19 = (bf16[144,384]{1,0:T(8,128)(2,1)S(1)}, bf16[144,384]{1,0:T(8,128)(2,1)S(1)}, u32[]{:S(2)}, u32[]{:S(2)}) collective-permute-start(bf16[144,384]{1,0:T(8,128)(2,1)S(1)} %get-tuple-element.93.refs_1_), channel_id=1, source_target_pairs={{0,1},{1,0},{2,3},{3,2},{4,5},{5,4},{6,7},{7,6},{8,9},{9,8},{10,11... | collective-permute-start | bytes 331784 | tf_op jit(solution)/shard_map/ppermute | solution.py:534
  61.5 5.8 %collective-permute-start.17 = (bf16[256,384]{1,0:T(8,128)(2,1)S(1)}, bf16[256,384]{1,0:T(8,128)(2,1)S(1)}, u32[]{:S(2)}, u32[]{:S(2)}) collective-permute-start(bf16[256,384]{1,0:T(8,128)(2,1)S(1)} %get-tuple-element.92.refs_2_), channel_id=1, source_target_pairs={{0,1},{1,0},{2,3},{3,2},{4,5},{5,4},{6,7},{7,6},{8,9},{9,8},{10,11... | collective-permute-start | bytes 589832 | tf_op jit(solution)/shard_map/ppermute | solution.py:534
  65.7 1.6 %collective-permute-start.26 = (bf16[256,384]{1,0:T(8,128)(2,1)S(1)}, bf16[256,384]{1,0:T(8,128)(2,1)S(1)}, u32[]{:S(2)}, u32[]{:S(2)}) collective-permute-start(bf16[256,384]{1,0:T(8,128)(2,1)S(1)} %collective-permute-done.18.refs_4_), channel_id=1, source_target_pairs={{0,1},{1,0},{2,3},{3,2},{4,5},{5,4},{6,7},{7,6},{8,9},{9,8},{10,11... | collective-permute-start | bytes 589832 | tf_op jit(solution)/shard_map/ppermute | solution.py:534
  65.7 6.7 %collective-permute-start.29 = (bf16[1,128,384]{2,1,0:T(8,128)(2,1)S(1)}, bf16[1,128,384]{2,1,0:T(8,128)(2,1)S(1)}, u32[]{:S(2)}, u32[]{:S(2)}) collective-permute-start(bf16[1,128,384]{2,1,0:T(8,128)(2,1)S(1)} %get-tuple-element.108), channel_id=1, source_target_pairs={{0,4},{1,5},{2,6},{3,7},{4,0},{5,1},{6,2},{7,3},{8,12},{9,13},{10,... | collective-permute-start | bytes 294920 | tf_op jit(solution)/shard_map/ppermute | solution.py:534
  68.5 8.4 %collective-permute-start.27 = (bf16[1,160,384]{2,1,0:T(8,128)(2,1)S(1)}, bf16[1,160,384]{2,1,0:T(8,128)(2,1)S(1)}, u32[]{:S(2)}, u32[]{:S(2)}) collective-permute-start(bf16[1,160,384]{2,1,0:T(8,128)(2,1)S(1)} %get-tuple-element.105), channel_id=1, source_target_pairs={{0,4},{1,5},{2,6},{3,7},{4,0},{5,1},{6,2},{7,3},{8,12},{9,13},{10,... | collective-permute-start | bytes 368648 | tf_op jit(solution)/shard_map/ppermute | solution.py:534
  70.0 7.6 %collective-permute-start.28 = (bf16[1,48,1024]{2,1,0:T(8,128)(2,1)S(1)}, bf16[1,48,1024]{2,1,0:T(8,128)(2,1)S(1)}, u32[]{:S(2)}, u32[]{:S(2)}) collective-permute-start(bf16[1,48,1024]{2,1,0:T(8,128)(2,1)S(1)} %get-tuple-element.106), channel_id=1, source_target_pairs={{0,8},{1,9},{2,10},{3,11},{4,12},{5,13},{6,14},{7,15},{8,0},{9,1},... | collective-permute-start | bytes 294920 | tf_op jit(solution)/shard_map/ppermute | solution.py:534
  72.5 10.0 %collective-permute-start.30 = (bf16[1,128,384]{2,1,0:T(8,128)(2,1)S(1)}, bf16[1,128,384]{2,1,0:T(8,128)(2,1)S(1)}, u32[]{:S(2)}, u32[]{:S(2)}) collective-permute-start(bf16[1,128,384]{2,1,0:T(8,128)(2,1)S(1)} %conv_send_on.3), channel_id=1, source_target_pairs={{0,8},{1,9},{2,10},{3,11},{4,12},{5,13},{6,14},{7,15},{8,0},{9,1},... | collective-permute-start | bytes 294920 | tf_op jit(solution)/shard_map/ppermute | solution.py:534
  73.7 11.9 %collective-permute-start.31 = (bf16[1,288,384]{2,1,0:T(8,128)(2,1)S(1)}, bf16[1,288,384]{2,1,0:T(8,128)(2,1)S(1)}, u32[]{:S(2)}, u32[]{:S(2)}) collective-permute-start(bf16[1,288,384]{2,1,0:T(8,128)(2,1)S(1)} %get-tuple-element.110), channel_id=1, source_target_pairs={{0,4},{1,5},{2,6},{3,7},{4,0},{5,1},{6,2},{7,3},{8,12},{9,13},{10,... | collective-permute-start | bytes 663560 | tf_op jit(solution)/shard_map/ppermute | solution.py:534
  76.9 8.7 %collective-permute-start.32 = (bf16[1,160,384]{2,1,0:T(8,128)(2,1)S(1)}, bf16[1,160,384]{2,1,0:T(8,128)(2,1)S(1)}, u32[]{:S(2)}, u32[]{:S(2)}) collective-permute-start(bf16[1,160,384]{2,1,0:T(8,128)(2,1)S(1)} %conv_send_on.2), channel_id=1, source_target_pairs={{0,8},{1,9},{2,10},{3,11},{4,12},{5,13},{6,14},{7,15},{8,0},{9,1},... | collective-permute-start | bytes 368648 | tf_op jit(solution)/shard_map/ppermute | solution.py:534
  (9 other events, 91.3 us)
